TPU v7x, 32 devices: a whole 2x2x4 slice. The times are simulated.
32 devices in a mesh: dp: 4 (over x, core), expert: 8 (over z, y).
Axes of the slice: x: 2, y: 2, z: 4, core: 2. Of those that a mesh axis runs over, the one named last changes fastest.
Arguments:
- designs: bfloat16 [4096, 1024], P(('dp', 'expert')), may hold values from -6 to 6
- archetype: int32 [4096, 1], P(('dp', 'expert')), may hold values from 0 to 3; in each aligned block of 128 rows (0 to 127, 128 to 255, ...) at most 36 rows name the same one
- w_gate: bfloat16 [1024, 16384], P(None, 'expert'), may hold values from -0.1875 to 0.1875
- w_up: bfloat16 [1024, 16384], P(None, 'expert'), may hold values from -0.1875 to 0.1875
- w_down: bfloat16 [16384, 1024], P('expert'), may hold values from -0.09375 to 0.09375
- cotangent: bfloat16 [4096, 1024], P(('dp', 'expert')), may hold values from -0.75 to 0.75
Outputs:
- outputs: bfloat16 [4096, 1024], P(('dp', 'expert'))
- grad_gate: bfloat16 [1024, 16384], P('dp', 'expert')
- grad_up: bfloat16 [1024, 16384], P('dp', 'expert')
Inputs may be any that keep to these rules, and one draw needn't show every extreme that they name: In each aligned block of 128 rows (the rows of one device) no archetype is named by more than 36 rows.
All inputs are finite; a program needn't handle non-finite values.
Results may differ from a plain program's by a relative error of at most 0.009.
Values may be sent and summed in bfloat16 or wider, within the bound.
No kernel may reach another device: no remote copies, remote signals or barrier semaphores. Data moves between devices by JAX's collectives and lax.ppermute only.
A program may use at most 128 MiB of HBM per device.

v0:
```python
import jax
import jax.numpy as jnp
from jax import lax
from jax.sharding import PartitionSpec as P

EXPERTS = 4
CAP = 36


def silu_parts(gate):
    sigma = jax.nn.sigmoid(gate)
    return (gate * sigma, sigma * (1.0 + gate * (1.0 - sigma)))


def contract_rows(left, right):
    return lax.dot_general(
        left, right, (((0,), (0,)), ((), ())), preferred_element_type=jnp.float32
    )


def per_device(designs, archetype, w_gate, w_up, w_down, cotangent):
    tok_rows, width = designs.shape
    owners = lax.axis_size("expert")
    sharers = owners // EXPERTS
    hidden_cols = w_gate.shape[1]
    labels = archetype[:, 0]
    onehot = (labels[:, None] == jnp.arange(EXPERTS, dtype=jnp.int32)[None, :]).astype(jnp.int32)
    ranks = jnp.cumsum(onehot, axis=0) - onehot
    target = labels * CAP + jnp.sum(ranks * onehot, axis=1)
    placer = (jnp.arange(EXPERTS * CAP, dtype=jnp.int32)[:, None] == target[None, :]).astype(
        jnp.bfloat16
    )
    packed_x = (
        jnp.dot(placer, designs, preferred_element_type=jnp.float32)
        .astype(jnp.bfloat16)
        .reshape(EXPERTS, CAP, width)
    )
    packed_g = (
        jnp.dot(placer, cotangent, preferred_element_type=jnp.float32)
        .astype(jnp.bfloat16)
        .reshape(EXPERTS, CAP, width)
    )
    send_x = jnp.repeat(packed_x, sharers, axis=0)
    send_g = jnp.repeat(packed_g, sharers, axis=0)
    recv_x, recv_g = (
        lax.all_to_all(send_x, "expert", split_axis=0, concat_axis=0, tiled=True),
        lax.all_to_all(send_g, "expert", split_axis=0, concat_axis=0, tiled=True),
    )
    flat_x = recv_x.reshape(owners * CAP, width)
    gate = jnp.dot(flat_x, w_gate, preferred_element_type=jnp.float32)
    up = jnp.dot(flat_x, w_up, preferred_element_type=jnp.float32)
    act, slope = silu_parts(gate)
    hidden = (act * up).astype(jnp.bfloat16)
    partial_value = (
        jnp.dot(hidden, w_down, preferred_element_type=jnp.float32)
        .astype(jnp.bfloat16)
        .reshape(owners, CAP, width)
    )
    returned = lax.all_to_all(partial_value, "expert", split_axis=0, concat_axis=0, tiled=True)
    summed = jnp.sum(
        returned.astype(jnp.float32).reshape(EXPERTS, sharers, CAP, width), axis=1
    ).reshape(EXPERTS * CAP, width)
    outputs = jnp.take(summed, target, axis=0).astype(jnp.bfloat16)
    flat_g = recv_g.reshape(owners * CAP, width)
    d_hidden = lax.dot_general(
        flat_g, w_down, (((1,), (1,)), ((), ())), preferred_element_type=jnp.float32
    )
    d_gate = (d_hidden * up * slope).astype(jnp.bfloat16)
    d_up = (d_hidden * act).astype(jnp.bfloat16)
    share = width // lax.axis_size("dp")
    totals = lax.psum(
        jnp.concatenate(
            [contract_rows(flat_x, d_gate), contract_rows(flat_x, d_up)], axis=1
        ).astype(jnp.bfloat16),
        "dp",
    ).astype(jnp.float32)
    mine = lax.dynamic_slice_in_dim(totals, lax.axis_index("dp") * share, share, 0)
    grad_gate = mine[:, :hidden_cols].astype(jnp.bfloat16)
    grad_up = mine[:, hidden_cols:].astype(jnp.bfloat16)
    return (outputs, grad_gate, grad_up)


def solution(mesh):
    return jax.shard_map(
        per_device,
        mesh=mesh,
        in_specs=(
            P(("dp", "expert"), None),
            P(("dp", "expert"), None),
            P(None, "expert"),
            P(None, "expert"),
            P("expert", None),
            P(("dp", "expert"), None),
        ),
        out_specs=(P(("dp", "expert"), None), P("dp", "expert"), P("dp", "expert")),
        check_vma=False,
    )
```

profile of v0, /device:TPU:0, one launch (start us, length us, event | category | flops | bytes accessed | tf_op | source)
XLA Modules:
  0.0 240.3 jit_solution(14598085051448861660)
XLA Ops:
  7.2 0.8 fusion.4
  8.0 0.2 reduce_window_sum.11
  8.2 0.8 select_reduce_fusion
  9.0 0.7 multiply_add_fusion
  9.7 0.2 convolution_convert_fusion.4
  10.0 0.9 broadcast_in_dim.20
  10.9 7.3 %all-to-all-start = ((bf16[8,36,1024]{2,1,0:T(8,128)(2,1)}), bf16[8,36,1024]{2,1,0:T(8,128)(2,1)S(1)}, u32[]{:S(2)}, u32[]{:S(2)}) async-start(bf16[8,36,1024]{2,1,0:T(8,128)(2,1)} %bitcast.3), calls=%async_computation | async-start | bytes 1310720 | tf_op jit(solution)/shard_map/all_to_all | solution.py:46
  18.2 0.2 convolution_convert_fusion.3
  18.5 17.0 %all-to-all-done = bf16[8,36,1024]{2,1,0:T(8,128)(2,1)S(1)} async-done(((bf16[8,36,1024]{2,1,0:T(8,128)(2,1)}), bf16[8,36,1024]{2,1,0:T(8,128)(2,1)S(1)}, u32[]{:S(2)}, u32[]{:S(2)}) %all-to-all-start) | async-done | bytes 589856 | tf_op jit(solution)/shard_map/all_to_all | solution.py:46
  35.5 0.9 broadcast_in_dim.22
  36.4 3.6 %all-to-all-start.2 = ((bf16[8,36,1024]{2,1,0:T(8,128)(2,1)}), bf16[8,36,1024]{2,1,0:T(8,128)(2,1)S(1)}, u32[]{:S(2)}, u32[]{:S(2)}) async-start(bf16[8,36,1024]{2,1,0:T(8,128)(2,1)} %bitcast.6), calls=%async_computation.2 | async-start | bytes 1310720 | tf_op jit(solution)/shard_map/all_to_all | solution.py:47
  40.1 0.1 reshape.52
  40.2 5.2 %fusion.12 = f32[288,2048]{1,0:T(8,128)} fusion(bf16[288,1024]{1,0:T(8,128)(2,1)S(1)} %reshape.52, bf16[1024,2048]{1,0:T(8,128)(2,1)} %param.9), kind=kOutput, calls=%fused_computation.32 | convolution fusion | flops 1207959552 | bytes 7143424 | tf_op jit(solution)/shard_map/dot_general | solution.py:51
  45.4 2.8 %fusion.11 = f32[288,2048]{1,0:T(8,128)} fusion(bf16[288,1024]{1,0:T(8,128)(2,1)S(1)} %reshape.52, bf16[1024,2048]{1,0:T(8,128)(2,1)S(1)} %copy-done.3), kind=kOutput, calls=%fused_computation.31 | convolution fusion | flops 1207959552 | bytes 7143424 | tf_op jit(solution)/shard_map/dot_general | solution.py:50
  48.2 9.3 %all-to-all-done.2 = bf16[8,36,1024]{2,1,0:T(8,128)(2,1)S(1)} async-done(((bf16[8,36,1024]{2,1,0:T(8,128)(2,1)}), bf16[8,36,1024]{2,1,0:T(8,128)(2,1)S(1)}, u32[]{:S(2)}, u32[]{:S(2)}) %all-to-all-start.2) | async-done | bytes 589856 | tf_op jit(solution)/shard_map/all_to_all | solution.py:47
  57.5 0.1 reshape.59
  57.6 3.8 %fusion.13 = f32[288,2048]{1,0:T(8,128)S(1)} fusion(bf16[288,1024]{1,0:T(8,128)(2,1)S(1)} %reshape.59, bf16[2048,1024]{1,0:T(8,128)(2,1)} %param.10), kind=kOutput, calls=%fused_computation.33 | convolution fusion | flops 1207959552 | bytes 7143424 | tf_op jit(solution)/shard_map/dot_general | solution.py:65
  61.4 4.5 %convolution_convert_fusion = bf16[1024,2048]{1,0:T(8,128)(2,1)} fusion(bf16[288,1024]{1,0:T(8,128)(2,1)S(1)} %reshape.52, f32[288,2048]{1,0:T(8,128)S(1)} %fusion.13, f32[288,2048]{1,0:T(8,128)S(1)} %copy-done.6), kind=kOutput, calls=%fused_computation.3 | convolution fusion | flops 1213595648 | bytes 9502720 | tf_op jit(solution)/shard_map/dot_general | solution.py:16
  65.9 4.5 %convolution_convert_fusion.1 = bf16[1024,2048]{1,0:T(8,128)(2,1)} fusion(bf16[288,1024]{1,0:T(8,128)(2,1)S(1)} %reshape.52, f32[288,2048]{1,0:T(8,128)S(1)} %copy-done.6, f32[288,2048]{1,0:T(8,128)S(1)} %fusion.13, f32[288,2048]{1,0:T(8,128)S(1)} %copy-done.4), kind=kOutput, calls=%fused_computation.4 | convolution fusion | flops 1215954944 | bytes 11862016 | tf_op jit(solution)/shard_map/dot_general | solution.py:16
  70.4 7.8 %pad_maximum_fusion = bf16[1024,4096]{1,0:T(8,128)(2,1)} fusion(bf16[1024,2048]{1,0:T(8,128)(2,1)} %convolution_convert_fusion, bf16[1024,2048]{1,0:T(8,128)(2,1)} %convolution_convert_fusion.1), kind=kLoop, calls=%fused_computation.1 | loop fusion | flops 16777216 | bytes 16777216 | tf_op jit(solution)/shard_map/concatenate | solution.py:72
  78.2 1.6 copy-done.5
  79.9 4.5 %convolution_convert_fusion.2 = bf16[288,1024]{1,0:T(8,128)(2,1)S(1)} fusion(bf16[2048,1024]{1,0:T(8,128)(2,1)} %param.10, f32[288,2048]{1,0:T(8,128)S(1)} %copy-done.5, f32[288,2048]{1,0:T(8,128)} %fusion.11), kind=kOutput, calls=%fused_computation.10 | convolution fusion | flops 1211793408 | bytes 9502720 | tf_op jit(solution)/shard_map/dot_general | solution.py:55
  84.4 0.9 reshape.53
  85.4 3.6 %all-to-all-start.1 = ((bf16[8,36,1024]{2,1,0:T(8,128)(2,1)}), bf16[8,36,1024]{2,1,0:T(8,128)(2,1)S(1)}, u32[]{:S(2)}, u32[]{:S(2)}) async-start(bf16[8,36,1024]{2,1,0:T(8,128)(2,1)} %reshape.53), calls=%async_computation.1 | async-start | bytes 1310720 | tf_op jit(solution)/shard_map/all_to_all | solution.py:59
  89.0 17.4 %all-to-all-done.1 = bf16[8,36,1024]{2,1,0:T(8,128)(2,1)S(1)} async-done(((bf16[8,36,1024]{2,1,0:T(8,128)(2,1)}), bf16[8,36,1024]{2,1,0:T(8,128)(2,1)S(1)}, u32[]{:S(2)}, u32[]{:S(2)}) %all-to-all-start.1) | async-done | bytes 589856 | tf_op jit(solution)/shard_map/all_to_all | solution.py:59
  106.4 0.1 convert_reduce_fusion
  106.6 0.1 reshape.56
  106.6 0.9 gather_fusion
  107.5 0.8 select_convert_fusion
  108.3 122.0 %all-reduce.2.cloned.1.call-done = bf16[1024,4096]{1,0:T(8,128)(2,1)} async-done(((bf16[1024,4096]{1,0:T(8,128)(2,1)}), bf16[1024,4096]{1,0:T(8,128)(2,1)}) %all-reduce.2.cloned.1.call-update) | async-done | bytes 8388624 | tf_op jit(solution)/shard_map/psum | solution.py:71
  230.3 1.7 convert_convert_fusion
  232.0 1.5 fusion.10
  (19 shorter events, 0.2 us)
Async XLA Ops:
  7.2 2.5 %copy-start = (bf16[128,1024]{1,0:T(8,128)(2,1)S(1)}, bf16[128,1024]{1,0:T(8,128)(2,1)}, u32[]{:S(2)}) copy-start(bf16[128,1024]{1,0:T(8,128)(2,1)} %param.6) | copy-start | bytes 786436
  7.2 11.0 %copy-start.1 = (bf16[128,1024]{1,0:T(8,128)(2,1)S(1)}, bf16[128,1024]{1,0:T(8,128)(2,1)}, u32[]{:S(2)}) copy-start(bf16[128,1024]{1,0:T(8,128)(2,1)} %param.11) | copy-start | bytes 786436
  10.9 24.6 %all-to-all-start = ((bf16[8,36,1024]{2,1,0:T(8,128)(2,1)}), bf16[8,36,1024]{2,1,0:T(8,128)(2,1)S(1)}, u32[]{:S(2)}, u32[]{:S(2)}) async-start(bf16[8,36,1024]{2,1,0:T(8,128)(2,1)} %bitcast.3), calls=%async_computation | async-start | bytes 1310720 | tf_op jit(solution)/shard_map/all_to_all | solution.py:46
  36.4 21.1 %all-to-all-start.2 = ((bf16[8,36,1024]{2,1,0:T(8,128)(2,1)}), bf16[8,36,1024]{2,1,0:T(8,128)(2,1)S(1)}, u32[]{:S(2)}, u32[]{:S(2)}) async-start(bf16[8,36,1024]{2,1,0:T(8,128)(2,1)} %bitcast.6), calls=%async_computation.2 | async-start | bytes 1310720 | tf_op jit(solution)/shard_map/all_to_all | solution.py:47
  40.0 190.3 %all-reduce.2.cloned.1.call-start = ((), (), s32[]{:S(2)}) async-start(), calls=%async_computation.3 | async-start | bytes 16777216 | tf_op jit(solution)/shard_map/psum | solution.py:71
  40.2 5.2 %copy-start.3 = (bf16[1024,2048]{1,0:T(8,128)(2,1)S(1)}, bf16[1024,2048]{1,0:T(8,128)(2,1)}, u32[]{:S(2)}) copy-start(bf16[1024,2048]{1,0:T(8,128)(2,1)} %param.8) | copy-start | bytes 12582916
  57.6 3.8 %copy-start.6 = (f32[288,2048]{1,0:T(8,128)S(1)}, f32[288,2048]{1,0:T(8,128)}, u32[]{:S(2)}) copy-start(f32[288,2048]{1,0:T(8,128)} %fusion.11) | copy-start | bytes 7077892
  61.4 4.5 %copy-start.4 = (f32[288,2048]{1,0:T(8,128)S(1)}, f32[288,2048]{1,0:T(8,128)}, u32[]{:S(2)}) copy-start(f32[288,2048]{1,0:T(8,128)} %fusion.12) | copy-start | bytes 7077892
  78.2 1.7 copy-start.5
  84.4 4.6 %copy-start.2 = (s32[128,1]{0,1:T(1,128)S(1)}, s32[128,1]{0,1:T(1,128)}, u32[]{:S(2)}) copy-start(s32[128,1]{0,1:T(1,128)} %param.7) | copy-start | bytes 1540
  85.4 21.1 %all-to-all-start.1 = ((bf16[8,36,1024]{2,1,0:T(8,128)(2,1)}), bf16[8,36,1024]{2,1,0:T(8,128)(2,1)S(1)}, u32[]{:S(2)}, u32[]{:S(2)}) async-start(bf16[8,36,1024]{2,1,0:T(8,128)(2,1)} %reshape.53), calls=%async_computation.1 | async-start | bytes 1310720 | tf_op jit(solution)/shard_map/all_to_all | solution.py:59
Sparse Core Ops, SparseCore 0:
  78.4 151.9 all-reduce.1
where the time goes:
time: 241 us; the launch traced here: 240 us
  waiting for transfers between devices  166 us (69%)
  matrix products  25.7 us (11%)
  starting transfers between devices  14.6 us (6%)
  between operations  14.2 us (6%)
  other arithmetic  12.9 us (5%)
  local copies, waits for them, and re-layouts  7.18 us (3%)
    psum x1, waiting for transfers between devices, per_device(): lax.psum(jnp.concatenate([contract_rows(flat_x, d_gate), contract_rows(fl...  122 us
    all_to_all x1, waiting for transfers between devices, per_device(): lax.all_to_all(partial_value, 'expert', split_axis=0, concat_axis=0, tile...  17.4 us
    all_to_all x1, waiting for transfers between devices, per_device(): lax.all_to_all(send_x, 'expert', split_axis=0, concat_axis=0, tiled=True)  17 us
    all_to_all x1, waiting for transfers between devices, per_device(): lax.all_to_all(send_g, 'expert', split_axis=0, concat_axis=0, tiled=True)  9.33 us
    dot_general x2, matrix products, contract_rows(): lax.dot_general(left, right, (((0,), (0,)), ((), ())), preferred_element_...  9 us
    concatenate x1, other arithmetic, per_device(): jnp.concatenate([contract_rows(flat_x, d_gate), contract_rows(flat_x, d_u...  7.8 us
    all_to_all x1, starting transfers between devices, per_device(): lax.all_to_all(send_x, 'expert', split_axis=0, concat_axis=0, tiled=True)  7.28 us
    dot_general x1, matrix products, per_device(): up = jnp.dot(flat_x, w_up, preferred_element_type=jnp.float32)  5.16 us
  transfers between devices with their start and end apart: 4, of which 4 were waited for; matrix products, arithmetic and copies ran while one was open for 7% of the time, Pallas kernels for 0%

commit v1 on v0

v1 whole, which is shorter than its diff:
```python
import functools

import jax
import jax.numpy as jnp
from jax import lax
from jax.experimental import pallas as pl
from jax.experimental.pallas import tpu as pltpu
from jax.sharding import Mesh
from jax.sharding import PartitionSpec as P

EXPERTS = 4
CAP = 36
SLOT = 40
BLOCK = 256
VMEM_LIMIT = 48 * 1024 * 1024
F32 = jnp.float32
BF16 = jnp.bfloat16


def silu_parts(gate):
    sigma = jax.nn.sigmoid(gate)
    return (gate * sigma, sigma * (1.0 + gate * (1.0 - sigma)))


def contract_rows(left, right):
    return lax.dot_general(left, right, (((0,), (0,)), ((), ())), preferred_element_type=F32)


def contract_cols(left, right):
    return lax.dot_general(left, right, (((1,), (1,)), ((), ())), preferred_element_type=F32)


def pack_kernel(plane_ref, kind_ref, x_ref, g_ref, *outs):
    rows = kind_ref.shape[0]
    key = kind_ref[...] ^ plane_ref[0]
    lane = lax.broadcasted_iota(jnp.int32, (rows, 128), 1)
    onehot = (key == lane).astype(F32)
    below = lax.broadcasted_iota(jnp.int32, (rows, rows), 0) > lax.broadcasted_iota(
        jnp.int32, (rows, rows), 1
    )
    ranks = jnp.dot(below.astype(BF16), onehot.astype(BF16), preferred_element_type=F32)
    rank = jnp.sum(ranks * onehot, axis=1, keepdims=True).astype(jnp.int32)
    place = key * SLOT + rank
    slots = EXPERTS * SLOT
    chosen = (place == lax.broadcasted_iota(jnp.int32, (rows, slots), 1)).astype(F32)
    outs[2 * EXPERTS][...] = chosen.astype(BF16)
    placer = chosen.T.astype(BF16)
    for source, first in ((x_ref, 0), (g_ref, EXPERTS)):
        packed = jnp.dot(placer, source[...], preferred_element_type=F32)
        for k in range(EXPERTS):
            outs[first + k][...] = packed[k * SLOT : (k + 1) * SLOT].astype(BF16)


def pack(plane, kind, x, g):
    rows, width = x.shape
    block = jax.ShapeDtypeStruct((SLOT, width), BF16)
    return pl.pallas_call(
        pack_kernel,
        out_shape=[block] * (2 * EXPERTS) + [jax.ShapeDtypeStruct((rows, EXPERTS * SLOT), BF16)],
        in_specs=[pl.BlockSpec(memory_space=pltpu.SMEM)] + [pl.BlockSpec(memory_space=pltpu.VMEM)] * 3,
        name="pack",
    )(plane, kind, x, g)


def forward_kernel(with_down, xa_ref, xb_ref, wg_ref, wu_ref, wd_ref, *refs):
    if with_down:
        act_ref, coef_ref, sa_ref, sb_ref, x_ref, acc_ref = refs
    else:
        act_ref, coef_ref, x_ref = refs
    step = pl.program_id(0)
    half = xa_ref.shape[0]

    @pl.when(step == 0)
    def _():
        x_ref[:half, :] = xa_ref[...]
        x_ref[half:, :] = xb_ref[...]

    x = x_ref[...]
    gate = jnp.dot(x, wg_ref[...], preferred_element_type=F32)
    up = jnp.dot(x, wu_ref[...], preferred_element_type=F32)
    act, slope = silu_parts(gate)
    act_ref[...] = act.astype(BF16)
    coef_ref[...] = (up * slope).astype(BF16)
    if with_down:
        hidden = (act * up).astype(BF16)
        part = jnp.dot(hidden, wd_ref[...], preferred_element_type=F32)

        @pl.when(step == 0)
        def _():
            acc_ref[...] = part

        @pl.when(step > 0)
        def _():
            acc_ref[...] += part

        @pl.when(step == pl.num_programs(0) - 1)
        def _():
            sa_ref[...] = acc_ref[:half, :].astype(BF16)
            sb_ref[...] = acc_ref[half:, :].astype(BF16)


def forward(xa, xb, wg, wu, wd, with_down):
    half, width = xa.shape
    cols = wg.shape[1]
    rows = 2 * half
    whole = pl.BlockSpec((half, width), lambda j: (0, 0))
    wide = pl.BlockSpec((rows, BLOCK), lambda j: (0, j))
    out_shape = [jax.ShapeDtypeStruct((rows, cols), BF16)] * 2
    out_specs = [wide, wide]
    scratch = [pltpu.VMEM((rows, width), BF16)]
    if with_down:
        out_shape += [jax.ShapeDtypeStruct((half, width), BF16)] * 2
        out_specs += [whole, whole]
        scratch += [pltpu.VMEM((rows, width), F32)]
    count = 3 if with_down else 2
    down_spec = pl.BlockSpec((BLOCK, width), (lambda j: (j, 0)) if with_down else (lambda j: (0, 0)))
    return pl.pallas_call(
        functools.partial(forward_kernel, with_down),
        grid=(cols // BLOCK,),
        in_specs=[
            whole,
            whole,
            pl.BlockSpec((width, BLOCK), lambda j: (0, j)),
            pl.BlockSpec((width, BLOCK), lambda j: (0, j)),
            down_spec,
        ],
        out_specs=out_specs,
        out_shape=out_shape,
        scratch_shapes=scratch,
        compiler_params=pltpu.CompilerParams(vmem_limit_bytes=VMEM_LIMIT),
        cost_estimate=pl.CostEstimate(
            flops=2 * count * rows * width * cols,
            bytes_accessed=2 * count * width * cols + 4 * rows * cols,
            transcendentals=rows * cols,
        ),
        name="forward_down" if with_down else "forward",
    )(xa, xb, wg, wu, wd)


def backward_kernel(where_ref, *refs):
    xs, gs = refs[0:4], refs[4:8]
    act0, coef0, act1, coef1, wd_ref = refs[8:13]
    own_gate, own_up, sib_gate, sib_up = refs[13:17]
    g_ref, xt_ref = refs[17:19]
    part = xs[0].shape[0]
    share = own_gate.shape[0]

    @pl.when(pl.program_id(0) == 0)
    def _():
        for i in range(4):
            g_ref[i * part : (i + 1) * part, :] = gs[i][...]
        whole = jnp.concatenate([x[...].astype(F32) for x in xs], axis=0)
        xt_ref[...] = whole.T.astype(BF16)

    d_hidden = contract_cols(g_ref[...], wd_ref[...])
    act = jnp.concatenate([act0[...], act1[...]], axis=0).astype(F32)
    coef = jnp.concatenate([coef0[...], coef1[...]], axis=0).astype(F32)
    d_gate = (d_hidden * coef).astype(BF16)
    d_up = (d_hidden * act).astype(BF16)
    mine = pl.multiple_of(where_ref[1] * share, share)
    other = pl.multiple_of((1 - where_ref[1]) * share, share)
    x_mine = xt_ref[pl.ds(mine, share), :]
    x_other = xt_ref[pl.ds(other, share), :]
    sib_gate[...] = jnp.dot(x_other, d_gate, preferred_element_type=F32).astype(BF16)
    sib_up[...] = jnp.dot(x_other, d_up, preferred_element_type=F32).astype(BF16)
    own_gate[...] = jnp.dot(x_mine, d_gate, preferred_element_type=F32).astype(BF16)
    own_up[...] = jnp.dot(x_mine, d_up, preferred_element_type=F32).astype(BF16)


def backward(where, xs, gs, act0, coef0, act1, coef1, wd, share):
    part, width = xs[0].shape
    cols = wd.shape[0]
    rows = 4 * part
    half = 2 * share
    wide = pl.BlockSpec((2 * part, BLOCK), lambda j, w: (0, j))
    grad = pl.BlockSpec((share, BLOCK), lambda j, w: (0, j))
    return pl.pallas_call(
        backward_kernel,
        grid_spec=pltpu.PrefetchScalarGridSpec(
            num_scalar_prefetch=1,
            grid=(cols // BLOCK,),
            in_specs=[pl.BlockSpec((part, half), lambda j, w: (0, w[0]))] * 4
            + [pl.BlockSpec((part, width), lambda j, w: (0, 0))] * 4
            + [wide] * 4
            + [pl.BlockSpec((BLOCK, width), lambda j, w: (j, 0))],
            out_specs=[grad] * 4,
            scratch_shapes=[pltpu.VMEM((rows, width), BF16), pltpu.VMEM((half, rows), BF16)],
        ),
        out_shape=[jax.ShapeDtypeStruct((share, cols), BF16)] * 4,
        compiler_params=pltpu.CompilerParams(vmem_limit_bytes=VMEM_LIMIT),
        cost_estimate=pl.CostEstimate(
            flops=2 * rows * cols * (width + 2 * half),
            bytes_accessed=2 * width * cols + 8 * rows * cols + 8 * share * cols,
            transcendentals=0,
        ),
        name="backward",
    )(where, *xs, *gs, act0, coef0, act1, coef1, wd)


def combine_kernel(mine_ref, theirs_ref, *outs):
    total = mine_ref[...].astype(F32) + theirs_ref[...].astype(F32)
    for k in range(EXPERTS):
        outs[k][...] = total[k * SLOT : (k + 1) * SLOT].astype(BF16)


def combine(mine, theirs):
    width = mine.shape[1]
    return pl.pallas_call(
        combine_kernel,
        out_shape=[jax.ShapeDtypeStruct((SLOT, width), BF16)] * EXPERTS,
        name="combine",
    )(mine, theirs)


def unpack_kernel(chosen_ref, *refs):
    parts = [r[...].astype(F32) for r in refs[:EXPERTS]]
    packed = jnp.concatenate(parts, axis=0).astype(BF16)
    refs[EXPERTS][...] = jnp.dot(chosen_ref[...], packed, preferred_element_type=F32).astype(BF16)


def unpack(chosen, parts):
    width = parts[0].shape[1]
    return pl.pallas_call(
        unpack_kernel,
        out_shape=jax.ShapeDtypeStruct((chosen.shape[0], width), BF16),
        name="unpack",
    )(chosen, *parts)


def swap(value, axes, sizes):
    count = 1
    for size in sizes:
        count *= size
    return lax.ppermute(value, axes, [(i, i ^ (count - 1)) for i in range(count)])


def to_planes(blocks):
    moved = [blocks[0]]
    for k in range(1, EXPERTS):
        moved.append(lax.ppermute(blocks[k], "arch", [(i, i ^ k) for i in range(EXPERTS)]))
    return moved


def gathering(designs, archetype, w_gate, w_up, w_down, cotangent):
    plane = lax.axis_index("arch").astype(jnp.int32)
    far = lax.axis_index("far").astype(jnp.int32)
    core = lax.axis_index("core").astype(jnp.int32)
    width = designs.shape[1]
    share = width // 4
    packed = pack(plane[None], archetype, designs, cotangent)
    chosen = packed[2 * EXPERTS]
    groups = []
    for blocks in (packed[:EXPERTS], packed[EXPERTS : 2 * EXPERTS]):
        own = jnp.concatenate(to_planes(blocks), axis=0)
        near = swap(own, "half", (2,))
        across = swap(own, "far", (2,))
        corner = swap(own, ("far", "half"), (2, 2))
        groups.append([own, near, across, corner])
    xs, gs = groups
    act0, coef0, share_own, share_near = forward(xs[0], xs[1], w_gate, w_up, w_down, True)
    returned = swap(share_near, "half", (2,))
    act1, coef1 = forward(xs[2], xs[3], w_gate, w_up, w_down, False)
    outputs = unpack(chosen, to_planes(combine(share_own, returned)))
    own_gate, own_up, sib_gate, sib_up = backward(
        jnp.stack([far, core]), xs, gs, act0, coef0, act1, coef1, w_down, share
    )
    got_gate = swap(sib_gate, "core", (2,))
    got_up = swap(sib_up, "core", (2,))
    grad_gate = (own_gate.astype(F32) + got_gate.astype(F32)).astype(BF16)
    grad_up = (own_up.astype(F32) + got_up.astype(F32)).astype(BF16)
    return outputs, grad_gate, grad_up


def reducing(designs, archetype, w_gate, w_up, w_down, cotangent):
    width = designs.shape[1]
    owners = lax.axis_size("expert")
    sharers = owners // EXPERTS
    hidden_cols = w_gate.shape[1]
    labels = archetype[:, 0]
    onehot = (labels[:, None] == jnp.arange(EXPERTS, dtype=jnp.int32)[None, :]).astype(jnp.int32)
    ranks = jnp.cumsum(onehot, axis=0) - onehot
    target = labels * CAP + jnp.sum(ranks * onehot, axis=1)
    placer = (jnp.arange(EXPERTS * CAP, dtype=jnp.int32)[:, None] == target[None, :]).astype(BF16)
    received = []
    for rows in (designs, cotangent):
        packed = jnp.dot(placer, rows, preferred_element_type=F32).astype(BF16)
        send = jnp.repeat(packed.reshape(EXPERTS, CAP, width), sharers, axis=0)
        received.append(
            lax.all_to_all(send, "expert", split_axis=0, concat_axis=0, tiled=True).reshape(
                owners * CAP, width
            )
        )
    flat_x, flat_g = received
    gate = jnp.dot(flat_x, w_gate, preferred_element_type=F32)
    up = jnp.dot(flat_x, w_up, preferred_element_type=F32)
    act, slope = silu_parts(gate)
    hidden = (act * up).astype(BF16)
    partial_value = (
        jnp.dot(hidden, w_down, preferred_element_type=F32).astype(BF16).reshape(owners, CAP, width)
    )
    returned = lax.all_to_all(partial_value, "expert", split_axis=0, concat_axis=0, tiled=True)
    summed = jnp.sum(returned.astype(F32).reshape(EXPERTS, sharers, CAP, width), axis=1).reshape(
        EXPERTS * CAP, width
    )
    outputs = jnp.take(summed, target, axis=0).astype(BF16)
    d_hidden = contract_cols(flat_g, w_down)
    d_gate = (d_hidden * up * slope).astype(BF16)
    d_up = (d_hidden * act).astype(BF16)
    grads = jnp.concatenate([contract_rows(flat_x, d_gate), contract_rows(flat_x, d_up)], axis=1)
    mine = lax.psum_scatter(grads.astype(BF16), "dp", scatter_dimension=0, tiled=True)
    return outputs, mine[:, :hidden_cols], mine[:, hidden_cols:]


def solution(mesh):
    dp, owners = mesh.devices.shape
    if (dp, owners) == (4, 2 * EXPERTS):
        rows, cols = ("far", "core"), ("arch", "half")
        mesh = Mesh(mesh.devices.reshape(2, 2, EXPERTS, 2), rows + cols)
        body = gathering
    else:
        rows, cols = ("dp",), ("expert",)
        body = reducing
    tokens = P(rows + cols, None)
    return jax.shard_map(
        body,
        mesh=mesh,
        in_specs=(tokens, tokens, P(None, cols), P(None, cols), P(cols, None), tokens),
        out_specs=(tokens, P(rows, cols), P(rows, cols)),
        check_vma=False,
    )
```

time: 241 us -> 112 us (0.46)
  waiting for transfers between devices: 166 us -> 27 us
  Pallas kernels: 0 us -> 42 us
  matrix products: 25.7 us -> 0 us
  between operations: 14.2 us -> 0.76 us
  starting transfers between devices: 14.6 us -> 27.6 us
  other arithmetic: 12.9 us -> 5.25 us
    psum x1 -> x0, waiting for transfers between devices: 122 us -> none  [per_device(): lax.psum(jnp.concatenate([contract_rows(flat_x, d_gate), contract_rows(fl...]
    all_to_all x3 -> x0, waiting for transfers between devices: 43.8 us -> none  [the longest x1 17.4 us: per_device(): lax.all_to_all(partial_value, 'expert', split_axis=0, concat_axis=0, tile...]
    pallas_call x0 -> x6, Pallas kernels: none -> 42 us  [the longest x2 18.8 us: forward(): pl.pallas_call(functools.partial(forward_kernel, with_down), grid=(cols /...]
    ppermute x0 -> x18, starting transfers between devices: none -> 27.6 us  [the longest x9 17.6 us: to_planes(): lax.ppermute(blocks[k], 'arch', [(i, i ^ k) for i in range(EXPERTS)])]
    ppermute x0 -> x18, waiting for transfers between devices: none -> 27 us  [the longest x9 16.9 us: swap(): return lax.ppermute(value, axes, [(i, i ^ count - 1) for i in range(count)])]
    dot_general x8 -> x0, matrix products: 25.7 us -> none  [the longest x2 9 us: contract_rows(): lax.dot_general(left, right, (((0,), (0,)), ((), ())), preferred_element_...]
    all_to_all x3 -> x0, starting transfers between devices: 14.5 us -> none  [the longest x1 7.28 us: per_device(): lax.all_to_all(send_x, 'expert', split_axis=0, concat_axis=0, tiled=True)]
    concatenate x1 -> x0, other arithmetic: 7.8 us -> none  [per_device(): jnp.concatenate([contract_rows(flat_x, d_gate), contract_rows(flat_x, d_u...]
  transfers between devices with their start and end apart: 4 -> 18, of which waited for: 4 -> 6; matrix products, arithmetic and copies ran while one was open for 7% -> 4% of each run, Pallas kernels for 0% -> 20%
where the time goes in v1:
time: 112 us
  Pallas kernels  42 us (38%)
  starting transfers between devices  27.6 us (25%)
  waiting for transfers between devices  27 us (24%)
  local copies, waits for them, and re-layouts  8.9 us (8%)
  other arithmetic  5.25 us (5%)
    pallas_call x2, Pallas kernels, forward(): pl.pallas_call(functools.partial(forward_kernel, with_down), grid=(cols /...  18.8 us
    ppermute x9, starting transfers between devices, to_planes(): lax.ppermute(blocks[k], 'arch', [(i, i ^ k) for i in range(EXPERTS)])  17.6 us
    pallas_call x1, Pallas kernels, backward(): pl.pallas_call(backward_kernel, grid_spec=pltpu.PrefetchScalarGridSpec(nu...  16.9 us
    ppermute x9, waiting for transfers between devices, swap(): return lax.ppermute(value, axes, [(i, i ^ count - 1) for i in range(count)])  16.9 us
    ppermute x9, waiting for transfers between devices, to_planes(): lax.ppermute(blocks[k], 'arch', [(i, i ^ k) for i in range(EXPERTS)])  10.1 us
    ppermute x9, starting transfers between devices, swap(): return lax.ppermute(value, axes, [(i, i ^ count - 1) for i in range(count)])  10.1 us
    unnamed x25, local copies, waits for them, and re-layouts  8.88 us
    convert_element_type x1, other arithmetic, gathering(): grad_gate = (own_gate.astype(F32) + got_gate.astype(F32)).astype(BF16)  2.59 us
  transfers between devices with their start and end apart: 18, of which 6 were waited for; matrix products, arithmetic and copies ran while one was open for 4% of the time, Pallas kernels for 20%

profile of v1, /device:TPU:0, one launch (start us, length us, event | category | flops | bytes accessed | tf_op | source)
XLA Modules:
  0.0 111.6 jit_solution(5040298453547424245)
XLA Ops:
  0.6 1.4 %copy.9.kind_ref = s32[128,1]{1,0:T(8,128)} copy(s32[128,1]{0,1:T(1,128)} %param.7) | data formatting | bytes 1024 | tf_op args[1]
  2.0 2.5 %pack.1 = (bf16[40,1024]{1,0:T(8,128)(2,1)}, bf16[40,1024]{1,0:T(8,128)(2,1)}, bf16[40,1024]{1,0:T(8,128)(2,1)}, bf16[40,1024]{1,0:T(8,128)(2,1)}, bf16[40,1024]...) custom-call(s32[1]{0:T(128)} %bitcast.plane_ref, ...), custom_call_target="tpu_custom_call" | custom-call | tf_op jit(solution)/shard_map/pack/pallas_call | solution.py:57
  4.5 3.0 %collective-permute-start = (bf16[40,1024]{1,0:T(8,128)(2,1)}, bf16[40,1024]{1,0:T(8,128)(2,1)S(1)}, u32[]{:S(2)}, u32[]{:S(2)}) collective-permute-start(bf16[40,1024]{1,0:T(8,128)(2,1)} %get-tuple-element.28), channel_id=1, source_target_pairs={{0,2},{2,0},{4,6},{6,4},{1,3},{3,1},{5,7},{7,5},{8,10},{10,8},{12,... | collective-permute-start | bytes 245768 | tf_op jit(solution)/shard_map/ppermute | solution.py:240
  7.6 2.6 %collective-permute-start.1 = (bf16[40,1024]{1,0:T(8,128)(2,1)}, bf16[40,1024]{1,0:T(8,128)(2,1)S(1)}, u32[]{:S(2)}, u32[]{:S(2)}) collective-permute-start(bf16[40,1024]{1,0:T(8,128)(2,1)} %get-tuple-element.29), channel_id=1, source_target_pairs={{0,4},{2,6},{4,0},{6,2},{1,5},{3,7},{5,1},{7,3},{8,12},{10,14},{12... | collective-permute-start | bytes 245768 | tf_op jit(solution)/shard_map/ppermute | solution.py:240
  10.2 0.9 collective-permute-start.10
  11.1 3.5 %collective-permute-start.11 = (bf16[40,1024]{1,0:T(8,128)(2,1)}, bf16[40,1024]{1,0:T(8,128)(2,1)S(1)}, u32[]{:S(2)}, u32[]{:S(2)}) collective-permute-start(bf16[40,1024]{1,0:T(8,128)(2,1)} %get-tuple-element.39), channel_id=1, source_target_pairs={{0,4},{2,6},{4,0},{6,2},{1,5},{3,7},{5,1},{7,3},{8,12},{10,14},{12... | collective-permute-start | bytes 245768 | tf_op jit(solution)/shard_map/ppermute | solution.py:240
  16.4 1.5 %collective-permute-done.1 = bf16[40,1024]{1,0:T(8,128)(2,1)S(1)} collective-permute-done((bf16[40,1024]{1,0:T(8,128)(2,1)}, bf16[40,1024]{1,0:T(8,128)(2,1)S(1)}, u32[]{:S(2)}, u32[]{:S(2)}) %collective-permute-start.1) | collective-permute-done | bytes 81952 | tf_op jit(solution)/shard_map/ppermute | solution.py:240
  18.0 1.6 %collective-permute-start.3 = (bf16[160,1024]{1,0:T(8,128)(2,1)S(1)}, bf16[160,1024]{1,0:T(8,128)(2,1)S(1)}, u32[]{:S(2)}, u32[]{:S(2)}) collective-permute-start(bf16[160,1024]{1,0:T(8,128)(2,1)S(1)} %constant_dynamic-update-slice_fusion.xa_ref.refs_0_), channel_id=1, source_target_pairs={{0,1},{1,0},{2,3},{3,2},{4,5},{5,4},{6,7},{7,6},{8,9},{9,8},{10,11... | collective-permute-start | bytes 983048 | tf_op jit(solution)/shard_map/ppermute | solution.py:234
  19.6 1.5 %collective-permute-start.8 = (bf16[160,1024]{1,0:T(8,128)(2,1)S(1)}, bf16[160,1024]{1,0:T(8,128)(2,1)S(1)}, u32[]{:S(2)}, u32[]{:S(2)}) collective-permute-start(bf16[160,1024]{1,0:T(8,128)(2,1)S(1)} %constant_dynamic-update-slice_fusion.xa_ref.refs_0_), channel_id=1, source_target_pairs={{0,16},{16,0},{1,17},{17,1},{2,18},{18,2},{3,19},{19,3},{4,20},{20... | collective-permute-start | bytes 983048 | tf_op jit(solution)/shard_map/ppermute | solution.py:234
  21.5 2.5 %collective-permute-done.11 = bf16[40,1024]{1,0:T(8,128)(2,1)S(1)} collective-permute-done((bf16[40,1024]{1,0:T(8,128)(2,1)}, bf16[40,1024]{1,0:T(8,128)(2,1)S(1)}, u32[]{:S(2)}, u32[]{:S(2)}) %collective-permute-start.11) | collective-permute-done | bytes 81952 | tf_op jit(solution)/shard_map/ppermute | solution.py:240
  24.0 1.6 %collective-permute-start.13 = (bf16[160,1024]{1,0:T(8,128)(2,1)S(1)}, bf16[160,1024]{1,0:T(8,128)(2,1)S(1)}, u32[]{:S(2)}, u32[]{:S(2)}) collective-permute-start(bf16[160,1024]{1,0:T(8,128)(2,1)S(1)} %constant_dynamic-update-slice_fusion.4.refs_4_), channel_id=1, source_target_pairs={{0,1},{1,0},{2,3},{3,2},{4,5},{5,4},{6,7},{7,6},{8,9},{9,8},{10,11... | collective-permute-start | bytes 983048 | tf_op jit(solution)/shard_map/ppermute | solution.py:234
  25.6 1.5 %collective-permute-start.14 = (bf16[160,1024]{1,0:T(8,128)(2,1)S(1)}, bf16[160,1024]{1,0:T(8,128)(2,1)S(1)}, u32[]{:S(2)}, u32[]{:S(2)}) collective-permute-start(bf16[160,1024]{1,0:T(8,128)(2,1)S(1)} %constant_dynamic-update-slice_fusion.4.refs_4_), channel_id=1, source_target_pairs={{0,16},{16,0},{1,17},{17,1},{2,18},{18,2},{3,19},{19,3},{4,20},{20... | collective-permute-start | bytes 983048 | tf_op jit(solution)/shard_map/ppermute | solution.py:234
  27.1 3.1 %collective-permute-done.8.xa_ref.refs_2_ = bf16[160,1024]{1,0:T(8,128)(2,1)S(1)} collective-permute-done((bf16[160,1024]{1,0:T(8,128)(2,1)S(1)}, bf16[160,1024]{1,0:T(8,128)(2,1)S(1)}, u32[]{:S(2)}, u32[]{:S(2)}) %collective-permute-start.8) | collective-permute-done | bytes 327712 | tf_op jit(solution)/shard_map/ppermute | solution.py:234
  30.2 1.4 %collective-permute-start.15 = (bf16[160,1024]{1,0:T(8,128)(2,1)S(1)}, bf16[160,1024]{1,0:T(8,128)(2,1)S(1)}, u32[]{:S(2)}, u32[]{:S(2)}) collective-permute-start(bf16[160,1024]{1,0:T(8,128)(2,1)S(1)} %constant_dynamic-update-slice_fusion.4.refs_4_), channel_id=1, source_target_pairs={{0,17},{1,16},{16,1},{17,0},{2,19},{3,18},{18,3},{19,2},{4,21},{5,... | collective-permute-start | bytes 983048 | tf_op jit(solution)/shard_map/ppermute | solution.py:234
  31.6 5.6 %collective-permute-done.9.xb_ref.refs_3_ = bf16[160,1024]{1,0:T(8,128)(2,1)S(1)} collective-permute-done((bf16[160,1024]{1,0:T(8,128)(2,1)S(1)}, bf16[160,1024]{1,0:T(8,128)(2,1)S(1)}, u32[]{:S(2)}, u32[]{:S(2)}) %collective-permute-start.9) | collective-permute-done | bytes 327712 | tf_op jit(solution)/shard_map/ppermute | solution.py:234
  37.3 8.2 %forward.1 = (bf16[320,2048]{1,0:T(8,128)(2,1)S(1)}, bf16[320,2048]{1,0:T(8,128)(2,1)S(1)}) custom-call(bf16[160,1024]{1,0:T(8,128)(2,1)S(1)} %collective-permute-done.8.xa_ref.refs_2_, bf16[160,1024]{1,0:T(8,128)(2,1)S(1)} %collective-permute-done.9.xb_ref.refs_3_, bf16[1024,2048]{1,0:T(8,128)(2,1)} %wg_ref.3, bf16[1024,2048]{1,0:T(8,128)(2,1)} %wu_ref.3, ...), custom_call_target="tpu_custom_call" | custom-call | flops 2684354560 | bytes 11010048 | tf_op jit(solution)/shard_map/forward/pallas_call | solution.py:117
  45.5 1.1 copy-done.1
  46.5 1.1 copy-done.2
  47.6 10.6 %forward_down.1 = (bf16[320,2048]{1,0:T(8,128)(2,1)S(1)}, bf16[320,2048]{1,0:T(8,128)(2,1)S(1)}, bf16[160,1024]{1,0:T(8,128)(2,1)S(1)}, bf16[160,1024]{1,0:T(8,128)(2,1)S(1)}) custom-call(bf16[160,1024]{1,0:T(8,128)(2,1)S(1)} %constant_dynamic-update-slice_fusion.xa_ref.refs_0_, bf16[160,1024]{1,0:T(8,128)(2,1)S(1)} %collective-permute-done.3.xb_ref.refs_1_, ...), custom_call_target="tpu_custom_call" | custom-call | flops 4026531840 | bytes 15204352 | tf_op jit(solution)/shard_map/forward_down/pallas_call | solution.py:117
  58.3 1.1 copy-done.3
  59.3 1.1 copy-done.4
  60.4 16.9 %backward.1 = (bf16[256,2048]{1,0:T(8,128)(2,1)S(1)}, bf16[256,2048]{1,0:T(8,128)(2,1)S(1)}, bf16[256,2048]{1,0:T(8,128)(2,1)S(1)}, bf16[256,2048]{1,0:T(8,128)(2,1)}) custom-call(s32[2]{0:T(128)S(1)} %pad_add_fusion.where_ref, bf16[160,1024]{1,0:T(8,128)(2,1)S(1)} %constant_dynamic-update-slice_fusion.xa_ref.refs_0_, ...), custom_call_target="tpu_custom_call" | custom-call | flops 5368709120 | bytes 18874368 | tf_op jit(solution)/shard_map/backward/pallas_call | solution.py:177
  77.9 1.5 %collective-permute-start.4 = (bf16[160,1024]{1,0:T(8,128)(2,1)S(1)}, bf16[160,1024]{1,0:T(8,128)(2,1)S(1)}, u32[]{:S(2)}, u32[]{:S(2)}) collective-permute-start(bf16[160,1024]{1,0:T(8,128)(2,1)S(1)} %get-tuple-element.32), channel_id=1, source_target_pairs={{0,1},{1,0},{2,3},{3,2},{4,5},{5,4},{6,7},{7,6},{8,9},{9,8},{10,11... | collective-permute-start | bytes 983048 | tf_op jit(solution)/shard_map/ppermute | solution.py:234
  79.4 8.2 %collective-permute-done.4.theirs_ref = bf16[160,1024]{1,0:T(8,128)(2,1)S(1)} collective-permute-done((bf16[160,1024]{1,0:T(8,128)(2,1)S(1)}, bf16[160,1024]{1,0:T(8,128)(2,1)S(1)}, u32[]{:S(2)}, u32[]{:S(2)}) %collective-permute-start.4) | collective-permute-done | bytes 327712 | tf_op jit(solution)/shard_map/ppermute | solution.py:234
  88.3 1.8 %combine.1 = (bf16[40,1024]{1,0:T(8,128)(2,1)}, bf16[40,1024]{1,0:T(8,128)(2,1)}, bf16[40,1024]{1,0:T(8,128)(2,1)}, bf16[40,1024]{1,0:T(8,128)(2,1)}) custom-call(bf16[160,1024]{1,0:T(8,128)(2,1)} %copy-done, bf16[160,1024]{1,0:T(8,128)(2,1)} %copy-done.5), custom_call_target="tpu_custom_call" | custom-call | tf_op jit(solution)/shard_map/combine/pallas_call | solution.py:208
  90.1 4.3 %collective-permute-start.5 = (bf16[40,1024]{1,0:T(8,128)(2,1)}, bf16[40,1024]{1,0:T(8,128)(2,1)S(1)}, u32[]{:S(2)}, u32[]{:S(2)}) collective-permute-start(bf16[40,1024]{1,0:T(8,128)(2,1)} %get-tuple-element.34), channel_id=1, source_target_pairs={{0,2},{2,0},{4,6},{6,4},{1,3},{3,1},{5,7},{7,5},{8,10},{10,8},{12,... | collective-permute-start | bytes 245768 | tf_op jit(solution)/shard_map/ppermute | solution.py:240
  94.4 1.8 %collective-permute-start.6 = (bf16[40,1024]{1,0:T(8,128)(2,1)}, bf16[40,1024]{1,0:T(8,128)(2,1)S(1)}, u32[]{:S(2)}, u32[]{:S(2)}) collective-permute-start(bf16[40,1024]{1,0:T(8,128)(2,1)} %get-tuple-element.35), channel_id=1, source_target_pairs={{0,4},{2,6},{4,0},{6,2},{1,5},{3,7},{5,1},{7,3},{8,12},{10,14},{12... | collective-permute-start | bytes 245768 | tf_op jit(solution)/shard_map/ppermute | solution.py:240
  96.2 1.5 %collective-permute-start.7 = (bf16[40,1024]{1,0:T(8,128)(2,1)}, bf16[40,1024]{1,0:T(8,128)(2,1)S(1)}, u32[]{:S(2)}, u32[]{:S(2)}) collective-permute-start(bf16[40,1024]{1,0:T(8,128)(2,1)} %get-tuple-element.36), channel_id=1, source_target_pairs={{0,6},{2,4},{4,2},{6,0},{1,7},{3,5},{5,3},{7,1},{8,14},{10,12},{12... | collective-permute-start | bytes 245768 | tf_op jit(solution)/shard_map/ppermute | solution.py:240
  97.6 6.1 %collective-permute-done.6.refs_2_ = bf16[40,1024]{1,0:T(8,128)(2,1)S(1)} collective-permute-done((bf16[40,1024]{1,0:T(8,128)(2,1)}, bf16[40,1024]{1,0:T(8,128)(2,1)S(1)}, u32[]{:S(2)}, u32[]{:S(2)}) %collective-permute-start.6) | collective-permute-done | bytes 81952 | tf_op jit(solution)/shard_map/ppermute | solution.py:240
  104.4 2.0 %unpack.1 = bf16[128,1024]{1,0:T(8,128)(2,1)} custom-call(bf16[128,160]{1,0:T(8,128)(2,1)} %get-tuple-element.26.chosen_ref, bf16[40,1024]{1,0:T(8,128)(2,1)} %get-tuple-element.33.refs_0_, bf16[40,1024]{1,0:T(8,128)(2,1)} %copy-done.6, bf16[40,1024]{1,0:T(8,128)(2,1)} %copy-done.7, bf16[40,1024]{1,0:T(8,128)(2,1)} %copy-done.8), custom_call_target="tpu_custom_call" | custom-call | tf_op jit(solution)/shard_map/unpack/pallas_call | solution.py:223
  106.4 2.6 %add_convert_fusion.1 = bf16[256,2048]{1,0:T(8,128)(2,1)} fusion(bf16[256,2048]{1,0:T(8,128)(2,1)} %collective-permute-done.16, bf16[256,2048]{1,0:T(8,128)(2,1)S(1)} %get-tuple-element.45), kind=kLoop, calls=%fused_computation.1 | loop fusion | flops 2097152 | bytes 3145728 | tf_op jit(solution)/shard_map/convert_element_type | solution.py:269
  109.0 2.6 %add_convert_fusion = bf16[256,2048]{1,0:T(8,128)(2,1)} fusion(bf16[256,2048]{1,0:T(8,128)(2,1)} %collective-permute-done.17, bf16[256,2048]{1,0:T(8,128)(2,1)S(1)} %get-tuple-element.47), kind=kLoop, calls=%fused_computation | loop fusion | flops 2097152 | bytes 3145728 | tf_op jit(solution)/shard_map/convert_element_type | solution.py:270
  (40 shorter events, 4.3 us)
Async XLA Ops:
  4.5 11.9 %collective-permute-start = (bf16[40,1024]{1,0:T(8,128)(2,1)}, bf16[40,1024]{1,0:T(8,128)(2,1)S(1)}, u32[]{:S(2)}, u32[]{:S(2)}) collective-permute-start(bf16[40,1024]{1,0:T(8,128)(2,1)} %get-tuple-element.28), channel_id=1, source_target_pairs={{0,2},{2,0},{4,6},{6,4},{1,3},{3,1},{5,7},{7,5},{8,10},{10,8},{12,... | collective-permute-start | bytes 245768 | tf_op jit(solution)/shard_map/ppermute | solution.py:240
  7.6 10.4 %collective-permute-start.1 = (bf16[40,1024]{1,0:T(8,128)(2,1)}, bf16[40,1024]{1,0:T(8,128)(2,1)S(1)}, u32[]{:S(2)}, u32[]{:S(2)}) collective-permute-start(bf16[40,1024]{1,0:T(8,128)(2,1)} %get-tuple-element.29), channel_id=1, source_target_pairs={{0,4},{2,6},{4,0},{6,2},{1,5},{3,7},{5,1},{7,3},{8,12},{10,14},{12... | collective-permute-start | bytes 245768 | tf_op jit(solution)/shard_map/ppermute | solution.py:240
  10.2 7.8 %collective-permute-start.2 = (bf16[40,1024]{1,0:T(8,128)(2,1)}, bf16[40,1024]{1,0:T(8,128)(2,1)S(1)}, u32[]{:S(2)}, u32[]{:S(2)}) collective-permute-start(bf16[40,1024]{1,0:T(8,128)(2,1)} %get-tuple-element.30), channel_id=1, source_target_pairs={{0,6},{2,4},{4,2},{6,0},{1,7},{3,5},{5,3},{7,1},{8,14},{10,12},{12... | collective-permute-start | bytes 245768 | tf_op jit(solution)/shard_map/ppermute | solution.py:240
  10.2 10.9 %collective-permute-start.10 = (bf16[40,1024]{1,0:T(8,128)(2,1)}, bf16[40,1024]{1,0:T(8,128)(2,1)S(1)}, u32[]{:S(2)}, u32[]{:S(2)}) collective-permute-start(bf16[40,1024]{1,0:T(8,128)(2,1)} %get-tuple-element.38), channel_id=1, source_target_pairs={{0,2},{2,0},{4,6},{6,4},{1,3},{3,1},{5,7},{7,5},{8,10},{10,8},{12,... | collective-permute-start | bytes 245768 | tf_op jit(solution)/shard_map/ppermute | solution.py:240
  11.1 12.9 %collective-permute-start.11 = (bf16[40,1024]{1,0:T(8,128)(2,1)}, bf16[40,1024]{1,0:T(8,128)(2,1)S(1)}, u32[]{:S(2)}, u32[]{:S(2)}) collective-permute-start(bf16[40,1024]{1,0:T(8,128)(2,1)} %get-tuple-element.39), channel_id=1, source_target_pairs={{0,4},{2,6},{4,0},{6,2},{1,5},{3,7},{5,1},{7,3},{8,12},{10,14},{12... | collective-permute-start | bytes 245768 | tf_op jit(solution)/shard_map/ppermute | solution.py:240
  16.4 7.6 %collective-permute-start.12 = (bf16[40,1024]{1,0:T(8,128)(2,1)}, bf16[40,1024]{1,0:T(8,128)(2,1)S(1)}, u32[]{:S(2)}, u32[]{:S(2)}) collective-permute-start(bf16[40,1024]{1,0:T(8,128)(2,1)} %get-tuple-element.40), channel_id=1, source_target_pairs={{0,6},{2,4},{4,2},{6,0},{1,7},{3,5},{5,3},{7,1},{8,14},{10,12},{12... | collective-permute-start | bytes 245768 | tf_op jit(solution)/shard_map/ppermute | solution.py:240
  18.0 29.7 %collective-permute-start.3 = (bf16[160,1024]{1,0:T(8,128)(2,1)S(1)}, bf16[160,1024]{1,0:T(8,128)(2,1)S(1)}, u32[]{:S(2)}, u32[]{:S(2)}) collective-permute-start(bf16[160,1024]{1,0:T(8,128)(2,1)S(1)} %constant_dynamic-update-slice_fusion.xa_ref.refs_0_), channel_id=1, source_target_pairs={{0,1},{1,0},{2,3},{3,2},{4,5},{5,4},{6,7},{7,6},{8,9},{9,8},{10,11... | collective-permute-start | bytes 983048 | tf_op jit(solution)/shard_map/ppermute | solution.py:234
  19.6 10.6 %collective-permute-start.8 = (bf16[160,1024]{1,0:T(8,128)(2,1)S(1)}, bf16[160,1024]{1,0:T(8,128)(2,1)S(1)}, u32[]{:S(2)}, u32[]{:S(2)}) collective-permute-start(bf16[160,1024]{1,0:T(8,128)(2,1)S(1)} %constant_dynamic-update-slice_fusion.xa_ref.refs_0_), channel_id=1, source_target_pairs={{0,16},{16,0},{1,17},{17,1},{2,18},{18,2},{3,19},{19,3},{4,20},{20... | collective-permute-start | bytes 983048 | tf_op jit(solution)/shard_map/ppermute | solution.py:234
  21.0 16.2 %collective-permute-start.9 = (bf16[160,1024]{1,0:T(8,128)(2,1)S(1)}, bf16[160,1024]{1,0:T(8,128)(2,1)S(1)}, u32[]{:S(2)}, u32[]{:S(2)}) collective-permute-start(bf16[160,1024]{1,0:T(8,128)(2,1)S(1)} %constant_dynamic-update-slice_fusion.xa_ref.refs_0_), channel_id=1, source_target_pairs={{0,17},{1,16},{16,1},{17,0},{2,19},{3,18},{18,3},{19,2},{4,21},{5,... | collective-permute-start | bytes 983048 | tf_op jit(solution)/shard_map/ppermute | solution.py:234
  24.0 36.4 %collective-permute-start.13 = (bf16[160,1024]{1,0:T(8,128)(2,1)S(1)}, bf16[160,1024]{1,0:T(8,128)(2,1)S(1)}, u32[]{:S(2)}, u32[]{:S(2)}) collective-permute-start(bf16[160,1024]{1,0:T(8,128)(2,1)S(1)} %constant_dynamic-update-slice_fusion.4.refs_4_), channel_id=1, source_target_pairs={{0,1},{1,0},{2,3},{3,2},{4,5},{5,4},{6,7},{7,6},{8,9},{9,8},{10,11... | collective-permute-start | bytes 983048 | tf_op jit(solution)/shard_map/ppermute | solution.py:234
  25.6 34.8 %collective-permute-start.14 = (bf16[160,1024]{1,0:T(8,128)(2,1)S(1)}, bf16[160,1024]{1,0:T(8,128)(2,1)S(1)}, u32[]{:S(2)}, u32[]{:S(2)}) collective-permute-start(bf16[160,1024]{1,0:T(8,128)(2,1)S(1)} %constant_dynamic-update-slice_fusion.4.refs_4_), channel_id=1, source_target_pairs={{0,16},{16,0},{1,17},{17,1},{2,18},{18,2},{3,19},{19,3},{4,20},{20... | collective-permute-start | bytes 983048 | tf_op jit(solution)/shard_map/ppermute | solution.py:234
  30.2 30.2 %collective-permute-start.15 = (bf16[160,1024]{1,0:T(8,128)(2,1)S(1)}, bf16[160,1024]{1,0:T(8,128)(2,1)S(1)}, u32[]{:S(2)}, u32[]{:S(2)}) collective-permute-start(bf16[160,1024]{1,0:T(8,128)(2,1)S(1)} %constant_dynamic-update-slice_fusion.4.refs_4_), channel_id=1, source_target_pairs={{0,17},{1,16},{16,1},{17,0},{2,19},{3,18},{18,3},{19,2},{4,21},{5,... | collective-permute-start | bytes 983048 | tf_op jit(solution)/shard_map/ppermute | solution.py:234
  45.5 1.1 copy-start.1
  46.5 1.1 copy-start.2
  58.2 1.1 copy-start.3
  59.3 1.1 copy-start.4
  60.4 17.0 %copy-start = (bf16[160,1024]{1,0:T(8,128)(2,1)}, bf16[160,1024]{1,0:T(8,128)(2,1)S(1)}, u32[]{:S(2)}) copy-start(bf16[160,1024]{1,0:T(8,128)(2,1)S(1)} %get-tuple-element.31.mine_ref) | copy-start | bytes 983044
  77.4 29.0 %collective-permute-start.16 = (bf16[256,2048]{1,0:T(8,128)(2,1)S(1)}, bf16[256,2048]{1,0:T(8,128)(2,1)}, u32[]{:S(2)}, u32[]{:S(2)}) collective-permute-start(bf16[256,2048]{1,0:T(8,128)(2,1)S(1)} %get-tuple-element.46), channel_id=1, source_target_pairs={{0,8},{8,0},{1,9},{9,1},{2,10},{10,2},{3,11},{11,3},{4,12},{12,4},... | collective-permute-start | bytes 3145736 | tf_op jit(solution)/shard_map/ppermute | solution.py:234
  77.4 31.6 %collective-permute-start.17 = (bf16[256,2048]{1,0:T(8,128)(2,1)}, bf16[256,2048]{1,0:T(8,128)(2,1)}, u32[]{:S(2)}, u32[]{:S(2)}) collective-permute-start(bf16[256,2048]{1,0:T(8,128)(2,1)} %get-tuple-element.48), channel_id=1, source_target_pairs={{0,8},{8,0},{1,9},{9,1},{2,10},{10,2},{3,11},{11,3},{4,12},{12,4},... | collective-permute-start | bytes 3145736 | tf_op jit(solution)/shard_map/ppermute | solution.py:234
  77.9 9.7 %collective-permute-start.4 = (bf16[160,1024]{1,0:T(8,128)(2,1)S(1)}, bf16[160,1024]{1,0:T(8,128)(2,1)S(1)}, u32[]{:S(2)}, u32[]{:S(2)}) collective-permute-start(bf16[160,1024]{1,0:T(8,128)(2,1)S(1)} %get-tuple-element.32), channel_id=1, source_target_pairs={{0,1},{1,0},{2,3},{3,2},{4,5},{5,4},{6,7},{7,6},{8,9},{9,8},{10,11... | collective-permute-start | bytes 983048 | tf_op jit(solution)/shard_map/ppermute | solution.py:234
  87.6 0.7 copy-start.5
  90.1 7.5 %collective-permute-start.5 = (bf16[40,1024]{1,0:T(8,128)(2,1)}, bf16[40,1024]{1,0:T(8,128)(2,1)S(1)}, u32[]{:S(2)}, u32[]{:S(2)}) collective-permute-start(bf16[40,1024]{1,0:T(8,128)(2,1)} %get-tuple-element.34), channel_id=1, source_target_pairs={{0,2},{2,0},{4,6},{6,4},{1,3},{3,1},{5,7},{7,5},{8,10},{10,8},{12,... | collective-permute-start | bytes 245768 | tf_op jit(solution)/shard_map/ppermute | solution.py:240
  94.4 9.4 %collective-permute-start.6 = (bf16[40,1024]{1,0:T(8,128)(2,1)}, bf16[40,1024]{1,0:T(8,128)(2,1)S(1)}, u32[]{:S(2)}, u32[]{:S(2)}) collective-permute-start(bf16[40,1024]{1,0:T(8,128)(2,1)} %get-tuple-element.35), channel_id=1, source_target_pairs={{0,4},{2,6},{4,0},{6,2},{1,5},{3,7},{5,1},{7,3},{8,12},{10,14},{12... | collective-permute-start | bytes 245768 | tf_op jit(solution)/shard_map/ppermute | solution.py:240
  96.2 7.6 %collective-permute-start.7 = (bf16[40,1024]{1,0:T(8,128)(2,1)}, bf16[40,1024]{1,0:T(8,128)(2,1)S(1)}, u32[]{:S(2)}, u32[]{:S(2)}) collective-permute-start(bf16[40,1024]{1,0:T(8,128)(2,1)} %get-tuple-element.36), channel_id=1, source_target_pairs={{0,6},{2,4},{4,2},{6,0},{1,7},{3,5},{5,3},{7,1},{8,14},{10,12},{12... | collective-permute-start | bytes 245768 | tf_op jit(solution)/shard_map/ppermute | solution.py:240
  97.6 6.2 %copy-start.6 = (bf16[40,1024]{1,0:T(8,128)(2,1)}, bf16[40,1024]{1,0:T(8,128)(2,1)S(1)}, u32[]{:S(2)}) copy-start(bf16[40,1024]{1,0:T(8,128)(2,1)S(1)} %collective-permute-done.5.refs_1_) | copy-start | bytes 245764
  103.8 0.6 copy-start.7
  103.8 0.6 copy-start.8

commit v2 on v0

v2 whole, which is shorter than its diff:
```python
import functools

import jax
import jax.numpy as jnp
from jax import lax
from jax.experimental import pallas as pl
from jax.experimental.pallas import tpu as pltpu
from jax.sharding import Mesh
from jax.sharding import PartitionSpec as P

EXPERTS = 4
CAP = 36
BLOCK = 512
STRIP = 256
VMEM_LIMIT = 24 * 1024 * 1024
F32 = jnp.float32
BF16 = jnp.bfloat16


def silu_parts(gate):
    sigma = 0.5 * jnp.tanh(0.5 * gate) + 0.5
    return (gate * sigma, sigma * (1.0 + gate * (1.0 - sigma)))


def contract_rows(left, right):
    return lax.dot_general(left, right, (((0,), (0,)), ((), ())), preferred_element_type=F32)


def contract_cols(left, right):
    return lax.dot_general(left, right, (((1,), (1,)), ((), ())), preferred_element_type=F32)


def stacked(values):
    return jnp.concatenate([v.astype(F32) for v in values], axis=0).astype(BF16)


def pack_kernel(plane_ref, kind_ref, x_ref, g_ref, placer_ref, *outs):
    tokens = kind_ref.shape[1]
    key = kind_ref[...] ^ plane_ref[0]
    onehot = (key == lax.broadcasted_iota(jnp.int32, (8, tokens), 0)).astype(F32)
    before = lax.broadcasted_iota(jnp.int32, (tokens, tokens), 0) < lax.broadcasted_iota(
        jnp.int32, (tokens, tokens), 1
    )
    ranks = jnp.dot(onehot.astype(BF16), before.astype(BF16), preferred_element_type=F32)
    rank = jnp.sum(ranks * onehot, axis=0, keepdims=True).astype(jnp.int32)
    place = key * CAP + rank
    slots = EXPERTS * CAP
    placer = (place == lax.broadcasted_iota(jnp.int32, (slots, tokens), 0)).astype(F32)
    placer_ref[...] = placer.astype(BF16)
    placer = placer.astype(BF16)
    packed_x = jnp.dot(placer, x_ref[...], preferred_element_type=F32)
    packed_g = jnp.dot(placer, g_ref[...], preferred_element_type=F32)
    for k in range(EXPERTS):
        rows = slice(k * CAP, (k + 1) * CAP)
        outs[k][...] = jnp.concatenate([packed_x[rows], packed_g[rows]], axis=0).astype(BF16)


def pack(plane, kind, x, g):
    tokens, width = x.shape
    return pl.pallas_call(
        pack_kernel,
        out_shape=[jax.ShapeDtypeStruct((EXPERTS * CAP, tokens), BF16)]
        + [jax.ShapeDtypeStruct((2 * CAP, width), BF16)] * EXPERTS,
        in_specs=[pl.BlockSpec(memory_space=pltpu.SMEM)] + [pl.BlockSpec(memory_space=pltpu.VMEM)] * 3,
        name="pack",
    )(plane, kind, x, g)


def split_kernel(*refs):
    blocks = [r[...].astype(F32) for r in refs[:EXPERTS]]
    refs[EXPERTS][...] = jnp.concatenate([b[:CAP] for b in blocks], axis=0).astype(BF16)
    refs[EXPERTS + 1][...] = jnp.concatenate([b[CAP:] for b in blocks], axis=0).astype(BF16)


def split(blocks):
    width = blocks[0].shape[1]
    return pl.pallas_call(
        split_kernel,
        out_shape=[jax.ShapeDtypeStruct((EXPERTS * CAP, width), BF16)] * 2,
        name="split",
    )(*blocks)


def slopes(x, g, wg, wu, wd):
    gate = jnp.dot(x, wg, preferred_element_type=F32)
    up = jnp.dot(x, wu, preferred_element_type=F32)
    d_hidden = contract_cols(g, wd)
    act, slope = silu_parts(gate)
    d_gate = (d_hidden * (up * slope)).astype(BF16)
    d_up = (d_hidden * act).astype(BF16)
    return (act * up).astype(BF16), d_gate, d_up


def chunk_kernel(n, *refs):
    xs, gs = refs[:n], refs[n : 2 * n]
    wg_ref, wu_ref, wd_ref, dg_ref, du_ref = refs[2 * n : 2 * n + 5]
    shares = refs[2 * n + 5 : 2 * n + 5 + EXPERTS]
    x_ref, g_ref, acc_ref = refs[2 * n + 5 + EXPERTS :]
    part = xs[0].shape[0]
    step = pl.program_id(0)

    @pl.when(step == 0)
    def _():
        for i in range(n):
            x_ref[i * part : (i + 1) * part, :] = xs[i][...]
            g_ref[i * part : (i + 1) * part, :] = gs[i][...]
        acc_ref[...] = jnp.zeros_like(acc_ref)

    x, g = x_ref[...], g_ref[...]
    total = acc_ref[...]
    for first in range(0, BLOCK, STRIP):
        cols = slice(first, first + STRIP)
        hidden, d_gate, d_up = slopes(x, g, wg_ref[:, cols], wu_ref[:, cols], wd_ref[cols, :])
        dg_ref[:, cols] = d_gate
        du_ref[:, cols] = d_up
        total += jnp.dot(hidden[:part], wd_ref[cols, :], preferred_element_type=F32)
    acc_ref[...] = total

    @pl.when(step == pl.num_programs(0) - 1)
    def _():
        for k in range(EXPERTS):
            shares[k][...] = total[k * CAP : (k + 1) * CAP].astype(BF16)


def chunk(xs, gs, wg, wu, wd):
    n = len(xs)
    part, width = xs[0].shape
    cols = wg.shape[1]
    rows = n * part
    whole = pl.BlockSpec((part, width), lambda j: (0, 0))
    wide = pl.BlockSpec((rows, BLOCK), lambda j: (0, j))
    deep = pl.BlockSpec((width, BLOCK), lambda j: (0, j))
    return pl.pallas_call(
        functools.partial(chunk_kernel, n),
        grid=(cols // BLOCK,),
        in_specs=[whole] * (2 * n) + [deep, deep, pl.BlockSpec((BLOCK, width), lambda j: (j, 0))],
        out_specs=[wide, wide] + [pl.BlockSpec((CAP, width), lambda j: (0, 0))] * EXPERTS,
        out_shape=[jax.ShapeDtypeStruct((rows, cols), BF16)] * 2
        + [jax.ShapeDtypeStruct((CAP, width), BF16)] * EXPERTS,
        scratch_shapes=[pltpu.VMEM((rows, width), BF16)] * 2 + [pltpu.VMEM((part, width), F32)],
        compiler_params=pltpu.CompilerParams(vmem_limit_bytes=VMEM_LIMIT),
        cost_estimate=pl.CostEstimate(
            flops=2 * (3 * rows + part) * width * cols,
            bytes_accessed=6 * width * cols + 4 * rows * cols,
            transcendentals=rows * cols,
        ),
        name="chunk",
    )(*xs, *gs, wg, wu, wd)


def grads_kernel(where_ref, *refs):
    own_x, sib_x = refs[0:4], refs[4:8]
    x_ref, g_ref, dg0, du0, dg1, du1, wg_ref, wu_ref, wd_ref, own_ref, sib_ref = refs[8:19]
    xt_ref, dg_ref, du_ref = refs[19:]
    part = x_ref.shape[0]
    share = own_ref.shape[0] // 2

    @pl.when(pl.program_id(0) == 0)
    def _():
        for first, blocks in ((0, own_x), (share, sib_x)):
            whole = jnp.concatenate([b[...].astype(F32) for b in blocks], axis=0)
            xt_ref[first : first + share, :] = whole.T.astype(BF16)

    _, d_gate, d_up = slopes(x_ref[...], g_ref[...], wg_ref[...], wu_ref[...], wd_ref[...])
    for whole, parts in ((dg_ref, (dg0[...], dg1[...], d_gate)), (du_ref, (du0[...], du1[...], d_up))):
        first = 0
        for value in parts:
            whole[first : first + value.shape[0], :] = value
            first += value.shape[0]
    for row, whole in ((0, dg_ref), (share, du_ref)):
        total = jnp.dot(xt_ref[...], whole[...], preferred_element_type=F32).astype(BF16)
        own_ref[row : row + share, :] = total[:share]
        sib_ref[row : row + share, :] = total[share:]


def grads(where, xs, g, dg0, du0, dg1, du1, wg, wu, wd, share, first, cols):
    part, width = xs[0].shape
    rows = 4 * part
    base = first // STRIP
    whole = pl.BlockSpec((part, width), lambda j, w: (0, 0))
    one = pl.BlockSpec((part, STRIP), lambda j, w: (0, base + j))
    two = pl.BlockSpec((2 * part, STRIP), lambda j, w: (0, base + j))
    deep = pl.BlockSpec((width, STRIP), lambda j, w: (0, base + j))
    out = pl.BlockSpec((2 * share, STRIP), lambda j, w: (0, j))
    return pl.pallas_call(
        grads_kernel,
        grid_spec=pltpu.PrefetchScalarGridSpec(
            num_scalar_prefetch=1,
            grid=(cols // STRIP,),
            in_specs=[pl.BlockSpec((part, share), lambda j, w: (0, w[0]))] * 4
            + [pl.BlockSpec((part, share), lambda j, w: (0, w[1]))] * 4
            + [whole, whole, one, one, two, two, deep, deep]
            + [pl.BlockSpec((STRIP, width), lambda j, w: (base + j, 0))],
            out_specs=[out, out],
            scratch_shapes=[pltpu.VMEM((2 * share, rows), BF16)] + [pltpu.VMEM((rows, STRIP), BF16)] * 2,
        ),
        out_shape=[jax.ShapeDtypeStruct((2 * share, cols), BF16)] * 2,
        compiler_params=pltpu.CompilerParams(vmem_limit_bytes=VMEM_LIMIT),
        cost_estimate=pl.CostEstimate(
            flops=2 * cols * (3 * part * width + 4 * rows * share),
            bytes_accessed=6 * width * cols + 4 * rows * cols + 8 * share * cols,
            transcendentals=part * cols,
        ),
        name="grads",
    )(where, *xs, *xs, xs[3], g, dg0, du0, dg1, du1, wg, wu, wd)


def finish_kernel(*refs):
    gate_ref, up_ref = refs[8:]
    half = refs[0].shape[1]
    for i in range(2):
        cols = slice(i * half, (i + 1) * half)
        own_gate, own_up, got_gate, got_up = [r[...].astype(F32) for r in refs[4 * i : 4 * i + 4]]
        gate_ref[:, cols] = (own_gate + got_gate).astype(BF16)
        up_ref[:, cols] = (own_up + got_up).astype(BF16)


def finish(own0, got0, own1, got1):
    share, half = own0.shape[0] // 2, own0.shape[1]
    steps = 4
    lines = share // steps
    upper = pl.BlockSpec((lines, half), lambda i: (i, 0))
    lower = pl.BlockSpec((lines, half), lambda i: (i + steps, 0))
    return pl.pallas_call(
        finish_kernel,
        grid=(steps,),
        in_specs=[upper, lower] * 4,
        out_specs=[pl.BlockSpec((lines, 2 * half), lambda i: (i, 0))] * 2,
        out_shape=[jax.ShapeDtypeStruct((share, 2 * half), BF16)] * 2,
        name="finish",
    )(own0, own0, got0, got0, own1, own1, got1, got1)


def unpack_kernel(placer_ref, *refs):
    mine = stacked([r[...] for r in refs[:EXPERTS]])
    theirs = stacked([r[...] for r in refs[EXPERTS : 2 * EXPERTS]])
    chosen = placer_ref[...].astype(F32).T.astype(BF16)
    total = jnp.dot(chosen, mine, preferred_element_type=F32)
    total += jnp.dot(chosen, theirs, preferred_element_type=F32)
    refs[2 * EXPERTS][...] = total.astype(BF16)


def unpack(placer, mine, theirs):
    width = mine[0].shape[1]
    return pl.pallas_call(
        unpack_kernel,
        out_shape=jax.ShapeDtypeStruct((placer.shape[1], width), BF16),
        name="unpack",
    )(placer, *mine, *theirs)


def swap(value, axis):
    return lax.ppermute(value, axis, [(0, 1), (1, 0)])


def across_planes(value, k):
    return lax.ppermute(value, "arch", [(i, i ^ k) for i in range(EXPERTS)])


def across_planes_and_halves(value, k):
    return lax.ppermute(value, ("arch", "half"), [(i, i ^ (2 * k + 1)) for i in range(2 * EXPERTS)])


def gathering(designs, archetype, w_gate, w_up, w_down, cotangent):
    plane = lax.axis_index("arch").astype(jnp.int32)
    far = lax.axis_index("far").astype(jnp.int32)
    core = lax.axis_index("core").astype(jnp.int32)
    tokens, width = designs.shape
    cols = w_gate.shape[1]
    share = width // 4
    weights = (w_gate, w_up, w_down)
    placer, *blocks = pack(plane[None], archetype.reshape(1, tokens), designs, cotangent)
    moved = {k: across_planes(blocks[k], k) for k in (3, 2, 1)}
    x_own, g_own = split([blocks[0], moved[1], moved[2], moved[3]])
    x_near = swap(x_own, "half")
    g_far = swap(g_own, "far")
    x_far = swap(x_own, "far")
    g_near = swap(g_own, "half")
    x_corner = swap(x_near, "far")
    g_corner = swap(g_far, "half")
    dg0, du0, *shares = chunk([x_own], [g_own], *weights)
    mine = [shares[0]] + [across_planes(shares[k], k) for k in range(1, EXPERTS)]
    dg1, du1, *shares = chunk([x_near, x_far], [g_near, g_far], *weights)
    theirs = [across_planes_and_halves(shares[k], k) for k in range(EXPERTS)]
    where = jnp.stack([2 * far + core, 2 * far + 1 - core])
    xs = [x_own, x_near, x_far, x_corner]
    half = cols // 2
    where, *mine = lax.optimization_barrier((where, *mine))
    own0, sib0 = grads(where, xs, g_corner, dg0, du0, dg1, du1, *weights, share, 0, half)
    got0 = swap(sib0, "core")
    own1, sib1 = grads(where, xs, g_corner, dg0, du0, dg1, du1, *weights, share, half, half)
    got1 = swap(sib1, "core")
    grad_gate, grad_up = finish(own0, got0, own1, got1)
    return unpack(placer, mine, theirs), grad_gate, grad_up


def reducing(designs, archetype, w_gate, w_up, w_down, cotangent):
    width = designs.shape[1]
    owners = lax.axis_size("expert")
    sharers = owners // EXPERTS
    hidden_cols = w_gate.shape[1]
    labels = archetype[:, 0]
    onehot = (labels[:, None] == jnp.arange(EXPERTS, dtype=jnp.int32)[None, :]).astype(jnp.int32)
    ranks = jnp.cumsum(onehot, axis=0) - onehot
    target = labels * CAP + jnp.sum(ranks * onehot, axis=1)
    placer = (jnp.arange(EXPERTS * CAP, dtype=jnp.int32)[:, None] == target[None, :]).astype(BF16)
    received = []
    for rows in (designs, cotangent):
        packed = jnp.dot(placer, rows, preferred_element_type=F32).astype(BF16)
        send = jnp.repeat(packed.reshape(EXPERTS, CAP, width), sharers, axis=0)
        received.append(
            lax.all_to_all(send, "expert", split_axis=0, concat_axis=0, tiled=True).reshape(
                owners * CAP, width
            )
        )
    flat_x, flat_g = received
    gate = jnp.dot(flat_x, w_gate, preferred_element_type=F32)
    up = jnp.dot(flat_x, w_up, preferred_element_type=F32)
    act, slope = silu_parts(gate)
    hidden = (act * up).astype(BF16)
    partial_value = (
        jnp.dot(hidden, w_down, preferred_element_type=F32).astype(BF16).reshape(owners, CAP, width)
    )
    returned = lax.all_to_all(partial_value, "expert", split_axis=0, concat_axis=0, tiled=True)
    summed = jnp.sum(returned.astype(F32).reshape(EXPERTS, sharers, CAP, width), axis=1).reshape(
        EXPERTS * CAP, width
    )
    outputs = jnp.take(summed, target, axis=0).astype(BF16)
    d_hidden = contract_cols(flat_g, w_down)
    d_gate = (d_hidden * up * slope).astype(BF16)
    d_up = (d_hidden * act).astype(BF16)
    grads = jnp.concatenate([contract_rows(flat_x, d_gate), contract_rows(flat_x, d_up)], axis=1)
    mine = lax.psum_scatter(grads.astype(BF16), "dp", scatter_dimension=0, tiled=True)
    return outputs, mine[:, :hidden_cols], mine[:, hidden_cols:]


def solution(mesh):
    dp, owners = mesh.devices.shape
    if (dp, owners) == (4, 2 * EXPERTS):
        rows, cols = ("far", "core"), ("arch", "half")
        mesh = Mesh(mesh.devices.reshape(2, 2, EXPERTS, 2), rows + cols)
        body = gathering
    else:
        rows, cols = ("dp",), ("expert",)
        body = reducing
    tokens = P(rows + cols, None)
    return jax.shard_map(
        body,
        mesh=mesh,
        in_specs=(tokens, tokens, P(None, cols), P(None, cols), P(cols, None), tokens),
        out_specs=(tokens, P(rows, cols), P(rows, cols)),
        check_vma=False,
    )
```

time: 241 us -> 118 us (0.49)
  waiting for transfers between devices: 166 us -> 33.5 us
  Pallas kernels: 0 us -> 37.7 us
  matrix products: 25.7 us -> 0 us
  between operations: 14.2 us -> 0.8 us
  other arithmetic: 12.9 us -> 0.07 us
  local copies, waits for them, and re-layouts: 7.18 us -> 20 us
  starting transfers between devices: 14.6 us -> 25.7 us
    psum x1 -> x0, waiting for transfers between devices: 122 us -> none  [per_device(): lax.psum(jnp.concatenate([contract_rows(flat_x, d_gate), contract_rows(fl...]
    all_to_all x3 -> x0, waiting for transfers between devices: 43.8 us -> none  [the longest x1 17.4 us: per_device(): lax.all_to_all(partial_value, 'expert', split_axis=0, concat_axis=0, tile...]
    pallas_call x0 -> x8, Pallas kernels: none -> 37.7 us  [the longest x2 14.4 us: grads(): pl.pallas_call(grads_kernel, grid_spec=pltpu.PrefetchScalarGridSpec(num_s...]
    ppermute x0 -> x18, waiting for transfers between devices: none -> 33.5 us  [the longest x6 23.4 us: across_planes(): return lax.ppermute(value, 'arch', [(i, i ^ k) for i in range(EXPERTS)])]
    dot_general x8 -> x0, matrix products: 25.7 us -> none  [the longest x2 9 us: contract_rows(): lax.dot_general(left, right, (((0,), (0,)), ((), ())), preferred_element_...]
    ppermute x0 -> x18, starting transfers between devices: none -> 25.7 us  [the longest x6 13.3 us: across_planes(): return lax.ppermute(value, 'arch', [(i, i ^ k) for i in range(EXPERTS)])]
    unnamed x14 -> x48, local copies, waits for them, and re-layouts: 1.68 us -> 20 us
    all_to_all x3 -> x0, starting transfers between devices: 14.5 us -> none  [the longest x1 7.28 us: per_device(): lax.all_to_all(send_x, 'expert', split_axis=0, concat_axis=0, tiled=True)]
  transfers between devices with their start and end apart: 4 -> 18, of which waited for: 4 -> 7; matrix products, arithmetic and copies ran while one was open for 7% -> 0% of each run, Pallas kernels for 0% -> 19%
where the time goes in v2:
time: 118 us
  Pallas kernels  37.7 us (32%)
  waiting for transfers between devices  33.5 us (28%)
  starting transfers between devices  25.7 us (22%)
  local copies, waits for them, and re-layouts  20 us (17%)
    ppermute x6, waiting for transfers between devices, across_planes(): return lax.ppermute(value, 'arch', [(i, i ^ k) for i in range(EXPERTS)])  23.4 us
    unnamed x48, local copies, waits for them, and re-layouts  20 us
    pallas_call x2, Pallas kernels, grads(): pl.pallas_call(grads_kernel, grid_spec=pltpu.PrefetchScalarGridSpec(num_s...  14.4 us
    ppermute x6, starting transfers between devices, across_planes(): return lax.ppermute(value, 'arch', [(i, i ^ k) for i in range(EXPERTS)])  13.3 us
    pallas_call x2, Pallas kernels, chunk(): pl.pallas_call(functools.partial(chunk_kernel, n), grid=(cols // BLOCK,),...  12.6 us
    ppermute x4, waiting for transfers between devices, across_planes_and_halves(): lax.ppermute(value, ('arch', 'half'), [(i, i ^ 2 * k + 1) for i in range(...  10.1 us
    ppermute x8, starting transfers between devices, swap(): return lax.ppermute(value, axis, [(0, 1), (1, 0)])  7.57 us
    ppermute x4, starting transfers between devices, across_planes_and_halves(): lax.ppermute(value, ('arch', 'half'), [(i, i ^ 2 * k + 1) for i in range(...  4.76 us
  transfers between devices with their start and end apart: 18, of which 7 were waited for; matrix products, arithmetic and copies ran while one was open for 0% of the time, Pallas kernels for 19%

profile of v2, /device:TPU:0, one launch (start us, length us, event | category | flops | bytes accessed | tf_op | source)
XLA Modules:
  0.0 117.7 jit_solution(6379427806236506813)
XLA Ops:
  0.6 2.3 %pack.1 = (bf16[144,128]{1,0:T(8,128)(2,1)}, bf16[72,1024]{1,0:T(8,128)(2,1)}, bf16[72,1024]{1,0:T(8,128)(2,1)}, bf16[72,1024]{1,0:T(8,128)(2,1)}, bf16[72,1024]{1,0:T(8,128)(2,1)}) custom-call(s32[1]{0:T(128)} %bitcast.plane_ref, s32[1,128]{1,0:T(1,128)} %bitcast.4, bf16[128,1024]{1,0:T(8,128)(2,1)} %x_ref.1, bf16[128,1024]{1,0:T(8,128)(2,1)} %g_ref.1), custom_call_target="tpu_custom_call" | custom-call | tf_op jit(solution)/shard_map/pack/pallas_call | solution.py:60
  2.9 3.0 %collective-permute-start = (bf16[72,1024]{1,0:T(8,128)(2,1)}, bf16[72,1024]{1,0:T(8,128)(2,1)S(1)}, u32[]{:S(2)}, u32[]{:S(2)}) collective-permute-start(bf16[72,1024]{1,0:T(8,128)(2,1)} %get-tuple-element.35), channel_id=1, source_target_pairs={{0,2},{2,0},{4,6},{6,4},{1,3},{3,1},{5,7},{7,5},{8,10},{10,8},{12,... | collective-permute-start | bytes 442376 | tf_op jit(solution)/shard_map/ppermute | solution.py:257
  5.9 2.6 %collective-permute-start.1 = (bf16[72,1024]{1,0:T(8,128)(2,1)}, bf16[72,1024]{1,0:T(8,128)(2,1)S(1)}, u32[]{:S(2)}, u32[]{:S(2)}) collective-permute-start(bf16[72,1024]{1,0:T(8,128)(2,1)} %get-tuple-element.36), channel_id=1, source_target_pairs={{0,4},{2,6},{4,0},{6,2},{1,5},{3,7},{5,1},{7,3},{8,12},{10,14},{12... | collective-permute-start | bytes 442376 | tf_op jit(solution)/shard_map/ppermute | solution.py:257
  8.5 3.5 %collective-permute-done.refs_1_ = bf16[72,1024]{1,0:T(8,128)(2,1)S(1)} collective-permute-done((bf16[72,1024]{1,0:T(8,128)(2,1)}, bf16[72,1024]{1,0:T(8,128)(2,1)S(1)}, u32[]{:S(2)}, u32[]{:S(2)}) %collective-permute-start) | collective-permute-done | bytes 147488 | tf_op jit(solution)/shard_map/ppermute | solution.py:257
  12.0 8.1 %collective-permute-done.1.refs_2_ = bf16[72,1024]{1,0:T(8,128)(2,1)S(1)} collective-permute-done((bf16[72,1024]{1,0:T(8,128)(2,1)}, bf16[72,1024]{1,0:T(8,128)(2,1)S(1)}, u32[]{:S(2)}, u32[]{:S(2)}) %collective-permute-start.1) | collective-permute-done | bytes 147488 | tf_op jit(solution)/shard_map/ppermute | solution.py:257
  20.8 2.0 %split.1 = (bf16[144,1024]{1,0:T(8,128)(2,1)}, bf16[144,1024]{1,0:T(8,128)(2,1)}) custom-call(bf16[72,1024]{1,0:T(8,128)(2,1)} %get-tuple-element.34.refs_0_, bf16[72,1024]{1,0:T(8,128)(2,1)} %copy-done.14, bf16[72,1024]{1,0:T(8,128)(2,1)} %copy-done.15, bf16[72,1024]{1,0:T(8,128)(2,1)} %copy-done.16), custom_call_target="tpu_custom_call" | custom-call | tf_op jit(solution)/shard_map/split/pallas_call | solution.py:77
  22.8 1.5 %collective-permute-start.6 = (bf16[144,1024]{1,0:T(8,128)(2,1)}, bf16[144,1024]{1,0:T(8,128)(2,1)S(1)}, u32[]{:S(2)}, u32[]{:S(2)}) collective-permute-start(bf16[144,1024]{1,0:T(8,128)(2,1)} %get-tuple-element.38.refs_0_.refs_4_), channel_id=1, source_target_pairs={{0,1},{1,0},{2,3},{3,2},{4,5},{5,4},{6,7},{7,6},{8,9},{9,8},{10,11... | collective-permute-start | bytes 884744 | tf_op jit(solution)/shard_map/ppermute | solution.py:253
  24.3 1.5 %collective-permute-start.7 = (bf16[144,1024]{1,0:T(8,128)(2,1)}, bf16[144,1024]{1,0:T(8,128)(2,1)S(1)}, u32[]{:S(2)}, u32[]{:S(2)}) collective-permute-start(bf16[144,1024]{1,0:T(8,128)(2,1)} %get-tuple-element.38.refs_0_.refs_4_), channel_id=1, source_target_pairs={{0,16},{16,0},{1,17},{17,1},{2,18},{18,2},{3,19},{19,3},{4,20},{20... | collective-permute-start | bytes 884744 | tf_op jit(solution)/shard_map/ppermute | solution.py:253
  26.9 2.2 %copy-done = bf16[1024,2048]{1,0:T(8,128)(2,1)S(1)} copy-done((bf16[1024,2048]{1,0:T(8,128)(2,1)S(1)}, bf16[1024,2048]{1,0:T(8,128)(2,1)}, u32[]{:S(2)}) %copy-start) | copy-done | bytes 4194328
  29.1 2.2 %copy-done.3 = bf16[1024,2048]{1,0:T(8,128)(2,1)S(1)} copy-done((bf16[1024,2048]{1,0:T(8,128)(2,1)S(1)}, bf16[1024,2048]{1,0:T(8,128)(2,1)}, u32[]{:S(2)}) %copy-start.3) | copy-done | bytes 4194328
  31.3 2.2 %copy-done.5 = bf16[2048,1024]{1,0:T(8,128)(2,1)S(1)} copy-done((bf16[2048,1024]{1,0:T(8,128)(2,1)S(1)}, bf16[2048,1024]{1,0:T(8,128)(2,1)}, u32[]{:S(2)}) %copy-start.5) | copy-done | bytes 4194328
  35.4 5.2 %chunk.2 = (bf16[144,2048]{1,0:T(8,128)(2,1)S(1)}, bf16[144,2048]{1,0:T(8,128)(2,1)S(1)}, bf16[36,1024]{1,0:T(8,128)(2,1)S(1)}, bf16[36,1024]{1,0:T(8,128)(2,1)S...) custom-call(bf16[144,1024]{1,0:T(8,128)(2,1)S(1)} %copy-done.7, bf16[144,1024]{1,0:T(8,128)(2,1)S(1)} %copy-done.11, ...), custom_call_target="tpu_custom_call" | custom-call | flops 2415919104 | bytes 13762560 | tf_op jit(solution)/shard_map/chunk/pallas_call | solution.py:133
  41.2 2.3 %collective-permute-start.3 = (bf16[36,1024]{1,0:T(8,128)(2,1)S(1)}, bf16[36,1024]{1,0:T(8,128)(2,1)S(1)}, u32[]{:S(2)}, u32[]{:S(2)}) collective-permute-start(bf16[36,1024]{1,0:T(8,128)(2,1)S(1)} %get-tuple-element.41), channel_id=1, source_target_pairs={{0,2},{2,0},{4,6},{6,4},{1,3},{3,1},{5,7},{7,5},{8,10},{10,8},{12,... | collective-permute-start | bytes 221192 | tf_op jit(solution)/shard_map/ppermute | solution.py:257
  43.5 2.4 %collective-permute-done.3.refs_1_ = bf16[36,1024]{1,0:T(8,128)(2,1)S(1)} collective-permute-done((bf16[36,1024]{1,0:T(8,128)(2,1)S(1)}, bf16[36,1024]{1,0:T(8,128)(2,1)S(1)}, u32[]{:S(2)}, u32[]{:S(2)}) %collective-permute-start.3) | collective-permute-done | bytes 73760 | tf_op jit(solution)/shard_map/ppermute | solution.py:257
  45.9 3.7 %collective-permute-start.4 = (bf16[36,1024]{1,0:T(8,128)(2,1)S(1)}, bf16[36,1024]{1,0:T(8,128)(2,1)S(1)}, u32[]{:S(2)}, u32[]{:S(2)}) collective-permute-start(bf16[36,1024]{1,0:T(8,128)(2,1)S(1)} %get-tuple-element.42), channel_id=1, source_target_pairs={{0,4},{2,6},{4,0},{6,2},{1,5},{3,7},{5,1},{7,3},{8,12},{10,14},{12... | collective-permute-start | bytes 221192 | tf_op jit(solution)/shard_map/ppermute | solution.py:257
  49.6 5.0 %collective-permute-done.4.refs_2_ = bf16[36,1024]{1,0:T(8,128)(2,1)S(1)} collective-permute-done((bf16[36,1024]{1,0:T(8,128)(2,1)S(1)}, bf16[36,1024]{1,0:T(8,128)(2,1)S(1)}, u32[]{:S(2)}, u32[]{:S(2)}) %collective-permute-start.4) | collective-permute-done | bytes 73760 | tf_op jit(solution)/shard_map/ppermute | solution.py:257
  54.5 1.8 %collective-permute-start.5 = (bf16[36,1024]{1,0:T(8,128)(2,1)S(1)}, bf16[36,1024]{1,0:T(8,128)(2,1)S(1)}, u32[]{:S(2)}, u32[]{:S(2)}) collective-permute-start(bf16[36,1024]{1,0:T(8,128)(2,1)S(1)} %get-tuple-element.43), channel_id=1, source_target_pairs={{0,6},{2,4},{4,2},{6,0},{1,7},{3,5},{5,3},{7,1},{8,14},{10,12},{12... | collective-permute-start | bytes 221192 | tf_op jit(solution)/shard_map/ppermute | solution.py:257
  56.4 4.4 %collective-permute-done.5.refs_3_ = bf16[36,1024]{1,0:T(8,128)(2,1)S(1)} collective-permute-done((bf16[36,1024]{1,0:T(8,128)(2,1)S(1)}, bf16[36,1024]{1,0:T(8,128)(2,1)S(1)}, u32[]{:S(2)}, u32[]{:S(2)}) %collective-permute-start.5) | collective-permute-done | bytes 73760 | tf_op jit(solution)/shard_map/ppermute | solution.py:257
  60.8 1.5 %collective-permute-start.14 = (bf16[144,1024]{1,0:T(8,128)(2,1)S(1)}, bf16[144,1024]{1,0:T(8,128)(2,1)S(1)}, u32[]{:S(2)}, u32[]{:S(2)}) collective-permute-start(bf16[144,1024]{1,0:T(8,128)(2,1)S(1)} %collective-permute-done.6.refs_0_.refs_1_.refs_5_), channel_id=1, source_target_pairs={{0,16},{16,0},{1,17},{17,1},{2,18},{18,2},{3,19},{19,3},{4,20},{20... | collective-permute-start | bytes 884744 | tf_op jit(solution)/shard_map/ppermute | solution.py:253
  62.3 1.5 %collective-permute-start.15 = (bf16[144,1024]{1,0:T(8,128)(2,1)S(1)}, bf16[144,1024]{1,0:T(8,128)(2,1)S(1)}, u32[]{:S(2)}, u32[]{:S(2)}) collective-permute-start(bf16[144,1024]{1,0:T(8,128)(2,1)S(1)} %collective-permute-done.9.refs_3_), channel_id=1, source_target_pairs={{0,1},{1,0},{2,3},{3,2},{4,5},{5,4},{6,7},{7,6},{8,9},{9,8},{10,11... | collective-permute-start | bytes 884744 | tf_op jit(solution)/shard_map/ppermute | solution.py:253
  63.8 2.2 %copy-done.1 = bf16[1024,2048]{1,0:T(8,128)(2,1)S(1)} copy-done((bf16[1024,2048]{1,0:T(8,128)(2,1)S(1)}, bf16[1024,2048]{1,0:T(8,128)(2,1)}, u32[]{:S(2)}) %copy-start.1) | copy-done | bytes 4194328
  66.0 2.2 %copy-done.4 = bf16[1024,2048]{1,0:T(8,128)(2,1)S(1)} copy-done((bf16[1024,2048]{1,0:T(8,128)(2,1)S(1)}, bf16[1024,2048]{1,0:T(8,128)(2,1)}, u32[]{:S(2)}) %copy-start.4) | copy-done | bytes 4194328
  68.2 2.2 %copy-done.6 = bf16[2048,1024]{1,0:T(8,128)(2,1)S(1)} copy-done((bf16[2048,1024]{1,0:T(8,128)(2,1)S(1)}, bf16[2048,1024]{1,0:T(8,128)(2,1)}, u32[]{:S(2)}) %copy-start.6) | copy-done | bytes 4194328
  70.4 7.4 %chunk.3 = (bf16[288,2048]{1,0:T(8,128)(2,1)S(1)}, bf16[288,2048]{1,0:T(8,128)(2,1)S(1)}, bf16[36,1024]{1,0:T(8,128)(2,1)S(1)}, bf16[36,1024]{1,0:T(8,128)(2,1)S...) custom-call(bf16[144,1024]{1,0:T(8,128)(2,1)S(1)} %collective-permute-done.6.refs_0_.refs_1_.refs_5_, ...), custom_call_target="tpu_custom_call" | custom-call | flops 4227858432 | bytes 14942208 | tf_op jit(solution)/shard_map/chunk/pallas_call | solution.py:133
  77.8 6.9 %grads.2 = (bf16[512,1024]{1,0:T(8,128)(2,1)S(1)}, bf16[512,1024]{1,0:T(8,128)(2,1)S(1)}) custom-call(s32[2]{0:T(128)S(1)} %pad_add_fusion.where_ref, bf16[144,1024]{1,0:T(8,128)(2,1)S(1)} %copy-done.8, bf16[144,1024]{1,0:T(8,128)(2,1)S(1)} %collective-permute-done.6.refs_0_.refs_1_.refs_5_, ...), custom_call_target="tpu_custom_call" | custom-call | flops 2113929216 | bytes 10747904 | tf_op jit(solution)/shard_map/grads/pallas_call | solution.py:185
  85.7 7.5 %grads.3 = (bf16[512,1024]{1,0:T(8,128)(2,1)S(1)}, bf16[512,1024]{1,0:T(8,128)(2,1)}) custom-call(s32[2]{0:T(128)S(1)} %pad_add_fusion.where_ref, bf16[144,1024]{1,0:T(8,128)(2,1)S(1)} %copy-done.8, bf16[144,1024]{1,0:T(8,128)(2,1)S(1)} %collective-permute-done.6.refs_0_.refs_1_.refs_5_, ...), custom_call_target="tpu_custom_call" | custom-call | flops 2113929216 | bytes 10747904 | tf_op jit(solution)/shard_map/grads/pallas_call | solution.py:185
  95.2 3.2 %collective-permute-start.12 = (bf16[36,1024]{1,0:T(8,128)(2,1)S(1)}, bf16[36,1024]{1,0:T(8,128)(2,1)S(1)}, u32[]{:S(2)}, u32[]{:S(2)}) collective-permute-start(bf16[36,1024]{1,0:T(8,128)(2,1)S(1)} %get-tuple-element.50), channel_id=1, source_target_pairs={{0,5},{1,4},{2,7},{3,6},{4,1},{5,0},{6,3},{7,2},{8,13},{9,12},{10,... | collective-permute-start | bytes 221192 | tf_op jit(solution)/shard_map/ppermute | solution.py:261
  98.4 4.0 %collective-permute-done.10.refs_4_ = bf16[36,1024]{1,0:T(8,128)(2,1)S(1)} collective-permute-done((bf16[36,1024]{1,0:T(8,128)(2,1)S(1)}, bf16[36,1024]{1,0:T(8,128)(2,1)S(1)}, u32[]{:S(2)}, u32[]{:S(2)}) %collective-permute-start.10) | collective-permute-done | bytes 73760 | tf_op jit(solution)/shard_map/ppermute | solution.py:261
  102.4 1.0 collective-permute-start.13
  103.5 6.1 %collective-permute-done.13.refs_7_ = bf16[36,1024]{1,0:T(8,128)(2,1)S(1)} collective-permute-done((bf16[36,1024]{1,0:T(8,128)(2,1)S(1)}, bf16[36,1024]{1,0:T(8,128)(2,1)S(1)}, u32[]{:S(2)}, u32[]{:S(2)}) %collective-permute-start.13) | collective-permute-done | bytes 73760 | tf_op jit(solution)/shard_map/ppermute | solution.py:261
  110.2 2.2 %unpack.1 = bf16[128,1024]{1,0:T(8,128)(2,1)} custom-call(bf16[144,128]{1,0:T(8,128)(2,1)} %get-tuple-element.33.placer_ref, bf16[36,1024]{1,0:T(8,128)(2,1)} %copy-done.12, bf16[36,1024]{1,0:T(8,128)(2,1)} %copy-done.17, bf16[36,1024]{1,0:T(8,128)(2,1)} %copy-done.18, bf16[36,1024]{1,0:T(8,128)(2,1)} %copy-done.19, bf16[36,1024]{1,0:T(8,128)(2,1)} %copy-done.20, ...), custom_call_target="tpu_custom_call" | custom-call | tf_op jit(solution)/shard_map/unpack/pallas_call | solution.py:245
  113.4 4.3 %finish.1 = (bf16[256,2048]{1,0:T(8,128)(2,1)}, bf16[256,2048]{1,0:T(8,128)(2,1)}) custom-call(bf16[512,1024]{1,0:T(8,128)(2,1)} %copy-done.9, bf16[512,1024]{1,0:T(8,128)(2,1)} %copy-done.9, bf16[512,1024]{1,0:T(8,128)(2,1)} %collective-permute-done.16.refs_2_.refs_3_, bf16[512,1024]{1,0:T(8,128)(2,1)} %collective-permute-done.16.refs_2_.refs_3_, ...), custom_call_target="tpu_custom_call" | custom-call | tf_op jit(solution)/shard_map/finish/pallas_call | solution.py:224
  (61 shorter events, 9.0 us)
Async XLA Ops:
  2.9 9.1 %collective-permute-start = (bf16[72,1024]{1,0:T(8,128)(2,1)}, bf16[72,1024]{1,0:T(8,128)(2,1)S(1)}, u32[]{:S(2)}, u32[]{:S(2)}) collective-permute-start(bf16[72,1024]{1,0:T(8,128)(2,1)} %get-tuple-element.35), channel_id=1, source_target_pairs={{0,2},{2,0},{4,6},{6,4},{1,3},{3,1},{5,7},{7,5},{8,10},{10,8},{12,... | collective-permute-start | bytes 442376 | tf_op jit(solution)/shard_map/ppermute | solution.py:257
  5.9 14.2 %collective-permute-start.1 = (bf16[72,1024]{1,0:T(8,128)(2,1)}, bf16[72,1024]{1,0:T(8,128)(2,1)S(1)}, u32[]{:S(2)}, u32[]{:S(2)}) collective-permute-start(bf16[72,1024]{1,0:T(8,128)(2,1)} %get-tuple-element.36), channel_id=1, source_target_pairs={{0,4},{2,6},{4,0},{6,2},{1,5},{3,7},{5,1},{7,3},{8,12},{10,14},{12... | collective-permute-start | bytes 442376 | tf_op jit(solution)/shard_map/ppermute | solution.py:257
  8.5 11.6 %collective-permute-start.2 = (bf16[72,1024]{1,0:T(8,128)(2,1)}, bf16[72,1024]{1,0:T(8,128)(2,1)S(1)}, u32[]{:S(2)}, u32[]{:S(2)}) collective-permute-start(bf16[72,1024]{1,0:T(8,128)(2,1)} %get-tuple-element.37), channel_id=1, source_target_pairs={{0,6},{2,4},{4,2},{6,0},{1,7},{3,5},{5,3},{7,1},{8,14},{10,12},{12... | collective-permute-start | bytes 442376 | tf_op jit(solution)/shard_map/ppermute | solution.py:257
  12.0 8.2 %copy-start.14 = (bf16[72,1024]{1,0:T(8,128)(2,1)}, bf16[72,1024]{1,0:T(8,128)(2,1)S(1)}, u32[]{:S(2)}) copy-start(bf16[72,1024]{1,0:T(8,128)(2,1)S(1)} %collective-permute-done.refs_1_) | copy-start | bytes 442372
  22.8 38.0 %collective-permute-start.6 = (bf16[144,1024]{1,0:T(8,128)(2,1)}, bf16[144,1024]{1,0:T(8,128)(2,1)S(1)}, u32[]{:S(2)}, u32[]{:S(2)}) collective-permute-start(bf16[144,1024]{1,0:T(8,128)(2,1)} %get-tuple-element.38.refs_0_.refs_4_), channel_id=1, source_target_pairs={{0,1},{1,0},{2,3},{3,2},{4,5},{5,4},{6,7},{7,6},{8,9},{9,8},{10,11... | collective-permute-start | bytes 884744 | tf_op jit(solution)/shard_map/ppermute | solution.py:253
  24.3 39.5 %collective-permute-start.7 = (bf16[144,1024]{1,0:T(8,128)(2,1)}, bf16[144,1024]{1,0:T(8,128)(2,1)S(1)}, u32[]{:S(2)}, u32[]{:S(2)}) collective-permute-start(bf16[144,1024]{1,0:T(8,128)(2,1)} %get-tuple-element.38.refs_0_.refs_4_), channel_id=1, source_target_pairs={{0,16},{16,0},{1,17},{17,1},{2,18},{18,2},{3,19},{19,3},{4,20},{20... | collective-permute-start | bytes 884744 | tf_op jit(solution)/shard_map/ppermute | solution.py:253
  25.8 38.0 %collective-permute-start.8 = (bf16[144,1024]{1,0:T(8,128)(2,1)}, bf16[144,1024]{1,0:T(8,128)(2,1)S(1)}, u32[]{:S(2)}, u32[]{:S(2)}) collective-permute-start(bf16[144,1024]{1,0:T(8,128)(2,1)} %get-tuple-element.39.refs_1_), channel_id=1, source_target_pairs={{0,1},{1,0},{2,3},{3,2},{4,5},{5,4},{6,7},{7,6},{8,9},{9,8},{10,11... | collective-permute-start | bytes 884744 | tf_op jit(solution)/shard_map/ppermute | solution.py:253
  26.3 36.0 %collective-permute-start.9 = (bf16[144,1024]{1,0:T(8,128)(2,1)}, bf16[144,1024]{1,0:T(8,128)(2,1)S(1)}, u32[]{:S(2)}, u32[]{:S(2)}) collective-permute-start(bf16[144,1024]{1,0:T(8,128)(2,1)} %get-tuple-element.39.refs_1_), channel_id=1, source_target_pairs={{0,16},{16,0},{1,17},{17,1},{2,18},{18,2},{3,19},{19,3},{4,20},{20... | collective-permute-start | bytes 884744 | tf_op jit(solution)/shard_map/ppermute | solution.py:253
  26.9 2.2 %copy-start = (bf16[1024,2048]{1,0:T(8,128)(2,1)S(1)}, bf16[1024,2048]{1,0:T(8,128)(2,1)}, u32[]{:S(2)}) copy-start(bf16[1024,2048]{1,0:T(8,128)(2,1)} %refs_14_.3) | copy-start | bytes 12582916
  29.1 2.2 %copy-start.3 = (bf16[1024,2048]{1,0:T(8,128)(2,1)S(1)}, bf16[1024,2048]{1,0:T(8,128)(2,1)}, u32[]{:S(2)}) copy-start(bf16[1024,2048]{1,0:T(8,128)(2,1)} %refs_15_.3) | copy-start | bytes 12582916
  31.3 2.2 %copy-start.5 = (bf16[2048,1024]{1,0:T(8,128)(2,1)S(1)}, bf16[2048,1024]{1,0:T(8,128)(2,1)}, u32[]{:S(2)}) copy-start(bf16[2048,1024]{1,0:T(8,128)(2,1)} %refs_16_.3) | copy-start | bytes 12582916
  41.2 4.7 %collective-permute-start.3 = (bf16[36,1024]{1,0:T(8,128)(2,1)S(1)}, bf16[36,1024]{1,0:T(8,128)(2,1)S(1)}, u32[]{:S(2)}, u32[]{:S(2)}) collective-permute-start(bf16[36,1024]{1,0:T(8,128)(2,1)S(1)} %get-tuple-element.41), channel_id=1, source_target_pairs={{0,2},{2,0},{4,6},{6,4},{1,3},{3,1},{5,7},{7,5},{8,10},{10,8},{12,... | collective-permute-start | bytes 221192 | tf_op jit(solution)/shard_map/ppermute | solution.py:257
  45.9 31.9 %copy-start.17 = (bf16[36,1024]{1,0:T(8,128)(2,1)}, bf16[36,1024]{1,0:T(8,128)(2,1)S(1)}, u32[]{:S(2)}) copy-start(bf16[36,1024]{1,0:T(8,128)(2,1)S(1)} %collective-permute-done.3.refs_1_) | copy-start | bytes 221188
  45.9 8.7 %collective-permute-start.4 = (bf16[36,1024]{1,0:T(8,128)(2,1)S(1)}, bf16[36,1024]{1,0:T(8,128)(2,1)S(1)}, u32[]{:S(2)}, u32[]{:S(2)}) collective-permute-start(bf16[36,1024]{1,0:T(8,128)(2,1)S(1)} %get-tuple-element.42), channel_id=1, source_target_pairs={{0,4},{2,6},{4,0},{6,2},{1,5},{3,7},{5,1},{7,3},{8,12},{10,14},{12... | collective-permute-start | bytes 221192 | tf_op jit(solution)/shard_map/ppermute | solution.py:257
  54.5 23.3 %copy-start.18 = (bf16[36,1024]{1,0:T(8,128)(2,1)}, bf16[36,1024]{1,0:T(8,128)(2,1)S(1)}, u32[]{:S(2)}) copy-start(bf16[36,1024]{1,0:T(8,128)(2,1)S(1)} %collective-permute-done.4.refs_2_) | copy-start | bytes 221188
  54.5 6.2 %collective-permute-start.5 = (bf16[36,1024]{1,0:T(8,128)(2,1)S(1)}, bf16[36,1024]{1,0:T(8,128)(2,1)S(1)}, u32[]{:S(2)}, u32[]{:S(2)}) collective-permute-start(bf16[36,1024]{1,0:T(8,128)(2,1)S(1)} %get-tuple-element.43), channel_id=1, source_target_pairs={{0,6},{2,4},{4,2},{6,0},{1,7},{3,5},{5,3},{7,1},{8,14},{10,12},{12... | collective-permute-start | bytes 221192 | tf_op jit(solution)/shard_map/ppermute | solution.py:257
  60.8 17.0 %copy-start.19 = (bf16[36,1024]{1,0:T(8,128)(2,1)}, bf16[36,1024]{1,0:T(8,128)(2,1)S(1)}, u32[]{:S(2)}) copy-start(bf16[36,1024]{1,0:T(8,128)(2,1)S(1)} %collective-permute-done.5.refs_3_) | copy-start | bytes 221188
  60.8 17.0 %collective-permute-start.14 = (bf16[144,1024]{1,0:T(8,128)(2,1)S(1)}, bf16[144,1024]{1,0:T(8,128)(2,1)S(1)}, u32[]{:S(2)}, u32[]{:S(2)}) collective-permute-start(bf16[144,1024]{1,0:T(8,128)(2,1)S(1)} %collective-permute-done.6.refs_0_.refs_1_.refs_5_), channel_id=1, source_target_pairs={{0,16},{16,0},{1,17},{17,1},{2,18},{18,2},{3,19},{19,3},{4,20},{20... | collective-permute-start | bytes 884744 | tf_op jit(solution)/shard_map/ppermute | solution.py:253
  62.3 15.5 %collective-permute-start.15 = (bf16[144,1024]{1,0:T(8,128)(2,1)S(1)}, bf16[144,1024]{1,0:T(8,128)(2,1)S(1)}, u32[]{:S(2)}, u32[]{:S(2)}) collective-permute-start(bf16[144,1024]{1,0:T(8,128)(2,1)S(1)} %collective-permute-done.9.refs_3_), channel_id=1, source_target_pairs={{0,1},{1,0},{2,3},{3,2},{4,5},{5,4},{6,7},{7,6},{8,9},{9,8},{10,11... | collective-permute-start | bytes 884744 | tf_op jit(solution)/shard_map/ppermute | solution.py:253
  63.8 2.2 %copy-start.1 = (bf16[1024,2048]{1,0:T(8,128)(2,1)S(1)}, bf16[1024,2048]{1,0:T(8,128)(2,1)}, u32[]{:S(2)}) copy-start(bf16[1024,2048]{1,0:T(8,128)(2,1)} %refs_14_.3) | copy-start | bytes 12582916
  66.0 2.2 %copy-start.4 = (bf16[1024,2048]{1,0:T(8,128)(2,1)S(1)}, bf16[1024,2048]{1,0:T(8,128)(2,1)}, u32[]{:S(2)}) copy-start(bf16[1024,2048]{1,0:T(8,128)(2,1)} %refs_15_.3) | copy-start | bytes 12582916
  70.4 7.5 %copy-start.2 = (bf16[1024,2048]{1,0:T(8,128)(2,1)S(1)}, bf16[1024,2048]{1,0:T(8,128)(2,1)}, u32[]{:S(2)}) copy-start(bf16[1024,2048]{1,0:T(8,128)(2,1)} %refs_14_.3) | copy-start | bytes 12582916
  70.4 7.5 %copy-start.8 = (bf16[144,1024]{1,0:T(8,128)(2,1)S(1)}, bf16[144,1024]{1,0:T(8,128)(2,1)}, u32[]{:S(2)}) copy-start(bf16[144,1024]{1,0:T(8,128)(2,1)} %get-tuple-element.38.refs_0_.refs_4_) | copy-start | bytes 884740
  85.7 26.7 %collective-permute-start.16 = (bf16[512,1024]{1,0:T(8,128)(2,1)S(1)}, bf16[512,1024]{1,0:T(8,128)(2,1)}, u32[]{:S(2)}, u32[]{:S(2)}) collective-permute-start(bf16[512,1024]{1,0:T(8,128)(2,1)S(1)} %get-tuple-element.58), channel_id=1, source_target_pairs={{0,8},{8,0},{1,9},{9,1},{2,10},{10,2},{3,11},{11,3},{4,12},{12,4},... | collective-permute-start | bytes 3145736 | tf_op jit(solution)/shard_map/ppermute | solution.py:253
  94.2 18.2 %collective-permute-start.17 = (bf16[512,1024]{1,0:T(8,128)(2,1)}, bf16[512,1024]{1,0:T(8,128)(2,1)S(1)}, u32[]{:S(2)}, u32[]{:S(2)}) collective-permute-start(bf16[512,1024]{1,0:T(8,128)(2,1)} %get-tuple-element.60), channel_id=1, source_target_pairs={{0,8},{8,0},{1,9},{9,1},{2,10},{10,2},{3,11},{11,3},{4,12},{12,4},... | collective-permute-start | bytes 3145736 | tf_op jit(solution)/shard_map/ppermute | solution.py:253
  94.7 7.7 %collective-permute-start.10 = (bf16[36,1024]{1,0:T(8,128)(2,1)S(1)}, bf16[36,1024]{1,0:T(8,128)(2,1)S(1)}, u32[]{:S(2)}, u32[]{:S(2)}) collective-permute-start(bf16[36,1024]{1,0:T(8,128)(2,1)S(1)} %get-tuple-element.48), channel_id=1, source_target_pairs={{0,1},{1,0},{2,3},{3,2},{4,5},{5,4},{6,7},{7,6},{8,9},{9,8},{10,11... | collective-permute-start | bytes 221192 | tf_op jit(solution)/shard_map/ppermute | solution.py:261
  95.2 8.2 %collective-permute-start.11 = (bf16[36,1024]{1,0:T(8,128)(2,1)S(1)}, bf16[36,1024]{1,0:T(8,128)(2,1)S(1)}, u32[]{:S(2)}, u32[]{:S(2)}) collective-permute-start(bf16[36,1024]{1,0:T(8,128)(2,1)S(1)} %get-tuple-element.49), channel_id=1, source_target_pairs={{0,3},{1,2},{2,1},{3,0},{4,7},{5,6},{6,5},{7,4},{8,11},{9,10},{10,... | collective-permute-start | bytes 221192 | tf_op jit(solution)/shard_map/ppermute | solution.py:261
  95.2 8.2 %collective-permute-start.12 = (bf16[36,1024]{1,0:T(8,128)(2,1)S(1)}, bf16[36,1024]{1,0:T(8,128)(2,1)S(1)}, u32[]{:S(2)}, u32[]{:S(2)}) collective-permute-start(bf16[36,1024]{1,0:T(8,128)(2,1)S(1)} %get-tuple-element.50), channel_id=1, source_target_pairs={{0,5},{1,4},{2,7},{3,6},{4,1},{5,0},{6,3},{7,2},{8,13},{9,12},{10,... | collective-permute-start | bytes 221192 | tf_op jit(solution)/shard_map/ppermute | solution.py:261
  102.4 7.1 %copy-start.20 = (bf16[36,1024]{1,0:T(8,128)(2,1)}, bf16[36,1024]{1,0:T(8,128)(2,1)S(1)}, u32[]{:S(2)}) copy-start(bf16[36,1024]{1,0:T(8,128)(2,1)S(1)} %collective-permute-done.10.refs_4_) | copy-start | bytes 221188
  102.4 7.1 %collective-permute-start.13 = (bf16[36,1024]{1,0:T(8,128)(2,1)S(1)}, bf16[36,1024]{1,0:T(8,128)(2,1)S(1)}, u32[]{:S(2)}, u32[]{:S(2)}) collective-permute-start(bf16[36,1024]{1,0:T(8,128)(2,1)S(1)} %get-tuple-element.51), channel_id=1, source_target_pairs={{0,7},{1,6},{2,5},{3,4},{4,3},{5,2},{6,1},{7,0},{8,15},{9,14},{10,... | collective-permute-start | bytes 221192 | tf_op jit(solution)/shard_map/ppermute | solution.py:261
  103.4 6.1 %copy-start.21 = (bf16[36,1024]{1,0:T(8,128)(2,1)}, bf16[36,1024]{1,0:T(8,128)(2,1)S(1)}, u32[]{:S(2)}) copy-start(bf16[36,1024]{1,0:T(8,128)(2,1)S(1)} %collective-permute-done.11.refs_5_) | copy-start | bytes 221188
  103.5 6.1 %copy-start.22 = (bf16[36,1024]{1,0:T(8,128)(2,1)}, bf16[36,1024]{1,0:T(8,128)(2,1)S(1)}, u32[]{:S(2)}) copy-start(bf16[36,1024]{1,0:T(8,128)(2,1)S(1)} %collective-permute-done.12.refs_6_) | copy-start | bytes 221188
  (10 other events, 9.7 us)

commit v3 on v2

v3 whole, which is shorter than its diff:
```python
import functools

import jax
import jax.numpy as jnp
from jax import lax
from jax.experimental import pallas as pl
from jax.experimental.pallas import tpu as pltpu
from jax.sharding import Mesh
from jax.sharding import PartitionSpec as P

EXPERTS = 4
CAP = 36
BLOCK = 512
STRIP = 256
MIB = 1024 * 1024
LARGE = pltpu.CompilerParams(vmem_limit_bytes=54 * MIB)
CHEAP = pl.CostEstimate(flops=0, bytes_accessed=0, transcendentals=0)
SMALL = pltpu.CompilerParams(vmem_limit_bytes=12 * MIB)
F32 = jnp.float32
BF16 = jnp.bfloat16


def silu_parts(gate):
    sigma = 0.5 * jnp.tanh(0.5 * gate) + 0.5
    return (gate * sigma, sigma * (1.0 + gate * (1.0 - sigma)))


def contract_rows(left, right):
    return lax.dot_general(left, right, (((0,), (0,)), ((), ())), preferred_element_type=F32)


def contract_cols(left, right):
    return lax.dot_general(left, right, (((1,), (1,)), ((), ())), preferred_element_type=F32)


def stacked(refs):
    return jnp.concatenate([r[...].astype(F32) for r in refs], axis=0)


def pack_kernel(plane_ref, kind_ref, x_ref, g_ref, placer_ref, *outs):
    tokens = kind_ref.shape[1]
    key = kind_ref[...] ^ plane_ref[0]
    onehot = (key == lax.broadcasted_iota(jnp.int32, (8, tokens), 0)).astype(F32)
    before = lax.broadcasted_iota(jnp.int32, (tokens, tokens), 0) < lax.broadcasted_iota(
        jnp.int32, (tokens, tokens), 1
    )
    ranks = jnp.dot(onehot.astype(BF16), before.astype(BF16), preferred_element_type=F32)
    rank = jnp.sum(ranks * onehot, axis=0, keepdims=True).astype(jnp.int32)
    place = key * CAP + rank
    slots = EXPERTS * CAP
    placer = (place == lax.broadcasted_iota(jnp.int32, (slots, tokens), 0)).astype(F32).astype(BF16)
    placer_ref[...] = placer
    for source, first in ((x_ref, 0), (g_ref, EXPERTS)):
        packed = jnp.dot(placer, source[...], preferred_element_type=F32)
        for k in range(EXPERTS):
            outs[first + k][...] = packed[k * CAP : (k + 1) * CAP].astype(BF16)


def pack(plane, kind, x, g):
    tokens, width = x.shape
    return pl.pallas_call(
        pack_kernel,
        out_shape=[jax.ShapeDtypeStruct((EXPERTS * CAP, tokens), BF16)]
        + [jax.ShapeDtypeStruct((CAP, width), BF16)] * (2 * EXPERTS),
        in_specs=[pl.BlockSpec(memory_space=pltpu.SMEM)] + [pl.BlockSpec(memory_space=pltpu.VMEM)] * 3,
        compiler_params=SMALL,
        cost_estimate=CHEAP,
        name="pack",
    )(plane, kind, x, g)


def join_kernel(*refs):
    refs[EXPERTS][...] = stacked(refs[:EXPERTS]).astype(BF16)


def join(blocks):
    width = blocks[0].shape[1]
    return pl.pallas_call(
        join_kernel,
        out_shape=jax.ShapeDtypeStruct((EXPERTS * CAP, width), BF16),
        compiler_params=SMALL,
        cost_estimate=CHEAP,
        name="join",
    )(*blocks)


def forward_kernel(down, xa_ref, xb_ref, wg_ref, wu_ref, *refs):
    if down:
        wd_ref, act_ref, coef_ref, sa_ref, sb_ref, x_ref, acc_ref = refs
    else:
        act_ref, coef_ref, x_ref = refs
    step = pl.program_id(0)
    half = xa_ref.shape[0]

    @pl.when(step == 0)
    def _():
        x_ref[:half, :] = xa_ref[...]
        x_ref[half:, :] = xb_ref[...]
        if down:
            acc_ref[...] = jnp.zeros_like(acc_ref)

    x = x_ref[...]
    for first in range(0, BLOCK, STRIP):
        cols = slice(first, first + STRIP)
        gate = jnp.dot(x, wg_ref[:, cols], preferred_element_type=F32)
        up = jnp.dot(x, wu_ref[:, cols], preferred_element_type=F32)
        act, slope = silu_parts(gate)
        act_ref[:, cols] = act.astype(BF16)
        coef_ref[:, cols] = (up * slope).astype(BF16)
        if down:
            hidden = (act * up).astype(BF16)
            acc_ref[...] += jnp.dot(hidden, wd_ref[cols, :], preferred_element_type=F32)

    if down:

        @pl.when(step == pl.num_programs(0) - 1)
        def _():
            sa_ref[...] = acc_ref[:half, :].astype(BF16)
            sb_ref[...] = acc_ref[half:, :].astype(BF16)


def forward(xa, xb, wg, wu, wd=None):
    half, width = xa.shape
    cols = wg.shape[1]
    rows = 2 * half
    down = wd is not None
    whole = pl.BlockSpec((half, width), lambda j: (0, 0))
    wide = pl.BlockSpec((rows, BLOCK), lambda j: (0, j))
    deep = pl.BlockSpec((width, BLOCK), lambda j: (0, j))
    tall = pl.BlockSpec((BLOCK, width), lambda j: (j, 0))
    count = 3 if down else 2
    return pl.pallas_call(
        functools.partial(forward_kernel, down),
        grid=(cols // BLOCK,),
        in_specs=[whole, whole, deep, deep] + [tall] * down,
        out_specs=[wide, wide] + [whole, whole] * down,
        out_shape=[jax.ShapeDtypeStruct((rows, cols), BF16)] * 2
        + [jax.ShapeDtypeStruct((half, width), BF16)] * (2 * down),
        scratch_shapes=[pltpu.VMEM((rows, width), BF16)] + [pltpu.VMEM((rows, width), F32)] * down,
        compiler_params=LARGE,
        cost_estimate=CHEAP,
        name="forward_down" if down else "forward",
    )(xa, xb, wg, wu, *([wd] * down))


def turn_kernel(where_ref, *refs):
    refs[8][: refs[0].shape[1], :] = stacked(refs[0:4]).T.astype(BF16)
    refs[8][refs[0].shape[1] :, :] = stacked(refs[4:8]).T.astype(BF16)


def turn(where, xs, share):
    part = xs[0].shape[0]
    rows = len(xs) * part
    return pl.pallas_call(
        turn_kernel,
        grid_spec=pltpu.PrefetchScalarGridSpec(
            num_scalar_prefetch=1,
            grid=(1,),
            in_specs=[pl.BlockSpec((part, share), lambda j, w: (0, w[0]))] * 4
            + [pl.BlockSpec((part, share), lambda j, w: (0, w[1]))] * 4,
            out_specs=pl.BlockSpec((2 * share, rows), lambda j, w: (0, 0)),
        ),
        out_shape=jax.ShapeDtypeStruct((2 * share, rows), BF16),
        compiler_params=SMALL,
        cost_estimate=CHEAP,
        name="turn",
    )(where, *xs, *xs)


def backward_kernel(xt_ref, *refs):
    gs = refs[0:4]
    act0, coef0, act1, coef1, wd_ref, own_ref, sib_ref, g_ref = refs[4:]
    part = gs[0].shape[0]
    share = own_ref.shape[0] // 2

    @pl.when(pl.program_id(0) == 0)
    def _():
        for i in range(4):
            g_ref[i * part : (i + 1) * part, :] = gs[i][...]

    for first in range(0, BLOCK, STRIP):
        cols = slice(first, first + STRIP)
        d_hidden = contract_cols(g_ref[...], wd_ref[cols, :])
        for row, low, high in ((0, coef0, coef1), (share, act0, act1)):
            factor = jnp.concatenate([low[:, cols], high[:, cols]], axis=0).astype(F32)
            d_cols = (d_hidden * factor).astype(BF16)
            total = jnp.dot(xt_ref[...], d_cols, preferred_element_type=F32).astype(BF16)
            own_ref[row : row + share, cols] = total[:share]
            sib_ref[row : row + share, cols] = total[share:]


def backward(xt, gs, act0, coef0, act1, coef1, wd, first, cols):
    part, width = gs[0].shape
    height, rows = xt.shape
    base = first // BLOCK
    wide = pl.BlockSpec((2 * part, BLOCK), lambda j: (0, base + j))
    out = pl.BlockSpec((height, BLOCK), lambda j: (0, j))
    return pl.pallas_call(
        backward_kernel,
        grid=(cols // BLOCK,),
        in_specs=[pl.BlockSpec((height, rows), lambda j: (0, 0))]
        + [pl.BlockSpec((part, width), lambda j: (0, 0))] * 4
        + [wide] * 4
        + [pl.BlockSpec((BLOCK, width), lambda j: (base + j, 0))],
        out_specs=[out, out],
        scratch_shapes=[pltpu.VMEM((rows, width), BF16)],
        out_shape=[jax.ShapeDtypeStruct((height, cols), BF16)] * 2,
        compiler_params=LARGE,
        cost_estimate=CHEAP,
        name="backward",
    )(xt, *gs, act0, coef0, act1, coef1, wd)


def finish_kernel(*refs):
    gate_ref, up_ref = refs[8:]
    half = refs[0].shape[1]
    for i in range(2):
        cols = slice(i * half, (i + 1) * half)
        own_gate, own_up, got_gate, got_up = [r[...].astype(F32) for r in refs[4 * i : 4 * i + 4]]
        gate_ref[:, cols] = (own_gate + got_gate).astype(BF16)
        up_ref[:, cols] = (own_up + got_up).astype(BF16)


def finish(own0, got0, own1, got1):
    share, half = own0.shape[0] // 2, own0.shape[1]
    steps = 2
    upper = pl.BlockSpec((share // steps, half), lambda i: (i, 0))
    lower = pl.BlockSpec((share // steps, half), lambda i: (i + steps, 0))
    return pl.pallas_call(
        finish_kernel,
        grid=(steps,),
        in_specs=[upper, lower] * 4,
        out_specs=[pl.BlockSpec((share // steps, 2 * half), lambda i: (i, 0))] * 2,
        out_shape=[jax.ShapeDtypeStruct((share, 2 * half), BF16)] * 2,
        compiler_params=SMALL,
        cost_estimate=CHEAP,
        name="finish",
    )(own0, own0, got0, got0, own1, own1, got1, got1)


def combine_kernel(mine_ref, theirs_ref, *outs):
    total = mine_ref[...].astype(F32) + theirs_ref[...].astype(F32)
    for k in range(EXPERTS):
        outs[k][...] = total[k * CAP : (k + 1) * CAP].astype(BF16)


def combine(mine, theirs):
    width = mine.shape[1]
    return pl.pallas_call(
        combine_kernel,
        out_shape=[jax.ShapeDtypeStruct((CAP, width), BF16)] * EXPERTS,
        compiler_params=SMALL,
        cost_estimate=CHEAP,
        name="combine",
    )(mine, theirs)


def unpack_kernel(placer_ref, *refs):
    packed = stacked(refs[:EXPERTS]).astype(BF16)
    chosen = placer_ref[...].astype(F32).T.astype(BF16)
    refs[EXPERTS][...] = jnp.dot(chosen, packed, preferred_element_type=F32).astype(BF16)


def unpack(placer, blocks):
    width = blocks[0].shape[1]
    return pl.pallas_call(
        unpack_kernel,
        out_shape=jax.ShapeDtypeStruct((placer.shape[1], width), BF16),
        compiler_params=SMALL,
        cost_estimate=CHEAP,
        name="unpack",
    )(placer, *blocks)


def swap(value, axis):
    return lax.ppermute(value, axis, [(0, 1), (1, 0)])


def across_planes(blocks):
    return [blocks[0]] + [
        lax.ppermute(blocks[k], "arch", [(i, i ^ k) for i in range(EXPERTS)]) for k in range(1, EXPERTS)
    ]


def after(values, earlier):
    n = len(values)
    return lax.optimization_barrier((*values, *earlier))[:n]


def gathering(designs, archetype, w_gate, w_up, w_down, cotangent):
    plane = lax.axis_index("arch").astype(jnp.int32)
    far = lax.axis_index("far").astype(jnp.int32)
    core = lax.axis_index("core").astype(jnp.int32)
    tokens, width = designs.shape
    share = width // 4
    placer, *blocks = pack(plane[None], archetype.reshape(1, tokens), designs, cotangent)

    x_own = join(across_planes(blocks[:EXPERTS]))
    x_near, x_far = after([swap(x_own, "half"), swap(x_own, "far")], [])
    x_corner = swap(x_near, "far")

    g_own = join(across_planes(after(blocks[EXPERTS:], [x_own])))
    g_near, g_far = after([swap(g_own, "half"), swap(g_own, "far")], [])
    g_corner = swap(g_near, "far")

    act0, coef0, share_own, share_near = forward(x_own, x_near, w_gate, w_up, w_down)
    act1, coef1 = forward(x_far, x_corner, w_gate, w_up)
    (share_got,) = after([swap(share_near, "half")], [act1])
    returned = across_planes(combine(share_own, share_got))
    outputs = unpack(placer, returned)

    where = jnp.stack([2 * far + core, 2 * far + 1 - core])
    xt = turn(where, [x_own, x_near, x_far, x_corner], share)
    gs = [g_own, g_near, g_far, g_corner]
    half = w_down.shape[0] // 2
    own0, sib0 = backward(xt, gs, act0, coef0, act1, coef1, w_down, 0, half)
    (xt,) = after([xt], returned[1:])
    own1, sib1 = backward(xt, gs, act0, coef0, act1, coef1, w_down, half, half)
    grad_gate, grad_up = finish(own0, swap(sib0, "core"), own1, swap(sib1, "core"))
    return outputs, grad_gate, grad_up


def reducing(designs, archetype, w_gate, w_up, w_down, cotangent):
    width = designs.shape[1]
    owners = lax.axis_size("expert")
    sharers = owners // EXPERTS
    hidden_cols = w_gate.shape[1]
    labels = archetype[:, 0]
    onehot = (labels[:, None] == jnp.arange(EXPERTS, dtype=jnp.int32)[None, :]).astype(jnp.int32)
    ranks = jnp.cumsum(onehot, axis=0) - onehot
    target = labels * CAP + jnp.sum(ranks * onehot, axis=1)
    placer = (jnp.arange(EXPERTS * CAP, dtype=jnp.int32)[:, None] == target[None, :]).astype(BF16)
    received = []
    for rows in (designs, cotangent):
        packed = jnp.dot(placer, rows, preferred_element_type=F32).astype(BF16)
        send = jnp.repeat(packed.reshape(EXPERTS, CAP, width), sharers, axis=0)
        received.append(
            lax.all_to_all(send, "expert", split_axis=0, concat_axis=0, tiled=True).reshape(
                owners * CAP, width
            )
        )
    flat_x, flat_g = received
    gate = jnp.dot(flat_x, w_gate, preferred_element_type=F32)
    up = jnp.dot(flat_x, w_up, preferred_element_type=F32)
    act, slope = silu_parts(gate)
    hidden = (act * up).astype(BF16)
    partial_value = (
        jnp.dot(hidden, w_down, preferred_element_type=F32).astype(BF16).reshape(owners, CAP, width)
    )
    returned = lax.all_to_all(partial_value, "expert", split_axis=0, concat_axis=0, tiled=True)
    summed = jnp.sum(returned.astype(F32).reshape(EXPERTS, sharers, CAP, width), axis=1).reshape(
        EXPERTS * CAP, width
    )
    outputs = jnp.take(summed, target, axis=0).astype(BF16)
    d_hidden = contract_cols(flat_g, w_down)
    d_gate = (d_hidden * up * slope).astype(BF16)
    d_up = (d_hidden * act).astype(BF16)
    grads = jnp.concatenate([contract_rows(flat_x, d_gate), contract_rows(flat_x, d_up)], axis=1)
    mine = lax.psum_scatter(grads.astype(BF16), "dp", scatter_dimension=0, tiled=True)
    return outputs, mine[:, :hidden_cols], mine[:, hidden_cols:]


def solution(mesh):
    dp, owners = mesh.devices.shape
    if (dp, owners) == (4, 2 * EXPERTS):
        rows, cols = ("far", "core"), ("arch", "half")
        mesh = Mesh(mesh.devices.reshape(2, 2, EXPERTS, 2), rows + cols)
        body = gathering
    else:
        rows, cols = ("dp",), ("expert",)
        body = reducing
    tokens = P(rows + cols, None)
    return jax.shard_map(
        body,
        mesh=mesh,
        in_specs=(tokens, tokens, P(None, cols), P(None, cols), P(cols, None), tokens),
        out_specs=(tokens, P(rows, cols), P(rows, cols)),
        check_vma=False,
    )
```

time: 118 us -> 83.9 us (0.71)
  waiting for transfers between devices: 33.5 us -> 14.7 us
  local copies, waits for them, and re-layouts: 20 us -> 7.07 us
  starting transfers between devices: 25.7 us -> 23 us
    ppermute x10 -> x9, waiting for transfers between devices: 33.5 us -> 13.2 us  [across_planes(): lax.ppermute(blocks[k], 'arch', [(i, i ^ k) for i in range(EXPERTS)])]
    unnamed x48 -> x38, local copies, waits for them, and re-layouts: 20 us -> 7.07 us
    pallas_call x5 -> x8, Pallas kernels: 28.9 us -> 35 us  [the longest x2 17.6 us: forward(): pl.pallas_call(functools.partial(forward_kernel, down), grid=(cols // BLO...]
    ppermute x10 -> x9, starting transfers between devices: 18.1 us -> 14.5 us  [across_planes(): lax.ppermute(blocks[k], 'arch', [(i, i ^ k) for i in range(EXPERTS)])]
    pallas_call x1, Pallas kernels: 4.3 us -> 1.49 us  [finish(): pl.pallas_call(finish_kernel, grid=(steps,), in_specs=[upper, lower] * 4,...]
    pallas_call x1, Pallas kernels: 2.26 us -> 0.43 us  [pack(): pl.pallas_call(pack_kernel, out_shape=[jax.ShapeDtypeStruct((EXPERTS * CA...]
    ppermute x8 -> x9, waiting for transfers between devices: 0.02 us -> 1.54 us  [swap(): return lax.ppermute(value, axis, [(0, 1), (1, 0)])]
    pallas_call x1, Pallas kernels: 2.22 us -> 0.97 us  [unpack(): pl.pallas_call(unpack_kernel, out_shape=jax.ShapeDtypeStruct((placer.shap...]
  transfers between devices with their start and end apart: 18 -> 18, of which waited for: 7 -> 7; matrix products, arithmetic and copies ran while one was open for 0% -> 0% of each run, Pallas kernels for 19% -> 33%
where the time goes in v3:
time: 83.9 us; the launch traced here: 83.6 us
  Pallas kernels  37.9 us (45%)
  starting transfers between devices  23 us (27%)
  waiting for transfers between devices  14.7 us (18%)
  local copies, waits for them, and re-layouts  7.07 us (8%)
    pallas_call x2, Pallas kernels, forward(): pl.pallas_call(functools.partial(forward_kernel, down), grid=(cols // BLO...  17.6 us
    pallas_call x2, Pallas kernels, backward(): pl.pallas_call(backward_kernel, grid=(cols // BLOCK,), in_specs=[pl.Block...  16.4 us
    ppermute x9, starting transfers between devices, across_planes(): lax.ppermute(blocks[k], 'arch', [(i, i ^ k) for i in range(EXPERTS)])  14.5 us
    ppermute x9, waiting for transfers between devices, across_planes(): lax.ppermute(blocks[k], 'arch', [(i, i ^ k) for i in range(EXPERTS)])  13.2 us
    ppermute x9, starting transfers between devices, swap(): return lax.ppermute(value, axis, [(0, 1), (1, 0)])  8.47 us
    unnamed x38, local copies, waits for them, and re-layouts  7.07 us
  transfers between devices with their start and end apart: 18, of which 7 were waited for; matrix products, arithmetic and copies ran while one was open for 0% of the time, Pallas kernels for 33%

profile of v3, /device:TPU:0, one launch (start us, length us, event | category | flops | bytes accessed | tf_op | source)
XLA Modules:
  0.0 83.6 jit_solution(13559768505140272799)
XLA Ops:
  0.6 0.9 %copy-done.13 = bf16[128,1024]{1,0:T(8,128)(2,1)S(1)} copy-done((bf16[128,1024]{1,0:T(8,128)(2,1)S(1)}, bf16[128,1024]{1,0:T(8,128)(2,1)}, u32[]{:S(2)}) %copy-start.13) | copy-done | bytes 262168
  1.6 0.9 %copy-done.14 = bf16[128,1024]{1,0:T(8,128)(2,1)S(1)} copy-done((bf16[128,1024]{1,0:T(8,128)(2,1)S(1)}, bf16[128,1024]{1,0:T(8,128)(2,1)}, u32[]{:S(2)}) %copy-start.14) | copy-done | bytes 262168
  3.6 3.1 %collective-permute-start = (bf16[36,1024]{1,0:T(8,128)(2,1)S(1)}, bf16[36,1024]{1,0:T(8,128)(2,1)S(1)}, u32[]{:S(2)}, u32[]{:S(2)}) collective-permute-start(bf16[36,1024]{1,0:T(8,128)(2,1)S(1)} %get-tuple-element.40), channel_id=1, source_target_pairs={{0,2},{2,0},{4,6},{6,4},{1,3},{3,1},{5,7},{7,5},{8,10},{10,8},{12,... | collective-permute-start | bytes 221192 | tf_op jit(solution)/shard_map/ppermute | solution.py:281
  6.7 2.6 %collective-permute-start.1 = (bf16[36,1024]{1,0:T(8,128)(2,1)S(1)}, bf16[36,1024]{1,0:T(8,128)(2,1)S(1)}, u32[]{:S(2)}, u32[]{:S(2)}) collective-permute-start(bf16[36,1024]{1,0:T(8,128)(2,1)S(1)} %get-tuple-element.41), channel_id=1, source_target_pairs={{0,4},{2,6},{4,0},{6,2},{1,5},{3,7},{5,1},{7,3},{8,12},{10,14},{12... | collective-permute-start | bytes 221192 | tf_op jit(solution)/shard_map/ppermute | solution.py:281
  9.3 6.6 %collective-permute-done.1.refs_2_ = bf16[36,1024]{1,0:T(8,128)(2,1)S(1)} collective-permute-done((bf16[36,1024]{1,0:T(8,128)(2,1)S(1)}, bf16[36,1024]{1,0:T(8,128)(2,1)S(1)}, u32[]{:S(2)}, u32[]{:S(2)}) %collective-permute-start.1) | collective-permute-done | bytes 73760 | tf_op jit(solution)/shard_map/ppermute | solution.py:281
  16.0 1.6 %collective-permute-start.3 = (bf16[144,1024]{1,0:T(8,128)(2,1)S(1)}, bf16[144,1024]{1,0:T(8,128)(2,1)S(1)}, u32[]{:S(2)}, u32[]{:S(2)}) collective-permute-start(bf16[144,1024]{1,0:T(8,128)(2,1)S(1)} %join.2.xa_ref.refs_0_.refs_4_), channel_id=1, source_target_pairs={{0,1},{1,0},{2,3},{3,2},{4,5},{5,4},{6,7},{7,6},{8,9},{9,8},{10,11... | collective-permute-start | bytes 884744 | tf_op jit(solution)/shard_map/ppermute | solution.py:276
  17.6 1.5 %collective-permute-start.4 = (bf16[144,1024]{1,0:T(8,128)(2,1)S(1)}, bf16[144,1024]{1,0:T(8,128)(2,1)S(1)}, u32[]{:S(2)}, u32[]{:S(2)}) collective-permute-start(bf16[144,1024]{1,0:T(8,128)(2,1)S(1)} %join.2.xa_ref.refs_0_.refs_4_), channel_id=1, source_target_pairs={{0,16},{16,0},{1,17},{17,1},{2,18},{18,2},{3,19},{19,3},{4,20},{20... | collective-permute-start | bytes 884744 | tf_op jit(solution)/shard_map/ppermute | solution.py:276
  19.1 1.4 %collective-permute-start.10 = (bf16[36,1024]{1,0:T(8,128)(2,1)S(1)}, bf16[36,1024]{1,0:T(8,128)(2,1)S(1)}, u32[]{:S(2)}, u32[]{:S(2)}) collective-permute-start(bf16[36,1024]{1,0:T(8,128)(2,1)S(1)} %get-tuple-element.58), channel_id=1, source_target_pairs={{0,2},{2,0},{4,6},{6,4},{1,3},{3,1},{5,7},{7,5},{8,10},{10,8},{12,... | collective-permute-start | bytes 221192 | tf_op jit(solution)/shard_map/ppermute | solution.py:281
  20.5 1.6 %collective-permute-start.11 = (bf16[36,1024]{1,0:T(8,128)(2,1)S(1)}, bf16[36,1024]{1,0:T(8,128)(2,1)S(1)}, u32[]{:S(2)}, u32[]{:S(2)}) collective-permute-start(bf16[36,1024]{1,0:T(8,128)(2,1)S(1)} %get-tuple-element.59), channel_id=1, source_target_pairs={{0,4},{2,6},{4,0},{6,2},{1,5},{3,7},{5,1},{7,3},{8,12},{10,14},{12... | collective-permute-start | bytes 221192 | tf_op jit(solution)/shard_map/ppermute | solution.py:281
  22.1 1.3 %collective-permute-start.12 = (bf16[36,1024]{1,0:T(8,128)(2,1)S(1)}, bf16[36,1024]{1,0:T(8,128)(2,1)S(1)}, u32[]{:S(2)}, u32[]{:S(2)}) collective-permute-start(bf16[36,1024]{1,0:T(8,128)(2,1)S(1)} %get-tuple-element.60), channel_id=1, source_target_pairs={{0,6},{2,4},{4,2},{6,0},{1,7},{3,5},{5,3},{7,1},{8,14},{10,12},{12... | collective-permute-start | bytes 221192 | tf_op jit(solution)/shard_map/ppermute | solution.py:281
  23.5 3.7 %collective-permute-done.11.refs_2_ = bf16[36,1024]{1,0:T(8,128)(2,1)S(1)} collective-permute-done((bf16[36,1024]{1,0:T(8,128)(2,1)S(1)}, bf16[36,1024]{1,0:T(8,128)(2,1)S(1)}, u32[]{:S(2)}, u32[]{:S(2)}) %collective-permute-start.11) | collective-permute-done | bytes 73760 | tf_op jit(solution)/shard_map/ppermute | solution.py:281
  27.2 1.2 %collective-permute-done.12.refs_3_ = bf16[36,1024]{1,0:T(8,128)(2,1)S(1)} collective-permute-done((bf16[36,1024]{1,0:T(8,128)(2,1)S(1)}, bf16[36,1024]{1,0:T(8,128)(2,1)S(1)}, u32[]{:S(2)}, u32[]{:S(2)}) %collective-permute-start.12) | collective-permute-done | bytes 73760 | tf_op jit(solution)/shard_map/ppermute | solution.py:281
  29.6 1.6 %collective-permute-start.6 = (bf16[144,1024]{1,0:T(8,128)(2,1)S(1)}, bf16[144,1024]{1,0:T(8,128)(2,1)S(1)}, u32[]{:S(2)}, u32[]{:S(2)}) collective-permute-start(bf16[144,1024]{1,0:T(8,128)(2,1)S(1)} %collective-permute-done.3.xb_ref.refs_1_.refs_5_), channel_id=1, source_target_pairs={{0,16},{16,0},{1,17},{17,1},{2,18},{18,2},{3,19},{19,3},{4,20},{20... | collective-permute-start | bytes 884744 | tf_op jit(solution)/shard_map/ppermute | solution.py:276
  31.2 10.0 %forward_down.1 = (bf16[288,2048]{1,0:T(8,128)(2,1)}, bf16[288,2048]{1,0:T(8,128)(2,1)}, bf16[144,1024]{1,0:T(8,128)(2,1)}, bf16[144,1024]{1,0:T(8,128)(2,1)}) custom-call(bf16[144,1024]{1,0:T(8,128)(2,1)} %copy-done.1, bf16[144,1024]{1,0:T(8,128)(2,1)} %copy-done.5, bf16[1024,2048]{1,0:T(8,128)(2,1)} %wg_ref.3, bf16[1024,2048]{1,0:T(8,128)(2,1)} %wu_ref.3, ...), custom_call_target="tpu_custom_call" | custom-call | tf_op jit(solution)/shard_map/forward_down/pallas_call | solution.py:132
  41.2 1.6 %collective-permute-start.5 = (bf16[144,1024]{1,0:T(8,128)(2,1)}, bf16[144,1024]{1,0:T(8,128)(2,1)S(1)}, u32[]{:S(2)}, u32[]{:S(2)}) collective-permute-start(bf16[144,1024]{1,0:T(8,128)(2,1)} %get-tuple-element.45), channel_id=1, source_target_pairs={{0,1},{1,0},{2,3},{3,2},{4,5},{5,4},{6,7},{7,6},{8,9},{9,8},{10,11... | collective-permute-start | bytes 884744 | tf_op jit(solution)/shard_map/ppermute | solution.py:276
  42.8 0.7 collective-permute-start.15
  43.5 0.7 copy-done.9
  44.2 7.6 %forward.1 = (bf16[288,2048]{1,0:T(8,128)(2,1)}, bf16[288,2048]{1,0:T(8,128)(2,1)}) custom-call(bf16[144,1024]{1,0:T(8,128)(2,1)} %copy-done.7, bf16[144,1024]{1,0:T(8,128)(2,1)} %copy-done.9, bf16[1024,2048]{1,0:T(8,128)(2,1)} %wg_ref.3, bf16[1024,2048]{1,0:T(8,128)(2,1)} %wu_ref.3), custom_call_target="tpu_custom_call" | custom-call | tf_op jit(solution)/shard_map/forward/pallas_call | solution.py:132
  52.0 1.2 %collective-permute-start.7 = (bf16[36,1024]{1,0:T(8,128)(2,1)S(1)}, bf16[36,1024]{1,0:T(8,128)(2,1)S(1)}, u32[]{:S(2)}, u32[]{:S(2)}) collective-permute-start(bf16[36,1024]{1,0:T(8,128)(2,1)S(1)} %get-tuple-element.50), channel_id=1, source_target_pairs={{0,2},{2,0},{4,6},{6,4},{1,3},{3,1},{5,7},{7,5},{8,10},{10,8},{12,... | collective-permute-start | bytes 221192 | tf_op jit(solution)/shard_map/ppermute | solution.py:281
  53.2 1.2 %collective-permute-start.8 = (bf16[36,1024]{1,0:T(8,128)(2,1)S(1)}, bf16[36,1024]{1,0:T(8,128)(2,1)S(1)}, u32[]{:S(2)}, u32[]{:S(2)}) collective-permute-start(bf16[36,1024]{1,0:T(8,128)(2,1)S(1)} %get-tuple-element.51), channel_id=1, source_target_pairs={{0,4},{2,6},{4,0},{6,2},{1,5},{3,7},{5,1},{7,3},{8,12},{10,14},{12... | collective-permute-start | bytes 221192 | tf_op jit(solution)/shard_map/ppermute | solution.py:281
  54.4 2.1 %collective-permute-start.9 = (bf16[36,1024]{1,0:T(8,128)(2,1)S(1)}, bf16[36,1024]{1,0:T(8,128)(2,1)S(1)}, u32[]{:S(2)}, u32[]{:S(2)}) collective-permute-start(bf16[36,1024]{1,0:T(8,128)(2,1)S(1)} %get-tuple-element.52), channel_id=1, source_target_pairs={{0,6},{2,4},{4,2},{6,0},{1,7},{3,5},{5,3},{7,1},{8,14},{10,12},{12... | collective-permute-start | bytes 221192 | tf_op jit(solution)/shard_map/ppermute | solution.py:281
  56.5 1.0 %copy-done.10 = bf16[144,1024]{1,0:T(8,128)(2,1)S(1)} copy-done((bf16[144,1024]{1,0:T(8,128)(2,1)S(1)}, bf16[144,1024]{1,0:T(8,128)(2,1)}, u32[]{:S(2)}) %copy-start.10) | copy-done | bytes 294936
  57.5 0.8 turn.1.xt_ref
  58.3 0.8 copy-done
  59.4 1.3 %collective-permute-done.9.refs_3_ = bf16[36,1024]{1,0:T(8,128)(2,1)S(1)} collective-permute-done((bf16[36,1024]{1,0:T(8,128)(2,1)S(1)}, bf16[36,1024]{1,0:T(8,128)(2,1)S(1)}, u32[]{:S(2)}, u32[]{:S(2)}) %collective-permute-start.9) | collective-permute-done | bytes 73760 | tf_op jit(solution)/shard_map/ppermute | solution.py:281
  60.7 0.7 copy-done.18
  61.4 8.1 %backward.2 = (bf16[512,1024]{1,0:T(8,128)(2,1)}, bf16[512,1024]{1,0:T(8,128)(2,1)}) custom-call(bf16[512,576]{1,0:T(8,128)(2,1)} %copy-done, bf16[144,1024]{1,0:T(8,128)(2,1)} %copy-done.11, bf16[144,1024]{1,0:T(8,128)(2,1)} %copy-done.16, bf16[144,1024]{1,0:T(8,128)(2,1)} %copy-done.17, bf16[144,1024]{1,0:T(8,128)(2,1)} %copy-done.18, ...), custom_call_target="tpu_custom_call" | custom-call | tf_op jit(solution)/shard_map/backward/pallas_call | solution.py:198
  69.5 8.3 %backward.3 = (bf16[512,1024]{1,0:T(8,128)(2,1)}, bf16[512,1024]{1,0:T(8,128)(2,1)}) custom-call(bf16[512,576]{1,0:T(8,128)(2,1)} %copy-done, bf16[144,1024]{1,0:T(8,128)(2,1)} %copy-done.11, bf16[144,1024]{1,0:T(8,128)(2,1)} %copy-done.16, bf16[144,1024]{1,0:T(8,128)(2,1)} %copy-done.17, bf16[144,1024]{1,0:T(8,128)(2,1)} %copy-done.18, ...), custom_call_target="tpu_custom_call" | custom-call | tf_op jit(solution)/shard_map/backward/pallas_call | solution.py:198
  78.3 1.0 %unpack.1 = bf16[128,1024]{1,0:T(8,128)(2,1)} custom-call(bf16[144,128]{1,0:T(8,128)(2,1)S(1)} %get-tuple-element.38.placer_ref, bf16[36,1024]{1,0:T(8,128)(2,1)S(1)} %get-tuple-element.49.refs_0_, bf16[36,1024]{1,0:T(8,128)(2,1)S(1)} %collective-permute-done.7.refs_1_, bf16[36,1024]{1,0:T(8,128)(2,1)S(1)} %collective-permute-done.8.refs_2_, ...), custom_call_target="tpu_custom_call" | custom-call | tf_op jit(solution)/shard_map/unpack/pallas_call | solution.py:266
  79.3 1.5 %collective-permute-done.17.refs_6_.refs_7_ = bf16[512,1024]{1,0:T(8,128)(2,1)S(1)} collective-permute-done((bf16[512,1024]{1,0:T(8,128)(2,1)}, bf16[512,1024]{1,0:T(8,128)(2,1)S(1)}, u32[]{:S(2)}, u32[]{:S(2)}) %collective-permute-start.17) | collective-permute-done | bytes 1048608 | tf_op jit(solution)/shard_map/ppermute | solution.py:276
  80.8 1.2 %copy-done.4 = bf16[512,1024]{1,0:T(8,128)(2,1)S(1)} copy-done((bf16[512,1024]{1,0:T(8,128)(2,1)S(1)}, bf16[512,1024]{1,0:T(8,128)(2,1)}, u32[]{:S(2)}) %copy-start.4) | copy-done | bytes 1048600
  82.1 1.5 %finish.1 = (bf16[256,2048]{1,0:T(8,128)(2,1)}, bf16[256,2048]{1,0:T(8,128)(2,1)}) custom-call(bf16[512,1024]{1,0:T(8,128)(2,1)S(1)} %copy-done.3, bf16[512,1024]{1,0:T(8,128)(2,1)S(1)} %copy-done.3, bf16[512,1024]{1,0:T(8,128)(2,1)S(1)} %collective-permute-done.16.refs_2_.refs_3_, bf16[512,1024]{1,0:T(8,128)(2,1)S(1)} %collective-permute-done.16.refs_2_.refs_3_, ...), custom_call_target="tpu_custom_call" | custom-call | tf_op jit(solution)/shard_map/finish/pallas_call | solution.py:229
  (54 shorter events, 3.4 us)
Async XLA Ops:
  0.6 1.0 %copy-start.13 = (bf16[128,1024]{1,0:T(8,128)(2,1)S(1)}, bf16[128,1024]{1,0:T(8,128)(2,1)}, u32[]{:S(2)}) copy-start(bf16[128,1024]{1,0:T(8,128)(2,1)} %x_ref.1) | copy-start | bytes 786436
  3.6 5.7 %collective-permute-start = (bf16[36,1024]{1,0:T(8,128)(2,1)S(1)}, bf16[36,1024]{1,0:T(8,128)(2,1)S(1)}, u32[]{:S(2)}, u32[]{:S(2)}) collective-permute-start(bf16[36,1024]{1,0:T(8,128)(2,1)S(1)} %get-tuple-element.40), channel_id=1, source_target_pairs={{0,2},{2,0},{4,6},{6,4},{1,3},{3,1},{5,7},{7,5},{8,10},{10,8},{12,... | collective-permute-start | bytes 221192 | tf_op jit(solution)/shard_map/ppermute | solution.py:281
  6.7 9.2 %collective-permute-start.1 = (bf16[36,1024]{1,0:T(8,128)(2,1)S(1)}, bf16[36,1024]{1,0:T(8,128)(2,1)S(1)}, u32[]{:S(2)}, u32[]{:S(2)}) collective-permute-start(bf16[36,1024]{1,0:T(8,128)(2,1)S(1)} %get-tuple-element.41), channel_id=1, source_target_pairs={{0,4},{2,6},{4,0},{6,2},{1,5},{3,7},{5,1},{7,3},{8,12},{10,14},{12... | collective-permute-start | bytes 221192 | tf_op jit(solution)/shard_map/ppermute | solution.py:281
  9.3 6.6 %collective-permute-start.2 = (bf16[36,1024]{1,0:T(8,128)(2,1)S(1)}, bf16[36,1024]{1,0:T(8,128)(2,1)S(1)}, u32[]{:S(2)}, u32[]{:S(2)}) collective-permute-start(bf16[36,1024]{1,0:T(8,128)(2,1)S(1)} %get-tuple-element.42), channel_id=1, source_target_pairs={{0,6},{2,4},{4,2},{6,0},{1,7},{3,5},{5,3},{7,1},{8,14},{10,12},{12... | collective-permute-start | bytes 221192 | tf_op jit(solution)/shard_map/ppermute | solution.py:281
  16.0 15.2 %copy-start.1 = (bf16[144,1024]{1,0:T(8,128)(2,1)}, bf16[144,1024]{1,0:T(8,128)(2,1)S(1)}, u32[]{:S(2)}) copy-start(bf16[144,1024]{1,0:T(8,128)(2,1)S(1)} %join.2.xa_ref.refs_0_.refs_4_) | copy-start | bytes 884740
  16.0 13.6 %collective-permute-start.3 = (bf16[144,1024]{1,0:T(8,128)(2,1)S(1)}, bf16[144,1024]{1,0:T(8,128)(2,1)S(1)}, u32[]{:S(2)}, u32[]{:S(2)}) collective-permute-start(bf16[144,1024]{1,0:T(8,128)(2,1)S(1)} %join.2.xa_ref.refs_0_.refs_4_), channel_id=1, source_target_pairs={{0,1},{1,0},{2,3},{3,2},{4,5},{5,4},{6,7},{7,6},{8,9},{9,8},{10,11... | collective-permute-start | bytes 884744 | tf_op jit(solution)/shard_map/ppermute | solution.py:276
  17.6 12.1 %collective-permute-start.4 = (bf16[144,1024]{1,0:T(8,128)(2,1)S(1)}, bf16[144,1024]{1,0:T(8,128)(2,1)S(1)}, u32[]{:S(2)}, u32[]{:S(2)}) collective-permute-start(bf16[144,1024]{1,0:T(8,128)(2,1)S(1)} %join.2.xa_ref.refs_0_.refs_4_), channel_id=1, source_target_pairs={{0,16},{16,0},{1,17},{17,1},{2,18},{18,2},{3,19},{19,3},{4,20},{20... | collective-permute-start | bytes 884744 | tf_op jit(solution)/shard_map/ppermute | solution.py:276
  19.1 4.5 %collective-permute-start.10 = (bf16[36,1024]{1,0:T(8,128)(2,1)S(1)}, bf16[36,1024]{1,0:T(8,128)(2,1)S(1)}, u32[]{:S(2)}, u32[]{:S(2)}) collective-permute-start(bf16[36,1024]{1,0:T(8,128)(2,1)S(1)} %get-tuple-element.58), channel_id=1, source_target_pairs={{0,2},{2,0},{4,6},{6,4},{1,3},{3,1},{5,7},{7,5},{8,10},{10,8},{12,... | collective-permute-start | bytes 221192 | tf_op jit(solution)/shard_map/ppermute | solution.py:281
  20.5 6.8 %collective-permute-start.11 = (bf16[36,1024]{1,0:T(8,128)(2,1)S(1)}, bf16[36,1024]{1,0:T(8,128)(2,1)S(1)}, u32[]{:S(2)}, u32[]{:S(2)}) collective-permute-start(bf16[36,1024]{1,0:T(8,128)(2,1)S(1)} %get-tuple-element.59), channel_id=1, source_target_pairs={{0,4},{2,6},{4,0},{6,2},{1,5},{3,7},{5,1},{7,3},{8,12},{10,14},{12... | collective-permute-start | bytes 221192 | tf_op jit(solution)/shard_map/ppermute | solution.py:281
  22.1 6.3 %collective-permute-start.12 = (bf16[36,1024]{1,0:T(8,128)(2,1)S(1)}, bf16[36,1024]{1,0:T(8,128)(2,1)S(1)}, u32[]{:S(2)}, u32[]{:S(2)}) collective-permute-start(bf16[36,1024]{1,0:T(8,128)(2,1)S(1)} %get-tuple-element.60), channel_id=1, source_target_pairs={{0,6},{2,4},{4,2},{6,0},{1,7},{3,5},{5,3},{7,1},{8,14},{10,12},{12... | collective-permute-start | bytes 221192 | tf_op jit(solution)/shard_map/ppermute | solution.py:281
  28.5 12.7 %copy-start.11 = (bf16[144,1024]{1,0:T(8,128)(2,1)}, bf16[144,1024]{1,0:T(8,128)(2,1)S(1)}, u32[]{:S(2)}) copy-start(bf16[144,1024]{1,0:T(8,128)(2,1)S(1)} %join.3.refs_0_) | copy-start | bytes 884740
  28.5 14.3 %collective-permute-start.13 = (bf16[144,1024]{1,0:T(8,128)(2,1)S(1)}, bf16[144,1024]{1,0:T(8,128)(2,1)S(1)}, u32[]{:S(2)}, u32[]{:S(2)}) collective-permute-start(bf16[144,1024]{1,0:T(8,128)(2,1)S(1)} %join.3.refs_0_), channel_id=1, source_target_pairs={{0,1},{1,0},{2,3},{3,2},{4,5},{5,4},{6,7},{7,6},{8,9},{9,8},{10,11... | collective-permute-start | bytes 884744 | tf_op jit(solution)/shard_map/ppermute | solution.py:276
  29.1 13.7 %collective-permute-start.14 = (bf16[144,1024]{1,0:T(8,128)(2,1)S(1)}, bf16[144,1024]{1,0:T(8,128)(2,1)S(1)}, u32[]{:S(2)}, u32[]{:S(2)}) collective-permute-start(bf16[144,1024]{1,0:T(8,128)(2,1)S(1)} %join.3.refs_0_), channel_id=1, source_target_pairs={{0,16},{16,0},{1,17},{17,1},{2,18},{18,2},{3,19},{19,3},{4,20},{20... | collective-permute-start | bytes 884744 | tf_op jit(solution)/shard_map/ppermute | solution.py:276
  29.6 1.6 %copy-start.5 = (bf16[144,1024]{1,0:T(8,128)(2,1)}, bf16[144,1024]{1,0:T(8,128)(2,1)S(1)}, u32[]{:S(2)}) copy-start(bf16[144,1024]{1,0:T(8,128)(2,1)S(1)} %collective-permute-done.3.xb_ref.refs_1_.refs_5_) | copy-start | bytes 884740
  29.6 11.6 %copy-start.7 = (bf16[144,1024]{1,0:T(8,128)(2,1)}, bf16[144,1024]{1,0:T(8,128)(2,1)S(1)}, u32[]{:S(2)}) copy-start(bf16[144,1024]{1,0:T(8,128)(2,1)S(1)} %collective-permute-done.4.xa_ref.refs_2_.refs_6_) | copy-start | bytes 884740
  29.6 13.9 %collective-permute-start.6 = (bf16[144,1024]{1,0:T(8,128)(2,1)S(1)}, bf16[144,1024]{1,0:T(8,128)(2,1)S(1)}, u32[]{:S(2)}, u32[]{:S(2)}) collective-permute-start(bf16[144,1024]{1,0:T(8,128)(2,1)S(1)} %collective-permute-done.3.xb_ref.refs_1_.refs_5_), channel_id=1, source_target_pairs={{0,16},{16,0},{1,17},{17,1},{2,18},{18,2},{3,19},{19,3},{4,20},{20... | collective-permute-start | bytes 884744 | tf_op jit(solution)/shard_map/ppermute | solution.py:276
  41.2 10.6 %collective-permute-start.5 = (bf16[144,1024]{1,0:T(8,128)(2,1)}, bf16[144,1024]{1,0:T(8,128)(2,1)S(1)}, u32[]{:S(2)}, u32[]{:S(2)}) collective-permute-start(bf16[144,1024]{1,0:T(8,128)(2,1)} %get-tuple-element.45), channel_id=1, source_target_pairs={{0,1},{1,0},{2,3},{3,2},{4,5},{5,4},{6,7},{7,6},{8,9},{9,8},{10,11... | collective-permute-start | bytes 884744 | tf_op jit(solution)/shard_map/ppermute | solution.py:276
  42.8 9.1 %copy-start.16 = (bf16[144,1024]{1,0:T(8,128)(2,1)}, bf16[144,1024]{1,0:T(8,128)(2,1)S(1)}, u32[]{:S(2)}) copy-start(bf16[144,1024]{1,0:T(8,128)(2,1)S(1)} %collective-permute-done.13.refs_1_) | copy-start | bytes 884740
  42.8 9.1 %copy-start.17 = (bf16[144,1024]{1,0:T(8,128)(2,1)}, bf16[144,1024]{1,0:T(8,128)(2,1)S(1)}, u32[]{:S(2)}) copy-start(bf16[144,1024]{1,0:T(8,128)(2,1)S(1)} %collective-permute-done.14.refs_2_) | copy-start | bytes 884740
  42.8 17.9 %collective-permute-start.15 = (bf16[144,1024]{1,0:T(8,128)(2,1)S(1)}, bf16[144,1024]{1,0:T(8,128)(2,1)S(1)}, u32[]{:S(2)}, u32[]{:S(2)}) collective-permute-start(bf16[144,1024]{1,0:T(8,128)(2,1)S(1)} %collective-permute-done.13.refs_1_), channel_id=1, source_target_pairs={{0,16},{16,0},{1,17},{17,1},{2,18},{18,2},{3,19},{19,3},{4,20},{20... | collective-permute-start | bytes 884744 | tf_op jit(solution)/shard_map/ppermute | solution.py:276
  43.5 8.4 %copy-start.12 = (bf16[144,1024]{1,0:T(8,128)(2,1)S(1)}, bf16[144,1024]{1,0:T(8,128)(2,1)}, u32[]{:S(2)}) copy-start(bf16[144,1024]{1,0:T(8,128)(2,1)} %get-tuple-element.44.mine_ref) | copy-start | bytes 884740
  43.5 13.0 %copy-start.2 = (bf16[144,1024]{1,0:T(8,128)(2,1)S(1)}, bf16[144,1024]{1,0:T(8,128)(2,1)}, u32[]{:S(2)}) copy-start(bf16[144,1024]{1,0:T(8,128)(2,1)} %copy-done.1) | copy-start | bytes 884740
  43.5 13.0 %copy-start.6 = (bf16[144,1024]{1,0:T(8,128)(2,1)S(1)}, bf16[144,1024]{1,0:T(8,128)(2,1)}, u32[]{:S(2)}) copy-start(bf16[144,1024]{1,0:T(8,128)(2,1)} %copy-done.5) | copy-start | bytes 884740
  43.5 13.0 %copy-start.8 = (bf16[144,1024]{1,0:T(8,128)(2,1)S(1)}, bf16[144,1024]{1,0:T(8,128)(2,1)}, u32[]{:S(2)}) copy-start(bf16[144,1024]{1,0:T(8,128)(2,1)} %copy-done.7) | copy-start | bytes 884740
  52.0 7.1 %collective-permute-start.7 = (bf16[36,1024]{1,0:T(8,128)(2,1)S(1)}, bf16[36,1024]{1,0:T(8,128)(2,1)S(1)}, u32[]{:S(2)}, u32[]{:S(2)}) collective-permute-start(bf16[36,1024]{1,0:T(8,128)(2,1)S(1)} %get-tuple-element.50), channel_id=1, source_target_pairs={{0,2},{2,0},{4,6},{6,4},{1,3},{3,1},{5,7},{7,5},{8,10},{10,8},{12,... | collective-permute-start | bytes 221192 | tf_op jit(solution)/shard_map/ppermute | solution.py:281
  53.2 6.2 %collective-permute-start.8 = (bf16[36,1024]{1,0:T(8,128)(2,1)S(1)}, bf16[36,1024]{1,0:T(8,128)(2,1)S(1)}, u32[]{:S(2)}, u32[]{:S(2)}) collective-permute-start(bf16[36,1024]{1,0:T(8,128)(2,1)S(1)} %get-tuple-element.51), channel_id=1, source_target_pairs={{0,4},{2,6},{4,0},{6,2},{1,5},{3,7},{5,1},{7,3},{8,12},{10,14},{12... | collective-permute-start | bytes 221192 | tf_op jit(solution)/shard_map/ppermute | solution.py:281
  54.4 6.3 %collective-permute-start.9 = (bf16[36,1024]{1,0:T(8,128)(2,1)S(1)}, bf16[36,1024]{1,0:T(8,128)(2,1)S(1)}, u32[]{:S(2)}, u32[]{:S(2)}) collective-permute-start(bf16[36,1024]{1,0:T(8,128)(2,1)S(1)} %get-tuple-element.52), channel_id=1, source_target_pairs={{0,6},{2,4},{4,2},{6,0},{1,7},{3,5},{5,3},{7,1},{8,14},{10,12},{12... | collective-permute-start | bytes 221192 | tf_op jit(solution)/shard_map/ppermute | solution.py:281
  56.5 1.0 %copy-start.10 = (bf16[144,1024]{1,0:T(8,128)(2,1)S(1)}, bf16[144,1024]{1,0:T(8,128)(2,1)}, u32[]{:S(2)}) copy-start(bf16[144,1024]{1,0:T(8,128)(2,1)} %copy-done.9) | copy-start | bytes 884740
  69.5 9.8 %collective-permute-start.16 = (bf16[512,1024]{1,0:T(8,128)(2,1)}, bf16[512,1024]{1,0:T(8,128)(2,1)S(1)}, u32[]{:S(2)}, u32[]{:S(2)}) collective-permute-start(bf16[512,1024]{1,0:T(8,128)(2,1)} %get-tuple-element.67), channel_id=1, source_target_pairs={{0,8},{8,0},{1,9},{9,1},{2,10},{10,2},{3,11},{11,3},{4,12},{12,4},... | collective-permute-start | bytes 3145736 | tf_op jit(solution)/shard_map/ppermute | solution.py:276
  69.5 11.3 %copy-start.3 = (bf16[512,1024]{1,0:T(8,128)(2,1)S(1)}, bf16[512,1024]{1,0:T(8,128)(2,1)}, u32[]{:S(2)}) copy-start(bf16[512,1024]{1,0:T(8,128)(2,1)} %get-tuple-element.66.refs_0_.refs_1_) | copy-start | bytes 3145732
  77.9 3.0 %collective-permute-start.17 = (bf16[512,1024]{1,0:T(8,128)(2,1)}, bf16[512,1024]{1,0:T(8,128)(2,1)S(1)}, u32[]{:S(2)}, u32[]{:S(2)}) collective-permute-start(bf16[512,1024]{1,0:T(8,128)(2,1)} %get-tuple-element.70), channel_id=1, source_target_pairs={{0,8},{8,0},{1,9},{9,1},{2,10},{10,2},{3,11},{11,3},{4,12},{12,4},... | collective-permute-start | bytes 3145736 | tf_op jit(solution)/shard_map/ppermute | solution.py:276
  80.8 1.2 %copy-start.4 = (bf16[512,1024]{1,0:T(8,128)(2,1)S(1)}, bf16[512,1024]{1,0:T(8,128)(2,1)}, u32[]{:S(2)}) copy-start(bf16[512,1024]{1,0:T(8,128)(2,1)} %get-tuple-element.69.refs_4_.refs_5_) | copy-start | bytes 3145732
  (5 other events, 3.9 us)

commit v4 on v3

--- a/solution.py
+++ b/solution.py
@@ -10,14 +10,16 @@
 
 EXPERTS = 4
 CAP = 36
-BLOCK = 512
 STRIP = 256
+PAIR = 2 * STRIP
 MIB = 1024 * 1024
-LARGE = pltpu.CompilerParams(vmem_limit_bytes=54 * MIB)
+LARGE = pltpu.CompilerParams(vmem_limit_bytes=16 * MIB)
+SMALL = pltpu.CompilerParams(vmem_limit_bytes=12 * MIB)
 CHEAP = pl.CostEstimate(flops=0, bytes_accessed=0, transcendentals=0)
-SMALL = pltpu.CompilerParams(vmem_limit_bytes=12 * MIB)
 F32 = jnp.float32
 BF16 = jnp.bfloat16
+HERE = pl.BlockSpec(memory_space=pltpu.VMEM)
+AFAR = pl.BlockSpec(memory_space=pltpu.HBM)
 
 
 def silu_parts(gate):
@@ -37,9 +39,21 @@
     return jnp.concatenate([r[...].astype(F32) for r in refs], axis=0)
 
 
-def pack_kernel(plane_ref, kind_ref, x_ref, g_ref, placer_ref, *outs):
-    tokens = kind_ref.shape[1]
-    key = kind_ref[...] ^ plane_ref[0]
+def kept(value):
+    return pltpu.with_memory_space_constraint(value, pltpu.HBM)
+
+
+def pack_kernel(plane_ref, kind_ref, x_ref, g_ref, placer_ref, *refs):
+    outs, (kind, x, g, sems) = refs[: 2 * EXPERTS], refs[2 * EXPERTS :]
+    copies = [
+        pltpu.make_async_copy(source, target, sems.at[i])
+        for i, (source, target) in enumerate(((kind_ref, kind), (x_ref, x), (g_ref, g)))
+    ]
+    for copy in copies:
+        copy.start()
+    tokens = kind.shape[1]
+    copies[0].wait()
+    key = kind[...] ^ plane_ref[0]
     onehot = (key == lax.broadcasted_iota(jnp.int32, (8, tokens), 0)).astype(F32)
     before = lax.broadcasted_iota(jnp.int32, (tokens, tokens), 0) < lax.broadcasted_iota(
         jnp.int32, (tokens, tokens), 1
@@ -50,7 +64,8 @@
     slots = EXPERTS * CAP
     placer = (place == lax.broadcasted_iota(jnp.int32, (slots, tokens), 0)).astype(F32).astype(BF16)
     placer_ref[...] = placer
-    for source, first in ((x_ref, 0), (g_ref, EXPERTS)):
+    for copy, source, first in ((copies[1], x, 0), (copies[2], g, EXPERTS)):
+        copy.wait()
         packed = jnp.dot(placer, source[...], preferred_element_type=F32)
         for k in range(EXPERTS):
             outs[first + k][...] = packed[k * CAP : (k + 1) * CAP].astype(BF16)
@@ -62,11 +77,47 @@
         pack_kernel,
         out_shape=[jax.ShapeDtypeStruct((EXPERTS * CAP, tokens), BF16)]
         + [jax.ShapeDtypeStruct((CAP, width), BF16)] * (2 * EXPERTS),
-        in_specs=[pl.BlockSpec(memory_space=pltpu.SMEM)] + [pl.BlockSpec(memory_space=pltpu.VMEM)] * 3,
+        in_specs=[pl.BlockSpec(memory_space=pltpu.SMEM)] + [AFAR] * 3,
+        scratch_shapes=[
+            pltpu.VMEM((1, tokens), jnp.int32),
+            pltpu.VMEM((tokens, width), BF16),
+            pltpu.VMEM((tokens, width), BF16),
+            pltpu.SemaphoreType.DMA((3,)),
+        ],
         compiler_params=SMALL,
         cost_estimate=CHEAP,
         name="pack",
-    )(plane, kind, x, g)
+    )(plane, kept(kind), kept(x), kept(g))
+
+
+def load_kernel(pieces, *refs):
+    n = len(refs) // 2
+    sems = refs[2 * n]
+    copies = []
+    for i in range(n):
+        lines = refs[i].shape[0] // pieces
+        for j in range(pieces):
+            rows = pl.ds(j * lines, lines)
+            copies.append(
+                pltpu.make_async_copy(refs[i].at[rows], refs[n + i].at[rows], sems.at[i * pieces + j])
+            )
+    for copy in copies:
+        copy.start()
+    for copy in copies:
+        copy.wait()
+
+
+def load(arrays, pieces=4):
+    return pl.pallas_call(
+        functools.partial(load_kernel, pieces),
+        out_shape=[pltpu.VMEM(a.shape, a.dtype) for a in arrays],
+        in_specs=[AFAR] * len(arrays),
+        out_specs=[HERE] * len(arrays),
+        scratch_shapes=[pltpu.SemaphoreType.DMA((len(arrays) * pieces,))],
+        compiler_params=SMALL,
+        cost_estimate=CHEAP,
+        name="load",
+    )(*[kept(a) for a in arrays])
 
 
 def join_kernel(*refs):
@@ -84,63 +135,55 @@
     )(*blocks)
 
 
-def forward_kernel(down, xa_ref, xb_ref, wg_ref, wu_ref, *refs):
+def forward_kernel(n, down, *refs):
+    xs, refs = refs[:n], refs[n:]
     if down:
-        wd_ref, act_ref, coef_ref, sa_ref, sb_ref, x_ref, acc_ref = refs
+        wg_ref, wu_ref, wd_ref, act_ref, coef_ref, share_ref = refs[:6]
+        acc_ref = refs[6]
+        acc_ref[...] = jnp.zeros_like(acc_ref)
     else:
-        act_ref, coef_ref, x_ref = refs
-    step = pl.program_id(0)
-    half = xa_ref.shape[0]
-
-    @pl.when(step == 0)
-    def _():
-        x_ref[:half, :] = xa_ref[...]
-        x_ref[half:, :] = xb_ref[...]
-        if down:
-            acc_ref[...] = jnp.zeros_like(acc_ref)
-
-    x = x_ref[...]
-    for first in range(0, BLOCK, STRIP):
-        cols = slice(first, first + STRIP)
-        gate = jnp.dot(x, wg_ref[:, cols], preferred_element_type=F32)
-        up = jnp.dot(x, wu_ref[:, cols], preferred_element_type=F32)
-        act, slope = silu_parts(gate)
-        act_ref[:, cols] = act.astype(BF16)
-        coef_ref[:, cols] = (up * slope).astype(BF16)
-        if down:
-            hidden = (act * up).astype(BF16)
-            acc_ref[...] += jnp.dot(hidden, wd_ref[cols, :], preferred_element_type=F32)
+        wg_ref, wu_ref, act_ref, coef_ref = refs[:4]
+    if n == 1:
+        x_ref = xs[0]
+    else:
+        x_ref = refs[-1]
+        part = xs[0].shape[0]
+        for i in range(n):
+            x_ref[i * part : (i + 1) * part, :] = xs[i][...]
+
+    @pl.loop(0, wg_ref.shape[1] // PAIR)
+    def _(j):
+        for i in range(PAIR // STRIP):
+            cols = pl.ds(pl.multiple_of(j * PAIR + i * STRIP, STRIP), STRIP)
+            gate = jnp.dot(x_ref[...], wg_ref[:, cols], preferred_element_type=F32)
+            up = jnp.dot(x_ref[...], wu_ref[:, cols], preferred_element_type=F32)
+            act, slope = silu_parts(gate)
+            act_ref[:, cols] = act.astype(BF16)
+            coef_ref[:, cols] = (up * slope).astype(BF16)
+            if down:
+                hidden = (act * up).astype(BF16)
+                acc_ref[...] += jnp.dot(hidden, wd_ref[cols, :], preferred_element_type=F32)
 
     if down:
-
-        @pl.when(step == pl.num_programs(0) - 1)
-        def _():
-            sa_ref[...] = acc_ref[:half, :].astype(BF16)
-            sb_ref[...] = acc_ref[half:, :].astype(BF16)
-
-
-def forward(xa, xb, wg, wu, wd=None):
-    half, width = xa.shape
+        share_ref[...] = acc_ref[...].astype(BF16)
+
+
+def forward(xs, wg, wu, wd=None):
+    n, (part, width) = len(xs), xs[0].shape
     cols = wg.shape[1]
-    rows = 2 * half
+    rows = n * part
     down = wd is not None
-    whole = pl.BlockSpec((half, width), lambda j: (0, 0))
-    wide = pl.BlockSpec((rows, BLOCK), lambda j: (0, j))
-    deep = pl.BlockSpec((width, BLOCK), lambda j: (0, j))
-    tall = pl.BlockSpec((BLOCK, width), lambda j: (j, 0))
-    count = 3 if down else 2
-    return pl.pallas_call(
-        functools.partial(forward_kernel, down),
-        grid=(cols // BLOCK,),
-        in_specs=[whole, whole, deep, deep] + [tall] * down,
-        out_specs=[wide, wide] + [whole, whole] * down,
+    return pl.pallas_call(
+        functools.partial(forward_kernel, n, down),
         out_shape=[jax.ShapeDtypeStruct((rows, cols), BF16)] * 2
-        + [jax.ShapeDtypeStruct((half, width), BF16)] * (2 * down),
-        scratch_shapes=[pltpu.VMEM((rows, width), BF16)] + [pltpu.VMEM((rows, width), F32)] * down,
+        + [jax.ShapeDtypeStruct((rows, width), BF16)] * down,
+        in_specs=[HERE] * (n + 2 + down),
+        scratch_shapes=[pltpu.VMEM((rows, width), F32)] * down
+        + [pltpu.VMEM((rows, width), BF16)] * (n > 1),
         compiler_params=LARGE,
         cost_estimate=CHEAP,
         name="forward_down" if down else "forward",
-    )(xa, xb, wg, wu, *([wd] * down))
+    )(*xs, wg, wu, *([wd] * down))
 
 
 def turn_kernel(where_ref, *refs):
@@ -167,48 +210,42 @@
     )(where, *xs, *xs)
 
 
-def backward_kernel(xt_ref, *refs):
-    gs = refs[0:4]
-    act0, coef0, act1, coef1, wd_ref, own_ref, sib_ref, g_ref = refs[4:]
+def backward_kernel(first, counts, xt_ref, *refs):
+    n = len(counts)
+    gs, acts, coefs = refs[:4], refs[4 : 4 + n], refs[4 + n : 4 + 2 * n]
+    wd_ref, own_ref, sib_ref, g_ref = refs[4 + 2 * n :]
     part = gs[0].shape[0]
     share = own_ref.shape[0] // 2
-
-    @pl.when(pl.program_id(0) == 0)
-    def _():
-        for i in range(4):
-            g_ref[i * part : (i + 1) * part, :] = gs[i][...]
-
-    for first in range(0, BLOCK, STRIP):
-        cols = slice(first, first + STRIP)
-        d_hidden = contract_cols(g_ref[...], wd_ref[cols, :])
-        for row, low, high in ((0, coef0, coef1), (share, act0, act1)):
-            factor = jnp.concatenate([low[:, cols], high[:, cols]], axis=0).astype(F32)
-            d_cols = (d_hidden * factor).astype(BF16)
-            total = jnp.dot(xt_ref[...], d_cols, preferred_element_type=F32).astype(BF16)
-            own_ref[row : row + share, cols] = total[:share]
-            sib_ref[row : row + share, cols] = total[share:]
-
-
-def backward(xt, gs, act0, coef0, act1, coef1, wd, first, cols):
+    for i in range(4):
+        g_ref[i * part : (i + 1) * part, :] = gs[i][...]
+
+    @pl.loop(0, own_ref.shape[1] // PAIR)
+    def _(j):
+        for i in range(PAIR // STRIP):
+            here = pl.ds(pl.multiple_of(j * PAIR + i * STRIP, STRIP), STRIP)
+            cols = pl.ds(pl.multiple_of(j * PAIR + i * STRIP + first, STRIP), STRIP)
+            d_hidden = contract_cols(g_ref[...], wd_ref[cols, :])
+            for row, parts in ((0, coefs), (share, acts)):
+                factor = jnp.concatenate([p[:, cols] for p in parts], axis=0).astype(F32)
+                d_cols = (d_hidden * factor).astype(BF16)
+                total = jnp.dot(xt_ref[...], d_cols, preferred_element_type=F32).astype(BF16)
+                own_ref[row : row + share, here] = total[:share]
+                sib_ref[row : row + share, here] = total[share:]
+
+
+def backward(xt, gs, acts, coefs, wd, first, cols):
     part, width = gs[0].shape
     height, rows = xt.shape
-    base = first // BLOCK
-    wide = pl.BlockSpec((2 * part, BLOCK), lambda j: (0, base + j))
-    out = pl.BlockSpec((height, BLOCK), lambda j: (0, j))
-    return pl.pallas_call(
-        backward_kernel,
-        grid=(cols // BLOCK,),
-        in_specs=[pl.BlockSpec((height, rows), lambda j: (0, 0))]
-        + [pl.BlockSpec((part, width), lambda j: (0, 0))] * 4
-        + [wide] * 4
-        + [pl.BlockSpec((BLOCK, width), lambda j: (base + j, 0))],
-        out_specs=[out, out],
+    counts = tuple(a.shape[0] for a in acts)
+    return pl.pallas_call(
+        functools.partial(backward_kernel, first, counts),
+        out_shape=[jax.ShapeDtypeStruct((height, cols), BF16)] * 2,
+        in_specs=[HERE] * (6 + 2 * len(acts)),
         scratch_shapes=[pltpu.VMEM((rows, width), BF16)],
-        out_shape=[jax.ShapeDtypeStruct((height, cols), BF16)] * 2,
         compiler_params=LARGE,
         cost_estimate=CHEAP,
         name="backward",
-    )(xt, *gs, act0, coef0, act1, coef1, wd)
+    )(xt, *gs, *acts, *coefs, wd)
 
 
 def finish_kernel(*refs):
@@ -284,7 +321,7 @@
 
 def after(values, earlier):
     n = len(values)
-    return lax.optimization_barrier((*values, *earlier))[:n]
+    return list(lax.optimization_barrier((*values, *earlier))[:n])
 
 
 def gathering(designs, archetype, w_gate, w_up, w_down, cotangent):
@@ -294,28 +331,33 @@
     tokens, width = designs.shape
     share = width // 4
     placer, *blocks = pack(plane[None], archetype.reshape(1, tokens), designs, cotangent)
-
-    x_own = join(across_planes(blocks[:EXPERTS]))
+    wg, wu, wd = load(after([w_gate, w_up, w_down], [placer]))
+
+    moved = across_planes(blocks[:EXPERTS])
+    x_own = join(after(moved[:1], [wg]) + moved[1:])
     x_near, x_far = after([swap(x_own, "half"), swap(x_own, "far")], [])
     x_corner = swap(x_near, "far")
 
-    g_own = join(across_planes(after(blocks[EXPERTS:], [x_own])))
+    act0, coef0, share_own = forward([x_own], wg, wu, wd)
+    moved = across_planes(after(blocks[EXPERTS:], [x_own]))
+    g_own = join(after(moved[:1], [act0, x_near, x_far]) + moved[1:])
     g_near, g_far = after([swap(g_own, "half"), swap(g_own, "far")], [])
     g_corner = swap(g_near, "far")
 
-    act0, coef0, share_own, share_near = forward(x_own, x_near, w_gate, w_up, w_down)
-    act1, coef1 = forward(x_far, x_corner, w_gate, w_up)
-    (share_got,) = after([swap(share_near, "half")], [act1])
+    (x_near,) = after([x_near], [act0])
+    act1, coef1, share_near = forward([x_near], wg, wu, wd)
+    act2, coef2 = forward([x_far, x_corner], wg, wu)
+    (share_got,) = after([swap(share_near, "half")], [act2])
     returned = across_planes(combine(share_own, share_got))
     outputs = unpack(placer, returned)
 
     where = jnp.stack([2 * far + core, 2 * far + 1 - core])
     xt = turn(where, [x_own, x_near, x_far, x_corner], share)
-    gs = [g_own, g_near, g_far, g_corner]
+    gs, acts, coefs = [g_own, g_near, g_far, g_corner], [act0, act1, act2], [coef0, coef1, coef2]
     half = w_down.shape[0] // 2
-    own0, sib0 = backward(xt, gs, act0, coef0, act1, coef1, w_down, 0, half)
+    own0, sib0 = backward(xt, gs, acts, coefs, wd, 0, half)
     (xt,) = after([xt], returned[1:])
-    own1, sib1 = backward(xt, gs, act0, coef0, act1, coef1, w_down, half, half)
+    own1, sib1 = backward(xt, gs, acts, coefs, wd, half, half)
     grad_gate, grad_up = finish(own0, swap(sib0, "core"), own1, swap(sib1, "core"))
     return outputs, grad_gate, grad_up
 

time: 83.9 us -> 77.7 us (0.926)
  Pallas kernels: 37.9 us -> 34.1 us
  waiting for transfers between devices: 14.7 us -> 12.6 us
    ppermute x9, waiting for transfers between devices: 13.2 us -> 6.81 us  [across_planes(): lax.ppermute(blocks[k], 'arch', [(i, i ^ k) for i in range(EXPERTS)])]
    pallas_call x4 -> x6, Pallas kernels: 34 us -> 28.2 us  [the longest x3 12 us: forward(): pl.pallas_call(functools.partial(forward_kernel, n, down), out_shape=[jax...]
    ppermute x9, waiting for transfers between devices: 1.54 us -> 5.81 us  [swap(): return lax.ppermute(value, axis, [(0, 1), (1, 0)])]
    pallas_call x1, Pallas kernels: 0.43 us -> 1.46 us  [pack(): pl.pallas_call(pack_kernel, out_shape=[jax.ShapeDtypeStruct((EXPERTS * CA...]
    pallas_call x1, Pallas kernels: 0.09 us -> 1.05 us  [combine(): pl.pallas_call(combine_kernel, out_shape=[jax.ShapeDtypeStruct((CAP, widt...]
    unnamed x38 -> x28, local copies, waits for them, and re-layouts: 7.07 us -> 6.57 us
  transfers between devices with their start and end apart: 18 -> 18, of which waited for: 7 -> 6; matrix products, arithmetic and copies ran while one was open for 0% -> 0% of each run, Pallas kernels for 33% -> 33%
where the time goes in v4:
time: 77.7 us; the launch traced here: 77.4 us
  Pallas kernels  34.1 us (44%)
  starting transfers between devices  23.2 us (30%)
  waiting for transfers between devices  12.6 us (16%)
  local copies, waits for them, and re-layouts  6.57 us (8%)
  between operations  0.86 us (1%)
    ppermute x9, starting transfers between devices, across_planes(): lax.ppermute(blocks[k], 'arch', [(i, i ^ k) for i in range(EXPERTS)])  14.8 us
    pallas_call x3, Pallas kernels, forward(): pl.pallas_call(functools.partial(forward_kernel, n, down), out_shape=[jax...  12 us
    pallas_call x2, Pallas kernels, backward(): pl.pallas_call(functools.partial(backward_kernel, first, counts), out_sha...  11.6 us
    ppermute x9, starting transfers between devices, swap(): return lax.ppermute(value, axis, [(0, 1), (1, 0)])  8.34 us
    ppermute x9, waiting for transfers between devices, across_planes(): lax.ppermute(blocks[k], 'arch', [(i, i ^ k) for i in range(EXPERTS)])  6.81 us
    unnamed x28, local copies, waits for them, and re-layouts  6.57 us
    ppermute x9, waiting for transfers between devices, swap(): return lax.ppermute(value, axis, [(0, 1), (1, 0)])  5.81 us
    pallas_call x1, Pallas kernels, load(): pl.pallas_call(functools.partial(load_kernel, pieces), out_shape=[pltpu.V...  4.7 us
  transfers between devices with their start and end apart: 18, of which 6 were waited for; matrix products, arithmetic and copies ran while one was open for 0% of the time, Pallas kernels for 33%

profile of v4, /device:TPU:0, one launch (start us, length us, event | category | flops | bytes accessed | tf_op | source)
XLA Modules:
  0.0 77.4 jit_solution(10923498664690582679)
XLA Ops:
  0.6 1.5 %pack.1 = (bf16[144,128]{1,0:T(8,128)(2,1)S(1)}, bf16[36,1024]{1,0:T(8,128)(2,1)S(1)}, bf16[36,1024]{1,0:T(8,128)(2,1)S(1)}, bf16[36,1024]{1,0:T(8,128)(2,1)S(1)...) custom-call(s32[1]{0:T(128)} %bitcast.plane_ref, ...), custom_call_target="tpu_custom_call" | custom-call | tf_op jit(solution)/shard_map/pack/pallas_call | solution.py:76
  2.7 3.0 %collective-permute-start = (bf16[36,1024]{1,0:T(8,128)(2,1)S(1)}, bf16[36,1024]{1,0:T(8,128)(2,1)S(1)}, u32[]{:S(2)}, u32[]{:S(2)}) collective-permute-start(bf16[36,1024]{1,0:T(8,128)(2,1)S(1)} %get-tuple-element.56), channel_id=1, source_target_pairs={{0,2},{2,0},{4,6},{6,4},{1,3},{3,1},{5,7},{7,5},{8,10},{10,8},{12,... | collective-permute-start | bytes 221192 | tf_op jit(solution)/shard_map/ppermute | solution.py:318
  5.7 2.6 %collective-permute-start.1 = (bf16[36,1024]{1,0:T(8,128)(2,1)S(1)}, bf16[36,1024]{1,0:T(8,128)(2,1)S(1)}, u32[]{:S(2)}, u32[]{:S(2)}) collective-permute-start(bf16[36,1024]{1,0:T(8,128)(2,1)S(1)} %get-tuple-element.57), channel_id=1, source_target_pairs={{0,4},{2,6},{4,0},{6,2},{1,5},{3,7},{5,1},{7,3},{8,12},{10,14},{12... | collective-permute-start | bytes 221192 | tf_op jit(solution)/shard_map/ppermute | solution.py:318
  8.3 4.7 %load.1 = (bf16[1024,2048]{1,0:T(8,128)(2,1)S(1)}, bf16[1024,2048]{1,0:T(8,128)(2,1)S(1)}, bf16[2048,1024]{1,0:T(8,128)(2,1)S(1)}) custom-call(bf16[1024,2048]{1,0:T(8,128)(2,1)} %refs_0_, bf16[1024,2048]{1,0:T(8,128)(2,1)} %refs_1_, bf16[2048,1024]{1,0:T(8,128)(2,1)} %refs_2_), custom_call_target="tpu_custom_call" | custom-call | tf_op jit(solution)/shard_map/load/pallas_call | solution.py:111
  13.1 1.9 %collective-permute-done.1.refs_2_ = bf16[36,1024]{1,0:T(8,128)(2,1)S(1)} collective-permute-done((bf16[36,1024]{1,0:T(8,128)(2,1)S(1)}, bf16[36,1024]{1,0:T(8,128)(2,1)S(1)}, u32[]{:S(2)}, u32[]{:S(2)}) %collective-permute-start.1) | collective-permute-done | bytes 73760 | tf_op jit(solution)/shard_map/ppermute | solution.py:318
  15.0 1.6 %collective-permute-start.3 = (bf16[144,1024]{1,0:T(8,128)(2,1)S(1)}, bf16[144,1024]{1,0:T(8,128)(2,1)S(1)}, u32[]{:S(2)}, u32[]{:S(2)}) collective-permute-start(bf16[144,1024]{1,0:T(8,128)(2,1)S(1)} %join.2.refs_0_.refs_4_), channel_id=1, source_target_pairs={{0,1},{1,0},{2,3},{3,2},{4,5},{5,4},{6,7},{7,6},{8,9},{9,8},{10,11... | collective-permute-start | bytes 884744 | tf_op jit(solution)/shard_map/ppermute | solution.py:313
  16.6 1.5 %collective-permute-start.4 = (bf16[144,1024]{1,0:T(8,128)(2,1)S(1)}, bf16[144,1024]{1,0:T(8,128)(2,1)S(1)}, u32[]{:S(2)}, u32[]{:S(2)}) collective-permute-start(bf16[144,1024]{1,0:T(8,128)(2,1)S(1)} %join.2.refs_0_.refs_4_), channel_id=1, source_target_pairs={{0,16},{16,0},{1,17},{17,1},{2,18},{18,2},{3,19},{19,3},{4,20},{20... | collective-permute-start | bytes 884744 | tf_op jit(solution)/shard_map/ppermute | solution.py:313
  18.1 1.4 %collective-permute-start.10 = (bf16[36,1024]{1,0:T(8,128)(2,1)S(1)}, bf16[36,1024]{1,0:T(8,128)(2,1)S(1)}, u32[]{:S(2)}, u32[]{:S(2)}) collective-permute-start(bf16[36,1024]{1,0:T(8,128)(2,1)S(1)} %get-tuple-element.79), channel_id=1, source_target_pairs={{0,2},{2,0},{4,6},{6,4},{1,3},{3,1},{5,7},{7,5},{8,10},{10,8},{12,... | collective-permute-start | bytes 221192 | tf_op jit(solution)/shard_map/ppermute | solution.py:318
  19.5 1.6 %collective-permute-start.11 = (bf16[36,1024]{1,0:T(8,128)(2,1)S(1)}, bf16[36,1024]{1,0:T(8,128)(2,1)S(1)}, u32[]{:S(2)}, u32[]{:S(2)}) collective-permute-start(bf16[36,1024]{1,0:T(8,128)(2,1)S(1)} %get-tuple-element.80), channel_id=1, source_target_pairs={{0,4},{2,6},{4,0},{6,2},{1,5},{3,7},{5,1},{7,3},{8,12},{10,14},{12... | collective-permute-start | bytes 221192 | tf_op jit(solution)/shard_map/ppermute | solution.py:318
  21.1 1.3 %collective-permute-start.12 = (bf16[36,1024]{1,0:T(8,128)(2,1)S(1)}, bf16[36,1024]{1,0:T(8,128)(2,1)S(1)}, u32[]{:S(2)}, u32[]{:S(2)}) collective-permute-start(bf16[36,1024]{1,0:T(8,128)(2,1)S(1)} %get-tuple-element.81), channel_id=1, source_target_pairs={{0,6},{2,4},{4,2},{6,0},{1,7},{3,5},{5,3},{7,1},{8,14},{10,12},{12... | collective-permute-start | bytes 221192 | tf_op jit(solution)/shard_map/ppermute | solution.py:318
  22.5 3.7 %forward_down.2 = (bf16[144,2048]{1,0:T(8,128)(2,1)S(1)}, bf16[144,2048]{1,0:T(8,128)(2,1)S(1)}, bf16[144,1024]{1,0:T(8,128)(2,1)S(1)}) custom-call(bf16[144,1024]{1,0:T(8,128)(2,1)S(1)} %join.2.refs_0_.refs_4_, bf16[1024,2048]{1,0:T(8,128)(2,1)S(1)} %get-tuple-element.54.refs_1_.refs_2_, bf16[1024,2048]{1,0:T(8,128)(2,1)S(1)} %get-tuple-element.59.refs_2_.refs_3_, ...), custom_call_target="tpu_custom_call" | custom-call | tf_op jit(solution)/shard_map/forward_down/pallas_call | solution.py:176
  26.3 1.2 %collective-permute-done.12.refs_3_ = bf16[36,1024]{1,0:T(8,128)(2,1)S(1)} collective-permute-done((bf16[36,1024]{1,0:T(8,128)(2,1)S(1)}, bf16[36,1024]{1,0:T(8,128)(2,1)S(1)}, u32[]{:S(2)}, u32[]{:S(2)}) %collective-permute-start.12) | collective-permute-done | bytes 73760 | tf_op jit(solution)/shard_map/ppermute | solution.py:318
  28.6 1.5 %collective-permute-start.6 = (bf16[144,1024]{1,0:T(8,128)(2,1)S(1)}, bf16[144,1024]{1,0:T(8,128)(2,1)S(1)}, u32[]{:S(2)}, u32[]{:S(2)}) collective-permute-start(bf16[144,1024]{1,0:T(8,128)(2,1)S(1)} %collective-permute-done.3.refs_0_.refs_1_.refs_5_), channel_id=1, source_target_pairs={{0,16},{16,0},{1,17},{17,1},{2,18},{18,2},{3,19},{19,3},{4,20},{20... | collective-permute-start | bytes 884744 | tf_op jit(solution)/shard_map/ppermute | solution.py:313
  30.1 4.4 %forward_down.3 = (bf16[144,2048]{1,0:T(8,128)(2,1)S(1)}, bf16[144,2048]{1,0:T(8,128)(2,1)S(1)}, bf16[144,1024]{1,0:T(8,128)(2,1)}) custom-call(bf16[144,1024]{1,0:T(8,128)(2,1)S(1)} %collective-permute-done.3.refs_0_.refs_1_.refs_5_, bf16[1024,2048]{1,0:T(8,128)(2,1)S(1)} %get-tuple-element.54.refs_1_.refs_2_, ...), custom_call_target="tpu_custom_call" | custom-call | tf_op jit(solution)/shard_map/forward_down/pallas_call | solution.py:176
  34.6 0.8 %copy-done.6 = bf16[144,2048]{1,0:T(8,128)(2,1)} copy-done((bf16[144,2048]{1,0:T(8,128)(2,1)}, bf16[144,2048]{1,0:T(8,128)(2,1)S(1)}, u32[]{:S(2)}) %copy-start.6) | copy-done | bytes 589848
  35.4 1.5 %collective-permute-start.5 = (bf16[144,1024]{1,0:T(8,128)(2,1)}, bf16[144,1024]{1,0:T(8,128)(2,1)}, u32[]{:S(2)}, u32[]{:S(2)}) collective-permute-start(bf16[144,1024]{1,0:T(8,128)(2,1)} %get-tuple-element.65), channel_id=1, source_target_pairs={{0,1},{1,0},{2,3},{3,2},{4,5},{5,4},{6,7},{7,6},{8,9},{9,8},{10,11... | collective-permute-start | bytes 884744 | tf_op jit(solution)/shard_map/ppermute | solution.py:313
  37.0 0.7 copy-done.8
  38.3 4.4 %collective-permute-done.6.refs_1_.refs_3_.refs_7_ = bf16[144,1024]{1,0:T(8,128)(2,1)S(1)} collective-permute-done((bf16[144,1024]{1,0:T(8,128)(2,1)S(1)}, bf16[144,1024]{1,0:T(8,128)(2,1)S(1)}, u32[]{:S(2)}, u32[]{:S(2)}) %collective-permute-start.6) | collective-permute-done | bytes 294944 | tf_op jit(solution)/shard_map/ppermute | solution.py:313
  42.6 2.2 %copy-done.3 = bf16[1024,2048]{1,0:T(8,128)(2,1)S(1)} copy-done((bf16[1024,2048]{1,0:T(8,128)(2,1)S(1)}, bf16[1024,2048]{1,0:T(8,128)(2,1)}, u32[]{:S(2)}) %copy-start.3) | copy-done | bytes 4194328
  44.8 2.2 %copy-done.5 = bf16[1024,2048]{1,0:T(8,128)(2,1)S(1)} copy-done((bf16[1024,2048]{1,0:T(8,128)(2,1)S(1)}, bf16[1024,2048]{1,0:T(8,128)(2,1)}, u32[]{:S(2)}) %copy-start.5) | copy-done | bytes 4194328
  47.0 3.8 %forward.1 = (bf16[288,2048]{1,0:T(8,128)(2,1)S(1)}, bf16[288,2048]{1,0:T(8,128)(2,1)S(1)}) custom-call(bf16[144,1024]{1,0:T(8,128)(2,1)S(1)} %collective-permute-done.4.refs_0_.refs_2_.refs_6_, bf16[144,1024]{1,0:T(8,128)(2,1)S(1)} %collective-permute-done.6.refs_1_.refs_3_.refs_7_, bf16[1024,2048]{1,0:T(8,128)(2,1)S(1)} %copy-done.3, ...), custom_call_target="tpu_custom_call" | custom-call | tf_op jit(solution)/shard_map/forward/pallas_call | solution.py:176
  50.8 1.1 %combine.1 = (bf16[36,1024]{1,0:T(8,128)(2,1)S(1)}, bf16[36,1024]{1,0:T(8,128)(2,1)S(1)}, bf16[36,1024]{1,0:T(8,128)(2,1)S(1)}, bf16[36,1024]{1,0:T(8,128)(2,1)S(1)}) custom-call(bf16[144,1024]{1,0:T(8,128)(2,1)S(1)} %copy-done.11, bf16[144,1024]{1,0:T(8,128)(2,1)} %collective-permute-done.5.theirs_ref), custom_call_target="tpu_custom_call" | custom-call | tf_op jit(solution)/shard_map/combine/pallas_call | solution.py:286
  51.9 2.4 %collective-permute-start.7 = (bf16[36,1024]{1,0:T(8,128)(2,1)S(1)}, bf16[36,1024]{1,0:T(8,128)(2,1)S(1)}, u32[]{:S(2)}, u32[]{:S(2)}) collective-permute-start(bf16[36,1024]{1,0:T(8,128)(2,1)S(1)} %get-tuple-element.70), channel_id=1, source_target_pairs={{0,2},{2,0},{4,6},{6,4},{1,3},{3,1},{5,7},{7,5},{8,10},{10,8},{12,... | collective-permute-start | bytes 221192 | tf_op jit(solution)/shard_map/ppermute | solution.py:318
  54.3 0.6 collective-permute-start.8
  54.9 1.8 %collective-permute-start.9 = (bf16[36,1024]{1,0:T(8,128)(2,1)S(1)}, bf16[36,1024]{1,0:T(8,128)(2,1)S(1)}, u32[]{:S(2)}, u32[]{:S(2)}) collective-permute-start(bf16[36,1024]{1,0:T(8,128)(2,1)S(1)} %get-tuple-element.72), channel_id=1, source_target_pairs={{0,6},{2,4},{4,2},{6,0},{1,7},{3,5},{5,3},{7,1},{8,14},{10,12},{12... | collective-permute-start | bytes 221192 | tf_op jit(solution)/shard_map/ppermute | solution.py:318
  56.8 0.8 %turn.1.xt_ref = bf16[512,576]{1,0:T(8,128)(2,1)S(1)} custom-call(s32[2]{0:T(128)S(1)} %pad_add_fusion.where_ref, bf16[144,1024]{1,0:T(8,128)(2,1)S(1)} %join.2.refs_0_.refs_4_, bf16[144,1024]{1,0:T(8,128)(2,1)S(1)} %collective-permute-done.3.refs_0_.refs_1_.refs_5_, bf16[144,1024]{1,0:T(8,128)(2,1)S(1)} %collective-permute-done.4.refs_0_.refs_2_.refs_6_, ...), custom_call_target="tpu_custom_call" | custom-call | tf_op jit(solution)/shard_map/turn/pallas_call | solution.py:197
  57.6 3.7 %collective-permute-done.8.refs_2_ = bf16[36,1024]{1,0:T(8,128)(2,1)S(1)} collective-permute-done((bf16[36,1024]{1,0:T(8,128)(2,1)S(1)}, bf16[36,1024]{1,0:T(8,128)(2,1)S(1)}, u32[]{:S(2)}, u32[]{:S(2)}) %collective-permute-start.8) | collective-permute-done | bytes 73760 | tf_op jit(solution)/shard_map/ppermute | solution.py:318
  61.3 5.8 %backward.2 = (bf16[512,1024]{1,0:T(8,128)(2,1)S(1)}, bf16[512,1024]{1,0:T(8,128)(2,1)S(1)}) custom-call(bf16[512,576]{1,0:T(8,128)(2,1)S(1)} %turn.1.xt_ref, bf16[144,1024]{1,0:T(8,128)(2,1)S(1)} %join.3.refs_0_, bf16[144,1024]{1,0:T(8,128)(2,1)S(1)} %collective-permute-done.13.refs_1_, bf16[144,1024]{1,0:T(8,128)(2,1)S(1)} %copy-done.9, ...), custom_call_target="tpu_custom_call" | custom-call | tf_op jit(solution)/shard_map/backward/pallas_call | solution.py:240
  67.2 5.8 %backward.3 = (bf16[512,1024]{1,0:T(8,128)(2,1)S(1)}, bf16[512,1024]{1,0:T(8,128)(2,1)S(1)}) custom-call(bf16[512,576]{1,0:T(8,128)(2,1)S(1)} %turn.1.xt_ref, bf16[144,1024]{1,0:T(8,128)(2,1)S(1)} %join.3.refs_0_, bf16[144,1024]{1,0:T(8,128)(2,1)S(1)} %collective-permute-done.13.refs_1_, bf16[144,1024]{1,0:T(8,128)(2,1)S(1)} %copy-done.9, ...), custom_call_target="tpu_custom_call" | custom-call | tf_op jit(solution)/shard_map/backward/pallas_call | solution.py:240
  73.6 1.0 %unpack.1 = bf16[128,1024]{1,0:T(8,128)(2,1)} custom-call(bf16[144,128]{1,0:T(8,128)(2,1)S(1)} %copy-done.13, bf16[36,1024]{1,0:T(8,128)(2,1)S(1)} %get-tuple-element.69.refs_0_, bf16[36,1024]{1,0:T(8,128)(2,1)S(1)} %collective-permute-done.7.refs_1_, bf16[36,1024]{1,0:T(8,128)(2,1)S(1)} %collective-permute-done.8.refs_2_, ...), custom_call_target="tpu_custom_call" | custom-call | tf_op jit(solution)/shard_map/unpack/pallas_call | solution.py:303
  74.6 1.3 %collective-permute-done.17.refs_6_.refs_7_ = bf16[512,1024]{1,0:T(8,128)(2,1)S(1)} collective-permute-done((bf16[512,1024]{1,0:T(8,128)(2,1)S(1)}, bf16[512,1024]{1,0:T(8,128)(2,1)S(1)}, u32[]{:S(2)}, u32[]{:S(2)}) %collective-permute-start.17) | collective-permute-done | bytes 1048608 | tf_op jit(solution)/shard_map/ppermute | solution.py:313
  75.9 1.5 %finish.1 = (bf16[256,2048]{1,0:T(8,128)(2,1)}, bf16[256,2048]{1,0:T(8,128)(2,1)}) custom-call(bf16[512,1024]{1,0:T(8,128)(2,1)S(1)} %get-tuple-element.88.refs_0_.refs_1_, bf16[512,1024]{1,0:T(8,128)(2,1)S(1)} %get-tuple-element.88.refs_0_.refs_1_, bf16[512,1024]{1,0:T(8,128)(2,1)S(1)} %collective-permute-done.16.refs_2_.refs_3_, ...), custom_call_target="tpu_custom_call" | custom-call | tf_op jit(solution)/shard_map/finish/pallas_call | solution.py:266
  (46 shorter events, 3.3 us)
Async XLA Ops:
  2.1 0.6 copy-start.12
  2.7 10.4 %collective-permute-start = (bf16[36,1024]{1,0:T(8,128)(2,1)S(1)}, bf16[36,1024]{1,0:T(8,128)(2,1)S(1)}, u32[]{:S(2)}, u32[]{:S(2)}) collective-permute-start(bf16[36,1024]{1,0:T(8,128)(2,1)S(1)} %get-tuple-element.56), channel_id=1, source_target_pairs={{0,2},{2,0},{4,6},{6,4},{1,3},{3,1},{5,7},{7,5},{8,10},{10,8},{12,... | collective-permute-start | bytes 221192 | tf_op jit(solution)/shard_map/ppermute | solution.py:318
  5.7 9.2 %collective-permute-start.1 = (bf16[36,1024]{1,0:T(8,128)(2,1)S(1)}, bf16[36,1024]{1,0:T(8,128)(2,1)S(1)}, u32[]{:S(2)}, u32[]{:S(2)}) collective-permute-start(bf16[36,1024]{1,0:T(8,128)(2,1)S(1)} %get-tuple-element.57), channel_id=1, source_target_pairs={{0,4},{2,6},{4,0},{6,2},{1,5},{3,7},{5,1},{7,3},{8,12},{10,14},{12... | collective-permute-start | bytes 221192 | tf_op jit(solution)/shard_map/ppermute | solution.py:318
  8.3 6.6 %collective-permute-start.2 = (bf16[36,1024]{1,0:T(8,128)(2,1)S(1)}, bf16[36,1024]{1,0:T(8,128)(2,1)S(1)}, u32[]{:S(2)}, u32[]{:S(2)}) collective-permute-start(bf16[36,1024]{1,0:T(8,128)(2,1)S(1)} %get-tuple-element.58), channel_id=1, source_target_pairs={{0,6},{2,4},{4,2},{6,0},{1,7},{3,5},{5,3},{7,1},{8,14},{10,12},{12... | collective-permute-start | bytes 221192 | tf_op jit(solution)/shard_map/ppermute | solution.py:318
  13.0 17.1 %copy-start = (bf16[2048,1024]{1,0:T(8,128)(2,1)}, bf16[2048,1024]{1,0:T(8,128)(2,1)S(1)}, u32[]{:S(2)}) copy-start(bf16[2048,1024]{1,0:T(8,128)(2,1)S(1)} %get-tuple-element.60.refs_3_.refs_10_) | copy-start | bytes 12582916
  13.1 17.1 %copy-start.2 = (bf16[1024,2048]{1,0:T(8,128)(2,1)}, bf16[1024,2048]{1,0:T(8,128)(2,1)S(1)}, u32[]{:S(2)}) copy-start(bf16[1024,2048]{1,0:T(8,128)(2,1)S(1)} %get-tuple-element.54.refs_1_.refs_2_) | copy-start | bytes 12582916
  13.1 17.0 %copy-start.4 = (bf16[1024,2048]{1,0:T(8,128)(2,1)}, bf16[1024,2048]{1,0:T(8,128)(2,1)S(1)}, u32[]{:S(2)}) copy-start(bf16[1024,2048]{1,0:T(8,128)(2,1)S(1)} %get-tuple-element.59.refs_2_.refs_3_) | copy-start | bytes 12582916
  15.0 11.2 %collective-permute-start.3 = (bf16[144,1024]{1,0:T(8,128)(2,1)S(1)}, bf16[144,1024]{1,0:T(8,128)(2,1)S(1)}, u32[]{:S(2)}, u32[]{:S(2)}) collective-permute-start(bf16[144,1024]{1,0:T(8,128)(2,1)S(1)} %join.2.refs_0_.refs_4_), channel_id=1, source_target_pairs={{0,1},{1,0},{2,3},{3,2},{4,5},{5,4},{6,7},{7,6},{8,9},{9,8},{10,11... | collective-permute-start | bytes 884744 | tf_op jit(solution)/shard_map/ppermute | solution.py:313
  16.6 9.6 %collective-permute-start.4 = (bf16[144,1024]{1,0:T(8,128)(2,1)S(1)}, bf16[144,1024]{1,0:T(8,128)(2,1)S(1)}, u32[]{:S(2)}, u32[]{:S(2)}) collective-permute-start(bf16[144,1024]{1,0:T(8,128)(2,1)S(1)} %join.2.refs_0_.refs_4_), channel_id=1, source_target_pairs={{0,16},{16,0},{1,17},{17,1},{2,18},{18,2},{3,19},{19,3},{4,20},{20... | collective-permute-start | bytes 884744 | tf_op jit(solution)/shard_map/ppermute | solution.py:313
  18.1 8.2 %collective-permute-start.10 = (bf16[36,1024]{1,0:T(8,128)(2,1)S(1)}, bf16[36,1024]{1,0:T(8,128)(2,1)S(1)}, u32[]{:S(2)}, u32[]{:S(2)}) collective-permute-start(bf16[36,1024]{1,0:T(8,128)(2,1)S(1)} %get-tuple-element.79), channel_id=1, source_target_pairs={{0,2},{2,0},{4,6},{6,4},{1,3},{3,1},{5,7},{7,5},{8,10},{10,8},{12,... | collective-permute-start | bytes 221192 | tf_op jit(solution)/shard_map/ppermute | solution.py:318
  19.5 6.8 %collective-permute-start.11 = (bf16[36,1024]{1,0:T(8,128)(2,1)S(1)}, bf16[36,1024]{1,0:T(8,128)(2,1)S(1)}, u32[]{:S(2)}, u32[]{:S(2)}) collective-permute-start(bf16[36,1024]{1,0:T(8,128)(2,1)S(1)} %get-tuple-element.80), channel_id=1, source_target_pairs={{0,4},{2,6},{4,0},{6,2},{1,5},{3,7},{5,1},{7,3},{8,12},{10,14},{12... | collective-permute-start | bytes 221192 | tf_op jit(solution)/shard_map/ppermute | solution.py:318
  21.1 6.3 %collective-permute-start.12 = (bf16[36,1024]{1,0:T(8,128)(2,1)S(1)}, bf16[36,1024]{1,0:T(8,128)(2,1)S(1)}, u32[]{:S(2)}, u32[]{:S(2)}) collective-permute-start(bf16[36,1024]{1,0:T(8,128)(2,1)S(1)} %get-tuple-element.81), channel_id=1, source_target_pairs={{0,6},{2,4},{4,2},{6,0},{1,7},{3,5},{5,3},{7,1},{8,14},{10,12},{12... | collective-permute-start | bytes 221192 | tf_op jit(solution)/shard_map/ppermute | solution.py:318
  26.2 1.9 %copy-start.10 = (bf16[144,1024]{1,0:T(8,128)(2,1)}, bf16[144,1024]{1,0:T(8,128)(2,1)S(1)}, u32[]{:S(2)}) copy-start(bf16[144,1024]{1,0:T(8,128)(2,1)S(1)} %get-tuple-element.61.mine_ref) | copy-start | bytes 884740
  27.5 9.4 %collective-permute-start.13 = (bf16[144,1024]{1,0:T(8,128)(2,1)S(1)}, bf16[144,1024]{1,0:T(8,128)(2,1)S(1)}, u32[]{:S(2)}, u32[]{:S(2)}) collective-permute-start(bf16[144,1024]{1,0:T(8,128)(2,1)S(1)} %join.3.refs_0_), channel_id=1, source_target_pairs={{0,1},{1,0},{2,3},{3,2},{4,5},{5,4},{6,7},{7,6},{8,9},{9,8},{10,11... | collective-permute-start | bytes 884744 | tf_op jit(solution)/shard_map/ppermute | solution.py:313
  28.1 8.9 %collective-permute-start.14 = (bf16[144,1024]{1,0:T(8,128)(2,1)S(1)}, bf16[144,1024]{1,0:T(8,128)(2,1)S(1)}, u32[]{:S(2)}, u32[]{:S(2)}) collective-permute-start(bf16[144,1024]{1,0:T(8,128)(2,1)S(1)} %join.3.refs_0_), channel_id=1, source_target_pairs={{0,16},{16,0},{1,17},{17,1},{2,18},{18,2},{3,19},{19,3},{4,20},{20... | collective-permute-start | bytes 884744 | tf_op jit(solution)/shard_map/ppermute | solution.py:313
  28.6 14.0 %collective-permute-start.6 = (bf16[144,1024]{1,0:T(8,128)(2,1)S(1)}, bf16[144,1024]{1,0:T(8,128)(2,1)S(1)}, u32[]{:S(2)}, u32[]{:S(2)}) collective-permute-start(bf16[144,1024]{1,0:T(8,128)(2,1)S(1)} %collective-permute-done.3.refs_0_.refs_1_.refs_5_), channel_id=1, source_target_pairs={{0,16},{16,0},{1,17},{17,1},{2,18},{18,2},{3,19},{19,3},{4,20},{20... | collective-permute-start | bytes 884744 | tf_op jit(solution)/shard_map/ppermute | solution.py:313
  34.6 0.8 %copy-start.6 = (bf16[144,2048]{1,0:T(8,128)(2,1)}, bf16[144,2048]{1,0:T(8,128)(2,1)S(1)}, u32[]{:S(2)}) copy-start(bf16[144,2048]{1,0:T(8,128)(2,1)S(1)} %get-tuple-element.86.refs_8_) | copy-start | bytes 1769476
  35.4 15.4 %collective-permute-start.5 = (bf16[144,1024]{1,0:T(8,128)(2,1)}, bf16[144,1024]{1,0:T(8,128)(2,1)}, u32[]{:S(2)}, u32[]{:S(2)}) collective-permute-start(bf16[144,1024]{1,0:T(8,128)(2,1)} %get-tuple-element.65), channel_id=1, source_target_pairs={{0,1},{1,0},{2,3},{3,2},{4,5},{5,4},{6,7},{7,6},{8,9},{9,8},{10,11... | collective-permute-start | bytes 884744 | tf_op jit(solution)/shard_map/ppermute | solution.py:313
  37.0 0.7 copy-start.8
  37.7 23.6 %collective-permute-start.15 = (bf16[144,1024]{1,0:T(8,128)(2,1)S(1)}, bf16[144,1024]{1,0:T(8,128)(2,1)}, u32[]{:S(2)}, u32[]{:S(2)}) collective-permute-start(bf16[144,1024]{1,0:T(8,128)(2,1)S(1)} %collective-permute-done.13.refs_1_), channel_id=1, source_target_pairs={{0,16},{16,0},{1,17},{17,1},{2,18},{18,2},{3,19},{19,3},{4,20},{20... | collective-permute-start | bytes 884744 | tf_op jit(solution)/shard_map/ppermute | solution.py:313
  38.3 23.1 %copy-start.1 = (bf16[2048,1024]{1,0:T(8,128)(2,1)S(1)}, bf16[2048,1024]{1,0:T(8,128)(2,1)}, u32[]{:S(2)}) copy-start(bf16[2048,1024]{1,0:T(8,128)(2,1)} %copy-done) | copy-start | bytes 12582916
  42.6 2.2 %copy-start.3 = (bf16[1024,2048]{1,0:T(8,128)(2,1)S(1)}, bf16[1024,2048]{1,0:T(8,128)(2,1)}, u32[]{:S(2)}) copy-start(bf16[1024,2048]{1,0:T(8,128)(2,1)} %copy-done.2) | copy-start | bytes 12582916
  44.8 2.2 %copy-start.5 = (bf16[1024,2048]{1,0:T(8,128)(2,1)S(1)}, bf16[1024,2048]{1,0:T(8,128)(2,1)}, u32[]{:S(2)}) copy-start(bf16[1024,2048]{1,0:T(8,128)(2,1)} %copy-done.4) | copy-start | bytes 12582916
  47.0 3.8 %copy-start.11 = (bf16[144,1024]{1,0:T(8,128)(2,1)S(1)}, bf16[144,1024]{1,0:T(8,128)(2,1)}, u32[]{:S(2)}) copy-start(bf16[144,1024]{1,0:T(8,128)(2,1)} %copy-done.10) | copy-start | bytes 884740
  47.0 14.3 %copy-start.7 = (bf16[144,2048]{1,0:T(8,128)(2,1)S(1)}, bf16[144,2048]{1,0:T(8,128)(2,1)}, u32[]{:S(2)}) copy-start(bf16[144,2048]{1,0:T(8,128)(2,1)} %copy-done.6) | copy-start | bytes 1769476
  47.0 14.3 %copy-start.9 = (bf16[144,1024]{1,0:T(8,128)(2,1)S(1)}, bf16[144,1024]{1,0:T(8,128)(2,1)}, u32[]{:S(2)}) copy-start(bf16[144,1024]{1,0:T(8,128)(2,1)} %copy-done.8) | copy-start | bytes 884740
  51.9 5.7 %collective-permute-start.7 = (bf16[36,1024]{1,0:T(8,128)(2,1)S(1)}, bf16[36,1024]{1,0:T(8,128)(2,1)S(1)}, u32[]{:S(2)}, u32[]{:S(2)}) collective-permute-start(bf16[36,1024]{1,0:T(8,128)(2,1)S(1)} %get-tuple-element.70), channel_id=1, source_target_pairs={{0,2},{2,0},{4,6},{6,4},{1,3},{3,1},{5,7},{7,5},{8,10},{10,8},{12,... | collective-permute-start | bytes 221192 | tf_op jit(solution)/shard_map/ppermute | solution.py:318
  54.3 7.0 %collective-permute-start.8 = (bf16[36,1024]{1,0:T(8,128)(2,1)S(1)}, bf16[36,1024]{1,0:T(8,128)(2,1)S(1)}, u32[]{:S(2)}, u32[]{:S(2)}) collective-permute-start(bf16[36,1024]{1,0:T(8,128)(2,1)S(1)} %get-tuple-element.71), channel_id=1, source_target_pairs={{0,4},{2,6},{4,0},{6,2},{1,5},{3,7},{5,1},{7,3},{8,12},{10,14},{12... | collective-permute-start | bytes 221192 | tf_op jit(solution)/shard_map/ppermute | solution.py:318
  54.9 6.4 %collective-permute-start.9 = (bf16[36,1024]{1,0:T(8,128)(2,1)S(1)}, bf16[36,1024]{1,0:T(8,128)(2,1)S(1)}, u32[]{:S(2)}, u32[]{:S(2)}) collective-permute-start(bf16[36,1024]{1,0:T(8,128)(2,1)S(1)} %get-tuple-element.72), channel_id=1, source_target_pairs={{0,6},{2,4},{4,2},{6,0},{1,7},{3,5},{5,3},{7,1},{8,14},{10,12},{12... | collective-permute-start | bytes 221192 | tf_op jit(solution)/shard_map/ppermute | solution.py:318
  67.1 6.4 %copy-start.13 = (bf16[144,128]{1,0:T(8,128)(2,1)S(1)}, bf16[144,128]{1,0:T(8,128)(2,1)}, u32[]{:S(2)}) copy-start(bf16[144,128]{1,0:T(8,128)(2,1)} %copy-done.12) | copy-start | bytes 110596
  67.1 7.4 %collective-permute-start.16 = (bf16[512,1024]{1,0:T(8,128)(2,1)S(1)}, bf16[512,1024]{1,0:T(8,128)(2,1)S(1)}, u32[]{:S(2)}, u32[]{:S(2)}) collective-permute-start(bf16[512,1024]{1,0:T(8,128)(2,1)S(1)} %get-tuple-element.89), channel_id=1, source_target_pairs={{0,8},{8,0},{1,9},{9,1},{2,10},{10,2},{3,11},{11,3},{4,12},{12,4},... | collective-permute-start | bytes 3145736 | tf_op jit(solution)/shard_map/ppermute | solution.py:313
  73.0 2.8 %collective-permute-start.17 = (bf16[512,1024]{1,0:T(8,128)(2,1)S(1)}, bf16[512,1024]{1,0:T(8,128)(2,1)S(1)}, u32[]{:S(2)}, u32[]{:S(2)}) collective-permute-start(bf16[512,1024]{1,0:T(8,128)(2,1)S(1)} %get-tuple-element.92), channel_id=1, source_target_pairs={{0,8},{8,0},{1,9},{9,1},{2,10},{10,2},{3,11},{11,3},{4,12},{12,4},... | collective-permute-start | bytes 3145736 | tf_op jit(solution)/shard_map/ppermute | solution.py:313

commit v5 on v4

--- a/solution.py
+++ b/solution.py
@@ -43,7 +43,7 @@
     return pltpu.with_memory_space_constraint(value, pltpu.HBM)
 
 
-def pack_kernel(plane_ref, kind_ref, x_ref, g_ref, placer_ref, *refs):
+def pack_kernel(plane_ref, _, __, kind_ref, x_ref, g_ref, placer_ref, *refs):
     outs, (kind, x, g, sems) = refs[: 2 * EXPERTS], refs[2 * EXPERTS :]
     copies = [
         pltpu.make_async_copy(source, target, sems.at[i])
@@ -71,13 +71,13 @@
             outs[first + k][...] = packed[k * CAP : (k + 1) * CAP].astype(BF16)
 
 
-def pack(plane, kind, x, g):
+def pack(scalars, kind, x, g):
     tokens, width = x.shape
     return pl.pallas_call(
         pack_kernel,
         out_shape=[jax.ShapeDtypeStruct((EXPERTS * CAP, tokens), BF16)]
         + [jax.ShapeDtypeStruct((CAP, width), BF16)] * (2 * EXPERTS),
-        in_specs=[pl.BlockSpec(memory_space=pltpu.SMEM)] + [AFAR] * 3,
+        in_specs=[pl.BlockSpec(memory_space=pltpu.SMEM)] * 3 + [AFAR] * 3,
         scratch_shapes=[
             pltpu.VMEM((1, tokens), jnp.int32),
             pltpu.VMEM((tokens, width), BF16),
@@ -87,7 +87,7 @@
         compiler_params=SMALL,
         cost_estimate=CHEAP,
         name="pack",
-    )(plane, kept(kind), kept(x), kept(g))
+    )(*scalars, kept(kind), kept(x), kept(g))
 
 
 def load_kernel(pieces, *refs):
@@ -121,7 +121,7 @@
 
 
 def join_kernel(*refs):
-    refs[EXPERTS][...] = stacked(refs[:EXPERTS]).astype(BF16)
+    refs[EXPERTS][...] = stacked(refs[EXPERTS - 1 :: -1]).astype(BF16)
 
 
 def join(blocks):
@@ -132,7 +132,26 @@
         compiler_params=SMALL,
         cost_estimate=CHEAP,
         name="join",
-    )(*blocks)
+    )(*blocks[::-1])
+
+
+def flip_kernel(source_ref, target_ref):
+    @pl.loop(0, source_ref.shape[0] // STRIP)
+    def _(j):
+        rows = pl.ds(pl.multiple_of(j * STRIP, STRIP), STRIP)
+        target_ref[:, rows] = source_ref[rows, :].T
+
+
+def flip(value):
+    return pl.pallas_call(
+        flip_kernel,
+        out_shape=pltpu.VMEM(value.shape[::-1], value.dtype),
+        in_specs=[HERE],
+        out_specs=HERE,
+        compiler_params=SMALL,
+        cost_estimate=CHEAP,
+        name="flip",
+    )(value)
 
 
 def forward_kernel(n, down, *refs):
@@ -186,34 +205,34 @@
     )(*xs, wg, wu, *([wd] * down))
 
 
-def turn_kernel(where_ref, *refs):
+def turn_kernel(_, __, *refs):
     refs[8][: refs[0].shape[1], :] = stacked(refs[0:4]).T.astype(BF16)
     refs[8][refs[0].shape[1] :, :] = stacked(refs[4:8]).T.astype(BF16)
 
 
-def turn(where, xs, share):
+def turn(own, sib, xs, share):
     part = xs[0].shape[0]
     rows = len(xs) * part
     return pl.pallas_call(
         turn_kernel,
         grid_spec=pltpu.PrefetchScalarGridSpec(
-            num_scalar_prefetch=1,
+            num_scalar_prefetch=2,
             grid=(1,),
-            in_specs=[pl.BlockSpec((part, share), lambda j, w: (0, w[0]))] * 4
-            + [pl.BlockSpec((part, share), lambda j, w: (0, w[1]))] * 4,
-            out_specs=pl.BlockSpec((2 * share, rows), lambda j, w: (0, 0)),
+            in_specs=[pl.BlockSpec((part, share), lambda j, a, b: (0, a[0]))] * 4
+            + [pl.BlockSpec((part, share), lambda j, a, b: (0, b[0]))] * 4,
+            out_specs=pl.BlockSpec((2 * share, rows), lambda j, a, b: (0, 0)),
         ),
         out_shape=jax.ShapeDtypeStruct((2 * share, rows), BF16),
         compiler_params=SMALL,
         cost_estimate=CHEAP,
         name="turn",
-    )(where, *xs, *xs)
+    )(own, sib, *xs, *xs)
 
 
 def backward_kernel(first, counts, xt_ref, *refs):
     n = len(counts)
     gs, acts, coefs = refs[:4], refs[4 : 4 + n], refs[4 + n : 4 + 2 * n]
-    wd_ref, own_ref, sib_ref, g_ref = refs[4 + 2 * n :]
+    wdt_ref, own_ref, sib_ref, g_ref = refs[4 + 2 * n :]
     part = gs[0].shape[0]
     share = own_ref.shape[0] // 2
     for i in range(4):
@@ -224,7 +243,7 @@
         for i in range(PAIR // STRIP):
             here = pl.ds(pl.multiple_of(j * PAIR + i * STRIP, STRIP), STRIP)
             cols = pl.ds(pl.multiple_of(j * PAIR + i * STRIP + first, STRIP), STRIP)
-            d_hidden = contract_cols(g_ref[...], wd_ref[cols, :])
+            d_hidden = jnp.dot(g_ref[...], wdt_ref[:, cols], preferred_element_type=F32)
             for row, parts in ((0, coefs), (share, acts)):
                 factor = jnp.concatenate([p[:, cols] for p in parts], axis=0).astype(F32)
                 d_cols = (d_hidden * factor).astype(BF16)
@@ -233,7 +252,7 @@
                 sib_ref[row : row + share, here] = total[share:]
 
 
-def backward(xt, gs, acts, coefs, wd, first, cols):
+def backward(xt, gs, acts, coefs, wdt, first, cols):
     part, width = gs[0].shape
     height, rows = xt.shape
     counts = tuple(a.shape[0] for a in acts)
@@ -245,7 +264,7 @@
         compiler_params=LARGE,
         cost_estimate=CHEAP,
         name="backward",
-    )(xt, *gs, *acts, *coefs, wd)
+    )(xt, *gs, *acts, *coefs, wdt)
 
 
 def finish_kernel(*refs):
@@ -325,39 +344,45 @@
 
 
 def gathering(designs, archetype, w_gate, w_up, w_down, cotangent):
-    plane = lax.axis_index("arch").astype(jnp.int32)
-    far = lax.axis_index("far").astype(jnp.int32)
-    core = lax.axis_index("core").astype(jnp.int32)
+    far, core = lax.axis_index("far"), lax.axis_index("core")
+    scalars = [lax.axis_index("arch"), 2 * far + core, 2 * far + 1 - core]
+    scalars = [v.astype(jnp.int32)[None] for v in scalars]
     tokens, width = designs.shape
     share = width // 4
-    placer, *blocks = pack(plane[None], archetype.reshape(1, tokens), designs, cotangent)
+    placer, *blocks = pack(scalars, archetype.reshape(1, tokens), designs, cotangent)
     wg, wu, wd = load(after([w_gate, w_up, w_down], [placer]))
+    wdt = flip(wd)
 
     moved = across_planes(blocks[:EXPERTS])
-    x_own = join(after(moved[:1], [wg]) + moved[1:])
+    x_own = join(after(moved[:1], [wdt]) + moved[1:])
     x_near, x_far = after([swap(x_own, "half"), swap(x_own, "far")], [])
-    x_corner = swap(x_near, "far")
+
+    g_own = join(across_planes(blocks[EXPERTS:]))
+    g_near, g_far = after([swap(g_own, "half"), swap(g_own, "far")], [])
 
     act0, coef0, share_own = forward([x_own], wg, wu, wd)
-    moved = across_planes(after(blocks[EXPERTS:], [x_own]))
-    g_own = join(after(moved[:1], [act0, x_near, x_far]) + moved[1:])
-    g_near, g_far = after([swap(g_own, "half"), swap(g_own, "far")], [])
-    g_corner = swap(g_near, "far")
-
     (x_near,) = after([x_near], [act0])
     act1, coef1, share_near = forward([x_near], wg, wu, wd)
-    act2, coef2 = forward([x_far, x_corner], wg, wu)
-    (share_got,) = after([swap(share_near, "half")], [act2])
-    returned = across_planes(combine(share_own, share_got))
-    outputs = unpack(placer, returned)
-
-    where = jnp.stack([2 * far + core, 2 * far + 1 - core])
-    xt = turn(where, [x_own, x_near, x_far, x_corner], share)
-    gs, acts, coefs = [g_own, g_near, g_far, g_corner], [act0, act1, act2], [coef0, coef1, coef2]
+    x_pass, g_pass = after([x_near, g_far], [act1, g_near])
+    x_corner, g_corner = swap(x_pass, "far"), swap(g_pass, "half")
+    (x_far,) = after([x_far], [act1])
+    act2, coef2 = forward([x_far], wg, wu)
+    (x_corner,) = after([x_corner], [act2])
+    act3, coef3 = forward([x_corner], wg, wu)
+    xt = turn(*scalars[1:], [x_own, x_near, x_far, x_corner], share)
+
+    (share_near,) = after([share_near], [g_corner, act3])
+    share_got = swap(share_near, "half")
+    gs = [g_own, g_near, g_far, g_corner]
+    acts, coefs = [act0, act1, act2, act3], [coef0, coef1, coef2, coef3]
     half = w_down.shape[0] // 2
-    own0, sib0 = backward(xt, gs, acts, coefs, wd, 0, half)
-    (xt,) = after([xt], returned[1:])
-    own1, sib1 = backward(xt, gs, acts, coefs, wd, half, half)
+    own0, sib0 = backward(xt, gs, acts, coefs, wdt, 0, half)
+    (share_got,) = after([share_got], [own0])
+    sums = combine(share_own, share_got)
+    (xt,) = after([xt], [sums[0]])
+    own1, sib1 = backward(xt, gs, acts, coefs, wdt, half, half)
+    outputs = unpack(placer, across_planes(sums))
+    (sib1,) = after([sib1], [outputs])
     grad_gate, grad_up = finish(own0, swap(sib0, "core"), own1, swap(sib1, "core"))
     return outputs, grad_gate, grad_up
 

time: 77.7 us -> 66.9 us (0.86)
  local copies, waits for them, and re-layouts: 6.57 us -> 0 us
  Pallas kernels: 34.1 us -> 30.1 us
  starting transfers between devices: 23.2 us -> 25.8 us
  waiting for transfers between devices: 12.6 us -> 10 us
    unnamed x28 -> x0, local copies, waits for them, and re-layouts: 6.57 us -> none
    ppermute x9, waiting for transfers between devices: 6.81 us -> 0.87 us  [across_planes(): lax.ppermute(blocks[k], 'arch', [(i, i ^ k) for i in range(EXPERTS)])]
    pallas_call x2, Pallas kernels: 11.6 us -> 7.56 us  [backward(): pl.pallas_call(functools.partial(backward_kernel, first, counts), out_sha...]
    ppermute x9, waiting for transfers between devices: 5.81 us -> 9.13 us  [swap(): return lax.ppermute(value, axis, [(0, 1), (1, 0)])]
    ppermute x9, starting transfers between devices: 14.8 us -> 17.5 us  [across_planes(): lax.ppermute(blocks[k], 'arch', [(i, i ^ k) for i in range(EXPERTS)])]
    pallas_call x0 -> x1, Pallas kernels: none -> 1.61 us  [flip(): pl.pallas_call(flip_kernel, out_shape=pltpu.VMEM(value.shape[::-1], value...]
    pallas_call x1, Pallas kernels: 1.05 us -> 0.09 us  [combine(): pl.pallas_call(combine_kernel, out_shape=[jax.ShapeDtypeStruct((CAP, widt...]
    pallas_call x3 -> x4, Pallas kernels: 12 us -> 11.9 us  [forward(): pl.pallas_call(functools.partial(forward_kernel, n, down), out_shape=[jax...]
  transfers between devices with their start and end apart: 18 -> 18, of which waited for: 6 -> 6; matrix products, arithmetic and copies ran while one was open for 0% -> 0% of each run, Pallas kernels for 33% -> 41%
where the time goes in v5:
time: 66.9 us; the launch traced here: 66.7 us
  Pallas kernels  30.1 us (45%)
  starting transfers between devices  25.8 us (39%)
  waiting for transfers between devices  10 us (15%)
  between operations  0.81 us (1%)
    ppermute x9, starting transfers between devices, across_planes(): lax.ppermute(blocks[k], 'arch', [(i, i ^ k) for i in range(EXPERTS)])  17.5 us
    pallas_call x4, Pallas kernels, forward(): pl.pallas_call(functools.partial(forward_kernel, n, down), out_shape=[jax...  11.9 us
    ppermute x9, waiting for transfers between devices, swap(): return lax.ppermute(value, axis, [(0, 1), (1, 0)])  9.13 us
    ppermute x9, starting transfers between devices, swap(): return lax.ppermute(value, axis, [(0, 1), (1, 0)])  8.29 us
    pallas_call x2, Pallas kernels, backward(): pl.pallas_call(functools.partial(backward_kernel, first, counts), out_sha...  7.56 us
    pallas_call x1, Pallas kernels, load(): pl.pallas_call(functools.partial(load_kernel, pieces), out_shape=[pltpu.V...  4.7 us
    pallas_call x1, Pallas kernels, flip(): pl.pallas_call(flip_kernel, out_shape=pltpu.VMEM(value.shape[::-1], value...  1.61 us
    pallas_call x1, Pallas kernels, finish(): pl.pallas_call(finish_kernel, grid=(steps,), in_specs=[upper, lower] * 4,...  1.49 us
  transfers between devices with their start and end apart: 18, of which 6 were waited for; matrix products, arithmetic and copies ran while one was open for 0% of the time, Pallas kernels for 41%

profile of v5, /device:TPU:0, one launch (start us, length us, event | category | flops | bytes accessed | tf_op | source)
XLA Modules:
  0.0 66.7 jit_solution(6458240614593157334)
XLA Ops:
  0.6 1.5 %pack.1 = (bf16[144,128]{1,0:T(8,128)(2,1)S(1)}, bf16[36,1024]{1,0:T(8,128)(2,1)S(1)}, bf16[36,1024]{1,0:T(8,128)(2,1)S(1)}, bf16[36,1024]{1,0:T(8,128)(2,1)S(1)...) custom-call(s32[1]{0:T(128)} %bitcast.plane_ref, ...), custom_call_target="tpu_custom_call" | custom-call | tf_op jit(solution)/shard_map/pack/pallas_call | solution.py:76
  2.1 5.1 %collective-permute-start = (bf16[36,1024]{1,0:T(8,128)(2,1)S(1)}, bf16[36,1024]{1,0:T(8,128)(2,1)S(1)}, u32[]{:S(2)}, u32[]{:S(2)}) collective-permute-start(bf16[36,1024]{1,0:T(8,128)(2,1)S(1)} %get-tuple-element.53), channel_id=1, source_target_pairs={{0,6},{2,4},{4,2},{6,0},{1,7},{3,5},{5,3},{7,1},{8,14},{10,12},{12... | collective-permute-start | bytes 221192 | tf_op jit(solution)/shard_map/ppermute | solution.py:337
  7.2 0.6 collective-permute-start.2
  7.9 3.7 %collective-permute-start.5 = (bf16[36,1024]{1,0:T(8,128)(2,1)S(1)}, bf16[36,1024]{1,0:T(8,128)(2,1)S(1)}, u32[]{:S(2)}, u32[]{:S(2)}) collective-permute-start(bf16[36,1024]{1,0:T(8,128)(2,1)S(1)} %get-tuple-element.69), channel_id=1, source_target_pairs={{0,6},{2,4},{4,2},{6,0},{1,7},{3,5},{5,3},{7,1},{8,14},{10,12},{12... | collective-permute-start | bytes 221192 | tf_op jit(solution)/shard_map/ppermute | solution.py:337
  11.6 3.6 %collective-permute-start.7 = (bf16[36,1024]{1,0:T(8,128)(2,1)S(1)}, bf16[36,1024]{1,0:T(8,128)(2,1)S(1)}, u32[]{:S(2)}, u32[]{:S(2)}) collective-permute-start(bf16[36,1024]{1,0:T(8,128)(2,1)S(1)} %get-tuple-element.71), channel_id=1, source_target_pairs={{0,2},{2,0},{4,6},{6,4},{1,3},{3,1},{5,7},{7,5},{8,10},{10,8},{12,... | collective-permute-start | bytes 221192 | tf_op jit(solution)/shard_map/ppermute | solution.py:337
  15.2 4.7 %load.1 = (bf16[1024,2048]{1,0:T(8,128)(2,1)S(1)}, bf16[1024,2048]{1,0:T(8,128)(2,1)S(1)}, bf16[2048,1024]{1,0:T(8,128)(2,1)S(1)}) custom-call(bf16[1024,2048]{1,0:T(8,128)(2,1)} %refs_0_, bf16[1024,2048]{1,0:T(8,128)(2,1)} %refs_1_, bf16[2048,1024]{1,0:T(8,128)(2,1)} %refs_2_), custom_call_target="tpu_custom_call" | custom-call | tf_op jit(solution)/shard_map/load/pallas_call | solution.py:111
  19.9 1.6 %flip.1.refs_12_ = bf16[1024,2048]{1,0:T(8,128)(2,1)S(1)} custom-call(bf16[2048,1024]{1,0:T(8,128)(2,1)S(1)} %get-tuple-element.60.source_ref.refs_3_), custom_call_target="tpu_custom_call" | custom-call | tf_op jit(solution)/shard_map/flip/pallas_call | solution.py:146
  21.6 1.2 %collective-permute-start.3 = (bf16[144,1024]{1,0:T(8,128)(2,1)S(1)}, bf16[144,1024]{1,0:T(8,128)(2,1)S(1)}, u32[]{:S(2)}, u32[]{:S(2)}) collective-permute-start(bf16[144,1024]{1,0:T(8,128)(2,1)S(1)} %join.2.refs_0_.refs_4_), channel_id=1, source_target_pairs={{0,1},{1,0},{2,3},{3,2},{4,5},{5,4},{6,7},{7,6},{8,9},{9,8},{10,11... | collective-permute-start | bytes 884744 | tf_op jit(solution)/shard_map/ppermute | solution.py:332
  22.7 1.5 %collective-permute-start.4 = (bf16[144,1024]{1,0:T(8,128)(2,1)S(1)}, bf16[144,1024]{1,0:T(8,128)(2,1)S(1)}, u32[]{:S(2)}, u32[]{:S(2)}) collective-permute-start(bf16[144,1024]{1,0:T(8,128)(2,1)S(1)} %join.2.refs_0_.refs_4_), channel_id=1, source_target_pairs={{0,16},{16,0},{1,17},{17,1},{2,18},{18,2},{3,19},{19,3},{4,20},{20... | collective-permute-start | bytes 884744 | tf_op jit(solution)/shard_map/ppermute | solution.py:332
  24.3 0.6 collective-permute-start.8
  24.9 0.9 %collective-permute-start.9 = (bf16[144,1024]{1,0:T(8,128)(2,1)S(1)}, bf16[144,1024]{1,0:T(8,128)(2,1)S(1)}, u32[]{:S(2)}, u32[]{:S(2)}) collective-permute-start(bf16[144,1024]{1,0:T(8,128)(2,1)S(1)} %join.3.refs_0_), channel_id=1, source_target_pairs={{0,16},{16,0},{1,17},{17,1},{2,18},{18,2},{3,19},{19,3},{4,20},{20... | collective-permute-start | bytes 884744 | tf_op jit(solution)/shard_map/ppermute | solution.py:332
  25.8 3.8 %forward_down.2 = (bf16[144,2048]{1,0:T(8,128)(2,1)S(1)}, bf16[144,2048]{1,0:T(8,128)(2,1)S(1)}, bf16[144,1024]{1,0:T(8,128)(2,1)S(1)}) custom-call(bf16[144,1024]{1,0:T(8,128)(2,1)S(1)} %join.2.refs_0_.refs_4_, bf16[1024,2048]{1,0:T(8,128)(2,1)S(1)} %get-tuple-element.62.refs_1_, bf16[1024,2048]{1,0:T(8,128)(2,1)S(1)} %get-tuple-element.63.refs_2_, ...), custom_call_target="tpu_custom_call" | custom-call | tf_op jit(solution)/shard_map/forward_down/pallas_call | solution.py:195
  29.6 1.2 %collective-permute-done.4.refs_0_.refs_2_.refs_6_ = bf16[144,1024]{1,0:T(8,128)(2,1)S(1)} collective-permute-done((bf16[144,1024]{1,0:T(8,128)(2,1)S(1)}, bf16[144,1024]{1,0:T(8,128)(2,1)S(1)}, u32[]{:S(2)}, u32[]{:S(2)}) %collective-permute-start.4) | collective-permute-done | bytes 294944 | tf_op jit(solution)/shard_map/ppermute | solution.py:332
  30.8 3.7 %forward_down.3 = (bf16[144,2048]{1,0:T(8,128)(2,1)S(1)}, bf16[144,2048]{1,0:T(8,128)(2,1)S(1)}, bf16[144,1024]{1,0:T(8,128)(2,1)S(1)}) custom-call(bf16[144,1024]{1,0:T(8,128)(2,1)S(1)} %collective-permute-done.3.refs_0_.refs_1_.refs_5_, bf16[1024,2048]{1,0:T(8,128)(2,1)S(1)} %get-tuple-element.62.refs_1_, ...), custom_call_target="tpu_custom_call" | custom-call | tf_op jit(solution)/shard_map/forward_down/pallas_call | solution.py:195
  34.6 2.4 %collective-permute-start.11 = (bf16[144,1024]{1,0:T(8,128)(2,1)S(1)}, bf16[144,1024]{1,0:T(8,128)(2,1)S(1)}, u32[]{:S(2)}, u32[]{:S(2)}) collective-permute-start(bf16[144,1024]{1,0:T(8,128)(2,1)S(1)} %collective-permute-done.3.refs_0_.refs_1_.refs_5_), channel_id=1, source_target_pairs={{0,16},{16,0},{1,17},{17,1},{2,18},{18,2},{3,19},{19,3},{4,20},{20... | collective-permute-start | bytes 884744 | tf_op jit(solution)/shard_map/ppermute | solution.py:332
  37.0 0.7 collective-permute-start.10
  37.7 2.2 %forward.2 = (bf16[144,2048]{1,0:T(8,128)(2,1)S(1)}, bf16[144,2048]{1,0:T(8,128)(2,1)S(1)}) custom-call(bf16[144,1024]{1,0:T(8,128)(2,1)S(1)} %collective-permute-done.4.refs_0_.refs_2_.refs_6_, bf16[1024,2048]{1,0:T(8,128)(2,1)S(1)} %get-tuple-element.62.refs_1_, bf16[1024,2048]{1,0:T(8,128)(2,1)S(1)} %get-tuple-element.63.refs_2_), custom_call_target="tpu_custom_call" | custom-call | tf_op jit(solution)/shard_map/forward/pallas_call | solution.py:195
  39.9 1.8 %collective-permute-done.11.refs_0_.refs_3_.refs_7_ = bf16[144,1024]{1,0:T(8,128)(2,1)S(1)} collective-permute-done((bf16[144,1024]{1,0:T(8,128)(2,1)S(1)}, bf16[144,1024]{1,0:T(8,128)(2,1)S(1)}, u32[]{:S(2)}, u32[]{:S(2)}) %collective-permute-start.11) | collective-permute-done | bytes 294944 | tf_op jit(solution)/shard_map/ppermute | solution.py:332
  41.7 2.2 %forward.3 = (bf16[144,2048]{1,0:T(8,128)(2,1)S(1)}, bf16[144,2048]{1,0:T(8,128)(2,1)S(1)}) custom-call(bf16[144,1024]{1,0:T(8,128)(2,1)S(1)} %collective-permute-done.11.refs_0_.refs_3_.refs_7_, bf16[1024,2048]{1,0:T(8,128)(2,1)S(1)} %get-tuple-element.62.refs_1_, bf16[1024,2048]{1,0:T(8,128)(2,1)S(1)} %get-tuple-element.63.refs_2_), custom_call_target="tpu_custom_call" | custom-call | tf_op jit(solution)/shard_map/forward/pallas_call | solution.py:195
  43.9 1.7 %collective-permute-done.10.refs_3_ = bf16[144,1024]{1,0:T(8,128)(2,1)S(1)} collective-permute-done((bf16[144,1024]{1,0:T(8,128)(2,1)S(1)}, bf16[144,1024]{1,0:T(8,128)(2,1)S(1)}, u32[]{:S(2)}, u32[]{:S(2)}) %collective-permute-start.10) | collective-permute-done | bytes 294944 | tf_op jit(solution)/shard_map/ppermute | solution.py:332
  45.7 1.0 %collective-permute-start.12 = (bf16[144,1024]{1,0:T(8,128)(2,1)S(1)}, bf16[144,1024]{1,0:T(8,128)(2,1)S(1)}, u32[]{:S(2)}, u32[]{:S(2)}) collective-permute-start(bf16[144,1024]{1,0:T(8,128)(2,1)S(1)} %get-tuple-element.83), channel_id=1, source_target_pairs={{0,1},{1,0},{2,3},{3,2},{4,5},{5,4},{6,7},{7,6},{8,9},{9,8},{10,11... | collective-permute-start | bytes 884744 | tf_op jit(solution)/shard_map/ppermute | solution.py:332
  46.7 0.2 turn.1.xt_ref
  46.9 3.8 %backward.2 = (bf16[512,1024]{1,0:T(8,128)(2,1)S(1)}, bf16[512,1024]{1,0:T(8,128)(2,1)S(1)}) custom-call(bf16[512,576]{1,0:T(8,128)(2,1)S(1)} %turn.1.xt_ref, bf16[144,1024]{1,0:T(8,128)(2,1)S(1)} %join.3.refs_0_, bf16[144,1024]{1,0:T(8,128)(2,1)S(1)} %collective-permute-done.8.refs_1_, bf16[144,1024]{1,0:T(8,128)(2,1)S(1)} %collective-permute-done.9.refs_2_, ...), custom_call_target="tpu_custom_call" | custom-call | tf_op jit(solution)/shard_map/backward/pallas_call | solution.py:259
  50.7 1.7 %collective-permute-done.12.theirs_ref = bf16[144,1024]{1,0:T(8,128)(2,1)S(1)} collective-permute-done((bf16[144,1024]{1,0:T(8,128)(2,1)S(1)}, bf16[144,1024]{1,0:T(8,128)(2,1)S(1)}, u32[]{:S(2)}, u32[]{:S(2)}) %collective-permute-start.12) | collective-permute-done | bytes 294944 | tf_op jit(solution)/shard_map/ppermute | solution.py:332
  52.5 0.4 collective-permute-start.13
  52.9 2.4 %collective-permute-start.14 = (bf16[36,1024]{1,0:T(8,128)(2,1)S(1)}, bf16[36,1024]{1,0:T(8,128)(2,1)S(1)}, u32[]{:S(2)}, u32[]{:S(2)}) collective-permute-start(bf16[36,1024]{1,0:T(8,128)(2,1)S(1)} %get-tuple-element.92), channel_id=1, source_target_pairs={{0,4},{2,6},{4,0},{6,2},{1,5},{3,7},{5,1},{7,3},{8,12},{10,14},{12... | collective-permute-start | bytes 221192 | tf_op jit(solution)/shard_map/ppermute | solution.py:337
  55.4 1.6 %collective-permute-start.15 = (bf16[36,1024]{1,0:T(8,128)(2,1)S(1)}, bf16[36,1024]{1,0:T(8,128)(2,1)S(1)}, u32[]{:S(2)}, u32[]{:S(2)}) collective-permute-start(bf16[36,1024]{1,0:T(8,128)(2,1)S(1)} %get-tuple-element.93), channel_id=1, source_target_pairs={{0,6},{2,4},{4,2},{6,0},{1,7},{3,5},{5,3},{7,1},{8,14},{10,12},{12... | collective-permute-start | bytes 221192 | tf_op jit(solution)/shard_map/ppermute | solution.py:337
  56.9 3.8 %backward.3 = (bf16[512,1024]{1,0:T(8,128)(2,1)S(1)}, bf16[512,1024]{1,0:T(8,128)(2,1)S(1)}) custom-call(bf16[512,576]{1,0:T(8,128)(2,1)S(1)} %turn.1.xt_ref, bf16[144,1024]{1,0:T(8,128)(2,1)S(1)} %join.3.refs_0_, bf16[144,1024]{1,0:T(8,128)(2,1)S(1)} %collective-permute-done.8.refs_1_, bf16[144,1024]{1,0:T(8,128)(2,1)S(1)} %collective-permute-done.9.refs_2_, ...), custom_call_target="tpu_custom_call" | custom-call | tf_op jit(solution)/shard_map/backward/pallas_call | solution.py:259
  60.7 0.8 %collective-permute-done.15.refs_3_ = bf16[36,1024]{1,0:T(8,128)(2,1)S(1)} collective-permute-done((bf16[36,1024]{1,0:T(8,128)(2,1)S(1)}, bf16[36,1024]{1,0:T(8,128)(2,1)S(1)}, u32[]{:S(2)}, u32[]{:S(2)}) %collective-permute-start.15) | collective-permute-done | bytes 73760 | tf_op jit(solution)/shard_map/ppermute | solution.py:337
  61.6 1.0 %unpack.1 = bf16[128,1024]{1,0:T(8,128)(2,1)} custom-call(bf16[144,128]{1,0:T(8,128)(2,1)S(1)} %get-tuple-element.52.placer_ref, bf16[36,1024]{1,0:T(8,128)(2,1)S(1)} %get-tuple-element.90.refs_0_, bf16[36,1024]{1,0:T(8,128)(2,1)S(1)} %collective-permute-done.13.refs_1_, bf16[36,1024]{1,0:T(8,128)(2,1)S(1)} %collective-permute-done.14.refs_2_, ...), custom_call_target="tpu_custom_call" | custom-call | tf_op jit(solution)/shard_map/unpack/pallas_call | solution.py:322
  62.6 2.7 %collective-permute-done.17.refs_6_.refs_7_ = bf16[512,1024]{1,0:T(8,128)(2,1)S(1)} collective-permute-done((bf16[512,1024]{1,0:T(8,128)(2,1)S(1)}, bf16[512,1024]{1,0:T(8,128)(2,1)S(1)}, u32[]{:S(2)}, u32[]{:S(2)}) %collective-permute-start.17) | collective-permute-done | bytes 1048608 | tf_op jit(solution)/shard_map/ppermute | solution.py:332
  65.2 1.5 %finish.1 = (bf16[256,2048]{1,0:T(8,128)(2,1)}, bf16[256,2048]{1,0:T(8,128)(2,1)}) custom-call(bf16[512,1024]{1,0:T(8,128)(2,1)S(1)} %get-tuple-element.88.refs_0_.refs_1_, bf16[512,1024]{1,0:T(8,128)(2,1)S(1)} %get-tuple-element.88.refs_0_.refs_1_, bf16[512,1024]{1,0:T(8,128)(2,1)S(1)} %collective-permute-done.16.refs_2_.refs_3_, ...), custom_call_target="tpu_custom_call" | custom-call | tf_op jit(solution)/shard_map/finish/pallas_call | solution.py:285
  (19 shorter events, 0.2 us)
Async XLA Ops:
  2.1 9.5 %collective-permute-start = (bf16[36,1024]{1,0:T(8,128)(2,1)S(1)}, bf16[36,1024]{1,0:T(8,128)(2,1)S(1)}, u32[]{:S(2)}, u32[]{:S(2)}) collective-permute-start(bf16[36,1024]{1,0:T(8,128)(2,1)S(1)} %get-tuple-element.53), channel_id=1, source_target_pairs={{0,6},{2,4},{4,2},{6,0},{1,7},{3,5},{5,3},{7,1},{8,14},{10,12},{12... | collective-permute-start | bytes 221192 | tf_op jit(solution)/shard_map/ppermute | solution.py:337
  7.2 14.3 %collective-permute-start.1 = (bf16[36,1024]{1,0:T(8,128)(2,1)S(1)}, bf16[36,1024]{1,0:T(8,128)(2,1)S(1)}, u32[]{:S(2)}, u32[]{:S(2)}) collective-permute-start(bf16[36,1024]{1,0:T(8,128)(2,1)S(1)} %get-tuple-element.54), channel_id=1, source_target_pairs={{0,4},{2,6},{4,0},{6,2},{1,5},{3,7},{5,1},{7,3},{8,12},{10,14},{12... | collective-permute-start | bytes 221192 | tf_op jit(solution)/shard_map/ppermute | solution.py:337
  7.2 14.3 %collective-permute-start.2 = (bf16[36,1024]{1,0:T(8,128)(2,1)S(1)}, bf16[36,1024]{1,0:T(8,128)(2,1)S(1)}, u32[]{:S(2)}, u32[]{:S(2)}) collective-permute-start(bf16[36,1024]{1,0:T(8,128)(2,1)S(1)} %get-tuple-element.55), channel_id=1, source_target_pairs={{0,2},{2,0},{4,6},{6,4},{1,3},{3,1},{5,7},{7,5},{8,10},{10,8},{12,... | collective-permute-start | bytes 221192 | tf_op jit(solution)/shard_map/ppermute | solution.py:337
  7.9 16.4 %collective-permute-start.5 = (bf16[36,1024]{1,0:T(8,128)(2,1)S(1)}, bf16[36,1024]{1,0:T(8,128)(2,1)S(1)}, u32[]{:S(2)}, u32[]{:S(2)}) collective-permute-start(bf16[36,1024]{1,0:T(8,128)(2,1)S(1)} %get-tuple-element.69), channel_id=1, source_target_pairs={{0,6},{2,4},{4,2},{6,0},{1,7},{3,5},{5,3},{7,1},{8,14},{10,12},{12... | collective-permute-start | bytes 221192 | tf_op jit(solution)/shard_map/ppermute | solution.py:337
  11.6 12.7 %collective-permute-start.6 = (bf16[36,1024]{1,0:T(8,128)(2,1)S(1)}, bf16[36,1024]{1,0:T(8,128)(2,1)S(1)}, u32[]{:S(2)}, u32[]{:S(2)}) collective-permute-start(bf16[36,1024]{1,0:T(8,128)(2,1)S(1)} %get-tuple-element.70), channel_id=1, source_target_pairs={{0,4},{2,6},{4,0},{6,2},{1,5},{3,7},{5,1},{7,3},{8,12},{10,14},{12... | collective-permute-start | bytes 221192 | tf_op jit(solution)/shard_map/ppermute | solution.py:337
  11.6 12.7 %collective-permute-start.7 = (bf16[36,1024]{1,0:T(8,128)(2,1)S(1)}, bf16[36,1024]{1,0:T(8,128)(2,1)S(1)}, u32[]{:S(2)}, u32[]{:S(2)}) collective-permute-start(bf16[36,1024]{1,0:T(8,128)(2,1)S(1)} %get-tuple-element.71), channel_id=1, source_target_pairs={{0,2},{2,0},{4,6},{6,4},{1,3},{3,1},{5,7},{7,5},{8,10},{10,8},{12,... | collective-permute-start | bytes 221192 | tf_op jit(solution)/shard_map/ppermute | solution.py:337
  21.6 8.0 %collective-permute-start.3 = (bf16[144,1024]{1,0:T(8,128)(2,1)S(1)}, bf16[144,1024]{1,0:T(8,128)(2,1)S(1)}, u32[]{:S(2)}, u32[]{:S(2)}) collective-permute-start(bf16[144,1024]{1,0:T(8,128)(2,1)S(1)} %join.2.refs_0_.refs_4_), channel_id=1, source_target_pairs={{0,1},{1,0},{2,3},{3,2},{4,5},{5,4},{6,7},{7,6},{8,9},{9,8},{10,11... | collective-permute-start | bytes 884744 | tf_op jit(solution)/shard_map/ppermute | solution.py:332
  22.7 8.1 %collective-permute-start.4 = (bf16[144,1024]{1,0:T(8,128)(2,1)S(1)}, bf16[144,1024]{1,0:T(8,128)(2,1)S(1)}, u32[]{:S(2)}, u32[]{:S(2)}) collective-permute-start(bf16[144,1024]{1,0:T(8,128)(2,1)S(1)} %join.2.refs_0_.refs_4_), channel_id=1, source_target_pairs={{0,16},{16,0},{1,17},{17,1},{2,18},{18,2},{3,19},{19,3},{4,20},{20... | collective-permute-start | bytes 884744 | tf_op jit(solution)/shard_map/ppermute | solution.py:332
  24.3 10.2 %collective-permute-start.8 = (bf16[144,1024]{1,0:T(8,128)(2,1)S(1)}, bf16[144,1024]{1,0:T(8,128)(2,1)S(1)}, u32[]{:S(2)}, u32[]{:S(2)}) collective-permute-start(bf16[144,1024]{1,0:T(8,128)(2,1)S(1)} %join.3.refs_0_), channel_id=1, source_target_pairs={{0,1},{1,0},{2,3},{3,2},{4,5},{5,4},{6,7},{7,6},{8,9},{9,8},{10,11... | collective-permute-start | bytes 884744 | tf_op jit(solution)/shard_map/ppermute | solution.py:332
  24.9 9.7 %collective-permute-start.9 = (bf16[144,1024]{1,0:T(8,128)(2,1)S(1)}, bf16[144,1024]{1,0:T(8,128)(2,1)S(1)}, u32[]{:S(2)}, u32[]{:S(2)}) collective-permute-start(bf16[144,1024]{1,0:T(8,128)(2,1)S(1)} %join.3.refs_0_), channel_id=1, source_target_pairs={{0,16},{16,0},{1,17},{17,1},{2,18},{18,2},{3,19},{19,3},{4,20},{20... | collective-permute-start | bytes 884744 | tf_op jit(solution)/shard_map/ppermute | solution.py:332
  34.6 7.1 %collective-permute-start.11 = (bf16[144,1024]{1,0:T(8,128)(2,1)S(1)}, bf16[144,1024]{1,0:T(8,128)(2,1)S(1)}, u32[]{:S(2)}, u32[]{:S(2)}) collective-permute-start(bf16[144,1024]{1,0:T(8,128)(2,1)S(1)} %collective-permute-done.3.refs_0_.refs_1_.refs_5_), channel_id=1, source_target_pairs={{0,16},{16,0},{1,17},{17,1},{2,18},{18,2},{3,19},{19,3},{4,20},{20... | collective-permute-start | bytes 884744 | tf_op jit(solution)/shard_map/ppermute | solution.py:332
  37.0 8.6 %collective-permute-start.10 = (bf16[144,1024]{1,0:T(8,128)(2,1)S(1)}, bf16[144,1024]{1,0:T(8,128)(2,1)S(1)}, u32[]{:S(2)}, u32[]{:S(2)}) collective-permute-start(bf16[144,1024]{1,0:T(8,128)(2,1)S(1)} %collective-permute-done.9.refs_2_), channel_id=1, source_target_pairs={{0,1},{1,0},{2,3},{3,2},{4,5},{5,4},{6,7},{7,6},{8,9},{9,8},{10,11... | collective-permute-start | bytes 884744 | tf_op jit(solution)/shard_map/ppermute | solution.py:332
  45.7 6.7 %collective-permute-start.12 = (bf16[144,1024]{1,0:T(8,128)(2,1)S(1)}, bf16[144,1024]{1,0:T(8,128)(2,1)S(1)}, u32[]{:S(2)}, u32[]{:S(2)}) collective-permute-start(bf16[144,1024]{1,0:T(8,128)(2,1)S(1)} %get-tuple-element.83), channel_id=1, source_target_pairs={{0,1},{1,0},{2,3},{3,2},{4,5},{5,4},{6,7},{7,6},{8,9},{9,8},{10,11... | collective-permute-start | bytes 884744 | tf_op jit(solution)/shard_map/ppermute | solution.py:332
  52.5 8.2 %collective-permute-start.13 = (bf16[36,1024]{1,0:T(8,128)(2,1)S(1)}, bf16[36,1024]{1,0:T(8,128)(2,1)S(1)}, u32[]{:S(2)}, u32[]{:S(2)}) collective-permute-start(bf16[36,1024]{1,0:T(8,128)(2,1)S(1)} %get-tuple-element.91), channel_id=1, source_target_pairs={{0,2},{2,0},{4,6},{6,4},{1,3},{3,1},{5,7},{7,5},{8,10},{10,8},{12,... | collective-permute-start | bytes 221192 | tf_op jit(solution)/shard_map/ppermute | solution.py:337
  52.9 7.8 %collective-permute-start.14 = (bf16[36,1024]{1,0:T(8,128)(2,1)S(1)}, bf16[36,1024]{1,0:T(8,128)(2,1)S(1)}, u32[]{:S(2)}, u32[]{:S(2)}) collective-permute-start(bf16[36,1024]{1,0:T(8,128)(2,1)S(1)} %get-tuple-element.92), channel_id=1, source_target_pairs={{0,4},{2,6},{4,0},{6,2},{1,5},{3,7},{5,1},{7,3},{8,12},{10,14},{12... | collective-permute-start | bytes 221192 | tf_op jit(solution)/shard_map/ppermute | solution.py:337
  55.4 6.2 %collective-permute-start.15 = (bf16[36,1024]{1,0:T(8,128)(2,1)S(1)}, bf16[36,1024]{1,0:T(8,128)(2,1)S(1)}, u32[]{:S(2)}, u32[]{:S(2)}) collective-permute-start(bf16[36,1024]{1,0:T(8,128)(2,1)S(1)} %get-tuple-element.93), channel_id=1, source_target_pairs={{0,6},{2,4},{4,2},{6,0},{1,7},{3,5},{5,3},{7,1},{8,14},{10,12},{12... | collective-permute-start | bytes 221192 | tf_op jit(solution)/shard_map/ppermute | solution.py:337
  56.9 5.6 %collective-permute-start.16 = (bf16[512,1024]{1,0:T(8,128)(2,1)S(1)}, bf16[512,1024]{1,0:T(8,128)(2,1)S(1)}, u32[]{:S(2)}, u32[]{:S(2)}) collective-permute-start(bf16[512,1024]{1,0:T(8,128)(2,1)S(1)} %get-tuple-element.94), channel_id=1, source_target_pairs={{0,8},{8,0},{1,9},{9,1},{2,10},{10,2},{3,11},{11,3},{4,12},{12,4},... | collective-permute-start | bytes 3145736 | tf_op jit(solution)/shard_map/ppermute | solution.py:332
  62.6 2.7 %collective-permute-start.17 = (bf16[512,1024]{1,0:T(8,128)(2,1)S(1)}, bf16[512,1024]{1,0:T(8,128)(2,1)S(1)}, u32[]{:S(2)}, u32[]{:S(2)}) collective-permute-start(bf16[512,1024]{1,0:T(8,128)(2,1)S(1)} %get-tuple-element.98), channel_id=1, source_target_pairs={{0,8},{8,0},{1,9},{9,1},{2,10},{10,2},{3,11},{11,3},{4,12},{12,4},... | collective-permute-start | bytes 3145736 | tf_op jit(solution)/shard_map/ppermute | solution.py:332

commit v6 on v5

--- a/solution.py
+++ b/solution.py
@@ -90,36 +90,6 @@
     )(*scalars, kept(kind), kept(x), kept(g))
 
 
-def load_kernel(pieces, *refs):
-    n = len(refs) // 2
-    sems = refs[2 * n]
-    copies = []
-    for i in range(n):
-        lines = refs[i].shape[0] // pieces
-        for j in range(pieces):
-            rows = pl.ds(j * lines, lines)
-            copies.append(
-                pltpu.make_async_copy(refs[i].at[rows], refs[n + i].at[rows], sems.at[i * pieces + j])
-            )
-    for copy in copies:
-        copy.start()
-    for copy in copies:
-        copy.wait()
-
-
-def load(arrays, pieces=4):
-    return pl.pallas_call(
-        functools.partial(load_kernel, pieces),
-        out_shape=[pltpu.VMEM(a.shape, a.dtype) for a in arrays],
-        in_specs=[AFAR] * len(arrays),
-        out_specs=[HERE] * len(arrays),
-        scratch_shapes=[pltpu.SemaphoreType.DMA((len(arrays) * pieces,))],
-        compiler_params=SMALL,
-        cost_estimate=CHEAP,
-        name="load",
-    )(*[kept(a) for a in arrays])
-
-
 def join_kernel(*refs):
     refs[EXPERTS][...] = stacked(refs[EXPERTS - 1 :: -1]).astype(BF16)
 
@@ -154,24 +124,37 @@
     )(value)
 
 
-def forward_kernel(n, down, *refs):
-    xs, refs = refs[:n], refs[n:]
+def forward_kernel(down, fetch, x_ref, *refs):
+    if fetch:
+        sources, refs = refs[:3], refs[3:]
+        act_ref, coef_ref, share_ref, wg_ref, wu_ref, wd_ref, acc_ref, sems = refs
+        targets = (wg_ref, wu_ref, wd_ref)
+    elif down:
+        wg_ref, wu_ref, wd_ref, act_ref, coef_ref, share_ref, acc_ref = refs
+    else:
+        wg_ref, wu_ref, act_ref, coef_ref = refs
+    steps = wg_ref.shape[1] // PAIR
+
+    def copies(j):
+        cols = pl.ds(pl.multiple_of(j * PAIR, PAIR), PAIR)
+        views = ((slice(None), cols), (slice(None), cols), (cols, slice(None)))
+        return [
+            pltpu.make_async_copy(source.at[view], target.at[view], sems.at[j, i])
+            for i, (source, target, view) in enumerate(zip(sources, targets, views))
+        ]
+
+    if fetch:
+        for j in range(steps):
+            for copy in copies(j):
+                copy.start()
     if down:
-        wg_ref, wu_ref, wd_ref, act_ref, coef_ref, share_ref = refs[:6]
-        acc_ref = refs[6]
         acc_ref[...] = jnp.zeros_like(acc_ref)
-    else:
-        wg_ref, wu_ref, act_ref, coef_ref = refs[:4]
-    if n == 1:
-        x_ref = xs[0]
-    else:
-        x_ref = refs[-1]
-        part = xs[0].shape[0]
-        for i in range(n):
-            x_ref[i * part : (i + 1) * part, :] = xs[i][...]
-
-    @pl.loop(0, wg_ref.shape[1] // PAIR)
+
+    @pl.loop(0, steps)
     def _(j):
+        if fetch:
+            for copy in copies(j):
+                copy.wait()
         for i in range(PAIR // STRIP):
             cols = pl.ds(pl.multiple_of(j * PAIR + i * STRIP, STRIP), STRIP)
             gate = jnp.dot(x_ref[...], wg_ref[:, cols], preferred_element_type=F32)
@@ -187,22 +170,22 @@
         share_ref[...] = acc_ref[...].astype(BF16)
 
 
-def forward(xs, wg, wu, wd=None):
-    n, (part, width) = len(xs), xs[0].shape
-    cols = wg.shape[1]
-    rows = n * part
+def forward(x, wg, wu, wd=None, fetch=False):
+    (rows, width), cols = x.shape, wg.shape[1]
     down = wd is not None
-    return pl.pallas_call(
-        functools.partial(forward_kernel, n, down),
+    weights = [wg, wu, wd][: 2 + down]
+    return pl.pallas_call(
+        functools.partial(forward_kernel, down, fetch),
         out_shape=[jax.ShapeDtypeStruct((rows, cols), BF16)] * 2
-        + [jax.ShapeDtypeStruct((rows, width), BF16)] * down,
-        in_specs=[HERE] * (n + 2 + down),
+        + [jax.ShapeDtypeStruct((rows, width), BF16)] * down
+        + [pltpu.VMEM(w.shape, w.dtype) for w in weights] * fetch,
+        in_specs=[HERE] + [AFAR if fetch else HERE] * len(weights),
         scratch_shapes=[pltpu.VMEM((rows, width), F32)] * down
-        + [pltpu.VMEM((rows, width), BF16)] * (n > 1),
+        + [pltpu.SemaphoreType.DMA((cols // PAIR, 3))] * fetch,
         compiler_params=LARGE,
         cost_estimate=CHEAP,
-        name="forward_down" if down else "forward",
-    )(*xs, wg, wu, *([wd] * down))
+        name="forward_fetch" if fetch else "forward_down" if down else "forward",
+    )(x, *([kept(w) for w in weights] if fetch else weights))
 
 
 def turn_kernel(_, __, *refs):
@@ -350,25 +333,24 @@
     tokens, width = designs.shape
     share = width // 4
     placer, *blocks = pack(scalars, archetype.reshape(1, tokens), designs, cotangent)
-    wg, wu, wd = load(after([w_gate, w_up, w_down], [placer]))
-    wdt = flip(wd)
-
     moved = across_planes(blocks[:EXPERTS])
-    x_own = join(after(moved[:1], [wdt]) + moved[1:])
+    x_own = join(moved)
     x_near, x_far = after([swap(x_own, "half"), swap(x_own, "far")], [])
 
-    g_own = join(across_planes(blocks[EXPERTS:]))
+    moved = across_planes(blocks[EXPERTS:])
+    g_own = join(after(moved[:1], [x_own]) + moved[1:])
     g_near, g_far = after([swap(g_own, "half"), swap(g_own, "far")], [])
 
-    act0, coef0, share_own = forward([x_own], wg, wu, wd)
+    act0, coef0, share_own, wg, wu, wd = forward(x_own, w_gate, w_up, w_down, fetch=True)
     (x_near,) = after([x_near], [act0])
-    act1, coef1, share_near = forward([x_near], wg, wu, wd)
-    x_pass, g_pass = after([x_near, g_far], [act1, g_near])
+    act1, coef1, share_near = forward(x_near, wg, wu, wd)
+    x_pass, g_pass = after([x_near, g_far], [act0, g_near])
     x_corner, g_corner = swap(x_pass, "far"), swap(g_pass, "half")
     (x_far,) = after([x_far], [act1])
-    act2, coef2 = forward([x_far], wg, wu)
-    (x_corner,) = after([x_corner], [act2])
-    act3, coef3 = forward([x_corner], wg, wu)
+    act2, coef2 = forward(x_far, wg, wu)
+    wdt = flip(after([wd], [act2])[0])
+    (x_corner,) = after([x_corner], [act2, wdt])
+    act3, coef3 = forward(x_corner, wg, wu)
     xt = turn(*scalars[1:], [x_own, x_near, x_far, x_corner], share)
 
     (share_near,) = after([share_near], [g_corner, act3])
@@ -381,8 +363,9 @@
     sums = combine(share_own, share_got)
     (xt,) = after([xt], [sums[0]])
     own1, sib1 = backward(xt, gs, acts, coefs, wdt, half, half)
-    outputs = unpack(placer, across_planes(sums))
-    (sib1,) = after([sib1], [outputs])
+    returned = across_planes(sums)
+    (sib1,) = after([sib1], returned[1:])
+    outputs = unpack(placer, returned)
     grad_gate, grad_up = finish(own0, swap(sib0, "core"), own1, swap(sib1, "core"))
     return outputs, grad_gate, grad_up
 

time: 66.9 us -> 65.9 us (0.985)
  Pallas kernels: 30.1 us -> 27.4 us
  starting transfers between devices: 25.8 us -> 26.8 us
  waiting for transfers between devices: 10 us -> 10.7 us
    ppermute x9, waiting for transfers between devices: 0.87 us -> 4.96 us  [across_planes(): lax.ppermute(blocks[k], 'arch', [(i, i ^ k) for i in range(EXPERTS)])]
    ppermute x9, waiting for transfers between devices: 9.13 us -> 5.79 us  [swap(): return lax.ppermute(value, axis, [(0, 1), (1, 0)])]
    pallas_call x5 -> x4, Pallas kernels: 16.6 us -> 13.9 us  [forward(): pl.pallas_call(functools.partial(forward_kernel, down, fetch), out_shape=...]
    ppermute x9, starting transfers between devices: 8.29 us -> 9.31 us  [swap(): return lax.ppermute(value, axis, [(0, 1), (1, 0)])]
  transfers between devices with their start and end apart: 18 -> 18, of which waited for: 6 -> 6; matrix products, arithmetic and copies ran while one was open for 0% -> 0% of each run, Pallas kernels for 41% -> 37%
where the time goes in v6:
time: 65.9 us; the launch traced here: 65.7 us
  Pallas kernels  27.4 us (42%)
  starting transfers between devices  26.8 us (41%)
  waiting for transfers between devices  10.7 us (16%)
  between operations  0.8 us (1%)
    ppermute x9, starting transfers between devices, across_planes(): lax.ppermute(blocks[k], 'arch', [(i, i ^ k) for i in range(EXPERTS)])  17.5 us
    pallas_call x4, Pallas kernels, forward(): pl.pallas_call(functools.partial(forward_kernel, down, fetch), out_shape=...  13.9 us
    ppermute x9, starting transfers between devices, swap(): return lax.ppermute(value, axis, [(0, 1), (1, 0)])  9.31 us
    pallas_call x2, Pallas kernels, backward(): pl.pallas_call(functools.partial(backward_kernel, first, counts), out_sha...  7.56 us
    ppermute x9, waiting for transfers between devices, swap(): return lax.ppermute(value, axis, [(0, 1), (1, 0)])  5.79 us
    ppermute x9, waiting for transfers between devices, across_planes(): lax.ppermute(blocks[k], 'arch', [(i, i ^ k) for i in range(EXPERTS)])  4.96 us
    pallas_call x1, Pallas kernels, flip(): pl.pallas_call(flip_kernel, out_shape=pltpu.VMEM(value.shape[::-1], value...  1.61 us
    pallas_call x1, Pallas kernels, finish(): pl.pallas_call(finish_kernel, grid=(steps,), in_specs=[upper, lower] * 4,...  1.49 us
  transfers between devices with their start and end apart: 18, of which 6 were waited for; matrix products, arithmetic and copies ran while one was open for 0% of the time, Pallas kernels for 37%

profile of v6, /device:TPU:0, one launch (start us, length us, event | category | flops | bytes accessed | tf_op | source)
XLA Modules:
  0.0 65.7 jit_solution(394285989986728530)
XLA Ops:
  0.6 1.5 %pack.1 = (bf16[144,128]{1,0:T(8,128)(2,1)S(1)}, bf16[36,1024]{1,0:T(8,128)(2,1)S(1)}, bf16[36,1024]{1,0:T(8,128)(2,1)S(1)}, bf16[36,1024]{1,0:T(8,128)(2,1)S(1)...) custom-call(s32[1]{0:T(128)} %bitcast.plane_ref, ...), custom_call_target="tpu_custom_call" | custom-call | tf_op jit(solution)/shard_map/pack/pallas_call | solution.py:76
  2.1 5.1 %collective-permute-start = (bf16[36,1024]{1,0:T(8,128)(2,1)S(1)}, bf16[36,1024]{1,0:T(8,128)(2,1)S(1)}, u32[]{:S(2)}, u32[]{:S(2)}) collective-permute-start(bf16[36,1024]{1,0:T(8,128)(2,1)S(1)} %get-tuple-element.51), channel_id=1, source_target_pairs={{0,6},{2,4},{4,2},{6,0},{1,7},{3,5},{5,3},{7,1},{8,14},{10,12},{12... | collective-permute-start | bytes 221192 | tf_op jit(solution)/shard_map/ppermute | solution.py:320
  7.2 0.6 collective-permute-start.2
  7.9 3.7 %collective-permute-start.5 = (bf16[36,1024]{1,0:T(8,128)(2,1)S(1)}, bf16[36,1024]{1,0:T(8,128)(2,1)S(1)}, u32[]{:S(2)}, u32[]{:S(2)}) collective-permute-start(bf16[36,1024]{1,0:T(8,128)(2,1)S(1)} %get-tuple-element.63), channel_id=1, source_target_pairs={{0,6},{2,4},{4,2},{6,0},{1,7},{3,5},{5,3},{7,1},{8,14},{10,12},{12... | collective-permute-start | bytes 221192 | tf_op jit(solution)/shard_map/ppermute | solution.py:320
  11.6 3.6 %collective-permute-start.7 = (bf16[36,1024]{1,0:T(8,128)(2,1)S(1)}, bf16[36,1024]{1,0:T(8,128)(2,1)S(1)}, u32[]{:S(2)}, u32[]{:S(2)}) collective-permute-start(bf16[36,1024]{1,0:T(8,128)(2,1)S(1)} %get-tuple-element.65), channel_id=1, source_target_pairs={{0,2},{2,0},{4,6},{6,4},{1,3},{3,1},{5,7},{7,5},{8,10},{10,8},{12,... | collective-permute-start | bytes 221192 | tf_op jit(solution)/shard_map/ppermute | solution.py:320
  15.2 3.2 %collective-permute-done.1.refs_1_ = bf16[36,1024]{1,0:T(8,128)(2,1)S(1)} collective-permute-done((bf16[36,1024]{1,0:T(8,128)(2,1)S(1)}, bf16[36,1024]{1,0:T(8,128)(2,1)S(1)}, u32[]{:S(2)}, u32[]{:S(2)}) %collective-permute-start.1) | collective-permute-done | bytes 73760 | tf_op jit(solution)/shard_map/ppermute | solution.py:320
  18.5 1.4 %collective-permute-start.3 = (bf16[144,1024]{1,0:T(8,128)(2,1)S(1)}, bf16[144,1024]{1,0:T(8,128)(2,1)S(1)}, u32[]{:S(2)}, u32[]{:S(2)}) collective-permute-start(bf16[144,1024]{1,0:T(8,128)(2,1)S(1)} %join.2.x_ref.refs_0_.refs_4_), channel_id=1, source_target_pairs={{0,1},{1,0},{2,3},{3,2},{4,5},{5,4},{6,7},{7,6},{8,9},{9,8},{10,11... | collective-permute-start | bytes 884744 | tf_op jit(solution)/shard_map/ppermute | solution.py:315
  19.9 1.5 %collective-permute-start.4 = (bf16[144,1024]{1,0:T(8,128)(2,1)S(1)}, bf16[144,1024]{1,0:T(8,128)(2,1)S(1)}, u32[]{:S(2)}, u32[]{:S(2)}) collective-permute-start(bf16[144,1024]{1,0:T(8,128)(2,1)S(1)} %join.2.x_ref.refs_0_.refs_4_), channel_id=1, source_target_pairs={{0,16},{16,0},{1,17},{17,1},{2,18},{18,2},{3,19},{19,3},{4,20},{20... | collective-permute-start | bytes 884744 | tf_op jit(solution)/shard_map/ppermute | solution.py:315
  21.5 1.3 %collective-permute-start.8 = (bf16[144,1024]{1,0:T(8,128)(2,1)S(1)}, bf16[144,1024]{1,0:T(8,128)(2,1)S(1)}, u32[]{:S(2)}, u32[]{:S(2)}) collective-permute-start(bf16[144,1024]{1,0:T(8,128)(2,1)S(1)} %join.3.refs_0_), channel_id=1, source_target_pairs={{0,1},{1,0},{2,3},{3,2},{4,5},{5,4},{6,7},{7,6},{8,9},{9,8},{10,11... | collective-permute-start | bytes 884744 | tf_op jit(solution)/shard_map/ppermute | solution.py:315
  22.7 1.5 %collective-permute-start.9 = (bf16[144,1024]{1,0:T(8,128)(2,1)S(1)}, bf16[144,1024]{1,0:T(8,128)(2,1)S(1)}, u32[]{:S(2)}, u32[]{:S(2)}) collective-permute-start(bf16[144,1024]{1,0:T(8,128)(2,1)S(1)} %join.3.refs_0_), channel_id=1, source_target_pairs={{0,16},{16,0},{1,17},{17,1},{2,18},{18,2},{3,19},{19,3},{4,20},{20... | collective-permute-start | bytes 884744 | tf_op jit(solution)/shard_map/ppermute | solution.py:315
  24.2 5.7 %forward_fetch.1 = (bf16[144,2048]{1,0:T(8,128)(2,1)S(1)}, bf16[144,2048]{1,0:T(8,128)(2,1)S(1)}, bf16[144,1024]{1,0:T(8,128)(2,1)S(1)}, bf16[1024,2048]{1,0:T(8...) custom-call(bf16[144,1024]{1,0:T(8,128)(2,1)S(1)} %join.2.x_ref.refs_0_.refs_4_, ...), custom_call_target="tpu_custom_call" | custom-call | tf_op jit(solution)/shard_map/forward_fetch/pallas_call | solution.py:177
  30.0 1.6 %collective-permute-done.8.refs_1_ = bf16[144,1024]{1,0:T(8,128)(2,1)S(1)} collective-permute-done((bf16[144,1024]{1,0:T(8,128)(2,1)S(1)}, bf16[144,1024]{1,0:T(8,128)(2,1)S(1)}, u32[]{:S(2)}, u32[]{:S(2)}) %collective-permute-start.8) | collective-permute-done | bytes 294944 | tf_op jit(solution)/shard_map/ppermute | solution.py:315
  31.6 1.4 %collective-permute-done.9.refs_2_ = bf16[144,1024]{1,0:T(8,128)(2,1)S(1)} collective-permute-done((bf16[144,1024]{1,0:T(8,128)(2,1)S(1)}, bf16[144,1024]{1,0:T(8,128)(2,1)S(1)}, u32[]{:S(2)}, u32[]{:S(2)}) %collective-permute-start.9) | collective-permute-done | bytes 294944 | tf_op jit(solution)/shard_map/ppermute | solution.py:315
  32.9 1.5 %collective-permute-start.11 = (bf16[144,1024]{1,0:T(8,128)(2,1)S(1)}, bf16[144,1024]{1,0:T(8,128)(2,1)S(1)}, u32[]{:S(2)}, u32[]{:S(2)}) collective-permute-start(bf16[144,1024]{1,0:T(8,128)(2,1)S(1)} %collective-permute-done.3.x_ref.refs_1_.refs_5_), channel_id=1, source_target_pairs={{0,16},{16,0},{1,17},{17,1},{2,18},{18,2},{3,19},{19,3},{4,20},{20... | collective-permute-start | bytes 884744 | tf_op jit(solution)/shard_map/ppermute | solution.py:315
  34.4 0.5 collective-permute-start.10
  34.9 3.7 %forward_down.1 = (bf16[144,2048]{1,0:T(8,128)(2,1)S(1)}, bf16[144,2048]{1,0:T(8,128)(2,1)S(1)}, bf16[144,1024]{1,0:T(8,128)(2,1)S(1)}) custom-call(bf16[144,1024]{1,0:T(8,128)(2,1)S(1)} %collective-permute-done.3.x_ref.refs_1_.refs_5_, bf16[1024,2048]{1,0:T(8,128)(2,1)S(1)} %get-tuple-element.59.refs_0_, bf16[1024,2048]{1,0:T(8,128)(2,1)S(1)} %get-tuple-element.60.refs_1_, ...), custom_call_target="tpu_custom_call" | custom-call | tf_op jit(solution)/shard_map/forward_down/pallas_call | solution.py:177
  38.7 2.2 %forward.2 = (bf16[144,2048]{1,0:T(8,128)(2,1)S(1)}, bf16[144,2048]{1,0:T(8,128)(2,1)S(1)}) custom-call(bf16[144,1024]{1,0:T(8,128)(2,1)S(1)} %collective-permute-done.4.x_ref.refs_2_.refs_6_, bf16[1024,2048]{1,0:T(8,128)(2,1)S(1)} %get-tuple-element.59.refs_0_, bf16[1024,2048]{1,0:T(8,128)(2,1)S(1)} %get-tuple-element.60.refs_1_), custom_call_target="tpu_custom_call" | custom-call | tf_op jit(solution)/shard_map/forward/pallas_call | solution.py:177
  40.9 1.6 %flip.1.refs_12_ = bf16[1024,2048]{1,0:T(8,128)(2,1)S(1)} custom-call(bf16[2048,1024]{1,0:T(8,128)(2,1)S(1)} %get-tuple-element.76.refs_2_.source_ref), custom_call_target="tpu_custom_call" | custom-call | tf_op jit(solution)/shard_map/flip/pallas_call | solution.py:116
  42.5 2.2 %forward.3 = (bf16[144,2048]{1,0:T(8,128)(2,1)S(1)}, bf16[144,2048]{1,0:T(8,128)(2,1)S(1)}) custom-call(bf16[144,1024]{1,0:T(8,128)(2,1)S(1)} %collective-permute-done.11.x_ref.refs_3_.refs_7_, bf16[1024,2048]{1,0:T(8,128)(2,1)S(1)} %get-tuple-element.59.refs_0_, bf16[1024,2048]{1,0:T(8,128)(2,1)S(1)} %get-tuple-element.60.refs_1_), custom_call_target="tpu_custom_call" | custom-call | tf_op jit(solution)/shard_map/forward/pallas_call | solution.py:177
  44.7 1.6 %collective-permute-start.12 = (bf16[144,1024]{1,0:T(8,128)(2,1)S(1)}, bf16[144,1024]{1,0:T(8,128)(2,1)S(1)}, u32[]{:S(2)}, u32[]{:S(2)}) collective-permute-start(bf16[144,1024]{1,0:T(8,128)(2,1)S(1)} %get-tuple-element.79), channel_id=1, source_target_pairs={{0,1},{1,0},{2,3},{3,2},{4,5},{5,4},{6,7},{7,6},{8,9},{9,8},{10,11... | collective-permute-start | bytes 884744 | tf_op jit(solution)/shard_map/ppermute | solution.py:315
  46.3 0.2 turn.1.xt_ref
  46.5 3.8 %backward.2 = (bf16[512,1024]{1,0:T(8,128)(2,1)S(1)}, bf16[512,1024]{1,0:T(8,128)(2,1)S(1)}) custom-call(bf16[512,576]{1,0:T(8,128)(2,1)S(1)} %turn.1.xt_ref, bf16[144,1024]{1,0:T(8,128)(2,1)S(1)} %join.3.refs_0_, bf16[144,1024]{1,0:T(8,128)(2,1)S(1)} %collective-permute-done.8.refs_1_, bf16[144,1024]{1,0:T(8,128)(2,1)S(1)} %collective-permute-done.9.refs_2_, ...), custom_call_target="tpu_custom_call" | custom-call | tf_op jit(solution)/shard_map/backward/pallas_call | solution.py:242
  50.3 1.2 %collective-permute-done.12.theirs_ref = bf16[144,1024]{1,0:T(8,128)(2,1)S(1)} collective-permute-done((bf16[144,1024]{1,0:T(8,128)(2,1)S(1)}, bf16[144,1024]{1,0:T(8,128)(2,1)S(1)}, u32[]{:S(2)}, u32[]{:S(2)}) %collective-permute-start.12) | collective-permute-done | bytes 294944 | tf_op jit(solution)/shard_map/ppermute | solution.py:315
  51.5 0.1 combine.1
  51.6 0.1 collective-permute-start.13
  51.7 3.7 %collective-permute-start.14 = (bf16[36,1024]{1,0:T(8,128)(2,1)S(1)}, bf16[36,1024]{1,0:T(8,128)(2,1)S(1)}, u32[]{:S(2)}, u32[]{:S(2)}) collective-permute-start(bf16[36,1024]{1,0:T(8,128)(2,1)S(1)} %get-tuple-element.88), channel_id=1, source_target_pairs={{0,4},{2,6},{4,0},{6,2},{1,5},{3,7},{5,1},{7,3},{8,12},{10,14},{12... | collective-permute-start | bytes 221192 | tf_op jit(solution)/shard_map/ppermute | solution.py:320
  55.4 0.7 %collective-permute-start.15 = (bf16[36,1024]{1,0:T(8,128)(2,1)S(1)}, bf16[36,1024]{1,0:T(8,128)(2,1)S(1)}, u32[]{:S(2)}, u32[]{:S(2)}) collective-permute-start(bf16[36,1024]{1,0:T(8,128)(2,1)S(1)} %get-tuple-element.89), channel_id=1, source_target_pairs={{0,6},{2,4},{4,2},{6,0},{1,7},{3,5},{5,3},{7,1},{8,14},{10,12},{12... | collective-permute-start | bytes 221192 | tf_op jit(solution)/shard_map/ppermute | solution.py:320
  56.1 3.8 %backward.3 = (bf16[512,1024]{1,0:T(8,128)(2,1)S(1)}, bf16[512,1024]{1,0:T(8,128)(2,1)S(1)}) custom-call(bf16[512,576]{1,0:T(8,128)(2,1)S(1)} %turn.1.xt_ref, bf16[144,1024]{1,0:T(8,128)(2,1)S(1)} %join.3.refs_0_, bf16[144,1024]{1,0:T(8,128)(2,1)S(1)} %collective-permute-done.8.refs_1_, bf16[144,1024]{1,0:T(8,128)(2,1)S(1)} %collective-permute-done.9.refs_2_, ...), custom_call_target="tpu_custom_call" | custom-call | tf_op jit(solution)/shard_map/backward/pallas_call | solution.py:242
  59.9 1.7 %collective-permute-done.15.refs_3_ = bf16[36,1024]{1,0:T(8,128)(2,1)S(1)} collective-permute-done((bf16[36,1024]{1,0:T(8,128)(2,1)S(1)}, bf16[36,1024]{1,0:T(8,128)(2,1)S(1)}, u32[]{:S(2)}, u32[]{:S(2)}) %collective-permute-start.15) | collective-permute-done | bytes 73760 | tf_op jit(solution)/shard_map/ppermute | solution.py:320
  61.6 1.0 %unpack.1 = bf16[128,1024]{1,0:T(8,128)(2,1)} custom-call(bf16[144,128]{1,0:T(8,128)(2,1)S(1)} %get-tuple-element.50.placer_ref, bf16[36,1024]{1,0:T(8,128)(2,1)S(1)} %get-tuple-element.86.refs_0_, bf16[36,1024]{1,0:T(8,128)(2,1)S(1)} %collective-permute-done.13.refs_1_, bf16[36,1024]{1,0:T(8,128)(2,1)S(1)} %collective-permute-done.14.refs_2_, ...), custom_call_target="tpu_custom_call" | custom-call | tf_op jit(solution)/shard_map/unpack/pallas_call | solution.py:305
  62.6 1.7 %collective-permute-done.17.refs_6_.refs_7_ = bf16[512,1024]{1,0:T(8,128)(2,1)S(1)} collective-permute-done((bf16[512,1024]{1,0:T(8,128)(2,1)S(1)}, bf16[512,1024]{1,0:T(8,128)(2,1)S(1)}, u32[]{:S(2)}, u32[]{:S(2)}) %collective-permute-start.17) | collective-permute-done | bytes 1048608 | tf_op jit(solution)/shard_map/ppermute | solution.py:315
  64.3 1.5 %finish.1 = (bf16[256,2048]{1,0:T(8,128)(2,1)}, bf16[256,2048]{1,0:T(8,128)(2,1)}) custom-call(bf16[512,1024]{1,0:T(8,128)(2,1)S(1)} %get-tuple-element.84.refs_0_.refs_1_, bf16[512,1024]{1,0:T(8,128)(2,1)S(1)} %get-tuple-element.84.refs_0_.refs_1_, bf16[512,1024]{1,0:T(8,128)(2,1)S(1)} %collective-permute-done.16.refs_2_.refs_3_, ...), custom_call_target="tpu_custom_call" | custom-call | tf_op jit(solution)/shard_map/finish/pallas_call | solution.py:268
  (18 shorter events, 0.1 us)
Async XLA Ops:
  2.1 9.5 %collective-permute-start = (bf16[36,1024]{1,0:T(8,128)(2,1)S(1)}, bf16[36,1024]{1,0:T(8,128)(2,1)S(1)}, u32[]{:S(2)}, u32[]{:S(2)}) collective-permute-start(bf16[36,1024]{1,0:T(8,128)(2,1)S(1)} %get-tuple-element.51), channel_id=1, source_target_pairs={{0,6},{2,4},{4,2},{6,0},{1,7},{3,5},{5,3},{7,1},{8,14},{10,12},{12... | collective-permute-start | bytes 221192 | tf_op jit(solution)/shard_map/ppermute | solution.py:320
  7.2 11.2 %collective-permute-start.1 = (bf16[36,1024]{1,0:T(8,128)(2,1)S(1)}, bf16[36,1024]{1,0:T(8,128)(2,1)S(1)}, u32[]{:S(2)}, u32[]{:S(2)}) collective-permute-start(bf16[36,1024]{1,0:T(8,128)(2,1)S(1)} %get-tuple-element.52), channel_id=1, source_target_pairs={{0,4},{2,6},{4,0},{6,2},{1,5},{3,7},{5,1},{7,3},{8,12},{10,14},{12... | collective-permute-start | bytes 221192 | tf_op jit(solution)/shard_map/ppermute | solution.py:320
  7.2 11.2 %collective-permute-start.2 = (bf16[36,1024]{1,0:T(8,128)(2,1)S(1)}, bf16[36,1024]{1,0:T(8,128)(2,1)S(1)}, u32[]{:S(2)}, u32[]{:S(2)}) collective-permute-start(bf16[36,1024]{1,0:T(8,128)(2,1)S(1)} %get-tuple-element.53), channel_id=1, source_target_pairs={{0,2},{2,0},{4,6},{6,4},{1,3},{3,1},{5,7},{7,5},{8,10},{10,8},{12,... | collective-permute-start | bytes 221192 | tf_op jit(solution)/shard_map/ppermute | solution.py:320
  7.9 13.5 %collective-permute-start.5 = (bf16[36,1024]{1,0:T(8,128)(2,1)S(1)}, bf16[36,1024]{1,0:T(8,128)(2,1)S(1)}, u32[]{:S(2)}, u32[]{:S(2)}) collective-permute-start(bf16[36,1024]{1,0:T(8,128)(2,1)S(1)} %get-tuple-element.63), channel_id=1, source_target_pairs={{0,6},{2,4},{4,2},{6,0},{1,7},{3,5},{5,3},{7,1},{8,14},{10,12},{12... | collective-permute-start | bytes 221192 | tf_op jit(solution)/shard_map/ppermute | solution.py:320
  11.6 9.8 %collective-permute-start.6 = (bf16[36,1024]{1,0:T(8,128)(2,1)S(1)}, bf16[36,1024]{1,0:T(8,128)(2,1)S(1)}, u32[]{:S(2)}, u32[]{:S(2)}) collective-permute-start(bf16[36,1024]{1,0:T(8,128)(2,1)S(1)} %get-tuple-element.64), channel_id=1, source_target_pairs={{0,4},{2,6},{4,0},{6,2},{1,5},{3,7},{5,1},{7,3},{8,12},{10,14},{12... | collective-permute-start | bytes 221192 | tf_op jit(solution)/shard_map/ppermute | solution.py:320
  11.6 9.8 %collective-permute-start.7 = (bf16[36,1024]{1,0:T(8,128)(2,1)S(1)}, bf16[36,1024]{1,0:T(8,128)(2,1)S(1)}, u32[]{:S(2)}, u32[]{:S(2)}) collective-permute-start(bf16[36,1024]{1,0:T(8,128)(2,1)S(1)} %get-tuple-element.65), channel_id=1, source_target_pairs={{0,2},{2,0},{4,6},{6,4},{1,3},{3,1},{5,7},{7,5},{8,10},{10,8},{12,... | collective-permute-start | bytes 221192 | tf_op jit(solution)/shard_map/ppermute | solution.py:320
  18.5 11.5 %collective-permute-start.3 = (bf16[144,1024]{1,0:T(8,128)(2,1)S(1)}, bf16[144,1024]{1,0:T(8,128)(2,1)S(1)}, u32[]{:S(2)}, u32[]{:S(2)}) collective-permute-start(bf16[144,1024]{1,0:T(8,128)(2,1)S(1)} %join.2.x_ref.refs_0_.refs_4_), channel_id=1, source_target_pairs={{0,1},{1,0},{2,3},{3,2},{4,5},{5,4},{6,7},{7,6},{8,9},{9,8},{10,11... | collective-permute-start | bytes 884744 | tf_op jit(solution)/shard_map/ppermute | solution.py:315
  19.9 10.1 %collective-permute-start.4 = (bf16[144,1024]{1,0:T(8,128)(2,1)S(1)}, bf16[144,1024]{1,0:T(8,128)(2,1)S(1)}, u32[]{:S(2)}, u32[]{:S(2)}) collective-permute-start(bf16[144,1024]{1,0:T(8,128)(2,1)S(1)} %join.2.x_ref.refs_0_.refs_4_), channel_id=1, source_target_pairs={{0,16},{16,0},{1,17},{17,1},{2,18},{18,2},{3,19},{19,3},{4,20},{20... | collective-permute-start | bytes 884744 | tf_op jit(solution)/shard_map/ppermute | solution.py:315
  21.5 10.1 %collective-permute-start.8 = (bf16[144,1024]{1,0:T(8,128)(2,1)S(1)}, bf16[144,1024]{1,0:T(8,128)(2,1)S(1)}, u32[]{:S(2)}, u32[]{:S(2)}) collective-permute-start(bf16[144,1024]{1,0:T(8,128)(2,1)S(1)} %join.3.refs_0_), channel_id=1, source_target_pairs={{0,1},{1,0},{2,3},{3,2},{4,5},{5,4},{6,7},{7,6},{8,9},{9,8},{10,11... | collective-permute-start | bytes 884744 | tf_op jit(solution)/shard_map/ppermute | solution.py:315
  22.7 10.2 %collective-permute-start.9 = (bf16[144,1024]{1,0:T(8,128)(2,1)S(1)}, bf16[144,1024]{1,0:T(8,128)(2,1)S(1)}, u32[]{:S(2)}, u32[]{:S(2)}) collective-permute-start(bf16[144,1024]{1,0:T(8,128)(2,1)S(1)} %join.3.refs_0_), channel_id=1, source_target_pairs={{0,16},{16,0},{1,17},{17,1},{2,18},{18,2},{3,19},{19,3},{4,20},{20... | collective-permute-start | bytes 884744 | tf_op jit(solution)/shard_map/ppermute | solution.py:315
  32.9 9.6 %collective-permute-start.11 = (bf16[144,1024]{1,0:T(8,128)(2,1)S(1)}, bf16[144,1024]{1,0:T(8,128)(2,1)S(1)}, u32[]{:S(2)}, u32[]{:S(2)}) collective-permute-start(bf16[144,1024]{1,0:T(8,128)(2,1)S(1)} %collective-permute-done.3.x_ref.refs_1_.refs_5_), channel_id=1, source_target_pairs={{0,16},{16,0},{1,17},{17,1},{2,18},{18,2},{3,19},{19,3},{4,20},{20... | collective-permute-start | bytes 884744 | tf_op jit(solution)/shard_map/ppermute | solution.py:315
  34.4 10.3 %collective-permute-start.10 = (bf16[144,1024]{1,0:T(8,128)(2,1)S(1)}, bf16[144,1024]{1,0:T(8,128)(2,1)S(1)}, u32[]{:S(2)}, u32[]{:S(2)}) collective-permute-start(bf16[144,1024]{1,0:T(8,128)(2,1)S(1)} %collective-permute-done.9.refs_2_), channel_id=1, source_target_pairs={{0,1},{1,0},{2,3},{3,2},{4,5},{5,4},{6,7},{7,6},{8,9},{9,8},{10,11... | collective-permute-start | bytes 884744 | tf_op jit(solution)/shard_map/ppermute | solution.py:315
  44.7 6.8 %collective-permute-start.12 = (bf16[144,1024]{1,0:T(8,128)(2,1)S(1)}, bf16[144,1024]{1,0:T(8,128)(2,1)S(1)}, u32[]{:S(2)}, u32[]{:S(2)}) collective-permute-start(bf16[144,1024]{1,0:T(8,128)(2,1)S(1)} %get-tuple-element.79), channel_id=1, source_target_pairs={{0,1},{1,0},{2,3},{3,2},{4,5},{5,4},{6,7},{7,6},{8,9},{9,8},{10,11... | collective-permute-start | bytes 884744 | tf_op jit(solution)/shard_map/ppermute | solution.py:315
  51.6 8.2 %collective-permute-start.13 = (bf16[36,1024]{1,0:T(8,128)(2,1)S(1)}, bf16[36,1024]{1,0:T(8,128)(2,1)S(1)}, u32[]{:S(2)}, u32[]{:S(2)}) collective-permute-start(bf16[36,1024]{1,0:T(8,128)(2,1)S(1)} %get-tuple-element.87), channel_id=1, source_target_pairs={{0,2},{2,0},{4,6},{6,4},{1,3},{3,1},{5,7},{7,5},{8,10},{10,8},{12,... | collective-permute-start | bytes 221192 | tf_op jit(solution)/shard_map/ppermute | solution.py:320
  51.7 8.2 %collective-permute-start.14 = (bf16[36,1024]{1,0:T(8,128)(2,1)S(1)}, bf16[36,1024]{1,0:T(8,128)(2,1)S(1)}, u32[]{:S(2)}, u32[]{:S(2)}) collective-permute-start(bf16[36,1024]{1,0:T(8,128)(2,1)S(1)} %get-tuple-element.88), channel_id=1, source_target_pairs={{0,4},{2,6},{4,0},{6,2},{1,5},{3,7},{5,1},{7,3},{8,12},{10,14},{12... | collective-permute-start | bytes 221192 | tf_op jit(solution)/shard_map/ppermute | solution.py:320
  55.4 6.2 %collective-permute-start.15 = (bf16[36,1024]{1,0:T(8,128)(2,1)S(1)}, bf16[36,1024]{1,0:T(8,128)(2,1)S(1)}, u32[]{:S(2)}, u32[]{:S(2)}) collective-permute-start(bf16[36,1024]{1,0:T(8,128)(2,1)S(1)} %get-tuple-element.89), channel_id=1, source_target_pairs={{0,6},{2,4},{4,2},{6,0},{1,7},{3,5},{5,3},{7,1},{8,14},{10,12},{12... | collective-permute-start | bytes 221192 | tf_op jit(solution)/shard_map/ppermute | solution.py:320
  56.1 6.5 %collective-permute-start.16 = (bf16[512,1024]{1,0:T(8,128)(2,1)S(1)}, bf16[512,1024]{1,0:T(8,128)(2,1)S(1)}, u32[]{:S(2)}, u32[]{:S(2)}) collective-permute-start(bf16[512,1024]{1,0:T(8,128)(2,1)S(1)} %get-tuple-element.90), channel_id=1, source_target_pairs={{0,8},{8,0},{1,9},{9,1},{2,10},{10,2},{3,11},{11,3},{4,12},{12,4},... | collective-permute-start | bytes 3145736 | tf_op jit(solution)/shard_map/ppermute | solution.py:315
  61.6 2.7 %collective-permute-start.17 = (bf16[512,1024]{1,0:T(8,128)(2,1)S(1)}, bf16[512,1024]{1,0:T(8,128)(2,1)S(1)}, u32[]{:S(2)}, u32[]{:S(2)}) collective-permute-start(bf16[512,1024]{1,0:T(8,128)(2,1)S(1)} %get-tuple-element.94), channel_id=1, source_target_pairs={{0,8},{8,0},{1,9},{9,1},{2,10},{10,2},{3,11},{11,3},{4,12},{12,4},... | collective-permute-start | bytes 3145736 | tf_op jit(solution)/shard_map/ppermute | solution.py:315

commit v7 on v6

--- a/solution.py
+++ b/solution.py
@@ -20,6 +20,7 @@
 BF16 = jnp.bfloat16
 HERE = pl.BlockSpec(memory_space=pltpu.VMEM)
 AFAR = pl.BlockSpec(memory_space=pltpu.HBM)
+ANYWHERE = pl.BlockSpec(memory_space=pl.ANY)
 
 
 def silu_parts(gate):
@@ -91,56 +92,99 @@
 
 
 def join_kernel(*refs):
-    refs[EXPERTS][...] = stacked(refs[EXPERTS - 1 :: -1]).astype(BF16)
-
-
-def join(blocks):
+    refs[-1][...] = stacked(refs[EXPERTS - 1 :: -1]).astype(BF16)
+
+
+def join(blocks, earlier=()):
     width = blocks[0].shape[1]
     return pl.pallas_call(
         join_kernel,
         out_shape=jax.ShapeDtypeStruct((EXPERTS * CAP, width), BF16),
+        in_specs=[HERE] * EXPERTS + [ANYWHERE] * len(earlier),
         compiler_params=SMALL,
         cost_estimate=CHEAP,
         name="join",
-    )(*blocks[::-1])
-
-
-def flip_kernel(source_ref, target_ref):
-    @pl.loop(0, source_ref.shape[0] // STRIP)
-    def _(j):
-        rows = pl.ds(pl.multiple_of(j * STRIP, STRIP), STRIP)
-        target_ref[:, rows] = source_ref[rows, :].T
+    )(*blocks[::-1], *earlier)
+
+
+def relay_kernel(n, *refs):
+    for i in range(n):
+        refs[len(refs) - n + i][...] = refs[i][...]
+
+
+def relay(values, earlier):
+    n = len(values)
+    return pl.pallas_call(
+        functools.partial(relay_kernel, n),
+        out_shape=[jax.ShapeDtypeStruct(v.shape, v.dtype) for v in values],
+        in_specs=[HERE] * n + [ANYWHERE] * len(earlier),
+        compiler_params=SMALL,
+        cost_estimate=CHEAP,
+        name="relay",
+    )(*values, *earlier)
+
+
+def mark_kernel(value_ref, mark_ref):
+    mark_ref[...] = value_ref[: mark_ref.shape[0], : mark_ref.shape[1]]
+
+
+def mark(value):
+    return pl.pallas_call(
+        mark_kernel,
+        out_shape=jax.ShapeDtypeStruct((16, 128), value.dtype),
+        in_specs=[HERE],
+        compiler_params=SMALL,
+        cost_estimate=CHEAP,
+        name="mark",
+    )(value)
+
+
+def flip_kernel(source_ref, here_ref, flipped_ref, sems):
+    steps = source_ref.shape[0] // STRIP
+    copies = []
+    for j in range(steps):
+        rows = pl.ds(j * STRIP, STRIP)
+        copies.append(pltpu.make_async_copy(source_ref.at[rows], here_ref.at[rows], sems.at[j]))
+        copies[j].start()
+    for j in range(steps):
+        copies[j].wait()
+        rows = slice(j * STRIP, (j + 1) * STRIP)
+        flipped_ref[:, rows] = here_ref[rows, :].T
 
 
 def flip(value):
     return pl.pallas_call(
         flip_kernel,
-        out_shape=pltpu.VMEM(value.shape[::-1], value.dtype),
-        in_specs=[HERE],
-        out_specs=HERE,
+        out_shape=[pltpu.VMEM(value.shape, value.dtype), pltpu.VMEM(value.shape[::-1], value.dtype)],
+        in_specs=[AFAR],
+        out_specs=[HERE, HERE],
+        scratch_shapes=[pltpu.SemaphoreType.DMA((value.shape[0] // STRIP,))],
         compiler_params=SMALL,
         cost_estimate=CHEAP,
         name="flip",
-    )(value)
-
-
-def forward_kernel(down, fetch, x_ref, *refs):
+    )(kept(value))
+
+
+def forward_kernel(fetch, down, pair, unused, x_ref, wg_ref, wu_ref, *refs):
+    refs = list(refs)
+    wd_ref = refs.pop(0) if down else None
+    other_ref = refs.pop(0) if pair else None
+    refs = refs[unused:]
+    act_ref, coef_ref = refs.pop(0), refs.pop(0)
+    if down:
+        shares = [refs.pop(0) for _ in range(EXPERTS if pair else 1)]
     if fetch:
-        sources, refs = refs[:3], refs[3:]
-        act_ref, coef_ref, share_ref, wg_ref, wu_ref, wd_ref, acc_ref, sems = refs
-        targets = (wg_ref, wu_ref, wd_ref)
-    elif down:
-        wg_ref, wu_ref, wd_ref, act_ref, coef_ref, share_ref, acc_ref = refs
-    else:
-        wg_ref, wu_ref, act_ref, coef_ref = refs
+        sources, sems = (wg_ref, wu_ref), refs.pop()
+        wg_ref, wu_ref = refs.pop(0), refs.pop(0)
+    if down:
+        acc_ref = refs.pop(0)
     steps = wg_ref.shape[1] // PAIR
 
     def copies(j):
         cols = pl.ds(pl.multiple_of(j * PAIR, PAIR), PAIR)
-        views = ((slice(None), cols), (slice(None), cols), (cols, slice(None)))
         return [
-            pltpu.make_async_copy(source.at[view], target.at[view], sems.at[j, i])
-            for i, (source, target, view) in enumerate(zip(sources, targets, views))
+            pltpu.make_async_copy(source.at[:, cols], target.at[:, cols], sems.at[j, i])
+            for i, (source, target) in enumerate(zip(sources, (wg_ref, wu_ref)))
         ]
 
     if fetch:
@@ -166,26 +210,34 @@
                 hidden = (act * up).astype(BF16)
                 acc_ref[...] += jnp.dot(hidden, wd_ref[cols, :], preferred_element_type=F32)
 
-    if down:
-        share_ref[...] = acc_ref[...].astype(BF16)
-
-
-def forward(x, wg, wu, wd=None, fetch=False):
+    if pair:
+        other = other_ref[...].astype(F32)
+        for k in range(EXPERTS):
+            rows = slice(k * CAP, (k + 1) * CAP)
+            shares[k][...] = jnp.concatenate([other[rows], acc_ref[rows, :]], axis=0).astype(BF16)
+    elif down:
+        shares[0][...] = acc_ref[...].astype(BF16)
+
+
+def forward(x, wg, wu, wd=None, other=None, fetch=False, earlier=()):
     (rows, width), cols = x.shape, wg.shape[1]
-    down = wd is not None
-    weights = [wg, wu, wd][: 2 + down]
-    return pl.pallas_call(
-        functools.partial(forward_kernel, down, fetch),
+    down, pair = wd is not None, other is not None
+    shares = [jax.ShapeDtypeStruct((rows, width), BF16)]
+    if pair:
+        shares = [jax.ShapeDtypeStruct((2 * CAP, width), BF16)] * EXPERTS
+    weights = [kept(wg), kept(wu)] if fetch else [wg, wu]
+    return pl.pallas_call(
+        functools.partial(forward_kernel, fetch, down, pair, len(earlier)),
         out_shape=[jax.ShapeDtypeStruct((rows, cols), BF16)] * 2
-        + [jax.ShapeDtypeStruct((rows, width), BF16)] * down
-        + [pltpu.VMEM(w.shape, w.dtype) for w in weights] * fetch,
-        in_specs=[HERE] + [AFAR if fetch else HERE] * len(weights),
+        + shares * down
+        + [pltpu.VMEM(wg.shape, wg.dtype)] * (2 * fetch),
+        in_specs=[HERE] + [AFAR if fetch else HERE] * 2 + [HERE] * (down + pair) + [ANYWHERE] * len(earlier),
         scratch_shapes=[pltpu.VMEM((rows, width), F32)] * down
-        + [pltpu.SemaphoreType.DMA((cols // PAIR, 3))] * fetch,
+        + [pltpu.SemaphoreType.DMA((cols // PAIR, 2))] * fetch,
         compiler_params=LARGE,
         cost_estimate=CHEAP,
-        name="forward_fetch" if fetch else "forward_down" if down else "forward",
-    )(x, *([kept(w) for w in weights] if fetch else weights))
+        name="forward" + "_fetch" * fetch + "_down" * down,
+    )(x, *weights, *([wd] * down), *([other] * pair), *earlier)
 
 
 def turn_kernel(_, __, *refs):
@@ -277,38 +329,38 @@
     )(own0, own0, got0, got0, own1, own1, got1, got1)
 
 
-def combine_kernel(mine_ref, theirs_ref, *outs):
-    total = mine_ref[...].astype(F32) + theirs_ref[...].astype(F32)
-    for k in range(EXPERTS):
-        outs[k][...] = total[k * CAP : (k + 1) * CAP].astype(BF16)
-
-
-def combine(mine, theirs):
-    width = mine.shape[1]
-    return pl.pallas_call(
-        combine_kernel,
-        out_shape=[jax.ShapeDtypeStruct((CAP, width), BF16)] * EXPERTS,
-        compiler_params=SMALL,
-        cost_estimate=CHEAP,
-        name="combine",
-    )(mine, theirs)
-
-
-def unpack_kernel(placer_ref, *refs):
-    packed = stacked(refs[:EXPERTS]).astype(BF16)
+def split_kernel(*refs):
+    blocks = [r[...].astype(F32) for r in refs[:EXPERTS]]
+    refs[EXPERTS][...] = jnp.concatenate([b[:CAP] for b in blocks], axis=0).astype(BF16)
+    refs[EXPERTS + 1][...] = jnp.concatenate([b[CAP:] for b in blocks], axis=0).astype(BF16)
+
+
+def split(blocks):
+    width = blocks[0].shape[1]
+    return pl.pallas_call(
+        split_kernel,
+        out_shape=[jax.ShapeDtypeStruct((EXPERTS * CAP, width), BF16)] * 2,
+        compiler_params=SMALL,
+        cost_estimate=CHEAP,
+        name="split",
+    )(*blocks)
+
+
+def unpack_kernel(placer_ref, mine_ref, got_ref, out_ref):
     chosen = placer_ref[...].astype(F32).T.astype(BF16)
-    refs[EXPERTS][...] = jnp.dot(chosen, packed, preferred_element_type=F32).astype(BF16)
-
-
-def unpack(placer, blocks):
-    width = blocks[0].shape[1]
+    total = jnp.dot(chosen, mine_ref[...], preferred_element_type=F32)
+    total += jnp.dot(chosen, got_ref[...], preferred_element_type=F32)
+    out_ref[...] = total.astype(BF16)
+
+
+def unpack(placer, mine, got):
     return pl.pallas_call(
         unpack_kernel,
-        out_shape=jax.ShapeDtypeStruct((placer.shape[1], width), BF16),
+        out_shape=jax.ShapeDtypeStruct((placer.shape[1], mine.shape[1]), BF16),
         compiler_params=SMALL,
         cost_estimate=CHEAP,
         name="unpack",
-    )(placer, *blocks)
+    )(placer, mine, got)
 
 
 def swap(value, axis):
@@ -333,39 +385,36 @@
     tokens, width = designs.shape
     share = width // 4
     placer, *blocks = pack(scalars, archetype.reshape(1, tokens), designs, cotangent)
+    wd, wdt = flip(after([w_down], [placer])[0])
+
     moved = across_planes(blocks[:EXPERTS])
-    x_own = join(moved)
-    x_near, x_far = after([swap(x_own, "half"), swap(x_own, "far")], [])
-
+    x_own = join(moved, [wdt])
+    x_near, x_far = swap(x_own, "half"), swap(x_own, "far")
     moved = across_planes(blocks[EXPERTS:])
-    g_own = join(after(moved[:1], [x_own]) + moved[1:])
-    g_near, g_far = after([swap(g_own, "half"), swap(g_own, "far")], [])
-
-    act0, coef0, share_own, wg, wu, wd = forward(x_own, w_gate, w_up, w_down, fetch=True)
-    (x_near,) = after([x_near], [act0])
-    act1, coef1, share_near = forward(x_near, wg, wu, wd)
-    x_pass, g_pass = after([x_near, g_far], [act0, g_near])
+    g_own = join(moved, [x_own])
+    g_near, g_far = swap(g_own, "half"), swap(g_own, "far")
+
+    act0, coef0, share_own, wg, wu = forward(x_own, w_gate, w_up, wd, fetch=True)
+    act1, coef1, *shares = forward(x_near, wg, wu, wd, other=share_own, earlier=[x_far])
+    x_pass, g_pass = relay([x_near, g_far], [mark(act1), g_near])
     x_corner, g_corner = swap(x_pass, "far"), swap(g_pass, "half")
+    returned = across_planes(shares)
     (x_far,) = after([x_far], [act1])
     act2, coef2 = forward(x_far, wg, wu)
-    wdt = flip(after([wd], [act2])[0])
-    (x_corner,) = after([x_corner], [act2, wdt])
+    (x_corner,) = after([x_corner], [act2])
     act3, coef3 = forward(x_corner, wg, wu)
     xt = turn(*scalars[1:], [x_own, x_near, x_far, x_corner], share)
 
-    (share_near,) = after([share_near], [g_corner, act3])
-    share_got = swap(share_near, "half")
     gs = [g_own, g_near, g_far, g_corner]
     acts, coefs = [act0, act1, act2, act3], [coef0, coef1, coef2, coef3]
     half = w_down.shape[0] // 2
     own0, sib0 = backward(xt, gs, acts, coefs, wdt, 0, half)
-    (share_got,) = after([share_got], [own0])
-    sums = combine(share_own, share_got)
-    (xt,) = after([xt], [sums[0]])
+    mine, theirs = split(after(returned[:1], [own0]) + returned[1:])
+    (xt,) = after([xt], [mine])
     own1, sib1 = backward(xt, gs, acts, coefs, wdt, half, half)
-    returned = across_planes(sums)
-    (sib1,) = after([sib1], returned[1:])
-    outputs = unpack(placer, returned)
+    got = swap(theirs, "half")
+    (sib1,) = after([sib1], [got])
+    outputs = unpack(placer, mine, got)
     grad_gate, grad_up = finish(own0, swap(sib0, "core"), own1, swap(sib1, "core"))
     return outputs, grad_gate, grad_up
 

time: 65.9 us -> 59.1 us (0.90)
  waiting for transfers between devices: 10.7 us -> 3.07 us
  Pallas kernels: 27.4 us -> 28.3 us
    ppermute x9, waiting for transfers between devices: 4.96 us -> 0.49 us  [across_planes(): lax.ppermute(blocks[k], 'arch', [(i, i ^ k) for i in range(EXPERTS)])]
    ppermute x9, waiting for transfers between devices: 5.79 us -> 2.58 us  [swap(): return lax.ppermute(value, axis, [(0, 1), (1, 0)])]
    pallas_call x6 -> x8, Pallas kernels: 15.6 us -> 16.3 us  [the longest x4 13.5 us: forward(): pl.pallas_call(functools.partial(forward_kernel, fetch, down, pair, len(e...]
  transfers between devices with their start and end apart: 18 -> 18, of which waited for: 6 -> 3; matrix products, arithmetic and copies ran while one was open for 0% -> 0% of each run, Pallas kernels for 37% -> 43%
where the time goes in v7:
time: 59.1 us; the launch traced here: 59 us
  Pallas kernels  28.3 us (48%)
  starting transfers between devices  26.8 us (45%)
  waiting for transfers between devices  3.07 us (5%)
  between operations  0.83 us (1%)
    ppermute x9, starting transfers between devices, across_planes(): lax.ppermute(blocks[k], 'arch', [(i, i ^ k) for i in range(EXPERTS)])  17.5 us
    pallas_call x4, Pallas kernels, forward(): pl.pallas_call(functools.partial(forward_kernel, fetch, down, pair, len(e...  13.5 us
    ppermute x9, starting transfers between devices, swap(): return lax.ppermute(value, axis, [(0, 1), (1, 0)])  9.36 us
    pallas_call x2, Pallas kernels, backward(): pl.pallas_call(functools.partial(backward_kernel, first, counts), out_sha...  7.56 us
    pallas_call x1, Pallas kernels, flip(): pl.pallas_call(flip_kernel, out_shape=[pltpu.VMEM(value.shape, value.dtyp...  2.73 us
    ppermute x9, waiting for transfers between devices, swap(): return lax.ppermute(value, axis, [(0, 1), (1, 0)])  2.58 us
    pallas_call x1, Pallas kernels, finish(): pl.pallas_call(finish_kernel, grid=(steps,), in_specs=[upper, lower] * 4,...  1.5 us
    pallas_call x1, Pallas kernels, pack(): pl.pallas_call(pack_kernel, out_shape=[jax.ShapeDtypeStruct((EXPERTS * CA...  1.46 us
  transfers between devices with their start and end apart: 18, of which 3 were waited for; matrix products, arithmetic and copies ran while one was open for 0% of the time, Pallas kernels for 43%

profile of v7, /device:TPU:0, one launch (start us, length us, event | category | flops | bytes accessed | tf_op | source)
XLA Modules:
  0.0 59.0 jit_solution(1811644237156019348)
XLA Ops:
  0.6 1.5 %pack.1 = (bf16[144,128]{1,0:T(8,128)(2,1)S(1)}, bf16[36,1024]{1,0:T(8,128)(2,1)S(1)}, bf16[36,1024]{1,0:T(8,128)(2,1)S(1)}, bf16[36,1024]{1,0:T(8,128)(2,1)S(1)...) custom-call(s32[1]{0:T(128)} %bitcast.plane_ref, ...), custom_call_target="tpu_custom_call" | custom-call | tf_op jit(solution)/shard_map/pack/pallas_call | solution.py:77
  2.1 5.1 %collective-permute-start = (bf16[36,1024]{1,0:T(8,128)(2,1)S(1)}, bf16[36,1024]{1,0:T(8,128)(2,1)S(1)}, u32[]{:S(2)}, u32[]{:S(2)}) collective-permute-start(bf16[36,1024]{1,0:T(8,128)(2,1)S(1)} %get-tuple-element.46), channel_id=1, source_target_pairs={{0,6},{2,4},{4,2},{6,0},{1,7},{3,5},{5,3},{7,1},{8,14},{10,12},{12... | collective-permute-start | bytes 221192 | tf_op jit(solution)/shard_map/ppermute | solution.py:372
  7.2 0.0 collective-permute-start.1
  7.2 0.6 %collective-permute-start.2 = (bf16[36,1024]{1,0:T(8,128)(2,1)S(1)}, bf16[36,1024]{1,0:T(8,128)(2,1)S(1)}, u32[]{:S(2)}, u32[]{:S(2)}) collective-permute-start(bf16[36,1024]{1,0:T(8,128)(2,1)S(1)} %get-tuple-element.48), channel_id=1, source_target_pairs={{0,2},{2,0},{4,6},{6,4},{1,3},{3,1},{5,7},{7,5},{8,10},{10,8},{12,... | collective-permute-start | bytes 221192 | tf_op jit(solution)/shard_map/ppermute | solution.py:372
  7.9 3.7 %collective-permute-start.5 = (bf16[36,1024]{1,0:T(8,128)(2,1)S(1)}, bf16[36,1024]{1,0:T(8,128)(2,1)S(1)}, u32[]{:S(2)}, u32[]{:S(2)}) collective-permute-start(bf16[36,1024]{1,0:T(8,128)(2,1)S(1)} %get-tuple-element.59), channel_id=1, source_target_pairs={{0,6},{2,4},{4,2},{6,0},{1,7},{3,5},{5,3},{7,1},{8,14},{10,12},{12... | collective-permute-start | bytes 221192 | tf_op jit(solution)/shard_map/ppermute | solution.py:372
  11.6 0.0 collective-permute-start.6
  11.6 3.6 %collective-permute-start.7 = (bf16[36,1024]{1,0:T(8,128)(2,1)S(1)}, bf16[36,1024]{1,0:T(8,128)(2,1)S(1)}, u32[]{:S(2)}, u32[]{:S(2)}) collective-permute-start(bf16[36,1024]{1,0:T(8,128)(2,1)S(1)} %get-tuple-element.61), channel_id=1, source_target_pairs={{0,2},{2,0},{4,6},{6,4},{1,3},{3,1},{5,7},{7,5},{8,10},{10,8},{12,... | collective-permute-start | bytes 221192 | tf_op jit(solution)/shard_map/ppermute | solution.py:372
  15.2 2.7 %flip.1 = (bf16[2048,1024]{1,0:T(8,128)(2,1)S(1)}, bf16[1024,2048]{1,0:T(8,128)(2,1)S(1)}) custom-call(bf16[2048,1024]{1,0:T(8,128)(2,1)} %source_ref), custom_call_target="tpu_custom_call" | custom-call | tf_op jit(solution)/shard_map/flip/pallas_call | solution.py:156
  17.9 0.5 collective-permute-done.1.refs_1_
  18.4 0.0 collective-permute-done.2.refs_2_
  18.5 1.4 %collective-permute-start.3 = (bf16[144,1024]{1,0:T(8,128)(2,1)S(1)}, bf16[144,1024]{1,0:T(8,128)(2,1)S(1)}, u32[]{:S(2)}, u32[]{:S(2)}) collective-permute-start(bf16[144,1024]{1,0:T(8,128)(2,1)S(1)} %join.2.x_ref.refs_4_.refs_0_), channel_id=1, source_target_pairs={{0,1},{1,0},{2,3},{3,2},{4,5},{5,4},{6,7},{7,6},{8,9},{9,8},{10,11... | collective-permute-start | bytes 884744 | tf_op jit(solution)/shard_map/ppermute | solution.py:367
  19.9 1.5 %collective-permute-start.4 = (bf16[144,1024]{1,0:T(8,128)(2,1)S(1)}, bf16[144,1024]{1,0:T(8,128)(2,1)S(1)}, u32[]{:S(2)}, u32[]{:S(2)}) collective-permute-start(bf16[144,1024]{1,0:T(8,128)(2,1)S(1)} %join.2.x_ref.refs_4_.refs_0_), channel_id=1, source_target_pairs={{0,16},{16,0},{1,17},{17,1},{2,18},{18,2},{3,19},{19,3},{4,20},{20... | collective-permute-start | bytes 884744 | tf_op jit(solution)/shard_map/ppermute | solution.py:367
  21.5 1.3 %collective-permute-start.8 = (bf16[144,1024]{1,0:T(8,128)(2,1)S(1)}, bf16[144,1024]{1,0:T(8,128)(2,1)S(1)}, u32[]{:S(2)}, u32[]{:S(2)}) collective-permute-start(bf16[144,1024]{1,0:T(8,128)(2,1)S(1)} %join.3.refs_0_), channel_id=1, source_target_pairs={{0,16},{16,0},{1,17},{17,1},{2,18},{18,2},{3,19},{19,3},{4,20},{20... | collective-permute-start | bytes 884744 | tf_op jit(solution)/shard_map/ppermute | solution.py:367
  22.7 1.5 %collective-permute-start.9 = (bf16[144,1024]{1,0:T(8,128)(2,1)S(1)}, bf16[144,1024]{1,0:T(8,128)(2,1)S(1)}, u32[]{:S(2)}, u32[]{:S(2)}) collective-permute-start(bf16[144,1024]{1,0:T(8,128)(2,1)S(1)} %join.3.refs_0_), channel_id=1, source_target_pairs={{0,1},{1,0},{2,3},{3,2},{4,5},{5,4},{6,7},{7,6},{8,9},{9,8},{10,11... | collective-permute-start | bytes 884744 | tf_op jit(solution)/shard_map/ppermute | solution.py:367
  24.2 5.3 %forward_fetch_down.1 = (bf16[144,2048]{1,0:T(8,128)(2,1)S(1)}, bf16[144,2048]{1,0:T(8,128)(2,1)S(1)}, bf16[144,1024]{1,0:T(8,128)(2,1)S(1)}, bf16[1024,2048]{1,0:T(8,128)(2,1)S(1)}, bf16[1024,2048]{1,0:T(8,128)(2,1)S(1)}) custom-call(bf16[144,1024]{1,0:T(8,128)(2,1)S(1)} %join.2.x_ref.refs_4_.refs_0_, bf16[1024,2048]{1,0:T(8,128)(2,1)} %wg_ref.1, ...), custom_call_target="tpu_custom_call" | custom-call | tf_op jit(solution)/shard_map/forward_fetch_down/pallas_call | solution.py:229
  29.6 0.0 collective-permute-done.3.x_ref.refs_0_.refs_1_.refs_5_
  29.6 3.8 %forward_down.1 = (bf16[144,2048]{1,0:T(8,128)(2,1)S(1)}, bf16[144,2048]{1,0:T(8,128)(2,1)S(1)}, bf16[72,1024]{1,0:T(8,128)(2,1)S(1)}, bf16[72,1024]{1,0:T(8,128...) custom-call(bf16[144,1024]{1,0:T(8,128)(2,1)S(1)} %collective-permute-done.3.x_ref.refs_0_.refs_1_.refs_5_, ...), custom_call_target="tpu_custom_call" | custom-call | tf_op jit(solution)/shard_map/forward_down/pallas_call | solution.py:229
  33.5 1.5 %collective-permute-start.10 = (bf16[144,1024]{1,0:T(8,128)(2,1)S(1)}, bf16[144,1024]{1,0:T(8,128)(2,1)S(1)}, u32[]{:S(2)}, u32[]{:S(2)}) collective-permute-start(bf16[144,1024]{1,0:T(8,128)(2,1)S(1)} %get-tuple-element.63), channel_id=1, source_target_pairs={{0,16},{16,0},{1,17},{17,1},{2,18},{18,2},{3,19},{19,3},{4,20},{20... | collective-permute-start | bytes 884744 | tf_op jit(solution)/shard_map/ppermute | solution.py:367
  35.0 0.0 collective-permute-start.11
  35.1 4.2 %collective-permute-start.13 = (bf16[72,1024]{1,0:T(8,128)(2,1)S(1)}, bf16[72,1024]{1,0:T(8,128)(2,1)S(1)}, u32[]{:S(2)}, u32[]{:S(2)}) collective-permute-start(bf16[72,1024]{1,0:T(8,128)(2,1)S(1)} %get-tuple-element.76), channel_id=1, source_target_pairs={{0,4},{2,6},{4,0},{6,2},{1,5},{3,7},{5,1},{7,3},{8,12},{10,14},{12... | collective-permute-start | bytes 442376 | tf_op jit(solution)/shard_map/ppermute | solution.py:372
  39.2 0.2 collective-permute-start.14
  39.4 2.2 %forward.2 = (bf16[144,2048]{1,0:T(8,128)(2,1)S(1)}, bf16[144,2048]{1,0:T(8,128)(2,1)S(1)}) custom-call(bf16[144,1024]{1,0:T(8,128)(2,1)S(1)} %collective-permute-done.4.refs_2_.x_ref.refs_6_, bf16[1024,2048]{1,0:T(8,128)(2,1)S(1)} %get-tuple-element.53.wg_ref, bf16[1024,2048]{1,0:T(8,128)(2,1)S(1)} %get-tuple-element.54.wu_ref), custom_call_target="tpu_custom_call" | custom-call | tf_op jit(solution)/shard_map/forward/pallas_call | solution.py:229
  41.7 2.2 %forward.3 = (bf16[144,2048]{1,0:T(8,128)(2,1)S(1)}, bf16[144,2048]{1,0:T(8,128)(2,1)S(1)}) custom-call(bf16[144,1024]{1,0:T(8,128)(2,1)S(1)} %collective-permute-done.10.refs_3_.refs_7_.x_ref, bf16[1024,2048]{1,0:T(8,128)(2,1)S(1)} %get-tuple-element.53.wg_ref, bf16[1024,2048]{1,0:T(8,128)(2,1)S(1)} %get-tuple-element.54.wu_ref), custom_call_target="tpu_custom_call" | custom-call | tf_op jit(solution)/shard_map/forward/pallas_call | solution.py:229
  43.9 0.2 turn.1.xt_ref
  44.1 3.8 %backward.2 = (bf16[512,1024]{1,0:T(8,128)(2,1)S(1)}, bf16[512,1024]{1,0:T(8,128)(2,1)S(1)}) custom-call(bf16[512,576]{1,0:T(8,128)(2,1)S(1)} %turn.1.xt_ref, bf16[144,1024]{1,0:T(8,128)(2,1)S(1)} %join.3.refs_0_, bf16[144,1024]{1,0:T(8,128)(2,1)S(1)} %collective-permute-done.9.refs_3_.refs_1_, bf16[144,1024]{1,0:T(8,128)(2,1)S(1)} %collective-permute-done.8.refs_1_.refs_2_, ...), custom_call_target="tpu_custom_call" | custom-call | tf_op jit(solution)/shard_map/backward/pallas_call | solution.py:294
  47.9 0.1 split.1
  48.0 2.0 %collective-permute-start.15 = (bf16[144,1024]{1,0:T(8,128)(2,1)S(1)}, bf16[144,1024]{1,0:T(8,128)(2,1)S(1)}, u32[]{:S(2)}, u32[]{:S(2)}) collective-permute-start(bf16[144,1024]{1,0:T(8,128)(2,1)S(1)} %get-tuple-element.79), channel_id=1, source_target_pairs={{0,1},{1,0},{2,3},{3,2},{4,5},{5,4},{6,7},{7,6},{8,9},{9,8},{10,11... | collective-permute-start | bytes 884744 | tf_op jit(solution)/shard_map/ppermute | solution.py:367
  50.1 3.8 %backward.3 = (bf16[512,1024]{1,0:T(8,128)(2,1)S(1)}, bf16[512,1024]{1,0:T(8,128)(2,1)S(1)}) custom-call(bf16[512,576]{1,0:T(8,128)(2,1)S(1)} %turn.1.xt_ref, bf16[144,1024]{1,0:T(8,128)(2,1)S(1)} %join.3.refs_0_, bf16[144,1024]{1,0:T(8,128)(2,1)S(1)} %collective-permute-done.9.refs_3_.refs_1_, bf16[144,1024]{1,0:T(8,128)(2,1)S(1)} %collective-permute-done.8.refs_1_.refs_2_, ...), custom_call_target="tpu_custom_call" | custom-call | tf_op jit(solution)/shard_map/backward/pallas_call | solution.py:294
  53.9 1.0 %collective-permute-done.15.got_ref = bf16[144,1024]{1,0:T(8,128)(2,1)S(1)} collective-permute-done((bf16[144,1024]{1,0:T(8,128)(2,1)S(1)}, bf16[144,1024]{1,0:T(8,128)(2,1)S(1)}, u32[]{:S(2)}, u32[]{:S(2)}) %collective-permute-start.15) | collective-permute-done | bytes 294944 | tf_op jit(solution)/shard_map/ppermute | solution.py:367
  54.8 1.0 %unpack.1 = bf16[128,1024]{1,0:T(8,128)(2,1)} custom-call(bf16[144,128]{1,0:T(8,128)(2,1)S(1)} %get-tuple-element.45.placer_ref, bf16[144,1024]{1,0:T(8,128)(2,1)S(1)} %get-tuple-element.78.mine_ref, bf16[144,1024]{1,0:T(8,128)(2,1)S(1)} %collective-permute-done.15.got_ref), custom_call_target="tpu_custom_call" | custom-call | tf_op jit(solution)/shard_map/unpack/pallas_call | solution.py:357
  55.9 1.6 %collective-permute-done.17.refs_6_.refs_7_ = bf16[512,1024]{1,0:T(8,128)(2,1)S(1)} collective-permute-done((bf16[512,1024]{1,0:T(8,128)(2,1)S(1)}, bf16[512,1024]{1,0:T(8,128)(2,1)S(1)}, u32[]{:S(2)}, u32[]{:S(2)}) %collective-permute-start.17) | collective-permute-done | bytes 1048608 | tf_op jit(solution)/shard_map/ppermute | solution.py:367
  57.5 1.5 %finish.1 = (bf16[256,2048]{1,0:T(8,128)(2,1)}, bf16[256,2048]{1,0:T(8,128)(2,1)}) custom-call(bf16[512,1024]{1,0:T(8,128)(2,1)S(1)} %get-tuple-element.73.refs_0_.refs_1_, bf16[512,1024]{1,0:T(8,128)(2,1)S(1)} %get-tuple-element.73.refs_0_.refs_1_, bf16[512,1024]{1,0:T(8,128)(2,1)S(1)} %collective-permute-done.16.refs_2_.refs_3_, ...), custom_call_target="tpu_custom_call" | custom-call | tf_op jit(solution)/shard_map/finish/pallas_call | solution.py:320
  (20 shorter events, 0.2 us)
Async XLA Ops:
  2.1 9.5 %collective-permute-start = (bf16[36,1024]{1,0:T(8,128)(2,1)S(1)}, bf16[36,1024]{1,0:T(8,128)(2,1)S(1)}, u32[]{:S(2)}, u32[]{:S(2)}) collective-permute-start(bf16[36,1024]{1,0:T(8,128)(2,1)S(1)} %get-tuple-element.46), channel_id=1, source_target_pairs={{0,6},{2,4},{4,2},{6,0},{1,7},{3,5},{5,3},{7,1},{8,14},{10,12},{12... | collective-permute-start | bytes 221192 | tf_op jit(solution)/shard_map/ppermute | solution.py:372
  7.2 11.2 %collective-permute-start.1 = (bf16[36,1024]{1,0:T(8,128)(2,1)S(1)}, bf16[36,1024]{1,0:T(8,128)(2,1)S(1)}, u32[]{:S(2)}, u32[]{:S(2)}) collective-permute-start(bf16[36,1024]{1,0:T(8,128)(2,1)S(1)} %get-tuple-element.47), channel_id=1, source_target_pairs={{0,4},{2,6},{4,0},{6,2},{1,5},{3,7},{5,1},{7,3},{8,12},{10,14},{12... | collective-permute-start | bytes 221192 | tf_op jit(solution)/shard_map/ppermute | solution.py:372
  7.2 11.2 %collective-permute-start.2 = (bf16[36,1024]{1,0:T(8,128)(2,1)S(1)}, bf16[36,1024]{1,0:T(8,128)(2,1)S(1)}, u32[]{:S(2)}, u32[]{:S(2)}) collective-permute-start(bf16[36,1024]{1,0:T(8,128)(2,1)S(1)} %get-tuple-element.48), channel_id=1, source_target_pairs={{0,2},{2,0},{4,6},{6,4},{1,3},{3,1},{5,7},{7,5},{8,10},{10,8},{12,... | collective-permute-start | bytes 221192 | tf_op jit(solution)/shard_map/ppermute | solution.py:372
  7.9 13.5 %collective-permute-start.5 = (bf16[36,1024]{1,0:T(8,128)(2,1)S(1)}, bf16[36,1024]{1,0:T(8,128)(2,1)S(1)}, u32[]{:S(2)}, u32[]{:S(2)}) collective-permute-start(bf16[36,1024]{1,0:T(8,128)(2,1)S(1)} %get-tuple-element.59), channel_id=1, source_target_pairs={{0,6},{2,4},{4,2},{6,0},{1,7},{3,5},{5,3},{7,1},{8,14},{10,12},{12... | collective-permute-start | bytes 221192 | tf_op jit(solution)/shard_map/ppermute | solution.py:372
  11.6 9.8 %collective-permute-start.6 = (bf16[36,1024]{1,0:T(8,128)(2,1)S(1)}, bf16[36,1024]{1,0:T(8,128)(2,1)S(1)}, u32[]{:S(2)}, u32[]{:S(2)}) collective-permute-start(bf16[36,1024]{1,0:T(8,128)(2,1)S(1)} %get-tuple-element.60), channel_id=1, source_target_pairs={{0,4},{2,6},{4,0},{6,2},{1,5},{3,7},{5,1},{7,3},{8,12},{10,14},{12... | collective-permute-start | bytes 221192 | tf_op jit(solution)/shard_map/ppermute | solution.py:372
  11.6 9.8 %collective-permute-start.7 = (bf16[36,1024]{1,0:T(8,128)(2,1)S(1)}, bf16[36,1024]{1,0:T(8,128)(2,1)S(1)}, u32[]{:S(2)}, u32[]{:S(2)}) collective-permute-start(bf16[36,1024]{1,0:T(8,128)(2,1)S(1)} %get-tuple-element.61), channel_id=1, source_target_pairs={{0,2},{2,0},{4,6},{6,4},{1,3},{3,1},{5,7},{7,5},{8,10},{10,8},{12,... | collective-permute-start | bytes 221192 | tf_op jit(solution)/shard_map/ppermute | solution.py:372
  18.5 11.1 %collective-permute-start.3 = (bf16[144,1024]{1,0:T(8,128)(2,1)S(1)}, bf16[144,1024]{1,0:T(8,128)(2,1)S(1)}, u32[]{:S(2)}, u32[]{:S(2)}) collective-permute-start(bf16[144,1024]{1,0:T(8,128)(2,1)S(1)} %join.2.x_ref.refs_4_.refs_0_), channel_id=1, source_target_pairs={{0,1},{1,0},{2,3},{3,2},{4,5},{5,4},{6,7},{7,6},{8,9},{9,8},{10,11... | collective-permute-start | bytes 884744 | tf_op jit(solution)/shard_map/ppermute | solution.py:367
  19.9 9.7 %collective-permute-start.4 = (bf16[144,1024]{1,0:T(8,128)(2,1)S(1)}, bf16[144,1024]{1,0:T(8,128)(2,1)S(1)}, u32[]{:S(2)}, u32[]{:S(2)}) collective-permute-start(bf16[144,1024]{1,0:T(8,128)(2,1)S(1)} %join.2.x_ref.refs_4_.refs_0_), channel_id=1, source_target_pairs={{0,16},{16,0},{1,17},{17,1},{2,18},{18,2},{3,19},{19,3},{4,20},{20... | collective-permute-start | bytes 884744 | tf_op jit(solution)/shard_map/ppermute | solution.py:367
  21.5 11.9 %collective-permute-start.8 = (bf16[144,1024]{1,0:T(8,128)(2,1)S(1)}, bf16[144,1024]{1,0:T(8,128)(2,1)S(1)}, u32[]{:S(2)}, u32[]{:S(2)}) collective-permute-start(bf16[144,1024]{1,0:T(8,128)(2,1)S(1)} %join.3.refs_0_), channel_id=1, source_target_pairs={{0,16},{16,0},{1,17},{17,1},{2,18},{18,2},{3,19},{19,3},{4,20},{20... | collective-permute-start | bytes 884744 | tf_op jit(solution)/shard_map/ppermute | solution.py:367
  22.7 10.7 %collective-permute-start.9 = (bf16[144,1024]{1,0:T(8,128)(2,1)S(1)}, bf16[144,1024]{1,0:T(8,128)(2,1)S(1)}, u32[]{:S(2)}, u32[]{:S(2)}) collective-permute-start(bf16[144,1024]{1,0:T(8,128)(2,1)S(1)} %join.3.refs_0_), channel_id=1, source_target_pairs={{0,1},{1,0},{2,3},{3,2},{4,5},{5,4},{6,7},{7,6},{8,9},{9,8},{10,11... | collective-permute-start | bytes 884744 | tf_op jit(solution)/shard_map/ppermute | solution.py:367
  33.5 8.2 %collective-permute-start.10 = (bf16[144,1024]{1,0:T(8,128)(2,1)S(1)}, bf16[144,1024]{1,0:T(8,128)(2,1)S(1)}, u32[]{:S(2)}, u32[]{:S(2)}) collective-permute-start(bf16[144,1024]{1,0:T(8,128)(2,1)S(1)} %get-tuple-element.63), channel_id=1, source_target_pairs={{0,16},{16,0},{1,17},{17,1},{2,18},{18,2},{3,19},{19,3},{4,20},{20... | collective-permute-start | bytes 884744 | tf_op jit(solution)/shard_map/ppermute | solution.py:367
  35.0 9.1 %collective-permute-start.11 = (bf16[144,1024]{1,0:T(8,128)(2,1)S(1)}, bf16[144,1024]{1,0:T(8,128)(2,1)S(1)}, u32[]{:S(2)}, u32[]{:S(2)}) collective-permute-start(bf16[144,1024]{1,0:T(8,128)(2,1)S(1)} %get-tuple-element.66), channel_id=1, source_target_pairs={{0,1},{1,0},{2,3},{3,2},{4,5},{5,4},{6,7},{7,6},{8,9},{9,8},{10,11... | collective-permute-start | bytes 884744 | tf_op jit(solution)/shard_map/ppermute | solution.py:367
  35.1 12.9 %collective-permute-start.12 = (bf16[72,1024]{1,0:T(8,128)(2,1)S(1)}, bf16[72,1024]{1,0:T(8,128)(2,1)S(1)}, u32[]{:S(2)}, u32[]{:S(2)}) collective-permute-start(bf16[72,1024]{1,0:T(8,128)(2,1)S(1)} %get-tuple-element.75), channel_id=1, source_target_pairs={{0,2},{2,0},{4,6},{6,4},{1,3},{3,1},{5,7},{7,5},{8,10},{10,8},{12,... | collective-permute-start | bytes 442376 | tf_op jit(solution)/shard_map/ppermute | solution.py:372
  35.1 12.9 %collective-permute-start.13 = (bf16[72,1024]{1,0:T(8,128)(2,1)S(1)}, bf16[72,1024]{1,0:T(8,128)(2,1)S(1)}, u32[]{:S(2)}, u32[]{:S(2)}) collective-permute-start(bf16[72,1024]{1,0:T(8,128)(2,1)S(1)} %get-tuple-element.76), channel_id=1, source_target_pairs={{0,4},{2,6},{4,0},{6,2},{1,5},{3,7},{5,1},{7,3},{8,12},{10,14},{12... | collective-permute-start | bytes 442376 | tf_op jit(solution)/shard_map/ppermute | solution.py:372
  39.2 8.7 %collective-permute-start.14 = (bf16[72,1024]{1,0:T(8,128)(2,1)S(1)}, bf16[72,1024]{1,0:T(8,128)(2,1)S(1)}, u32[]{:S(2)}, u32[]{:S(2)}) collective-permute-start(bf16[72,1024]{1,0:T(8,128)(2,1)S(1)} %get-tuple-element.77), channel_id=1, source_target_pairs={{0,6},{2,4},{4,2},{6,0},{1,7},{3,5},{5,3},{7,1},{8,14},{10,12},{12... | collective-permute-start | bytes 442376 | tf_op jit(solution)/shard_map/ppermute | solution.py:372
  48.0 6.8 %collective-permute-start.15 = (bf16[144,1024]{1,0:T(8,128)(2,1)S(1)}, bf16[144,1024]{1,0:T(8,128)(2,1)S(1)}, u32[]{:S(2)}, u32[]{:S(2)}) collective-permute-start(bf16[144,1024]{1,0:T(8,128)(2,1)S(1)} %get-tuple-element.79), channel_id=1, source_target_pairs={{0,1},{1,0},{2,3},{3,2},{4,5},{5,4},{6,7},{7,6},{8,9},{9,8},{10,11... | collective-permute-start | bytes 884744 | tf_op jit(solution)/shard_map/ppermute | solution.py:367
  50.1 5.8 %collective-permute-start.16 = (bf16[512,1024]{1,0:T(8,128)(2,1)S(1)}, bf16[512,1024]{1,0:T(8,128)(2,1)S(1)}, u32[]{:S(2)}, u32[]{:S(2)}) collective-permute-start(bf16[512,1024]{1,0:T(8,128)(2,1)S(1)} %get-tuple-element.80), channel_id=1, source_target_pairs={{0,8},{8,0},{1,9},{9,1},{2,10},{10,2},{3,11},{11,3},{4,12},{12,4},... | collective-permute-start | bytes 3145736 | tf_op jit(solution)/shard_map/ppermute | solution.py:367
  54.8 2.7 %collective-permute-start.17 = (bf16[512,1024]{1,0:T(8,128)(2,1)S(1)}, bf16[512,1024]{1,0:T(8,128)(2,1)S(1)}, u32[]{:S(2)}, u32[]{:S(2)}) collective-permute-start(bf16[512,1024]{1,0:T(8,128)(2,1)S(1)} %get-tuple-element.84), channel_id=1, source_target_pairs={{0,8},{8,0},{1,9},{9,1},{2,10},{10,2},{3,11},{11,3},{4,12},{12,4},... | collective-permute-start | bytes 3145736 | tf_op jit(solution)/shard_map/ppermute | solution.py:367

commit v8 on v7

--- a/solution.py
+++ b/solution.py
@@ -16,6 +16,7 @@
 LARGE = pltpu.CompilerParams(vmem_limit_bytes=16 * MIB)
 SMALL = pltpu.CompilerParams(vmem_limit_bytes=12 * MIB)
 CHEAP = pl.CostEstimate(flops=0, bytes_accessed=0, transcendentals=0)
+DEAR = pl.CostEstimate(flops=20_000_000_000, bytes_accessed=0, transcendentals=0)
 F32 = jnp.float32
 BF16 = jnp.bfloat16
 HERE = pl.BlockSpec(memory_space=pltpu.VMEM)
@@ -165,19 +166,25 @@
     )(kept(value))
 
 
-def forward_kernel(fetch, down, pair, unused, x_ref, wg_ref, wu_ref, *refs):
+def forward_kernel(n, fetch, down, pair, unused, *refs):
     refs = list(refs)
+    xs = [refs.pop(0) for _ in range(n)]
+    wg_ref, wu_ref = refs.pop(0), refs.pop(0)
     wd_ref = refs.pop(0) if down else None
     other_ref = refs.pop(0) if pair else None
     refs = refs[unused:]
     act_ref, coef_ref = refs.pop(0), refs.pop(0)
-    if down:
-        shares = [refs.pop(0) for _ in range(EXPERTS if pair else 1)]
+    shares = [refs.pop(0) for _ in range(EXPERTS if pair else down)]
     if fetch:
         sources, sems = (wg_ref, wu_ref), refs.pop()
         wg_ref, wu_ref = refs.pop(0), refs.pop(0)
-    if down:
-        acc_ref = refs.pop(0)
+    acc_ref = refs.pop(0) if down else None
+    part = xs[0].shape[0]
+    x_ref = xs[0]
+    if n > 1:
+        x_ref = refs.pop(0)
+        for i in range(n):
+            x_ref[i * part : (i + 1) * part, :] = xs[i][...]
     steps = wg_ref.shape[1] // PAIR
 
     def copies(j):
@@ -207,37 +214,43 @@
             act_ref[:, cols] = act.astype(BF16)
             coef_ref[:, cols] = (up * slope).astype(BF16)
             if down:
-                hidden = (act * up).astype(BF16)
+                hidden = (act[:part] * up[:part]).astype(BF16)
                 acc_ref[...] += jnp.dot(hidden, wd_ref[cols, :], preferred_element_type=F32)
 
     if pair:
         other = other_ref[...].astype(F32)
         for k in range(EXPERTS):
             rows = slice(k * CAP, (k + 1) * CAP)
-            shares[k][...] = jnp.concatenate([other[rows], acc_ref[rows, :]], axis=0).astype(BF16)
+            block = jnp.concatenate([other[rows], acc_ref[rows, :]], axis=0).astype(BF16)
+            shares[k][...] = block
     elif down:
         shares[0][...] = acc_ref[...].astype(BF16)
 
 
-def forward(x, wg, wu, wd=None, other=None, fetch=False, earlier=()):
-    (rows, width), cols = x.shape, wg.shape[1]
+def forward(xs, wg, wu, wd=None, other=None, fetch=False, earlier=()):
+    n, (part, width), cols = len(xs), xs[0].shape, wg.shape[1]
+    rows = n * part
     down, pair = wd is not None, other is not None
-    shares = [jax.ShapeDtypeStruct((rows, width), BF16)]
+    shares = [jax.ShapeDtypeStruct((part, width), BF16)] * down
     if pair:
         shares = [jax.ShapeDtypeStruct((2 * CAP, width), BF16)] * EXPERTS
     weights = [kept(wg), kept(wu)] if fetch else [wg, wu]
     return pl.pallas_call(
-        functools.partial(forward_kernel, fetch, down, pair, len(earlier)),
+        functools.partial(forward_kernel, n, fetch, down, pair, len(earlier)),
         out_shape=[jax.ShapeDtypeStruct((rows, cols), BF16)] * 2
-        + shares * down
+        + shares
         + [pltpu.VMEM(wg.shape, wg.dtype)] * (2 * fetch),
-        in_specs=[HERE] + [AFAR if fetch else HERE] * 2 + [HERE] * (down + pair) + [ANYWHERE] * len(earlier),
-        scratch_shapes=[pltpu.VMEM((rows, width), F32)] * down
+        in_specs=[HERE] * n
+        + [AFAR if fetch else HERE] * 2
+        + [HERE] * (down + pair)
+        + [ANYWHERE] * len(earlier),
+        scratch_shapes=[pltpu.VMEM((part, width), F32)] * down
+        + [pltpu.VMEM((rows, width), BF16)] * (n > 1)
         + [pltpu.SemaphoreType.DMA((cols // PAIR, 2))] * fetch,
         compiler_params=LARGE,
         cost_estimate=CHEAP,
         name="forward" + "_fetch" * fetch + "_down" * down,
-    )(x, *weights, *([wd] * down), *([other] * pair), *earlier)
+    )(*xs, *weights, *([wd] * down), *([other] * pair), *earlier)
 
 
 def turn_kernel(_, __, *refs):
@@ -267,100 +280,121 @@
 def backward_kernel(first, counts, xt_ref, *refs):
     n = len(counts)
     gs, acts, coefs = refs[:4], refs[4 : 4 + n], refs[4 + n : 4 + 2 * n]
-    wdt_ref, own_ref, sib_ref, g_ref = refs[4 + 2 * n :]
+    wdt_ref, *_, own_ref, sib_ref, g_ref = refs[4 + 2 * n :]
     part = gs[0].shape[0]
     share = own_ref.shape[0] // 2
     for i in range(4):
         g_ref[i * part : (i + 1) * part, :] = gs[i][...]
 
-    @pl.loop(0, own_ref.shape[1] // PAIR)
+    def strip(start):
+        here = pl.ds(pl.multiple_of(start, STRIP), STRIP)
+        cols = pl.ds(pl.multiple_of(start + first, STRIP), STRIP)
+        d_hidden = jnp.dot(g_ref[...], wdt_ref[:, cols], preferred_element_type=F32)
+        for row, parts in ((0, coefs), (share, acts)):
+            factor = jnp.concatenate([p[:, cols] for p in parts], axis=0).astype(F32)
+            d_cols = (d_hidden * factor).astype(BF16)
+            total = jnp.dot(xt_ref[...], d_cols, preferred_element_type=F32).astype(BF16)
+            own_ref[row : row + share, here] = total[:share]
+            sib_ref[row : row + share, here] = total[share:]
+
+    pairs = own_ref.shape[1] // PAIR
+
+    @pl.loop(0, pairs)
     def _(j):
         for i in range(PAIR // STRIP):
-            here = pl.ds(pl.multiple_of(j * PAIR + i * STRIP, STRIP), STRIP)
-            cols = pl.ds(pl.multiple_of(j * PAIR + i * STRIP + first, STRIP), STRIP)
-            d_hidden = jnp.dot(g_ref[...], wdt_ref[:, cols], preferred_element_type=F32)
-            for row, parts in ((0, coefs), (share, acts)):
-                factor = jnp.concatenate([p[:, cols] for p in parts], axis=0).astype(F32)
-                d_cols = (d_hidden * factor).astype(BF16)
-                total = jnp.dot(xt_ref[...], d_cols, preferred_element_type=F32).astype(BF16)
-                own_ref[row : row + share, here] = total[:share]
-                sib_ref[row : row + share, here] = total[share:]
-
-
-def backward(xt, gs, acts, coefs, wdt, first, cols):
+            strip(j * PAIR + i * STRIP)
+
+    for start in range(pairs * PAIR, own_ref.shape[1], STRIP):
+        strip(start)
+
+
+def backward(xt, gs, acts, coefs, wdt, first, cols, earlier=()):
     part, width = gs[0].shape
     height, rows = xt.shape
     counts = tuple(a.shape[0] for a in acts)
     return pl.pallas_call(
         functools.partial(backward_kernel, first, counts),
         out_shape=[jax.ShapeDtypeStruct((height, cols), BF16)] * 2,
-        in_specs=[HERE] * (6 + 2 * len(acts)),
+        in_specs=[HERE] * (6 + 2 * len(acts)) + [ANYWHERE] * len(earlier),
         scratch_shapes=[pltpu.VMEM((rows, width), BF16)],
         compiler_params=LARGE,
-        cost_estimate=CHEAP,
+        cost_estimate=DEAR,
         name="backward",
-    )(xt, *gs, *acts, *coefs, wdt)
-
-
-def finish_kernel(*refs):
-    gate_ref, up_ref = refs[8:]
-    half = refs[0].shape[1]
-    for i in range(2):
-        cols = slice(i * half, (i + 1) * half)
-        own_gate, own_up, got_gate, got_up = [r[...].astype(F32) for r in refs[4 * i : 4 * i + 4]]
-        gate_ref[:, cols] = (own_gate + got_gate).astype(BF16)
-        up_ref[:, cols] = (own_up + got_up).astype(BF16)
-
-
-def finish(own0, got0, own1, got1):
-    share, half = own0.shape[0] // 2, own0.shape[1]
-    steps = 2
-    upper = pl.BlockSpec((share // steps, half), lambda i: (i, 0))
-    lower = pl.BlockSpec((share // steps, half), lambda i: (i + steps, 0))
-    return pl.pallas_call(
-        finish_kernel,
-        grid=(steps,),
-        in_specs=[upper, lower] * 4,
-        out_specs=[pl.BlockSpec((share // steps, 2 * half), lambda i: (i, 0))] * 2,
-        out_shape=[jax.ShapeDtypeStruct((share, 2 * half), BF16)] * 2,
+    )(xt, *gs, *acts, *coefs, wdt, *earlier)
+
+
+def finish_kernel(spans, more, *refs):
+    n = len(spans)
+    pairs = [refs[2 * i : 2 * i + 2] for i in range(n)]
+    gate_ref, up_ref, gate, up, sems = refs[2 * n + 2 * more :]
+    share = gate_ref.shape[0]
+    low = spans[0][0]
+    copies = []
+    for i, ((first, cols), (own, got)) in enumerate(zip(spans, pairs)):
+        for j, (target, held) in enumerate(((gate_ref, gate), (up_ref, up))):
+            rows = slice(j * share, (j + 1) * share)
+            here = pl.ds(first - low, cols)
+            held[:, here] = (own[rows, :].astype(F32) + got[rows, :].astype(F32)).astype(BF16)
+            copies.append(
+                pltpu.make_async_copy(held.at[:, here], target.at[:, pl.ds(first, cols)], sems.at[i, j])
+            )
+            copies[-1].start()
+    for copy in copies:
+        copy.wait()
+
+
+def finish(owns, gots, firsts, width, held=()):
+    share = owns[0].shape[0] // 2
+    spans = tuple((first, own.shape[1]) for first, own in zip(firsts, owns))
+    total = sum(cols for _, cols in spans)
+    n, more = len(owns), len(held) > 0
+    return pl.pallas_call(
+        functools.partial(finish_kernel, spans, more),
+        out_shape=[jax.ShapeDtypeStruct((share, width), BF16)] * 2,
+        in_specs=[HERE] * (2 * n) + [ANYWHERE] * (2 * more),
+        out_specs=[ANYWHERE] * 2,
+        scratch_shapes=[pltpu.VMEM((share, total), BF16)] * 2 + [pltpu.SemaphoreType.DMA((n, 2))],
+        input_output_aliases={2 * n: 0, 2 * n + 1: 1} if more else {},
         compiler_params=SMALL,
         cost_estimate=CHEAP,
         name="finish",
-    )(own0, own0, got0, got0, own1, own1, got1, got1)
+    )(*[v for both in zip(owns, gots) for v in both], *held)
 
 
 def split_kernel(*refs):
     blocks = [r[...].astype(F32) for r in refs[:EXPERTS]]
-    refs[EXPERTS][...] = jnp.concatenate([b[:CAP] for b in blocks], axis=0).astype(BF16)
-    refs[EXPERTS + 1][...] = jnp.concatenate([b[CAP:] for b in blocks], axis=0).astype(BF16)
-
-
-def split(blocks):
+    refs[-2][...] = jnp.concatenate([b[:CAP] for b in blocks], axis=0).astype(BF16)
+    refs[-1][...] = jnp.concatenate([b[CAP:] for b in blocks], axis=0).astype(BF16)
+
+
+def split(blocks, earlier):
     width = blocks[0].shape[1]
     return pl.pallas_call(
         split_kernel,
         out_shape=[jax.ShapeDtypeStruct((EXPERTS * CAP, width), BF16)] * 2,
+        in_specs=[HERE] * EXPERTS + [ANYWHERE] * len(earlier),
         compiler_params=SMALL,
         cost_estimate=CHEAP,
         name="split",
-    )(*blocks)
-
-
-def unpack_kernel(placer_ref, mine_ref, got_ref, out_ref):
+    )(*blocks, *earlier)
+
+
+def unpack_kernel(placer_ref, mine_ref, got_ref, *refs):
     chosen = placer_ref[...].astype(F32).T.astype(BF16)
     total = jnp.dot(chosen, mine_ref[...], preferred_element_type=F32)
     total += jnp.dot(chosen, got_ref[...], preferred_element_type=F32)
-    out_ref[...] = total.astype(BF16)
-
-
-def unpack(placer, mine, got):
+    refs[-1][...] = total.astype(BF16)
+
+
+def unpack(placer, mine, got, earlier):
     return pl.pallas_call(
         unpack_kernel,
         out_shape=jax.ShapeDtypeStruct((placer.shape[1], mine.shape[1]), BF16),
-        compiler_params=SMALL,
-        cost_estimate=CHEAP,
+        in_specs=[HERE] * 3 + [AFAR] * len(earlier),
+        compiler_params=SMALL,
+        cost_estimate=DEAR,
         name="unpack",
-    )(placer, mine, got)
+    )(placer, mine, got, *[kept(v) for v in earlier])
 
 
 def swap(value, axis):
@@ -394,28 +428,27 @@
     g_own = join(moved, [x_own])
     g_near, g_far = swap(g_own, "half"), swap(g_own, "far")
 
-    act0, coef0, share_own, wg, wu = forward(x_own, w_gate, w_up, wd, fetch=True)
-    act1, coef1, *shares = forward(x_near, wg, wu, wd, other=share_own, earlier=[x_far])
+    wg, wu = w_gate, w_up
+    act0, coef0, share_own = forward([x_own], wg, wu, wd)
+    act1, coef1, *shares = forward([x_near, x_far], wg, wu, wd, other=share_own)
     x_pass, g_pass = relay([x_near, g_far], [mark(act1), g_near])
     x_corner, g_corner = swap(x_pass, "far"), swap(g_pass, "half")
     returned = across_planes(shares)
-    (x_far,) = after([x_far], [act1])
-    act2, coef2 = forward(x_far, wg, wu)
-    (x_corner,) = after([x_corner], [act2])
-    act3, coef3 = forward(x_corner, wg, wu)
+    act2, coef2 = forward([x_corner], wg, wu)
     xt = turn(*scalars[1:], [x_own, x_near, x_far, x_corner], share)
 
     gs = [g_own, g_near, g_far, g_corner]
-    acts, coefs = [act0, act1, act2, act3], [coef0, coef1, coef2, coef3]
-    half = w_down.shape[0] // 2
+    acts, coefs = [act0, act1, act2], [coef0, coef1, coef2]
+    cols = w_down.shape[0]
+    half = cols // 2
     own0, sib0 = backward(xt, gs, acts, coefs, wdt, 0, half)
-    mine, theirs = split(after(returned[:1], [own0]) + returned[1:])
-    (xt,) = after([xt], [mine])
-    own1, sib1 = backward(xt, gs, acts, coefs, wdt, half, half)
+    mine, theirs = split(returned, [own0])
     got = swap(theirs, "half")
-    (sib1,) = after([sib1], [got])
-    outputs = unpack(placer, mine, got)
-    grad_gate, grad_up = finish(own0, swap(sib0, "core"), own1, swap(sib1, "core"))
+    own1, sib1 = backward(xt, gs, acts, coefs, wdt, half, half, [mine])
+    got0, got1 = swap(sib0, "core"), swap(sib1, "core")
+    held = finish([own0], [got0], (0,), cols)
+    outputs = unpack(placer, mine, got, held[:1])
+    grad_gate, grad_up = finish([own1], [got1], (half,), cols, held)
     return outputs, grad_gate, grad_up
 
 

time: 59.1 us -> 57 us (0.964)
  Pallas kernels: 28.3 us -> 26.6 us
    pallas_call x5, Pallas kernels: 15 us -> 13.2 us  [the longest x3 11 us: forward(): pl.pallas_call(functools.partial(forward_kernel, n, fetch, down, pair, le...]
  transfers between devices with their start and end apart: 18 -> 18, of which waited for: 3 -> 4; matrix products, arithmetic and copies ran while one was open for 0% -> 0% of each run, Pallas kernels for 43% -> 42%
where the time goes in v8:
time: 57 us; the launch traced here: 56.9 us
  starting transfers between devices  26.8 us (47%)
  Pallas kernels  26.6 us (47%)
  waiting for transfers between devices  2.6 us (5%)
  between operations  0.83 us (1%)
    ppermute x9, starting transfers between devices, across_planes(): lax.ppermute(blocks[k], 'arch', [(i, i ^ k) for i in range(EXPERTS)])  17.5 us
    pallas_call x3, Pallas kernels, forward(): pl.pallas_call(functools.partial(forward_kernel, n, fetch, down, pair, le...  11 us
    ppermute x9, starting transfers between devices, swap(): return lax.ppermute(value, axis, [(0, 1), (1, 0)])  9.38 us
    pallas_call x2, Pallas kernels, backward(): pl.pallas_call(functools.partial(backward_kernel, first, counts), out_sha...  7.56 us
    pallas_call x1, Pallas kernels, flip(): pl.pallas_call(flip_kernel, out_shape=[pltpu.VMEM(value.shape, value.dtyp...  2.88 us
    ppermute x9, waiting for transfers between devices, swap(): return lax.ppermute(value, axis, [(0, 1), (1, 0)])  2.26 us
    pallas_call x2, Pallas kernels, finish(): pl.pallas_call(functools.partial(finish_kernel, spans, more), out_shape=[...  2.21 us
    pallas_call x1, Pallas kernels, pack(): pl.pallas_call(pack_kernel, out_shape=[jax.ShapeDtypeStruct((EXPERTS * CA...  1.46 us
  transfers between devices with their start and end apart: 18, of which 4 were waited for; matrix products, arithmetic and copies ran while one was open for 0% of the time, Pallas kernels for 42%

profile of v8, /device:TPU:0, one launch (start us, length us, event | category | flops | bytes accessed | tf_op | source)
XLA Modules:
  0.0 56.9 jit_solution(4826821698642418111)
XLA Ops:
  0.6 1.5 %pack.1 = (bf16[144,128]{1,0:T(8,128)(2,1)S(1)}, bf16[36,1024]{1,0:T(8,128)(2,1)S(1)}, bf16[36,1024]{1,0:T(8,128)(2,1)S(1)}, bf16[36,1024]{1,0:T(8,128)(2,1)S(1)...) custom-call(s32[1]{0:T(128)} %bitcast.plane_ref, ...), custom_call_target="tpu_custom_call" | custom-call | tf_op jit(solution)/shard_map/pack/pallas_call | solution.py:78
  2.1 5.1 %collective-permute-start = (bf16[36,1024]{1,0:T(8,128)(2,1)S(1)}, bf16[36,1024]{1,0:T(8,128)(2,1)S(1)}, u32[]{:S(2)}, u32[]{:S(2)}) collective-permute-start(bf16[36,1024]{1,0:T(8,128)(2,1)S(1)} %get-tuple-element.39), channel_id=1, source_target_pairs={{0,6},{2,4},{4,2},{6,0},{1,7},{3,5},{5,3},{7,1},{8,14},{10,12},{12... | collective-permute-start | bytes 221192 | tf_op jit(solution)/shard_map/ppermute | solution.py:406
  7.2 0.6 %collective-permute-start.2 = (bf16[36,1024]{1,0:T(8,128)(2,1)S(1)}, bf16[36,1024]{1,0:T(8,128)(2,1)S(1)}, u32[]{:S(2)}, u32[]{:S(2)}) collective-permute-start(bf16[36,1024]{1,0:T(8,128)(2,1)S(1)} %get-tuple-element.41), channel_id=1, source_target_pairs={{0,2},{2,0},{4,6},{6,4},{1,3},{3,1},{5,7},{7,5},{8,10},{10,8},{12,... | collective-permute-start | bytes 221192 | tf_op jit(solution)/shard_map/ppermute | solution.py:406
  7.9 3.7 %collective-permute-start.8 = (bf16[36,1024]{1,0:T(8,128)(2,1)S(1)}, bf16[36,1024]{1,0:T(8,128)(2,1)S(1)}, u32[]{:S(2)}, u32[]{:S(2)}) collective-permute-start(bf16[36,1024]{1,0:T(8,128)(2,1)S(1)} %get-tuple-element.51), channel_id=1, source_target_pairs={{0,6},{2,4},{4,2},{6,0},{1,7},{3,5},{5,3},{7,1},{8,14},{10,12},{12... | collective-permute-start | bytes 221192 | tf_op jit(solution)/shard_map/ppermute | solution.py:406
  11.6 0.0 collective-permute-done.refs_0_
  11.6 3.6 %collective-permute-start.10 = (bf16[36,1024]{1,0:T(8,128)(2,1)S(1)}, bf16[36,1024]{1,0:T(8,128)(2,1)S(1)}, u32[]{:S(2)}, u32[]{:S(2)}) collective-permute-start(bf16[36,1024]{1,0:T(8,128)(2,1)S(1)} %get-tuple-element.53), channel_id=1, source_target_pairs={{0,2},{2,0},{4,6},{6,4},{1,3},{3,1},{5,7},{7,5},{8,10},{10,8},{12,... | collective-permute-start | bytes 221192 | tf_op jit(solution)/shard_map/ppermute | solution.py:406
  15.2 2.9 %flip.1 = (bf16[2048,1024]{1,0:T(8,128)(2,1)S(1)}, bf16[1024,2048]{1,0:T(8,128)(2,1)S(1)}) custom-call(bf16[2048,1024]{1,0:T(8,128)(2,1)} %source_ref), custom_call_target="tpu_custom_call" | custom-call | tf_op jit(solution)/shard_map/flip/pallas_call | solution.py:157
  18.1 0.3 collective-permute-done.1.refs_1_
  18.5 1.4 %collective-permute-start.3 = (bf16[144,1024]{1,0:T(8,128)(2,1)S(1)}, bf16[144,1024]{1,0:T(8,128)(2,1)S(1)}, u32[]{:S(2)}, u32[]{:S(2)}) collective-permute-start(bf16[144,1024]{1,0:T(8,128)(2,1)S(1)} %join.2.refs_0_.refs_4_), channel_id=1, source_target_pairs={{0,1},{1,0},{2,3},{3,2},{4,5},{5,4},{6,7},{7,6},{8,9},{9,8},{10,11... | collective-permute-start | bytes 884744 | tf_op jit(solution)/shard_map/ppermute | solution.py:401
  19.9 1.5 %collective-permute-start.4 = (bf16[144,1024]{1,0:T(8,128)(2,1)S(1)}, bf16[144,1024]{1,0:T(8,128)(2,1)S(1)}, u32[]{:S(2)}, u32[]{:S(2)}) collective-permute-start(bf16[144,1024]{1,0:T(8,128)(2,1)S(1)} %join.2.refs_0_.refs_4_), channel_id=1, source_target_pairs={{0,16},{16,0},{1,17},{17,1},{2,18},{18,2},{3,19},{19,3},{4,20},{20... | collective-permute-start | bytes 884744 | tf_op jit(solution)/shard_map/ppermute | solution.py:401
  21.4 0.0 collective-permute-done.8.refs_0_
  21.4 0.0 collective-permute-done.9.refs_1_
  21.5 1.3 %collective-permute-start.11 = (bf16[144,1024]{1,0:T(8,128)(2,1)S(1)}, bf16[144,1024]{1,0:T(8,128)(2,1)S(1)}, u32[]{:S(2)}, u32[]{:S(2)}) collective-permute-start(bf16[144,1024]{1,0:T(8,128)(2,1)S(1)} %join.3.refs_0_), channel_id=1, source_target_pairs={{0,16},{16,0},{1,17},{17,1},{2,18},{18,2},{3,19},{19,3},{4,20},{20... | collective-permute-start | bytes 884744 | tf_op jit(solution)/shard_map/ppermute | solution.py:401
  22.7 1.5 %collective-permute-start.12 = (bf16[144,1024]{1,0:T(8,128)(2,1)S(1)}, bf16[144,1024]{1,0:T(8,128)(2,1)S(1)}, u32[]{:S(2)}, u32[]{:S(2)}) collective-permute-start(bf16[144,1024]{1,0:T(8,128)(2,1)S(1)} %join.3.refs_0_), channel_id=1, source_target_pairs={{0,1},{1,0},{2,3},{3,2},{4,5},{5,4},{6,7},{7,6},{8,9},{9,8},{10,11... | collective-permute-start | bytes 884744 | tf_op jit(solution)/shard_map/ppermute | solution.py:401
  24.2 3.7 %forward_down.2 = (bf16[144,2048]{1,0:T(8,128)(2,1)S(1)}, bf16[144,2048]{1,0:T(8,128)(2,1)S(1)}, bf16[144,1024]{1,0:T(8,128)(2,1)S(1)}) custom-call(bf16[144,1024]{1,0:T(8,128)(2,1)S(1)} %join.2.refs_0_.refs_4_, bf16[1024,2048]{1,0:T(8,128)(2,1)S(1)} %copy-done, bf16[1024,2048]{1,0:T(8,128)(2,1)S(1)} %copy-done.1, ...), custom_call_target="tpu_custom_call" | custom-call | tf_op jit(solution)/shard_map/forward_down/pallas_call | solution.py:238
  28.0 1.4 %collective-permute-done.4.refs_1_.refs_2_.refs_6_ = bf16[144,1024]{1,0:T(8,128)(2,1)S(1)} collective-permute-done((bf16[144,1024]{1,0:T(8,128)(2,1)S(1)}, bf16[144,1024]{1,0:T(8,128)(2,1)S(1)}, u32[]{:S(2)}, u32[]{:S(2)}) %collective-permute-start.4) | collective-permute-done | bytes 294944 | tf_op jit(solution)/shard_map/ppermute | solution.py:401
  29.4 5.0 %forward_down.3 = (bf16[288,2048]{1,0:T(8,128)(2,1)S(1)}, bf16[288,2048]{1,0:T(8,128)(2,1)S(1)}, bf16[72,1024]{1,0:T(8,128)(2,1)S(1)}, bf16[72,1024]{1,0:T(8,128...) custom-call(bf16[144,1024]{1,0:T(8,128)(2,1)S(1)} %collective-permute-done.3.refs_0_.refs_1_.refs_5_, ...), custom_call_target="tpu_custom_call" | custom-call | tf_op jit(solution)/shard_map/forward_down/pallas_call | solution.py:238
  34.5 1.7 %collective-permute-start.13 = (bf16[144,1024]{1,0:T(8,128)(2,1)S(1)}, bf16[144,1024]{1,0:T(8,128)(2,1)S(1)}, u32[]{:S(2)}, u32[]{:S(2)}) collective-permute-start(bf16[144,1024]{1,0:T(8,128)(2,1)S(1)} %get-tuple-element.56), channel_id=1, source_target_pairs={{0,16},{16,0},{1,17},{17,1},{2,18},{18,2},{3,19},{19,3},{4,20},{20... | collective-permute-start | bytes 884744 | tf_op jit(solution)/shard_map/ppermute | solution.py:401
  36.3 4.2 %collective-permute-start.6 = (bf16[72,1024]{1,0:T(8,128)(2,1)S(1)}, bf16[72,1024]{1,0:T(8,128)(2,1)S(1)}, u32[]{:S(2)}, u32[]{:S(2)}) collective-permute-start(bf16[72,1024]{1,0:T(8,128)(2,1)S(1)} %get-tuple-element.49), channel_id=1, source_target_pairs={{0,4},{2,6},{4,0},{6,2},{1,5},{3,7},{5,1},{7,3},{8,12},{10,14},{12... | collective-permute-start | bytes 442376 | tf_op jit(solution)/shard_map/ppermute | solution.py:406
  40.4 0.2 collective-permute-start.7
  40.6 0.7 %collective-permute-done.13.refs_3_.refs_7_.refs_0_ = bf16[144,1024]{1,0:T(8,128)(2,1)S(1)} collective-permute-done((bf16[144,1024]{1,0:T(8,128)(2,1)S(1)}, bf16[144,1024]{1,0:T(8,128)(2,1)S(1)}, u32[]{:S(2)}, u32[]{:S(2)}) %collective-permute-start.13) | collective-permute-done | bytes 294944 | tf_op jit(solution)/shard_map/ppermute | solution.py:401
  41.3 0.2 turn.1.xt_ref
  41.6 2.2 %forward.1 = (bf16[144,2048]{1,0:T(8,128)(2,1)S(1)}, bf16[144,2048]{1,0:T(8,128)(2,1)S(1)}) custom-call(bf16[144,1024]{1,0:T(8,128)(2,1)S(1)} %collective-permute-done.13.refs_3_.refs_7_.refs_0_, bf16[1024,2048]{1,0:T(8,128)(2,1)S(1)} %copy-done, bf16[1024,2048]{1,0:T(8,128)(2,1)S(1)} %copy-done.1), custom_call_target="tpu_custom_call" | custom-call | tf_op jit(solution)/shard_map/forward/pallas_call | solution.py:238
  43.8 3.8 %backward.2 = (bf16[512,1024]{1,0:T(8,128)(2,1)S(1)}, bf16[512,1024]{1,0:T(8,128)(2,1)S(1)}) custom-call(bf16[512,576]{1,0:T(8,128)(2,1)S(1)} %turn.1.xt_ref, bf16[144,1024]{1,0:T(8,128)(2,1)S(1)} %join.3.refs_0_, bf16[144,1024]{1,0:T(8,128)(2,1)S(1)} %collective-permute-done.12.refs_3_.refs_1_, ...), custom_call_target="tpu_custom_call" | custom-call | flops 20000000000 | tf_op jit(solution)/shard_map/backward/pallas_call | solution.py:315
  47.6 0.1 split.1
  47.7 1.4 %collective-permute-start.15 = (bf16[144,1024]{1,0:T(8,128)(2,1)S(1)}, bf16[144,1024]{1,0:T(8,128)(2,1)S(1)}, u32[]{:S(2)}, u32[]{:S(2)}) collective-permute-start(bf16[144,1024]{1,0:T(8,128)(2,1)S(1)} %get-tuple-element.65), channel_id=1, source_target_pairs={{0,1},{1,0},{2,3},{3,2},{4,5},{5,4},{6,7},{7,6},{8,9},{9,8},{10,11... | collective-permute-start | bytes 884744 | tf_op jit(solution)/shard_map/ppermute | solution.py:401
  49.1 3.8 %backward.3 = (bf16[512,1024]{1,0:T(8,128)(2,1)S(1)}, bf16[512,1024]{1,0:T(8,128)(2,1)S(1)}) custom-call(bf16[512,576]{1,0:T(8,128)(2,1)S(1)} %turn.1.xt_ref, bf16[144,1024]{1,0:T(8,128)(2,1)S(1)} %join.3.refs_0_, bf16[144,1024]{1,0:T(8,128)(2,1)S(1)} %collective-permute-done.12.refs_3_.refs_1_, ...), custom_call_target="tpu_custom_call" | custom-call | flops 20000000000 | tf_op jit(solution)/shard_map/backward/pallas_call | solution.py:315
  52.9 0.6 %collective-permute-start.17 = (bf16[512,1024]{1,0:T(8,128)(2,1)S(1)}, bf16[512,1024]{1,0:T(8,128)(2,1)S(1)}, u32[]{:S(2)}, u32[]{:S(2)}) collective-permute-start(bf16[512,1024]{1,0:T(8,128)(2,1)S(1)} %get-tuple-element.69), channel_id=1, source_target_pairs={{0,8},{8,0},{1,9},{9,1},{2,10},{10,2},{3,11},{11,3},{4,12},{12,4},... | collective-permute-start | bytes 3145736 | tf_op jit(solution)/shard_map/ppermute | solution.py:401
  53.5 1.1 %finish.2 = (bf16[256,2048]{1,0:T(8,128)(2,1)}, bf16[256,2048]{1,0:T(8,128)(2,1)}) custom-call(bf16[512,1024]{1,0:T(8,128)(2,1)S(1)} %get-tuple-element.63.refs_4_.refs_0_, bf16[512,1024]{1,0:T(8,128)(2,1)S(1)} %collective-permute-done.16.refs_1_), custom_call_target="tpu_custom_call" | custom-call | tf_op jit(solution)/shard_map/finish/pallas_call | solution.py:351
  54.6 1.0 %unpack.1 = bf16[128,1024]{1,0:T(8,128)(2,1)} custom-call(bf16[144,128]{1,0:T(8,128)(2,1)S(1)} %get-tuple-element.38.placer_ref, bf16[144,1024]{1,0:T(8,128)(2,1)S(1)} %get-tuple-element.64.mine_ref.refs_11_, bf16[144,1024]{1,0:T(8,128)(2,1)S(1)} %collective-permute-done.15.got_ref, bf16[256,2048]{1,0:T(8,128)(2,1)} %get-tuple-element.67.refs_0_.refs_2_), custom_call_target="tpu_custom_call" | custom-call | flops 20000000000 | tf_op jit(solution)/shard_map/unpack/pallas_call | solution.py:390
  55.6 0.1 collective-permute-done.17.refs_1_
  55.8 1.1 %finish.3 = (bf16[256,2048]{1,0:T(8,128)(2,1)}, bf16[256,2048]{1,0:T(8,128)(2,1)}) custom-call(bf16[512,1024]{1,0:T(8,128)(2,1)S(1)} %get-tuple-element.68.refs_0_, bf16[512,1024]{1,0:T(8,128)(2,1)S(1)} %collective-permute-done.17.refs_1_, bf16[256,2048]{1,0:T(8,128)(2,1)} %get-tuple-element.67.refs_0_.refs_2_, ...), custom_call_target="tpu_custom_call", output_to_operand_aliasing={{0}: (2, {}), {1}: (3, {})} | custom-call | tf_op jit(solution)/shard_map/finish/pallas_call | solution.py:351
  (24 shorter events, 0.2 us)
Async XLA Ops:
  2.1 9.5 %collective-permute-start = (bf16[36,1024]{1,0:T(8,128)(2,1)S(1)}, bf16[36,1024]{1,0:T(8,128)(2,1)S(1)}, u32[]{:S(2)}, u32[]{:S(2)}) collective-permute-start(bf16[36,1024]{1,0:T(8,128)(2,1)S(1)} %get-tuple-element.39), channel_id=1, source_target_pairs={{0,6},{2,4},{4,2},{6,0},{1,7},{3,5},{5,3},{7,1},{8,14},{10,12},{12... | collective-permute-start | bytes 221192 | tf_op jit(solution)/shard_map/ppermute | solution.py:406
  7.2 11.2 %collective-permute-start.1 = (bf16[36,1024]{1,0:T(8,128)(2,1)S(1)}, bf16[36,1024]{1,0:T(8,128)(2,1)S(1)}, u32[]{:S(2)}, u32[]{:S(2)}) collective-permute-start(bf16[36,1024]{1,0:T(8,128)(2,1)S(1)} %get-tuple-element.40), channel_id=1, source_target_pairs={{0,4},{2,6},{4,0},{6,2},{1,5},{3,7},{5,1},{7,3},{8,12},{10,14},{12... | collective-permute-start | bytes 221192 | tf_op jit(solution)/shard_map/ppermute | solution.py:406
  7.2 11.2 %collective-permute-start.2 = (bf16[36,1024]{1,0:T(8,128)(2,1)S(1)}, bf16[36,1024]{1,0:T(8,128)(2,1)S(1)}, u32[]{:S(2)}, u32[]{:S(2)}) collective-permute-start(bf16[36,1024]{1,0:T(8,128)(2,1)S(1)} %get-tuple-element.41), channel_id=1, source_target_pairs={{0,2},{2,0},{4,6},{6,4},{1,3},{3,1},{5,7},{7,5},{8,10},{10,8},{12,... | collective-permute-start | bytes 221192 | tf_op jit(solution)/shard_map/ppermute | solution.py:406
  7.9 13.5 %collective-permute-start.8 = (bf16[36,1024]{1,0:T(8,128)(2,1)S(1)}, bf16[36,1024]{1,0:T(8,128)(2,1)S(1)}, u32[]{:S(2)}, u32[]{:S(2)}) collective-permute-start(bf16[36,1024]{1,0:T(8,128)(2,1)S(1)} %get-tuple-element.51), channel_id=1, source_target_pairs={{0,6},{2,4},{4,2},{6,0},{1,7},{3,5},{5,3},{7,1},{8,14},{10,12},{12... | collective-permute-start | bytes 221192 | tf_op jit(solution)/shard_map/ppermute | solution.py:406
  11.6 9.8 %collective-permute-start.9 = (bf16[36,1024]{1,0:T(8,128)(2,1)S(1)}, bf16[36,1024]{1,0:T(8,128)(2,1)S(1)}, u32[]{:S(2)}, u32[]{:S(2)}) collective-permute-start(bf16[36,1024]{1,0:T(8,128)(2,1)S(1)} %get-tuple-element.52), channel_id=1, source_target_pairs={{0,4},{2,6},{4,0},{6,2},{1,5},{3,7},{5,1},{7,3},{8,12},{10,14},{12... | collective-permute-start | bytes 221192 | tf_op jit(solution)/shard_map/ppermute | solution.py:406
  11.6 9.8 %collective-permute-start.10 = (bf16[36,1024]{1,0:T(8,128)(2,1)S(1)}, bf16[36,1024]{1,0:T(8,128)(2,1)S(1)}, u32[]{:S(2)}, u32[]{:S(2)}) collective-permute-start(bf16[36,1024]{1,0:T(8,128)(2,1)S(1)} %get-tuple-element.53), channel_id=1, source_target_pairs={{0,2},{2,0},{4,6},{6,4},{1,3},{3,1},{5,7},{7,5},{8,10},{10,8},{12,... | collective-permute-start | bytes 221192 | tf_op jit(solution)/shard_map/ppermute | solution.py:406
  15.2 9.1 %copy-start = (bf16[1024,2048]{1,0:T(8,128)(2,1)S(1)}, bf16[1024,2048]{1,0:T(8,128)(2,1)}, u32[]{:S(2)}) copy-start(bf16[1024,2048]{1,0:T(8,128)(2,1)} %refs_1_.3) | copy-start | bytes 12582916
  15.2 9.1 %copy-start.1 = (bf16[1024,2048]{1,0:T(8,128)(2,1)S(1)}, bf16[1024,2048]{1,0:T(8,128)(2,1)}, u32[]{:S(2)}) copy-start(bf16[1024,2048]{1,0:T(8,128)(2,1)} %refs_2_.5) | copy-start | bytes 12582916
  18.5 9.5 %collective-permute-start.3 = (bf16[144,1024]{1,0:T(8,128)(2,1)S(1)}, bf16[144,1024]{1,0:T(8,128)(2,1)S(1)}, u32[]{:S(2)}, u32[]{:S(2)}) collective-permute-start(bf16[144,1024]{1,0:T(8,128)(2,1)S(1)} %join.2.refs_0_.refs_4_), channel_id=1, source_target_pairs={{0,1},{1,0},{2,3},{3,2},{4,5},{5,4},{6,7},{7,6},{8,9},{9,8},{10,11... | collective-permute-start | bytes 884744 | tf_op jit(solution)/shard_map/ppermute | solution.py:401
  19.9 9.5 %collective-permute-start.4 = (bf16[144,1024]{1,0:T(8,128)(2,1)S(1)}, bf16[144,1024]{1,0:T(8,128)(2,1)S(1)}, u32[]{:S(2)}, u32[]{:S(2)}) collective-permute-start(bf16[144,1024]{1,0:T(8,128)(2,1)S(1)} %join.2.refs_0_.refs_4_), channel_id=1, source_target_pairs={{0,16},{16,0},{1,17},{17,1},{2,18},{18,2},{3,19},{19,3},{4,20},{20... | collective-permute-start | bytes 884744 | tf_op jit(solution)/shard_map/ppermute | solution.py:401
  21.5 13.0 %collective-permute-start.11 = (bf16[144,1024]{1,0:T(8,128)(2,1)S(1)}, bf16[144,1024]{1,0:T(8,128)(2,1)S(1)}, u32[]{:S(2)}, u32[]{:S(2)}) collective-permute-start(bf16[144,1024]{1,0:T(8,128)(2,1)S(1)} %join.3.refs_0_), channel_id=1, source_target_pairs={{0,16},{16,0},{1,17},{17,1},{2,18},{18,2},{3,19},{19,3},{4,20},{20... | collective-permute-start | bytes 884744 | tf_op jit(solution)/shard_map/ppermute | solution.py:401
  22.7 11.8 %collective-permute-start.12 = (bf16[144,1024]{1,0:T(8,128)(2,1)S(1)}, bf16[144,1024]{1,0:T(8,128)(2,1)S(1)}, u32[]{:S(2)}, u32[]{:S(2)}) collective-permute-start(bf16[144,1024]{1,0:T(8,128)(2,1)S(1)} %join.3.refs_0_), channel_id=1, source_target_pairs={{0,1},{1,0},{2,3},{3,2},{4,5},{5,4},{6,7},{7,6},{8,9},{9,8},{10,11... | collective-permute-start | bytes 884744 | tf_op jit(solution)/shard_map/ppermute | solution.py:401
  34.5 6.8 %collective-permute-start.13 = (bf16[144,1024]{1,0:T(8,128)(2,1)S(1)}, bf16[144,1024]{1,0:T(8,128)(2,1)S(1)}, u32[]{:S(2)}, u32[]{:S(2)}) collective-permute-start(bf16[144,1024]{1,0:T(8,128)(2,1)S(1)} %get-tuple-element.56), channel_id=1, source_target_pairs={{0,16},{16,0},{1,17},{17,1},{2,18},{18,2},{3,19},{19,3},{4,20},{20... | collective-permute-start | bytes 884744 | tf_op jit(solution)/shard_map/ppermute | solution.py:401
  36.3 7.6 %collective-permute-start.14 = (bf16[144,1024]{1,0:T(8,128)(2,1)S(1)}, bf16[144,1024]{1,0:T(8,128)(2,1)S(1)}, u32[]{:S(2)}, u32[]{:S(2)}) collective-permute-start(bf16[144,1024]{1,0:T(8,128)(2,1)S(1)} %get-tuple-element.57), channel_id=1, source_target_pairs={{0,1},{1,0},{2,3},{3,2},{4,5},{5,4},{6,7},{7,6},{8,9},{9,8},{10,11... | collective-permute-start | bytes 884744 | tf_op jit(solution)/shard_map/ppermute | solution.py:401
  36.3 11.3 %collective-permute-start.5 = (bf16[72,1024]{1,0:T(8,128)(2,1)S(1)}, bf16[72,1024]{1,0:T(8,128)(2,1)S(1)}, u32[]{:S(2)}, u32[]{:S(2)}) collective-permute-start(bf16[72,1024]{1,0:T(8,128)(2,1)S(1)} %get-tuple-element.48), channel_id=1, source_target_pairs={{0,2},{2,0},{4,6},{6,4},{1,3},{3,1},{5,7},{7,5},{8,10},{10,8},{12,... | collective-permute-start | bytes 442376 | tf_op jit(solution)/shard_map/ppermute | solution.py:406
  36.3 11.4 %collective-permute-start.6 = (bf16[72,1024]{1,0:T(8,128)(2,1)S(1)}, bf16[72,1024]{1,0:T(8,128)(2,1)S(1)}, u32[]{:S(2)}, u32[]{:S(2)}) collective-permute-start(bf16[72,1024]{1,0:T(8,128)(2,1)S(1)} %get-tuple-element.49), channel_id=1, source_target_pairs={{0,4},{2,6},{4,0},{6,2},{1,5},{3,7},{5,1},{7,3},{8,12},{10,14},{12... | collective-permute-start | bytes 442376 | tf_op jit(solution)/shard_map/ppermute | solution.py:406
  40.4 7.2 %collective-permute-start.7 = (bf16[72,1024]{1,0:T(8,128)(2,1)S(1)}, bf16[72,1024]{1,0:T(8,128)(2,1)S(1)}, u32[]{:S(2)}, u32[]{:S(2)}) collective-permute-start(bf16[72,1024]{1,0:T(8,128)(2,1)S(1)} %get-tuple-element.50), channel_id=1, source_target_pairs={{0,6},{2,4},{4,2},{6,0},{1,7},{3,5},{5,3},{7,1},{8,14},{10,12},{12... | collective-permute-start | bytes 442376 | tf_op jit(solution)/shard_map/ppermute | solution.py:406
  47.7 6.9 %collective-permute-start.15 = (bf16[144,1024]{1,0:T(8,128)(2,1)S(1)}, bf16[144,1024]{1,0:T(8,128)(2,1)S(1)}, u32[]{:S(2)}, u32[]{:S(2)}) collective-permute-start(bf16[144,1024]{1,0:T(8,128)(2,1)S(1)} %get-tuple-element.65), channel_id=1, source_target_pairs={{0,1},{1,0},{2,3},{3,2},{4,5},{5,4},{6,7},{7,6},{8,9},{9,8},{10,11... | collective-permute-start | bytes 884744 | tf_op jit(solution)/shard_map/ppermute | solution.py:401
  49.1 4.4 %collective-permute-start.16 = (bf16[512,1024]{1,0:T(8,128)(2,1)S(1)}, bf16[512,1024]{1,0:T(8,128)(2,1)S(1)}, u32[]{:S(2)}, u32[]{:S(2)}) collective-permute-start(bf16[512,1024]{1,0:T(8,128)(2,1)S(1)} %get-tuple-element.66), channel_id=1, source_target_pairs={{0,8},{8,0},{1,9},{9,1},{2,10},{10,2},{3,11},{11,3},{4,12},{12,4},... | collective-permute-start | bytes 3145736 | tf_op jit(solution)/shard_map/ppermute | solution.py:401
  52.9 2.9 %collective-permute-start.17 = (bf16[512,1024]{1,0:T(8,128)(2,1)S(1)}, bf16[512,1024]{1,0:T(8,128)(2,1)S(1)}, u32[]{:S(2)}, u32[]{:S(2)}) collective-permute-start(bf16[512,1024]{1,0:T(8,128)(2,1)S(1)} %get-tuple-element.69), channel_id=1, source_target_pairs={{0,8},{8,0},{1,9},{9,1},{2,10},{10,2},{3,11},{11,3},{4,12},{12,4},... | collective-permute-start | bytes 3145736 | tf_op jit(solution)/shard_map/ppermute | solution.py:401

commit v9 on v8

--- a/solution.py
+++ b/solution.py
@@ -172,9 +172,10 @@
     wg_ref, wu_ref = refs.pop(0), refs.pop(0)
     wd_ref = refs.pop(0) if down else None
     other_ref = refs.pop(0) if pair else None
+    plane_ref = refs.pop(0) if pair else None
     refs = refs[unused:]
     act_ref, coef_ref = refs.pop(0), refs.pop(0)
-    shares = [refs.pop(0) for _ in range(EXPERTS if pair else down)]
+    share_ref = refs.pop(0) if down else None
     if fetch:
         sources, sems = (wg_ref, wu_ref), refs.pop()
         wg_ref, wu_ref = refs.pop(0), refs.pop(0)
@@ -222,27 +223,26 @@
         for k in range(EXPERTS):
             rows = slice(k * CAP, (k + 1) * CAP)
             block = jnp.concatenate([other[rows], acc_ref[rows, :]], axis=0).astype(BF16)
-            shares[k][...] = block
+            share_ref[plane_ref[0] ^ k] = block
     elif down:
-        shares[0][...] = acc_ref[...].astype(BF16)
-
-
-def forward(xs, wg, wu, wd=None, other=None, fetch=False, earlier=()):
+        share_ref[...] = acc_ref[...].astype(BF16)
+
+
+def forward(xs, wg, wu, wd=None, other=None, plane=None, fetch=False, earlier=()):
     n, (part, width), cols = len(xs), xs[0].shape, wg.shape[1]
     rows = n * part
     down, pair = wd is not None, other is not None
-    shares = [jax.ShapeDtypeStruct((part, width), BF16)] * down
-    if pair:
-        shares = [jax.ShapeDtypeStruct((2 * CAP, width), BF16)] * EXPERTS
+    shares = jax.ShapeDtypeStruct((EXPERTS, 2 * CAP, width) if pair else (part, width), BF16)
     weights = [kept(wg), kept(wu)] if fetch else [wg, wu]
     return pl.pallas_call(
         functools.partial(forward_kernel, n, fetch, down, pair, len(earlier)),
         out_shape=[jax.ShapeDtypeStruct((rows, cols), BF16)] * 2
-        + shares
+        + [shares] * down
         + [pltpu.VMEM(wg.shape, wg.dtype)] * (2 * fetch),
         in_specs=[HERE] * n
         + [AFAR if fetch else HERE] * 2
         + [HERE] * (down + pair)
+        + [pl.BlockSpec(memory_space=pltpu.SMEM)] * pair
         + [ANYWHERE] * len(earlier),
         scratch_shapes=[pltpu.VMEM((part, width), F32)] * down
         + [pltpu.VMEM((rows, width), BF16)] * (n > 1)
@@ -250,7 +250,7 @@
         compiler_params=LARGE,
         cost_estimate=CHEAP,
         name="forward" + "_fetch" * fetch + "_down" * down,
-    )(*xs, *weights, *([wd] * down), *([other] * pair), *earlier)
+    )(*xs, *weights, *([wd] * down), *([other, plane] if pair else []), *earlier)
 
 
 def turn_kernel(_, __, *refs):
@@ -361,22 +361,22 @@
     )(*[v for both in zip(owns, gots) for v in both], *held)
 
 
-def split_kernel(*refs):
-    blocks = [r[...].astype(F32) for r in refs[:EXPERTS]]
-    refs[-2][...] = jnp.concatenate([b[:CAP] for b in blocks], axis=0).astype(BF16)
-    refs[-1][...] = jnp.concatenate([b[CAP:] for b in blocks], axis=0).astype(BF16)
-
-
-def split(blocks, earlier):
-    width = blocks[0].shape[1]
+def split_kernel(plane_ref, blocks_ref, _, upper_ref, lower_ref):
+    blocks = [blocks_ref[plane_ref[0] ^ k].astype(F32) for k in range(EXPERTS)]
+    upper_ref[...] = jnp.concatenate([b[:CAP] for b in blocks], axis=0).astype(BF16)
+    lower_ref[...] = jnp.concatenate([b[CAP:] for b in blocks], axis=0).astype(BF16)
+
+
+def split(plane, blocks, earlier):
+    width = blocks.shape[2]
     return pl.pallas_call(
         split_kernel,
         out_shape=[jax.ShapeDtypeStruct((EXPERTS * CAP, width), BF16)] * 2,
-        in_specs=[HERE] * EXPERTS + [ANYWHERE] * len(earlier),
+        in_specs=[pl.BlockSpec(memory_space=pltpu.SMEM), HERE, ANYWHERE],
         compiler_params=SMALL,
         cost_estimate=CHEAP,
         name="split",
-    )(*blocks, *earlier)
+    )(plane, blocks, earlier)
 
 
 def unpack_kernel(placer_ref, mine_ref, got_ref, *refs):
@@ -430,10 +430,10 @@
 
     wg, wu = w_gate, w_up
     act0, coef0, share_own = forward([x_own], wg, wu, wd)
-    act1, coef1, *shares = forward([x_near, x_far], wg, wu, wd, other=share_own)
+    act1, coef1, shares = forward([x_near, x_far], wg, wu, wd, other=share_own, plane=scalars[0])
     x_pass, g_pass = relay([x_near, g_far], [mark(act1), g_near])
     x_corner, g_corner = swap(x_pass, "far"), swap(g_pass, "half")
-    returned = across_planes(shares)
+    returned = lax.all_to_all(shares, "arch", split_axis=0, concat_axis=0, tiled=True)
     act2, coef2 = forward([x_corner], wg, wu)
     xt = turn(*scalars[1:], [x_own, x_near, x_far, x_corner], share)
 
@@ -442,7 +442,7 @@
     cols = w_down.shape[0]
     half = cols // 2
     own0, sib0 = backward(xt, gs, acts, coefs, wdt, 0, half)
-    mine, theirs = split(returned, [own0])
+    mine, theirs = split(scalars[0], returned, own0)
     got = swap(theirs, "half")
     own1, sib1 = backward(xt, gs, acts, coefs, wdt, half, half, [mine])
     got0, got1 = swap(sib0, "core"), swap(sib1, "core")

time: 57 us -> 79.1 us (1.39)
  local copies, waits for them, and re-layouts: 0.01 us -> 18.8 us
  Pallas kernels: 26.6 us -> 32.5 us
  starting transfers between devices: 26.8 us -> 24.2 us
    unnamed x4 -> x54, local copies, waits for them, and re-layouts: 0.01 us -> 18.8 us
    ppermute x9 -> x6, starting transfers between devices: 17.5 us -> 13.1 us  [across_planes(): lax.ppermute(blocks[k], 'arch', [(i, i ^ k) for i in range(EXPERTS)])]
    all_to_all x0 -> x1, starting transfers between devices: none -> 3.48 us  [gathering(): lax.all_to_all(shares, 'arch', split_axis=0, concat_axis=0, tiled=True)]
    pallas_call x2, Pallas kernels: 7.56 us -> 10.5 us  [backward(): pl.pallas_call(functools.partial(backward_kernel, first, counts), out_sha...]
    ppermute x9, starting transfers between devices: 9.38 us -> 7.69 us  [swap(): return lax.ppermute(value, axis, [(0, 1), (1, 0)])]
    pallas_call x2, Pallas kernels: 2.21 us -> 3.43 us  [finish(): pl.pallas_call(functools.partial(finish_kernel, spans, more), out_shape=[...]
    pallas_call x1, Pallas kernels: 0.04 us -> 0.99 us  [relay(): pl.pallas_call(functools.partial(relay_kernel, n), out_shape=[jax.ShapeDt...]
    pallas_call x3, Pallas kernels: 11 us -> 11.8 us  [forward(): pl.pallas_call(functools.partial(forward_kernel, n, fetch, down, pair, le...]
  transfers between devices with their start and end apart: 18 -> 16, of which waited for: 4 -> 2; matrix products, arithmetic and copies ran while one was open for 0% -> 0% of each run, Pallas kernels for 42% -> 37%
where the time goes in v9:
time: 79.1 us; the launch traced here: 78.5 us
  Pallas kernels  32.5 us (41%)
  starting transfers between devices  24.2 us (31%)
  local copies, waits for them, and re-layouts  18.8 us (24%)
  waiting for transfers between devices  2.01 us (3%)
  between operations  0.88 us (1%)
    unnamed x54, local copies, waits for them, and re-layouts  18.8 us
    ppermute x6, starting transfers between devices, across_planes(): lax.ppermute(blocks[k], 'arch', [(i, i ^ k) for i in range(EXPERTS)])  13.1 us
    pallas_call x3, Pallas kernels, forward(): pl.pallas_call(functools.partial(forward_kernel, n, fetch, down, pair, le...  11.8 us
    pallas_call x2, Pallas kernels, backward(): pl.pallas_call(functools.partial(backward_kernel, first, counts), out_sha...  10.5 us
    ppermute x9, starting transfers between devices, swap(): return lax.ppermute(value, axis, [(0, 1), (1, 0)])  7.69 us
    all_to_all x1, starting transfers between devices, gathering(): lax.all_to_all(shares, 'arch', split_axis=0, concat_axis=0, tiled=True)  3.48 us
    pallas_call x2, Pallas kernels, finish(): pl.pallas_call(functools.partial(finish_kernel, spans, more), out_shape=[...  3.43 us
    pallas_call x1, Pallas kernels, flip(): pl.pallas_call(flip_kernel, out_shape=[pltpu.VMEM(value.shape, value.dtyp...  2.88 us
  transfers between devices with their start and end apart: 16, of which 2 were waited for; matrix products, arithmetic and copies ran while one was open for 0% of the time, Pallas kernels for 37%

profile of v9, /device:TPU:0, one launch (start us, length us, event | category | flops | bytes accessed | tf_op | source)
XLA Modules:
  0.0 78.5 jit_solution(9283673870271023054)
XLA Ops:
  0.6 1.5 %pack.1 = (bf16[144,128]{1,0:T(8,128)(2,1)S(1)}, bf16[36,1024]{1,0:T(8,128)(2,1)S(1)}, bf16[36,1024]{1,0:T(8,128)(2,1)S(1)}, bf16[36,1024]{1,0:T(8,128)(2,1)S(1)...) custom-call(s32[1]{0:T(128)} %bitcast.plane_ref.refs_6_, ...), custom_call_target="tpu_custom_call" | custom-call | tf_op jit(solution)/shard_map/pack/pallas_call | solution.py:78
  2.1 5.1 %collective-permute-start = (bf16[36,1024]{1,0:T(8,128)(2,1)S(1)}, bf16[36,1024]{1,0:T(8,128)(2,1)S(1)}, u32[]{:S(2)}, u32[]{:S(2)}) collective-permute-start(bf16[36,1024]{1,0:T(8,128)(2,1)S(1)} %get-tuple-element.36), channel_id=1, source_target_pairs={{0,6},{2,4},{4,2},{6,0},{1,7},{3,5},{5,3},{7,1},{8,14},{10,12},{12... | collective-permute-start | bytes 221192 | tf_op jit(solution)/shard_map/ppermute | solution.py:406
  7.9 3.7 %collective-permute-start.5 = (bf16[36,1024]{1,0:T(8,128)(2,1)S(1)}, bf16[36,1024]{1,0:T(8,128)(2,1)S(1)}, u32[]{:S(2)}, u32[]{:S(2)}) collective-permute-start(bf16[36,1024]{1,0:T(8,128)(2,1)S(1)} %get-tuple-element.45), channel_id=1, source_target_pairs={{0,6},{2,4},{4,2},{6,0},{1,7},{3,5},{5,3},{7,1},{8,14},{10,12},{12... | collective-permute-start | bytes 221192 | tf_op jit(solution)/shard_map/ppermute | solution.py:406
  11.6 3.6 %collective-permute-start.7 = (bf16[36,1024]{1,0:T(8,128)(2,1)S(1)}, bf16[36,1024]{1,0:T(8,128)(2,1)S(1)}, u32[]{:S(2)}, u32[]{:S(2)}) collective-permute-start(bf16[36,1024]{1,0:T(8,128)(2,1)S(1)} %get-tuple-element.47), channel_id=1, source_target_pairs={{0,2},{2,0},{4,6},{6,4},{1,3},{3,1},{5,7},{7,5},{8,10},{10,8},{12,... | collective-permute-start | bytes 221192 | tf_op jit(solution)/shard_map/ppermute | solution.py:406
  15.2 2.9 %flip.1 = (bf16[2048,1024]{1,0:T(8,128)(2,1)S(1)}, bf16[1024,2048]{1,0:T(8,128)(2,1)S(1)}) custom-call(bf16[2048,1024]{1,0:T(8,128)(2,1)} %source_ref), custom_call_target="tpu_custom_call" | custom-call | tf_op jit(solution)/shard_map/flip/pallas_call | solution.py:157
  18.5 1.7 %copy-done.4 = bf16[1024,2048]{1,0:T(8,128)(2,1)} copy-done((bf16[1024,2048]{1,0:T(8,128)(2,1)}, bf16[1024,2048]{1,0:T(8,128)(2,1)S(1)}, u32[]{:S(2)}) %copy-start.4) | copy-done | bytes 4194328
  20.2 1.1 %collective-permute-start.3 = (bf16[144,1024]{1,0:T(8,128)(2,1)S(1)}, bf16[144,1024]{1,0:T(8,128)(2,1)S(1)}, u32[]{:S(2)}, u32[]{:S(2)}) collective-permute-start(bf16[144,1024]{1,0:T(8,128)(2,1)S(1)} %join.2.refs_0_.refs_4_), channel_id=1, source_target_pairs={{0,1},{1,0},{2,3},{3,2},{4,5},{5,4},{6,7},{7,6},{8,9},{9,8},{10,11... | collective-permute-start | bytes 884744 | tf_op jit(solution)/shard_map/ppermute | solution.py:401
  21.3 1.5 %collective-permute-start.4 = (bf16[144,1024]{1,0:T(8,128)(2,1)S(1)}, bf16[144,1024]{1,0:T(8,128)(2,1)S(1)}, u32[]{:S(2)}, u32[]{:S(2)}) collective-permute-start(bf16[144,1024]{1,0:T(8,128)(2,1)S(1)} %join.2.refs_0_.refs_4_), channel_id=1, source_target_pairs={{0,16},{16,0},{1,17},{17,1},{2,18},{18,2},{3,19},{19,3},{4,20},{20... | collective-permute-start | bytes 884744 | tf_op jit(solution)/shard_map/ppermute | solution.py:401
  23.5 0.9 %collective-permute-start.9 = (bf16[144,1024]{1,0:T(8,128)(2,1)S(1)}, bf16[144,1024]{1,0:T(8,128)(2,1)S(1)}, u32[]{:S(2)}, u32[]{:S(2)}) collective-permute-start(bf16[144,1024]{1,0:T(8,128)(2,1)S(1)} %join.3.refs_0_), channel_id=1, source_target_pairs={{0,1},{1,0},{2,3},{3,2},{4,5},{5,4},{6,7},{7,6},{8,9},{9,8},{10,11... | collective-permute-start | bytes 884744 | tf_op jit(solution)/shard_map/ppermute | solution.py:401
  24.4 3.8 %forward_down.2 = (bf16[144,2048]{1,0:T(8,128)(2,1)S(1)}, bf16[144,2048]{1,0:T(8,128)(2,1)S(1)}, bf16[144,1024]{1,0:T(8,128)(2,1)S(1)}) custom-call(bf16[144,1024]{1,0:T(8,128)(2,1)S(1)} %join.2.refs_0_.refs_4_, bf16[1024,2048]{1,0:T(8,128)(2,1)S(1)} %copy-done, bf16[1024,2048]{1,0:T(8,128)(2,1)S(1)} %copy-done.2, ...), custom_call_target="tpu_custom_call" | custom-call | tf_op jit(solution)/shard_map/forward_down/pallas_call | solution.py:237
  29.9 5.8 %forward_down.3 = (bf16[288,2048]{1,0:T(8,128)(2,1)S(1)}, bf16[288,2048]{1,0:T(8,128)(2,1)S(1)}, bf16[4,72,1024]{2,1,0:T(8,128)(2,1)}) custom-call(bf16[144,1024]{1,0:T(8,128)(2,1)S(1)} %collective-permute-done.3.refs_0_.refs_1_.refs_5_, bf16[144,1024]{1,0:T(8,128)(2,1)S(1)} %collective-permute-done.4.refs_1_.refs_2_.refs_6_, ...), custom_call_target="tpu_custom_call" | custom-call | tf_op jit(solution)/shard_map/forward_down/pallas_call | solution.py:237
  35.7 1.0 %relay.1 = (bf16[144,1024]{1,0:T(8,128)(2,1)}, bf16[144,1024]{1,0:T(8,128)(2,1)}) custom-call(bf16[144,1024]{1,0:T(8,128)(2,1)S(1)} %collective-permute-done.3.refs_0_.refs_1_.refs_5_, bf16[144,1024]{1,0:T(8,128)(2,1)S(1)} %collective-permute-done.8.refs_1_.refs_2_, bf16[16,128]{1,0:T(8,128)(2,1)S(1)} %mark.1.refs_2_, ...), custom_call_target="tpu_custom_call" | custom-call | tf_op jit(solution)/shard_map/relay/pallas_call | solution.py:118
  37.1 1.3 %collective-permute-start.10 = (bf16[144,1024]{1,0:T(8,128)(2,1)}, bf16[144,1024]{1,0:T(8,128)(2,1)S(1)}, u32[]{:S(2)}, u32[]{:S(2)}) collective-permute-start(bf16[144,1024]{1,0:T(8,128)(2,1)} %get-tuple-element.50), channel_id=1, source_target_pairs={{0,16},{16,0},{1,17},{17,1},{2,18},{18,2},{3,19},{19,3},{4,20},{20... | collective-permute-start | bytes 884744 | tf_op jit(solution)/shard_map/ppermute | solution.py:401
  38.4 1.4 %collective-permute-start.11 = (bf16[144,1024]{1,0:T(8,128)(2,1)}, bf16[144,1024]{1,0:T(8,128)(2,1)}, u32[]{:S(2)}, u32[]{:S(2)}) collective-permute-start(bf16[144,1024]{1,0:T(8,128)(2,1)} %get-tuple-element.51), channel_id=1, source_target_pairs={{0,1},{1,0},{2,3},{3,2},{4,5},{5,4},{6,7},{7,6},{8,9},{9,8},{10,11... | collective-permute-start | bytes 884744 | tf_op jit(solution)/shard_map/ppermute | solution.py:401
  39.8 3.5 %all-to-all-start = ((bf16[4,72,1024]{2,1,0:T(8,128)(2,1)}), bf16[4,72,1024]{2,1,0:T(8,128)(2,1)S(1)}, u32[]{:S(2)}, u32[]{:S(2)}) async-start(bf16[4,72,1024]{2,1,0:T(8,128)(2,1)} %get-tuple-element.44), calls=%async_computation | async-start | bytes 1179648 | tf_op jit(solution)/shard_map/all_to_all | solution.py:436
  43.3 1.7 %collective-permute-done.10.refs_3_.refs_7_.refs_0_ = bf16[144,1024]{1,0:T(8,128)(2,1)S(1)} collective-permute-done((bf16[144,1024]{1,0:T(8,128)(2,1)}, bf16[144,1024]{1,0:T(8,128)(2,1)S(1)}, u32[]{:S(2)}, u32[]{:S(2)}) %collective-permute-start.10) | collective-permute-done | bytes 294944 | tf_op jit(solution)/shard_map/ppermute | solution.py:401
  45.2 2.2 %copy-done.1 = bf16[1024,2048]{1,0:T(8,128)(2,1)S(1)} copy-done((bf16[1024,2048]{1,0:T(8,128)(2,1)S(1)}, bf16[1024,2048]{1,0:T(8,128)(2,1)}, u32[]{:S(2)}) %copy-start.1) | copy-done | bytes 4194328
  47.4 2.2 %copy-done.3 = bf16[1024,2048]{1,0:T(8,128)(2,1)S(1)} copy-done((bf16[1024,2048]{1,0:T(8,128)(2,1)S(1)}, bf16[1024,2048]{1,0:T(8,128)(2,1)}, u32[]{:S(2)}) %copy-start.3) | copy-done | bytes 4194328
  49.6 2.2 %forward.1 = (bf16[144,2048]{1,0:T(8,128)(2,1)S(1)}, bf16[144,2048]{1,0:T(8,128)(2,1)S(1)}) custom-call(bf16[144,1024]{1,0:T(8,128)(2,1)S(1)} %collective-permute-done.10.refs_3_.refs_7_.refs_0_, bf16[1024,2048]{1,0:T(8,128)(2,1)S(1)} %copy-done.1, bf16[1024,2048]{1,0:T(8,128)(2,1)S(1)} %copy-done.3), custom_call_target="tpu_custom_call" | custom-call | tf_op jit(solution)/shard_map/forward/pallas_call | solution.py:237
  52.7 5.7 %backward.2 = (bf16[512,1024]{1,0:T(8,128)(2,1)S(1)}, bf16[512,1024]{1,0:T(8,128)(2,1)}) custom-call(bf16[512,576]{1,0:T(8,128)(2,1)S(1)} %turn.1.xt_ref, bf16[144,1024]{1,0:T(8,128)(2,1)S(1)} %join.3.refs_0_, bf16[144,1024]{1,0:T(8,128)(2,1)S(1)} %copy-done.10, bf16[144,1024]{1,0:T(8,128)(2,1)S(1)} %collective-permute-done.8.refs_1_.refs_2_, ...), custom_call_target="tpu_custom_call" | custom-call | flops 20000000000 | tf_op jit(solution)/shard_map/backward/pallas_call | solution.py:315
  59.1 2.2 %copy-done.6 = bf16[1024,2048]{1,0:T(8,128)(2,1)S(1)} copy-done((bf16[1024,2048]{1,0:T(8,128)(2,1)S(1)}, bf16[1024,2048]{1,0:T(8,128)(2,1)}, u32[]{:S(2)}) %copy-start.6) | copy-done | bytes 4194328
  61.3 1.1 %copy-done.8 = bf16[512,576]{1,0:T(8,128)(2,1)S(1)} copy-done((bf16[512,576]{1,0:T(8,128)(2,1)S(1)}, bf16[512,576]{1,0:T(8,128)(2,1)}, u32[]{:S(2)}) %copy-start.8) | copy-done | bytes 589848
  62.4 1.0 %copy-done.11 = bf16[144,1024]{1,0:T(8,128)(2,1)S(1)} copy-done((bf16[144,1024]{1,0:T(8,128)(2,1)S(1)}, bf16[144,1024]{1,0:T(8,128)(2,1)}, u32[]{:S(2)}) %copy-start.11) | copy-done | bytes 294936
  63.4 1.3 %copy-done.14 = bf16[288,2048]{1,0:T(8,128)(2,1)S(1)} copy-done((bf16[288,2048]{1,0:T(8,128)(2,1)S(1)}, bf16[288,2048]{1,0:T(8,128)(2,1)}, u32[]{:S(2)}) %copy-start.14) | copy-done | bytes 1179672
  64.7 1.1 %copy-done.17 = bf16[144,2048]{1,0:T(8,128)(2,1)S(1)} copy-done((bf16[144,2048]{1,0:T(8,128)(2,1)S(1)}, bf16[144,2048]{1,0:T(8,128)(2,1)}, u32[]{:S(2)}) %copy-start.17) | copy-done | bytes 589848
  65.7 1.1 %copy-done.20 = bf16[144,2048]{1,0:T(8,128)(2,1)S(1)} copy-done((bf16[144,2048]{1,0:T(8,128)(2,1)S(1)}, bf16[144,2048]{1,0:T(8,128)(2,1)}, u32[]{:S(2)}) %copy-start.20) | copy-done | bytes 589848
  66.8 1.1 %copy-done.22 = bf16[144,2048]{1,0:T(8,128)(2,1)S(1)} copy-done((bf16[144,2048]{1,0:T(8,128)(2,1)S(1)}, bf16[144,2048]{1,0:T(8,128)(2,1)}, u32[]{:S(2)}) %copy-start.22) | copy-done | bytes 589848
  67.8 1.1 %copy-done.24 = bf16[144,2048]{1,0:T(8,128)(2,1)S(1)} copy-done((bf16[144,2048]{1,0:T(8,128)(2,1)S(1)}, bf16[144,2048]{1,0:T(8,128)(2,1)}, u32[]{:S(2)}) %copy-start.24) | copy-done | bytes 589848
  68.9 4.7 %backward.3 = (bf16[512,1024]{1,0:T(8,128)(2,1)S(1)}, bf16[512,1024]{1,0:T(8,128)(2,1)S(1)}) custom-call(bf16[512,576]{1,0:T(8,128)(2,1)S(1)} %copy-done.8, bf16[144,1024]{1,0:T(8,128)(2,1)S(1)} %join.3.refs_0_, bf16[144,1024]{1,0:T(8,128)(2,1)S(1)} %copy-done.11, bf16[144,1024]{1,0:T(8,128)(2,1)S(1)} %collective-permute-done.8.refs_1_.refs_2_, ...), custom_call_target="tpu_custom_call" | custom-call | flops 20000000000 | tf_op jit(solution)/shard_map/backward/pallas_call | solution.py:315
  73.9 2.3 %finish.2 = (bf16[256,2048]{1,0:T(8,128)(2,1)}, bf16[256,2048]{1,0:T(8,128)(2,1)}) custom-call(bf16[512,1024]{1,0:T(8,128)(2,1)S(1)} %get-tuple-element.57._.refs_0_, bf16[512,1024]{1,0:T(8,128)(2,1)} %collective-permute-done.13.refs_1_), custom_call_target="tpu_custom_call" | custom-call | tf_op jit(solution)/shard_map/finish/pallas_call | solution.py:351
  76.3 1.0 %unpack.1 = bf16[128,1024]{1,0:T(8,128)(2,1)} custom-call(bf16[144,128]{1,0:T(8,128)(2,1)S(1)} %copy-done.26, bf16[144,1024]{1,0:T(8,128)(2,1)S(1)} %get-tuple-element.58.mine_ref.refs_11_, bf16[144,1024]{1,0:T(8,128)(2,1)S(1)} %collective-permute-done.12.got_ref, bf16[256,2048]{1,0:T(8,128)(2,1)} %get-tuple-element.61.refs_0_.refs_2_), custom_call_target="tpu_custom_call" | custom-call | flops 20000000000 | tf_op jit(solution)/shard_map/unpack/pallas_call | solution.py:390
  77.4 1.1 %finish.3 = (bf16[256,2048]{1,0:T(8,128)(2,1)}, bf16[256,2048]{1,0:T(8,128)(2,1)}) custom-call(bf16[512,1024]{1,0:T(8,128)(2,1)S(1)} %get-tuple-element.62.refs_0_, bf16[512,1024]{1,0:T(8,128)(2,1)S(1)} %collective-permute-done.14.refs_1_, bf16[256,2048]{1,0:T(8,128)(2,1)} %get-tuple-element.61.refs_0_.refs_2_, ...), custom_call_target="tpu_custom_call", output_to_operand_aliasing={{0}: (2, {}), {1}: (3, {})} | custom-call | tf_op jit(solution)/shard_map/finish/pallas_call | solution.py:351
  (70 shorter events, 5.9 us)
Async XLA Ops:
  2.1 16.3 %copy-start.25 = (bf16[144,128]{1,0:T(8,128)(2,1)}, bf16[144,128]{1,0:T(8,128)(2,1)S(1)}, u32[]{:S(2)}) copy-start(bf16[144,128]{1,0:T(8,128)(2,1)S(1)} %get-tuple-element.35.placer_ref) | copy-start | bytes 110596
  2.1 9.5 %collective-permute-start = (bf16[36,1024]{1,0:T(8,128)(2,1)S(1)}, bf16[36,1024]{1,0:T(8,128)(2,1)S(1)}, u32[]{:S(2)}, u32[]{:S(2)}) collective-permute-start(bf16[36,1024]{1,0:T(8,128)(2,1)S(1)} %get-tuple-element.36), channel_id=1, source_target_pairs={{0,6},{2,4},{4,2},{6,0},{1,7},{3,5},{5,3},{7,1},{8,14},{10,12},{12... | collective-permute-start | bytes 221192 | tf_op jit(solution)/shard_map/ppermute | solution.py:406
  7.2 11.2 %collective-permute-start.1 = (bf16[36,1024]{1,0:T(8,128)(2,1)S(1)}, bf16[36,1024]{1,0:T(8,128)(2,1)S(1)}, u32[]{:S(2)}, u32[]{:S(2)}) collective-permute-start(bf16[36,1024]{1,0:T(8,128)(2,1)S(1)} %get-tuple-element.37), channel_id=1, source_target_pairs={{0,4},{2,6},{4,0},{6,2},{1,5},{3,7},{5,1},{7,3},{8,12},{10,14},{12... | collective-permute-start | bytes 221192 | tf_op jit(solution)/shard_map/ppermute | solution.py:406
  7.2 11.2 %collective-permute-start.2 = (bf16[36,1024]{1,0:T(8,128)(2,1)S(1)}, bf16[36,1024]{1,0:T(8,128)(2,1)S(1)}, u32[]{:S(2)}, u32[]{:S(2)}) collective-permute-start(bf16[36,1024]{1,0:T(8,128)(2,1)S(1)} %get-tuple-element.38), channel_id=1, source_target_pairs={{0,2},{2,0},{4,6},{6,4},{1,3},{3,1},{5,7},{7,5},{8,10},{10,8},{12,... | collective-permute-start | bytes 221192 | tf_op jit(solution)/shard_map/ppermute | solution.py:406
  7.9 15.0 %collective-permute-start.5 = (bf16[36,1024]{1,0:T(8,128)(2,1)S(1)}, bf16[36,1024]{1,0:T(8,128)(2,1)S(1)}, u32[]{:S(2)}, u32[]{:S(2)}) collective-permute-start(bf16[36,1024]{1,0:T(8,128)(2,1)S(1)} %get-tuple-element.45), channel_id=1, source_target_pairs={{0,6},{2,4},{4,2},{6,0},{1,7},{3,5},{5,3},{7,1},{8,14},{10,12},{12... | collective-permute-start | bytes 221192 | tf_op jit(solution)/shard_map/ppermute | solution.py:406
  11.6 11.2 %collective-permute-start.6 = (bf16[36,1024]{1,0:T(8,128)(2,1)S(1)}, bf16[36,1024]{1,0:T(8,128)(2,1)S(1)}, u32[]{:S(2)}, u32[]{:S(2)}) collective-permute-start(bf16[36,1024]{1,0:T(8,128)(2,1)S(1)} %get-tuple-element.46), channel_id=1, source_target_pairs={{0,4},{2,6},{4,0},{6,2},{1,5},{3,7},{5,1},{7,3},{8,12},{10,14},{12... | collective-permute-start | bytes 221192 | tf_op jit(solution)/shard_map/ppermute | solution.py:406
  11.6 11.2 %collective-permute-start.7 = (bf16[36,1024]{1,0:T(8,128)(2,1)S(1)}, bf16[36,1024]{1,0:T(8,128)(2,1)S(1)}, u32[]{:S(2)}, u32[]{:S(2)}) collective-permute-start(bf16[36,1024]{1,0:T(8,128)(2,1)S(1)} %get-tuple-element.47), channel_id=1, source_target_pairs={{0,2},{2,0},{4,6},{6,4},{1,3},{3,1},{5,7},{7,5},{8,10},{10,8},{12,... | collective-permute-start | bytes 221192 | tf_op jit(solution)/shard_map/ppermute | solution.py:406
  15.2 9.2 %copy-start = (bf16[1024,2048]{1,0:T(8,128)(2,1)S(1)}, bf16[1024,2048]{1,0:T(8,128)(2,1)}, u32[]{:S(2)}) copy-start(bf16[1024,2048]{1,0:T(8,128)(2,1)} %refs_1_.3) | copy-start | bytes 12582916
  15.2 9.2 %copy-start.2 = (bf16[1024,2048]{1,0:T(8,128)(2,1)S(1)}, bf16[1024,2048]{1,0:T(8,128)(2,1)}, u32[]{:S(2)}) copy-start(bf16[1024,2048]{1,0:T(8,128)(2,1)} %refs_2_.5) | copy-start | bytes 12582916
  18.1 2.1 %copy-start.4 = (bf16[1024,2048]{1,0:T(8,128)(2,1)}, bf16[1024,2048]{1,0:T(8,128)(2,1)S(1)}, u32[]{:S(2)}) copy-start(bf16[1024,2048]{1,0:T(8,128)(2,1)S(1)} %get-tuple-element.41.refs_4_.refs_10_) | copy-start | bytes 12582916
  20.2 9.7 %collective-permute-start.3 = (bf16[144,1024]{1,0:T(8,128)(2,1)S(1)}, bf16[144,1024]{1,0:T(8,128)(2,1)S(1)}, u32[]{:S(2)}, u32[]{:S(2)}) collective-permute-start(bf16[144,1024]{1,0:T(8,128)(2,1)S(1)} %join.2.refs_0_.refs_4_), channel_id=1, source_target_pairs={{0,1},{1,0},{2,3},{3,2},{4,5},{5,4},{6,7},{7,6},{8,9},{9,8},{10,11... | collective-permute-start | bytes 884744 | tf_op jit(solution)/shard_map/ppermute | solution.py:401
  21.3 8.5 %collective-permute-start.4 = (bf16[144,1024]{1,0:T(8,128)(2,1)S(1)}, bf16[144,1024]{1,0:T(8,128)(2,1)S(1)}, u32[]{:S(2)}, u32[]{:S(2)}) collective-permute-start(bf16[144,1024]{1,0:T(8,128)(2,1)S(1)} %join.2.refs_0_.refs_4_), channel_id=1, source_target_pairs={{0,16},{16,0},{1,17},{17,1},{2,18},{18,2},{3,19},{19,3},{4,20},{20... | collective-permute-start | bytes 884744 | tf_op jit(solution)/shard_map/ppermute | solution.py:401
  22.9 12.8 %collective-permute-start.8 = (bf16[144,1024]{1,0:T(8,128)(2,1)S(1)}, bf16[144,1024]{1,0:T(8,128)(2,1)S(1)}, u32[]{:S(2)}, u32[]{:S(2)}) collective-permute-start(bf16[144,1024]{1,0:T(8,128)(2,1)S(1)} %join.3.refs_0_), channel_id=1, source_target_pairs={{0,16},{16,0},{1,17},{17,1},{2,18},{18,2},{3,19},{19,3},{4,20},{20... | collective-permute-start | bytes 884744 | tf_op jit(solution)/shard_map/ppermute | solution.py:401
  23.5 12.2 %collective-permute-start.9 = (bf16[144,1024]{1,0:T(8,128)(2,1)S(1)}, bf16[144,1024]{1,0:T(8,128)(2,1)S(1)}, u32[]{:S(2)}, u32[]{:S(2)}) collective-permute-start(bf16[144,1024]{1,0:T(8,128)(2,1)S(1)} %join.3.refs_0_), channel_id=1, source_target_pairs={{0,1},{1,0},{2,3},{3,2},{4,5},{5,4},{6,7},{7,6},{8,9},{9,8},{10,11... | collective-permute-start | bytes 884744 | tf_op jit(solution)/shard_map/ppermute | solution.py:401
  37.1 7.9 %collective-permute-start.10 = (bf16[144,1024]{1,0:T(8,128)(2,1)}, bf16[144,1024]{1,0:T(8,128)(2,1)S(1)}, u32[]{:S(2)}, u32[]{:S(2)}) collective-permute-start(bf16[144,1024]{1,0:T(8,128)(2,1)} %get-tuple-element.50), channel_id=1, source_target_pairs={{0,16},{16,0},{1,17},{17,1},{2,18},{18,2},{3,19},{19,3},{4,20},{20... | collective-permute-start | bytes 884744 | tf_op jit(solution)/shard_map/ppermute | solution.py:401
  38.4 13.4 %collective-permute-start.11 = (bf16[144,1024]{1,0:T(8,128)(2,1)}, bf16[144,1024]{1,0:T(8,128)(2,1)}, u32[]{:S(2)}, u32[]{:S(2)}) collective-permute-start(bf16[144,1024]{1,0:T(8,128)(2,1)} %get-tuple-element.51), channel_id=1, source_target_pairs={{0,1},{1,0},{2,3},{3,2},{4,5},{5,4},{6,7},{7,6},{8,9},{9,8},{10,11... | collective-permute-start | bytes 884744 | tf_op jit(solution)/shard_map/ppermute | solution.py:401
  39.8 18.7 %all-to-all-start = ((bf16[4,72,1024]{2,1,0:T(8,128)(2,1)}), bf16[4,72,1024]{2,1,0:T(8,128)(2,1)S(1)}, u32[]{:S(2)}, u32[]{:S(2)}) async-start(bf16[4,72,1024]{2,1,0:T(8,128)(2,1)} %get-tuple-element.44), calls=%async_computation | async-start | bytes 1179648 | tf_op jit(solution)/shard_map/all_to_all | solution.py:436
  45.2 2.2 %copy-start.1 = (bf16[1024,2048]{1,0:T(8,128)(2,1)S(1)}, bf16[1024,2048]{1,0:T(8,128)(2,1)}, u32[]{:S(2)}) copy-start(bf16[1024,2048]{1,0:T(8,128)(2,1)} %refs_1_.3) | copy-start | bytes 12582916
  47.4 2.2 %copy-start.3 = (bf16[1024,2048]{1,0:T(8,128)(2,1)S(1)}, bf16[1024,2048]{1,0:T(8,128)(2,1)}, u32[]{:S(2)}) copy-start(bf16[1024,2048]{1,0:T(8,128)(2,1)} %refs_2_.5) | copy-start | bytes 12582916
  49.6 2.3 %copy-start.7 = (bf16[512,576]{1,0:T(8,128)(2,1)}, bf16[512,576]{1,0:T(8,128)(2,1)S(1)}, u32[]{:S(2)}) copy-start(bf16[512,576]{1,0:T(8,128)(2,1)S(1)} %turn.1.xt_ref) | copy-start | bytes 1769476
  49.6 2.4 %copy-start.5 = (bf16[1024,2048]{1,0:T(8,128)(2,1)S(1)}, bf16[1024,2048]{1,0:T(8,128)(2,1)}, u32[]{:S(2)}) copy-start(bf16[1024,2048]{1,0:T(8,128)(2,1)} %copy-done.4) | copy-start | bytes 12582916
  49.6 2.5 %copy-start.10 = (bf16[144,1024]{1,0:T(8,128)(2,1)S(1)}, bf16[144,1024]{1,0:T(8,128)(2,1)}, u32[]{:S(2)}) copy-start(bf16[144,1024]{1,0:T(8,128)(2,1)} %copy-done.9) | copy-start | bytes 884740
  49.6 2.9 %copy-start.13 = (bf16[288,2048]{1,0:T(8,128)(2,1)S(1)}, bf16[288,2048]{1,0:T(8,128)(2,1)}, u32[]{:S(2)}) copy-start(bf16[288,2048]{1,0:T(8,128)(2,1)} %copy-done.12) | copy-start | bytes 3538948
  49.6 3.0 %copy-start.16 = (bf16[144,2048]{1,0:T(8,128)(2,1)S(1)}, bf16[144,2048]{1,0:T(8,128)(2,1)}, u32[]{:S(2)}) copy-start(bf16[144,2048]{1,0:T(8,128)(2,1)} %copy-done.15) | copy-start | bytes 1769476
  49.6 3.1 %copy-start.19 = (bf16[144,2048]{1,0:T(8,128)(2,1)S(1)}, bf16[144,2048]{1,0:T(8,128)(2,1)}, u32[]{:S(2)}) copy-start(bf16[144,2048]{1,0:T(8,128)(2,1)} %copy-done.18) | copy-start | bytes 1769476
  51.8 6.6 %copy-start.21 = (bf16[144,2048]{1,0:T(8,128)(2,1)}, bf16[144,2048]{1,0:T(8,128)(2,1)S(1)}, u32[]{:S(2)}) copy-start(bf16[144,2048]{1,0:T(8,128)(2,1)S(1)} %get-tuple-element.53.refs_6_) | copy-start | bytes 1769476
  51.8 6.6 %copy-start.23 = (bf16[144,2048]{1,0:T(8,128)(2,1)}, bf16[144,2048]{1,0:T(8,128)(2,1)S(1)}, u32[]{:S(2)}) copy-start(bf16[144,2048]{1,0:T(8,128)(2,1)S(1)} %get-tuple-element.56.refs_9_) | copy-start | bytes 1769476
  58.5 15.5 %collective-permute-start.13 = (bf16[512,1024]{1,0:T(8,128)(2,1)}, bf16[512,1024]{1,0:T(8,128)(2,1)}, u32[]{:S(2)}, u32[]{:S(2)}) collective-permute-start(bf16[512,1024]{1,0:T(8,128)(2,1)} %get-tuple-element.60), channel_id=1, source_target_pairs={{0,8},{8,0},{1,9},{9,1},{2,10},{10,2},{3,11},{11,3},{4,12},{12,4},... | collective-permute-start | bytes 3145736 | tf_op jit(solution)/shard_map/ppermute | solution.py:401
  58.6 17.7 %collective-permute-start.12 = (bf16[144,1024]{1,0:T(8,128)(2,1)S(1)}, bf16[144,1024]{1,0:T(8,128)(2,1)S(1)}, u32[]{:S(2)}, u32[]{:S(2)}) collective-permute-start(bf16[144,1024]{1,0:T(8,128)(2,1)S(1)} %get-tuple-element.59), channel_id=1, source_target_pairs={{0,1},{1,0},{2,3},{3,2},{4,5},{5,4},{6,7},{7,6},{8,9},{9,8},{10,11... | collective-permute-start | bytes 884744 | tf_op jit(solution)/shard_map/ppermute | solution.py:401
  59.1 2.2 %copy-start.6 = (bf16[1024,2048]{1,0:T(8,128)(2,1)S(1)}, bf16[1024,2048]{1,0:T(8,128)(2,1)}, u32[]{:S(2)}) copy-start(bf16[1024,2048]{1,0:T(8,128)(2,1)} %copy-done.4) | copy-start | bytes 12582916
  68.9 7.4 %copy-start.26 = (bf16[144,128]{1,0:T(8,128)(2,1)S(1)}, bf16[144,128]{1,0:T(8,128)(2,1)}, u32[]{:S(2)}) copy-start(bf16[144,128]{1,0:T(8,128)(2,1)} %copy-done.25) | copy-start | bytes 110596
  73.7 3.7 %collective-permute-start.14 = (bf16[512,1024]{1,0:T(8,128)(2,1)S(1)}, bf16[512,1024]{1,0:T(8,128)(2,1)S(1)}, u32[]{:S(2)}, u32[]{:S(2)}) collective-permute-start(bf16[512,1024]{1,0:T(8,128)(2,1)S(1)} %get-tuple-element.63), channel_id=1, source_target_pairs={{0,8},{8,0},{1,9},{9,1},{2,10},{10,2},{3,11},{11,3},{4,12},{12,4},... | collective-permute-start | bytes 3145736 | tf_op jit(solution)/shard_map/ppermute | solution.py:401
  (11 other events, 11.7 us)

commit v10 on v8

--- a/solution.py
+++ b/solution.py
@@ -10,7 +10,7 @@
 
 EXPERTS = 4
 CAP = 36
-STRIP = 256
+STRIP = 512
 PAIR = 2 * STRIP
 MIB = 1024 * 1024
 LARGE = pltpu.CompilerParams(vmem_limit_bytes=16 * MIB)
@@ -425,11 +425,11 @@
     x_own = join(moved, [wdt])
     x_near, x_far = swap(x_own, "half"), swap(x_own, "far")
     moved = across_planes(blocks[EXPERTS:])
-    g_own = join(moved, [x_own])
-    g_near, g_far = swap(g_own, "half"), swap(g_own, "far")
 
     wg, wu = w_gate, w_up
     act0, coef0, share_own = forward([x_own], wg, wu, wd)
+    g_own = join(moved, [act0])
+    g_near, g_far = swap(g_own, "half"), swap(g_own, "far")
     act1, coef1, *shares = forward([x_near, x_far], wg, wu, wd, other=share_own)
     x_pass, g_pass = relay([x_near, g_far], [mark(act1), g_near])
     x_corner, g_corner = swap(x_pass, "far"), swap(g_pass, "half")

time: 57 us -> 56 us (0.982)
  waiting for transfers between devices: 2.6 us -> 7.84 us
  Pallas kernels: 26.6 us -> 23 us
  starting transfers between devices: 26.8 us -> 24.2 us
    ppermute x9, waiting for transfers between devices: 2.26 us -> 6.43 us  [swap(): return lax.ppermute(value, axis, [(0, 1), (1, 0)])]
    ppermute x9, starting transfers between devices: 9.38 us -> 6.72 us  [swap(): return lax.ppermute(value, axis, [(0, 1), (1, 0)])]
    pallas_call x3, Pallas kernels: 11 us -> 8.7 us  [forward(): pl.pallas_call(functools.partial(forward_kernel, n, fetch, down, pair, le...]
    pallas_call x2, Pallas kernels: 7.56 us -> 6.35 us  [backward(): pl.pallas_call(functools.partial(backward_kernel, first, counts), out_sha...]
    ppermute x9, waiting for transfers between devices: 0.34 us -> 1.4 us  [across_planes(): lax.ppermute(blocks[k], 'arch', [(i, i ^ k) for i in range(EXPERTS)])]
  transfers between devices with their start and end apart: 18 -> 18, of which waited for: 4 -> 6; matrix products, arithmetic and copies ran while one was open for 0% -> 0% of each run, Pallas kernels for 42% -> 36%
where the time goes in v10:
time: 56 us; the launch traced here: 55.9 us
  starting transfers between devices  24.2 us (43%)
  Pallas kernels  23 us (41%)
  waiting for transfers between devices  7.84 us (14%)
  between operations  0.82 us (1%)
    ppermute x9, starting transfers between devices, across_planes(): lax.ppermute(blocks[k], 'arch', [(i, i ^ k) for i in range(EXPERTS)])  17.5 us
    pallas_call x3, Pallas kernels, forward(): pl.pallas_call(functools.partial(forward_kernel, n, fetch, down, pair, le...  8.7 us
    ppermute x9, starting transfers between devices, swap(): return lax.ppermute(value, axis, [(0, 1), (1, 0)])  6.72 us
    ppermute x9, waiting for transfers between devices, swap(): return lax.ppermute(value, axis, [(0, 1), (1, 0)])  6.43 us
    pallas_call x2, Pallas kernels, backward(): pl.pallas_call(functools.partial(backward_kernel, first, counts), out_sha...  6.35 us
    pallas_call x1, Pallas kernels, flip(): pl.pallas_call(flip_kernel, out_shape=[pltpu.VMEM(value.shape, value.dtyp...  2.81 us
    pallas_call x2, Pallas kernels, finish(): pl.pallas_call(functools.partial(finish_kernel, spans, more), out_shape=[...  2.21 us
    pallas_call x1, Pallas kernels, pack(): pl.pallas_call(pack_kernel, out_shape=[jax.ShapeDtypeStruct((EXPERTS * CA...  1.46 us
  transfers between devices with their start and end apart: 18, of which 6 were waited for; matrix products, arithmetic and copies ran while one was open for 0% of the time, Pallas kernels for 36%

profile of v10, /device:TPU:0, one launch (start us, length us, event | category | flops | bytes accessed | tf_op | source)
XLA Modules:
  0.0 55.9 jit_solution(9038228018826856999)
XLA Ops:
  0.6 1.5 %pack.1 = (bf16[144,128]{1,0:T(8,128)(2,1)S(1)}, bf16[36,1024]{1,0:T(8,128)(2,1)S(1)}, bf16[36,1024]{1,0:T(8,128)(2,1)S(1)}, bf16[36,1024]{1,0:T(8,128)(2,1)S(1)...) custom-call(s32[1]{0:T(128)} %bitcast.plane_ref, ...), custom_call_target="tpu_custom_call" | custom-call | tf_op jit(solution)/shard_map/pack/pallas_call | solution.py:78
  2.1 5.1 %collective-permute-start = (bf16[36,1024]{1,0:T(8,128)(2,1)S(1)}, bf16[36,1024]{1,0:T(8,128)(2,1)S(1)}, u32[]{:S(2)}, u32[]{:S(2)}) collective-permute-start(bf16[36,1024]{1,0:T(8,128)(2,1)S(1)} %get-tuple-element.39), channel_id=1, source_target_pairs={{0,6},{2,4},{4,2},{6,0},{1,7},{3,5},{5,3},{7,1},{8,14},{10,12},{12... | collective-permute-start | bytes 221192 | tf_op jit(solution)/shard_map/ppermute | solution.py:406
  7.2 0.6 %collective-permute-start.2 = (bf16[36,1024]{1,0:T(8,128)(2,1)S(1)}, bf16[36,1024]{1,0:T(8,128)(2,1)S(1)}, u32[]{:S(2)}, u32[]{:S(2)}) collective-permute-start(bf16[36,1024]{1,0:T(8,128)(2,1)S(1)} %get-tuple-element.41), channel_id=1, source_target_pairs={{0,2},{2,0},{4,6},{6,4},{1,3},{3,1},{5,7},{7,5},{8,10},{10,8},{12,... | collective-permute-start | bytes 221192 | tf_op jit(solution)/shard_map/ppermute | solution.py:406
  7.9 3.7 %collective-permute-start.8 = (bf16[36,1024]{1,0:T(8,128)(2,1)S(1)}, bf16[36,1024]{1,0:T(8,128)(2,1)S(1)}, u32[]{:S(2)}, u32[]{:S(2)}) collective-permute-start(bf16[36,1024]{1,0:T(8,128)(2,1)S(1)} %get-tuple-element.51), channel_id=1, source_target_pairs={{0,6},{2,4},{4,2},{6,0},{1,7},{3,5},{5,3},{7,1},{8,14},{10,12},{12... | collective-permute-start | bytes 221192 | tf_op jit(solution)/shard_map/ppermute | solution.py:406
  11.6 0.0 collective-permute-done.refs_0_
  11.6 3.6 %collective-permute-start.10 = (bf16[36,1024]{1,0:T(8,128)(2,1)S(1)}, bf16[36,1024]{1,0:T(8,128)(2,1)S(1)}, u32[]{:S(2)}, u32[]{:S(2)}) collective-permute-start(bf16[36,1024]{1,0:T(8,128)(2,1)S(1)} %get-tuple-element.53), channel_id=1, source_target_pairs={{0,2},{2,0},{4,6},{6,4},{1,3},{3,1},{5,7},{7,5},{8,10},{10,8},{12,... | collective-permute-start | bytes 221192 | tf_op jit(solution)/shard_map/ppermute | solution.py:406
  15.2 2.8 %flip.1 = (bf16[2048,1024]{1,0:T(8,128)(2,1)S(1)}, bf16[1024,2048]{1,0:T(8,128)(2,1)S(1)}) custom-call(bf16[2048,1024]{1,0:T(8,128)(2,1)} %source_ref), custom_call_target="tpu_custom_call" | custom-call | tf_op jit(solution)/shard_map/flip/pallas_call | solution.py:157
  18.0 0.4 collective-permute-done.1.refs_1_
  18.5 1.4 %collective-permute-start.3 = (bf16[144,1024]{1,0:T(8,128)(2,1)S(1)}, bf16[144,1024]{1,0:T(8,128)(2,1)S(1)}, u32[]{:S(2)}, u32[]{:S(2)}) collective-permute-start(bf16[144,1024]{1,0:T(8,128)(2,1)S(1)} %join.2.refs_0_.refs_4_), channel_id=1, source_target_pairs={{0,1},{1,0},{2,3},{3,2},{4,5},{5,4},{6,7},{7,6},{8,9},{9,8},{10,11... | collective-permute-start | bytes 884744 | tf_op jit(solution)/shard_map/ppermute | solution.py:401
  19.9 1.5 %collective-permute-start.4 = (bf16[144,1024]{1,0:T(8,128)(2,1)S(1)}, bf16[144,1024]{1,0:T(8,128)(2,1)S(1)}, u32[]{:S(2)}, u32[]{:S(2)}) collective-permute-start(bf16[144,1024]{1,0:T(8,128)(2,1)S(1)} %join.2.refs_0_.refs_4_), channel_id=1, source_target_pairs={{0,16},{16,0},{1,17},{17,1},{2,18},{18,2},{3,19},{19,3},{4,20},{20... | collective-permute-start | bytes 884744 | tf_op jit(solution)/shard_map/ppermute | solution.py:401
  21.4 2.8 %forward_down.2 = (bf16[144,2048]{1,0:T(8,128)(2,1)S(1)}, bf16[144,2048]{1,0:T(8,128)(2,1)S(1)}, bf16[144,1024]{1,0:T(8,128)(2,1)S(1)}) custom-call(bf16[144,1024]{1,0:T(8,128)(2,1)S(1)} %join.2.refs_0_.refs_4_, bf16[1024,2048]{1,0:T(8,128)(2,1)S(1)} %copy-done, bf16[1024,2048]{1,0:T(8,128)(2,1)S(1)} %copy-done.1, ...), custom_call_target="tpu_custom_call" | custom-call | tf_op jit(solution)/shard_map/forward_down/pallas_call | solution.py:238
  24.3 0.6 %collective-permute-start.11 = (bf16[144,1024]{1,0:T(8,128)(2,1)S(1)}, bf16[144,1024]{1,0:T(8,128)(2,1)S(1)}, u32[]{:S(2)}, u32[]{:S(2)}) collective-permute-start(bf16[144,1024]{1,0:T(8,128)(2,1)S(1)} %join.3.refs_0_), channel_id=1, source_target_pairs={{0,16},{16,0},{1,17},{17,1},{2,18},{18,2},{3,19},{19,3},{4,20},{20... | collective-permute-start | bytes 884744 | tf_op jit(solution)/shard_map/ppermute | solution.py:401
  24.9 0.6 %collective-permute-start.12 = (bf16[144,1024]{1,0:T(8,128)(2,1)S(1)}, bf16[144,1024]{1,0:T(8,128)(2,1)S(1)}, u32[]{:S(2)}, u32[]{:S(2)}) collective-permute-start(bf16[144,1024]{1,0:T(8,128)(2,1)S(1)} %join.3.refs_0_), channel_id=1, source_target_pairs={{0,1},{1,0},{2,3},{3,2},{4,5},{5,4},{6,7},{7,6},{8,9},{9,8},{10,11... | collective-permute-start | bytes 884744 | tf_op jit(solution)/shard_map/ppermute | solution.py:401
  25.6 0.4 collective-permute-done.3.refs_0_.refs_1_.refs_5_
  25.9 3.7 %collective-permute-done.4.refs_1_.refs_2_.refs_6_ = bf16[144,1024]{1,0:T(8,128)(2,1)S(1)} collective-permute-done((bf16[144,1024]{1,0:T(8,128)(2,1)S(1)}, bf16[144,1024]{1,0:T(8,128)(2,1)S(1)}, u32[]{:S(2)}, u32[]{:S(2)}) %collective-permute-start.4) | collective-permute-done | bytes 294944 | tf_op jit(solution)/shard_map/ppermute | solution.py:401
  29.6 4.1 %forward_down.3 = (bf16[288,2048]{1,0:T(8,128)(2,1)S(1)}, bf16[288,2048]{1,0:T(8,128)(2,1)S(1)}, bf16[72,1024]{1,0:T(8,128)(2,1)S(1)}, bf16[72,1024]{1,0:T(8,128...) custom-call(bf16[144,1024]{1,0:T(8,128)(2,1)S(1)} %collective-permute-done.3.refs_0_.refs_1_.refs_5_, ...), custom_call_target="tpu_custom_call" | custom-call | tf_op jit(solution)/shard_map/forward_down/pallas_call | solution.py:238
  33.8 1.5 %collective-permute-start.13 = (bf16[144,1024]{1,0:T(8,128)(2,1)S(1)}, bf16[144,1024]{1,0:T(8,128)(2,1)S(1)}, u32[]{:S(2)}, u32[]{:S(2)}) collective-permute-start(bf16[144,1024]{1,0:T(8,128)(2,1)S(1)} %get-tuple-element.57), channel_id=1, source_target_pairs={{0,16},{16,0},{1,17},{17,1},{2,18},{18,2},{3,19},{19,3},{4,20},{20... | collective-permute-start | bytes 884744 | tf_op jit(solution)/shard_map/ppermute | solution.py:401
  35.3 4.2 %collective-permute-start.6 = (bf16[72,1024]{1,0:T(8,128)(2,1)S(1)}, bf16[72,1024]{1,0:T(8,128)(2,1)S(1)}, u32[]{:S(2)}, u32[]{:S(2)}) collective-permute-start(bf16[72,1024]{1,0:T(8,128)(2,1)S(1)} %get-tuple-element.49), channel_id=1, source_target_pairs={{0,4},{2,6},{4,0},{6,2},{1,5},{3,7},{5,1},{7,3},{8,12},{10,14},{12... | collective-permute-start | bytes 442376 | tf_op jit(solution)/shard_map/ppermute | solution.py:406
  39.5 0.2 collective-permute-start.7
  39.7 0.9 %collective-permute-done.13.refs_3_.refs_7_.refs_0_ = bf16[144,1024]{1,0:T(8,128)(2,1)S(1)} collective-permute-done((bf16[144,1024]{1,0:T(8,128)(2,1)S(1)}, bf16[144,1024]{1,0:T(8,128)(2,1)S(1)}, u32[]{:S(2)}, u32[]{:S(2)}) %collective-permute-start.13) | collective-permute-done | bytes 294944 | tf_op jit(solution)/shard_map/ppermute | solution.py:401
  40.6 0.2 turn.1.xt_ref
  40.8 1.8 %forward.1 = (bf16[144,2048]{1,0:T(8,128)(2,1)S(1)}, bf16[144,2048]{1,0:T(8,128)(2,1)S(1)}) custom-call(bf16[144,1024]{1,0:T(8,128)(2,1)S(1)} %collective-permute-done.13.refs_3_.refs_7_.refs_0_, bf16[1024,2048]{1,0:T(8,128)(2,1)S(1)} %copy-done, bf16[1024,2048]{1,0:T(8,128)(2,1)S(1)} %copy-done.1), custom_call_target="tpu_custom_call" | custom-call | tf_op jit(solution)/shard_map/forward/pallas_call | solution.py:238
  42.7 3.2 %backward.2 = (bf16[512,1024]{1,0:T(8,128)(2,1)S(1)}, bf16[512,1024]{1,0:T(8,128)(2,1)S(1)}) custom-call(bf16[512,576]{1,0:T(8,128)(2,1)S(1)} %turn.1.xt_ref, bf16[144,1024]{1,0:T(8,128)(2,1)S(1)} %join.3.refs_0_, bf16[144,1024]{1,0:T(8,128)(2,1)S(1)} %collective-permute-done.12.refs_3_.refs_1_, ...), custom_call_target="tpu_custom_call" | custom-call | flops 20000000000 | tf_op jit(solution)/shard_map/backward/pallas_call | solution.py:315
  45.9 1.0 %collective-permute-done.6.refs_2_ = bf16[72,1024]{1,0:T(8,128)(2,1)S(1)} collective-permute-done((bf16[72,1024]{1,0:T(8,128)(2,1)S(1)}, bf16[72,1024]{1,0:T(8,128)(2,1)S(1)}, u32[]{:S(2)}, u32[]{:S(2)}) %collective-permute-start.6) | collective-permute-done | bytes 147488 | tf_op jit(solution)/shard_map/ppermute | solution.py:406
  46.8 0.1 split.1
  46.9 0.4 collective-permute-start.15
  47.3 3.2 %backward.3 = (bf16[512,1024]{1,0:T(8,128)(2,1)S(1)}, bf16[512,1024]{1,0:T(8,128)(2,1)S(1)}) custom-call(bf16[512,576]{1,0:T(8,128)(2,1)S(1)} %turn.1.xt_ref, bf16[144,1024]{1,0:T(8,128)(2,1)S(1)} %join.3.refs_0_, bf16[144,1024]{1,0:T(8,128)(2,1)S(1)} %collective-permute-done.12.refs_3_.refs_1_, ...), custom_call_target="tpu_custom_call" | custom-call | flops 20000000000 | tf_op jit(solution)/shard_map/backward/pallas_call | solution.py:315
  50.5 0.6 %collective-permute-start.17 = (bf16[512,1024]{1,0:T(8,128)(2,1)S(1)}, bf16[512,1024]{1,0:T(8,128)(2,1)S(1)}, u32[]{:S(2)}, u32[]{:S(2)}) collective-permute-start(bf16[512,1024]{1,0:T(8,128)(2,1)S(1)} %get-tuple-element.69), channel_id=1, source_target_pairs={{0,8},{8,0},{1,9},{9,1},{2,10},{10,2},{3,11},{11,3},{4,12},{12,4},... | collective-permute-start | bytes 3145736 | tf_op jit(solution)/shard_map/ppermute | solution.py:401
  51.1 1.1 %finish.2 = (bf16[256,2048]{1,0:T(8,128)(2,1)}, bf16[256,2048]{1,0:T(8,128)(2,1)}) custom-call(bf16[512,1024]{1,0:T(8,128)(2,1)S(1)} %get-tuple-element.63.refs_4_.refs_0_, bf16[512,1024]{1,0:T(8,128)(2,1)S(1)} %collective-permute-done.16.refs_1_), custom_call_target="tpu_custom_call" | custom-call | tf_op jit(solution)/shard_map/finish/pallas_call | solution.py:351
  52.2 1.5 %collective-permute-done.15.got_ref = bf16[144,1024]{1,0:T(8,128)(2,1)S(1)} collective-permute-done((bf16[144,1024]{1,0:T(8,128)(2,1)S(1)}, bf16[144,1024]{1,0:T(8,128)(2,1)S(1)}, u32[]{:S(2)}, u32[]{:S(2)}) %collective-permute-start.15) | collective-permute-done | bytes 294944 | tf_op jit(solution)/shard_map/ppermute | solution.py:401
  53.7 1.0 %unpack.1 = bf16[128,1024]{1,0:T(8,128)(2,1)} custom-call(bf16[144,128]{1,0:T(8,128)(2,1)S(1)} %get-tuple-element.38.placer_ref, bf16[144,1024]{1,0:T(8,128)(2,1)S(1)} %get-tuple-element.64.mine_ref.refs_11_, bf16[144,1024]{1,0:T(8,128)(2,1)S(1)} %collective-permute-done.15.got_ref, bf16[256,2048]{1,0:T(8,128)(2,1)} %get-tuple-element.67.refs_0_.refs_2_), custom_call_target="tpu_custom_call" | custom-call | flops 20000000000 | tf_op jit(solution)/shard_map/unpack/pallas_call | solution.py:390
  54.8 1.1 %finish.3 = (bf16[256,2048]{1,0:T(8,128)(2,1)}, bf16[256,2048]{1,0:T(8,128)(2,1)}) custom-call(bf16[512,1024]{1,0:T(8,128)(2,1)S(1)} %get-tuple-element.68.refs_0_, bf16[512,1024]{1,0:T(8,128)(2,1)S(1)} %collective-permute-done.17.refs_1_, bf16[256,2048]{1,0:T(8,128)(2,1)} %get-tuple-element.67.refs_0_.refs_2_, ...), custom_call_target="tpu_custom_call", output_to_operand_aliasing={{0}: (2, {}), {1}: (3, {})} | custom-call | tf_op jit(solution)/shard_map/finish/pallas_call | solution.py:351
  (24 shorter events, 0.2 us)
Async XLA Ops:
  2.1 9.5 %collective-permute-start = (bf16[36,1024]{1,0:T(8,128)(2,1)S(1)}, bf16[36,1024]{1,0:T(8,128)(2,1)S(1)}, u32[]{:S(2)}, u32[]{:S(2)}) collective-permute-start(bf16[36,1024]{1,0:T(8,128)(2,1)S(1)} %get-tuple-element.39), channel_id=1, source_target_pairs={{0,6},{2,4},{4,2},{6,0},{1,7},{3,5},{5,3},{7,1},{8,14},{10,12},{12... | collective-permute-start | bytes 221192 | tf_op jit(solution)/shard_map/ppermute | solution.py:406
  7.2 11.2 %collective-permute-start.1 = (bf16[36,1024]{1,0:T(8,128)(2,1)S(1)}, bf16[36,1024]{1,0:T(8,128)(2,1)S(1)}, u32[]{:S(2)}, u32[]{:S(2)}) collective-permute-start(bf16[36,1024]{1,0:T(8,128)(2,1)S(1)} %get-tuple-element.40), channel_id=1, source_target_pairs={{0,4},{2,6},{4,0},{6,2},{1,5},{3,7},{5,1},{7,3},{8,12},{10,14},{12... | collective-permute-start | bytes 221192 | tf_op jit(solution)/shard_map/ppermute | solution.py:406
  7.2 11.2 %collective-permute-start.2 = (bf16[36,1024]{1,0:T(8,128)(2,1)S(1)}, bf16[36,1024]{1,0:T(8,128)(2,1)S(1)}, u32[]{:S(2)}, u32[]{:S(2)}) collective-permute-start(bf16[36,1024]{1,0:T(8,128)(2,1)S(1)} %get-tuple-element.41), channel_id=1, source_target_pairs={{0,2},{2,0},{4,6},{6,4},{1,3},{3,1},{5,7},{7,5},{8,10},{10,8},{12,... | collective-permute-start | bytes 221192 | tf_op jit(solution)/shard_map/ppermute | solution.py:406
  7.9 16.3 %collective-permute-start.8 = (bf16[36,1024]{1,0:T(8,128)(2,1)S(1)}, bf16[36,1024]{1,0:T(8,128)(2,1)S(1)}, u32[]{:S(2)}, u32[]{:S(2)}) collective-permute-start(bf16[36,1024]{1,0:T(8,128)(2,1)S(1)} %get-tuple-element.51), channel_id=1, source_target_pairs={{0,6},{2,4},{4,2},{6,0},{1,7},{3,5},{5,3},{7,1},{8,14},{10,12},{12... | collective-permute-start | bytes 221192 | tf_op jit(solution)/shard_map/ppermute | solution.py:406
  11.6 12.6 %collective-permute-start.9 = (bf16[36,1024]{1,0:T(8,128)(2,1)S(1)}, bf16[36,1024]{1,0:T(8,128)(2,1)S(1)}, u32[]{:S(2)}, u32[]{:S(2)}) collective-permute-start(bf16[36,1024]{1,0:T(8,128)(2,1)S(1)} %get-tuple-element.52), channel_id=1, source_target_pairs={{0,4},{2,6},{4,0},{6,2},{1,5},{3,7},{5,1},{7,3},{8,12},{10,14},{12... | collective-permute-start | bytes 221192 | tf_op jit(solution)/shard_map/ppermute | solution.py:406
  11.6 12.6 %collective-permute-start.10 = (bf16[36,1024]{1,0:T(8,128)(2,1)S(1)}, bf16[36,1024]{1,0:T(8,128)(2,1)S(1)}, u32[]{:S(2)}, u32[]{:S(2)}) collective-permute-start(bf16[36,1024]{1,0:T(8,128)(2,1)S(1)} %get-tuple-element.53), channel_id=1, source_target_pairs={{0,2},{2,0},{4,6},{6,4},{1,3},{3,1},{5,7},{7,5},{8,10},{10,8},{12,... | collective-permute-start | bytes 221192 | tf_op jit(solution)/shard_map/ppermute | solution.py:406
  15.2 6.2 %copy-start = (bf16[1024,2048]{1,0:T(8,128)(2,1)S(1)}, bf16[1024,2048]{1,0:T(8,128)(2,1)}, u32[]{:S(2)}) copy-start(bf16[1024,2048]{1,0:T(8,128)(2,1)} %refs_1_.3) | copy-start | bytes 12582916
  15.2 6.2 %copy-start.1 = (bf16[1024,2048]{1,0:T(8,128)(2,1)S(1)}, bf16[1024,2048]{1,0:T(8,128)(2,1)}, u32[]{:S(2)}) copy-start(bf16[1024,2048]{1,0:T(8,128)(2,1)} %refs_2_.5) | copy-start | bytes 12582916
  18.5 7.5 %collective-permute-start.3 = (bf16[144,1024]{1,0:T(8,128)(2,1)S(1)}, bf16[144,1024]{1,0:T(8,128)(2,1)S(1)}, u32[]{:S(2)}, u32[]{:S(2)}) collective-permute-start(bf16[144,1024]{1,0:T(8,128)(2,1)S(1)} %join.2.refs_0_.refs_4_), channel_id=1, source_target_pairs={{0,1},{1,0},{2,3},{3,2},{4,5},{5,4},{6,7},{7,6},{8,9},{9,8},{10,11... | collective-permute-start | bytes 884744 | tf_op jit(solution)/shard_map/ppermute | solution.py:401
  19.9 9.7 %collective-permute-start.4 = (bf16[144,1024]{1,0:T(8,128)(2,1)S(1)}, bf16[144,1024]{1,0:T(8,128)(2,1)S(1)}, u32[]{:S(2)}, u32[]{:S(2)}) collective-permute-start(bf16[144,1024]{1,0:T(8,128)(2,1)S(1)} %join.2.refs_0_.refs_4_), channel_id=1, source_target_pairs={{0,16},{16,0},{1,17},{17,1},{2,18},{18,2},{3,19},{19,3},{4,20},{20... | collective-permute-start | bytes 884744 | tf_op jit(solution)/shard_map/ppermute | solution.py:401
  24.3 9.4 %collective-permute-start.11 = (bf16[144,1024]{1,0:T(8,128)(2,1)S(1)}, bf16[144,1024]{1,0:T(8,128)(2,1)S(1)}, u32[]{:S(2)}, u32[]{:S(2)}) collective-permute-start(bf16[144,1024]{1,0:T(8,128)(2,1)S(1)} %join.3.refs_0_), channel_id=1, source_target_pairs={{0,16},{16,0},{1,17},{17,1},{2,18},{18,2},{3,19},{19,3},{4,20},{20... | collective-permute-start | bytes 884744 | tf_op jit(solution)/shard_map/ppermute | solution.py:401
  24.9 8.8 %collective-permute-start.12 = (bf16[144,1024]{1,0:T(8,128)(2,1)S(1)}, bf16[144,1024]{1,0:T(8,128)(2,1)S(1)}, u32[]{:S(2)}, u32[]{:S(2)}) collective-permute-start(bf16[144,1024]{1,0:T(8,128)(2,1)S(1)} %join.3.refs_0_), channel_id=1, source_target_pairs={{0,1},{1,0},{2,3},{3,2},{4,5},{5,4},{6,7},{7,6},{8,9},{9,8},{10,11... | collective-permute-start | bytes 884744 | tf_op jit(solution)/shard_map/ppermute | solution.py:401
  33.8 6.8 %collective-permute-start.13 = (bf16[144,1024]{1,0:T(8,128)(2,1)S(1)}, bf16[144,1024]{1,0:T(8,128)(2,1)S(1)}, u32[]{:S(2)}, u32[]{:S(2)}) collective-permute-start(bf16[144,1024]{1,0:T(8,128)(2,1)S(1)} %get-tuple-element.57), channel_id=1, source_target_pairs={{0,16},{16,0},{1,17},{17,1},{2,18},{18,2},{3,19},{19,3},{4,20},{20... | collective-permute-start | bytes 884744 | tf_op jit(solution)/shard_map/ppermute | solution.py:401
  35.3 7.3 %collective-permute-start.14 = (bf16[144,1024]{1,0:T(8,128)(2,1)S(1)}, bf16[144,1024]{1,0:T(8,128)(2,1)S(1)}, u32[]{:S(2)}, u32[]{:S(2)}) collective-permute-start(bf16[144,1024]{1,0:T(8,128)(2,1)S(1)} %get-tuple-element.58), channel_id=1, source_target_pairs={{0,1},{1,0},{2,3},{3,2},{4,5},{5,4},{6,7},{7,6},{8,9},{9,8},{10,11... | collective-permute-start | bytes 884744 | tf_op jit(solution)/shard_map/ppermute | solution.py:401
  35.3 10.5 %collective-permute-start.5 = (bf16[72,1024]{1,0:T(8,128)(2,1)S(1)}, bf16[72,1024]{1,0:T(8,128)(2,1)S(1)}, u32[]{:S(2)}, u32[]{:S(2)}) collective-permute-start(bf16[72,1024]{1,0:T(8,128)(2,1)S(1)} %get-tuple-element.48), channel_id=1, source_target_pairs={{0,2},{2,0},{4,6},{6,4},{1,3},{3,1},{5,7},{7,5},{8,10},{10,8},{12,... | collective-permute-start | bytes 442376 | tf_op jit(solution)/shard_map/ppermute | solution.py:406
  35.3 11.5 %collective-permute-start.6 = (bf16[72,1024]{1,0:T(8,128)(2,1)S(1)}, bf16[72,1024]{1,0:T(8,128)(2,1)S(1)}, u32[]{:S(2)}, u32[]{:S(2)}) collective-permute-start(bf16[72,1024]{1,0:T(8,128)(2,1)S(1)} %get-tuple-element.49), channel_id=1, source_target_pairs={{0,4},{2,6},{4,0},{6,2},{1,5},{3,7},{5,1},{7,3},{8,12},{10,14},{12... | collective-permute-start | bytes 442376 | tf_op jit(solution)/shard_map/ppermute | solution.py:406
  39.5 7.3 %collective-permute-start.7 = (bf16[72,1024]{1,0:T(8,128)(2,1)S(1)}, bf16[72,1024]{1,0:T(8,128)(2,1)S(1)}, u32[]{:S(2)}, u32[]{:S(2)}) collective-permute-start(bf16[72,1024]{1,0:T(8,128)(2,1)S(1)} %get-tuple-element.50), channel_id=1, source_target_pairs={{0,6},{2,4},{4,2},{6,0},{1,7},{3,5},{5,3},{7,1},{8,14},{10,12},{12... | collective-permute-start | bytes 442376 | tf_op jit(solution)/shard_map/ppermute | solution.py:406
  46.9 6.8 %collective-permute-start.15 = (bf16[144,1024]{1,0:T(8,128)(2,1)S(1)}, bf16[144,1024]{1,0:T(8,128)(2,1)S(1)}, u32[]{:S(2)}, u32[]{:S(2)}) collective-permute-start(bf16[144,1024]{1,0:T(8,128)(2,1)S(1)} %get-tuple-element.65), channel_id=1, source_target_pairs={{0,1},{1,0},{2,3},{3,2},{4,5},{5,4},{6,7},{7,6},{8,9},{9,8},{10,11... | collective-permute-start | bytes 884744 | tf_op jit(solution)/shard_map/ppermute | solution.py:401
  47.3 3.8 %collective-permute-start.16 = (bf16[512,1024]{1,0:T(8,128)(2,1)S(1)}, bf16[512,1024]{1,0:T(8,128)(2,1)S(1)}, u32[]{:S(2)}, u32[]{:S(2)}) collective-permute-start(bf16[512,1024]{1,0:T(8,128)(2,1)S(1)} %get-tuple-element.66), channel_id=1, source_target_pairs={{0,8},{8,0},{1,9},{9,1},{2,10},{10,2},{3,11},{11,3},{4,12},{12,4},... | collective-permute-start | bytes 3145736 | tf_op jit(solution)/shard_map/ppermute | solution.py:401
  50.5 4.2 %collective-permute-start.17 = (bf16[512,1024]{1,0:T(8,128)(2,1)S(1)}, bf16[512,1024]{1,0:T(8,128)(2,1)S(1)}, u32[]{:S(2)}, u32[]{:S(2)}) collective-permute-start(bf16[512,1024]{1,0:T(8,128)(2,1)S(1)} %get-tuple-element.69), channel_id=1, source_target_pairs={{0,8},{8,0},{1,9},{9,1},{2,10},{10,2},{3,11},{11,3},{4,12},{12,4},... | collective-permute-start | bytes 3145736 | tf_op jit(solution)/shard_map/ppermute | solution.py:401

commit v11 on v10

--- a/solution.py
+++ b/solution.py
@@ -10,8 +10,9 @@
 
 EXPERTS = 4
 CAP = 36
-STRIP = 512
+STRIP = 1024
 PAIR = 2 * STRIP
+SLICE = 256
 MIB = 1024 * 1024
 LARGE = pltpu.CompilerParams(vmem_limit_bytes=16 * MIB)
 SMALL = pltpu.CompilerParams(vmem_limit_bytes=12 * MIB)
@@ -141,15 +142,15 @@
 
 
 def flip_kernel(source_ref, here_ref, flipped_ref, sems):
-    steps = source_ref.shape[0] // STRIP
+    steps = source_ref.shape[0] // SLICE
     copies = []
     for j in range(steps):
-        rows = pl.ds(j * STRIP, STRIP)
+        rows = pl.ds(j * SLICE, SLICE)
         copies.append(pltpu.make_async_copy(source_ref.at[rows], here_ref.at[rows], sems.at[j]))
         copies[j].start()
     for j in range(steps):
         copies[j].wait()
-        rows = slice(j * STRIP, (j + 1) * STRIP)
+        rows = slice(j * SLICE, (j + 1) * SLICE)
         flipped_ref[:, rows] = here_ref[rows, :].T
 
 
@@ -159,7 +160,7 @@
         out_shape=[pltpu.VMEM(value.shape, value.dtype), pltpu.VMEM(value.shape[::-1], value.dtype)],
         in_specs=[AFAR],
         out_specs=[HERE, HERE],
-        scratch_shapes=[pltpu.SemaphoreType.DMA((value.shape[0] // STRIP,))],
+        scratch_shapes=[pltpu.SemaphoreType.DMA((value.shape[0] // SLICE,))],
         compiler_params=SMALL,
         cost_estimate=CHEAP,
         name="flip",
@@ -167,12 +168,11 @@
 
 
 def forward_kernel(n, fetch, down, pair, unused, *refs):
-    refs = list(refs)
+    refs = list(refs[unused:])
     xs = [refs.pop(0) for _ in range(n)]
     wg_ref, wu_ref = refs.pop(0), refs.pop(0)
     wd_ref = refs.pop(0) if down else None
     other_ref = refs.pop(0) if pair else None
-    refs = refs[unused:]
     act_ref, coef_ref = refs.pop(0), refs.pop(0)
     shares = [refs.pop(0) for _ in range(EXPERTS if pair else down)]
     if fetch:
@@ -240,17 +240,17 @@
         out_shape=[jax.ShapeDtypeStruct((rows, cols), BF16)] * 2
         + shares
         + [pltpu.VMEM(wg.shape, wg.dtype)] * (2 * fetch),
-        in_specs=[HERE] * n
+        in_specs=[ANYWHERE] * len(earlier)
+        + [HERE] * n
         + [AFAR if fetch else HERE] * 2
-        + [HERE] * (down + pair)
-        + [ANYWHERE] * len(earlier),
+        + [HERE] * (down + pair),
         scratch_shapes=[pltpu.VMEM((part, width), F32)] * down
         + [pltpu.VMEM((rows, width), BF16)] * (n > 1)
         + [pltpu.SemaphoreType.DMA((cols // PAIR, 2))] * fetch,
         compiler_params=LARGE,
         cost_estimate=CHEAP,
         name="forward" + "_fetch" * fetch + "_down" * down,
-    )(*xs, *weights, *([wd] * down), *([other] * pair), *earlier)
+    )(*earlier, *xs, *weights, *([wd] * down), *([other] * pair))
 
 
 def turn_kernel(_, __, *refs):
@@ -362,7 +362,7 @@
 
 
 def split_kernel(*refs):
-    blocks = [r[...].astype(F32) for r in refs[:EXPERTS]]
+    blocks = [r[...].astype(F32) for r in refs[EXPERTS - 1 :: -1]]
     refs[-2][...] = jnp.concatenate([b[:CAP] for b in blocks], axis=0).astype(BF16)
     refs[-1][...] = jnp.concatenate([b[CAP:] for b in blocks], axis=0).astype(BF16)
 
@@ -376,7 +376,7 @@
         compiler_params=SMALL,
         cost_estimate=CHEAP,
         name="split",
-    )(*blocks, *earlier)
+    )(*blocks[::-1], *earlier)
 
 
 def unpack_kernel(placer_ref, mine_ref, got_ref, *refs):
@@ -423,22 +423,24 @@
 
     moved = across_planes(blocks[:EXPERTS])
     x_own = join(moved, [wdt])
-    x_near, x_far = swap(x_own, "half"), swap(x_own, "far")
+    x_far, x_near = swap(x_own, "far"), swap(x_own, "half")
     moved = across_planes(blocks[EXPERTS:])
 
     wg, wu = w_gate, w_up
     act0, coef0, share_own = forward([x_own], wg, wu, wd)
     g_own = join(moved, [act0])
-    g_near, g_far = swap(g_own, "half"), swap(g_own, "far")
-    act1, coef1, *shares = forward([x_near, x_far], wg, wu, wd, other=share_own)
-    x_pass, g_pass = relay([x_near, g_far], [mark(act1), g_near])
+    g_far, g_near = swap(g_own, "far"), swap(g_own, "half")
+    act2, coef2 = forward([x_far], wg, wu)
+    act1, coef1, *shares = forward([x_near], wg, wu, wd, other=share_own, earlier=[act2])
+    (x_pass,) = relay([x_near], [mark(act1), g_far])
+    (g_pass,) = relay([g_far], [x_pass, g_near])
     x_corner, g_corner = swap(x_pass, "far"), swap(g_pass, "half")
     returned = across_planes(shares)
-    act2, coef2 = forward([x_corner], wg, wu)
+    act3, coef3 = forward([x_corner], wg, wu)
     xt = turn(*scalars[1:], [x_own, x_near, x_far, x_corner], share)
 
     gs = [g_own, g_near, g_far, g_corner]
-    acts, coefs = [act0, act1, act2], [coef0, coef1, coef2]
+    acts, coefs = [act0, act1, act2, act3], [coef0, coef1, coef2, coef3]
     cols = w_down.shape[0]
     half = cols // 2
     own0, sib0 = backward(xt, gs, acts, coefs, wdt, 0, half)

time: 56 us -> 57.9 us (1.034)
  starting transfers between devices: 24.2 us -> 25.8 us
  waiting for transfers between devices: 7.84 us -> 8.88 us
  Pallas kernels: 23 us -> 22.1 us
    ppermute x9, waiting for transfers between devices: 1.4 us -> 3.97 us  [across_planes(): lax.ppermute(blocks[k], 'arch', [(i, i ^ k) for i in range(EXPERTS)])]
    ppermute x9, starting transfers between devices: 6.72 us -> 8.31 us  [swap(): return lax.ppermute(value, axis, [(0, 1), (1, 0)])]
    ppermute x9, waiting for transfers between devices: 6.43 us -> 4.91 us  [swap(): return lax.ppermute(value, axis, [(0, 1), (1, 0)])]
    pallas_call x3 -> x4, Pallas kernels: 8.7 us -> 7.64 us  [forward(): pl.pallas_call(functools.partial(forward_kernel, n, fetch, down, pair, le...]
  transfers between devices with their start and end apart: 18 -> 18, of which waited for: 6 -> 5; matrix products, arithmetic and copies ran while one was open for 0% -> 0% of each run, Pallas kernels for 36% -> 34%
where the time goes in v11:
time: 57.9 us; the launch traced here: 57.8 us
  starting transfers between devices  25.8 us (45%)
  Pallas kernels  22.1 us (38%)
  waiting for transfers between devices  8.88 us (15%)
  between operations  0.98 us (2%)
    ppermute x9, starting transfers between devices, across_planes(): lax.ppermute(blocks[k], 'arch', [(i, i ^ k) for i in range(EXPERTS)])  17.5 us
    ppermute x9, starting transfers between devices, swap(): return lax.ppermute(value, axis, [(0, 1), (1, 0)])  8.31 us
    pallas_call x4, Pallas kernels, forward(): pl.pallas_call(functools.partial(forward_kernel, n, fetch, down, pair, le...  7.64 us
    pallas_call x2, Pallas kernels, backward(): pl.pallas_call(functools.partial(backward_kernel, first, counts), out_sha...  6.45 us
    ppermute x9, waiting for transfers between devices, swap(): return lax.ppermute(value, axis, [(0, 1), (1, 0)])  4.91 us
    ppermute x9, waiting for transfers between devices, across_planes(): lax.ppermute(blocks[k], 'arch', [(i, i ^ k) for i in range(EXPERTS)])  3.97 us
    pallas_call x1, Pallas kernels, flip(): pl.pallas_call(flip_kernel, out_shape=[pltpu.VMEM(value.shape, value.dtyp...  2.88 us
    pallas_call x2, Pallas kernels, finish(): pl.pallas_call(functools.partial(finish_kernel, spans, more), out_shape=[...  2.21 us
  transfers between devices with their start and end apart: 18, of which 5 were waited for; matrix products, arithmetic and copies ran while one was open for 0% of the time, Pallas kernels for 34%

profile of v11, /device:TPU:0, one launch (start us, length us, event | category | flops | bytes accessed | tf_op | source)
XLA Modules:
  0.0 57.8 jit_solution(15031224636456826852)
XLA Ops:
  0.6 1.5 %pack.1 = (bf16[144,128]{1,0:T(8,128)(2,1)S(1)}, bf16[36,1024]{1,0:T(8,128)(2,1)S(1)}, bf16[36,1024]{1,0:T(8,128)(2,1)S(1)}, bf16[36,1024]{1,0:T(8,128)(2,1)S(1)...) custom-call(s32[1]{0:T(128)} %bitcast.plane_ref, ...), custom_call_target="tpu_custom_call" | custom-call | tf_op jit(solution)/shard_map/pack/pallas_call | solution.py:79
  2.1 5.1 %collective-permute-start = (bf16[36,1024]{1,0:T(8,128)(2,1)S(1)}, bf16[36,1024]{1,0:T(8,128)(2,1)S(1)}, u32[]{:S(2)}, u32[]{:S(2)}) collective-permute-start(bf16[36,1024]{1,0:T(8,128)(2,1)S(1)} %get-tuple-element.39), channel_id=1, source_target_pairs={{0,6},{2,4},{4,2},{6,0},{1,7},{3,5},{5,3},{7,1},{8,14},{10,12},{12... | collective-permute-start | bytes 221192 | tf_op jit(solution)/shard_map/ppermute | solution.py:406
  7.2 0.6 %collective-permute-start.2 = (bf16[36,1024]{1,0:T(8,128)(2,1)S(1)}, bf16[36,1024]{1,0:T(8,128)(2,1)S(1)}, u32[]{:S(2)}, u32[]{:S(2)}) collective-permute-start(bf16[36,1024]{1,0:T(8,128)(2,1)S(1)} %get-tuple-element.41), channel_id=1, source_target_pairs={{0,2},{2,0},{4,6},{6,4},{1,3},{3,1},{5,7},{7,5},{8,10},{10,8},{12,... | collective-permute-start | bytes 221192 | tf_op jit(solution)/shard_map/ppermute | solution.py:406
  7.9 3.7 %collective-permute-start.8 = (bf16[36,1024]{1,0:T(8,128)(2,1)S(1)}, bf16[36,1024]{1,0:T(8,128)(2,1)S(1)}, u32[]{:S(2)}, u32[]{:S(2)}) collective-permute-start(bf16[36,1024]{1,0:T(8,128)(2,1)S(1)} %get-tuple-element.53), channel_id=1, source_target_pairs={{0,6},{2,4},{4,2},{6,0},{1,7},{3,5},{5,3},{7,1},{8,14},{10,12},{12... | collective-permute-start | bytes 221192 | tf_op jit(solution)/shard_map/ppermute | solution.py:406
  11.6 3.6 %collective-permute-start.10 = (bf16[36,1024]{1,0:T(8,128)(2,1)S(1)}, bf16[36,1024]{1,0:T(8,128)(2,1)S(1)}, u32[]{:S(2)}, u32[]{:S(2)}) collective-permute-start(bf16[36,1024]{1,0:T(8,128)(2,1)S(1)} %get-tuple-element.55), channel_id=1, source_target_pairs={{0,2},{2,0},{4,6},{6,4},{1,3},{3,1},{5,7},{7,5},{8,10},{10,8},{12,... | collective-permute-start | bytes 221192 | tf_op jit(solution)/shard_map/ppermute | solution.py:406
  15.2 2.9 %flip.1 = (bf16[2048,1024]{1,0:T(8,128)(2,1)S(1)}, bf16[1024,2048]{1,0:T(8,128)(2,1)S(1)}) custom-call(bf16[2048,1024]{1,0:T(8,128)(2,1)} %source_ref), custom_call_target="tpu_custom_call" | custom-call | tf_op jit(solution)/shard_map/flip/pallas_call | solution.py:158
  18.1 0.3 collective-permute-done.1.refs_1_
  18.5 1.4 %collective-permute-start.3 = (bf16[144,1024]{1,0:T(8,128)(2,1)S(1)}, bf16[144,1024]{1,0:T(8,128)(2,1)S(1)}, u32[]{:S(2)}, u32[]{:S(2)}) collective-permute-start(bf16[144,1024]{1,0:T(8,128)(2,1)S(1)} %join.2.refs_0_.refs_4_), channel_id=1, source_target_pairs={{0,16},{16,0},{1,17},{17,1},{2,18},{18,2},{3,19},{19,3},{4,20},{20... | collective-permute-start | bytes 884744 | tf_op jit(solution)/shard_map/ppermute | solution.py:401
  19.9 1.5 %collective-permute-start.4 = (bf16[144,1024]{1,0:T(8,128)(2,1)S(1)}, bf16[144,1024]{1,0:T(8,128)(2,1)S(1)}, u32[]{:S(2)}, u32[]{:S(2)}) collective-permute-start(bf16[144,1024]{1,0:T(8,128)(2,1)S(1)} %join.2.refs_0_.refs_4_), channel_id=1, source_target_pairs={{0,1},{1,0},{2,3},{3,2},{4,5},{5,4},{6,7},{7,6},{8,9},{9,8},{10,11... | collective-permute-start | bytes 884744 | tf_op jit(solution)/shard_map/ppermute | solution.py:401
  21.4 2.2 %forward_down.2 = (bf16[144,2048]{1,0:T(8,128)(2,1)S(1)}, bf16[144,2048]{1,0:T(8,128)(2,1)S(1)}, bf16[144,1024]{1,0:T(8,128)(2,1)S(1)}) custom-call(bf16[144,1024]{1,0:T(8,128)(2,1)S(1)} %join.2.refs_0_.refs_4_, bf16[1024,2048]{1,0:T(8,128)(2,1)S(1)} %copy-done, bf16[1024,2048]{1,0:T(8,128)(2,1)S(1)} %copy-done.1, ...), custom_call_target="tpu_custom_call" | custom-call | tf_op jit(solution)/shard_map/forward_down/pallas_call | solution.py:238
  23.7 0.6 %collective-permute-start.11 = (bf16[144,1024]{1,0:T(8,128)(2,1)S(1)}, bf16[144,1024]{1,0:T(8,128)(2,1)S(1)}, u32[]{:S(2)}, u32[]{:S(2)}) collective-permute-start(bf16[144,1024]{1,0:T(8,128)(2,1)S(1)} %join.3.refs_0_), channel_id=1, source_target_pairs={{0,16},{16,0},{1,17},{17,1},{2,18},{18,2},{3,19},{19,3},{4,20},{20... | collective-permute-start | bytes 884744 | tf_op jit(solution)/shard_map/ppermute | solution.py:401
  24.3 0.6 %collective-permute-start.13 = (bf16[144,1024]{1,0:T(8,128)(2,1)S(1)}, bf16[144,1024]{1,0:T(8,128)(2,1)S(1)}, u32[]{:S(2)}, u32[]{:S(2)}) collective-permute-start(bf16[144,1024]{1,0:T(8,128)(2,1)S(1)} %join.3.refs_0_), channel_id=1, source_target_pairs={{0,1},{1,0},{2,3},{3,2},{4,5},{5,4},{6,7},{7,6},{8,9},{9,8},{10,11... | collective-permute-start | bytes 884744 | tf_op jit(solution)/shard_map/ppermute | solution.py:401
  25.0 2.4 %collective-permute-done.3.refs_0_.refs_2_.refs_6_ = bf16[144,1024]{1,0:T(8,128)(2,1)S(1)} collective-permute-done((bf16[144,1024]{1,0:T(8,128)(2,1)S(1)}, bf16[144,1024]{1,0:T(8,128)(2,1)S(1)}, u32[]{:S(2)}, u32[]{:S(2)}) %collective-permute-start.3) | collective-permute-done | bytes 294944 | tf_op jit(solution)/shard_map/ppermute | solution.py:401
  27.4 1.6 %forward.2 = (bf16[144,2048]{1,0:T(8,128)(2,1)S(1)}, bf16[144,2048]{1,0:T(8,128)(2,1)S(1)}) custom-call(bf16[144,1024]{1,0:T(8,128)(2,1)S(1)} %collective-permute-done.3.refs_0_.refs_2_.refs_6_, bf16[1024,2048]{1,0:T(8,128)(2,1)S(1)} %copy-done, bf16[1024,2048]{1,0:T(8,128)(2,1)S(1)} %copy-done.1), custom_call_target="tpu_custom_call" | custom-call | tf_op jit(solution)/shard_map/forward/pallas_call | solution.py:238
  29.0 2.2 %forward_down.3 = (bf16[144,2048]{1,0:T(8,128)(2,1)S(1)}, bf16[144,2048]{1,0:T(8,128)(2,1)S(1)}, bf16[72,1024]{1,0:T(8,128)(2,1)S(1)}, bf16[72,1024]{1,0:T(8,128...) custom-call(bf16[144,2048]{1,0:T(8,128)(2,1)S(1)} %get-tuple-element.45.refs_0_.refs_6_, ...), custom_call_target="tpu_custom_call" | custom-call | tf_op jit(solution)/shard_map/forward_down/pallas_call | solution.py:238
  31.2 0.3 collective-permute-done.11.refs_2_.refs_0_
  31.6 1.4 %collective-permute-start.12 = (bf16[144,1024]{1,0:T(8,128)(2,1)S(1)}, bf16[144,1024]{1,0:T(8,128)(2,1)S(1)}, u32[]{:S(2)}, u32[]{:S(2)}) collective-permute-start(bf16[144,1024]{1,0:T(8,128)(2,1)S(1)} %relay.2.refs_1_), channel_id=1, source_target_pairs={{0,16},{16,0},{1,17},{17,1},{2,18},{18,2},{3,19},{19,3},{4,20},{20... | collective-permute-start | bytes 884744 | tf_op jit(solution)/shard_map/ppermute | solution.py:401
  33.0 1.6 %collective-permute-start.14 = (bf16[144,1024]{1,0:T(8,128)(2,1)S(1)}, bf16[144,1024]{1,0:T(8,128)(2,1)S(1)}, u32[]{:S(2)}, u32[]{:S(2)}) collective-permute-start(bf16[144,1024]{1,0:T(8,128)(2,1)S(1)} %relay.3), channel_id=1, source_target_pairs={{0,1},{1,0},{2,3},{3,2},{4,5},{5,4},{6,7},{7,6},{8,9},{9,8},{10,11... | collective-permute-start | bytes 884744 | tf_op jit(solution)/shard_map/ppermute | solution.py:401
  34.6 3.2 %collective-permute-start.5 = (bf16[72,1024]{1,0:T(8,128)(2,1)S(1)}, bf16[72,1024]{1,0:T(8,128)(2,1)S(1)}, u32[]{:S(2)}, u32[]{:S(2)}) collective-permute-start(bf16[72,1024]{1,0:T(8,128)(2,1)S(1)} %get-tuple-element.48), channel_id=1, source_target_pairs={{0,6},{2,4},{4,2},{6,0},{1,7},{3,5},{5,3},{7,1},{8,14},{10,12},{12... | collective-permute-start | bytes 442376 | tf_op jit(solution)/shard_map/ppermute | solution.py:406
  37.8 1.2 %collective-permute-start.7 = (bf16[72,1024]{1,0:T(8,128)(2,1)S(1)}, bf16[72,1024]{1,0:T(8,128)(2,1)S(1)}, u32[]{:S(2)}, u32[]{:S(2)}) collective-permute-start(bf16[72,1024]{1,0:T(8,128)(2,1)S(1)} %get-tuple-element.50), channel_id=1, source_target_pairs={{0,2},{2,0},{4,6},{6,4},{1,3},{3,1},{5,7},{7,5},{8,10},{10,8},{12,... | collective-permute-start | bytes 442376 | tf_op jit(solution)/shard_map/ppermute | solution.py:406
  39.0 0.2 turn.1.xt_ref
  39.3 1.6 %forward.3 = (bf16[144,2048]{1,0:T(8,128)(2,1)S(1)}, bf16[144,2048]{1,0:T(8,128)(2,1)S(1)}) custom-call(bf16[144,1024]{1,0:T(8,128)(2,1)S(1)} %collective-permute-done.12.refs_3_.refs_7_.refs_0_, bf16[1024,2048]{1,0:T(8,128)(2,1)S(1)} %copy-done, bf16[1024,2048]{1,0:T(8,128)(2,1)S(1)} %copy-done.1), custom_call_target="tpu_custom_call" | custom-call | tf_op jit(solution)/shard_map/forward/pallas_call | solution.py:238
  40.9 3.3 %backward.2 = (bf16[512,1024]{1,0:T(8,128)(2,1)S(1)}, bf16[512,1024]{1,0:T(8,128)(2,1)S(1)}) custom-call(bf16[512,576]{1,0:T(8,128)(2,1)S(1)} %turn.1.xt_ref, bf16[144,1024]{1,0:T(8,128)(2,1)S(1)} %join.3.refs_0_, bf16[144,1024]{1,0:T(8,128)(2,1)S(1)} %collective-permute-done.13.refs_2_.refs_1_, ...), custom_call_target="tpu_custom_call" | custom-call | flops 20000000000 | tf_op jit(solution)/shard_map/backward/pallas_call | solution.py:315
  44.2 3.6 %collective-permute-done.6.refs_1_ = bf16[72,1024]{1,0:T(8,128)(2,1)S(1)} collective-permute-done((bf16[72,1024]{1,0:T(8,128)(2,1)S(1)}, bf16[72,1024]{1,0:T(8,128)(2,1)S(1)}, u32[]{:S(2)}, u32[]{:S(2)}) %collective-permute-start.6) | collective-permute-done | bytes 147488 | tf_op jit(solution)/shard_map/ppermute | solution.py:406
  47.8 0.1 split.1
  47.9 0.6 collective-permute-start.15
  48.5 3.1 %backward.3 = (bf16[512,1024]{1,0:T(8,128)(2,1)S(1)}, bf16[512,1024]{1,0:T(8,128)(2,1)S(1)}) custom-call(bf16[512,576]{1,0:T(8,128)(2,1)S(1)} %turn.1.xt_ref, bf16[144,1024]{1,0:T(8,128)(2,1)S(1)} %join.3.refs_0_, bf16[144,1024]{1,0:T(8,128)(2,1)S(1)} %collective-permute-done.13.refs_2_.refs_1_, ...), custom_call_target="tpu_custom_call" | custom-call | flops 20000000000 | tf_op jit(solution)/shard_map/backward/pallas_call | solution.py:315
  51.6 0.6 collective-permute-start.17
  52.2 1.1 %finish.2 = (bf16[256,2048]{1,0:T(8,128)(2,1)}, bf16[256,2048]{1,0:T(8,128)(2,1)}) custom-call(bf16[512,1024]{1,0:T(8,128)(2,1)S(1)} %get-tuple-element.63.refs_4_.refs_0_, bf16[512,1024]{1,0:T(8,128)(2,1)S(1)} %collective-permute-done.16.refs_1_), custom_call_target="tpu_custom_call" | custom-call | tf_op jit(solution)/shard_map/finish/pallas_call | solution.py:351
  53.3 2.2 %collective-permute-done.15.got_ref = bf16[144,1024]{1,0:T(8,128)(2,1)S(1)} collective-permute-done((bf16[144,1024]{1,0:T(8,128)(2,1)S(1)}, bf16[144,1024]{1,0:T(8,128)(2,1)S(1)}, u32[]{:S(2)}, u32[]{:S(2)}) %collective-permute-start.15) | collective-permute-done | bytes 294944 | tf_op jit(solution)/shard_map/ppermute | solution.py:401
  55.5 1.0 %unpack.1 = bf16[128,1024]{1,0:T(8,128)(2,1)} custom-call(bf16[144,128]{1,0:T(8,128)(2,1)S(1)} %get-tuple-element.38.placer_ref, bf16[144,1024]{1,0:T(8,128)(2,1)S(1)} %get-tuple-element.64.mine_ref.refs_13_, bf16[144,1024]{1,0:T(8,128)(2,1)S(1)} %collective-permute-done.15.got_ref, bf16[256,2048]{1,0:T(8,128)(2,1)} %get-tuple-element.67.refs_0_.refs_2_), custom_call_target="tpu_custom_call" | custom-call | flops 20000000000 | tf_op jit(solution)/shard_map/unpack/pallas_call | solution.py:390
  56.5 1.1 %finish.3 = (bf16[256,2048]{1,0:T(8,128)(2,1)}, bf16[256,2048]{1,0:T(8,128)(2,1)}) custom-call(bf16[512,1024]{1,0:T(8,128)(2,1)S(1)} %get-tuple-element.68.refs_0_, bf16[512,1024]{1,0:T(8,128)(2,1)S(1)} %collective-permute-done.17.refs_1_, bf16[256,2048]{1,0:T(8,128)(2,1)} %get-tuple-element.67.refs_0_.refs_2_, ...), custom_call_target="tpu_custom_call", output_to_operand_aliasing={{0}: (2, {}), {1}: (3, {})} | custom-call | tf_op jit(solution)/shard_map/finish/pallas_call | solution.py:351
  (26 shorter events, 0.2 us)
Async XLA Ops:
  2.1 9.5 %collective-permute-start = (bf16[36,1024]{1,0:T(8,128)(2,1)S(1)}, bf16[36,1024]{1,0:T(8,128)(2,1)S(1)}, u32[]{:S(2)}, u32[]{:S(2)}) collective-permute-start(bf16[36,1024]{1,0:T(8,128)(2,1)S(1)} %get-tuple-element.39), channel_id=1, source_target_pairs={{0,6},{2,4},{4,2},{6,0},{1,7},{3,5},{5,3},{7,1},{8,14},{10,12},{12... | collective-permute-start | bytes 221192 | tf_op jit(solution)/shard_map/ppermute | solution.py:406
  7.2 11.2 %collective-permute-start.1 = (bf16[36,1024]{1,0:T(8,128)(2,1)S(1)}, bf16[36,1024]{1,0:T(8,128)(2,1)S(1)}, u32[]{:S(2)}, u32[]{:S(2)}) collective-permute-start(bf16[36,1024]{1,0:T(8,128)(2,1)S(1)} %get-tuple-element.40), channel_id=1, source_target_pairs={{0,4},{2,6},{4,0},{6,2},{1,5},{3,7},{5,1},{7,3},{8,12},{10,14},{12... | collective-permute-start | bytes 221192 | tf_op jit(solution)/shard_map/ppermute | solution.py:406
  7.2 11.2 %collective-permute-start.2 = (bf16[36,1024]{1,0:T(8,128)(2,1)S(1)}, bf16[36,1024]{1,0:T(8,128)(2,1)S(1)}, u32[]{:S(2)}, u32[]{:S(2)}) collective-permute-start(bf16[36,1024]{1,0:T(8,128)(2,1)S(1)} %get-tuple-element.41), channel_id=1, source_target_pairs={{0,2},{2,0},{4,6},{6,4},{1,3},{3,1},{5,7},{7,5},{8,10},{10,8},{12,... | collective-permute-start | bytes 221192 | tf_op jit(solution)/shard_map/ppermute | solution.py:406
  7.9 15.8 %collective-permute-start.8 = (bf16[36,1024]{1,0:T(8,128)(2,1)S(1)}, bf16[36,1024]{1,0:T(8,128)(2,1)S(1)}, u32[]{:S(2)}, u32[]{:S(2)}) collective-permute-start(bf16[36,1024]{1,0:T(8,128)(2,1)S(1)} %get-tuple-element.53), channel_id=1, source_target_pairs={{0,6},{2,4},{4,2},{6,0},{1,7},{3,5},{5,3},{7,1},{8,14},{10,12},{12... | collective-permute-start | bytes 221192 | tf_op jit(solution)/shard_map/ppermute | solution.py:406
  11.6 12.0 %collective-permute-start.9 = (bf16[36,1024]{1,0:T(8,128)(2,1)S(1)}, bf16[36,1024]{1,0:T(8,128)(2,1)S(1)}, u32[]{:S(2)}, u32[]{:S(2)}) collective-permute-start(bf16[36,1024]{1,0:T(8,128)(2,1)S(1)} %get-tuple-element.54), channel_id=1, source_target_pairs={{0,4},{2,6},{4,0},{6,2},{1,5},{3,7},{5,1},{7,3},{8,12},{10,14},{12... | collective-permute-start | bytes 221192 | tf_op jit(solution)/shard_map/ppermute | solution.py:406
  11.6 12.0 %collective-permute-start.10 = (bf16[36,1024]{1,0:T(8,128)(2,1)S(1)}, bf16[36,1024]{1,0:T(8,128)(2,1)S(1)}, u32[]{:S(2)}, u32[]{:S(2)}) collective-permute-start(bf16[36,1024]{1,0:T(8,128)(2,1)S(1)} %get-tuple-element.55), channel_id=1, source_target_pairs={{0,2},{2,0},{4,6},{6,4},{1,3},{3,1},{5,7},{7,5},{8,10},{10,8},{12,... | collective-permute-start | bytes 221192 | tf_op jit(solution)/shard_map/ppermute | solution.py:406
  15.2 6.2 %copy-start = (bf16[1024,2048]{1,0:T(8,128)(2,1)S(1)}, bf16[1024,2048]{1,0:T(8,128)(2,1)}, u32[]{:S(2)}) copy-start(bf16[1024,2048]{1,0:T(8,128)(2,1)} %refs_1_.5) | copy-start | bytes 12582916
  15.2 6.2 %copy-start.1 = (bf16[1024,2048]{1,0:T(8,128)(2,1)S(1)}, bf16[1024,2048]{1,0:T(8,128)(2,1)}, u32[]{:S(2)}) copy-start(bf16[1024,2048]{1,0:T(8,128)(2,1)} %refs_2_.7) | copy-start | bytes 12582916
  18.5 8.9 %collective-permute-start.3 = (bf16[144,1024]{1,0:T(8,128)(2,1)S(1)}, bf16[144,1024]{1,0:T(8,128)(2,1)S(1)}, u32[]{:S(2)}, u32[]{:S(2)}) collective-permute-start(bf16[144,1024]{1,0:T(8,128)(2,1)S(1)} %join.2.refs_0_.refs_4_), channel_id=1, source_target_pairs={{0,16},{16,0},{1,17},{17,1},{2,18},{18,2},{3,19},{19,3},{4,20},{20... | collective-permute-start | bytes 884744 | tf_op jit(solution)/shard_map/ppermute | solution.py:401
  19.9 9.1 %collective-permute-start.4 = (bf16[144,1024]{1,0:T(8,128)(2,1)S(1)}, bf16[144,1024]{1,0:T(8,128)(2,1)S(1)}, u32[]{:S(2)}, u32[]{:S(2)}) collective-permute-start(bf16[144,1024]{1,0:T(8,128)(2,1)S(1)} %join.2.refs_0_.refs_4_), channel_id=1, source_target_pairs={{0,1},{1,0},{2,3},{3,2},{4,5},{5,4},{6,7},{7,6},{8,9},{9,8},{10,11... | collective-permute-start | bytes 884744 | tf_op jit(solution)/shard_map/ppermute | solution.py:401
  23.7 7.8 %collective-permute-start.11 = (bf16[144,1024]{1,0:T(8,128)(2,1)S(1)}, bf16[144,1024]{1,0:T(8,128)(2,1)S(1)}, u32[]{:S(2)}, u32[]{:S(2)}) collective-permute-start(bf16[144,1024]{1,0:T(8,128)(2,1)S(1)} %join.3.refs_0_), channel_id=1, source_target_pairs={{0,16},{16,0},{1,17},{17,1},{2,18},{18,2},{3,19},{19,3},{4,20},{20... | collective-permute-start | bytes 884744 | tf_op jit(solution)/shard_map/ppermute | solution.py:401
  24.3 8.7 %collective-permute-start.13 = (bf16[144,1024]{1,0:T(8,128)(2,1)S(1)}, bf16[144,1024]{1,0:T(8,128)(2,1)S(1)}, u32[]{:S(2)}, u32[]{:S(2)}) collective-permute-start(bf16[144,1024]{1,0:T(8,128)(2,1)S(1)} %join.3.refs_0_), channel_id=1, source_target_pairs={{0,1},{1,0},{2,3},{3,2},{4,5},{5,4},{6,7},{7,6},{8,9},{9,8},{10,11... | collective-permute-start | bytes 884744 | tf_op jit(solution)/shard_map/ppermute | solution.py:401
  31.6 7.4 %collective-permute-start.12 = (bf16[144,1024]{1,0:T(8,128)(2,1)S(1)}, bf16[144,1024]{1,0:T(8,128)(2,1)S(1)}, u32[]{:S(2)}, u32[]{:S(2)}) collective-permute-start(bf16[144,1024]{1,0:T(8,128)(2,1)S(1)} %relay.2.refs_1_), channel_id=1, source_target_pairs={{0,16},{16,0},{1,17},{17,1},{2,18},{18,2},{3,19},{19,3},{4,20},{20... | collective-permute-start | bytes 884744 | tf_op jit(solution)/shard_map/ppermute | solution.py:401
  33.0 7.8 %collective-permute-start.14 = (bf16[144,1024]{1,0:T(8,128)(2,1)S(1)}, bf16[144,1024]{1,0:T(8,128)(2,1)S(1)}, u32[]{:S(2)}, u32[]{:S(2)}) collective-permute-start(bf16[144,1024]{1,0:T(8,128)(2,1)S(1)} %relay.3), channel_id=1, source_target_pairs={{0,1},{1,0},{2,3},{3,2},{4,5},{5,4},{6,7},{7,6},{8,9},{9,8},{10,11... | collective-permute-start | bytes 884744 | tf_op jit(solution)/shard_map/ppermute | solution.py:401
  34.6 9.6 %collective-permute-start.5 = (bf16[72,1024]{1,0:T(8,128)(2,1)S(1)}, bf16[72,1024]{1,0:T(8,128)(2,1)S(1)}, u32[]{:S(2)}, u32[]{:S(2)}) collective-permute-start(bf16[72,1024]{1,0:T(8,128)(2,1)S(1)} %get-tuple-element.48), channel_id=1, source_target_pairs={{0,6},{2,4},{4,2},{6,0},{1,7},{3,5},{5,3},{7,1},{8,14},{10,12},{12... | collective-permute-start | bytes 442376 | tf_op jit(solution)/shard_map/ppermute | solution.py:406
  37.8 10.0 %collective-permute-start.6 = (bf16[72,1024]{1,0:T(8,128)(2,1)S(1)}, bf16[72,1024]{1,0:T(8,128)(2,1)S(1)}, u32[]{:S(2)}, u32[]{:S(2)}) collective-permute-start(bf16[72,1024]{1,0:T(8,128)(2,1)S(1)} %get-tuple-element.49), channel_id=1, source_target_pairs={{0,4},{2,6},{4,0},{6,2},{1,5},{3,7},{5,1},{7,3},{8,12},{10,14},{12... | collective-permute-start | bytes 442376 | tf_op jit(solution)/shard_map/ppermute | solution.py:406
  37.8 10.0 %collective-permute-start.7 = (bf16[72,1024]{1,0:T(8,128)(2,1)S(1)}, bf16[72,1024]{1,0:T(8,128)(2,1)S(1)}, u32[]{:S(2)}, u32[]{:S(2)}) collective-permute-start(bf16[72,1024]{1,0:T(8,128)(2,1)S(1)} %get-tuple-element.50), channel_id=1, source_target_pairs={{0,2},{2,0},{4,6},{6,4},{1,3},{3,1},{5,7},{7,5},{8,10},{10,8},{12,... | collective-permute-start | bytes 442376 | tf_op jit(solution)/shard_map/ppermute | solution.py:406
  47.9 7.6 %collective-permute-start.15 = (bf16[144,1024]{1,0:T(8,128)(2,1)S(1)}, bf16[144,1024]{1,0:T(8,128)(2,1)S(1)}, u32[]{:S(2)}, u32[]{:S(2)}) collective-permute-start(bf16[144,1024]{1,0:T(8,128)(2,1)S(1)} %get-tuple-element.65), channel_id=1, source_target_pairs={{0,1},{1,0},{2,3},{3,2},{4,5},{5,4},{6,7},{7,6},{8,9},{9,8},{10,11... | collective-permute-start | bytes 884744 | tf_op jit(solution)/shard_map/ppermute | solution.py:401
  48.5 3.7 %collective-permute-start.16 = (bf16[512,1024]{1,0:T(8,128)(2,1)S(1)}, bf16[512,1024]{1,0:T(8,128)(2,1)S(1)}, u32[]{:S(2)}, u32[]{:S(2)}) collective-permute-start(bf16[512,1024]{1,0:T(8,128)(2,1)S(1)} %get-tuple-element.66), channel_id=1, source_target_pairs={{0,8},{8,0},{1,9},{9,1},{2,10},{10,2},{3,11},{11,3},{4,12},{12,4},... | collective-permute-start | bytes 3145736 | tf_op jit(solution)/shard_map/ppermute | solution.py:401
  51.6 4.9 %collective-permute-start.17 = (bf16[512,1024]{1,0:T(8,128)(2,1)S(1)}, bf16[512,1024]{1,0:T(8,128)(2,1)S(1)}, u32[]{:S(2)}, u32[]{:S(2)}) collective-permute-start(bf16[512,1024]{1,0:T(8,128)(2,1)S(1)} %get-tuple-element.69), channel_id=1, source_target_pairs={{0,8},{8,0},{1,9},{9,1},{2,10},{10,2},{3,11},{11,3},{4,12},{12,4},... | collective-permute-start | bytes 3145736 | tf_op jit(solution)/shard_map/ppermute | solution.py:401

commit v12 on v11

--- a/solution.py
+++ b/solution.py
@@ -10,8 +10,8 @@
 
 EXPERTS = 4
 CAP = 36
-STRIP = 1024
-PAIR = 2 * STRIP
+WIDE = 1024
+STRIP = 512
 SLICE = 256
 MIB = 1024 * 1024
 LARGE = pltpu.CompilerParams(vmem_limit_bytes=16 * MIB)
@@ -94,7 +94,7 @@
 
 
 def join_kernel(*refs):
-    refs[-1][...] = stacked(refs[EXPERTS - 1 :: -1]).astype(BF16)
+    refs[-1][...] = stacked(refs[-2 : -2 - EXPERTS : -1]).astype(BF16)
 
 
 def join(blocks, earlier=()):
@@ -102,11 +102,11 @@
     return pl.pallas_call(
         join_kernel,
         out_shape=jax.ShapeDtypeStruct((EXPERTS * CAP, width), BF16),
-        in_specs=[HERE] * EXPERTS + [ANYWHERE] * len(earlier),
+        in_specs=[ANYWHERE] * len(earlier) + [HERE] * EXPERTS,
         compiler_params=SMALL,
         cost_estimate=CHEAP,
         name="join",
-    )(*blocks[::-1], *earlier)
+    )(*earlier, *blocks[::-1])
 
 
 def relay_kernel(n, *refs):
@@ -185,10 +185,10 @@
         x_ref = refs.pop(0)
         for i in range(n):
             x_ref[i * part : (i + 1) * part, :] = xs[i][...]
-    steps = wg_ref.shape[1] // PAIR
+    steps = wg_ref.shape[1] // (2 * WIDE)
 
     def copies(j):
-        cols = pl.ds(pl.multiple_of(j * PAIR, PAIR), PAIR)
+        cols = pl.ds(pl.multiple_of(j * (2 * WIDE), (2 * WIDE)), (2 * WIDE))
         return [
             pltpu.make_async_copy(source.at[:, cols], target.at[:, cols], sems.at[j, i])
             for i, (source, target) in enumerate(zip(sources, (wg_ref, wu_ref)))
@@ -206,8 +206,8 @@
         if fetch:
             for copy in copies(j):
                 copy.wait()
-        for i in range(PAIR // STRIP):
-            cols = pl.ds(pl.multiple_of(j * PAIR + i * STRIP, STRIP), STRIP)
+        for i in range(2):
+            cols = pl.ds(pl.multiple_of(j * (2 * WIDE) + i * WIDE, WIDE), WIDE)
             gate = jnp.dot(x_ref[...], wg_ref[:, cols], preferred_element_type=F32)
             up = jnp.dot(x_ref[...], wu_ref[:, cols], preferred_element_type=F32)
             act, slope = silu_parts(gate)
@@ -246,7 +246,7 @@
         + [HERE] * (down + pair),
         scratch_shapes=[pltpu.VMEM((part, width), F32)] * down
         + [pltpu.VMEM((rows, width), BF16)] * (n > 1)
-        + [pltpu.SemaphoreType.DMA((cols // PAIR, 2))] * fetch,
+        + [pltpu.SemaphoreType.DMA((cols // (2 * WIDE), 2))] * fetch,
         compiler_params=LARGE,
         cost_estimate=CHEAP,
         name="forward" + "_fetch" * fetch + "_down" * down,
@@ -272,7 +272,7 @@
         ),
         out_shape=jax.ShapeDtypeStruct((2 * share, rows), BF16),
         compiler_params=SMALL,
-        cost_estimate=CHEAP,
+        cost_estimate=DEAR,
         name="turn",
     )(own, sib, *xs, *xs)
 
@@ -297,14 +297,7 @@
             own_ref[row : row + share, here] = total[:share]
             sib_ref[row : row + share, here] = total[share:]
 
-    pairs = own_ref.shape[1] // PAIR
-
-    @pl.loop(0, pairs)
-    def _(j):
-        for i in range(PAIR // STRIP):
-            strip(j * PAIR + i * STRIP)
-
-    for start in range(pairs * PAIR, own_ref.shape[1], STRIP):
+    for start in range(0, own_ref.shape[1], STRIP):
         strip(start)
 
 
@@ -362,7 +355,7 @@
 
 
 def split_kernel(*refs):
-    blocks = [r[...].astype(F32) for r in refs[EXPERTS - 1 :: -1]]
+    blocks = [r[...].astype(F32) for r in refs[:EXPERTS]]
     refs[-2][...] = jnp.concatenate([b[:CAP] for b in blocks], axis=0).astype(BF16)
     refs[-1][...] = jnp.concatenate([b[CAP:] for b in blocks], axis=0).astype(BF16)
 
@@ -376,7 +369,7 @@
         compiler_params=SMALL,
         cost_estimate=CHEAP,
         name="split",
-    )(*blocks[::-1], *earlier)
+    )(*blocks, *earlier)
 
 
 def unpack_kernel(placer_ref, mine_ref, got_ref, *refs):
@@ -421,32 +414,33 @@
     placer, *blocks = pack(scalars, archetype.reshape(1, tokens), designs, cotangent)
     wd, wdt = flip(after([w_down], [placer])[0])
 
-    moved = across_planes(blocks[:EXPERTS])
-    x_own = join(moved, [wdt])
+    x_own = join(across_planes(blocks[:EXPERTS]), [wdt])
     x_far, x_near = swap(x_own, "far"), swap(x_own, "half")
-    moved = across_planes(blocks[EXPERTS:])
+    moved = across_planes(relay(blocks[EXPERTS:], [x_own]))
 
     wg, wu = w_gate, w_up
     act0, coef0, share_own = forward([x_own], wg, wu, wd)
-    g_own = join(moved, [act0])
+    (x_pass,) = relay([x_near], [act0, x_far])
+    x_corner = swap(x_pass, "far")
+    act1, coef1, *shares = forward([x_near], wg, wu, wd, other=share_own, earlier=[x_pass])
+    g_own = join(moved, [act1])
     g_far, g_near = swap(g_own, "far"), swap(g_own, "half")
-    act2, coef2 = forward([x_far], wg, wu)
-    act1, coef1, *shares = forward([x_near], wg, wu, wd, other=share_own, earlier=[act2])
-    (x_pass,) = relay([x_near], [mark(act1), g_far])
-    (g_pass,) = relay([g_far], [x_pass, g_near])
-    x_corner, g_corner = swap(x_pass, "far"), swap(g_pass, "half")
     returned = across_planes(shares)
-    act3, coef3 = forward([x_corner], wg, wu)
+    act2, coef2 = forward([x_far], wg, wu, earlier=[g_own])
+    act3, coef3 = forward([x_corner], wg, wu, earlier=[act2])
     xt = turn(*scalars[1:], [x_own, x_near, x_far, x_corner], share)
+    (g_pass,) = relay([g_far], [act3])
+    (g_pass,) = relay([g_pass], [g_near])
+    g_corner = swap(g_pass, "half")
 
     gs = [g_own, g_near, g_far, g_corner]
     acts, coefs = [act0, act1, act2, act3], [coef0, coef1, coef2, coef3]
     cols = w_down.shape[0]
     half = cols // 2
-    own0, sib0 = backward(xt, gs, acts, coefs, wdt, 0, half)
-    mine, theirs = split(returned, [own0])
+    mine, theirs = split(returned, [g_corner])
     got = swap(theirs, "half")
-    own1, sib1 = backward(xt, gs, acts, coefs, wdt, half, half, [mine])
+    own0, sib0 = backward(xt, gs, acts, coefs, wdt, 0, half, [mine])
+    own1, sib1 = backward(xt, gs, acts, coefs, wdt, half, half, [own0])
     got0, got1 = swap(sib0, "core"), swap(sib1, "core")
     held = finish([own0], [got0], (0,), cols)
     outputs = unpack(placer, mine, got, held[:1])

time: 57.9 us -> 57.5 us (level)
  starting transfers between devices: 25.8 us -> 23.9 us
  waiting for transfers between devices: 8.88 us -> 10.2 us
    ppermute x9, starting transfers between devices: 17.5 us -> 15.1 us  [across_planes(): lax.ppermute(blocks[k], 'arch', [(i, i ^ k) for i in range(EXPERTS)])]
    ppermute x9, waiting for transfers between devices: 3.97 us -> 5.89 us  [across_planes(): lax.ppermute(blocks[k], 'arch', [(i, i ^ k) for i in range(EXPERTS)])]
    ppermute x9, waiting for transfers between devices: 4.91 us -> 4.27 us  [swap(): return lax.ppermute(value, axis, [(0, 1), (1, 0)])]
  transfers between devices with their start and end apart: 18 -> 18, of which waited for: 5 -> 4; matrix products, arithmetic and copies ran while one was open for 0% -> 0% of each run, Pallas kernels for 34% -> 34%
where the time goes in v12:
time: 57.5 us; the launch traced here: 57.3 us
  starting transfers between devices  23.9 us (42%)
  Pallas kernels  22.3 us (39%)
  waiting for transfers between devices  10.2 us (18%)
  between operations  1.03 us (2%)
    ppermute x9, starting transfers between devices, across_planes(): lax.ppermute(blocks[k], 'arch', [(i, i ^ k) for i in range(EXPERTS)])  15.1 us
    ppermute x9, starting transfers between devices, swap(): return lax.ppermute(value, axis, [(0, 1), (1, 0)])  8.74 us
    pallas_call x4, Pallas kernels, forward(): pl.pallas_call(functools.partial(forward_kernel, n, fetch, down, pair, le...  7.62 us
    pallas_call x2, Pallas kernels, backward(): pl.pallas_call(functools.partial(backward_kernel, first, counts), out_sha...  6.56 us
    ppermute x9, waiting for transfers between devices, across_planes(): lax.ppermute(blocks[k], 'arch', [(i, i ^ k) for i in range(EXPERTS)])  5.89 us
    ppermute x9, waiting for transfers between devices, swap(): return lax.ppermute(value, axis, [(0, 1), (1, 0)])  4.27 us
    pallas_call x1, Pallas kernels, flip(): pl.pallas_call(flip_kernel, out_shape=[pltpu.VMEM(value.shape, value.dtyp...  2.88 us
    pallas_call x2, Pallas kernels, finish(): pl.pallas_call(functools.partial(finish_kernel, spans, more), out_shape=[...  2.21 us
  transfers between devices with their start and end apart: 18, of which 4 were waited for; matrix products, arithmetic and copies ran while one was open for 0% of the time, Pallas kernels for 34%

profile of v12, /device:TPU:0, one launch (start us, length us, event | category | flops | bytes accessed | tf_op | source)
XLA Modules:
  0.0 57.3 jit_solution(16707770879147361619)
XLA Ops:
  0.6 1.5 %pack.1 = (bf16[144,128]{1,0:T(8,128)(2,1)S(1)}, bf16[36,1024]{1,0:T(8,128)(2,1)S(1)}, bf16[36,1024]{1,0:T(8,128)(2,1)S(1)}, bf16[36,1024]{1,0:T(8,128)(2,1)S(1)...) custom-call(s32[1]{0:T(128)} %bitcast.plane_ref, ...), custom_call_target="tpu_custom_call" | custom-call | tf_op jit(solution)/shard_map/pack/pallas_call | solution.py:79
  2.1 5.1 %collective-permute-start = (bf16[36,1024]{1,0:T(8,128)(2,1)S(1)}, bf16[36,1024]{1,0:T(8,128)(2,1)S(1)}, u32[]{:S(2)}, u32[]{:S(2)}) collective-permute-start(bf16[36,1024]{1,0:T(8,128)(2,1)S(1)} %get-tuple-element.45), channel_id=1, source_target_pairs={{0,6},{2,4},{4,2},{6,0},{1,7},{3,5},{5,3},{7,1},{8,14},{10,12},{12... | collective-permute-start | bytes 221192 | tf_op jit(solution)/shard_map/ppermute | solution.py:399
  7.2 0.6 %collective-permute-start.2 = (bf16[36,1024]{1,0:T(8,128)(2,1)S(1)}, bf16[36,1024]{1,0:T(8,128)(2,1)S(1)}, u32[]{:S(2)}, u32[]{:S(2)}) collective-permute-start(bf16[36,1024]{1,0:T(8,128)(2,1)S(1)} %get-tuple-element.47), channel_id=1, source_target_pairs={{0,2},{2,0},{4,6},{6,4},{1,3},{3,1},{5,7},{7,5},{8,10},{10,8},{12,... | collective-permute-start | bytes 221192 | tf_op jit(solution)/shard_map/ppermute | solution.py:399
  7.9 2.9 %flip.1 = (bf16[2048,1024]{1,0:T(8,128)(2,1)S(1)}, bf16[1024,2048]{1,0:T(8,128)(2,1)S(1)}) custom-call(bf16[2048,1024]{1,0:T(8,128)(2,1)} %source_ref), custom_call_target="tpu_custom_call" | custom-call | tf_op jit(solution)/shard_map/flip/pallas_call | solution.py:158
  10.8 3.3 %collective-permute-done.1.refs_2_ = bf16[36,1024]{1,0:T(8,128)(2,1)S(1)} collective-permute-done((bf16[36,1024]{1,0:T(8,128)(2,1)S(1)}, bf16[36,1024]{1,0:T(8,128)(2,1)S(1)}, u32[]{:S(2)}, u32[]{:S(2)}) %collective-permute-start.1) | collective-permute-done | bytes 73760 | tf_op jit(solution)/shard_map/ppermute | solution.py:399
  14.1 1.6 %collective-permute-start.4 = (bf16[144,1024]{1,0:T(8,128)(2,1)S(1)}, bf16[144,1024]{1,0:T(8,128)(2,1)S(1)}, u32[]{:S(2)}, u32[]{:S(2)}) collective-permute-start(bf16[144,1024]{1,0:T(8,128)(2,1)S(1)} %join.2.refs_0_.refs_4_), channel_id=1, source_target_pairs={{0,16},{16,0},{1,17},{17,1},{2,18},{18,2},{3,19},{19,3},{4,20},{20... | collective-permute-start | bytes 884744 | tf_op jit(solution)/shard_map/ppermute | solution.py:394
  15.7 1.5 %collective-permute-start.3 = (bf16[144,1024]{1,0:T(8,128)(2,1)S(1)}, bf16[144,1024]{1,0:T(8,128)(2,1)S(1)}, u32[]{:S(2)}, u32[]{:S(2)}) collective-permute-start(bf16[144,1024]{1,0:T(8,128)(2,1)S(1)} %join.2.refs_0_.refs_4_), channel_id=1, source_target_pairs={{0,1},{1,0},{2,3},{3,2},{4,5},{5,4},{6,7},{7,6},{8,9},{9,8},{10,11... | collective-permute-start | bytes 884744 | tf_op jit(solution)/shard_map/ppermute | solution.py:394
  17.2 2.8 %collective-permute-start.8 = (bf16[36,1024]{1,0:T(8,128)(2,1)S(1)}, bf16[36,1024]{1,0:T(8,128)(2,1)S(1)}, u32[]{:S(2)}, u32[]{:S(2)}) collective-permute-start(bf16[36,1024]{1,0:T(8,128)(2,1)S(1)} %get-tuple-element.61), channel_id=1, source_target_pairs={{0,6},{2,4},{4,2},{6,0},{1,7},{3,5},{5,3},{7,1},{8,14},{10,12},{12... | collective-permute-start | bytes 221192 | tf_op jit(solution)/shard_map/ppermute | solution.py:399
  20.0 1.7 %collective-permute-start.10 = (bf16[36,1024]{1,0:T(8,128)(2,1)S(1)}, bf16[36,1024]{1,0:T(8,128)(2,1)S(1)}, u32[]{:S(2)}, u32[]{:S(2)}) collective-permute-start(bf16[36,1024]{1,0:T(8,128)(2,1)S(1)} %get-tuple-element.63), channel_id=1, source_target_pairs={{0,2},{2,0},{4,6},{6,4},{1,3},{3,1},{5,7},{7,5},{8,10},{10,8},{12,... | collective-permute-start | bytes 221192 | tf_op jit(solution)/shard_map/ppermute | solution.py:399
  21.7 2.2 %forward_down.2 = (bf16[144,2048]{1,0:T(8,128)(2,1)S(1)}, bf16[144,2048]{1,0:T(8,128)(2,1)S(1)}, bf16[144,1024]{1,0:T(8,128)(2,1)S(1)}) custom-call(bf16[144,1024]{1,0:T(8,128)(2,1)S(1)} %join.2.refs_0_.refs_4_, bf16[1024,2048]{1,0:T(8,128)(2,1)S(1)} %copy-done, bf16[1024,2048]{1,0:T(8,128)(2,1)S(1)} %copy-done.1, ...), custom_call_target="tpu_custom_call" | custom-call | tf_op jit(solution)/shard_map/forward_down/pallas_call | solution.py:238
  24.0 0.6 %collective-permute-start.12 = (bf16[144,1024]{1,0:T(8,128)(2,1)S(1)}, bf16[144,1024]{1,0:T(8,128)(2,1)S(1)}, u32[]{:S(2)}, u32[]{:S(2)}) collective-permute-start(bf16[144,1024]{1,0:T(8,128)(2,1)S(1)} %relay.4.refs_0_), channel_id=1, source_target_pairs={{0,16},{16,0},{1,17},{17,1},{2,18},{18,2},{3,19},{19,3},{4,20},{20... | collective-permute-start | bytes 884744 | tf_op jit(solution)/shard_map/ppermute | solution.py:394
  24.6 2.2 %forward_down.3 = (bf16[144,2048]{1,0:T(8,128)(2,1)S(1)}, bf16[144,2048]{1,0:T(8,128)(2,1)S(1)}, bf16[72,1024]{1,0:T(8,128)(2,1)S(1)}, bf16[72,1024]{1,0:T(8,128...) custom-call(bf16[144,1024]{1,0:T(8,128)(2,1)S(1)} %relay.4.refs_0_, ...), custom_call_target="tpu_custom_call" | custom-call | tf_op jit(solution)/shard_map/forward_down/pallas_call | solution.py:238
  26.9 1.6 %collective-permute-start.11 = (bf16[144,1024]{1,0:T(8,128)(2,1)S(1)}, bf16[144,1024]{1,0:T(8,128)(2,1)S(1)}, u32[]{:S(2)}, u32[]{:S(2)}) collective-permute-start(bf16[144,1024]{1,0:T(8,128)(2,1)S(1)} %join.3.refs_0_), channel_id=1, source_target_pairs={{0,16},{16,0},{1,17},{17,1},{2,18},{18,2},{3,19},{19,3},{4,20},{20... | collective-permute-start | bytes 884744 | tf_op jit(solution)/shard_map/ppermute | solution.py:394
  28.5 1.3 %collective-permute-start.13 = (bf16[144,1024]{1,0:T(8,128)(2,1)S(1)}, bf16[144,1024]{1,0:T(8,128)(2,1)S(1)}, u32[]{:S(2)}, u32[]{:S(2)}) collective-permute-start(bf16[144,1024]{1,0:T(8,128)(2,1)S(1)} %join.3.refs_0_), channel_id=1, source_target_pairs={{0,1},{1,0},{2,3},{3,2},{4,5},{5,4},{6,7},{7,6},{8,9},{9,8},{10,11... | collective-permute-start | bytes 884744 | tf_op jit(solution)/shard_map/ppermute | solution.py:394
  29.8 0.1 collective-permute-start.5
  29.9 2.3 %collective-permute-start.6 = (bf16[72,1024]{1,0:T(8,128)(2,1)S(1)}, bf16[72,1024]{1,0:T(8,128)(2,1)S(1)}, u32[]{:S(2)}, u32[]{:S(2)}) collective-permute-start(bf16[72,1024]{1,0:T(8,128)(2,1)S(1)} %get-tuple-element.54), channel_id=1, source_target_pairs={{0,4},{2,6},{4,0},{6,2},{1,5},{3,7},{5,1},{7,3},{8,12},{10,14},{12... | collective-permute-start | bytes 442376 | tf_op jit(solution)/shard_map/ppermute | solution.py:399
  32.3 1.6 %forward.2 = (bf16[144,2048]{1,0:T(8,128)(2,1)S(1)}, bf16[144,2048]{1,0:T(8,128)(2,1)S(1)}) custom-call(bf16[144,1024]{1,0:T(8,128)(2,1)S(1)} %join.3.refs_0_, bf16[144,1024]{1,0:T(8,128)(2,1)S(1)} %collective-permute-done.4.refs_2_.refs_1_.refs_6_, bf16[1024,2048]{1,0:T(8,128)(2,1)S(1)} %copy-done, bf16[1024,2048]{1,0:T(8,128)(2,1)S(1)} %copy-done.1), custom_call_target="tpu_custom_call" | custom-call | tf_op jit(solution)/shard_map/forward/pallas_call | solution.py:238
  33.8 2.5 %collective-permute-start.7 = (bf16[72,1024]{1,0:T(8,128)(2,1)S(1)}, bf16[72,1024]{1,0:T(8,128)(2,1)S(1)}, u32[]{:S(2)}, u32[]{:S(2)}) collective-permute-start(bf16[72,1024]{1,0:T(8,128)(2,1)S(1)} %get-tuple-element.55), channel_id=1, source_target_pairs={{0,6},{2,4},{4,2},{6,0},{1,7},{3,5},{5,3},{7,1},{8,14},{10,12},{12... | collective-permute-start | bytes 442376 | tf_op jit(solution)/shard_map/ppermute | solution.py:399
  36.3 1.6 %forward.3 = (bf16[144,2048]{1,0:T(8,128)(2,1)S(1)}, bf16[144,2048]{1,0:T(8,128)(2,1)S(1)}) custom-call(bf16[144,2048]{1,0:T(8,128)(2,1)S(1)} %get-tuple-element.65.refs_0_.refs_6_, bf16[144,1024]{1,0:T(8,128)(2,1)S(1)} %collective-permute-done.12.refs_1_.refs_3_.refs_7_, bf16[1024,2048]{1,0:T(8,128)(2,1)S(1)} %copy-done, bf16[1024,2048]{1,0:T(8,128)(2,1)S(1)} %copy-done.1), custom_call_target="tpu_custom_call" | custom-call | tf_op jit(solution)/shard_map/forward/pallas_call | solution.py:238
  38.0 1.0 %collective-permute-start.14 = (bf16[144,1024]{1,0:T(8,128)(2,1)S(1)}, bf16[144,1024]{1,0:T(8,128)(2,1)S(1)}, u32[]{:S(2)}, u32[]{:S(2)}) collective-permute-start(bf16[144,1024]{1,0:T(8,128)(2,1)S(1)} %relay.7), channel_id=1, source_target_pairs={{0,1},{1,0},{2,3},{3,2},{4,5},{5,4},{6,7},{7,6},{8,9},{9,8},{10,11... | collective-permute-start | bytes 884744 | tf_op jit(solution)/shard_map/ppermute | solution.py:394
  39.0 0.2 turn.1.xt_ref
  39.2 2.6 %collective-permute-done.6.refs_2_ = bf16[72,1024]{1,0:T(8,128)(2,1)S(1)} collective-permute-done((bf16[72,1024]{1,0:T(8,128)(2,1)S(1)}, bf16[72,1024]{1,0:T(8,128)(2,1)S(1)}, u32[]{:S(2)}, u32[]{:S(2)}) %collective-permute-start.6) | collective-permute-done | bytes 147488 | tf_op jit(solution)/shard_map/ppermute | solution.py:399
  41.8 4.1 %collective-permute-done.14.refs_4_.refs_3_ = bf16[144,1024]{1,0:T(8,128)(2,1)S(1)} collective-permute-done((bf16[144,1024]{1,0:T(8,128)(2,1)S(1)}, bf16[144,1024]{1,0:T(8,128)(2,1)S(1)}, u32[]{:S(2)}, u32[]{:S(2)}) %collective-permute-start.14) | collective-permute-done | bytes 294944 | tf_op jit(solution)/shard_map/ppermute | solution.py:394
  45.9 0.1 split.1
  46.0 0.6 collective-permute-start.15
  46.6 3.4 %backward.2 = (bf16[512,1024]{1,0:T(8,128)(2,1)S(1)}, bf16[512,1024]{1,0:T(8,128)(2,1)S(1)}) custom-call(bf16[512,576]{1,0:T(8,128)(2,1)S(1)} %turn.1.xt_ref, bf16[144,1024]{1,0:T(8,128)(2,1)S(1)} %join.3.refs_0_, bf16[144,1024]{1,0:T(8,128)(2,1)S(1)} %collective-permute-done.13.refs_1_, bf16[144,1024]{1,0:T(8,128)(2,1)S(1)} %collective-permute-done.11.refs_0_.refs_2_, ...), custom_call_target="tpu_custom_call" | custom-call | flops 20000000000 | tf_op jit(solution)/shard_map/backward/pallas_call | solution.py:308
  50.0 3.2 %backward.3 = (bf16[512,1024]{1,0:T(8,128)(2,1)S(1)}, bf16[512,1024]{1,0:T(8,128)(2,1)S(1)}) custom-call(bf16[512,576]{1,0:T(8,128)(2,1)S(1)} %turn.1.xt_ref, bf16[144,1024]{1,0:T(8,128)(2,1)S(1)} %join.3.refs_0_, bf16[144,1024]{1,0:T(8,128)(2,1)S(1)} %collective-permute-done.13.refs_1_, bf16[144,1024]{1,0:T(8,128)(2,1)S(1)} %collective-permute-done.11.refs_0_.refs_2_, ...), custom_call_target="tpu_custom_call" | custom-call | flops 20000000000 | tf_op jit(solution)/shard_map/backward/pallas_call | solution.py:308
  53.2 0.6 collective-permute-start.17
  53.8 1.1 %finish.2 = (bf16[256,2048]{1,0:T(8,128)(2,1)}, bf16[256,2048]{1,0:T(8,128)(2,1)}) custom-call(bf16[512,1024]{1,0:T(8,128)(2,1)S(1)} %get-tuple-element.73.refs_0_.refs_13_, bf16[512,1024]{1,0:T(8,128)(2,1)S(1)} %collective-permute-done.16.refs_1_), custom_call_target="tpu_custom_call" | custom-call | tf_op jit(solution)/shard_map/finish/pallas_call | solution.py:344
  54.9 1.0 %unpack.1 = bf16[128,1024]{1,0:T(8,128)(2,1)} custom-call(bf16[144,128]{1,0:T(8,128)(2,1)S(1)} %get-tuple-element.42.placer_ref, bf16[144,1024]{1,0:T(8,128)(2,1)S(1)} %get-tuple-element.67.refs_13_.mine_ref, bf16[144,1024]{1,0:T(8,128)(2,1)S(1)} %collective-permute-done.15.got_ref, bf16[256,2048]{1,0:T(8,128)(2,1)} %get-tuple-element.75.refs_0_.refs_2_), custom_call_target="tpu_custom_call" | custom-call | flops 20000000000 | tf_op jit(solution)/shard_map/unpack/pallas_call | solution.py:383
  56.0 0.1 collective-permute-done.17.refs_1_
  56.1 1.1 %finish.3 = (bf16[256,2048]{1,0:T(8,128)(2,1)}, bf16[256,2048]{1,0:T(8,128)(2,1)}) custom-call(bf16[512,1024]{1,0:T(8,128)(2,1)S(1)} %get-tuple-element.76.refs_0_, bf16[512,1024]{1,0:T(8,128)(2,1)S(1)} %collective-permute-done.17.refs_1_, bf16[256,2048]{1,0:T(8,128)(2,1)} %get-tuple-element.75.refs_0_.refs_2_, ...), custom_call_target="tpu_custom_call", output_to_operand_aliasing={{0}: (2, {}), {1}: (3, {})} | custom-call | tf_op jit(solution)/shard_map/finish/pallas_call | solution.py:344
  (27 shorter events, 0.3 us)
Async XLA Ops:
  2.1 8.7 %collective-permute-start = (bf16[36,1024]{1,0:T(8,128)(2,1)S(1)}, bf16[36,1024]{1,0:T(8,128)(2,1)S(1)}, u32[]{:S(2)}, u32[]{:S(2)}) collective-permute-start(bf16[36,1024]{1,0:T(8,128)(2,1)S(1)} %get-tuple-element.45), channel_id=1, source_target_pairs={{0,6},{2,4},{4,2},{6,0},{1,7},{3,5},{5,3},{7,1},{8,14},{10,12},{12... | collective-permute-start | bytes 221192 | tf_op jit(solution)/shard_map/ppermute | solution.py:399
  7.2 6.9 %collective-permute-start.1 = (bf16[36,1024]{1,0:T(8,128)(2,1)S(1)}, bf16[36,1024]{1,0:T(8,128)(2,1)S(1)}, u32[]{:S(2)}, u32[]{:S(2)}) collective-permute-start(bf16[36,1024]{1,0:T(8,128)(2,1)S(1)} %get-tuple-element.46), channel_id=1, source_target_pairs={{0,4},{2,6},{4,0},{6,2},{1,5},{3,7},{5,1},{7,3},{8,12},{10,14},{12... | collective-permute-start | bytes 221192 | tf_op jit(solution)/shard_map/ppermute | solution.py:399
  7.2 6.9 %collective-permute-start.2 = (bf16[36,1024]{1,0:T(8,128)(2,1)S(1)}, bf16[36,1024]{1,0:T(8,128)(2,1)S(1)}, u32[]{:S(2)}, u32[]{:S(2)}) collective-permute-start(bf16[36,1024]{1,0:T(8,128)(2,1)S(1)} %get-tuple-element.47), channel_id=1, source_target_pairs={{0,2},{2,0},{4,6},{6,4},{1,3},{3,1},{5,7},{7,5},{8,10},{10,8},{12,... | collective-permute-start | bytes 221192 | tf_op jit(solution)/shard_map/ppermute | solution.py:399
  7.9 13.8 %copy-start = (bf16[1024,2048]{1,0:T(8,128)(2,1)S(1)}, bf16[1024,2048]{1,0:T(8,128)(2,1)}, u32[]{:S(2)}) copy-start(bf16[1024,2048]{1,0:T(8,128)(2,1)} %refs_2_.7) | copy-start | bytes 12582916
  7.9 13.8 %copy-start.1 = (bf16[1024,2048]{1,0:T(8,128)(2,1)S(1)}, bf16[1024,2048]{1,0:T(8,128)(2,1)}, u32[]{:S(2)}) copy-start(bf16[1024,2048]{1,0:T(8,128)(2,1)} %refs_3_.5) | copy-start | bytes 12582916
  14.1 9.8 %collective-permute-start.4 = (bf16[144,1024]{1,0:T(8,128)(2,1)S(1)}, bf16[144,1024]{1,0:T(8,128)(2,1)S(1)}, u32[]{:S(2)}, u32[]{:S(2)}) collective-permute-start(bf16[144,1024]{1,0:T(8,128)(2,1)S(1)} %join.2.refs_0_.refs_4_), channel_id=1, source_target_pairs={{0,16},{16,0},{1,17},{17,1},{2,18},{18,2},{3,19},{19,3},{4,20},{20... | collective-permute-start | bytes 884744 | tf_op jit(solution)/shard_map/ppermute | solution.py:394
  15.7 8.3 %collective-permute-start.3 = (bf16[144,1024]{1,0:T(8,128)(2,1)S(1)}, bf16[144,1024]{1,0:T(8,128)(2,1)S(1)}, u32[]{:S(2)}, u32[]{:S(2)}) collective-permute-start(bf16[144,1024]{1,0:T(8,128)(2,1)S(1)} %join.2.refs_0_.refs_4_), channel_id=1, source_target_pairs={{0,1},{1,0},{2,3},{3,2},{4,5},{5,4},{6,7},{7,6},{8,9},{9,8},{10,11... | collective-permute-start | bytes 884744 | tf_op jit(solution)/shard_map/ppermute | solution.py:394
  17.2 9.6 %collective-permute-start.8 = (bf16[36,1024]{1,0:T(8,128)(2,1)S(1)}, bf16[36,1024]{1,0:T(8,128)(2,1)S(1)}, u32[]{:S(2)}, u32[]{:S(2)}) collective-permute-start(bf16[36,1024]{1,0:T(8,128)(2,1)S(1)} %get-tuple-element.61), channel_id=1, source_target_pairs={{0,6},{2,4},{4,2},{6,0},{1,7},{3,5},{5,3},{7,1},{8,14},{10,12},{12... | collective-permute-start | bytes 221192 | tf_op jit(solution)/shard_map/ppermute | solution.py:399
  20.0 6.8 %collective-permute-start.9 = (bf16[36,1024]{1,0:T(8,128)(2,1)S(1)}, bf16[36,1024]{1,0:T(8,128)(2,1)S(1)}, u32[]{:S(2)}, u32[]{:S(2)}) collective-permute-start(bf16[36,1024]{1,0:T(8,128)(2,1)S(1)} %get-tuple-element.62), channel_id=1, source_target_pairs={{0,4},{2,6},{4,0},{6,2},{1,5},{3,7},{5,1},{7,3},{8,12},{10,14},{12... | collective-permute-start | bytes 221192 | tf_op jit(solution)/shard_map/ppermute | solution.py:399
  20.0 6.9 %collective-permute-start.10 = (bf16[36,1024]{1,0:T(8,128)(2,1)S(1)}, bf16[36,1024]{1,0:T(8,128)(2,1)S(1)}, u32[]{:S(2)}, u32[]{:S(2)}) collective-permute-start(bf16[36,1024]{1,0:T(8,128)(2,1)S(1)} %get-tuple-element.63), channel_id=1, source_target_pairs={{0,2},{2,0},{4,6},{6,4},{1,3},{3,1},{5,7},{7,5},{8,10},{10,8},{12,... | collective-permute-start | bytes 221192 | tf_op jit(solution)/shard_map/ppermute | solution.py:399
  24.0 9.9 %collective-permute-start.12 = (bf16[144,1024]{1,0:T(8,128)(2,1)S(1)}, bf16[144,1024]{1,0:T(8,128)(2,1)S(1)}, u32[]{:S(2)}, u32[]{:S(2)}) collective-permute-start(bf16[144,1024]{1,0:T(8,128)(2,1)S(1)} %relay.4.refs_0_), channel_id=1, source_target_pairs={{0,16},{16,0},{1,17},{17,1},{2,18},{18,2},{3,19},{19,3},{4,20},{20... | collective-permute-start | bytes 884744 | tf_op jit(solution)/shard_map/ppermute | solution.py:394
  26.9 11.0 %collective-permute-start.11 = (bf16[144,1024]{1,0:T(8,128)(2,1)S(1)}, bf16[144,1024]{1,0:T(8,128)(2,1)S(1)}, u32[]{:S(2)}, u32[]{:S(2)}) collective-permute-start(bf16[144,1024]{1,0:T(8,128)(2,1)S(1)} %join.3.refs_0_), channel_id=1, source_target_pairs={{0,16},{16,0},{1,17},{17,1},{2,18},{18,2},{3,19},{19,3},{4,20},{20... | collective-permute-start | bytes 884744 | tf_op jit(solution)/shard_map/ppermute | solution.py:394
  28.5 9.5 %collective-permute-start.13 = (bf16[144,1024]{1,0:T(8,128)(2,1)S(1)}, bf16[144,1024]{1,0:T(8,128)(2,1)S(1)}, u32[]{:S(2)}, u32[]{:S(2)}) collective-permute-start(bf16[144,1024]{1,0:T(8,128)(2,1)S(1)} %join.3.refs_0_), channel_id=1, source_target_pairs={{0,1},{1,0},{2,3},{3,2},{4,5},{5,4},{6,7},{7,6},{8,9},{9,8},{10,11... | collective-permute-start | bytes 884744 | tf_op jit(solution)/shard_map/ppermute | solution.py:394
  29.8 9.4 %collective-permute-start.5 = (bf16[72,1024]{1,0:T(8,128)(2,1)S(1)}, bf16[72,1024]{1,0:T(8,128)(2,1)S(1)}, u32[]{:S(2)}, u32[]{:S(2)}) collective-permute-start(bf16[72,1024]{1,0:T(8,128)(2,1)S(1)} %get-tuple-element.53), channel_id=1, source_target_pairs={{0,2},{2,0},{4,6},{6,4},{1,3},{3,1},{5,7},{7,5},{8,10},{10,8},{12,... | collective-permute-start | bytes 442376 | tf_op jit(solution)/shard_map/ppermute | solution.py:399
  29.9 11.9 %collective-permute-start.6 = (bf16[72,1024]{1,0:T(8,128)(2,1)S(1)}, bf16[72,1024]{1,0:T(8,128)(2,1)S(1)}, u32[]{:S(2)}, u32[]{:S(2)}) collective-permute-start(bf16[72,1024]{1,0:T(8,128)(2,1)S(1)} %get-tuple-element.54), channel_id=1, source_target_pairs={{0,4},{2,6},{4,0},{6,2},{1,5},{3,7},{5,1},{7,3},{8,12},{10,14},{12... | collective-permute-start | bytes 442376 | tf_op jit(solution)/shard_map/ppermute | solution.py:399
  33.8 8.0 %collective-permute-start.7 = (bf16[72,1024]{1,0:T(8,128)(2,1)S(1)}, bf16[72,1024]{1,0:T(8,128)(2,1)S(1)}, u32[]{:S(2)}, u32[]{:S(2)}) collective-permute-start(bf16[72,1024]{1,0:T(8,128)(2,1)S(1)} %get-tuple-element.55), channel_id=1, source_target_pairs={{0,6},{2,4},{4,2},{6,0},{1,7},{3,5},{5,3},{7,1},{8,14},{10,12},{12... | collective-permute-start | bytes 442376 | tf_op jit(solution)/shard_map/ppermute | solution.py:399
  38.0 8.0 %collective-permute-start.14 = (bf16[144,1024]{1,0:T(8,128)(2,1)S(1)}, bf16[144,1024]{1,0:T(8,128)(2,1)S(1)}, u32[]{:S(2)}, u32[]{:S(2)}) collective-permute-start(bf16[144,1024]{1,0:T(8,128)(2,1)S(1)} %relay.7), channel_id=1, source_target_pairs={{0,1},{1,0},{2,3},{3,2},{4,5},{5,4},{6,7},{7,6},{8,9},{9,8},{10,11... | collective-permute-start | bytes 884744 | tf_op jit(solution)/shard_map/ppermute | solution.py:394
  46.0 8.9 %collective-permute-start.15 = (bf16[144,1024]{1,0:T(8,128)(2,1)S(1)}, bf16[144,1024]{1,0:T(8,128)(2,1)S(1)}, u32[]{:S(2)}, u32[]{:S(2)}) collective-permute-start(bf16[144,1024]{1,0:T(8,128)(2,1)S(1)} %get-tuple-element.68), channel_id=1, source_target_pairs={{0,1},{1,0},{2,3},{3,2},{4,5},{5,4},{6,7},{7,6},{8,9},{9,8},{10,11... | collective-permute-start | bytes 884744 | tf_op jit(solution)/shard_map/ppermute | solution.py:394
  50.0 3.8 %collective-permute-start.16 = (bf16[512,1024]{1,0:T(8,128)(2,1)S(1)}, bf16[512,1024]{1,0:T(8,128)(2,1)S(1)}, u32[]{:S(2)}, u32[]{:S(2)}) collective-permute-start(bf16[512,1024]{1,0:T(8,128)(2,1)S(1)} %get-tuple-element.74), channel_id=1, source_target_pairs={{0,8},{8,0},{1,9},{9,1},{2,10},{10,2},{3,11},{11,3},{4,12},{12,4},... | collective-permute-start | bytes 3145736 | tf_op jit(solution)/shard_map/ppermute | solution.py:394
  53.2 2.8 %collective-permute-start.17 = (bf16[512,1024]{1,0:T(8,128)(2,1)S(1)}, bf16[512,1024]{1,0:T(8,128)(2,1)S(1)}, u32[]{:S(2)}, u32[]{:S(2)}) collective-permute-start(bf16[512,1024]{1,0:T(8,128)(2,1)S(1)} %get-tuple-element.77), channel_id=1, source_target_pairs={{0,8},{8,0},{1,9},{9,1},{2,10},{10,2},{3,11},{11,3},{4,12},{12,4},... | collective-permute-start | bytes 3145736 | tf_op jit(solution)/shard_map/ppermute | solution.py:394

commit v13 on v12

--- a/solution.py
+++ b/solution.py
@@ -272,7 +272,7 @@
         ),
         out_shape=jax.ShapeDtypeStruct((2 * share, rows), BF16),
         compiler_params=SMALL,
-        cost_estimate=DEAR,
+        cost_estimate=CHEAP,
         name="turn",
     )(own, sib, *xs, *xs)
 
@@ -414,37 +414,35 @@
     placer, *blocks = pack(scalars, archetype.reshape(1, tokens), designs, cotangent)
     wd, wdt = flip(after([w_down], [placer])[0])
 
-    x_own = join(across_planes(blocks[:EXPERTS]), [wdt])
+    x_own = join(across_planes(blocks[:EXPERTS]))
+    moved = across_planes(relay(blocks[EXPERTS:], [wdt]))
     x_far, x_near = swap(x_own, "far"), swap(x_own, "half")
-    moved = across_planes(relay(blocks[EXPERTS:], [x_own]))
 
     wg, wu = w_gate, w_up
     act0, coef0, share_own = forward([x_own], wg, wu, wd)
-    (x_pass,) = relay([x_near], [act0, x_far])
-    x_corner = swap(x_pass, "far")
-    act1, coef1, *shares = forward([x_near], wg, wu, wd, other=share_own, earlier=[x_pass])
-    g_own = join(moved, [act1])
+    g_own = join(moved, [act0])
     g_far, g_near = swap(g_own, "far"), swap(g_own, "half")
+    act1, coef1, *shares = forward([x_near], wg, wu, wd, other=share_own)
+    act2, coef2 = forward([x_far], wg, wu, earlier=[act1])
+    (x_pass,) = relay([x_near], [mark(act2), g_far])
+    (g_pass,) = relay([g_far], [x_pass, g_near])
+    x_corner, g_corner = swap(x_pass, "far"), swap(g_pass, "half")
     returned = across_planes(shares)
-    act2, coef2 = forward([x_far], wg, wu, earlier=[g_own])
-    act3, coef3 = forward([x_corner], wg, wu, earlier=[act2])
+    act3, coef3 = forward([x_corner], wg, wu)
     xt = turn(*scalars[1:], [x_own, x_near, x_far, x_corner], share)
-    (g_pass,) = relay([g_far], [act3])
-    (g_pass,) = relay([g_pass], [g_near])
-    g_corner = swap(g_pass, "half")
 
     gs = [g_own, g_near, g_far, g_corner]
     acts, coefs = [act0, act1, act2, act3], [coef0, coef1, coef2, coef3]
     cols = w_down.shape[0]
-    half = cols // 2
-    mine, theirs = split(returned, [g_corner])
+    cut = 3 * cols // 4
+    own0, sib0 = backward(xt, gs, acts, coefs, wdt, 0, cut)
+    mine, theirs = split(returned, [own0])
     got = swap(theirs, "half")
-    own0, sib0 = backward(xt, gs, acts, coefs, wdt, 0, half, [mine])
-    own1, sib1 = backward(xt, gs, acts, coefs, wdt, half, half, [own0])
+    own1, sib1 = backward(xt, gs, acts, coefs, wdt, cut, cols - cut, [mine])
     got0, got1 = swap(sib0, "core"), swap(sib1, "core")
     held = finish([own0], [got0], (0,), cols)
     outputs = unpack(placer, mine, got, held[:1])
-    grad_gate, grad_up = finish([own1], [got1], (half,), cols, held)
+    grad_gate, grad_up = finish([own1], [got1], (cut,), cols, held)
     return outputs, grad_gate, grad_up
 
 

time: 57.5 us -> 55.3 us (0.962)
  waiting for transfers between devices: 10.2 us -> 6.75 us
  starting transfers between devices: 23.9 us -> 25.2 us
    ppermute x9, waiting for transfers between devices: 5.89 us -> 2.56 us  [across_planes(): lax.ppermute(blocks[k], 'arch', [(i, i ^ k) for i in range(EXPERTS)])]
    ppermute x9, starting transfers between devices: 8.74 us -> 10.6 us  [swap(): return lax.ppermute(value, axis, [(0, 1), (1, 0)])]
  transfers between devices with their start and end apart: 18 -> 18, of which waited for: 4 -> 5; matrix products, arithmetic and copies ran while one was open for 0% -> 0% of each run, Pallas kernels for 34% -> 36%
where the time goes in v13:
time: 55.3 us; the launch traced here: 55.1 us
  starting transfers between devices  25.2 us (46%)
  Pallas kernels  22.2 us (40%)
  waiting for transfers between devices  6.75 us (12%)
  between operations  0.97 us (2%)
    ppermute x9, starting transfers between devices, across_planes(): lax.ppermute(blocks[k], 'arch', [(i, i ^ k) for i in range(EXPERTS)])  14.6 us
    ppermute x9, starting transfers between devices, swap(): return lax.ppermute(value, axis, [(0, 1), (1, 0)])  10.6 us
    pallas_call x4, Pallas kernels, forward(): pl.pallas_call(functools.partial(forward_kernel, n, fetch, down, pair, le...  7.62 us
    pallas_call x2, Pallas kernels, backward(): pl.pallas_call(functools.partial(backward_kernel, first, counts), out_sha...  6.54 us
    ppermute x9, waiting for transfers between devices, swap(): return lax.ppermute(value, axis, [(0, 1), (1, 0)])  4.19 us
    pallas_call x1, Pallas kernels, flip(): pl.pallas_call(flip_kernel, out_shape=[pltpu.VMEM(value.shape, value.dtyp...  2.88 us
    ppermute x9, waiting for transfers between devices, across_planes(): lax.ppermute(blocks[k], 'arch', [(i, i ^ k) for i in range(EXPERTS)])  2.56 us
    pallas_call x2, Pallas kernels, finish(): pl.pallas_call(functools.partial(finish_kernel, spans, more), out_shape=[...  2.2 us
  transfers between devices with their start and end apart: 18, of which 5 were waited for; matrix products, arithmetic and copies ran while one was open for 0% of the time, Pallas kernels for 36%

profile of v13, /device:TPU:0, one launch (start us, length us, event | category | flops | bytes accessed | tf_op | source)
XLA Modules:
  0.0 55.1 jit_solution(11574407751988282557)
XLA Ops:
  0.6 1.5 %pack.1 = (bf16[144,128]{1,0:T(8,128)(2,1)S(1)}, bf16[36,1024]{1,0:T(8,128)(2,1)S(1)}, bf16[36,1024]{1,0:T(8,128)(2,1)S(1)}, bf16[36,1024]{1,0:T(8,128)(2,1)S(1)...) custom-call(s32[1]{0:T(128)} %bitcast.plane_ref, ...), custom_call_target="tpu_custom_call" | custom-call | tf_op jit(solution)/shard_map/pack/pallas_call | solution.py:79
  2.1 5.1 %collective-permute-start = (bf16[36,1024]{1,0:T(8,128)(2,1)S(1)}, bf16[36,1024]{1,0:T(8,128)(2,1)S(1)}, u32[]{:S(2)}, u32[]{:S(2)}) collective-permute-start(bf16[36,1024]{1,0:T(8,128)(2,1)S(1)} %get-tuple-element.43), channel_id=1, source_target_pairs={{0,6},{2,4},{4,2},{6,0},{1,7},{3,5},{5,3},{7,1},{8,14},{10,12},{12... | collective-permute-start | bytes 221192 | tf_op jit(solution)/shard_map/ppermute | solution.py:399
  7.2 0.6 %collective-permute-start.2 = (bf16[36,1024]{1,0:T(8,128)(2,1)S(1)}, bf16[36,1024]{1,0:T(8,128)(2,1)S(1)}, u32[]{:S(2)}, u32[]{:S(2)}) collective-permute-start(bf16[36,1024]{1,0:T(8,128)(2,1)S(1)} %get-tuple-element.45), channel_id=1, source_target_pairs={{0,2},{2,0},{4,6},{6,4},{1,3},{3,1},{5,7},{7,5},{8,10},{10,8},{12,... | collective-permute-start | bytes 221192 | tf_op jit(solution)/shard_map/ppermute | solution.py:399
  7.9 2.9 %flip.1 = (bf16[2048,1024]{1,0:T(8,128)(2,1)S(1)}, bf16[1024,2048]{1,0:T(8,128)(2,1)S(1)}) custom-call(bf16[2048,1024]{1,0:T(8,128)(2,1)} %source_ref), custom_call_target="tpu_custom_call" | custom-call | tf_op jit(solution)/shard_map/flip/pallas_call | solution.py:158
  10.8 3.8 %collective-permute-start.8 = (bf16[36,1024]{1,0:T(8,128)(2,1)S(1)}, bf16[36,1024]{1,0:T(8,128)(2,1)S(1)}, u32[]{:S(2)}, u32[]{:S(2)}) collective-permute-start(bf16[36,1024]{1,0:T(8,128)(2,1)S(1)} %get-tuple-element.62), channel_id=1, source_target_pairs={{0,6},{2,4},{4,2},{6,0},{1,7},{3,5},{5,3},{7,1},{8,14},{10,12},{12... | collective-permute-start | bytes 221192 | tf_op jit(solution)/shard_map/ppermute | solution.py:399
  14.6 0.6 %collective-permute-start.10 = (bf16[36,1024]{1,0:T(8,128)(2,1)S(1)}, bf16[36,1024]{1,0:T(8,128)(2,1)S(1)}, u32[]{:S(2)}, u32[]{:S(2)}) collective-permute-start(bf16[36,1024]{1,0:T(8,128)(2,1)S(1)} %get-tuple-element.64), channel_id=1, source_target_pairs={{0,2},{2,0},{4,6},{6,4},{1,3},{3,1},{5,7},{7,5},{8,10},{10,8},{12,... | collective-permute-start | bytes 221192 | tf_op jit(solution)/shard_map/ppermute | solution.py:399
  15.3 1.7 %collective-permute-start.7 = (bf16[144,1024]{1,0:T(8,128)(2,1)S(1)}, bf16[144,1024]{1,0:T(8,128)(2,1)S(1)}, u32[]{:S(2)}, u32[]{:S(2)}) collective-permute-start(bf16[144,1024]{1,0:T(8,128)(2,1)S(1)} %join.2.refs_0_.refs_4_), channel_id=1, source_target_pairs={{0,16},{16,0},{1,17},{17,1},{2,18},{18,2},{3,19},{19,3},{4,20},{20... | collective-permute-start | bytes 884744 | tf_op jit(solution)/shard_map/ppermute | solution.py:394
  17.0 1.5 %collective-permute-start.3 = (bf16[144,1024]{1,0:T(8,128)(2,1)S(1)}, bf16[144,1024]{1,0:T(8,128)(2,1)S(1)}, u32[]{:S(2)}, u32[]{:S(2)}) collective-permute-start(bf16[144,1024]{1,0:T(8,128)(2,1)S(1)} %join.2.refs_0_.refs_4_), channel_id=1, source_target_pairs={{0,1},{1,0},{2,3},{3,2},{4,5},{5,4},{6,7},{7,6},{8,9},{9,8},{10,11... | collective-permute-start | bytes 884744 | tf_op jit(solution)/shard_map/ppermute | solution.py:394
  18.5 2.2 %forward_down.2 = (bf16[144,2048]{1,0:T(8,128)(2,1)S(1)}, bf16[144,2048]{1,0:T(8,128)(2,1)S(1)}, bf16[144,1024]{1,0:T(8,128)(2,1)S(1)}) custom-call(bf16[144,1024]{1,0:T(8,128)(2,1)S(1)} %join.2.refs_0_.refs_4_, bf16[1024,2048]{1,0:T(8,128)(2,1)S(1)} %copy-done, bf16[1024,2048]{1,0:T(8,128)(2,1)S(1)} %copy-done.1, ...), custom_call_target="tpu_custom_call" | custom-call | tf_op jit(solution)/shard_map/forward_down/pallas_call | solution.py:238
  20.8 0.3 collective-permute-done.9.refs_2_
  21.2 1.6 %collective-permute-start.11 = (bf16[144,1024]{1,0:T(8,128)(2,1)S(1)}, bf16[144,1024]{1,0:T(8,128)(2,1)S(1)}, u32[]{:S(2)}, u32[]{:S(2)}) collective-permute-start(bf16[144,1024]{1,0:T(8,128)(2,1)S(1)} %join.3.refs_0_), channel_id=1, source_target_pairs={{0,16},{16,0},{1,17},{17,1},{2,18},{18,2},{3,19},{19,3},{4,20},{20... | collective-permute-start | bytes 884744 | tf_op jit(solution)/shard_map/ppermute | solution.py:394
  22.7 1.5 %collective-permute-start.13 = (bf16[144,1024]{1,0:T(8,128)(2,1)S(1)}, bf16[144,1024]{1,0:T(8,128)(2,1)S(1)}, u32[]{:S(2)}, u32[]{:S(2)}) collective-permute-start(bf16[144,1024]{1,0:T(8,128)(2,1)S(1)} %join.3.refs_0_), channel_id=1, source_target_pairs={{0,1},{1,0},{2,3},{3,2},{4,5},{5,4},{6,7},{7,6},{8,9},{9,8},{10,11... | collective-permute-start | bytes 884744 | tf_op jit(solution)/shard_map/ppermute | solution.py:394
  24.2 2.2 %forward_down.3 = (bf16[144,2048]{1,0:T(8,128)(2,1)S(1)}, bf16[144,2048]{1,0:T(8,128)(2,1)S(1)}, bf16[72,1024]{1,0:T(8,128)(2,1)S(1)}, bf16[72,1024]{1,0:T(8,128...) custom-call(bf16[144,1024]{1,0:T(8,128)(2,1)S(1)} %collective-permute-done.3.refs_0_.refs_1_.refs_5_, ...), custom_call_target="tpu_custom_call" | custom-call | tf_op jit(solution)/shard_map/forward_down/pallas_call | solution.py:238
  26.5 1.6 %forward.2 = (bf16[144,2048]{1,0:T(8,128)(2,1)S(1)}, bf16[144,2048]{1,0:T(8,128)(2,1)S(1)}) custom-call(bf16[144,2048]{1,0:T(8,128)(2,1)S(1)} %get-tuple-element.54.refs_0_.refs_5_, bf16[144,1024]{1,0:T(8,128)(2,1)S(1)} %collective-permute-done.7.refs_1_.refs_2_.refs_6_, bf16[1024,2048]{1,0:T(8,128)(2,1)S(1)} %copy-done, bf16[1024,2048]{1,0:T(8,128)(2,1)S(1)} %copy-done.1), custom_call_target="tpu_custom_call" | custom-call | tf_op jit(solution)/shard_map/forward/pallas_call | solution.py:238
  28.1 1.5 %collective-permute-done.11.refs_2_.refs_0_ = bf16[144,1024]{1,0:T(8,128)(2,1)S(1)} collective-permute-done((bf16[144,1024]{1,0:T(8,128)(2,1)S(1)}, bf16[144,1024]{1,0:T(8,128)(2,1)S(1)}, u32[]{:S(2)}, u32[]{:S(2)}) %collective-permute-start.11) | collective-permute-done | bytes 294944 | tf_op jit(solution)/shard_map/ppermute | solution.py:394
  29.7 1.5 %collective-permute-start.12 = (bf16[144,1024]{1,0:T(8,128)(2,1)S(1)}, bf16[144,1024]{1,0:T(8,128)(2,1)S(1)}, u32[]{:S(2)}, u32[]{:S(2)}) collective-permute-start(bf16[144,1024]{1,0:T(8,128)(2,1)S(1)} %relay.4.refs_1_), channel_id=1, source_target_pairs={{0,16},{16,0},{1,17},{17,1},{2,18},{18,2},{3,19},{19,3},{4,20},{20... | collective-permute-start | bytes 884744 | tf_op jit(solution)/shard_map/ppermute | solution.py:394
  31.2 1.6 %collective-permute-start.14 = (bf16[144,1024]{1,0:T(8,128)(2,1)S(1)}, bf16[144,1024]{1,0:T(8,128)(2,1)S(1)}, u32[]{:S(2)}, u32[]{:S(2)}) collective-permute-start(bf16[144,1024]{1,0:T(8,128)(2,1)S(1)} %relay.5), channel_id=1, source_target_pairs={{0,1},{1,0},{2,3},{3,2},{4,5},{5,4},{6,7},{7,6},{8,9},{9,8},{10,11... | collective-permute-start | bytes 884744 | tf_op jit(solution)/shard_map/ppermute | solution.py:394
  32.8 0.8 %collective-permute-start.4 = (bf16[72,1024]{1,0:T(8,128)(2,1)S(1)}, bf16[72,1024]{1,0:T(8,128)(2,1)S(1)}, u32[]{:S(2)}, u32[]{:S(2)}) collective-permute-start(bf16[72,1024]{1,0:T(8,128)(2,1)S(1)} %get-tuple-element.51), channel_id=1, source_target_pairs={{0,2},{2,0},{4,6},{6,4},{1,3},{3,1},{5,7},{7,5},{8,10},{10,8},{12,... | collective-permute-start | bytes 442376 | tf_op jit(solution)/shard_map/ppermute | solution.py:399
  33.6 2.6 %collective-permute-start.5 = (bf16[72,1024]{1,0:T(8,128)(2,1)S(1)}, bf16[72,1024]{1,0:T(8,128)(2,1)S(1)}, u32[]{:S(2)}, u32[]{:S(2)}) collective-permute-start(bf16[72,1024]{1,0:T(8,128)(2,1)S(1)} %get-tuple-element.52), channel_id=1, source_target_pairs={{0,4},{2,6},{4,0},{6,2},{1,5},{3,7},{5,1},{7,3},{8,12},{10,14},{12... | collective-permute-start | bytes 442376 | tf_op jit(solution)/shard_map/ppermute | solution.py:399
  36.3 1.0 %collective-permute-start.6 = (bf16[72,1024]{1,0:T(8,128)(2,1)S(1)}, bf16[72,1024]{1,0:T(8,128)(2,1)S(1)}, u32[]{:S(2)}, u32[]{:S(2)}) collective-permute-start(bf16[72,1024]{1,0:T(8,128)(2,1)S(1)} %get-tuple-element.53), channel_id=1, source_target_pairs={{0,6},{2,4},{4,2},{6,0},{1,7},{3,5},{5,3},{7,1},{8,14},{10,12},{12... | collective-permute-start | bytes 442376 | tf_op jit(solution)/shard_map/ppermute | solution.py:399
  37.2 0.2 turn.1.xt_ref
  37.5 1.6 %forward.3 = (bf16[144,2048]{1,0:T(8,128)(2,1)S(1)}, bf16[144,2048]{1,0:T(8,128)(2,1)S(1)}) custom-call(bf16[144,1024]{1,0:T(8,128)(2,1)S(1)} %collective-permute-done.12.refs_3_.refs_7_.refs_0_, bf16[1024,2048]{1,0:T(8,128)(2,1)S(1)} %copy-done, bf16[1024,2048]{1,0:T(8,128)(2,1)S(1)} %copy-done.1), custom_call_target="tpu_custom_call" | custom-call | tf_op jit(solution)/shard_map/forward/pallas_call | solution.py:238
  39.1 4.9 %backward.2 = (bf16[512,1536]{1,0:T(8,128)(2,1)S(1)}, bf16[512,1536]{1,0:T(8,128)(2,1)S(1)}) custom-call(bf16[512,576]{1,0:T(8,128)(2,1)S(1)} %turn.1.xt_ref, bf16[144,1024]{1,0:T(8,128)(2,1)S(1)} %join.3.refs_0_, bf16[144,1024]{1,0:T(8,128)(2,1)S(1)} %collective-permute-done.13.refs_2_.refs_1_, ...), custom_call_target="tpu_custom_call" | custom-call | flops 20000000000 | tf_op jit(solution)/shard_map/backward/pallas_call | solution.py:308
  44.0 2.2 %collective-permute-done.5.refs_2_ = bf16[72,1024]{1,0:T(8,128)(2,1)S(1)} collective-permute-done((bf16[72,1024]{1,0:T(8,128)(2,1)S(1)}, bf16[72,1024]{1,0:T(8,128)(2,1)S(1)}, u32[]{:S(2)}, u32[]{:S(2)}) %collective-permute-start.5) | collective-permute-done | bytes 147488 | tf_op jit(solution)/shard_map/ppermute | solution.py:399
  46.3 0.6 %collective-permute-start.15 = (bf16[144,1024]{1,0:T(8,128)(2,1)S(1)}, bf16[144,1024]{1,0:T(8,128)(2,1)S(1)}, u32[]{:S(2)}, u32[]{:S(2)}) collective-permute-start(bf16[144,1024]{1,0:T(8,128)(2,1)S(1)} %get-tuple-element.73), channel_id=1, source_target_pairs={{0,1},{1,0},{2,3},{3,2},{4,5},{5,4},{6,7},{7,6},{8,9},{9,8},{10,11... | collective-permute-start | bytes 884744 | tf_op jit(solution)/shard_map/ppermute | solution.py:394
  46.8 1.7 %backward.3 = (bf16[512,512]{1,0:T(8,128)(2,1)S(1)}, bf16[512,512]{1,0:T(8,128)(2,1)S(1)}) custom-call(bf16[512,576]{1,0:T(8,128)(2,1)S(1)} %turn.1.xt_ref, bf16[144,1024]{1,0:T(8,128)(2,1)S(1)} %join.3.refs_0_, bf16[144,1024]{1,0:T(8,128)(2,1)S(1)} %collective-permute-done.13.refs_2_.refs_1_, bf16[144,1024]{1,0:T(8,128)(2,1)S(1)} %collective-permute-done.11.refs_2_.refs_0_, ...), custom_call_target="tpu_custom_call" | custom-call | flops 20000000000 | tf_op jit(solution)/shard_map/backward/pallas_call | solution.py:308
  48.5 0.6 %collective-permute-start.17 = (bf16[512,512]{1,0:T(8,128)(2,1)S(1)}, bf16[512,512]{1,0:T(8,128)(2,1)S(1)}, u32[]{:S(2)}, u32[]{:S(2)}) collective-permute-start(bf16[512,512]{1,0:T(8,128)(2,1)S(1)} %get-tuple-element.77), channel_id=1, source_target_pairs={{0,8},{8,0},{1,9},{9,1},{2,10},{10,2},{3,11},{11,3},{4,12},{12,4},... | collective-permute-start | bytes 1572872 | tf_op jit(solution)/shard_map/ppermute | solution.py:394
  49.1 1.1 %collective-permute-done.16.refs_1_ = bf16[512,1536]{1,0:T(8,128)(2,1)S(1)} collective-permute-done((bf16[512,1536]{1,0:T(8,128)(2,1)S(1)}, bf16[512,1536]{1,0:T(8,128)(2,1)S(1)}, u32[]{:S(2)}, u32[]{:S(2)}) %collective-permute-start.16) | collective-permute-done | bytes 1572896 | tf_op jit(solution)/shard_map/ppermute | solution.py:394
  50.2 1.3 %finish.2 = (bf16[256,2048]{1,0:T(8,128)(2,1)}, bf16[256,2048]{1,0:T(8,128)(2,1)}) custom-call(bf16[512,1536]{1,0:T(8,128)(2,1)S(1)} %get-tuple-element.71.refs_4_.refs_0_, bf16[512,1536]{1,0:T(8,128)(2,1)S(1)} %collective-permute-done.16.refs_1_), custom_call_target="tpu_custom_call" | custom-call | tf_op jit(solution)/shard_map/finish/pallas_call | solution.py:344
  51.6 1.5 %collective-permute-done.15.got_ref = bf16[144,1024]{1,0:T(8,128)(2,1)S(1)} collective-permute-done((bf16[144,1024]{1,0:T(8,128)(2,1)S(1)}, bf16[144,1024]{1,0:T(8,128)(2,1)S(1)}, u32[]{:S(2)}, u32[]{:S(2)}) %collective-permute-start.15) | collective-permute-done | bytes 294944 | tf_op jit(solution)/shard_map/ppermute | solution.py:394
  53.0 1.0 %unpack.1 = bf16[128,1024]{1,0:T(8,128)(2,1)} custom-call(bf16[144,128]{1,0:T(8,128)(2,1)S(1)} %get-tuple-element.42.placer_ref, bf16[144,1024]{1,0:T(8,128)(2,1)S(1)} %get-tuple-element.72.mine_ref.refs_13_, bf16[144,1024]{1,0:T(8,128)(2,1)S(1)} %collective-permute-done.15.got_ref, bf16[256,2048]{1,0:T(8,128)(2,1)} %get-tuple-element.75.refs_0_.refs_2_), custom_call_target="tpu_custom_call" | custom-call | flops 20000000000 | tf_op jit(solution)/shard_map/unpack/pallas_call | solution.py:383
  54.1 0.9 %finish.3 = (bf16[256,2048]{1,0:T(8,128)(2,1)}, bf16[256,2048]{1,0:T(8,128)(2,1)}) custom-call(bf16[512,512]{1,0:T(8,128)(2,1)S(1)} %get-tuple-element.76.refs_0_, bf16[512,512]{1,0:T(8,128)(2,1)S(1)} %collective-permute-done.17.refs_1_, bf16[256,2048]{1,0:T(8,128)(2,1)} %get-tuple-element.75.refs_0_.refs_2_, ...), custom_call_target="tpu_custom_call", output_to_operand_aliasing={{0}: (2, {}), {1}: (3, {})} | custom-call | tf_op jit(solution)/shard_map/finish/pallas_call | solution.py:344
  (27 shorter events, 0.3 us)
Async XLA Ops:
  2.1 12.5 %collective-permute-start = (bf16[36,1024]{1,0:T(8,128)(2,1)S(1)}, bf16[36,1024]{1,0:T(8,128)(2,1)S(1)}, u32[]{:S(2)}, u32[]{:S(2)}) collective-permute-start(bf16[36,1024]{1,0:T(8,128)(2,1)S(1)} %get-tuple-element.43), channel_id=1, source_target_pairs={{0,6},{2,4},{4,2},{6,0},{1,7},{3,5},{5,3},{7,1},{8,14},{10,12},{12... | collective-permute-start | bytes 221192 | tf_op jit(solution)/shard_map/ppermute | solution.py:399
  7.2 8.0 %collective-permute-start.1 = (bf16[36,1024]{1,0:T(8,128)(2,1)S(1)}, bf16[36,1024]{1,0:T(8,128)(2,1)S(1)}, u32[]{:S(2)}, u32[]{:S(2)}) collective-permute-start(bf16[36,1024]{1,0:T(8,128)(2,1)S(1)} %get-tuple-element.44), channel_id=1, source_target_pairs={{0,4},{2,6},{4,0},{6,2},{1,5},{3,7},{5,1},{7,3},{8,12},{10,14},{12... | collective-permute-start | bytes 221192 | tf_op jit(solution)/shard_map/ppermute | solution.py:399
  7.2 8.0 %collective-permute-start.2 = (bf16[36,1024]{1,0:T(8,128)(2,1)S(1)}, bf16[36,1024]{1,0:T(8,128)(2,1)S(1)}, u32[]{:S(2)}, u32[]{:S(2)}) collective-permute-start(bf16[36,1024]{1,0:T(8,128)(2,1)S(1)} %get-tuple-element.45), channel_id=1, source_target_pairs={{0,2},{2,0},{4,6},{6,4},{1,3},{3,1},{5,7},{7,5},{8,10},{10,8},{12,... | collective-permute-start | bytes 221192 | tf_op jit(solution)/shard_map/ppermute | solution.py:399
  7.9 10.7 %copy-start = (bf16[1024,2048]{1,0:T(8,128)(2,1)S(1)}, bf16[1024,2048]{1,0:T(8,128)(2,1)}, u32[]{:S(2)}) copy-start(bf16[1024,2048]{1,0:T(8,128)(2,1)} %refs_1_.5) | copy-start | bytes 12582916
  7.9 10.7 %copy-start.1 = (bf16[1024,2048]{1,0:T(8,128)(2,1)S(1)}, bf16[1024,2048]{1,0:T(8,128)(2,1)}, u32[]{:S(2)}) copy-start(bf16[1024,2048]{1,0:T(8,128)(2,1)} %refs_2_.7) | copy-start | bytes 12582916
  10.8 10.0 %collective-permute-start.8 = (bf16[36,1024]{1,0:T(8,128)(2,1)S(1)}, bf16[36,1024]{1,0:T(8,128)(2,1)S(1)}, u32[]{:S(2)}, u32[]{:S(2)}) collective-permute-start(bf16[36,1024]{1,0:T(8,128)(2,1)S(1)} %get-tuple-element.62), channel_id=1, source_target_pairs={{0,6},{2,4},{4,2},{6,0},{1,7},{3,5},{5,3},{7,1},{8,14},{10,12},{12... | collective-permute-start | bytes 221192 | tf_op jit(solution)/shard_map/ppermute | solution.py:399
  14.6 6.5 %collective-permute-start.9 = (bf16[36,1024]{1,0:T(8,128)(2,1)S(1)}, bf16[36,1024]{1,0:T(8,128)(2,1)S(1)}, u32[]{:S(2)}, u32[]{:S(2)}) collective-permute-start(bf16[36,1024]{1,0:T(8,128)(2,1)S(1)} %get-tuple-element.63), channel_id=1, source_target_pairs={{0,4},{2,6},{4,0},{6,2},{1,5},{3,7},{5,1},{7,3},{8,12},{10,14},{12... | collective-permute-start | bytes 221192 | tf_op jit(solution)/shard_map/ppermute | solution.py:399
  14.6 6.5 %collective-permute-start.10 = (bf16[36,1024]{1,0:T(8,128)(2,1)S(1)}, bf16[36,1024]{1,0:T(8,128)(2,1)S(1)}, u32[]{:S(2)}, u32[]{:S(2)}) collective-permute-start(bf16[36,1024]{1,0:T(8,128)(2,1)S(1)} %get-tuple-element.64), channel_id=1, source_target_pairs={{0,2},{2,0},{4,6},{6,4},{1,3},{3,1},{5,7},{7,5},{8,10},{10,8},{12,... | collective-permute-start | bytes 221192 | tf_op jit(solution)/shard_map/ppermute | solution.py:399
  15.3 11.2 %collective-permute-start.7 = (bf16[144,1024]{1,0:T(8,128)(2,1)S(1)}, bf16[144,1024]{1,0:T(8,128)(2,1)S(1)}, u32[]{:S(2)}, u32[]{:S(2)}) collective-permute-start(bf16[144,1024]{1,0:T(8,128)(2,1)S(1)} %join.2.refs_0_.refs_4_), channel_id=1, source_target_pairs={{0,16},{16,0},{1,17},{17,1},{2,18},{18,2},{3,19},{19,3},{4,20},{20... | collective-permute-start | bytes 884744 | tf_op jit(solution)/shard_map/ppermute | solution.py:394
  17.0 7.2 %collective-permute-start.3 = (bf16[144,1024]{1,0:T(8,128)(2,1)S(1)}, bf16[144,1024]{1,0:T(8,128)(2,1)S(1)}, u32[]{:S(2)}, u32[]{:S(2)}) collective-permute-start(bf16[144,1024]{1,0:T(8,128)(2,1)S(1)} %join.2.refs_0_.refs_4_), channel_id=1, source_target_pairs={{0,1},{1,0},{2,3},{3,2},{4,5},{5,4},{6,7},{7,6},{8,9},{9,8},{10,11... | collective-permute-start | bytes 884744 | tf_op jit(solution)/shard_map/ppermute | solution.py:394
  21.2 8.5 %collective-permute-start.11 = (bf16[144,1024]{1,0:T(8,128)(2,1)S(1)}, bf16[144,1024]{1,0:T(8,128)(2,1)S(1)}, u32[]{:S(2)}, u32[]{:S(2)}) collective-permute-start(bf16[144,1024]{1,0:T(8,128)(2,1)S(1)} %join.3.refs_0_), channel_id=1, source_target_pairs={{0,16},{16,0},{1,17},{17,1},{2,18},{18,2},{3,19},{19,3},{4,20},{20... | collective-permute-start | bytes 884744 | tf_op jit(solution)/shard_map/ppermute | solution.py:394
  22.7 8.5 %collective-permute-start.13 = (bf16[144,1024]{1,0:T(8,128)(2,1)S(1)}, bf16[144,1024]{1,0:T(8,128)(2,1)S(1)}, u32[]{:S(2)}, u32[]{:S(2)}) collective-permute-start(bf16[144,1024]{1,0:T(8,128)(2,1)S(1)} %join.3.refs_0_), channel_id=1, source_target_pairs={{0,1},{1,0},{2,3},{3,2},{4,5},{5,4},{6,7},{7,6},{8,9},{9,8},{10,11... | collective-permute-start | bytes 884744 | tf_op jit(solution)/shard_map/ppermute | solution.py:394
  29.7 7.6 %collective-permute-start.12 = (bf16[144,1024]{1,0:T(8,128)(2,1)S(1)}, bf16[144,1024]{1,0:T(8,128)(2,1)S(1)}, u32[]{:S(2)}, u32[]{:S(2)}) collective-permute-start(bf16[144,1024]{1,0:T(8,128)(2,1)S(1)} %relay.4.refs_1_), channel_id=1, source_target_pairs={{0,16},{16,0},{1,17},{17,1},{2,18},{18,2},{3,19},{19,3},{4,20},{20... | collective-permute-start | bytes 884744 | tf_op jit(solution)/shard_map/ppermute | solution.py:394
  31.2 7.8 %collective-permute-start.14 = (bf16[144,1024]{1,0:T(8,128)(2,1)S(1)}, bf16[144,1024]{1,0:T(8,128)(2,1)S(1)}, u32[]{:S(2)}, u32[]{:S(2)}) collective-permute-start(bf16[144,1024]{1,0:T(8,128)(2,1)S(1)} %relay.5), channel_id=1, source_target_pairs={{0,1},{1,0},{2,3},{3,2},{4,5},{5,4},{6,7},{7,6},{8,9},{9,8},{10,11... | collective-permute-start | bytes 884744 | tf_op jit(solution)/shard_map/ppermute | solution.py:394
  32.8 11.1 %collective-permute-start.4 = (bf16[72,1024]{1,0:T(8,128)(2,1)S(1)}, bf16[72,1024]{1,0:T(8,128)(2,1)S(1)}, u32[]{:S(2)}, u32[]{:S(2)}) collective-permute-start(bf16[72,1024]{1,0:T(8,128)(2,1)S(1)} %get-tuple-element.51), channel_id=1, source_target_pairs={{0,2},{2,0},{4,6},{6,4},{1,3},{3,1},{5,7},{7,5},{8,10},{10,8},{12,... | collective-permute-start | bytes 442376 | tf_op jit(solution)/shard_map/ppermute | solution.py:399
  33.6 12.5 %collective-permute-start.5 = (bf16[72,1024]{1,0:T(8,128)(2,1)S(1)}, bf16[72,1024]{1,0:T(8,128)(2,1)S(1)}, u32[]{:S(2)}, u32[]{:S(2)}) collective-permute-start(bf16[72,1024]{1,0:T(8,128)(2,1)S(1)} %get-tuple-element.52), channel_id=1, source_target_pairs={{0,4},{2,6},{4,0},{6,2},{1,5},{3,7},{5,1},{7,3},{8,12},{10,14},{12... | collective-permute-start | bytes 442376 | tf_op jit(solution)/shard_map/ppermute | solution.py:399
  36.3 9.9 %collective-permute-start.6 = (bf16[72,1024]{1,0:T(8,128)(2,1)S(1)}, bf16[72,1024]{1,0:T(8,128)(2,1)S(1)}, u32[]{:S(2)}, u32[]{:S(2)}) collective-permute-start(bf16[72,1024]{1,0:T(8,128)(2,1)S(1)} %get-tuple-element.53), channel_id=1, source_target_pairs={{0,6},{2,4},{4,2},{6,0},{1,7},{3,5},{5,3},{7,1},{8,14},{10,12},{12... | collective-permute-start | bytes 442376 | tf_op jit(solution)/shard_map/ppermute | solution.py:399
  46.3 6.8 %collective-permute-start.15 = (bf16[144,1024]{1,0:T(8,128)(2,1)S(1)}, bf16[144,1024]{1,0:T(8,128)(2,1)S(1)}, u32[]{:S(2)}, u32[]{:S(2)}) collective-permute-start(bf16[144,1024]{1,0:T(8,128)(2,1)S(1)} %get-tuple-element.73), channel_id=1, source_target_pairs={{0,1},{1,0},{2,3},{3,2},{4,5},{5,4},{6,7},{7,6},{8,9},{9,8},{10,11... | collective-permute-start | bytes 884744 | tf_op jit(solution)/shard_map/ppermute | solution.py:394
  46.8 3.4 %collective-permute-start.16 = (bf16[512,1536]{1,0:T(8,128)(2,1)S(1)}, bf16[512,1536]{1,0:T(8,128)(2,1)S(1)}, u32[]{:S(2)}, u32[]{:S(2)}) collective-permute-start(bf16[512,1536]{1,0:T(8,128)(2,1)S(1)} %get-tuple-element.74), channel_id=1, source_target_pairs={{0,8},{8,0},{1,9},{9,1},{2,10},{10,2},{3,11},{11,3},{4,12},{12,4},... | collective-permute-start | bytes 4718600 | tf_op jit(solution)/shard_map/ppermute | solution.py:394
  48.5 5.6 %collective-permute-start.17 = (bf16[512,512]{1,0:T(8,128)(2,1)S(1)}, bf16[512,512]{1,0:T(8,128)(2,1)S(1)}, u32[]{:S(2)}, u32[]{:S(2)}) collective-permute-start(bf16[512,512]{1,0:T(8,128)(2,1)S(1)} %get-tuple-element.77), channel_id=1, source_target_pairs={{0,8},{8,0},{1,9},{9,1},{2,10},{10,2},{3,11},{11,3},{4,12},{12,4},... | collective-permute-start | bytes 1572872 | tf_op jit(solution)/shard_map/ppermute | solution.py:394

commit v14 on v13

--- a/solution.py
+++ b/solution.py
@@ -227,7 +227,7 @@
         shares[0][...] = acc_ref[...].astype(BF16)
 
 
-def forward(xs, wg, wu, wd=None, other=None, fetch=False, earlier=()):
+def forward(xs, wg, wu, wd=None, other=None, fetch=False, earlier=(), cost=CHEAP):
     n, (part, width), cols = len(xs), xs[0].shape, wg.shape[1]
     rows = n * part
     down, pair = wd is not None, other is not None
@@ -248,7 +248,7 @@
         + [pltpu.VMEM((rows, width), BF16)] * (n > 1)
         + [pltpu.SemaphoreType.DMA((cols // (2 * WIDE), 2))] * fetch,
         compiler_params=LARGE,
-        cost_estimate=CHEAP,
+        cost_estimate=cost,
         name="forward" + "_fetch" * fetch + "_down" * down,
     )(*earlier, *xs, *weights, *([wd] * down), *([other] * pair))
 
@@ -316,7 +316,8 @@
     )(xt, *gs, *acts, *coefs, wdt, *earlier)
 
 
-def finish_kernel(spans, more, *refs):
+def finish_kernel(spans, more, unused, *refs):
+    refs = refs[unused:]
     n = len(spans)
     pairs = [refs[2 * i : 2 * i + 2] for i in range(n)]
     gate_ref, up_ref, gate, up, sems = refs[2 * n + 2 * more :]
@@ -336,22 +337,22 @@
         copy.wait()
 
 
-def finish(owns, gots, firsts, width, held=()):
+def finish(owns, gots, firsts, width, held=(), earlier=()):
     share = owns[0].shape[0] // 2
     spans = tuple((first, own.shape[1]) for first, own in zip(firsts, owns))
     total = sum(cols for _, cols in spans)
     n, more = len(owns), len(held) > 0
     return pl.pallas_call(
-        functools.partial(finish_kernel, spans, more),
+        functools.partial(finish_kernel, spans, more, len(earlier)),
         out_shape=[jax.ShapeDtypeStruct((share, width), BF16)] * 2,
-        in_specs=[HERE] * (2 * n) + [ANYWHERE] * (2 * more),
+        in_specs=[AFAR] * len(earlier) + [HERE] * (2 * n) + [ANYWHERE] * (2 * more),
         out_specs=[ANYWHERE] * 2,
         scratch_shapes=[pltpu.VMEM((share, total), BF16)] * 2 + [pltpu.SemaphoreType.DMA((n, 2))],
-        input_output_aliases={2 * n: 0, 2 * n + 1: 1} if more else {},
+        input_output_aliases={len(earlier) + 2 * n: 0, len(earlier) + 2 * n + 1: 1} if more else {},
         compiler_params=SMALL,
         cost_estimate=CHEAP,
         name="finish",
-    )(*[v for both in zip(owns, gots) for v in both], *held)
+    )(*[kept(v) for v in earlier], *[v for both in zip(owns, gots) for v in both], *held)
 
 
 def split_kernel(*refs):
@@ -383,11 +384,11 @@
     return pl.pallas_call(
         unpack_kernel,
         out_shape=jax.ShapeDtypeStruct((placer.shape[1], mine.shape[1]), BF16),
-        in_specs=[HERE] * 3 + [AFAR] * len(earlier),
+        in_specs=[HERE] * 3 + [ANYWHERE] * len(earlier),
         compiler_params=SMALL,
         cost_estimate=DEAR,
         name="unpack",
-    )(placer, mine, got, *[kept(v) for v in earlier])
+    )(placer, mine, got, *earlier)
 
 
 def swap(value, axis):
@@ -422,26 +423,26 @@
     act0, coef0, share_own = forward([x_own], wg, wu, wd)
     g_own = join(moved, [act0])
     g_far, g_near = swap(g_own, "far"), swap(g_own, "half")
-    act1, coef1, *shares = forward([x_near], wg, wu, wd, other=share_own)
-    act2, coef2 = forward([x_far], wg, wu, earlier=[act1])
-    (x_pass,) = relay([x_near], [mark(act2), g_far])
+    act1, coef1, *shares = forward([x_near], wg, wu, wd, other=share_own, earlier=[x_far])
+    (x_pass,) = relay([x_near], [mark(act1), g_far])
     (g_pass,) = relay([g_far], [x_pass, g_near])
     x_corner, g_corner = swap(x_pass, "far"), swap(g_pass, "half")
     returned = across_planes(shares)
-    act3, coef3 = forward([x_corner], wg, wu)
+    act2, coef2 = forward([x_far], wg, wu, earlier=[g_pass], cost=DEAR)
+    mine, theirs = split(returned, [act2])
+    got = swap(theirs, "half")
+    act3, coef3 = forward([x_corner], wg, wu, earlier=[mine])
     xt = turn(*scalars[1:], [x_own, x_near, x_far, x_corner], share)
 
     gs = [g_own, g_near, g_far, g_corner]
     acts, coefs = [act0, act1, act2, act3], [coef0, coef1, coef2, coef3]
     cols = w_down.shape[0]
-    cut = 3 * cols // 4
+    cut = cols // 2
     own0, sib0 = backward(xt, gs, acts, coefs, wdt, 0, cut)
-    mine, theirs = split(returned, [own0])
-    got = swap(theirs, "half")
-    own1, sib1 = backward(xt, gs, acts, coefs, wdt, cut, cols - cut, [mine])
+    own1, sib1 = backward(xt, gs, acts, coefs, wdt, cut, cols - cut, [own0])
     got0, got1 = swap(sib0, "core"), swap(sib1, "core")
-    held = finish([own0], [got0], (0,), cols)
-    outputs = unpack(placer, mine, got, held[:1])
+    outputs = unpack(placer, mine, got, [own1, got0])
+    held = finish([own0], [got0], (0,), cols, earlier=[outputs])
     grad_gate, grad_up = finish([own1], [got1], (cut,), cols, held)
     return outputs, grad_gate, grad_up
 

time: 55.3 us -> 53.9 us (0.975)
  waiting for transfers between devices: 6.75 us -> 5.27 us
    ppermute x9, waiting for transfers between devices: 4.19 us -> 0.92 us  [swap(): return lax.ppermute(value, axis, [(0, 1), (1, 0)])]
    ppermute x9, waiting for transfers between devices: 2.56 us -> 4.36 us  [across_planes(): lax.ppermute(blocks[k], 'arch', [(i, i ^ k) for i in range(EXPERTS)])]
    ppermute x9, starting transfers between devices: 14.6 us -> 16.2 us  [across_planes(): lax.ppermute(blocks[k], 'arch', [(i, i ^ k) for i in range(EXPERTS)])]
    ppermute x9, starting transfers between devices: 10.6 us -> 9.02 us  [swap(): return lax.ppermute(value, axis, [(0, 1), (1, 0)])]
  transfers between devices with their start and end apart: 18 -> 18, of which waited for: 5 -> 5; matrix products, arithmetic and copies ran while one was open for 0% -> 0% of each run, Pallas kernels for 36% -> 37%
where the time goes in v14:
time: 53.9 us; the launch traced here: 53.7 us
  starting transfers between devices  25.2 us (47%)
  Pallas kernels  22.3 us (41%)
  waiting for transfers between devices  5.27 us (10%)
  between operations  0.97 us (2%)
    ppermute x9, starting transfers between devices, across_planes(): lax.ppermute(blocks[k], 'arch', [(i, i ^ k) for i in range(EXPERTS)])  16.2 us
    ppermute x9, starting transfers between devices, swap(): return lax.ppermute(value, axis, [(0, 1), (1, 0)])  9.02 us
    pallas_call x4, Pallas kernels, forward(): pl.pallas_call(functools.partial(forward_kernel, n, fetch, down, pair, le...  7.62 us
    pallas_call x2, Pallas kernels, backward(): pl.pallas_call(functools.partial(backward_kernel, first, counts), out_sha...  6.55 us
    ppermute x9, waiting for transfers between devices, across_planes(): lax.ppermute(blocks[k], 'arch', [(i, i ^ k) for i in range(EXPERTS)])  4.36 us
    pallas_call x1, Pallas kernels, flip(): pl.pallas_call(flip_kernel, out_shape=[pltpu.VMEM(value.shape, value.dtyp...  2.88 us
    pallas_call x2, Pallas kernels, finish(): pl.pallas_call(functools.partial(finish_kernel, spans, more, len(earlier)...  2.2 us
    pallas_call x1, Pallas kernels, pack(): pl.pallas_call(pack_kernel, out_shape=[jax.ShapeDtypeStruct((EXPERTS * CA...  1.46 us
  transfers between devices with their start and end apart: 18, of which 5 were waited for; matrix products, arithmetic and copies ran while one was open for 0% of the time, Pallas kernels for 37%

profile of v14, /device:TPU:0, one launch (start us, length us, event | category | flops | bytes accessed | tf_op | source)
XLA Modules:
  0.0 53.7 jit_solution(11108709004137281537)
XLA Ops:
  0.6 1.5 %pack.1 = (bf16[144,128]{1,0:T(8,128)(2,1)S(1)}, bf16[36,1024]{1,0:T(8,128)(2,1)S(1)}, bf16[36,1024]{1,0:T(8,128)(2,1)S(1)}, bf16[36,1024]{1,0:T(8,128)(2,1)S(1)...) custom-call(s32[1]{0:T(128)} %bitcast.plane_ref, ...), custom_call_target="tpu_custom_call" | custom-call | tf_op jit(solution)/shard_map/pack/pallas_call | solution.py:79
  2.1 5.1 %collective-permute-start = (bf16[36,1024]{1,0:T(8,128)(2,1)S(1)}, bf16[36,1024]{1,0:T(8,128)(2,1)S(1)}, u32[]{:S(2)}, u32[]{:S(2)}) collective-permute-start(bf16[36,1024]{1,0:T(8,128)(2,1)S(1)} %get-tuple-element.43), channel_id=1, source_target_pairs={{0,6},{2,4},{4,2},{6,0},{1,7},{3,5},{5,3},{7,1},{8,14},{10,12},{12... | collective-permute-start | bytes 221192 | tf_op jit(solution)/shard_map/ppermute | solution.py:400
  7.2 0.6 %collective-permute-start.2 = (bf16[36,1024]{1,0:T(8,128)(2,1)S(1)}, bf16[36,1024]{1,0:T(8,128)(2,1)S(1)}, u32[]{:S(2)}, u32[]{:S(2)}) collective-permute-start(bf16[36,1024]{1,0:T(8,128)(2,1)S(1)} %get-tuple-element.45), channel_id=1, source_target_pairs={{0,2},{2,0},{4,6},{6,4},{1,3},{3,1},{5,7},{7,5},{8,10},{10,8},{12,... | collective-permute-start | bytes 221192 | tf_op jit(solution)/shard_map/ppermute | solution.py:400
  7.9 2.9 %flip.1 = (bf16[2048,1024]{1,0:T(8,128)(2,1)S(1)}, bf16[1024,2048]{1,0:T(8,128)(2,1)S(1)}) custom-call(bf16[2048,1024]{1,0:T(8,128)(2,1)} %source_ref), custom_call_target="tpu_custom_call" | custom-call | tf_op jit(solution)/shard_map/flip/pallas_call | solution.py:158
  10.8 3.8 %collective-permute-start.8 = (bf16[36,1024]{1,0:T(8,128)(2,1)S(1)}, bf16[36,1024]{1,0:T(8,128)(2,1)S(1)}, u32[]{:S(2)}, u32[]{:S(2)}) collective-permute-start(bf16[36,1024]{1,0:T(8,128)(2,1)S(1)} %get-tuple-element.60), channel_id=1, source_target_pairs={{0,6},{2,4},{4,2},{6,0},{1,7},{3,5},{5,3},{7,1},{8,14},{10,12},{12... | collective-permute-start | bytes 221192 | tf_op jit(solution)/shard_map/ppermute | solution.py:400
  14.6 0.6 %collective-permute-start.10 = (bf16[36,1024]{1,0:T(8,128)(2,1)S(1)}, bf16[36,1024]{1,0:T(8,128)(2,1)S(1)}, u32[]{:S(2)}, u32[]{:S(2)}) collective-permute-start(bf16[36,1024]{1,0:T(8,128)(2,1)S(1)} %get-tuple-element.62), channel_id=1, source_target_pairs={{0,2},{2,0},{4,6},{6,4},{1,3},{3,1},{5,7},{7,5},{8,10},{10,8},{12,... | collective-permute-start | bytes 221192 | tf_op jit(solution)/shard_map/ppermute | solution.py:400
  15.3 1.7 %collective-permute-start.4 = (bf16[144,1024]{1,0:T(8,128)(2,1)S(1)}, bf16[144,1024]{1,0:T(8,128)(2,1)S(1)}, u32[]{:S(2)}, u32[]{:S(2)}) collective-permute-start(bf16[144,1024]{1,0:T(8,128)(2,1)S(1)} %join.2.refs_0_.refs_4_), channel_id=1, source_target_pairs={{0,1},{1,0},{2,3},{3,2},{4,5},{5,4},{6,7},{7,6},{8,9},{9,8},{10,11... | collective-permute-start | bytes 884744 | tf_op jit(solution)/shard_map/ppermute | solution.py:395
  17.0 1.5 %collective-permute-start.3 = (bf16[144,1024]{1,0:T(8,128)(2,1)S(1)}, bf16[144,1024]{1,0:T(8,128)(2,1)S(1)}, u32[]{:S(2)}, u32[]{:S(2)}) collective-permute-start(bf16[144,1024]{1,0:T(8,128)(2,1)S(1)} %join.2.refs_0_.refs_4_), channel_id=1, source_target_pairs={{0,16},{16,0},{1,17},{17,1},{2,18},{18,2},{3,19},{19,3},{4,20},{20... | collective-permute-start | bytes 884744 | tf_op jit(solution)/shard_map/ppermute | solution.py:395
  18.5 2.2 %forward_down.2 = (bf16[144,2048]{1,0:T(8,128)(2,1)S(1)}, bf16[144,2048]{1,0:T(8,128)(2,1)S(1)}, bf16[144,1024]{1,0:T(8,128)(2,1)S(1)}) custom-call(bf16[144,1024]{1,0:T(8,128)(2,1)S(1)} %join.2.refs_0_.refs_4_, bf16[1024,2048]{1,0:T(8,128)(2,1)S(1)} %copy-done, bf16[1024,2048]{1,0:T(8,128)(2,1)S(1)} %copy-done.1, ...), custom_call_target="tpu_custom_call" | custom-call | tf_op jit(solution)/shard_map/forward_down/pallas_call | solution.py:238
  20.8 0.3 collective-permute-done.9.refs_2_
  21.2 1.6 %collective-permute-start.11 = (bf16[144,1024]{1,0:T(8,128)(2,1)S(1)}, bf16[144,1024]{1,0:T(8,128)(2,1)S(1)}, u32[]{:S(2)}, u32[]{:S(2)}) collective-permute-start(bf16[144,1024]{1,0:T(8,128)(2,1)S(1)} %join.3.refs_0_), channel_id=1, source_target_pairs={{0,16},{16,0},{1,17},{17,1},{2,18},{18,2},{3,19},{19,3},{4,20},{20... | collective-permute-start | bytes 884744 | tf_op jit(solution)/shard_map/ppermute | solution.py:395
  22.7 1.5 %collective-permute-start.12 = (bf16[144,1024]{1,0:T(8,128)(2,1)S(1)}, bf16[144,1024]{1,0:T(8,128)(2,1)S(1)}, u32[]{:S(2)}, u32[]{:S(2)}) collective-permute-start(bf16[144,1024]{1,0:T(8,128)(2,1)S(1)} %join.3.refs_0_), channel_id=1, source_target_pairs={{0,1},{1,0},{2,3},{3,2},{4,5},{5,4},{6,7},{7,6},{8,9},{9,8},{10,11... | collective-permute-start | bytes 884744 | tf_op jit(solution)/shard_map/ppermute | solution.py:395
  24.2 0.3 collective-permute-done.3.refs_0_.refs_1_.refs_2_.refs_6_
  24.5 2.2 %forward_down.3 = (bf16[144,2048]{1,0:T(8,128)(2,1)S(1)}, bf16[144,2048]{1,0:T(8,128)(2,1)S(1)}, bf16[72,1024]{1,0:T(8,128)(2,1)S(1)}, bf16[72,1024]{1,0:T(8,128...) custom-call(bf16[144,1024]{1,0:T(8,128)(2,1)S(1)} %collective-permute-done.3.refs_0_.refs_1_.refs_2_.refs_6_, ...), custom_call_target="tpu_custom_call" | custom-call | tf_op jit(solution)/shard_map/forward_down/pallas_call | solution.py:238
  26.8 3.5 %collective-permute-start.5 = (bf16[72,1024]{1,0:T(8,128)(2,1)S(1)}, bf16[72,1024]{1,0:T(8,128)(2,1)S(1)}, u32[]{:S(2)}, u32[]{:S(2)}) collective-permute-start(bf16[72,1024]{1,0:T(8,128)(2,1)S(1)} %get-tuple-element.51), channel_id=1, source_target_pairs={{0,2},{2,0},{4,6},{6,4},{1,3},{3,1},{5,7},{7,5},{8,10},{10,8},{12,... | collective-permute-start | bytes 442376 | tf_op jit(solution)/shard_map/ppermute | solution.py:400
  30.3 2.0 %collective-permute-start.6 = (bf16[72,1024]{1,0:T(8,128)(2,1)S(1)}, bf16[72,1024]{1,0:T(8,128)(2,1)S(1)}, u32[]{:S(2)}, u32[]{:S(2)}) collective-permute-start(bf16[72,1024]{1,0:T(8,128)(2,1)S(1)} %get-tuple-element.52), channel_id=1, source_target_pairs={{0,4},{2,6},{4,0},{6,2},{1,5},{3,7},{5,1},{7,3},{8,12},{10,14},{12... | collective-permute-start | bytes 442376 | tf_op jit(solution)/shard_map/ppermute | solution.py:400
  32.3 0.5 collective-permute-start.7
  32.8 1.7 %collective-permute-start.14 = (bf16[144,1024]{1,0:T(8,128)(2,1)S(1)}, bf16[144,1024]{1,0:T(8,128)(2,1)S(1)}, u32[]{:S(2)}, u32[]{:S(2)}) collective-permute-start(bf16[144,1024]{1,0:T(8,128)(2,1)S(1)} %relay.4.refs_1_), channel_id=1, source_target_pairs={{0,16},{16,0},{1,17},{17,1},{2,18},{18,2},{3,19},{19,3},{4,20},{20... | collective-permute-start | bytes 884744 | tf_op jit(solution)/shard_map/ppermute | solution.py:395
  34.6 1.6 %forward.2 = (bf16[144,2048]{1,0:T(8,128)(2,1)S(1)}, bf16[144,2048]{1,0:T(8,128)(2,1)S(1)}) custom-call(bf16[144,1024]{1,0:T(8,128)(2,1)S(1)} %relay.5.refs_0_, bf16[144,1024]{1,0:T(8,128)(2,1)S(1)} %collective-permute-done.3.refs_0_.refs_1_.refs_2_.refs_6_, bf16[1024,2048]{1,0:T(8,128)(2,1)S(1)} %copy-done, bf16[1024,2048]{1,0:T(8,128)(2,1)S(1)} %copy-done.1), custom_call_target="tpu_custom_call" | custom-call | flops 20000000000 | tf_op jit(solution)/shard_map/forward/pallas_call | solution.py:238
  36.2 4.0 %collective-permute-done.6.refs_2_ = bf16[72,1024]{1,0:T(8,128)(2,1)S(1)} collective-permute-done((bf16[72,1024]{1,0:T(8,128)(2,1)S(1)}, bf16[72,1024]{1,0:T(8,128)(2,1)S(1)}, u32[]{:S(2)}, u32[]{:S(2)}) %collective-permute-start.6) | collective-permute-done | bytes 147488 | tf_op jit(solution)/shard_map/ppermute | solution.py:400
  40.2 0.1 split.1
  40.3 0.4 collective-permute-start.13
  40.7 0.2 turn.1.xt_ref
  40.9 1.6 %forward.3 = (bf16[144,2048]{1,0:T(8,128)(2,1)S(1)}, bf16[144,2048]{1,0:T(8,128)(2,1)S(1)}) custom-call(bf16[144,1024]{1,0:T(8,128)(2,1)S(1)} %get-tuple-element.66.refs_0_.mine_ref, bf16[144,1024]{1,0:T(8,128)(2,1)S(1)} %collective-permute-done.14.refs_3_.refs_7_.refs_1_, bf16[1024,2048]{1,0:T(8,128)(2,1)S(1)} %copy-done, bf16[1024,2048]{1,0:T(8,128)(2,1)S(1)} %copy-done.1), custom_call_target="tpu_custom_call" | custom-call | tf_op jit(solution)/shard_map/forward/pallas_call | solution.py:238
  42.5 0.5 collective-permute-done.15.refs_3_
  43.0 3.4 %backward.2 = (bf16[512,1024]{1,0:T(8,128)(2,1)S(1)}, bf16[512,1024]{1,0:T(8,128)(2,1)S(1)}) custom-call(bf16[512,576]{1,0:T(8,128)(2,1)S(1)} %turn.1.xt_ref, bf16[144,1024]{1,0:T(8,128)(2,1)S(1)} %join.3.refs_0_, bf16[144,1024]{1,0:T(8,128)(2,1)S(1)} %collective-permute-done.12.refs_2_.refs_1_, ...), custom_call_target="tpu_custom_call" | custom-call | flops 20000000000 | tf_op jit(solution)/shard_map/backward/pallas_call | solution.py:308
  46.4 3.2 %backward.3 = (bf16[512,1024]{1,0:T(8,128)(2,1)S(1)}, bf16[512,1024]{1,0:T(8,128)(2,1)S(1)}) custom-call(bf16[512,576]{1,0:T(8,128)(2,1)S(1)} %turn.1.xt_ref, bf16[144,1024]{1,0:T(8,128)(2,1)S(1)} %join.3.refs_0_, bf16[144,1024]{1,0:T(8,128)(2,1)S(1)} %collective-permute-done.12.refs_2_.refs_1_, ...), custom_call_target="tpu_custom_call" | custom-call | flops 20000000000 | tf_op jit(solution)/shard_map/backward/pallas_call | solution.py:308
  49.6 0.6 %collective-permute-start.17 = (bf16[512,1024]{1,0:T(8,128)(2,1)S(1)}, bf16[512,1024]{1,0:T(8,128)(2,1)S(1)}, u32[]{:S(2)}, u32[]{:S(2)}) collective-permute-start(bf16[512,1024]{1,0:T(8,128)(2,1)S(1)} %get-tuple-element.76), channel_id=1, source_target_pairs={{0,8},{8,0},{1,9},{9,1},{2,10},{10,2},{3,11},{11,3},{4,12},{12,4},... | collective-permute-start | bytes 3145736 | tf_op jit(solution)/shard_map/ppermute | solution.py:395
  50.2 1.0 %unpack.1.refs_0_ = bf16[128,1024]{1,0:T(8,128)(2,1)} custom-call(bf16[144,128]{1,0:T(8,128)(2,1)S(1)} %get-tuple-element.42.placer_ref, bf16[144,1024]{1,0:T(8,128)(2,1)S(1)} %get-tuple-element.66.refs_0_.mine_ref, bf16[144,1024]{1,0:T(8,128)(2,1)S(1)} %collective-permute-done.13.got_ref, bf16[512,1024]{1,0:T(8,128)(2,1)S(1)} %get-tuple-element.74.refs_0_, ...), custom_call_target="tpu_custom_call" | custom-call | flops 20000000000 | tf_op jit(solution)/shard_map/unpack/pallas_call | solution.py:384
  51.2 1.1 %finish.2 = (bf16[256,2048]{1,0:T(8,128)(2,1)}, bf16[256,2048]{1,0:T(8,128)(2,1)}) custom-call(bf16[128,1024]{1,0:T(8,128)(2,1)} %unpack.1.refs_0_, bf16[512,1024]{1,0:T(8,128)(2,1)S(1)} %get-tuple-element.73.refs_13_.refs_1_, bf16[512,1024]{1,0:T(8,128)(2,1)S(1)} %collective-permute-done.16.refs_1_.refs_2_), custom_call_target="tpu_custom_call" | custom-call | tf_op jit(solution)/shard_map/finish/pallas_call | solution.py:345
  52.4 0.1 collective-permute-done.17.refs_1_
  52.5 1.1 %finish.3 = (bf16[256,2048]{1,0:T(8,128)(2,1)}, bf16[256,2048]{1,0:T(8,128)(2,1)}) custom-call(bf16[512,1024]{1,0:T(8,128)(2,1)S(1)} %get-tuple-element.74.refs_0_, bf16[512,1024]{1,0:T(8,128)(2,1)S(1)} %collective-permute-done.17.refs_1_, bf16[256,2048]{1,0:T(8,128)(2,1)} %get-tuple-element.77.refs_2_, ...), custom_call_target="tpu_custom_call", output_to_operand_aliasing={{0}: (2, {}), {1}: (3, {})} | custom-call | tf_op jit(solution)/shard_map/finish/pallas_call | solution.py:345
  (27 shorter events, 0.4 us)
Async XLA Ops:
  2.1 12.5 %collective-permute-start = (bf16[36,1024]{1,0:T(8,128)(2,1)S(1)}, bf16[36,1024]{1,0:T(8,128)(2,1)S(1)}, u32[]{:S(2)}, u32[]{:S(2)}) collective-permute-start(bf16[36,1024]{1,0:T(8,128)(2,1)S(1)} %get-tuple-element.43), channel_id=1, source_target_pairs={{0,6},{2,4},{4,2},{6,0},{1,7},{3,5},{5,3},{7,1},{8,14},{10,12},{12... | collective-permute-start | bytes 221192 | tf_op jit(solution)/shard_map/ppermute | solution.py:400
  7.2 8.0 %collective-permute-start.1 = (bf16[36,1024]{1,0:T(8,128)(2,1)S(1)}, bf16[36,1024]{1,0:T(8,128)(2,1)S(1)}, u32[]{:S(2)}, u32[]{:S(2)}) collective-permute-start(bf16[36,1024]{1,0:T(8,128)(2,1)S(1)} %get-tuple-element.44), channel_id=1, source_target_pairs={{0,4},{2,6},{4,0},{6,2},{1,5},{3,7},{5,1},{7,3},{8,12},{10,14},{12... | collective-permute-start | bytes 221192 | tf_op jit(solution)/shard_map/ppermute | solution.py:400
  7.2 8.0 %collective-permute-start.2 = (bf16[36,1024]{1,0:T(8,128)(2,1)S(1)}, bf16[36,1024]{1,0:T(8,128)(2,1)S(1)}, u32[]{:S(2)}, u32[]{:S(2)}) collective-permute-start(bf16[36,1024]{1,0:T(8,128)(2,1)S(1)} %get-tuple-element.45), channel_id=1, source_target_pairs={{0,2},{2,0},{4,6},{6,4},{1,3},{3,1},{5,7},{7,5},{8,10},{10,8},{12,... | collective-permute-start | bytes 221192 | tf_op jit(solution)/shard_map/ppermute | solution.py:400
  7.9 10.7 %copy-start = (bf16[1024,2048]{1,0:T(8,128)(2,1)S(1)}, bf16[1024,2048]{1,0:T(8,128)(2,1)}, u32[]{:S(2)}) copy-start(bf16[1024,2048]{1,0:T(8,128)(2,1)} %refs_2_.7) | copy-start | bytes 12582916
  7.9 10.7 %copy-start.1 = (bf16[1024,2048]{1,0:T(8,128)(2,1)S(1)}, bf16[1024,2048]{1,0:T(8,128)(2,1)}, u32[]{:S(2)}) copy-start(bf16[1024,2048]{1,0:T(8,128)(2,1)} %refs_3_.5) | copy-start | bytes 12582916
  10.8 10.0 %collective-permute-start.8 = (bf16[36,1024]{1,0:T(8,128)(2,1)S(1)}, bf16[36,1024]{1,0:T(8,128)(2,1)S(1)}, u32[]{:S(2)}, u32[]{:S(2)}) collective-permute-start(bf16[36,1024]{1,0:T(8,128)(2,1)S(1)} %get-tuple-element.60), channel_id=1, source_target_pairs={{0,6},{2,4},{4,2},{6,0},{1,7},{3,5},{5,3},{7,1},{8,14},{10,12},{12... | collective-permute-start | bytes 221192 | tf_op jit(solution)/shard_map/ppermute | solution.py:400
  14.6 6.5 %collective-permute-start.9 = (bf16[36,1024]{1,0:T(8,128)(2,1)S(1)}, bf16[36,1024]{1,0:T(8,128)(2,1)S(1)}, u32[]{:S(2)}, u32[]{:S(2)}) collective-permute-start(bf16[36,1024]{1,0:T(8,128)(2,1)S(1)} %get-tuple-element.61), channel_id=1, source_target_pairs={{0,4},{2,6},{4,0},{6,2},{1,5},{3,7},{5,1},{7,3},{8,12},{10,14},{12... | collective-permute-start | bytes 221192 | tf_op jit(solution)/shard_map/ppermute | solution.py:400
  14.6 6.5 %collective-permute-start.10 = (bf16[36,1024]{1,0:T(8,128)(2,1)S(1)}, bf16[36,1024]{1,0:T(8,128)(2,1)S(1)}, u32[]{:S(2)}, u32[]{:S(2)}) collective-permute-start(bf16[36,1024]{1,0:T(8,128)(2,1)S(1)} %get-tuple-element.62), channel_id=1, source_target_pairs={{0,2},{2,0},{4,6},{6,4},{1,3},{3,1},{5,7},{7,5},{8,10},{10,8},{12,... | collective-permute-start | bytes 221192 | tf_op jit(solution)/shard_map/ppermute | solution.py:400
  15.3 8.9 %collective-permute-start.4 = (bf16[144,1024]{1,0:T(8,128)(2,1)S(1)}, bf16[144,1024]{1,0:T(8,128)(2,1)S(1)}, u32[]{:S(2)}, u32[]{:S(2)}) collective-permute-start(bf16[144,1024]{1,0:T(8,128)(2,1)S(1)} %join.2.refs_0_.refs_4_), channel_id=1, source_target_pairs={{0,1},{1,0},{2,3},{3,2},{4,5},{5,4},{6,7},{7,6},{8,9},{9,8},{10,11... | collective-permute-start | bytes 884744 | tf_op jit(solution)/shard_map/ppermute | solution.py:395
  17.0 7.5 %collective-permute-start.3 = (bf16[144,1024]{1,0:T(8,128)(2,1)S(1)}, bf16[144,1024]{1,0:T(8,128)(2,1)S(1)}, u32[]{:S(2)}, u32[]{:S(2)}) collective-permute-start(bf16[144,1024]{1,0:T(8,128)(2,1)S(1)} %join.2.refs_0_.refs_4_), channel_id=1, source_target_pairs={{0,16},{16,0},{1,17},{17,1},{2,18},{18,2},{3,19},{19,3},{4,20},{20... | collective-permute-start | bytes 884744 | tf_op jit(solution)/shard_map/ppermute | solution.py:395
  21.2 11.6 %collective-permute-start.11 = (bf16[144,1024]{1,0:T(8,128)(2,1)S(1)}, bf16[144,1024]{1,0:T(8,128)(2,1)S(1)}, u32[]{:S(2)}, u32[]{:S(2)}) collective-permute-start(bf16[144,1024]{1,0:T(8,128)(2,1)S(1)} %join.3.refs_0_), channel_id=1, source_target_pairs={{0,16},{16,0},{1,17},{17,1},{2,18},{18,2},{3,19},{19,3},{4,20},{20... | collective-permute-start | bytes 884744 | tf_op jit(solution)/shard_map/ppermute | solution.py:395
  22.7 11.8 %collective-permute-start.12 = (bf16[144,1024]{1,0:T(8,128)(2,1)S(1)}, bf16[144,1024]{1,0:T(8,128)(2,1)S(1)}, u32[]{:S(2)}, u32[]{:S(2)}) collective-permute-start(bf16[144,1024]{1,0:T(8,128)(2,1)S(1)} %join.3.refs_0_), channel_id=1, source_target_pairs={{0,1},{1,0},{2,3},{3,2},{4,5},{5,4},{6,7},{7,6},{8,9},{9,8},{10,11... | collective-permute-start | bytes 884744 | tf_op jit(solution)/shard_map/ppermute | solution.py:395
  26.8 9.4 %collective-permute-start.5 = (bf16[72,1024]{1,0:T(8,128)(2,1)S(1)}, bf16[72,1024]{1,0:T(8,128)(2,1)S(1)}, u32[]{:S(2)}, u32[]{:S(2)}) collective-permute-start(bf16[72,1024]{1,0:T(8,128)(2,1)S(1)} %get-tuple-element.51), channel_id=1, source_target_pairs={{0,2},{2,0},{4,6},{6,4},{1,3},{3,1},{5,7},{7,5},{8,10},{10,8},{12,... | collective-permute-start | bytes 442376 | tf_op jit(solution)/shard_map/ppermute | solution.py:400
  30.3 9.9 %collective-permute-start.6 = (bf16[72,1024]{1,0:T(8,128)(2,1)S(1)}, bf16[72,1024]{1,0:T(8,128)(2,1)S(1)}, u32[]{:S(2)}, u32[]{:S(2)}) collective-permute-start(bf16[72,1024]{1,0:T(8,128)(2,1)S(1)} %get-tuple-element.52), channel_id=1, source_target_pairs={{0,4},{2,6},{4,0},{6,2},{1,5},{3,7},{5,1},{7,3},{8,12},{10,14},{12... | collective-permute-start | bytes 442376 | tf_op jit(solution)/shard_map/ppermute | solution.py:400
  32.3 7.9 %collective-permute-start.7 = (bf16[72,1024]{1,0:T(8,128)(2,1)S(1)}, bf16[72,1024]{1,0:T(8,128)(2,1)S(1)}, u32[]{:S(2)}, u32[]{:S(2)}) collective-permute-start(bf16[72,1024]{1,0:T(8,128)(2,1)S(1)} %get-tuple-element.53), channel_id=1, source_target_pairs={{0,6},{2,4},{4,2},{6,0},{1,7},{3,5},{5,3},{7,1},{8,14},{10,12},{12... | collective-permute-start | bytes 442376 | tf_op jit(solution)/shard_map/ppermute | solution.py:400
  32.8 7.9 %collective-permute-start.14 = (bf16[144,1024]{1,0:T(8,128)(2,1)S(1)}, bf16[144,1024]{1,0:T(8,128)(2,1)S(1)}, u32[]{:S(2)}, u32[]{:S(2)}) collective-permute-start(bf16[144,1024]{1,0:T(8,128)(2,1)S(1)} %relay.4.refs_1_), channel_id=1, source_target_pairs={{0,16},{16,0},{1,17},{17,1},{2,18},{18,2},{3,19},{19,3},{4,20},{20... | collective-permute-start | bytes 884744 | tf_op jit(solution)/shard_map/ppermute | solution.py:395
  34.5 8.4 %collective-permute-start.15 = (bf16[144,1024]{1,0:T(8,128)(2,1)S(1)}, bf16[144,1024]{1,0:T(8,128)(2,1)S(1)}, u32[]{:S(2)}, u32[]{:S(2)}) collective-permute-start(bf16[144,1024]{1,0:T(8,128)(2,1)S(1)} %relay.5.refs_0_), channel_id=1, source_target_pairs={{0,1},{1,0},{2,3},{3,2},{4,5},{5,4},{6,7},{7,6},{8,9},{9,8},{10,11... | collective-permute-start | bytes 884744 | tf_op jit(solution)/shard_map/ppermute | solution.py:395
  40.3 9.9 %collective-permute-start.13 = (bf16[144,1024]{1,0:T(8,128)(2,1)S(1)}, bf16[144,1024]{1,0:T(8,128)(2,1)S(1)}, u32[]{:S(2)}, u32[]{:S(2)}) collective-permute-start(bf16[144,1024]{1,0:T(8,128)(2,1)S(1)} %get-tuple-element.67), channel_id=1, source_target_pairs={{0,1},{1,0},{2,3},{3,2},{4,5},{5,4},{6,7},{7,6},{8,9},{9,8},{10,11... | collective-permute-start | bytes 884744 | tf_op jit(solution)/shard_map/ppermute | solution.py:395
  46.4 3.8 %collective-permute-start.16 = (bf16[512,1024]{1,0:T(8,128)(2,1)S(1)}, bf16[512,1024]{1,0:T(8,128)(2,1)S(1)}, u32[]{:S(2)}, u32[]{:S(2)}) collective-permute-start(bf16[512,1024]{1,0:T(8,128)(2,1)S(1)} %get-tuple-element.75), channel_id=1, source_target_pairs={{0,8},{8,0},{1,9},{9,1},{2,10},{10,2},{3,11},{11,3},{4,12},{12,4},... | collective-permute-start | bytes 3145736 | tf_op jit(solution)/shard_map/ppermute | solution.py:395
  49.6 2.8 %collective-permute-start.17 = (bf16[512,1024]{1,0:T(8,128)(2,1)S(1)}, bf16[512,1024]{1,0:T(8,128)(2,1)S(1)}, u32[]{:S(2)}, u32[]{:S(2)}) collective-permute-start(bf16[512,1024]{1,0:T(8,128)(2,1)S(1)} %get-tuple-element.76), channel_id=1, source_target_pairs={{0,8},{8,0},{1,9},{9,1},{2,10},{10,2},{3,11},{11,3},{4,12},{12,4},... | collective-permute-start | bytes 3145736 | tf_op jit(solution)/shard_map/ppermute | solution.py:395

commit v15 on v14

--- a/solution.py
+++ b/solution.py
@@ -126,19 +126,19 @@
     )(*values, *earlier)
 
 
-def mark_kernel(value_ref, mark_ref):
+def mark_kernel(value_ref, _, mark_ref):
     mark_ref[...] = value_ref[: mark_ref.shape[0], : mark_ref.shape[1]]
 
 
-def mark(value):
+def mark(value, earlier):
     return pl.pallas_call(
         mark_kernel,
         out_shape=jax.ShapeDtypeStruct((16, 128), value.dtype),
-        in_specs=[HERE],
+        in_specs=[HERE, ANYWHERE],
         compiler_params=SMALL,
         cost_estimate=CHEAP,
         name="mark",
-    )(value)
+    )(value, earlier)
 
 
 def flip_kernel(source_ref, here_ref, flipped_ref, sems):
@@ -277,43 +277,58 @@
     )(own, sib, *xs, *xs)
 
 
-def backward_kernel(first, counts, xt_ref, *refs):
-    n = len(counts)
-    gs, acts, coefs = refs[:4], refs[4 : 4 + n], refs[4 + n : 4 + 2 * n]
-    wdt_ref, *_, own_ref, sib_ref, g_ref = refs[4 + 2 * n :]
+def slopes_kernel(n, *refs):
+    gs, acts, coefs = refs[:n], refs[n : 2 * n], refs[2 * n : 3 * n]
+    wdt_ref, dg_ref, du_ref, g_ref = refs[3 * n :]
     part = gs[0].shape[0]
+    for i in range(n):
+        g_ref[i * part : (i + 1) * part, :] = gs[i][...]
+    for start in range(0, wdt_ref.shape[1], STRIP):
+        cols = slice(start, start + STRIP)
+        d_hidden = jnp.dot(g_ref[...], wdt_ref[:, cols], preferred_element_type=F32)
+        for i in range(n):
+            rows = slice(i * part, (i + 1) * part)
+            dg_ref[rows, cols] = (d_hidden[rows] * coefs[i][:, cols].astype(F32)).astype(BF16)
+            du_ref[rows, cols] = (d_hidden[rows] * acts[i][:, cols].astype(F32)).astype(BF16)
+
+
+def slopes(gs, acts, coefs, wdt):
+    n, (part, width) = len(gs), gs[0].shape
+    return pl.pallas_call(
+        functools.partial(slopes_kernel, n),
+        out_shape=[jax.ShapeDtypeStruct((n * part, wdt.shape[1]), BF16)] * 2,
+        in_specs=[HERE] * (3 * n + 1),
+        scratch_shapes=[pltpu.VMEM((n * part, width), BF16)],
+        compiler_params=LARGE,
+        cost_estimate=CHEAP,
+        name="slopes",
+    )(*gs, *acts, *coefs, wdt)
+
+
+def backward_kernel(first, xt_ref, g_ref, act_ref, coef_ref, dg_ref, du_ref, wdt_ref, *refs):
+    own_ref, sib_ref = refs[-2:]
     share = own_ref.shape[0] // 2
-    for i in range(4):
-        g_ref[i * part : (i + 1) * part, :] = gs[i][...]
-
-    def strip(start):
-        here = pl.ds(pl.multiple_of(start, STRIP), STRIP)
-        cols = pl.ds(pl.multiple_of(start + first, STRIP), STRIP)
+    for start in range(0, own_ref.shape[1], STRIP):
+        here = slice(start, start + STRIP)
+        cols = slice(first + start, first + start + STRIP)
         d_hidden = jnp.dot(g_ref[...], wdt_ref[:, cols], preferred_element_type=F32)
-        for row, parts in ((0, coefs), (share, acts)):
-            factor = jnp.concatenate([p[:, cols] for p in parts], axis=0).astype(F32)
-            d_cols = (d_hidden * factor).astype(BF16)
+        for row, factor_ref, known_ref in ((0, coef_ref, dg_ref), (share, act_ref, du_ref)):
+            d_cols = (d_hidden * factor_ref[:, cols].astype(F32)).astype(BF16)
+            d_cols = jnp.concatenate([known_ref[:, cols], d_cols], axis=0)
             total = jnp.dot(xt_ref[...], d_cols, preferred_element_type=F32).astype(BF16)
             own_ref[row : row + share, here] = total[:share]
             sib_ref[row : row + share, here] = total[share:]
 
-    for start in range(0, own_ref.shape[1], STRIP):
-        strip(start)
-
-
-def backward(xt, gs, acts, coefs, wdt, first, cols, earlier=()):
-    part, width = gs[0].shape
-    height, rows = xt.shape
-    counts = tuple(a.shape[0] for a in acts)
-    return pl.pallas_call(
-        functools.partial(backward_kernel, first, counts),
-        out_shape=[jax.ShapeDtypeStruct((height, cols), BF16)] * 2,
-        in_specs=[HERE] * (6 + 2 * len(acts)) + [ANYWHERE] * len(earlier),
-        scratch_shapes=[pltpu.VMEM((rows, width), BF16)],
+
+def backward(xt, g, act, coef, dg, du, wdt, first, cols, earlier=()):
+    return pl.pallas_call(
+        functools.partial(backward_kernel, first),
+        out_shape=[jax.ShapeDtypeStruct((xt.shape[0], cols), BF16)] * 2,
+        in_specs=[HERE] * 7 + [ANYWHERE] * len(earlier),
         compiler_params=LARGE,
         cost_estimate=DEAR,
         name="backward",
-    )(xt, *gs, *acts, *coefs, wdt, *earlier)
+    )(xt, g, act, coef, dg, du, wdt, *earlier)
 
 
 def finish_kernel(spans, more, unused, *refs):
@@ -423,23 +438,23 @@
     act0, coef0, share_own = forward([x_own], wg, wu, wd)
     g_own = join(moved, [act0])
     g_far, g_near = swap(g_own, "far"), swap(g_own, "half")
-    act1, coef1, *shares = forward([x_near], wg, wu, wd, other=share_own, earlier=[x_far])
-    (x_pass,) = relay([x_near], [mark(act1), g_far])
+    act1, coef1, *shares = forward([x_near], wg, wu, wd, other=share_own)
+    (x_pass,) = relay([x_near], [mark(act1, x_far), g_far])
     (g_pass,) = relay([g_far], [x_pass, g_near])
     x_corner, g_corner = swap(x_pass, "far"), swap(g_pass, "half")
     returned = across_planes(shares)
     act2, coef2 = forward([x_far], wg, wu, earlier=[g_pass], cost=DEAR)
-    mine, theirs = split(returned, [act2])
+    dg, du = slopes([g_own, g_near, g_far], [act0, act1, act2], [coef0, coef1, coef2], wdt)
+    mine, theirs = split(returned, [dg])
     got = swap(theirs, "half")
     act3, coef3 = forward([x_corner], wg, wu, earlier=[mine])
     xt = turn(*scalars[1:], [x_own, x_near, x_far, x_corner], share)
 
-    gs = [g_own, g_near, g_far, g_corner]
-    acts, coefs = [act0, act1, act2, act3], [coef0, coef1, coef2, coef3]
+    rest = (xt, g_corner, act3, coef3, dg, du, wdt)
     cols = w_down.shape[0]
     cut = cols // 2
-    own0, sib0 = backward(xt, gs, acts, coefs, wdt, 0, cut)
-    own1, sib1 = backward(xt, gs, acts, coefs, wdt, cut, cols - cut, [own0])
+    own0, sib0 = backward(*rest, 0, cut)
+    own1, sib1 = backward(*rest, cut, cols - cut, [own0])
     got0, got1 = swap(sib0, "core"), swap(sib1, "core")
     outputs = unpack(placer, mine, got, [own1, got0])
     held = finish([own0], [got0], (0,), cols, earlier=[outputs])

time: 53.9 us -> 51.3 us (0.952)
  waiting for transfers between devices: 5.27 us -> 2.71 us
    ppermute x9, waiting for transfers between devices: 4.36 us -> 2.56 us  [across_planes(): lax.ppermute(blocks[k], 'arch', [(i, i ^ k) for i in range(EXPERTS)])]
    ppermute x9, starting transfers between devices: 16.2 us -> 14.7 us  [across_planes(): lax.ppermute(blocks[k], 'arch', [(i, i ^ k) for i in range(EXPERTS)])]
    ppermute x9, starting transfers between devices: 9.02 us -> 10.5 us  [swap(): return lax.ppermute(value, axis, [(0, 1), (1, 0)])]
    ppermute x9, waiting for transfers between devices: 0.92 us -> 0.15 us  [swap(): return lax.ppermute(value, axis, [(0, 1), (1, 0)])]
    pallas_call x2 -> x3, Pallas kernels: 6.55 us -> 6.63 us  [the longest x2 4.44 us: backward(): pl.pallas_call(functools.partial(backward_kernel, first), out_shape=[jax....]
  transfers between devices with their start and end apart: 18 -> 18, of which waited for: 5 -> 3; matrix products, arithmetic and copies ran while one was open for 0% -> 0% of each run, Pallas kernels for 37% -> 39%
where the time goes in v15:
time: 51.3 us; the launch traced here: 51.2 us
  starting transfers between devices  25.1 us (49%)
  Pallas kernels  22.3 us (43%)
  waiting for transfers between devices  2.71 us (5%)
  between operations  0.97 us (2%)
    ppermute x9, starting transfers between devices, across_planes(): lax.ppermute(blocks[k], 'arch', [(i, i ^ k) for i in range(EXPERTS)])  14.7 us
    ppermute x9, starting transfers between devices, swap(): return lax.ppermute(value, axis, [(0, 1), (1, 0)])  10.5 us
    pallas_call x4, Pallas kernels, forward(): pl.pallas_call(functools.partial(forward_kernel, n, fetch, down, pair, le...  7.63 us
    pallas_call x2, Pallas kernels, backward(): pl.pallas_call(functools.partial(backward_kernel, first), out_shape=[jax....  4.44 us
    pallas_call x1, Pallas kernels, flip(): pl.pallas_call(flip_kernel, out_shape=[pltpu.VMEM(value.shape, value.dtyp...  2.88 us
    ppermute x9, waiting for transfers between devices, across_planes(): lax.ppermute(blocks[k], 'arch', [(i, i ^ k) for i in range(EXPERTS)])  2.56 us
    pallas_call x2, Pallas kernels, finish(): pl.pallas_call(functools.partial(finish_kernel, spans, more, len(earlier)...  2.2 us
    pallas_call x1, Pallas kernels, slopes(): pl.pallas_call(functools.partial(slopes_kernel, n), out_shape=[jax.ShapeD...  2.19 us
  transfers between devices with their start and end apart: 18, of which 3 were waited for; matrix products, arithmetic and copies ran while one was open for 0% of the time, Pallas kernels for 39%

profile of v15, /device:TPU:0, one launch (start us, length us, event | category | flops | bytes accessed | tf_op | source)
XLA Modules:
  0.0 51.2 jit_solution(12056664485876056678)
XLA Ops:
  0.6 1.5 %pack.1 = (bf16[144,128]{1,0:T(8,128)(2,1)S(1)}, bf16[36,1024]{1,0:T(8,128)(2,1)S(1)}, bf16[36,1024]{1,0:T(8,128)(2,1)S(1)}, bf16[36,1024]{1,0:T(8,128)(2,1)S(1)...) custom-call(s32[1]{0:T(128)} %bitcast.plane_ref, ...), custom_call_target="tpu_custom_call" | custom-call | tf_op jit(solution)/shard_map/pack/pallas_call | solution.py:79
  2.1 5.1 %collective-permute-start = (bf16[36,1024]{1,0:T(8,128)(2,1)S(1)}, bf16[36,1024]{1,0:T(8,128)(2,1)S(1)}, u32[]{:S(2)}, u32[]{:S(2)}) collective-permute-start(bf16[36,1024]{1,0:T(8,128)(2,1)S(1)} %get-tuple-element.45), channel_id=1, source_target_pairs={{0,6},{2,4},{4,2},{6,0},{1,7},{3,5},{5,3},{7,1},{8,14},{10,12},{12... | collective-permute-start | bytes 221192 | tf_op jit(solution)/shard_map/ppermute | solution.py:415
  7.2 0.6 %collective-permute-start.2 = (bf16[36,1024]{1,0:T(8,128)(2,1)S(1)}, bf16[36,1024]{1,0:T(8,128)(2,1)S(1)}, u32[]{:S(2)}, u32[]{:S(2)}) collective-permute-start(bf16[36,1024]{1,0:T(8,128)(2,1)S(1)} %get-tuple-element.47), channel_id=1, source_target_pairs={{0,2},{2,0},{4,6},{6,4},{1,3},{3,1},{5,7},{7,5},{8,10},{10,8},{12,... | collective-permute-start | bytes 221192 | tf_op jit(solution)/shard_map/ppermute | solution.py:415
  7.9 2.9 %flip.1 = (bf16[2048,1024]{1,0:T(8,128)(2,1)S(1)}, bf16[1024,2048]{1,0:T(8,128)(2,1)S(1)}) custom-call(bf16[2048,1024]{1,0:T(8,128)(2,1)} %source_ref), custom_call_target="tpu_custom_call" | custom-call | tf_op jit(solution)/shard_map/flip/pallas_call | solution.py:158
  10.8 3.8 %collective-permute-start.7 = (bf16[36,1024]{1,0:T(8,128)(2,1)S(1)}, bf16[36,1024]{1,0:T(8,128)(2,1)S(1)}, u32[]{:S(2)}, u32[]{:S(2)}) collective-permute-start(bf16[36,1024]{1,0:T(8,128)(2,1)S(1)} %get-tuple-element.62), channel_id=1, source_target_pairs={{0,6},{2,4},{4,2},{6,0},{1,7},{3,5},{5,3},{7,1},{8,14},{10,12},{12... | collective-permute-start | bytes 221192 | tf_op jit(solution)/shard_map/ppermute | solution.py:415
  14.6 0.6 %collective-permute-start.9 = (bf16[36,1024]{1,0:T(8,128)(2,1)S(1)}, bf16[36,1024]{1,0:T(8,128)(2,1)S(1)}, u32[]{:S(2)}, u32[]{:S(2)}) collective-permute-start(bf16[36,1024]{1,0:T(8,128)(2,1)S(1)} %get-tuple-element.64), channel_id=1, source_target_pairs={{0,2},{2,0},{4,6},{6,4},{1,3},{3,1},{5,7},{7,5},{8,10},{10,8},{12,... | collective-permute-start | bytes 221192 | tf_op jit(solution)/shard_map/ppermute | solution.py:415
  15.3 1.7 %collective-permute-start.3 = (bf16[144,1024]{1,0:T(8,128)(2,1)S(1)}, bf16[144,1024]{1,0:T(8,128)(2,1)S(1)}, u32[]{:S(2)}, u32[]{:S(2)}) collective-permute-start(bf16[144,1024]{1,0:T(8,128)(2,1)S(1)} %join.2.refs_0_.refs_4_), channel_id=1, source_target_pairs={{0,1},{1,0},{2,3},{3,2},{4,5},{5,4},{6,7},{7,6},{8,9},{9,8},{10,11... | collective-permute-start | bytes 884744 | tf_op jit(solution)/shard_map/ppermute | solution.py:410
  17.0 1.5 %collective-permute-start.12 = (bf16[144,1024]{1,0:T(8,128)(2,1)S(1)}, bf16[144,1024]{1,0:T(8,128)(2,1)S(1)}, u32[]{:S(2)}, u32[]{:S(2)}) collective-permute-start(bf16[144,1024]{1,0:T(8,128)(2,1)S(1)} %join.2.refs_0_.refs_4_), channel_id=1, source_target_pairs={{0,16},{16,0},{1,17},{17,1},{2,18},{18,2},{3,19},{19,3},{4,20},{20... | collective-permute-start | bytes 884744 | tf_op jit(solution)/shard_map/ppermute | solution.py:410
  18.5 2.2 %forward_down.2 = (bf16[144,2048]{1,0:T(8,128)(2,1)S(1)}, bf16[144,2048]{1,0:T(8,128)(2,1)S(1)}, bf16[144,1024]{1,0:T(8,128)(2,1)S(1)}) custom-call(bf16[144,1024]{1,0:T(8,128)(2,1)S(1)} %join.2.refs_0_.refs_4_, bf16[1024,2048]{1,0:T(8,128)(2,1)S(1)} %copy-done, bf16[1024,2048]{1,0:T(8,128)(2,1)S(1)} %copy-done.1, ...), custom_call_target="tpu_custom_call" | custom-call | tf_op jit(solution)/shard_map/forward_down/pallas_call | solution.py:238
  20.8 0.3 collective-permute-done.8.refs_2_
  21.2 1.6 %collective-permute-start.11 = (bf16[144,1024]{1,0:T(8,128)(2,1)S(1)}, bf16[144,1024]{1,0:T(8,128)(2,1)S(1)}, u32[]{:S(2)}, u32[]{:S(2)}) collective-permute-start(bf16[144,1024]{1,0:T(8,128)(2,1)S(1)} %join.3.refs_0_), channel_id=1, source_target_pairs={{0,16},{16,0},{1,17},{17,1},{2,18},{18,2},{3,19},{19,3},{4,20},{20... | collective-permute-start | bytes 884744 | tf_op jit(solution)/shard_map/ppermute | solution.py:410
  22.7 1.5 %collective-permute-start.10 = (bf16[144,1024]{1,0:T(8,128)(2,1)S(1)}, bf16[144,1024]{1,0:T(8,128)(2,1)S(1)}, u32[]{:S(2)}, u32[]{:S(2)}) collective-permute-start(bf16[144,1024]{1,0:T(8,128)(2,1)S(1)} %join.3.refs_0_), channel_id=1, source_target_pairs={{0,1},{1,0},{2,3},{3,2},{4,5},{5,4},{6,7},{7,6},{8,9},{9,8},{10,11... | collective-permute-start | bytes 884744 | tf_op jit(solution)/shard_map/ppermute | solution.py:410
  24.2 2.2 %forward_down.3 = (bf16[144,2048]{1,0:T(8,128)(2,1)S(1)}, bf16[144,2048]{1,0:T(8,128)(2,1)S(1)}, bf16[72,1024]{1,0:T(8,128)(2,1)S(1)}, bf16[72,1024]{1,0:T(8,128...) custom-call(bf16[144,1024]{1,0:T(8,128)(2,1)S(1)} %collective-permute-done.3.refs_0_.refs_1_.refs_5_, ...), custom_call_target="tpu_custom_call" | custom-call | tf_op jit(solution)/shard_map/forward_down/pallas_call | solution.py:238
  26.5 0.5 collective-permute-start.4
  27.0 2.9 %collective-permute-start.5 = (bf16[72,1024]{1,0:T(8,128)(2,1)S(1)}, bf16[72,1024]{1,0:T(8,128)(2,1)S(1)}, u32[]{:S(2)}, u32[]{:S(2)}) collective-permute-start(bf16[72,1024]{1,0:T(8,128)(2,1)S(1)} %get-tuple-element.54), channel_id=1, source_target_pairs={{0,4},{2,6},{4,0},{6,2},{1,5},{3,7},{5,1},{7,3},{8,12},{10,14},{12... | collective-permute-start | bytes 442376 | tf_op jit(solution)/shard_map/ppermute | solution.py:415
  29.8 1.1 %collective-permute-start.6 = (bf16[72,1024]{1,0:T(8,128)(2,1)S(1)}, bf16[72,1024]{1,0:T(8,128)(2,1)S(1)}, u32[]{:S(2)}, u32[]{:S(2)}) collective-permute-start(bf16[72,1024]{1,0:T(8,128)(2,1)S(1)} %get-tuple-element.55), channel_id=1, source_target_pairs={{0,6},{2,4},{4,2},{6,0},{1,7},{3,5},{5,3},{7,1},{8,14},{10,12},{12... | collective-permute-start | bytes 442376 | tf_op jit(solution)/shard_map/ppermute | solution.py:415
  31.0 0.9 %collective-permute-start.14 = (bf16[144,1024]{1,0:T(8,128)(2,1)S(1)}, bf16[144,1024]{1,0:T(8,128)(2,1)S(1)}, u32[]{:S(2)}, u32[]{:S(2)}) collective-permute-start(bf16[144,1024]{1,0:T(8,128)(2,1)S(1)} %relay.4.refs_1_), channel_id=1, source_target_pairs={{0,16},{16,0},{1,17},{17,1},{2,18},{18,2},{3,19},{19,3},{4,20},{20... | collective-permute-start | bytes 884744 | tf_op jit(solution)/shard_map/ppermute | solution.py:410
  31.9 1.9 %collective-permute-start.15 = (bf16[144,1024]{1,0:T(8,128)(2,1)S(1)}, bf16[144,1024]{1,0:T(8,128)(2,1)S(1)}, u32[]{:S(2)}, u32[]{:S(2)}) collective-permute-start(bf16[144,1024]{1,0:T(8,128)(2,1)S(1)} %relay.5.refs_0_), channel_id=1, source_target_pairs={{0,1},{1,0},{2,3},{3,2},{4,5},{5,4},{6,7},{7,6},{8,9},{9,8},{10,11... | collective-permute-start | bytes 884744 | tf_op jit(solution)/shard_map/ppermute | solution.py:410
  33.8 1.6 %forward.2 = (bf16[144,2048]{1,0:T(8,128)(2,1)S(1)}, bf16[144,2048]{1,0:T(8,128)(2,1)S(1)}) custom-call(bf16[144,1024]{1,0:T(8,128)(2,1)S(1)} %relay.5.refs_0_, bf16[144,1024]{1,0:T(8,128)(2,1)S(1)} %collective-permute-done.12._.refs_1_.refs_2_.refs_6_, bf16[1024,2048]{1,0:T(8,128)(2,1)S(1)} %copy-done, bf16[1024,2048]{1,0:T(8,128)(2,1)S(1)} %copy-done.1), custom_call_target="tpu_custom_call" | custom-call | flops 20000000000 | tf_op jit(solution)/shard_map/forward/pallas_call | solution.py:238
  35.4 2.2 %slopes.1 = (bf16[432,2048]{1,0:T(8,128)(2,1)S(1)}, bf16[432,2048]{1,0:T(8,128)(2,1)S(1)}) custom-call(bf16[144,1024]{1,0:T(8,128)(2,1)S(1)} %join.3.refs_0_, bf16[144,1024]{1,0:T(8,128)(2,1)S(1)} %collective-permute-done.10.refs_2_.refs_1_, bf16[144,1024]{1,0:T(8,128)(2,1)S(1)} %collective-permute-done.11.refs_2_.refs_0_, ...), custom_call_target="tpu_custom_call" | custom-call | tf_op jit(solution)/shard_map/slopes/pallas_call | solution.py:297
  37.6 2.2 %collective-permute-done.5.refs_2_ = bf16[72,1024]{1,0:T(8,128)(2,1)S(1)} collective-permute-done((bf16[72,1024]{1,0:T(8,128)(2,1)S(1)}, bf16[72,1024]{1,0:T(8,128)(2,1)S(1)}, u32[]{:S(2)}, u32[]{:S(2)}) %collective-permute-start.5) | collective-permute-done | bytes 147488 | tf_op jit(solution)/shard_map/ppermute | solution.py:415
  39.9 0.1 split.1
  39.9 0.7 %collective-permute-start.13 = (bf16[144,1024]{1,0:T(8,128)(2,1)S(1)}, bf16[144,1024]{1,0:T(8,128)(2,1)S(1)}, u32[]{:S(2)}, u32[]{:S(2)}) collective-permute-start(bf16[144,1024]{1,0:T(8,128)(2,1)S(1)} %get-tuple-element.73), channel_id=1, source_target_pairs={{0,1},{1,0},{2,3},{3,2},{4,5},{5,4},{6,7},{7,6},{8,9},{9,8},{10,11... | collective-permute-start | bytes 884744 | tf_op jit(solution)/shard_map/ppermute | solution.py:410
  40.7 0.2 turn.1.xt_ref
  40.9 1.6 %forward.3 = (bf16[144,2048]{1,0:T(8,128)(2,1)S(1)}, bf16[144,2048]{1,0:T(8,128)(2,1)S(1)}) custom-call(bf16[144,1024]{1,0:T(8,128)(2,1)S(1)} %get-tuple-element.72.refs_0_.mine_ref, bf16[144,1024]{1,0:T(8,128)(2,1)S(1)} %collective-permute-done.14.refs_3_.refs_7_.refs_1_, bf16[1024,2048]{1,0:T(8,128)(2,1)S(1)} %copy-done, bf16[1024,2048]{1,0:T(8,128)(2,1)S(1)} %copy-done.1), custom_call_target="tpu_custom_call" | custom-call | tf_op jit(solution)/shard_map/forward/pallas_call | solution.py:238
  42.5 2.3 %backward.2 = (bf16[512,1024]{1,0:T(8,128)(2,1)S(1)}, bf16[512,1024]{1,0:T(8,128)(2,1)S(1)}) custom-call(bf16[512,576]{1,0:T(8,128)(2,1)S(1)} %turn.1.xt_ref, bf16[144,1024]{1,0:T(8,128)(2,1)S(1)} %collective-permute-done.15.g_ref, bf16[144,2048]{1,0:T(8,128)(2,1)S(1)} %get-tuple-element.74.act_ref, bf16[144,2048]{1,0:T(8,128)(2,1)S(1)} %get-tuple-element.75.coef_ref, ...), custom_call_target="tpu_custom_call" | custom-call | flops 20000000000 | tf_op jit(solution)/shard_map/backward/pallas_call | solution.py:324
  44.9 2.1 %backward.3 = (bf16[512,1024]{1,0:T(8,128)(2,1)S(1)}, bf16[512,1024]{1,0:T(8,128)(2,1)S(1)}) custom-call(bf16[512,576]{1,0:T(8,128)(2,1)S(1)} %turn.1.xt_ref, bf16[144,1024]{1,0:T(8,128)(2,1)S(1)} %collective-permute-done.15.g_ref, bf16[144,2048]{1,0:T(8,128)(2,1)S(1)} %get-tuple-element.74.act_ref, bf16[144,2048]{1,0:T(8,128)(2,1)S(1)} %get-tuple-element.75.coef_ref, ...), custom_call_target="tpu_custom_call" | custom-call | flops 20000000000 | tf_op jit(solution)/shard_map/backward/pallas_call | solution.py:324
  47.0 0.6 %collective-permute-start.17 = (bf16[512,1024]{1,0:T(8,128)(2,1)S(1)}, bf16[512,1024]{1,0:T(8,128)(2,1)S(1)}, u32[]{:S(2)}, u32[]{:S(2)}) collective-permute-start(bf16[512,1024]{1,0:T(8,128)(2,1)S(1)} %get-tuple-element.80), channel_id=1, source_target_pairs={{0,8},{8,0},{1,9},{9,1},{2,10},{10,2},{3,11},{11,3},{4,12},{12,4},... | collective-permute-start | bytes 3145736 | tf_op jit(solution)/shard_map/ppermute | solution.py:410
  47.6 1.0 %unpack.1.refs_0_ = bf16[128,1024]{1,0:T(8,128)(2,1)} custom-call(bf16[144,128]{1,0:T(8,128)(2,1)S(1)} %get-tuple-element.44.placer_ref, bf16[144,1024]{1,0:T(8,128)(2,1)S(1)} %get-tuple-element.72.refs_0_.mine_ref, bf16[144,1024]{1,0:T(8,128)(2,1)S(1)} %collective-permute-done.13.got_ref, bf16[512,1024]{1,0:T(8,128)(2,1)S(1)} %get-tuple-element.78.refs_0_, ...), custom_call_target="tpu_custom_call" | custom-call | flops 20000000000 | tf_op jit(solution)/shard_map/unpack/pallas_call | solution.py:399
  48.7 1.1 %finish.2 = (bf16[256,2048]{1,0:T(8,128)(2,1)}, bf16[256,2048]{1,0:T(8,128)(2,1)}) custom-call(bf16[128,1024]{1,0:T(8,128)(2,1)} %unpack.1.refs_0_, bf16[512,1024]{1,0:T(8,128)(2,1)S(1)} %get-tuple-element.77.refs_0_.refs_1_, bf16[512,1024]{1,0:T(8,128)(2,1)S(1)} %collective-permute-done.16.refs_1_.refs_2_), custom_call_target="tpu_custom_call" | custom-call | tf_op jit(solution)/shard_map/finish/pallas_call | solution.py:360
  49.8 0.1 collective-permute-done.17.refs_1_
  49.9 1.1 %finish.3 = (bf16[256,2048]{1,0:T(8,128)(2,1)}, bf16[256,2048]{1,0:T(8,128)(2,1)}) custom-call(bf16[512,1024]{1,0:T(8,128)(2,1)S(1)} %get-tuple-element.78.refs_0_, bf16[512,1024]{1,0:T(8,128)(2,1)S(1)} %collective-permute-done.17.refs_1_, bf16[256,2048]{1,0:T(8,128)(2,1)} %get-tuple-element.81.refs_2_, ...), custom_call_target="tpu_custom_call", output_to_operand_aliasing={{0}: (2, {}), {1}: (3, {})} | custom-call | tf_op jit(solution)/shard_map/finish/pallas_call | solution.py:360
  (28 shorter events, 0.3 us)
Async XLA Ops:
  2.1 12.5 %collective-permute-start = (bf16[36,1024]{1,0:T(8,128)(2,1)S(1)}, bf16[36,1024]{1,0:T(8,128)(2,1)S(1)}, u32[]{:S(2)}, u32[]{:S(2)}) collective-permute-start(bf16[36,1024]{1,0:T(8,128)(2,1)S(1)} %get-tuple-element.45), channel_id=1, source_target_pairs={{0,6},{2,4},{4,2},{6,0},{1,7},{3,5},{5,3},{7,1},{8,14},{10,12},{12... | collective-permute-start | bytes 221192 | tf_op jit(solution)/shard_map/ppermute | solution.py:415
  7.2 8.0 %collective-permute-start.1 = (bf16[36,1024]{1,0:T(8,128)(2,1)S(1)}, bf16[36,1024]{1,0:T(8,128)(2,1)S(1)}, u32[]{:S(2)}, u32[]{:S(2)}) collective-permute-start(bf16[36,1024]{1,0:T(8,128)(2,1)S(1)} %get-tuple-element.46), channel_id=1, source_target_pairs={{0,4},{2,6},{4,0},{6,2},{1,5},{3,7},{5,1},{7,3},{8,12},{10,14},{12... | collective-permute-start | bytes 221192 | tf_op jit(solution)/shard_map/ppermute | solution.py:415
  7.2 8.0 %collective-permute-start.2 = (bf16[36,1024]{1,0:T(8,128)(2,1)S(1)}, bf16[36,1024]{1,0:T(8,128)(2,1)S(1)}, u32[]{:S(2)}, u32[]{:S(2)}) collective-permute-start(bf16[36,1024]{1,0:T(8,128)(2,1)S(1)} %get-tuple-element.47), channel_id=1, source_target_pairs={{0,2},{2,0},{4,6},{6,4},{1,3},{3,1},{5,7},{7,5},{8,10},{10,8},{12,... | collective-permute-start | bytes 221192 | tf_op jit(solution)/shard_map/ppermute | solution.py:415
  7.9 10.7 %copy-start = (bf16[1024,2048]{1,0:T(8,128)(2,1)S(1)}, bf16[1024,2048]{1,0:T(8,128)(2,1)}, u32[]{:S(2)}) copy-start(bf16[1024,2048]{1,0:T(8,128)(2,1)} %refs_2_.7) | copy-start | bytes 12582916
  7.9 10.7 %copy-start.1 = (bf16[1024,2048]{1,0:T(8,128)(2,1)S(1)}, bf16[1024,2048]{1,0:T(8,128)(2,1)}, u32[]{:S(2)}) copy-start(bf16[1024,2048]{1,0:T(8,128)(2,1)} %refs_3_.3) | copy-start | bytes 12582916
  10.8 10.0 %collective-permute-start.7 = (bf16[36,1024]{1,0:T(8,128)(2,1)S(1)}, bf16[36,1024]{1,0:T(8,128)(2,1)S(1)}, u32[]{:S(2)}, u32[]{:S(2)}) collective-permute-start(bf16[36,1024]{1,0:T(8,128)(2,1)S(1)} %get-tuple-element.62), channel_id=1, source_target_pairs={{0,6},{2,4},{4,2},{6,0},{1,7},{3,5},{5,3},{7,1},{8,14},{10,12},{12... | collective-permute-start | bytes 221192 | tf_op jit(solution)/shard_map/ppermute | solution.py:415
  14.6 6.5 %collective-permute-start.8 = (bf16[36,1024]{1,0:T(8,128)(2,1)S(1)}, bf16[36,1024]{1,0:T(8,128)(2,1)S(1)}, u32[]{:S(2)}, u32[]{:S(2)}) collective-permute-start(bf16[36,1024]{1,0:T(8,128)(2,1)S(1)} %get-tuple-element.63), channel_id=1, source_target_pairs={{0,4},{2,6},{4,0},{6,2},{1,5},{3,7},{5,1},{7,3},{8,12},{10,14},{12... | collective-permute-start | bytes 221192 | tf_op jit(solution)/shard_map/ppermute | solution.py:415
  14.6 6.5 %collective-permute-start.9 = (bf16[36,1024]{1,0:T(8,128)(2,1)S(1)}, bf16[36,1024]{1,0:T(8,128)(2,1)S(1)}, u32[]{:S(2)}, u32[]{:S(2)}) collective-permute-start(bf16[36,1024]{1,0:T(8,128)(2,1)S(1)} %get-tuple-element.64), channel_id=1, source_target_pairs={{0,2},{2,0},{4,6},{6,4},{1,3},{3,1},{5,7},{7,5},{8,10},{10,8},{12,... | collective-permute-start | bytes 221192 | tf_op jit(solution)/shard_map/ppermute | solution.py:415
  15.3 8.9 %collective-permute-start.3 = (bf16[144,1024]{1,0:T(8,128)(2,1)S(1)}, bf16[144,1024]{1,0:T(8,128)(2,1)S(1)}, u32[]{:S(2)}, u32[]{:S(2)}) collective-permute-start(bf16[144,1024]{1,0:T(8,128)(2,1)S(1)} %join.2.refs_0_.refs_4_), channel_id=1, source_target_pairs={{0,1},{1,0},{2,3},{3,2},{4,5},{5,4},{6,7},{7,6},{8,9},{9,8},{10,11... | collective-permute-start | bytes 884744 | tf_op jit(solution)/shard_map/ppermute | solution.py:410
  17.0 12.8 %collective-permute-start.12 = (bf16[144,1024]{1,0:T(8,128)(2,1)S(1)}, bf16[144,1024]{1,0:T(8,128)(2,1)S(1)}, u32[]{:S(2)}, u32[]{:S(2)}) collective-permute-start(bf16[144,1024]{1,0:T(8,128)(2,1)S(1)} %join.2.refs_0_.refs_4_), channel_id=1, source_target_pairs={{0,16},{16,0},{1,17},{17,1},{2,18},{18,2},{3,19},{19,3},{4,20},{20... | collective-permute-start | bytes 884744 | tf_op jit(solution)/shard_map/ppermute | solution.py:410
  21.2 9.8 %collective-permute-start.11 = (bf16[144,1024]{1,0:T(8,128)(2,1)S(1)}, bf16[144,1024]{1,0:T(8,128)(2,1)S(1)}, u32[]{:S(2)}, u32[]{:S(2)}) collective-permute-start(bf16[144,1024]{1,0:T(8,128)(2,1)S(1)} %join.3.refs_0_), channel_id=1, source_target_pairs={{0,16},{16,0},{1,17},{17,1},{2,18},{18,2},{3,19},{19,3},{4,20},{20... | collective-permute-start | bytes 884744 | tf_op jit(solution)/shard_map/ppermute | solution.py:410
  22.7 9.2 %collective-permute-start.10 = (bf16[144,1024]{1,0:T(8,128)(2,1)S(1)}, bf16[144,1024]{1,0:T(8,128)(2,1)S(1)}, u32[]{:S(2)}, u32[]{:S(2)}) collective-permute-start(bf16[144,1024]{1,0:T(8,128)(2,1)S(1)} %join.3.refs_0_), channel_id=1, source_target_pairs={{0,1},{1,0},{2,3},{3,2},{4,5},{5,4},{6,7},{7,6},{8,9},{9,8},{10,11... | collective-permute-start | bytes 884744 | tf_op jit(solution)/shard_map/ppermute | solution.py:410
  26.5 11.1 %collective-permute-start.4 = (bf16[72,1024]{1,0:T(8,128)(2,1)S(1)}, bf16[72,1024]{1,0:T(8,128)(2,1)S(1)}, u32[]{:S(2)}, u32[]{:S(2)}) collective-permute-start(bf16[72,1024]{1,0:T(8,128)(2,1)S(1)} %get-tuple-element.53), channel_id=1, source_target_pairs={{0,2},{2,0},{4,6},{6,4},{1,3},{3,1},{5,7},{7,5},{8,10},{10,8},{12,... | collective-permute-start | bytes 442376 | tf_op jit(solution)/shard_map/ppermute | solution.py:415
  27.0 12.9 %collective-permute-start.5 = (bf16[72,1024]{1,0:T(8,128)(2,1)S(1)}, bf16[72,1024]{1,0:T(8,128)(2,1)S(1)}, u32[]{:S(2)}, u32[]{:S(2)}) collective-permute-start(bf16[72,1024]{1,0:T(8,128)(2,1)S(1)} %get-tuple-element.54), channel_id=1, source_target_pairs={{0,4},{2,6},{4,0},{6,2},{1,5},{3,7},{5,1},{7,3},{8,12},{10,14},{12... | collective-permute-start | bytes 442376 | tf_op jit(solution)/shard_map/ppermute | solution.py:415
  29.8 10.0 %collective-permute-start.6 = (bf16[72,1024]{1,0:T(8,128)(2,1)S(1)}, bf16[72,1024]{1,0:T(8,128)(2,1)S(1)}, u32[]{:S(2)}, u32[]{:S(2)}) collective-permute-start(bf16[72,1024]{1,0:T(8,128)(2,1)S(1)} %get-tuple-element.55), channel_id=1, source_target_pairs={{0,6},{2,4},{4,2},{6,0},{1,7},{3,5},{5,3},{7,1},{8,14},{10,12},{12... | collective-permute-start | bytes 442376 | tf_op jit(solution)/shard_map/ppermute | solution.py:415
  31.0 9.7 %collective-permute-start.14 = (bf16[144,1024]{1,0:T(8,128)(2,1)S(1)}, bf16[144,1024]{1,0:T(8,128)(2,1)S(1)}, u32[]{:S(2)}, u32[]{:S(2)}) collective-permute-start(bf16[144,1024]{1,0:T(8,128)(2,1)S(1)} %relay.4.refs_1_), channel_id=1, source_target_pairs={{0,16},{16,0},{1,17},{17,1},{2,18},{18,2},{3,19},{19,3},{4,20},{20... | collective-permute-start | bytes 884744 | tf_op jit(solution)/shard_map/ppermute | solution.py:410
  31.9 10.6 %collective-permute-start.15 = (bf16[144,1024]{1,0:T(8,128)(2,1)S(1)}, bf16[144,1024]{1,0:T(8,128)(2,1)S(1)}, u32[]{:S(2)}, u32[]{:S(2)}) collective-permute-start(bf16[144,1024]{1,0:T(8,128)(2,1)S(1)} %relay.5.refs_0_), channel_id=1, source_target_pairs={{0,1},{1,0},{2,3},{3,2},{4,5},{5,4},{6,7},{7,6},{8,9},{9,8},{10,11... | collective-permute-start | bytes 884744 | tf_op jit(solution)/shard_map/ppermute | solution.py:410
  39.9 7.7 %collective-permute-start.13 = (bf16[144,1024]{1,0:T(8,128)(2,1)S(1)}, bf16[144,1024]{1,0:T(8,128)(2,1)S(1)}, u32[]{:S(2)}, u32[]{:S(2)}) collective-permute-start(bf16[144,1024]{1,0:T(8,128)(2,1)S(1)} %get-tuple-element.73), channel_id=1, source_target_pairs={{0,1},{1,0},{2,3},{3,2},{4,5},{5,4},{6,7},{7,6},{8,9},{9,8},{10,11... | collective-permute-start | bytes 884744 | tf_op jit(solution)/shard_map/ppermute | solution.py:410
  44.8 2.8 %collective-permute-start.16 = (bf16[512,1024]{1,0:T(8,128)(2,1)S(1)}, bf16[512,1024]{1,0:T(8,128)(2,1)S(1)}, u32[]{:S(2)}, u32[]{:S(2)}) collective-permute-start(bf16[512,1024]{1,0:T(8,128)(2,1)S(1)} %get-tuple-element.79), channel_id=1, source_target_pairs={{0,8},{8,0},{1,9},{9,1},{2,10},{10,2},{3,11},{11,3},{4,12},{12,4},... | collective-permute-start | bytes 3145736 | tf_op jit(solution)/shard_map/ppermute | solution.py:410
  47.0 2.8 %collective-permute-start.17 = (bf16[512,1024]{1,0:T(8,128)(2,1)S(1)}, bf16[512,1024]{1,0:T(8,128)(2,1)S(1)}, u32[]{:S(2)}, u32[]{:S(2)}) collective-permute-start(bf16[512,1024]{1,0:T(8,128)(2,1)S(1)} %get-tuple-element.80), channel_id=1, source_target_pairs={{0,8},{8,0},{1,9},{9,1},{2,10},{10,2},{3,11},{11,3},{4,12},{12,4},... | collective-permute-start | bytes 3145736 | tf_op jit(solution)/shard_map/ppermute | solution.py:410

commit v16 on v15

--- a/solution.py
+++ b/solution.py
@@ -399,11 +399,11 @@
     return pl.pallas_call(
         unpack_kernel,
         out_shape=jax.ShapeDtypeStruct((placer.shape[1], mine.shape[1]), BF16),
-        in_specs=[HERE] * 3 + [ANYWHERE] * len(earlier),
+        in_specs=[HERE] * 3 + [AFAR] * len(earlier),
         compiler_params=SMALL,
         cost_estimate=DEAR,
         name="unpack",
-    )(placer, mine, got, *earlier)
+    )(placer, mine, got, *[kept(v) for v in earlier])
 
 
 def swap(value, axis):
@@ -445,9 +445,9 @@
     returned = across_planes(shares)
     act2, coef2 = forward([x_far], wg, wu, earlier=[g_pass], cost=DEAR)
     dg, du = slopes([g_own, g_near, g_far], [act0, act1, act2], [coef0, coef1, coef2], wdt)
-    mine, theirs = split(returned, [dg])
+    act3, coef3 = forward([x_corner], wg, wu, earlier=[dg])
+    mine, theirs = split(returned, [act3])
     got = swap(theirs, "half")
-    act3, coef3 = forward([x_corner], wg, wu, earlier=[mine])
     xt = turn(*scalars[1:], [x_own, x_near, x_far, x_corner], share)
 
     rest = (xt, g_corner, act3, coef3, dg, du, wdt)
@@ -456,8 +456,8 @@
     own0, sib0 = backward(*rest, 0, cut)
     own1, sib1 = backward(*rest, cut, cols - cut, [own0])
     got0, got1 = swap(sib0, "core"), swap(sib1, "core")
-    outputs = unpack(placer, mine, got, [own1, got0])
-    held = finish([own0], [got0], (0,), cols, earlier=[outputs])
+    held = finish([own0], [got0], (0,), cols)
+    outputs = unpack(placer, mine, got, held[:1])
     grad_gate, grad_up = finish([own1], [got1], (cut,), cols, held)
     return outputs, grad_gate, grad_up
 

time: 51.3 us -> 49.7 us (0.969)
  waiting for transfers between devices: 2.71 us -> 1.37 us
    ppermute x9, waiting for transfers between devices: 2.56 us -> 0.33 us  [across_planes(): lax.ppermute(blocks[k], 'arch', [(i, i ^ k) for i in range(EXPERTS)])]
    ppermute x9, waiting for transfers between devices: 0.15 us -> 1.03 us  [swap(): return lax.ppermute(value, axis, [(0, 1), (1, 0)])]
  transfers between devices with their start and end apart: 18 -> 18, of which waited for: 3 -> 3; matrix products, arithmetic and copies ran while one was open for 0% -> 0% of each run, Pallas kernels for 39% -> 40%
where the time goes in v16:
time: 49.7 us; the launch traced here: 49.6 us
  starting transfers between devices  24.8 us (50%)
  Pallas kernels  22.3 us (45%)
  waiting for transfers between devices  1.37 us (3%)
  between operations  0.99 us (2%)
    ppermute x9, starting transfers between devices, across_planes(): lax.ppermute(blocks[k], 'arch', [(i, i ^ k) for i in range(EXPERTS)])  14.7 us
    ppermute x9, starting transfers between devices, swap(): return lax.ppermute(value, axis, [(0, 1), (1, 0)])  10.2 us
    pallas_call x4, Pallas kernels, forward(): pl.pallas_call(functools.partial(forward_kernel, n, fetch, down, pair, le...  7.62 us
    pallas_call x2, Pallas kernels, backward(): pl.pallas_call(functools.partial(backward_kernel, first), out_shape=[jax....  4.45 us
    pallas_call x1, Pallas kernels, flip(): pl.pallas_call(flip_kernel, out_shape=[pltpu.VMEM(value.shape, value.dtyp...  2.88 us
    pallas_call x2, Pallas kernels, finish(): pl.pallas_call(functools.partial(finish_kernel, spans, more, len(earlier)...  2.21 us
    pallas_call x1, Pallas kernels, slopes(): pl.pallas_call(functools.partial(slopes_kernel, n), out_shape=[jax.ShapeD...  2.19 us
    pallas_call x1, Pallas kernels, pack(): pl.pallas_call(pack_kernel, out_shape=[jax.ShapeDtypeStruct((EXPERTS * CA...  1.46 us
  transfers between devices with their start and end apart: 18, of which 3 were waited for; matrix products, arithmetic and copies ran while one was open for 0% of the time, Pallas kernels for 40%

profile of v16, /device:TPU:0, one launch (start us, length us, event | category | flops | bytes accessed | tf_op | source)
XLA Modules:
  0.0 49.6 jit_solution(4626032985036360487)
XLA Ops:
  0.6 1.5 %pack.1 = (bf16[144,128]{1,0:T(8,128)(2,1)S(1)}, bf16[36,1024]{1,0:T(8,128)(2,1)S(1)}, bf16[36,1024]{1,0:T(8,128)(2,1)S(1)}, bf16[36,1024]{1,0:T(8,128)(2,1)S(1)...) custom-call(s32[1]{0:T(128)} %bitcast.plane_ref, ...), custom_call_target="tpu_custom_call" | custom-call | tf_op jit(solution)/shard_map/pack/pallas_call | solution.py:79
  2.1 5.1 %collective-permute-start = (bf16[36,1024]{1,0:T(8,128)(2,1)S(1)}, bf16[36,1024]{1,0:T(8,128)(2,1)S(1)}, u32[]{:S(2)}, u32[]{:S(2)}) collective-permute-start(bf16[36,1024]{1,0:T(8,128)(2,1)S(1)} %get-tuple-element.45), channel_id=1, source_target_pairs={{0,6},{2,4},{4,2},{6,0},{1,7},{3,5},{5,3},{7,1},{8,14},{10,12},{12... | collective-permute-start | bytes 221192 | tf_op jit(solution)/shard_map/ppermute | solution.py:415
  7.2 0.6 %collective-permute-start.2 = (bf16[36,1024]{1,0:T(8,128)(2,1)S(1)}, bf16[36,1024]{1,0:T(8,128)(2,1)S(1)}, u32[]{:S(2)}, u32[]{:S(2)}) collective-permute-start(bf16[36,1024]{1,0:T(8,128)(2,1)S(1)} %get-tuple-element.47), channel_id=1, source_target_pairs={{0,2},{2,0},{4,6},{6,4},{1,3},{3,1},{5,7},{7,5},{8,10},{10,8},{12,... | collective-permute-start | bytes 221192 | tf_op jit(solution)/shard_map/ppermute | solution.py:415
  7.9 2.9 %flip.1 = (bf16[2048,1024]{1,0:T(8,128)(2,1)S(1)}, bf16[1024,2048]{1,0:T(8,128)(2,1)S(1)}) custom-call(bf16[2048,1024]{1,0:T(8,128)(2,1)} %source_ref), custom_call_target="tpu_custom_call" | custom-call | tf_op jit(solution)/shard_map/flip/pallas_call | solution.py:158
  10.8 3.8 %collective-permute-start.7 = (bf16[36,1024]{1,0:T(8,128)(2,1)S(1)}, bf16[36,1024]{1,0:T(8,128)(2,1)S(1)}, u32[]{:S(2)}, u32[]{:S(2)}) collective-permute-start(bf16[36,1024]{1,0:T(8,128)(2,1)S(1)} %get-tuple-element.62), channel_id=1, source_target_pairs={{0,6},{2,4},{4,2},{6,0},{1,7},{3,5},{5,3},{7,1},{8,14},{10,12},{12... | collective-permute-start | bytes 221192 | tf_op jit(solution)/shard_map/ppermute | solution.py:415
  14.6 0.6 %collective-permute-start.9 = (bf16[36,1024]{1,0:T(8,128)(2,1)S(1)}, bf16[36,1024]{1,0:T(8,128)(2,1)S(1)}, u32[]{:S(2)}, u32[]{:S(2)}) collective-permute-start(bf16[36,1024]{1,0:T(8,128)(2,1)S(1)} %get-tuple-element.64), channel_id=1, source_target_pairs={{0,2},{2,0},{4,6},{6,4},{1,3},{3,1},{5,7},{7,5},{8,10},{10,8},{12,... | collective-permute-start | bytes 221192 | tf_op jit(solution)/shard_map/ppermute | solution.py:415
  15.3 1.7 %collective-permute-start.3 = (bf16[144,1024]{1,0:T(8,128)(2,1)S(1)}, bf16[144,1024]{1,0:T(8,128)(2,1)S(1)}, u32[]{:S(2)}, u32[]{:S(2)}) collective-permute-start(bf16[144,1024]{1,0:T(8,128)(2,1)S(1)} %join.2.refs_0_.refs_4_), channel_id=1, source_target_pairs={{0,1},{1,0},{2,3},{3,2},{4,5},{5,4},{6,7},{7,6},{8,9},{9,8},{10,11... | collective-permute-start | bytes 884744 | tf_op jit(solution)/shard_map/ppermute | solution.py:410
  17.0 1.5 %collective-permute-start.12 = (bf16[144,1024]{1,0:T(8,128)(2,1)S(1)}, bf16[144,1024]{1,0:T(8,128)(2,1)S(1)}, u32[]{:S(2)}, u32[]{:S(2)}) collective-permute-start(bf16[144,1024]{1,0:T(8,128)(2,1)S(1)} %join.2.refs_0_.refs_4_), channel_id=1, source_target_pairs={{0,16},{16,0},{1,17},{17,1},{2,18},{18,2},{3,19},{19,3},{4,20},{20... | collective-permute-start | bytes 884744 | tf_op jit(solution)/shard_map/ppermute | solution.py:410
  18.5 2.2 %forward_down.2 = (bf16[144,2048]{1,0:T(8,128)(2,1)S(1)}, bf16[144,2048]{1,0:T(8,128)(2,1)S(1)}, bf16[144,1024]{1,0:T(8,128)(2,1)S(1)}) custom-call(bf16[144,1024]{1,0:T(8,128)(2,1)S(1)} %join.2.refs_0_.refs_4_, bf16[1024,2048]{1,0:T(8,128)(2,1)S(1)} %copy-done, bf16[1024,2048]{1,0:T(8,128)(2,1)S(1)} %copy-done.1, ...), custom_call_target="tpu_custom_call" | custom-call | tf_op jit(solution)/shard_map/forward_down/pallas_call | solution.py:238
  20.8 0.3 collective-permute-done.8.refs_2_
  21.2 1.6 %collective-permute-start.11 = (bf16[144,1024]{1,0:T(8,128)(2,1)S(1)}, bf16[144,1024]{1,0:T(8,128)(2,1)S(1)}, u32[]{:S(2)}, u32[]{:S(2)}) collective-permute-start(bf16[144,1024]{1,0:T(8,128)(2,1)S(1)} %join.3.refs_0_), channel_id=1, source_target_pairs={{0,16},{16,0},{1,17},{17,1},{2,18},{18,2},{3,19},{19,3},{4,20},{20... | collective-permute-start | bytes 884744 | tf_op jit(solution)/shard_map/ppermute | solution.py:410
  22.7 1.5 %collective-permute-start.10 = (bf16[144,1024]{1,0:T(8,128)(2,1)S(1)}, bf16[144,1024]{1,0:T(8,128)(2,1)S(1)}, u32[]{:S(2)}, u32[]{:S(2)}) collective-permute-start(bf16[144,1024]{1,0:T(8,128)(2,1)S(1)} %join.3.refs_0_), channel_id=1, source_target_pairs={{0,1},{1,0},{2,3},{3,2},{4,5},{5,4},{6,7},{7,6},{8,9},{9,8},{10,11... | collective-permute-start | bytes 884744 | tf_op jit(solution)/shard_map/ppermute | solution.py:410
  24.2 2.2 %forward_down.3 = (bf16[144,2048]{1,0:T(8,128)(2,1)S(1)}, bf16[144,2048]{1,0:T(8,128)(2,1)S(1)}, bf16[72,1024]{1,0:T(8,128)(2,1)S(1)}, bf16[72,1024]{1,0:T(8,128...) custom-call(bf16[144,1024]{1,0:T(8,128)(2,1)S(1)} %collective-permute-done.3.refs_0_.refs_1_.refs_5_, ...), custom_call_target="tpu_custom_call" | custom-call | tf_op jit(solution)/shard_map/forward_down/pallas_call | solution.py:238
  26.5 0.5 collective-permute-start.4
  27.0 2.9 %collective-permute-start.5 = (bf16[72,1024]{1,0:T(8,128)(2,1)S(1)}, bf16[72,1024]{1,0:T(8,128)(2,1)S(1)}, u32[]{:S(2)}, u32[]{:S(2)}) collective-permute-start(bf16[72,1024]{1,0:T(8,128)(2,1)S(1)} %get-tuple-element.54), channel_id=1, source_target_pairs={{0,4},{2,6},{4,0},{6,2},{1,5},{3,7},{5,1},{7,3},{8,12},{10,14},{12... | collective-permute-start | bytes 442376 | tf_op jit(solution)/shard_map/ppermute | solution.py:415
  29.8 1.1 %collective-permute-start.6 = (bf16[72,1024]{1,0:T(8,128)(2,1)S(1)}, bf16[72,1024]{1,0:T(8,128)(2,1)S(1)}, u32[]{:S(2)}, u32[]{:S(2)}) collective-permute-start(bf16[72,1024]{1,0:T(8,128)(2,1)S(1)} %get-tuple-element.55), channel_id=1, source_target_pairs={{0,6},{2,4},{4,2},{6,0},{1,7},{3,5},{5,3},{7,1},{8,14},{10,12},{12... | collective-permute-start | bytes 442376 | tf_op jit(solution)/shard_map/ppermute | solution.py:415
  31.0 0.9 %collective-permute-start.13 = (bf16[144,1024]{1,0:T(8,128)(2,1)S(1)}, bf16[144,1024]{1,0:T(8,128)(2,1)S(1)}, u32[]{:S(2)}, u32[]{:S(2)}) collective-permute-start(bf16[144,1024]{1,0:T(8,128)(2,1)S(1)} %relay.4.refs_1_), channel_id=1, source_target_pairs={{0,16},{16,0},{1,17},{17,1},{2,18},{18,2},{3,19},{19,3},{4,20},{20... | collective-permute-start | bytes 884744 | tf_op jit(solution)/shard_map/ppermute | solution.py:410
  31.9 1.9 %collective-permute-start.15 = (bf16[144,1024]{1,0:T(8,128)(2,1)S(1)}, bf16[144,1024]{1,0:T(8,128)(2,1)S(1)}, u32[]{:S(2)}, u32[]{:S(2)}) collective-permute-start(bf16[144,1024]{1,0:T(8,128)(2,1)S(1)} %relay.5.refs_0_), channel_id=1, source_target_pairs={{0,1},{1,0},{2,3},{3,2},{4,5},{5,4},{6,7},{7,6},{8,9},{9,8},{10,11... | collective-permute-start | bytes 884744 | tf_op jit(solution)/shard_map/ppermute | solution.py:410
  33.8 1.6 %forward.2 = (bf16[144,2048]{1,0:T(8,128)(2,1)S(1)}, bf16[144,2048]{1,0:T(8,128)(2,1)S(1)}) custom-call(bf16[144,1024]{1,0:T(8,128)(2,1)S(1)} %relay.5.refs_0_, bf16[144,1024]{1,0:T(8,128)(2,1)S(1)} %collective-permute-done.12._.refs_1_.refs_2_.refs_6_, bf16[1024,2048]{1,0:T(8,128)(2,1)S(1)} %copy-done, bf16[1024,2048]{1,0:T(8,128)(2,1)S(1)} %copy-done.1), custom_call_target="tpu_custom_call" | custom-call | flops 20000000000 | tf_op jit(solution)/shard_map/forward/pallas_call | solution.py:238
  35.4 2.2 %slopes.1 = (bf16[432,2048]{1,0:T(8,128)(2,1)S(1)}, bf16[432,2048]{1,0:T(8,128)(2,1)S(1)}) custom-call(bf16[144,1024]{1,0:T(8,128)(2,1)S(1)} %join.3.refs_0_, bf16[144,1024]{1,0:T(8,128)(2,1)S(1)} %collective-permute-done.10.refs_2_.refs_1_, bf16[144,1024]{1,0:T(8,128)(2,1)S(1)} %collective-permute-done.11.refs_2_.refs_0_, ...), custom_call_target="tpu_custom_call" | custom-call | tf_op jit(solution)/shard_map/slopes/pallas_call | solution.py:297
  37.6 0.9 %collective-permute-done.13.refs_1_.refs_3_.refs_7_ = bf16[144,1024]{1,0:T(8,128)(2,1)S(1)} collective-permute-done((bf16[144,1024]{1,0:T(8,128)(2,1)S(1)}, bf16[144,1024]{1,0:T(8,128)(2,1)S(1)}, u32[]{:S(2)}, u32[]{:S(2)}) %collective-permute-start.13) | collective-permute-done | bytes 294944 | tf_op jit(solution)/shard_map/ppermute | solution.py:410
  38.5 1.6 %forward.3 = (bf16[144,2048]{1,0:T(8,128)(2,1)S(1)}, bf16[144,2048]{1,0:T(8,128)(2,1)S(1)}) custom-call(bf16[432,2048]{1,0:T(8,128)(2,1)S(1)} %get-tuple-element.71.refs_0_.dg_ref, bf16[144,1024]{1,0:T(8,128)(2,1)S(1)} %collective-permute-done.13.refs_1_.refs_3_.refs_7_, bf16[1024,2048]{1,0:T(8,128)(2,1)S(1)} %copy-done, bf16[1024,2048]{1,0:T(8,128)(2,1)S(1)} %copy-done.1), custom_call_target="tpu_custom_call" | custom-call | tf_op jit(solution)/shard_map/forward/pallas_call | solution.py:238
  40.1 0.1 split.1
  40.2 0.4 collective-permute-start.14
  40.7 0.2 turn.1.xt_ref
  40.9 2.3 %backward.2 = (bf16[512,1024]{1,0:T(8,128)(2,1)S(1)}, bf16[512,1024]{1,0:T(8,128)(2,1)S(1)}) custom-call(bf16[512,576]{1,0:T(8,128)(2,1)S(1)} %turn.1.xt_ref, bf16[144,1024]{1,0:T(8,128)(2,1)S(1)} %collective-permute-done.15.g_ref, bf16[144,2048]{1,0:T(8,128)(2,1)S(1)} %get-tuple-element.72.refs_4_.act_ref, ...), custom_call_target="tpu_custom_call" | custom-call | flops 20000000000 | tf_op jit(solution)/shard_map/backward/pallas_call | solution.py:324
  43.3 2.1 %backward.3 = (bf16[512,1024]{1,0:T(8,128)(2,1)S(1)}, bf16[512,1024]{1,0:T(8,128)(2,1)S(1)}) custom-call(bf16[512,576]{1,0:T(8,128)(2,1)S(1)} %turn.1.xt_ref, bf16[144,1024]{1,0:T(8,128)(2,1)S(1)} %collective-permute-done.15.g_ref, bf16[144,2048]{1,0:T(8,128)(2,1)S(1)} %get-tuple-element.72.refs_4_.act_ref, ...), custom_call_target="tpu_custom_call" | custom-call | flops 20000000000 | tf_op jit(solution)/shard_map/backward/pallas_call | solution.py:324
  45.5 0.5 %collective-permute-start.17 = (bf16[512,1024]{1,0:T(8,128)(2,1)S(1)}, bf16[512,1024]{1,0:T(8,128)(2,1)S(1)}, u32[]{:S(2)}, u32[]{:S(2)}) collective-permute-start(bf16[512,1024]{1,0:T(8,128)(2,1)S(1)} %get-tuple-element.81), channel_id=1, source_target_pairs={{0,8},{8,0},{1,9},{9,1},{2,10},{10,2},{3,11},{11,3},{4,12},{12,4},... | collective-permute-start | bytes 3145736 | tf_op jit(solution)/shard_map/ppermute | solution.py:410
  46.0 1.1 %finish.2 = (bf16[256,2048]{1,0:T(8,128)(2,1)}, bf16[256,2048]{1,0:T(8,128)(2,1)}) custom-call(bf16[512,1024]{1,0:T(8,128)(2,1)S(1)} %get-tuple-element.77.refs_0_, bf16[512,1024]{1,0:T(8,128)(2,1)S(1)} %collective-permute-done.16.refs_1_), custom_call_target="tpu_custom_call" | custom-call | tf_op jit(solution)/shard_map/finish/pallas_call | solution.py:360
  47.1 1.1 %unpack.1 = bf16[128,1024]{1,0:T(8,128)(2,1)} custom-call(bf16[144,128]{1,0:T(8,128)(2,1)S(1)} %get-tuple-element.44.placer_ref, bf16[144,1024]{1,0:T(8,128)(2,1)S(1)} %get-tuple-element.73.mine_ref, bf16[144,1024]{1,0:T(8,128)(2,1)S(1)} %collective-permute-done.14.got_ref, bf16[256,2048]{1,0:T(8,128)(2,1)} %get-tuple-element.79.refs_0_.refs_2_), custom_call_target="tpu_custom_call" | custom-call | flops 20000000000 | tf_op jit(solution)/shard_map/unpack/pallas_call | solution.py:399
  48.2 0.1 collective-permute-done.17.refs_1_
  48.3 1.1 %finish.3 = (bf16[256,2048]{1,0:T(8,128)(2,1)}, bf16[256,2048]{1,0:T(8,128)(2,1)}) custom-call(bf16[512,1024]{1,0:T(8,128)(2,1)S(1)} %get-tuple-element.80.refs_0_, bf16[512,1024]{1,0:T(8,128)(2,1)S(1)} %collective-permute-done.17.refs_1_, bf16[256,2048]{1,0:T(8,128)(2,1)} %get-tuple-element.79.refs_0_.refs_2_, ...), custom_call_target="tpu_custom_call", output_to_operand_aliasing={{0}: (2, {}), {1}: (3, {})} | custom-call | tf_op jit(solution)/shard_map/finish/pallas_call | solution.py:360
  (28 shorter events, 0.3 us)
Async XLA Ops:
  2.1 12.5 %collective-permute-start = (bf16[36,1024]{1,0:T(8,128)(2,1)S(1)}, bf16[36,1024]{1,0:T(8,128)(2,1)S(1)}, u32[]{:S(2)}, u32[]{:S(2)}) collective-permute-start(bf16[36,1024]{1,0:T(8,128)(2,1)S(1)} %get-tuple-element.45), channel_id=1, source_target_pairs={{0,6},{2,4},{4,2},{6,0},{1,7},{3,5},{5,3},{7,1},{8,14},{10,12},{12... | collective-permute-start | bytes 221192 | tf_op jit(solution)/shard_map/ppermute | solution.py:415
  7.2 8.0 %collective-permute-start.1 = (bf16[36,1024]{1,0:T(8,128)(2,1)S(1)}, bf16[36,1024]{1,0:T(8,128)(2,1)S(1)}, u32[]{:S(2)}, u32[]{:S(2)}) collective-permute-start(bf16[36,1024]{1,0:T(8,128)(2,1)S(1)} %get-tuple-element.46), channel_id=1, source_target_pairs={{0,4},{2,6},{4,0},{6,2},{1,5},{3,7},{5,1},{7,3},{8,12},{10,14},{12... | collective-permute-start | bytes 221192 | tf_op jit(solution)/shard_map/ppermute | solution.py:415
  7.2 8.0 %collective-permute-start.2 = (bf16[36,1024]{1,0:T(8,128)(2,1)S(1)}, bf16[36,1024]{1,0:T(8,128)(2,1)S(1)}, u32[]{:S(2)}, u32[]{:S(2)}) collective-permute-start(bf16[36,1024]{1,0:T(8,128)(2,1)S(1)} %get-tuple-element.47), channel_id=1, source_target_pairs={{0,2},{2,0},{4,6},{6,4},{1,3},{3,1},{5,7},{7,5},{8,10},{10,8},{12,... | collective-permute-start | bytes 221192 | tf_op jit(solution)/shard_map/ppermute | solution.py:415
  7.9 10.7 %copy-start = (bf16[1024,2048]{1,0:T(8,128)(2,1)S(1)}, bf16[1024,2048]{1,0:T(8,128)(2,1)}, u32[]{:S(2)}) copy-start(bf16[1024,2048]{1,0:T(8,128)(2,1)} %refs_2_.7) | copy-start | bytes 12582916
  7.9 10.7 %copy-start.1 = (bf16[1024,2048]{1,0:T(8,128)(2,1)S(1)}, bf16[1024,2048]{1,0:T(8,128)(2,1)}, u32[]{:S(2)}) copy-start(bf16[1024,2048]{1,0:T(8,128)(2,1)} %refs_3_.3) | copy-start | bytes 12582916
  10.8 10.0 %collective-permute-start.7 = (bf16[36,1024]{1,0:T(8,128)(2,1)S(1)}, bf16[36,1024]{1,0:T(8,128)(2,1)S(1)}, u32[]{:S(2)}, u32[]{:S(2)}) collective-permute-start(bf16[36,1024]{1,0:T(8,128)(2,1)S(1)} %get-tuple-element.62), channel_id=1, source_target_pairs={{0,6},{2,4},{4,2},{6,0},{1,7},{3,5},{5,3},{7,1},{8,14},{10,12},{12... | collective-permute-start | bytes 221192 | tf_op jit(solution)/shard_map/ppermute | solution.py:415
  14.6 6.5 %collective-permute-start.8 = (bf16[36,1024]{1,0:T(8,128)(2,1)S(1)}, bf16[36,1024]{1,0:T(8,128)(2,1)S(1)}, u32[]{:S(2)}, u32[]{:S(2)}) collective-permute-start(bf16[36,1024]{1,0:T(8,128)(2,1)S(1)} %get-tuple-element.63), channel_id=1, source_target_pairs={{0,4},{2,6},{4,0},{6,2},{1,5},{3,7},{5,1},{7,3},{8,12},{10,14},{12... | collective-permute-start | bytes 221192 | tf_op jit(solution)/shard_map/ppermute | solution.py:415
  14.6 6.5 %collective-permute-start.9 = (bf16[36,1024]{1,0:T(8,128)(2,1)S(1)}, bf16[36,1024]{1,0:T(8,128)(2,1)S(1)}, u32[]{:S(2)}, u32[]{:S(2)}) collective-permute-start(bf16[36,1024]{1,0:T(8,128)(2,1)S(1)} %get-tuple-element.64), channel_id=1, source_target_pairs={{0,2},{2,0},{4,6},{6,4},{1,3},{3,1},{5,7},{7,5},{8,10},{10,8},{12,... | collective-permute-start | bytes 221192 | tf_op jit(solution)/shard_map/ppermute | solution.py:415
  15.3 8.9 %collective-permute-start.3 = (bf16[144,1024]{1,0:T(8,128)(2,1)S(1)}, bf16[144,1024]{1,0:T(8,128)(2,1)S(1)}, u32[]{:S(2)}, u32[]{:S(2)}) collective-permute-start(bf16[144,1024]{1,0:T(8,128)(2,1)S(1)} %join.2.refs_0_.refs_4_), channel_id=1, source_target_pairs={{0,1},{1,0},{2,3},{3,2},{4,5},{5,4},{6,7},{7,6},{8,9},{9,8},{10,11... | collective-permute-start | bytes 884744 | tf_op jit(solution)/shard_map/ppermute | solution.py:410
  17.0 12.8 %collective-permute-start.12 = (bf16[144,1024]{1,0:T(8,128)(2,1)S(1)}, bf16[144,1024]{1,0:T(8,128)(2,1)S(1)}, u32[]{:S(2)}, u32[]{:S(2)}) collective-permute-start(bf16[144,1024]{1,0:T(8,128)(2,1)S(1)} %join.2.refs_0_.refs_4_), channel_id=1, source_target_pairs={{0,16},{16,0},{1,17},{17,1},{2,18},{18,2},{3,19},{19,3},{4,20},{20... | collective-permute-start | bytes 884744 | tf_op jit(solution)/shard_map/ppermute | solution.py:410
  21.2 9.8 %collective-permute-start.11 = (bf16[144,1024]{1,0:T(8,128)(2,1)S(1)}, bf16[144,1024]{1,0:T(8,128)(2,1)S(1)}, u32[]{:S(2)}, u32[]{:S(2)}) collective-permute-start(bf16[144,1024]{1,0:T(8,128)(2,1)S(1)} %join.3.refs_0_), channel_id=1, source_target_pairs={{0,16},{16,0},{1,17},{17,1},{2,18},{18,2},{3,19},{19,3},{4,20},{20... | collective-permute-start | bytes 884744 | tf_op jit(solution)/shard_map/ppermute | solution.py:410
  22.7 9.2 %collective-permute-start.10 = (bf16[144,1024]{1,0:T(8,128)(2,1)S(1)}, bf16[144,1024]{1,0:T(8,128)(2,1)S(1)}, u32[]{:S(2)}, u32[]{:S(2)}) collective-permute-start(bf16[144,1024]{1,0:T(8,128)(2,1)S(1)} %join.3.refs_0_), channel_id=1, source_target_pairs={{0,1},{1,0},{2,3},{3,2},{4,5},{5,4},{6,7},{7,6},{8,9},{9,8},{10,11... | collective-permute-start | bytes 884744 | tf_op jit(solution)/shard_map/ppermute | solution.py:410
  26.5 13.6 %collective-permute-start.4 = (bf16[72,1024]{1,0:T(8,128)(2,1)S(1)}, bf16[72,1024]{1,0:T(8,128)(2,1)S(1)}, u32[]{:S(2)}, u32[]{:S(2)}) collective-permute-start(bf16[72,1024]{1,0:T(8,128)(2,1)S(1)} %get-tuple-element.53), channel_id=1, source_target_pairs={{0,2},{2,0},{4,6},{6,4},{1,3},{3,1},{5,7},{7,5},{8,10},{10,8},{12,... | collective-permute-start | bytes 442376 | tf_op jit(solution)/shard_map/ppermute | solution.py:415
  27.0 13.2 %collective-permute-start.5 = (bf16[72,1024]{1,0:T(8,128)(2,1)S(1)}, bf16[72,1024]{1,0:T(8,128)(2,1)S(1)}, u32[]{:S(2)}, u32[]{:S(2)}) collective-permute-start(bf16[72,1024]{1,0:T(8,128)(2,1)S(1)} %get-tuple-element.54), channel_id=1, source_target_pairs={{0,4},{2,6},{4,0},{6,2},{1,5},{3,7},{5,1},{7,3},{8,12},{10,14},{12... | collective-permute-start | bytes 442376 | tf_op jit(solution)/shard_map/ppermute | solution.py:415
  29.8 10.3 %collective-permute-start.6 = (bf16[72,1024]{1,0:T(8,128)(2,1)S(1)}, bf16[72,1024]{1,0:T(8,128)(2,1)S(1)}, u32[]{:S(2)}, u32[]{:S(2)}) collective-permute-start(bf16[72,1024]{1,0:T(8,128)(2,1)S(1)} %get-tuple-element.55), channel_id=1, source_target_pairs={{0,6},{2,4},{4,2},{6,0},{1,7},{3,5},{5,3},{7,1},{8,14},{10,12},{12... | collective-permute-start | bytes 442376 | tf_op jit(solution)/shard_map/ppermute | solution.py:415
  31.0 7.6 %collective-permute-start.13 = (bf16[144,1024]{1,0:T(8,128)(2,1)S(1)}, bf16[144,1024]{1,0:T(8,128)(2,1)S(1)}, u32[]{:S(2)}, u32[]{:S(2)}) collective-permute-start(bf16[144,1024]{1,0:T(8,128)(2,1)S(1)} %relay.4.refs_1_), channel_id=1, source_target_pairs={{0,16},{16,0},{1,17},{17,1},{2,18},{18,2},{3,19},{19,3},{4,20},{20... | collective-permute-start | bytes 884744 | tf_op jit(solution)/shard_map/ppermute | solution.py:410
  31.9 9.0 %collective-permute-start.15 = (bf16[144,1024]{1,0:T(8,128)(2,1)S(1)}, bf16[144,1024]{1,0:T(8,128)(2,1)S(1)}, u32[]{:S(2)}, u32[]{:S(2)}) collective-permute-start(bf16[144,1024]{1,0:T(8,128)(2,1)S(1)} %relay.5.refs_0_), channel_id=1, source_target_pairs={{0,1},{1,0},{2,3},{3,2},{4,5},{5,4},{6,7},{7,6},{8,9},{9,8},{10,11... | collective-permute-start | bytes 884744 | tf_op jit(solution)/shard_map/ppermute | solution.py:410
  40.2 6.9 %collective-permute-start.14 = (bf16[144,1024]{1,0:T(8,128)(2,1)S(1)}, bf16[144,1024]{1,0:T(8,128)(2,1)S(1)}, u32[]{:S(2)}, u32[]{:S(2)}) collective-permute-start(bf16[144,1024]{1,0:T(8,128)(2,1)S(1)} %get-tuple-element.74), channel_id=1, source_target_pairs={{0,1},{1,0},{2,3},{3,2},{4,5},{5,4},{6,7},{7,6},{8,9},{9,8},{10,11... | collective-permute-start | bytes 884744 | tf_op jit(solution)/shard_map/ppermute | solution.py:410
  43.2 2.8 %collective-permute-start.16 = (bf16[512,1024]{1,0:T(8,128)(2,1)S(1)}, bf16[512,1024]{1,0:T(8,128)(2,1)S(1)}, u32[]{:S(2)}, u32[]{:S(2)}) collective-permute-start(bf16[512,1024]{1,0:T(8,128)(2,1)S(1)} %get-tuple-element.78), channel_id=1, source_target_pairs={{0,8},{8,0},{1,9},{9,1},{2,10},{10,2},{3,11},{11,3},{4,12},{12,4},... | collective-permute-start | bytes 3145736 | tf_op jit(solution)/shard_map/ppermute | solution.py:410
  45.5 2.8 %collective-permute-start.17 = (bf16[512,1024]{1,0:T(8,128)(2,1)S(1)}, bf16[512,1024]{1,0:T(8,128)(2,1)S(1)}, u32[]{:S(2)}, u32[]{:S(2)}) collective-permute-start(bf16[512,1024]{1,0:T(8,128)(2,1)S(1)} %get-tuple-element.81), channel_id=1, source_target_pairs={{0,8},{8,0},{1,9},{9,1},{2,10},{10,2},{3,11},{11,3},{4,12},{12,4},... | collective-permute-start | bytes 3145736 | tf_op jit(solution)/shard_map/ppermute | solution.py:410

commit v17 on v16

--- a/solution.py
+++ b/solution.py
@@ -10,8 +10,9 @@
 
 EXPERTS = 4
 CAP = 36
-WIDE = 1024
+WIDE = 2048
 STRIP = 512
+SLOPES = 1024
 SLICE = 256
 MIB = 1024 * 1024
 LARGE = pltpu.CompilerParams(vmem_limit_bytes=16 * MIB)
@@ -167,7 +168,7 @@
     )(kept(value))
 
 
-def forward_kernel(n, fetch, down, pair, unused, *refs):
+def forward_kernel(n, down, pair, unused, *refs):
     refs = list(refs[unused:])
     xs = [refs.pop(0) for _ in range(n)]
     wg_ref, wu_ref = refs.pop(0), refs.pop(0)
@@ -175,82 +176,54 @@
     other_ref = refs.pop(0) if pair else None
     act_ref, coef_ref = refs.pop(0), refs.pop(0)
     shares = [refs.pop(0) for _ in range(EXPERTS if pair else down)]
-    if fetch:
-        sources, sems = (wg_ref, wu_ref), refs.pop()
-        wg_ref, wu_ref = refs.pop(0), refs.pop(0)
-    acc_ref = refs.pop(0) if down else None
     part = xs[0].shape[0]
     x_ref = xs[0]
     if n > 1:
         x_ref = refs.pop(0)
         for i in range(n):
             x_ref[i * part : (i + 1) * part, :] = xs[i][...]
-    steps = wg_ref.shape[1] // (2 * WIDE)
-
-    def copies(j):
-        cols = pl.ds(pl.multiple_of(j * (2 * WIDE), (2 * WIDE)), (2 * WIDE))
-        return [
-            pltpu.make_async_copy(source.at[:, cols], target.at[:, cols], sems.at[j, i])
-            for i, (source, target) in enumerate(zip(sources, (wg_ref, wu_ref)))
-        ]
-
-    if fetch:
-        for j in range(steps):
-            for copy in copies(j):
-                copy.start()
-    if down:
-        acc_ref[...] = jnp.zeros_like(acc_ref)
-
-    @pl.loop(0, steps)
-    def _(j):
-        if fetch:
-            for copy in copies(j):
-                copy.wait()
-        for i in range(2):
-            cols = pl.ds(pl.multiple_of(j * (2 * WIDE) + i * WIDE, WIDE), WIDE)
-            gate = jnp.dot(x_ref[...], wg_ref[:, cols], preferred_element_type=F32)
-            up = jnp.dot(x_ref[...], wu_ref[:, cols], preferred_element_type=F32)
-            act, slope = silu_parts(gate)
-            act_ref[:, cols] = act.astype(BF16)
-            coef_ref[:, cols] = (up * slope).astype(BF16)
-            if down:
-                hidden = (act[:part] * up[:part]).astype(BF16)
-                acc_ref[...] += jnp.dot(hidden, wd_ref[cols, :], preferred_element_type=F32)
+    total = None
+    for start in range(0, wg_ref.shape[1], WIDE):
+        cols = slice(start, start + WIDE)
+        gate = jnp.dot(x_ref[...], wg_ref[:, cols], preferred_element_type=F32)
+        up = jnp.dot(x_ref[...], wu_ref[:, cols], preferred_element_type=F32)
+        act, slope = silu_parts(gate)
+        act_ref[:, cols] = act.astype(BF16)
+        coef_ref[:, cols] = (up * slope).astype(BF16)
+        if down:
+            hidden = (act[:part] * up[:part]).astype(BF16)
+            share = jnp.dot(hidden, wd_ref[cols, :], preferred_element_type=F32)
+            total = share if total is None else total + share
 
     if pair:
         other = other_ref[...].astype(F32)
         for k in range(EXPERTS):
             rows = slice(k * CAP, (k + 1) * CAP)
-            block = jnp.concatenate([other[rows], acc_ref[rows, :]], axis=0).astype(BF16)
+            block = jnp.concatenate([other[rows], total[rows]], axis=0).astype(BF16)
             shares[k][...] = block
     elif down:
-        shares[0][...] = acc_ref[...].astype(BF16)
-
-
-def forward(xs, wg, wu, wd=None, other=None, fetch=False, earlier=(), cost=CHEAP):
+        shares[0][...] = total.astype(BF16)
+
+
+def forward(xs, wg, wu, wd=None, other=None, earlier=(), cost=CHEAP):
     n, (part, width), cols = len(xs), xs[0].shape, wg.shape[1]
     rows = n * part
     down, pair = wd is not None, other is not None
     shares = [jax.ShapeDtypeStruct((part, width), BF16)] * down
     if pair:
         shares = [jax.ShapeDtypeStruct((2 * CAP, width), BF16)] * EXPERTS
-    weights = [kept(wg), kept(wu)] if fetch else [wg, wu]
-    return pl.pallas_call(
-        functools.partial(forward_kernel, n, fetch, down, pair, len(earlier)),
+    return pl.pallas_call(
+        functools.partial(forward_kernel, n, down, pair, len(earlier)),
         out_shape=[jax.ShapeDtypeStruct((rows, cols), BF16)] * 2
-        + shares
-        + [pltpu.VMEM(wg.shape, wg.dtype)] * (2 * fetch),
+        + shares,
         in_specs=[ANYWHERE] * len(earlier)
         + [HERE] * n
-        + [AFAR if fetch else HERE] * 2
-        + [HERE] * (down + pair),
-        scratch_shapes=[pltpu.VMEM((part, width), F32)] * down
-        + [pltpu.VMEM((rows, width), BF16)] * (n > 1)
-        + [pltpu.SemaphoreType.DMA((cols // (2 * WIDE), 2))] * fetch,
+        + [HERE] * (2 + down + pair),
+        scratch_shapes=[pltpu.VMEM((rows, width), BF16)] * (n > 1),
         compiler_params=LARGE,
         cost_estimate=cost,
-        name="forward" + "_fetch" * fetch + "_down" * down,
-    )(*earlier, *xs, *weights, *([wd] * down), *([other] * pair))
+        name="forward" + "_down" * down,
+    )(*earlier, *xs, wg, wu, *([wd] * down), *([other] * pair))
 
 
 def turn_kernel(_, __, *refs):
@@ -283,8 +256,8 @@
     part = gs[0].shape[0]
     for i in range(n):
         g_ref[i * part : (i + 1) * part, :] = gs[i][...]
-    for start in range(0, wdt_ref.shape[1], STRIP):
-        cols = slice(start, start + STRIP)
+    for start in range(0, wdt_ref.shape[1], SLOPES):
+        cols = slice(start, start + SLOPES)
         d_hidden = jnp.dot(g_ref[...], wdt_ref[:, cols], preferred_element_type=F32)
         for i in range(n):
             rows = slice(i * part, (i + 1) * part)

time: 49.7 us -> 49.6 us (level)
  no operation moved by 1% of the time
where the time goes in v17:
time: 49.6 us; the launch traced here: 49.4 us
  starting transfers between devices  24.7 us (50%)
  Pallas kernels  22.1 us (45%)
  waiting for transfers between devices  1.57 us (3%)
  between operations  0.99 us (2%)
    ppermute x9, starting transfers between devices, across_planes(): lax.ppermute(blocks[k], 'arch', [(i, i ^ k) for i in range(EXPERTS)])  14.7 us
    ppermute x9, starting transfers between devices, swap(): return lax.ppermute(value, axis, [(0, 1), (1, 0)])  10.1 us
    pallas_call x4, Pallas kernels, forward(): pl.pallas_call(functools.partial(forward_kernel, n, down, pair, len(earli...  7.45 us
    pallas_call x2, Pallas kernels, backward(): pl.pallas_call(functools.partial(backward_kernel, first), out_shape=[jax....  4.43 us
    pallas_call x1, Pallas kernels, flip(): pl.pallas_call(flip_kernel, out_shape=[pltpu.VMEM(value.shape, value.dtyp...  2.88 us
    pallas_call x2, Pallas kernels, finish(): pl.pallas_call(functools.partial(finish_kernel, spans, more, len(earlier)...  2.21 us
    pallas_call x1, Pallas kernels, slopes(): pl.pallas_call(functools.partial(slopes_kernel, n), out_shape=[jax.ShapeD...  2.19 us
    pallas_call x1, Pallas kernels, pack(): pl.pallas_call(pack_kernel, out_shape=[jax.ShapeDtypeStruct((EXPERTS * CA...  1.46 us
  transfers between devices with their start and end apart: 18, of which 3 were waited for; matrix products, arithmetic and copies ran while one was open for 0% of the time, Pallas kernels for 40%

profile of v17, /device:TPU:0, one launch (start us, length us, event | category | flops | bytes accessed | tf_op | source)
XLA Modules:
  0.0 49.4 jit_solution(2471774171707931082)
XLA Ops:
  0.6 1.5 %pack.1 = (bf16[144,128]{1,0:T(8,128)(2,1)S(1)}, bf16[36,1024]{1,0:T(8,128)(2,1)S(1)}, bf16[36,1024]{1,0:T(8,128)(2,1)S(1)}, bf16[36,1024]{1,0:T(8,128)(2,1)S(1)...) custom-call(s32[1]{0:T(128)} %bitcast.plane_ref, ...), custom_call_target="tpu_custom_call" | custom-call | tf_op jit(solution)/shard_map/pack/pallas_call | solution.py:80
  2.1 5.1 %collective-permute-start = (bf16[36,1024]{1,0:T(8,128)(2,1)S(1)}, bf16[36,1024]{1,0:T(8,128)(2,1)S(1)}, u32[]{:S(2)}, u32[]{:S(2)}) collective-permute-start(bf16[36,1024]{1,0:T(8,128)(2,1)S(1)} %get-tuple-element.45), channel_id=1, source_target_pairs={{0,6},{2,4},{4,2},{6,0},{1,7},{3,5},{5,3},{7,1},{8,14},{10,12},{12... | collective-permute-start | bytes 221192 | tf_op jit(solution)/shard_map/ppermute | solution.py:388
  7.2 0.6 %collective-permute-start.2 = (bf16[36,1024]{1,0:T(8,128)(2,1)S(1)}, bf16[36,1024]{1,0:T(8,128)(2,1)S(1)}, u32[]{:S(2)}, u32[]{:S(2)}) collective-permute-start(bf16[36,1024]{1,0:T(8,128)(2,1)S(1)} %get-tuple-element.47), channel_id=1, source_target_pairs={{0,2},{2,0},{4,6},{6,4},{1,3},{3,1},{5,7},{7,5},{8,10},{10,8},{12,... | collective-permute-start | bytes 221192 | tf_op jit(solution)/shard_map/ppermute | solution.py:388
  7.9 2.9 %flip.1 = (bf16[2048,1024]{1,0:T(8,128)(2,1)S(1)}, bf16[1024,2048]{1,0:T(8,128)(2,1)S(1)}) custom-call(bf16[2048,1024]{1,0:T(8,128)(2,1)} %source_ref), custom_call_target="tpu_custom_call" | custom-call | tf_op jit(solution)/shard_map/flip/pallas_call | solution.py:159
  10.8 3.8 %collective-permute-start.7 = (bf16[36,1024]{1,0:T(8,128)(2,1)S(1)}, bf16[36,1024]{1,0:T(8,128)(2,1)S(1)}, u32[]{:S(2)}, u32[]{:S(2)}) collective-permute-start(bf16[36,1024]{1,0:T(8,128)(2,1)S(1)} %get-tuple-element.62), channel_id=1, source_target_pairs={{0,6},{2,4},{4,2},{6,0},{1,7},{3,5},{5,3},{7,1},{8,14},{10,12},{12... | collective-permute-start | bytes 221192 | tf_op jit(solution)/shard_map/ppermute | solution.py:388
  14.6 0.6 %collective-permute-start.9 = (bf16[36,1024]{1,0:T(8,128)(2,1)S(1)}, bf16[36,1024]{1,0:T(8,128)(2,1)S(1)}, u32[]{:S(2)}, u32[]{:S(2)}) collective-permute-start(bf16[36,1024]{1,0:T(8,128)(2,1)S(1)} %get-tuple-element.64), channel_id=1, source_target_pairs={{0,2},{2,0},{4,6},{6,4},{1,3},{3,1},{5,7},{7,5},{8,10},{10,8},{12,... | collective-permute-start | bytes 221192 | tf_op jit(solution)/shard_map/ppermute | solution.py:388
  15.3 1.7 %collective-permute-start.3 = (bf16[144,1024]{1,0:T(8,128)(2,1)S(1)}, bf16[144,1024]{1,0:T(8,128)(2,1)S(1)}, u32[]{:S(2)}, u32[]{:S(2)}) collective-permute-start(bf16[144,1024]{1,0:T(8,128)(2,1)S(1)} %join.2.refs_0_.refs_4_), channel_id=1, source_target_pairs={{0,1},{1,0},{2,3},{3,2},{4,5},{5,4},{6,7},{7,6},{8,9},{9,8},{10,11... | collective-permute-start | bytes 884744 | tf_op jit(solution)/shard_map/ppermute | solution.py:383
  17.0 1.5 %collective-permute-start.12 = (bf16[144,1024]{1,0:T(8,128)(2,1)S(1)}, bf16[144,1024]{1,0:T(8,128)(2,1)S(1)}, u32[]{:S(2)}, u32[]{:S(2)}) collective-permute-start(bf16[144,1024]{1,0:T(8,128)(2,1)S(1)} %join.2.refs_0_.refs_4_), channel_id=1, source_target_pairs={{0,16},{16,0},{1,17},{17,1},{2,18},{18,2},{3,19},{19,3},{4,20},{20... | collective-permute-start | bytes 884744 | tf_op jit(solution)/shard_map/ppermute | solution.py:383
  18.5 2.1 %forward_down.2 = (bf16[144,2048]{1,0:T(8,128)(2,1)S(1)}, bf16[144,2048]{1,0:T(8,128)(2,1)S(1)}, bf16[144,1024]{1,0:T(8,128)(2,1)S(1)}) custom-call(bf16[144,1024]{1,0:T(8,128)(2,1)S(1)} %join.2.refs_0_.refs_4_, bf16[1024,2048]{1,0:T(8,128)(2,1)S(1)} %copy-done, bf16[1024,2048]{1,0:T(8,128)(2,1)S(1)} %copy-done.1, ...), custom_call_target="tpu_custom_call" | custom-call | tf_op jit(solution)/shard_map/forward_down/pallas_call | solution.py:215
  20.7 0.4 collective-permute-done.8.refs_2_
  21.2 1.6 %collective-permute-start.11 = (bf16[144,1024]{1,0:T(8,128)(2,1)S(1)}, bf16[144,1024]{1,0:T(8,128)(2,1)S(1)}, u32[]{:S(2)}, u32[]{:S(2)}) collective-permute-start(bf16[144,1024]{1,0:T(8,128)(2,1)S(1)} %join.3.refs_0_), channel_id=1, source_target_pairs={{0,16},{16,0},{1,17},{17,1},{2,18},{18,2},{3,19},{19,3},{4,20},{20... | collective-permute-start | bytes 884744 | tf_op jit(solution)/shard_map/ppermute | solution.py:383
  22.7 1.5 %collective-permute-start.10 = (bf16[144,1024]{1,0:T(8,128)(2,1)S(1)}, bf16[144,1024]{1,0:T(8,128)(2,1)S(1)}, u32[]{:S(2)}, u32[]{:S(2)}) collective-permute-start(bf16[144,1024]{1,0:T(8,128)(2,1)S(1)} %join.3.refs_0_), channel_id=1, source_target_pairs={{0,1},{1,0},{2,3},{3,2},{4,5},{5,4},{6,7},{7,6},{8,9},{9,8},{10,11... | collective-permute-start | bytes 884744 | tf_op jit(solution)/shard_map/ppermute | solution.py:383
  24.2 2.2 %forward_down.3 = (bf16[144,2048]{1,0:T(8,128)(2,1)S(1)}, bf16[144,2048]{1,0:T(8,128)(2,1)S(1)}, bf16[72,1024]{1,0:T(8,128)(2,1)S(1)}, bf16[72,1024]{1,0:T(8,128...) custom-call(bf16[144,1024]{1,0:T(8,128)(2,1)S(1)} %collective-permute-done.3.refs_0_.refs_1_.refs_5_, ...), custom_call_target="tpu_custom_call" | custom-call | tf_op jit(solution)/shard_map/forward_down/pallas_call | solution.py:215
  26.4 0.5 collective-permute-start.4
  26.9 2.9 %collective-permute-start.5 = (bf16[72,1024]{1,0:T(8,128)(2,1)S(1)}, bf16[72,1024]{1,0:T(8,128)(2,1)S(1)}, u32[]{:S(2)}, u32[]{:S(2)}) collective-permute-start(bf16[72,1024]{1,0:T(8,128)(2,1)S(1)} %get-tuple-element.54), channel_id=1, source_target_pairs={{0,4},{2,6},{4,0},{6,2},{1,5},{3,7},{5,1},{7,3},{8,12},{10,14},{12... | collective-permute-start | bytes 442376 | tf_op jit(solution)/shard_map/ppermute | solution.py:388
  29.7 1.1 %collective-permute-start.6 = (bf16[72,1024]{1,0:T(8,128)(2,1)S(1)}, bf16[72,1024]{1,0:T(8,128)(2,1)S(1)}, u32[]{:S(2)}, u32[]{:S(2)}) collective-permute-start(bf16[72,1024]{1,0:T(8,128)(2,1)S(1)} %get-tuple-element.55), channel_id=1, source_target_pairs={{0,6},{2,4},{4,2},{6,0},{1,7},{3,5},{5,3},{7,1},{8,14},{10,12},{12... | collective-permute-start | bytes 442376 | tf_op jit(solution)/shard_map/ppermute | solution.py:388
  30.9 1.0 %collective-permute-start.13 = (bf16[144,1024]{1,0:T(8,128)(2,1)S(1)}, bf16[144,1024]{1,0:T(8,128)(2,1)S(1)}, u32[]{:S(2)}, u32[]{:S(2)}) collective-permute-start(bf16[144,1024]{1,0:T(8,128)(2,1)S(1)} %relay.4.refs_1_), channel_id=1, source_target_pairs={{0,16},{16,0},{1,17},{17,1},{2,18},{18,2},{3,19},{19,3},{4,20},{20... | collective-permute-start | bytes 884744 | tf_op jit(solution)/shard_map/ppermute | solution.py:383
  31.9 1.8 %collective-permute-start.15 = (bf16[144,1024]{1,0:T(8,128)(2,1)S(1)}, bf16[144,1024]{1,0:T(8,128)(2,1)S(1)}, u32[]{:S(2)}, u32[]{:S(2)}) collective-permute-start(bf16[144,1024]{1,0:T(8,128)(2,1)S(1)} %relay.5.refs_0_), channel_id=1, source_target_pairs={{0,1},{1,0},{2,3},{3,2},{4,5},{5,4},{6,7},{7,6},{8,9},{9,8},{10,11... | collective-permute-start | bytes 884744 | tf_op jit(solution)/shard_map/ppermute | solution.py:383
  33.7 1.6 %forward.2 = (bf16[144,2048]{1,0:T(8,128)(2,1)S(1)}, bf16[144,2048]{1,0:T(8,128)(2,1)S(1)}) custom-call(bf16[144,1024]{1,0:T(8,128)(2,1)S(1)} %relay.5.refs_0_, bf16[144,1024]{1,0:T(8,128)(2,1)S(1)} %collective-permute-done.12._.refs_1_.refs_2_.refs_6_, bf16[1024,2048]{1,0:T(8,128)(2,1)S(1)} %copy-done, bf16[1024,2048]{1,0:T(8,128)(2,1)S(1)} %copy-done.1), custom_call_target="tpu_custom_call" | custom-call | flops 20000000000 | tf_op jit(solution)/shard_map/forward/pallas_call | solution.py:215
  35.3 2.2 %slopes.1 = (bf16[432,2048]{1,0:T(8,128)(2,1)S(1)}, bf16[432,2048]{1,0:T(8,128)(2,1)S(1)}) custom-call(bf16[144,1024]{1,0:T(8,128)(2,1)S(1)} %join.3.refs_0_, bf16[144,1024]{1,0:T(8,128)(2,1)S(1)} %collective-permute-done.10.refs_2_.refs_1_, bf16[144,1024]{1,0:T(8,128)(2,1)S(1)} %collective-permute-done.11.refs_2_.refs_0_, ...), custom_call_target="tpu_custom_call" | custom-call | tf_op jit(solution)/shard_map/slopes/pallas_call | solution.py:270
  37.5 1.0 %collective-permute-done.13.refs_1_.refs_3_.refs_7_ = bf16[144,1024]{1,0:T(8,128)(2,1)S(1)} collective-permute-done((bf16[144,1024]{1,0:T(8,128)(2,1)S(1)}, bf16[144,1024]{1,0:T(8,128)(2,1)S(1)}, u32[]{:S(2)}, u32[]{:S(2)}) %collective-permute-start.13) | collective-permute-done | bytes 294944 | tf_op jit(solution)/shard_map/ppermute | solution.py:383
  38.5 1.6 %forward.3 = (bf16[144,2048]{1,0:T(8,128)(2,1)S(1)}, bf16[144,2048]{1,0:T(8,128)(2,1)S(1)}) custom-call(bf16[432,2048]{1,0:T(8,128)(2,1)S(1)} %get-tuple-element.71.refs_0_.dg_ref, bf16[144,1024]{1,0:T(8,128)(2,1)S(1)} %collective-permute-done.13.refs_1_.refs_3_.refs_7_, bf16[1024,2048]{1,0:T(8,128)(2,1)S(1)} %copy-done, bf16[1024,2048]{1,0:T(8,128)(2,1)S(1)} %copy-done.1), custom_call_target="tpu_custom_call" | custom-call | tf_op jit(solution)/shard_map/forward/pallas_call | solution.py:215
  40.1 0.1 split.1
  40.2 0.3 collective-permute-start.14
  40.5 0.2 turn.1.xt_ref
  40.8 2.3 %backward.2 = (bf16[512,1024]{1,0:T(8,128)(2,1)S(1)}, bf16[512,1024]{1,0:T(8,128)(2,1)S(1)}) custom-call(bf16[512,576]{1,0:T(8,128)(2,1)S(1)} %turn.1.xt_ref, bf16[144,1024]{1,0:T(8,128)(2,1)S(1)} %collective-permute-done.15.g_ref, bf16[144,2048]{1,0:T(8,128)(2,1)S(1)} %get-tuple-element.72.refs_4_.act_ref, ...), custom_call_target="tpu_custom_call" | custom-call | flops 20000000000 | tf_op jit(solution)/shard_map/backward/pallas_call | solution.py:297
  43.2 2.1 %backward.3 = (bf16[512,1024]{1,0:T(8,128)(2,1)S(1)}, bf16[512,1024]{1,0:T(8,128)(2,1)S(1)}) custom-call(bf16[512,576]{1,0:T(8,128)(2,1)S(1)} %turn.1.xt_ref, bf16[144,1024]{1,0:T(8,128)(2,1)S(1)} %collective-permute-done.15.g_ref, bf16[144,2048]{1,0:T(8,128)(2,1)S(1)} %get-tuple-element.72.refs_4_.act_ref, ...), custom_call_target="tpu_custom_call" | custom-call | flops 20000000000 | tf_op jit(solution)/shard_map/backward/pallas_call | solution.py:297
  45.3 0.6 %collective-permute-start.17 = (bf16[512,1024]{1,0:T(8,128)(2,1)S(1)}, bf16[512,1024]{1,0:T(8,128)(2,1)S(1)}, u32[]{:S(2)}, u32[]{:S(2)}) collective-permute-start(bf16[512,1024]{1,0:T(8,128)(2,1)S(1)} %get-tuple-element.81), channel_id=1, source_target_pairs={{0,8},{8,0},{1,9},{9,1},{2,10},{10,2},{3,11},{11,3},{4,12},{12,4},... | collective-permute-start | bytes 3145736 | tf_op jit(solution)/shard_map/ppermute | solution.py:383
  45.9 1.1 %finish.2 = (bf16[256,2048]{1,0:T(8,128)(2,1)}, bf16[256,2048]{1,0:T(8,128)(2,1)}) custom-call(bf16[512,1024]{1,0:T(8,128)(2,1)S(1)} %get-tuple-element.77.refs_0_, bf16[512,1024]{1,0:T(8,128)(2,1)S(1)} %collective-permute-done.16.refs_1_), custom_call_target="tpu_custom_call" | custom-call | tf_op jit(solution)/shard_map/finish/pallas_call | solution.py:333
  47.0 1.0 %unpack.1 = bf16[128,1024]{1,0:T(8,128)(2,1)} custom-call(bf16[144,128]{1,0:T(8,128)(2,1)S(1)} %get-tuple-element.44.placer_ref, bf16[144,1024]{1,0:T(8,128)(2,1)S(1)} %get-tuple-element.73.mine_ref, bf16[144,1024]{1,0:T(8,128)(2,1)S(1)} %collective-permute-done.14.got_ref, bf16[256,2048]{1,0:T(8,128)(2,1)} %get-tuple-element.79.refs_0_.refs_2_), custom_call_target="tpu_custom_call" | custom-call | flops 20000000000 | tf_op jit(solution)/shard_map/unpack/pallas_call | solution.py:372
  48.1 0.1 collective-permute-done.17.refs_1_
  48.2 1.1 %finish.3 = (bf16[256,2048]{1,0:T(8,128)(2,1)}, bf16[256,2048]{1,0:T(8,128)(2,1)}) custom-call(bf16[512,1024]{1,0:T(8,128)(2,1)S(1)} %get-tuple-element.80.refs_0_, bf16[512,1024]{1,0:T(8,128)(2,1)S(1)} %collective-permute-done.17.refs_1_, bf16[256,2048]{1,0:T(8,128)(2,1)} %get-tuple-element.79.refs_0_.refs_2_, ...), custom_call_target="tpu_custom_call", output_to_operand_aliasing={{0}: (2, {}), {1}: (3, {})} | custom-call | tf_op jit(solution)/shard_map/finish/pallas_call | solution.py:333
  (28 shorter events, 0.3 us)
Async XLA Ops:
  2.1 12.5 %collective-permute-start = (bf16[36,1024]{1,0:T(8,128)(2,1)S(1)}, bf16[36,1024]{1,0:T(8,128)(2,1)S(1)}, u32[]{:S(2)}, u32[]{:S(2)}) collective-permute-start(bf16[36,1024]{1,0:T(8,128)(2,1)S(1)} %get-tuple-element.45), channel_id=1, source_target_pairs={{0,6},{2,4},{4,2},{6,0},{1,7},{3,5},{5,3},{7,1},{8,14},{10,12},{12... | collective-permute-start | bytes 221192 | tf_op jit(solution)/shard_map/ppermute | solution.py:388
  7.2 8.0 %collective-permute-start.1 = (bf16[36,1024]{1,0:T(8,128)(2,1)S(1)}, bf16[36,1024]{1,0:T(8,128)(2,1)S(1)}, u32[]{:S(2)}, u32[]{:S(2)}) collective-permute-start(bf16[36,1024]{1,0:T(8,128)(2,1)S(1)} %get-tuple-element.46), channel_id=1, source_target_pairs={{0,4},{2,6},{4,0},{6,2},{1,5},{3,7},{5,1},{7,3},{8,12},{10,14},{12... | collective-permute-start | bytes 221192 | tf_op jit(solution)/shard_map/ppermute | solution.py:388
  7.2 8.0 %collective-permute-start.2 = (bf16[36,1024]{1,0:T(8,128)(2,1)S(1)}, bf16[36,1024]{1,0:T(8,128)(2,1)S(1)}, u32[]{:S(2)}, u32[]{:S(2)}) collective-permute-start(bf16[36,1024]{1,0:T(8,128)(2,1)S(1)} %get-tuple-element.47), channel_id=1, source_target_pairs={{0,2},{2,0},{4,6},{6,4},{1,3},{3,1},{5,7},{7,5},{8,10},{10,8},{12,... | collective-permute-start | bytes 221192 | tf_op jit(solution)/shard_map/ppermute | solution.py:388
  7.9 10.7 %copy-start = (bf16[1024,2048]{1,0:T(8,128)(2,1)S(1)}, bf16[1024,2048]{1,0:T(8,128)(2,1)}, u32[]{:S(2)}) copy-start(bf16[1024,2048]{1,0:T(8,128)(2,1)} %refs_2_.7) | copy-start | bytes 12582916
  7.9 10.7 %copy-start.1 = (bf16[1024,2048]{1,0:T(8,128)(2,1)S(1)}, bf16[1024,2048]{1,0:T(8,128)(2,1)}, u32[]{:S(2)}) copy-start(bf16[1024,2048]{1,0:T(8,128)(2,1)} %refs_3_.3) | copy-start | bytes 12582916
  10.8 9.9 %collective-permute-start.7 = (bf16[36,1024]{1,0:T(8,128)(2,1)S(1)}, bf16[36,1024]{1,0:T(8,128)(2,1)S(1)}, u32[]{:S(2)}, u32[]{:S(2)}) collective-permute-start(bf16[36,1024]{1,0:T(8,128)(2,1)S(1)} %get-tuple-element.62), channel_id=1, source_target_pairs={{0,6},{2,4},{4,2},{6,0},{1,7},{3,5},{5,3},{7,1},{8,14},{10,12},{12... | collective-permute-start | bytes 221192 | tf_op jit(solution)/shard_map/ppermute | solution.py:388
  14.6 6.5 %collective-permute-start.8 = (bf16[36,1024]{1,0:T(8,128)(2,1)S(1)}, bf16[36,1024]{1,0:T(8,128)(2,1)S(1)}, u32[]{:S(2)}, u32[]{:S(2)}) collective-permute-start(bf16[36,1024]{1,0:T(8,128)(2,1)S(1)} %get-tuple-element.63), channel_id=1, source_target_pairs={{0,4},{2,6},{4,0},{6,2},{1,5},{3,7},{5,1},{7,3},{8,12},{10,14},{12... | collective-permute-start | bytes 221192 | tf_op jit(solution)/shard_map/ppermute | solution.py:388
  14.6 6.5 %collective-permute-start.9 = (bf16[36,1024]{1,0:T(8,128)(2,1)S(1)}, bf16[36,1024]{1,0:T(8,128)(2,1)S(1)}, u32[]{:S(2)}, u32[]{:S(2)}) collective-permute-start(bf16[36,1024]{1,0:T(8,128)(2,1)S(1)} %get-tuple-element.64), channel_id=1, source_target_pairs={{0,2},{2,0},{4,6},{6,4},{1,3},{3,1},{5,7},{7,5},{8,10},{10,8},{12,... | collective-permute-start | bytes 221192 | tf_op jit(solution)/shard_map/ppermute | solution.py:388
  15.3 8.9 %collective-permute-start.3 = (bf16[144,1024]{1,0:T(8,128)(2,1)S(1)}, bf16[144,1024]{1,0:T(8,128)(2,1)S(1)}, u32[]{:S(2)}, u32[]{:S(2)}) collective-permute-start(bf16[144,1024]{1,0:T(8,128)(2,1)S(1)} %join.2.refs_0_.refs_4_), channel_id=1, source_target_pairs={{0,1},{1,0},{2,3},{3,2},{4,5},{5,4},{6,7},{7,6},{8,9},{9,8},{10,11... | collective-permute-start | bytes 884744 | tf_op jit(solution)/shard_map/ppermute | solution.py:383
  17.0 12.7 %collective-permute-start.12 = (bf16[144,1024]{1,0:T(8,128)(2,1)S(1)}, bf16[144,1024]{1,0:T(8,128)(2,1)S(1)}, u32[]{:S(2)}, u32[]{:S(2)}) collective-permute-start(bf16[144,1024]{1,0:T(8,128)(2,1)S(1)} %join.2.refs_0_.refs_4_), channel_id=1, source_target_pairs={{0,16},{16,0},{1,17},{17,1},{2,18},{18,2},{3,19},{19,3},{4,20},{20... | collective-permute-start | bytes 884744 | tf_op jit(solution)/shard_map/ppermute | solution.py:383
  21.2 9.7 %collective-permute-start.11 = (bf16[144,1024]{1,0:T(8,128)(2,1)S(1)}, bf16[144,1024]{1,0:T(8,128)(2,1)S(1)}, u32[]{:S(2)}, u32[]{:S(2)}) collective-permute-start(bf16[144,1024]{1,0:T(8,128)(2,1)S(1)} %join.3.refs_0_), channel_id=1, source_target_pairs={{0,16},{16,0},{1,17},{17,1},{2,18},{18,2},{3,19},{19,3},{4,20},{20... | collective-permute-start | bytes 884744 | tf_op jit(solution)/shard_map/ppermute | solution.py:383
  22.7 9.2 %collective-permute-start.10 = (bf16[144,1024]{1,0:T(8,128)(2,1)S(1)}, bf16[144,1024]{1,0:T(8,128)(2,1)S(1)}, u32[]{:S(2)}, u32[]{:S(2)}) collective-permute-start(bf16[144,1024]{1,0:T(8,128)(2,1)S(1)} %join.3.refs_0_), channel_id=1, source_target_pairs={{0,1},{1,0},{2,3},{3,2},{4,5},{5,4},{6,7},{7,6},{8,9},{9,8},{10,11... | collective-permute-start | bytes 884744 | tf_op jit(solution)/shard_map/ppermute | solution.py:383
  26.4 13.7 %collective-permute-start.4 = (bf16[72,1024]{1,0:T(8,128)(2,1)S(1)}, bf16[72,1024]{1,0:T(8,128)(2,1)S(1)}, u32[]{:S(2)}, u32[]{:S(2)}) collective-permute-start(bf16[72,1024]{1,0:T(8,128)(2,1)S(1)} %get-tuple-element.53), channel_id=1, source_target_pairs={{0,2},{2,0},{4,6},{6,4},{1,3},{3,1},{5,7},{7,5},{8,10},{10,8},{12,... | collective-permute-start | bytes 442376 | tf_op jit(solution)/shard_map/ppermute | solution.py:388
  26.9 13.3 %collective-permute-start.5 = (bf16[72,1024]{1,0:T(8,128)(2,1)S(1)}, bf16[72,1024]{1,0:T(8,128)(2,1)S(1)}, u32[]{:S(2)}, u32[]{:S(2)}) collective-permute-start(bf16[72,1024]{1,0:T(8,128)(2,1)S(1)} %get-tuple-element.54), channel_id=1, source_target_pairs={{0,4},{2,6},{4,0},{6,2},{1,5},{3,7},{5,1},{7,3},{8,12},{10,14},{12... | collective-permute-start | bytes 442376 | tf_op jit(solution)/shard_map/ppermute | solution.py:388
  29.7 10.4 %collective-permute-start.6 = (bf16[72,1024]{1,0:T(8,128)(2,1)S(1)}, bf16[72,1024]{1,0:T(8,128)(2,1)S(1)}, u32[]{:S(2)}, u32[]{:S(2)}) collective-permute-start(bf16[72,1024]{1,0:T(8,128)(2,1)S(1)} %get-tuple-element.55), channel_id=1, source_target_pairs={{0,6},{2,4},{4,2},{6,0},{1,7},{3,5},{5,3},{7,1},{8,14},{10,12},{12... | collective-permute-start | bytes 442376 | tf_op jit(solution)/shard_map/ppermute | solution.py:388
  30.9 7.6 %collective-permute-start.13 = (bf16[144,1024]{1,0:T(8,128)(2,1)S(1)}, bf16[144,1024]{1,0:T(8,128)(2,1)S(1)}, u32[]{:S(2)}, u32[]{:S(2)}) collective-permute-start(bf16[144,1024]{1,0:T(8,128)(2,1)S(1)} %relay.4.refs_1_), channel_id=1, source_target_pairs={{0,16},{16,0},{1,17},{17,1},{2,18},{18,2},{3,19},{19,3},{4,20},{20... | collective-permute-start | bytes 884744 | tf_op jit(solution)/shard_map/ppermute | solution.py:383
  31.9 8.9 %collective-permute-start.15 = (bf16[144,1024]{1,0:T(8,128)(2,1)S(1)}, bf16[144,1024]{1,0:T(8,128)(2,1)S(1)}, u32[]{:S(2)}, u32[]{:S(2)}) collective-permute-start(bf16[144,1024]{1,0:T(8,128)(2,1)S(1)} %relay.5.refs_0_), channel_id=1, source_target_pairs={{0,1},{1,0},{2,3},{3,2},{4,5},{5,4},{6,7},{7,6},{8,9},{9,8},{10,11... | collective-permute-start | bytes 884744 | tf_op jit(solution)/shard_map/ppermute | solution.py:383
  40.2 6.8 %collective-permute-start.14 = (bf16[144,1024]{1,0:T(8,128)(2,1)S(1)}, bf16[144,1024]{1,0:T(8,128)(2,1)S(1)}, u32[]{:S(2)}, u32[]{:S(2)}) collective-permute-start(bf16[144,1024]{1,0:T(8,128)(2,1)S(1)} %get-tuple-element.74), channel_id=1, source_target_pairs={{0,1},{1,0},{2,3},{3,2},{4,5},{5,4},{6,7},{7,6},{8,9},{9,8},{10,11... | collective-permute-start | bytes 884744 | tf_op jit(solution)/shard_map/ppermute | solution.py:383
  43.1 2.8 %collective-permute-start.16 = (bf16[512,1024]{1,0:T(8,128)(2,1)S(1)}, bf16[512,1024]{1,0:T(8,128)(2,1)S(1)}, u32[]{:S(2)}, u32[]{:S(2)}) collective-permute-start(bf16[512,1024]{1,0:T(8,128)(2,1)S(1)} %get-tuple-element.78), channel_id=1, source_target_pairs={{0,8},{8,0},{1,9},{9,1},{2,10},{10,2},{3,11},{11,3},{4,12},{12,4},... | collective-permute-start | bytes 3145736 | tf_op jit(solution)/shard_map/ppermute | solution.py:383
  45.3 2.8 %collective-permute-start.17 = (bf16[512,1024]{1,0:T(8,128)(2,1)S(1)}, bf16[512,1024]{1,0:T(8,128)(2,1)S(1)}, u32[]{:S(2)}, u32[]{:S(2)}) collective-permute-start(bf16[512,1024]{1,0:T(8,128)(2,1)S(1)} %get-tuple-element.81), channel_id=1, source_target_pairs={{0,8},{8,0},{1,9},{9,1},{2,10},{10,2},{3,11},{11,3},{4,12},{12,4},... | collective-permute-start | bytes 3145736 | tf_op jit(solution)/shard_map/ppermute | solution.py:383

commit v18 on v16

--- a/solution.py
+++ b/solution.py
@@ -94,7 +94,7 @@
 
 
 def join_kernel(*refs):
-    refs[-1][...] = stacked(refs[-2 : -2 - EXPERTS : -1]).astype(BF16)
+    refs[-1][...] = stacked(refs[-1 - EXPERTS : -1]).astype(BF16)
 
 
 def join(blocks, earlier=()):
@@ -106,7 +106,7 @@
         compiler_params=SMALL,
         cost_estimate=CHEAP,
         name="join",
-    )(*earlier, *blocks[::-1])
+    )(*earlier, *blocks)
 
 
 def relay_kernel(n, *refs):

time: 49.7 us -> 51.2 us (1.030)
  waiting for transfers between devices: 1.37 us -> 3.91 us
  starting transfers between devices: 24.8 us -> 23.8 us
    ppermute x9, waiting for transfers between devices: 0.33 us -> 2.45 us  [across_planes(): lax.ppermute(blocks[k], 'arch', [(i, i ^ k) for i in range(EXPERTS)])]
    ppermute x9, starting transfers between devices: 10.2 us -> 9.19 us  [swap(): return lax.ppermute(value, axis, [(0, 1), (1, 0)])]
  transfers between devices with their start and end apart: 18 -> 18, of which waited for: 3 -> 4; matrix products, arithmetic and copies ran while one was open for 0% -> 0% of each run, Pallas kernels for 40% -> 39%
where the time goes in v18:
time: 51.2 us; the launch traced here: 51 us
  starting transfers between devices  23.8 us (46%)
  Pallas kernels  22.4 us (44%)
  waiting for transfers between devices  3.91 us (8%)
  between operations  0.99 us (2%)
    ppermute x9, starting transfers between devices, across_planes(): lax.ppermute(blocks[k], 'arch', [(i, i ^ k) for i in range(EXPERTS)])  14.6 us
    ppermute x9, starting transfers between devices, swap(): return lax.ppermute(value, axis, [(0, 1), (1, 0)])  9.19 us
    pallas_call x4, Pallas kernels, forward(): pl.pallas_call(functools.partial(forward_kernel, n, fetch, down, pair, le...  7.65 us
    pallas_call x2, Pallas kernels, backward(): pl.pallas_call(functools.partial(backward_kernel, first), out_shape=[jax....  4.44 us
    pallas_call x1, Pallas kernels, flip(): pl.pallas_call(flip_kernel, out_shape=[pltpu.VMEM(value.shape, value.dtyp...  2.89 us
    ppermute x9, waiting for transfers between devices, across_planes(): lax.ppermute(blocks[k], 'arch', [(i, i ^ k) for i in range(EXPERTS)])  2.45 us
    pallas_call x2, Pallas kernels, finish(): pl.pallas_call(functools.partial(finish_kernel, spans, more, len(earlier)...  2.21 us
    pallas_call x1, Pallas kernels, slopes(): pl.pallas_call(functools.partial(slopes_kernel, n), out_shape=[jax.ShapeD...  2.19 us
  transfers between devices with their start and end apart: 18, of which 4 were waited for; matrix products, arithmetic and copies ran while one was open for 0% of the time, Pallas kernels for 39%

profile of v18, /device:TPU:0, one launch (start us, length us, event | category | flops | bytes accessed | tf_op | source)
XLA Modules:
  0.0 51.0 jit_solution(11322174759233587722)
XLA Ops:
  0.6 1.5 %pack.1 = (bf16[144,128]{1,0:T(8,128)(2,1)S(1)}, bf16[36,1024]{1,0:T(8,128)(2,1)S(1)}, bf16[36,1024]{1,0:T(8,128)(2,1)S(1)}, bf16[36,1024]{1,0:T(8,128)(2,1)S(1)...) custom-call(s32[1]{0:T(128)} %bitcast.plane_ref, ...), custom_call_target="tpu_custom_call" | custom-call | tf_op jit(solution)/shard_map/pack/pallas_call | solution.py:79
  2.1 3.1 %collective-permute-start = (bf16[36,1024]{1,0:T(8,128)(2,1)S(1)}, bf16[36,1024]{1,0:T(8,128)(2,1)S(1)}, u32[]{:S(2)}, u32[]{:S(2)}) collective-permute-start(bf16[36,1024]{1,0:T(8,128)(2,1)S(1)} %get-tuple-element.46), channel_id=1, source_target_pairs={{0,2},{2,0},{4,6},{6,4},{1,3},{3,1},{5,7},{7,5},{8,10},{10,8},{12,... | collective-permute-start | bytes 221192 | tf_op jit(solution)/shard_map/ppermute | solution.py:415
  5.2 2.6 %collective-permute-start.1 = (bf16[36,1024]{1,0:T(8,128)(2,1)S(1)}, bf16[36,1024]{1,0:T(8,128)(2,1)S(1)}, u32[]{:S(2)}, u32[]{:S(2)}) collective-permute-start(bf16[36,1024]{1,0:T(8,128)(2,1)S(1)} %get-tuple-element.47), channel_id=1, source_target_pairs={{0,4},{2,6},{4,0},{6,2},{1,5},{3,7},{5,1},{7,3},{8,12},{10,14},{12... | collective-permute-start | bytes 221192 | tf_op jit(solution)/shard_map/ppermute | solution.py:415
  7.8 2.9 %flip.1 = (bf16[2048,1024]{1,0:T(8,128)(2,1)S(1)}, bf16[1024,2048]{1,0:T(8,128)(2,1)S(1)}) custom-call(bf16[2048,1024]{1,0:T(8,128)(2,1)} %source_ref), custom_call_target="tpu_custom_call" | custom-call | tf_op jit(solution)/shard_map/flip/pallas_call | solution.py:158
  10.7 1.0 %collective-permute-start.7 = (bf16[36,1024]{1,0:T(8,128)(2,1)S(1)}, bf16[36,1024]{1,0:T(8,128)(2,1)S(1)}, u32[]{:S(2)}, u32[]{:S(2)}) collective-permute-start(bf16[36,1024]{1,0:T(8,128)(2,1)S(1)} %get-tuple-element.63), channel_id=1, source_target_pairs={{0,2},{2,0},{4,6},{6,4},{1,3},{3,1},{5,7},{7,5},{8,10},{10,8},{12,... | collective-permute-start | bytes 221192 | tf_op jit(solution)/shard_map/ppermute | solution.py:415
  11.7 3.5 %collective-permute-start.8 = (bf16[36,1024]{1,0:T(8,128)(2,1)S(1)}, bf16[36,1024]{1,0:T(8,128)(2,1)S(1)}, u32[]{:S(2)}, u32[]{:S(2)}) collective-permute-start(bf16[36,1024]{1,0:T(8,128)(2,1)S(1)} %get-tuple-element.64), channel_id=1, source_target_pairs={{0,4},{2,6},{4,0},{6,2},{1,5},{3,7},{5,1},{7,3},{8,12},{10,14},{12... | collective-permute-start | bytes 221192 | tf_op jit(solution)/shard_map/ppermute | solution.py:415
  15.3 1.8 %collective-permute-start.3 = (bf16[144,1024]{1,0:T(8,128)(2,1)S(1)}, bf16[144,1024]{1,0:T(8,128)(2,1)S(1)}, u32[]{:S(2)}, u32[]{:S(2)}) collective-permute-start(bf16[144,1024]{1,0:T(8,128)(2,1)S(1)} %join.2.refs_0_.refs_4_), channel_id=1, source_target_pairs={{0,1},{1,0},{2,3},{3,2},{4,5},{5,4},{6,7},{7,6},{8,9},{9,8},{10,11... | collective-permute-start | bytes 884744 | tf_op jit(solution)/shard_map/ppermute | solution.py:410
  17.0 1.5 %collective-permute-start.12 = (bf16[144,1024]{1,0:T(8,128)(2,1)S(1)}, bf16[144,1024]{1,0:T(8,128)(2,1)S(1)}, u32[]{:S(2)}, u32[]{:S(2)}) collective-permute-start(bf16[144,1024]{1,0:T(8,128)(2,1)S(1)} %join.2.refs_0_.refs_4_), channel_id=1, source_target_pairs={{0,16},{16,0},{1,17},{17,1},{2,18},{18,2},{3,19},{19,3},{4,20},{20... | collective-permute-start | bytes 884744 | tf_op jit(solution)/shard_map/ppermute | solution.py:410
  18.5 2.2 %forward_down.2 = (bf16[144,2048]{1,0:T(8,128)(2,1)S(1)}, bf16[144,2048]{1,0:T(8,128)(2,1)S(1)}, bf16[144,1024]{1,0:T(8,128)(2,1)S(1)}) custom-call(bf16[144,1024]{1,0:T(8,128)(2,1)S(1)} %join.2.refs_0_.refs_4_, bf16[1024,2048]{1,0:T(8,128)(2,1)S(1)} %copy-done, bf16[1024,2048]{1,0:T(8,128)(2,1)S(1)} %copy-done.1, ...), custom_call_target="tpu_custom_call" | custom-call | tf_op jit(solution)/shard_map/forward_down/pallas_call | solution.py:238
  20.8 0.7 %collective-permute-done.9.refs_4_ = bf16[36,1024]{1,0:T(8,128)(2,1)S(1)} collective-permute-done((bf16[36,1024]{1,0:T(8,128)(2,1)S(1)}, bf16[36,1024]{1,0:T(8,128)(2,1)S(1)}, u32[]{:S(2)}, u32[]{:S(2)}) %collective-permute-start.9) | collective-permute-done | bytes 73760 | tf_op jit(solution)/shard_map/ppermute | solution.py:415
  21.6 1.5 %collective-permute-start.11 = (bf16[144,1024]{1,0:T(8,128)(2,1)S(1)}, bf16[144,1024]{1,0:T(8,128)(2,1)S(1)}, u32[]{:S(2)}, u32[]{:S(2)}) collective-permute-start(bf16[144,1024]{1,0:T(8,128)(2,1)S(1)} %join.3.refs_0_), channel_id=1, source_target_pairs={{0,16},{16,0},{1,17},{17,1},{2,18},{18,2},{3,19},{19,3},{4,20},{20... | collective-permute-start | bytes 884744 | tf_op jit(solution)/shard_map/ppermute | solution.py:410
  23.1 1.5 %collective-permute-start.10 = (bf16[144,1024]{1,0:T(8,128)(2,1)S(1)}, bf16[144,1024]{1,0:T(8,128)(2,1)S(1)}, u32[]{:S(2)}, u32[]{:S(2)}) collective-permute-start(bf16[144,1024]{1,0:T(8,128)(2,1)S(1)} %join.3.refs_0_), channel_id=1, source_target_pairs={{0,1},{1,0},{2,3},{3,2},{4,5},{5,4},{6,7},{7,6},{8,9},{9,8},{10,11... | collective-permute-start | bytes 884744 | tf_op jit(solution)/shard_map/ppermute | solution.py:410
  24.6 2.2 %forward_down.3 = (bf16[144,2048]{1,0:T(8,128)(2,1)S(1)}, bf16[144,2048]{1,0:T(8,128)(2,1)S(1)}, bf16[72,1024]{1,0:T(8,128)(2,1)S(1)}, bf16[72,1024]{1,0:T(8,128...) custom-call(bf16[144,1024]{1,0:T(8,128)(2,1)S(1)} %collective-permute-done.3.refs_0_.refs_1_.refs_5_, ...), custom_call_target="tpu_custom_call" | custom-call | tf_op jit(solution)/shard_map/forward_down/pallas_call | solution.py:238
  26.9 1.4 %collective-permute-start.4 = (bf16[72,1024]{1,0:T(8,128)(2,1)S(1)}, bf16[72,1024]{1,0:T(8,128)(2,1)S(1)}, u32[]{:S(2)}, u32[]{:S(2)}) collective-permute-start(bf16[72,1024]{1,0:T(8,128)(2,1)S(1)} %get-tuple-element.53), channel_id=1, source_target_pairs={{0,2},{2,0},{4,6},{6,4},{1,3},{3,1},{5,7},{7,5},{8,10},{10,8},{12,... | collective-permute-start | bytes 442376 | tf_op jit(solution)/shard_map/ppermute | solution.py:415
  28.3 1.4 %collective-permute-start.5 = (bf16[72,1024]{1,0:T(8,128)(2,1)S(1)}, bf16[72,1024]{1,0:T(8,128)(2,1)S(1)}, u32[]{:S(2)}, u32[]{:S(2)}) collective-permute-start(bf16[72,1024]{1,0:T(8,128)(2,1)S(1)} %get-tuple-element.54), channel_id=1, source_target_pairs={{0,4},{2,6},{4,0},{6,2},{1,5},{3,7},{5,1},{7,3},{8,12},{10,14},{12... | collective-permute-start | bytes 442376 | tf_op jit(solution)/shard_map/ppermute | solution.py:415
  29.7 1.6 %collective-permute-start.6 = (bf16[72,1024]{1,0:T(8,128)(2,1)S(1)}, bf16[72,1024]{1,0:T(8,128)(2,1)S(1)}, u32[]{:S(2)}, u32[]{:S(2)}) collective-permute-start(bf16[72,1024]{1,0:T(8,128)(2,1)S(1)} %get-tuple-element.55), channel_id=1, source_target_pairs={{0,6},{2,4},{4,2},{6,0},{1,7},{3,5},{5,3},{7,1},{8,14},{10,12},{12... | collective-permute-start | bytes 442376 | tf_op jit(solution)/shard_map/ppermute | solution.py:415
  31.4 0.6 %collective-permute-start.13 = (bf16[144,1024]{1,0:T(8,128)(2,1)S(1)}, bf16[144,1024]{1,0:T(8,128)(2,1)S(1)}, u32[]{:S(2)}, u32[]{:S(2)}) collective-permute-start(bf16[144,1024]{1,0:T(8,128)(2,1)S(1)} %relay.4.refs_1_), channel_id=1, source_target_pairs={{0,16},{16,0},{1,17},{17,1},{2,18},{18,2},{3,19},{19,3},{4,20},{20... | collective-permute-start | bytes 884744 | tf_op jit(solution)/shard_map/ppermute | solution.py:410
  32.0 1.1 %collective-permute-start.15 = (bf16[144,1024]{1,0:T(8,128)(2,1)S(1)}, bf16[144,1024]{1,0:T(8,128)(2,1)S(1)}, u32[]{:S(2)}, u32[]{:S(2)}) collective-permute-start(bf16[144,1024]{1,0:T(8,128)(2,1)S(1)} %relay.5.refs_0_), channel_id=1, source_target_pairs={{0,1},{1,0},{2,3},{3,2},{4,5},{5,4},{6,7},{7,6},{8,9},{9,8},{10,11... | collective-permute-start | bytes 884744 | tf_op jit(solution)/shard_map/ppermute | solution.py:410
  33.1 1.6 %forward.2 = (bf16[144,2048]{1,0:T(8,128)(2,1)S(1)}, bf16[144,2048]{1,0:T(8,128)(2,1)S(1)}) custom-call(bf16[144,1024]{1,0:T(8,128)(2,1)S(1)} %relay.5.refs_0_, bf16[144,1024]{1,0:T(8,128)(2,1)S(1)} %collective-permute-done.12._.refs_1_.refs_2_.refs_6_, bf16[1024,2048]{1,0:T(8,128)(2,1)S(1)} %copy-done, bf16[1024,2048]{1,0:T(8,128)(2,1)S(1)} %copy-done.1), custom_call_target="tpu_custom_call" | custom-call | flops 20000000000 | tf_op jit(solution)/shard_map/forward/pallas_call | solution.py:238
  34.7 2.2 %slopes.1 = (bf16[432,2048]{1,0:T(8,128)(2,1)S(1)}, bf16[432,2048]{1,0:T(8,128)(2,1)S(1)}) custom-call(bf16[144,1024]{1,0:T(8,128)(2,1)S(1)} %join.3.refs_0_, bf16[144,1024]{1,0:T(8,128)(2,1)S(1)} %collective-permute-done.10.refs_2_.refs_1_, bf16[144,1024]{1,0:T(8,128)(2,1)S(1)} %collective-permute-done.11.refs_2_.refs_0_, ...), custom_call_target="tpu_custom_call" | custom-call | tf_op jit(solution)/shard_map/slopes/pallas_call | solution.py:297
  36.9 1.3 %collective-permute-done.13.refs_1_.refs_3_.refs_7_ = bf16[144,1024]{1,0:T(8,128)(2,1)S(1)} collective-permute-done((bf16[144,1024]{1,0:T(8,128)(2,1)S(1)}, bf16[144,1024]{1,0:T(8,128)(2,1)S(1)}, u32[]{:S(2)}, u32[]{:S(2)}) %collective-permute-start.13) | collective-permute-done | bytes 294944 | tf_op jit(solution)/shard_map/ppermute | solution.py:410
  38.2 1.6 %forward.3 = (bf16[144,2048]{1,0:T(8,128)(2,1)S(1)}, bf16[144,2048]{1,0:T(8,128)(2,1)S(1)}) custom-call(bf16[432,2048]{1,0:T(8,128)(2,1)S(1)} %get-tuple-element.71.refs_0_.dg_ref, bf16[144,1024]{1,0:T(8,128)(2,1)S(1)} %collective-permute-done.13.refs_1_.refs_3_.refs_7_, bf16[1024,2048]{1,0:T(8,128)(2,1)S(1)} %copy-done, bf16[1024,2048]{1,0:T(8,128)(2,1)S(1)} %copy-done.1), custom_call_target="tpu_custom_call" | custom-call | tf_op jit(solution)/shard_map/forward/pallas_call | solution.py:238
  39.8 1.7 %collective-permute-done.5.refs_2_ = bf16[72,1024]{1,0:T(8,128)(2,1)S(1)} collective-permute-done((bf16[72,1024]{1,0:T(8,128)(2,1)S(1)}, bf16[72,1024]{1,0:T(8,128)(2,1)S(1)}, u32[]{:S(2)}, u32[]{:S(2)}) %collective-permute-start.5) | collective-permute-done | bytes 147488 | tf_op jit(solution)/shard_map/ppermute | solution.py:415
  41.6 0.6 %collective-permute-start.14 = (bf16[144,1024]{1,0:T(8,128)(2,1)S(1)}, bf16[144,1024]{1,0:T(8,128)(2,1)S(1)}, u32[]{:S(2)}, u32[]{:S(2)}) collective-permute-start(bf16[144,1024]{1,0:T(8,128)(2,1)S(1)} %get-tuple-element.74), channel_id=1, source_target_pairs={{0,1},{1,0},{2,3},{3,2},{4,5},{5,4},{6,7},{7,6},{8,9},{9,8},{10,11... | collective-permute-start | bytes 884744 | tf_op jit(solution)/shard_map/ppermute | solution.py:410
  42.1 0.2 turn.1.xt_ref
  42.4 2.3 %backward.2 = (bf16[512,1024]{1,0:T(8,128)(2,1)S(1)}, bf16[512,1024]{1,0:T(8,128)(2,1)S(1)}) custom-call(bf16[512,576]{1,0:T(8,128)(2,1)S(1)} %turn.1.xt_ref, bf16[144,1024]{1,0:T(8,128)(2,1)S(1)} %collective-permute-done.15.g_ref, bf16[144,2048]{1,0:T(8,128)(2,1)S(1)} %get-tuple-element.72.refs_4_.act_ref, ...), custom_call_target="tpu_custom_call" | custom-call | flops 20000000000 | tf_op jit(solution)/shard_map/backward/pallas_call | solution.py:324
  44.8 2.1 %backward.3 = (bf16[512,1024]{1,0:T(8,128)(2,1)S(1)}, bf16[512,1024]{1,0:T(8,128)(2,1)S(1)}) custom-call(bf16[512,576]{1,0:T(8,128)(2,1)S(1)} %turn.1.xt_ref, bf16[144,1024]{1,0:T(8,128)(2,1)S(1)} %collective-permute-done.15.g_ref, bf16[144,2048]{1,0:T(8,128)(2,1)S(1)} %get-tuple-element.72.refs_4_.act_ref, ...), custom_call_target="tpu_custom_call" | custom-call | flops 20000000000 | tf_op jit(solution)/shard_map/backward/pallas_call | solution.py:324
  46.9 0.6 %collective-permute-start.17 = (bf16[512,1024]{1,0:T(8,128)(2,1)S(1)}, bf16[512,1024]{1,0:T(8,128)(2,1)S(1)}, u32[]{:S(2)}, u32[]{:S(2)}) collective-permute-start(bf16[512,1024]{1,0:T(8,128)(2,1)S(1)} %get-tuple-element.81), channel_id=1, source_target_pairs={{0,8},{8,0},{1,9},{9,1},{2,10},{10,2},{3,11},{11,3},{4,12},{12,4},... | collective-permute-start | bytes 3145736 | tf_op jit(solution)/shard_map/ppermute | solution.py:410
  47.5 1.1 %finish.2 = (bf16[256,2048]{1,0:T(8,128)(2,1)}, bf16[256,2048]{1,0:T(8,128)(2,1)}) custom-call(bf16[512,1024]{1,0:T(8,128)(2,1)S(1)} %get-tuple-element.77.refs_0_, bf16[512,1024]{1,0:T(8,128)(2,1)S(1)} %collective-permute-done.16.refs_1_), custom_call_target="tpu_custom_call" | custom-call | tf_op jit(solution)/shard_map/finish/pallas_call | solution.py:360
  48.6 1.0 %unpack.1 = bf16[128,1024]{1,0:T(8,128)(2,1)} custom-call(bf16[144,128]{1,0:T(8,128)(2,1)S(1)} %get-tuple-element.44.placer_ref, bf16[144,1024]{1,0:T(8,128)(2,1)S(1)} %get-tuple-element.73.mine_ref, bf16[144,1024]{1,0:T(8,128)(2,1)S(1)} %collective-permute-done.14.got_ref, bf16[256,2048]{1,0:T(8,128)(2,1)} %get-tuple-element.79.refs_0_.refs_2_), custom_call_target="tpu_custom_call" | custom-call | flops 20000000000 | tf_op jit(solution)/shard_map/unpack/pallas_call | solution.py:399
  49.7 0.1 collective-permute-done.17.refs_1_
  49.8 1.1 %finish.3 = (bf16[256,2048]{1,0:T(8,128)(2,1)}, bf16[256,2048]{1,0:T(8,128)(2,1)}) custom-call(bf16[512,1024]{1,0:T(8,128)(2,1)S(1)} %get-tuple-element.80.refs_0_, bf16[512,1024]{1,0:T(8,128)(2,1)S(1)} %collective-permute-done.17.refs_1_, bf16[256,2048]{1,0:T(8,128)(2,1)} %get-tuple-element.79.refs_0_.refs_2_, ...), custom_call_target="tpu_custom_call", output_to_operand_aliasing={{0}: (2, {}), {1}: (3, {})} | custom-call | tf_op jit(solution)/shard_map/finish/pallas_call | solution.py:360
  (28 shorter events, 0.4 us)
Async XLA Ops:
  2.1 13.1 %collective-permute-start = (bf16[36,1024]{1,0:T(8,128)(2,1)S(1)}, bf16[36,1024]{1,0:T(8,128)(2,1)S(1)}, u32[]{:S(2)}, u32[]{:S(2)}) collective-permute-start(bf16[36,1024]{1,0:T(8,128)(2,1)S(1)} %get-tuple-element.46), channel_id=1, source_target_pairs={{0,2},{2,0},{4,6},{6,4},{1,3},{3,1},{5,7},{7,5},{8,10},{10,8},{12,... | collective-permute-start | bytes 221192 | tf_op jit(solution)/shard_map/ppermute | solution.py:415
  5.2 10.0 %collective-permute-start.1 = (bf16[36,1024]{1,0:T(8,128)(2,1)S(1)}, bf16[36,1024]{1,0:T(8,128)(2,1)S(1)}, u32[]{:S(2)}, u32[]{:S(2)}) collective-permute-start(bf16[36,1024]{1,0:T(8,128)(2,1)S(1)} %get-tuple-element.47), channel_id=1, source_target_pairs={{0,4},{2,6},{4,0},{6,2},{1,5},{3,7},{5,1},{7,3},{8,12},{10,14},{12... | collective-permute-start | bytes 221192 | tf_op jit(solution)/shard_map/ppermute | solution.py:415
  7.8 7.4 %collective-permute-start.2 = (bf16[36,1024]{1,0:T(8,128)(2,1)S(1)}, bf16[36,1024]{1,0:T(8,128)(2,1)S(1)}, u32[]{:S(2)}, u32[]{:S(2)}) collective-permute-start(bf16[36,1024]{1,0:T(8,128)(2,1)S(1)} %get-tuple-element.48), channel_id=1, source_target_pairs={{0,6},{2,4},{4,2},{6,0},{1,7},{3,5},{5,3},{7,1},{8,14},{10,12},{12... | collective-permute-start | bytes 221192 | tf_op jit(solution)/shard_map/ppermute | solution.py:415
  7.8 10.7 %copy-start = (bf16[1024,2048]{1,0:T(8,128)(2,1)S(1)}, bf16[1024,2048]{1,0:T(8,128)(2,1)}, u32[]{:S(2)}) copy-start(bf16[1024,2048]{1,0:T(8,128)(2,1)} %refs_2_.7) | copy-start | bytes 12582916
  7.8 10.7 %copy-start.1 = (bf16[1024,2048]{1,0:T(8,128)(2,1)S(1)}, bf16[1024,2048]{1,0:T(8,128)(2,1)}, u32[]{:S(2)}) copy-start(bf16[1024,2048]{1,0:T(8,128)(2,1)} %refs_3_.3) | copy-start | bytes 12582916
  10.7 10.1 %collective-permute-start.7 = (bf16[36,1024]{1,0:T(8,128)(2,1)S(1)}, bf16[36,1024]{1,0:T(8,128)(2,1)S(1)}, u32[]{:S(2)}, u32[]{:S(2)}) collective-permute-start(bf16[36,1024]{1,0:T(8,128)(2,1)S(1)} %get-tuple-element.63), channel_id=1, source_target_pairs={{0,2},{2,0},{4,6},{6,4},{1,3},{3,1},{5,7},{7,5},{8,10},{10,8},{12,... | collective-permute-start | bytes 221192 | tf_op jit(solution)/shard_map/ppermute | solution.py:415
  11.7 9.1 %collective-permute-start.8 = (bf16[36,1024]{1,0:T(8,128)(2,1)S(1)}, bf16[36,1024]{1,0:T(8,128)(2,1)S(1)}, u32[]{:S(2)}, u32[]{:S(2)}) collective-permute-start(bf16[36,1024]{1,0:T(8,128)(2,1)S(1)} %get-tuple-element.64), channel_id=1, source_target_pairs={{0,4},{2,6},{4,0},{6,2},{1,5},{3,7},{5,1},{7,3},{8,12},{10,14},{12... | collective-permute-start | bytes 221192 | tf_op jit(solution)/shard_map/ppermute | solution.py:415
  15.2 6.3 %collective-permute-start.9 = (bf16[36,1024]{1,0:T(8,128)(2,1)S(1)}, bf16[36,1024]{1,0:T(8,128)(2,1)S(1)}, u32[]{:S(2)}, u32[]{:S(2)}) collective-permute-start(bf16[36,1024]{1,0:T(8,128)(2,1)S(1)} %get-tuple-element.65), channel_id=1, source_target_pairs={{0,6},{2,4},{4,2},{6,0},{1,7},{3,5},{5,3},{7,1},{8,14},{10,12},{12... | collective-permute-start | bytes 221192 | tf_op jit(solution)/shard_map/ppermute | solution.py:415
  15.3 9.4 %collective-permute-start.3 = (bf16[144,1024]{1,0:T(8,128)(2,1)S(1)}, bf16[144,1024]{1,0:T(8,128)(2,1)S(1)}, u32[]{:S(2)}, u32[]{:S(2)}) collective-permute-start(bf16[144,1024]{1,0:T(8,128)(2,1)S(1)} %join.2.refs_0_.refs_4_), channel_id=1, source_target_pairs={{0,1},{1,0},{2,3},{3,2},{4,5},{5,4},{6,7},{7,6},{8,9},{9,8},{10,11... | collective-permute-start | bytes 884744 | tf_op jit(solution)/shard_map/ppermute | solution.py:410
  17.0 12.7 %collective-permute-start.12 = (bf16[144,1024]{1,0:T(8,128)(2,1)S(1)}, bf16[144,1024]{1,0:T(8,128)(2,1)S(1)}, u32[]{:S(2)}, u32[]{:S(2)}) collective-permute-start(bf16[144,1024]{1,0:T(8,128)(2,1)S(1)} %join.2.refs_0_.refs_4_), channel_id=1, source_target_pairs={{0,16},{16,0},{1,17},{17,1},{2,18},{18,2},{3,19},{19,3},{4,20},{20... | collective-permute-start | bytes 884744 | tf_op jit(solution)/shard_map/ppermute | solution.py:410
  21.6 9.8 %collective-permute-start.11 = (bf16[144,1024]{1,0:T(8,128)(2,1)S(1)}, bf16[144,1024]{1,0:T(8,128)(2,1)S(1)}, u32[]{:S(2)}, u32[]{:S(2)}) collective-permute-start(bf16[144,1024]{1,0:T(8,128)(2,1)S(1)} %join.3.refs_0_), channel_id=1, source_target_pairs={{0,16},{16,0},{1,17},{17,1},{2,18},{18,2},{3,19},{19,3},{4,20},{20... | collective-permute-start | bytes 884744 | tf_op jit(solution)/shard_map/ppermute | solution.py:410
  23.1 8.9 %collective-permute-start.10 = (bf16[144,1024]{1,0:T(8,128)(2,1)S(1)}, bf16[144,1024]{1,0:T(8,128)(2,1)S(1)}, u32[]{:S(2)}, u32[]{:S(2)}) collective-permute-start(bf16[144,1024]{1,0:T(8,128)(2,1)S(1)} %join.3.refs_0_), channel_id=1, source_target_pairs={{0,1},{1,0},{2,3},{3,2},{4,5},{5,4},{6,7},{7,6},{8,9},{9,8},{10,11... | collective-permute-start | bytes 884744 | tf_op jit(solution)/shard_map/ppermute | solution.py:410
  26.9 12.9 %collective-permute-start.4 = (bf16[72,1024]{1,0:T(8,128)(2,1)S(1)}, bf16[72,1024]{1,0:T(8,128)(2,1)S(1)}, u32[]{:S(2)}, u32[]{:S(2)}) collective-permute-start(bf16[72,1024]{1,0:T(8,128)(2,1)S(1)} %get-tuple-element.53), channel_id=1, source_target_pairs={{0,2},{2,0},{4,6},{6,4},{1,3},{3,1},{5,7},{7,5},{8,10},{10,8},{12,... | collective-permute-start | bytes 442376 | tf_op jit(solution)/shard_map/ppermute | solution.py:415
  28.3 13.2 %collective-permute-start.5 = (bf16[72,1024]{1,0:T(8,128)(2,1)S(1)}, bf16[72,1024]{1,0:T(8,128)(2,1)S(1)}, u32[]{:S(2)}, u32[]{:S(2)}) collective-permute-start(bf16[72,1024]{1,0:T(8,128)(2,1)S(1)} %get-tuple-element.54), channel_id=1, source_target_pairs={{0,4},{2,6},{4,0},{6,2},{1,5},{3,7},{5,1},{7,3},{8,12},{10,14},{12... | collective-permute-start | bytes 442376 | tf_op jit(solution)/shard_map/ppermute | solution.py:415
  29.7 11.8 %collective-permute-start.6 = (bf16[72,1024]{1,0:T(8,128)(2,1)S(1)}, bf16[72,1024]{1,0:T(8,128)(2,1)S(1)}, u32[]{:S(2)}, u32[]{:S(2)}) collective-permute-start(bf16[72,1024]{1,0:T(8,128)(2,1)S(1)} %get-tuple-element.55), channel_id=1, source_target_pairs={{0,6},{2,4},{4,2},{6,0},{1,7},{3,5},{5,3},{7,1},{8,14},{10,12},{12... | collective-permute-start | bytes 442376 | tf_op jit(solution)/shard_map/ppermute | solution.py:415
  31.4 6.8 %collective-permute-start.13 = (bf16[144,1024]{1,0:T(8,128)(2,1)S(1)}, bf16[144,1024]{1,0:T(8,128)(2,1)S(1)}, u32[]{:S(2)}, u32[]{:S(2)}) collective-permute-start(bf16[144,1024]{1,0:T(8,128)(2,1)S(1)} %relay.4.refs_1_), channel_id=1, source_target_pairs={{0,16},{16,0},{1,17},{17,1},{2,18},{18,2},{3,19},{19,3},{4,20},{20... | collective-permute-start | bytes 884744 | tf_op jit(solution)/shard_map/ppermute | solution.py:410
  32.0 10.4 %collective-permute-start.15 = (bf16[144,1024]{1,0:T(8,128)(2,1)S(1)}, bf16[144,1024]{1,0:T(8,128)(2,1)S(1)}, u32[]{:S(2)}, u32[]{:S(2)}) collective-permute-start(bf16[144,1024]{1,0:T(8,128)(2,1)S(1)} %relay.5.refs_0_), channel_id=1, source_target_pairs={{0,1},{1,0},{2,3},{3,2},{4,5},{5,4},{6,7},{7,6},{8,9},{9,8},{10,11... | collective-permute-start | bytes 884744 | tf_op jit(solution)/shard_map/ppermute | solution.py:410
  41.6 7.0 %collective-permute-start.14 = (bf16[144,1024]{1,0:T(8,128)(2,1)S(1)}, bf16[144,1024]{1,0:T(8,128)(2,1)S(1)}, u32[]{:S(2)}, u32[]{:S(2)}) collective-permute-start(bf16[144,1024]{1,0:T(8,128)(2,1)S(1)} %get-tuple-element.74), channel_id=1, source_target_pairs={{0,1},{1,0},{2,3},{3,2},{4,5},{5,4},{6,7},{7,6},{8,9},{9,8},{10,11... | collective-permute-start | bytes 884744 | tf_op jit(solution)/shard_map/ppermute | solution.py:410
  44.7 2.8 %collective-permute-start.16 = (bf16[512,1024]{1,0:T(8,128)(2,1)S(1)}, bf16[512,1024]{1,0:T(8,128)(2,1)S(1)}, u32[]{:S(2)}, u32[]{:S(2)}) collective-permute-start(bf16[512,1024]{1,0:T(8,128)(2,1)S(1)} %get-tuple-element.78), channel_id=1, source_target_pairs={{0,8},{8,0},{1,9},{9,1},{2,10},{10,2},{3,11},{11,3},{4,12},{12,4},... | collective-permute-start | bytes 3145736 | tf_op jit(solution)/shard_map/ppermute | solution.py:410
  46.9 2.8 %collective-permute-start.17 = (bf16[512,1024]{1,0:T(8,128)(2,1)S(1)}, bf16[512,1024]{1,0:T(8,128)(2,1)S(1)}, u32[]{:S(2)}, u32[]{:S(2)}) collective-permute-start(bf16[512,1024]{1,0:T(8,128)(2,1)S(1)} %get-tuple-element.81), channel_id=1, source_target_pairs={{0,8},{8,0},{1,9},{9,1},{2,10},{10,2},{3,11},{11,3},{4,12},{12,4},... | collective-permute-start | bytes 3145736 | tf_op jit(solution)/shard_map/ppermute | solution.py:410

commit v19 on v16

--- a/solution.py
+++ b/solution.py
@@ -88,7 +88,7 @@
             pltpu.SemaphoreType.DMA((3,)),
         ],
         compiler_params=SMALL,
-        cost_estimate=CHEAP,
+        cost_estimate=DEAR,
         name="pack",
     )(*scalars, kept(kind), kept(x), kept(g))
 
@@ -141,30 +141,23 @@
     )(value, earlier)
 
 
-def flip_kernel(source_ref, here_ref, flipped_ref, sems):
-    steps = source_ref.shape[0] // SLICE
-    copies = []
-    for j in range(steps):
-        rows = pl.ds(j * SLICE, SLICE)
-        copies.append(pltpu.make_async_copy(source_ref.at[rows], here_ref.at[rows], sems.at[j]))
-        copies[j].start()
-    for j in range(steps):
-        copies[j].wait()
+def flip_kernel(source_ref, *refs):
+    flipped_ref = refs[-1]
+    for j in range(source_ref.shape[0] // SLICE):
         rows = slice(j * SLICE, (j + 1) * SLICE)
-        flipped_ref[:, rows] = here_ref[rows, :].T
-
-
-def flip(value):
+        flipped_ref[:, rows] = source_ref[rows, :].T
+
+
+def flip(value, earlier):
     return pl.pallas_call(
         flip_kernel,
-        out_shape=[pltpu.VMEM(value.shape, value.dtype), pltpu.VMEM(value.shape[::-1], value.dtype)],
-        in_specs=[AFAR],
-        out_specs=[HERE, HERE],
-        scratch_shapes=[pltpu.SemaphoreType.DMA((value.shape[0] // SLICE,))],
+        out_shape=pltpu.VMEM(value.shape[::-1], value.dtype),
+        in_specs=[HERE] + [ANYWHERE] * len(earlier),
+        out_specs=HERE,
         compiler_params=SMALL,
         cost_estimate=CHEAP,
         name="flip",
-    )(kept(value))
+    )(value, *earlier)
 
 
 def forward_kernel(n, fetch, down, pair, unused, *refs):
@@ -428,7 +421,7 @@
     tokens, width = designs.shape
     share = width // 4
     placer, *blocks = pack(scalars, archetype.reshape(1, tokens), designs, cotangent)
-    wd, wdt = flip(after([w_down], [placer])[0])
+    wd, wdt = w_down, flip(w_down, [placer])
 
     x_own = join(across_planes(blocks[:EXPERTS]))
     moved = across_planes(relay(blocks[EXPERTS:], [wdt]))

time: 49.7 us -> 53.1 us (1.068); the launches traced: 49.6 us -> 52 us
  waiting for transfers between devices: 1.37 us -> 5.88 us
  Pallas kernels: 22.3 us -> 20.8 us
    ppermute x9, waiting for transfers between devices: 0.33 us -> 4.2 us  [across_planes(): lax.ppermute(blocks[k], 'arch', [(i, i ^ k) for i in range(EXPERTS)])]
    pallas_call x1, Pallas kernels: 2.88 us -> 1.23 us  [flip(): pl.pallas_call(flip_kernel, out_shape=pltpu.VMEM(value.shape[::-1], value...]
    ppermute x9, starting transfers between devices: 10.2 us -> 9.01 us  [swap(): return lax.ppermute(value, axis, [(0, 1), (1, 0)])]
    ppermute x9, waiting for transfers between devices: 1.03 us -> 1.68 us  [swap(): return lax.ppermute(value, axis, [(0, 1), (1, 0)])]
    ppermute x9, starting transfers between devices: 14.7 us -> 15.3 us  [across_planes(): lax.ppermute(blocks[k], 'arch', [(i, i ^ k) for i in range(EXPERTS)])]
  transfers between devices with their start and end apart: 18 -> 18, of which waited for: 3 -> 4; matrix products, arithmetic and copies ran while one was open for 0% -> 0% of each run, Pallas kernels for 40% -> 35%
where the time goes in v19:
time: 53.1 us; the launch traced here: 52 us
  starting transfers between devices  24.3 us (46%)
  Pallas kernels  20.8 us (39%)
  waiting for transfers between devices  5.88 us (11%)
  between operations  1.03 us (2%)
    ppermute x9, starting transfers between devices, across_planes(): lax.ppermute(blocks[k], 'arch', [(i, i ^ k) for i in range(EXPERTS)])  15.3 us
    ppermute x9, starting transfers between devices, swap(): return lax.ppermute(value, axis, [(0, 1), (1, 0)])  9.01 us
    pallas_call x4, Pallas kernels, forward(): pl.pallas_call(functools.partial(forward_kernel, n, fetch, down, pair, le...  7.61 us
    pallas_call x2, Pallas kernels, backward(): pl.pallas_call(functools.partial(backward_kernel, first), out_shape=[jax....  4.45 us
    ppermute x9, waiting for transfers between devices, across_planes(): lax.ppermute(blocks[k], 'arch', [(i, i ^ k) for i in range(EXPERTS)])  4.2 us
    pallas_call x2, Pallas kernels, finish(): pl.pallas_call(functools.partial(finish_kernel, spans, more, len(earlier)...  2.21 us
    pallas_call x1, Pallas kernels, slopes(): pl.pallas_call(functools.partial(slopes_kernel, n), out_shape=[jax.ShapeD...  2.19 us
    ppermute x9, waiting for transfers between devices, swap(): return lax.ppermute(value, axis, [(0, 1), (1, 0)])  1.68 us
  transfers between devices with their start and end apart: 18, of which 4 were waited for; matrix products, arithmetic and copies ran while one was open for 0% of the time, Pallas kernels for 35%

profile of v19, /device:TPU:0, one launch (start us, length us, event | category | flops | bytes accessed | tf_op | source)
XLA Modules:
  0.0 52.0 jit_solution(14963420375527004307)
XLA Ops:
  0.7 1.6 %pack.1 = (bf16[144,128]{1,0:T(8,128)(2,1)S(1)}, bf16[36,1024]{1,0:T(8,128)(2,1)S(1)}, bf16[36,1024]{1,0:T(8,128)(2,1)S(1)}, bf16[36,1024]{1,0:T(8,128)(2,1)S(1)...) custom-call(s32[1]{0:T(128)} %bitcast.plane_ref, ...), custom_call_target="tpu_custom_call" | custom-call | flops 20000000000 | tf_op jit(solution)/shard_map/pack/pallas_call | solution.py:79
  2.3 5.1 %collective-permute-start = (bf16[36,1024]{1,0:T(8,128)(2,1)S(1)}, bf16[36,1024]{1,0:T(8,128)(2,1)S(1)}, u32[]{:S(2)}, u32[]{:S(2)}) collective-permute-start(bf16[36,1024]{1,0:T(8,128)(2,1)S(1)} %get-tuple-element.42), channel_id=1, source_target_pairs={{0,6},{2,4},{4,2},{6,0},{1,7},{3,5},{5,3},{7,1},{8,14},{10,12},{12... | collective-permute-start | bytes 221192 | tf_op jit(solution)/shard_map/ppermute | solution.py:408
  7.4 0.6 %collective-permute-start.2 = (bf16[36,1024]{1,0:T(8,128)(2,1)S(1)}, bf16[36,1024]{1,0:T(8,128)(2,1)S(1)}, u32[]{:S(2)}, u32[]{:S(2)}) collective-permute-start(bf16[36,1024]{1,0:T(8,128)(2,1)S(1)} %get-tuple-element.44), channel_id=1, source_target_pairs={{0,2},{2,0},{4,6},{6,4},{1,3},{3,1},{5,7},{7,5},{8,10},{10,8},{12,... | collective-permute-start | bytes 221192 | tf_op jit(solution)/shard_map/ppermute | solution.py:408
  8.0 1.2 %flip.1.refs_4_.refs_9_.wdt_ref = bf16[1024,2048]{1,0:T(8,128)(2,1)S(1)} custom-call(bf16[2048,1024]{1,0:T(8,128)(2,1)S(1)} %copy-done.2, bf16[144,128]{1,0:T(8,128)(2,1)S(1)} %get-tuple-element.41.refs_0_.placer_ref), custom_call_target="tpu_custom_call" | custom-call | tf_op jit(solution)/shard_map/flip/pallas_call | solution.py:152
  9.3 3.8 %collective-permute-start.7 = (bf16[36,1024]{1,0:T(8,128)(2,1)S(1)}, bf16[36,1024]{1,0:T(8,128)(2,1)S(1)}, u32[]{:S(2)}, u32[]{:S(2)}) collective-permute-start(bf16[36,1024]{1,0:T(8,128)(2,1)S(1)} %get-tuple-element.56), channel_id=1, source_target_pairs={{0,6},{2,4},{4,2},{6,0},{1,7},{3,5},{5,3},{7,1},{8,14},{10,12},{12... | collective-permute-start | bytes 221192 | tf_op jit(solution)/shard_map/ppermute | solution.py:408
  13.1 1.3 %collective-permute-start.9 = (bf16[36,1024]{1,0:T(8,128)(2,1)S(1)}, bf16[36,1024]{1,0:T(8,128)(2,1)S(1)}, u32[]{:S(2)}, u32[]{:S(2)}) collective-permute-start(bf16[36,1024]{1,0:T(8,128)(2,1)S(1)} %get-tuple-element.58), channel_id=1, source_target_pairs={{0,2},{2,0},{4,6},{6,4},{1,3},{3,1},{5,7},{7,5},{8,10},{10,8},{12,... | collective-permute-start | bytes 221192 | tf_op jit(solution)/shard_map/ppermute | solution.py:408
  14.4 4.2 %collective-permute-done.1.refs_1_ = bf16[36,1024]{1,0:T(8,128)(2,1)S(1)} collective-permute-done((bf16[36,1024]{1,0:T(8,128)(2,1)S(1)}, bf16[36,1024]{1,0:T(8,128)(2,1)S(1)}, u32[]{:S(2)}, u32[]{:S(2)}) %collective-permute-start.1) | collective-permute-done | bytes 73760 | tf_op jit(solution)/shard_map/ppermute | solution.py:408
  18.6 1.4 %collective-permute-start.3 = (bf16[144,1024]{1,0:T(8,128)(2,1)S(1)}, bf16[144,1024]{1,0:T(8,128)(2,1)S(1)}, u32[]{:S(2)}, u32[]{:S(2)}) collective-permute-start(bf16[144,1024]{1,0:T(8,128)(2,1)S(1)} %join.2.refs_0_.refs_4_), channel_id=1, source_target_pairs={{0,1},{1,0},{2,3},{3,2},{4,5},{5,4},{6,7},{7,6},{8,9},{9,8},{10,11... | collective-permute-start | bytes 884744 | tf_op jit(solution)/shard_map/ppermute | solution.py:403
  20.1 1.5 %collective-permute-start.12 = (bf16[144,1024]{1,0:T(8,128)(2,1)S(1)}, bf16[144,1024]{1,0:T(8,128)(2,1)S(1)}, u32[]{:S(2)}, u32[]{:S(2)}) collective-permute-start(bf16[144,1024]{1,0:T(8,128)(2,1)S(1)} %join.2.refs_0_.refs_4_), channel_id=1, source_target_pairs={{0,16},{16,0},{1,17},{17,1},{2,18},{18,2},{3,19},{19,3},{4,20},{20... | collective-permute-start | bytes 884744 | tf_op jit(solution)/shard_map/ppermute | solution.py:403
  21.6 2.2 %forward_down.2 = (bf16[144,2048]{1,0:T(8,128)(2,1)S(1)}, bf16[144,2048]{1,0:T(8,128)(2,1)S(1)}, bf16[144,1024]{1,0:T(8,128)(2,1)S(1)}) custom-call(bf16[144,1024]{1,0:T(8,128)(2,1)S(1)} %join.2.refs_0_.refs_4_, bf16[1024,2048]{1,0:T(8,128)(2,1)S(1)} %copy-done, bf16[1024,2048]{1,0:T(8,128)(2,1)S(1)} %copy-done.1, bf16[2048,1024]{1,0:T(8,128)(2,1)S(1)} %copy-done.2), custom_call_target="tpu_custom_call" | custom-call | tf_op jit(solution)/shard_map/forward_down/pallas_call | solution.py:231
  23.9 0.6 %collective-permute-start.11 = (bf16[144,1024]{1,0:T(8,128)(2,1)S(1)}, bf16[144,1024]{1,0:T(8,128)(2,1)S(1)}, u32[]{:S(2)}, u32[]{:S(2)}) collective-permute-start(bf16[144,1024]{1,0:T(8,128)(2,1)S(1)} %join.3.refs_0_), channel_id=1, source_target_pairs={{0,16},{16,0},{1,17},{17,1},{2,18},{18,2},{3,19},{19,3},{4,20},{20... | collective-permute-start | bytes 884744 | tf_op jit(solution)/shard_map/ppermute | solution.py:403
  24.5 0.7 %collective-permute-start.10 = (bf16[144,1024]{1,0:T(8,128)(2,1)S(1)}, bf16[144,1024]{1,0:T(8,128)(2,1)S(1)}, u32[]{:S(2)}, u32[]{:S(2)}) collective-permute-start(bf16[144,1024]{1,0:T(8,128)(2,1)S(1)} %join.3.refs_0_), channel_id=1, source_target_pairs={{0,1},{1,0},{2,3},{3,2},{4,5},{5,4},{6,7},{7,6},{8,9},{9,8},{10,11... | collective-permute-start | bytes 884744 | tf_op jit(solution)/shard_map/ppermute | solution.py:403
  25.1 1.0 %collective-permute-done.3.refs_0_.refs_1_.refs_5_ = bf16[144,1024]{1,0:T(8,128)(2,1)S(1)} collective-permute-done((bf16[144,1024]{1,0:T(8,128)(2,1)S(1)}, bf16[144,1024]{1,0:T(8,128)(2,1)S(1)}, u32[]{:S(2)}, u32[]{:S(2)}) %collective-permute-start.3) | collective-permute-done | bytes 294944 | tf_op jit(solution)/shard_map/ppermute | solution.py:403
  26.1 2.2 %forward_down.3 = (bf16[144,2048]{1,0:T(8,128)(2,1)S(1)}, bf16[144,2048]{1,0:T(8,128)(2,1)S(1)}, bf16[72,1024]{1,0:T(8,128)(2,1)S(1)}, bf16[72,1024]{1,0:T(8,128...) custom-call(bf16[144,1024]{1,0:T(8,128)(2,1)S(1)} %collective-permute-done.3.refs_0_.refs_1_.refs_5_, ...), custom_call_target="tpu_custom_call" | custom-call | tf_op jit(solution)/shard_map/forward_down/pallas_call | solution.py:231
  28.4 4.0 %collective-permute-start.5 = (bf16[72,1024]{1,0:T(8,128)(2,1)S(1)}, bf16[72,1024]{1,0:T(8,128)(2,1)S(1)}, u32[]{:S(2)}, u32[]{:S(2)}) collective-permute-start(bf16[72,1024]{1,0:T(8,128)(2,1)S(1)} %get-tuple-element.49), channel_id=1, source_target_pairs={{0,4},{2,6},{4,0},{6,2},{1,5},{3,7},{5,1},{7,3},{8,12},{10,14},{12... | collective-permute-start | bytes 442376 | tf_op jit(solution)/shard_map/ppermute | solution.py:408
  32.4 0.4 collective-permute-start.6
  32.8 0.5 %collective-permute-done.11.refs_2_.refs_0_ = bf16[144,1024]{1,0:T(8,128)(2,1)S(1)} collective-permute-done((bf16[144,1024]{1,0:T(8,128)(2,1)S(1)}, bf16[144,1024]{1,0:T(8,128)(2,1)S(1)}, u32[]{:S(2)}, u32[]{:S(2)}) %collective-permute-start.11) | collective-permute-done | bytes 294944 | tf_op jit(solution)/shard_map/ppermute | solution.py:403
  33.4 1.8 %collective-permute-start.13 = (bf16[144,1024]{1,0:T(8,128)(2,1)S(1)}, bf16[144,1024]{1,0:T(8,128)(2,1)S(1)}, u32[]{:S(2)}, u32[]{:S(2)}) collective-permute-start(bf16[144,1024]{1,0:T(8,128)(2,1)S(1)} %relay.4.refs_1_), channel_id=1, source_target_pairs={{0,16},{16,0},{1,17},{17,1},{2,18},{18,2},{3,19},{19,3},{4,20},{20... | collective-permute-start | bytes 884744 | tf_op jit(solution)/shard_map/ppermute | solution.py:403
  35.2 1.5 %collective-permute-start.15 = (bf16[144,1024]{1,0:T(8,128)(2,1)S(1)}, bf16[144,1024]{1,0:T(8,128)(2,1)S(1)}, u32[]{:S(2)}, u32[]{:S(2)}) collective-permute-start(bf16[144,1024]{1,0:T(8,128)(2,1)S(1)} %relay.5.refs_0_), channel_id=1, source_target_pairs={{0,1},{1,0},{2,3},{3,2},{4,5},{5,4},{6,7},{7,6},{8,9},{9,8},{10,11... | collective-permute-start | bytes 884744 | tf_op jit(solution)/shard_map/ppermute | solution.py:403
  36.7 1.6 %forward.2 = (bf16[144,2048]{1,0:T(8,128)(2,1)S(1)}, bf16[144,2048]{1,0:T(8,128)(2,1)S(1)}) custom-call(bf16[144,1024]{1,0:T(8,128)(2,1)S(1)} %relay.5.refs_0_, bf16[144,1024]{1,0:T(8,128)(2,1)S(1)} %collective-permute-done.12._.refs_1_.refs_2_.refs_6_, bf16[1024,2048]{1,0:T(8,128)(2,1)S(1)} %copy-done, bf16[1024,2048]{1,0:T(8,128)(2,1)S(1)} %copy-done.1), custom_call_target="tpu_custom_call" | custom-call | flops 20000000000 | tf_op jit(solution)/shard_map/forward/pallas_call | solution.py:231
  38.3 2.2 %slopes.1 = (bf16[432,2048]{1,0:T(8,128)(2,1)S(1)}, bf16[432,2048]{1,0:T(8,128)(2,1)S(1)}) custom-call(bf16[144,1024]{1,0:T(8,128)(2,1)S(1)} %join.3.refs_0_, bf16[144,1024]{1,0:T(8,128)(2,1)S(1)} %collective-permute-done.10.refs_2_.refs_1_, bf16[144,1024]{1,0:T(8,128)(2,1)S(1)} %collective-permute-done.11.refs_2_.refs_0_, ...), custom_call_target="tpu_custom_call" | custom-call | tf_op jit(solution)/shard_map/slopes/pallas_call | solution.py:290
  40.5 1.6 %forward.3 = (bf16[144,2048]{1,0:T(8,128)(2,1)S(1)}, bf16[144,2048]{1,0:T(8,128)(2,1)S(1)}) custom-call(bf16[432,2048]{1,0:T(8,128)(2,1)S(1)} %get-tuple-element.65.refs_0_.dg_ref, bf16[144,1024]{1,0:T(8,128)(2,1)S(1)} %collective-permute-done.13.refs_1_.refs_3_.refs_7_, bf16[1024,2048]{1,0:T(8,128)(2,1)S(1)} %copy-done, bf16[1024,2048]{1,0:T(8,128)(2,1)S(1)} %copy-done.1), custom_call_target="tpu_custom_call" | custom-call | tf_op jit(solution)/shard_map/forward/pallas_call | solution.py:231
  42.1 0.1 split.1
  42.2 0.9 %collective-permute-start.14 = (bf16[144,1024]{1,0:T(8,128)(2,1)S(1)}, bf16[144,1024]{1,0:T(8,128)(2,1)S(1)}, u32[]{:S(2)}, u32[]{:S(2)}) collective-permute-start(bf16[144,1024]{1,0:T(8,128)(2,1)S(1)} %get-tuple-element.68), channel_id=1, source_target_pairs={{0,1},{1,0},{2,3},{3,2},{4,5},{5,4},{6,7},{7,6},{8,9},{9,8},{10,11... | collective-permute-start | bytes 884744 | tf_op jit(solution)/shard_map/ppermute | solution.py:403
  43.1 0.2 turn.1.xt_ref
  43.4 2.3 %backward.2 = (bf16[512,1024]{1,0:T(8,128)(2,1)S(1)}, bf16[512,1024]{1,0:T(8,128)(2,1)S(1)}) custom-call(bf16[512,576]{1,0:T(8,128)(2,1)S(1)} %turn.1.xt_ref, bf16[144,1024]{1,0:T(8,128)(2,1)S(1)} %collective-permute-done.15.g_ref, bf16[144,2048]{1,0:T(8,128)(2,1)S(1)} %get-tuple-element.66.refs_4_.act_ref, ...), custom_call_target="tpu_custom_call" | custom-call | flops 20000000000 | tf_op jit(solution)/shard_map/backward/pallas_call | solution.py:317
  45.8 2.1 %backward.3 = (bf16[512,1024]{1,0:T(8,128)(2,1)S(1)}, bf16[512,1024]{1,0:T(8,128)(2,1)S(1)}) custom-call(bf16[512,576]{1,0:T(8,128)(2,1)S(1)} %turn.1.xt_ref, bf16[144,1024]{1,0:T(8,128)(2,1)S(1)} %collective-permute-done.15.g_ref, bf16[144,2048]{1,0:T(8,128)(2,1)S(1)} %get-tuple-element.66.refs_4_.act_ref, ...), custom_call_target="tpu_custom_call" | custom-call | flops 20000000000 | tf_op jit(solution)/shard_map/backward/pallas_call | solution.py:317
  47.9 0.6 %collective-permute-start.17 = (bf16[512,1024]{1,0:T(8,128)(2,1)S(1)}, bf16[512,1024]{1,0:T(8,128)(2,1)S(1)}, u32[]{:S(2)}, u32[]{:S(2)}) collective-permute-start(bf16[512,1024]{1,0:T(8,128)(2,1)S(1)} %get-tuple-element.75), channel_id=1, source_target_pairs={{0,8},{8,0},{1,9},{9,1},{2,10},{10,2},{3,11},{11,3},{4,12},{12,4},... | collective-permute-start | bytes 3145736 | tf_op jit(solution)/shard_map/ppermute | solution.py:403
  48.5 1.1 %finish.2 = (bf16[256,2048]{1,0:T(8,128)(2,1)}, bf16[256,2048]{1,0:T(8,128)(2,1)}) custom-call(bf16[512,1024]{1,0:T(8,128)(2,1)S(1)} %get-tuple-element.71.refs_0_, bf16[512,1024]{1,0:T(8,128)(2,1)S(1)} %collective-permute-done.16.refs_1_), custom_call_target="tpu_custom_call" | custom-call | tf_op jit(solution)/shard_map/finish/pallas_call | solution.py:353
  49.6 1.0 %unpack.1 = bf16[128,1024]{1,0:T(8,128)(2,1)} custom-call(bf16[144,128]{1,0:T(8,128)(2,1)S(1)} %get-tuple-element.41.refs_0_.placer_ref, bf16[144,1024]{1,0:T(8,128)(2,1)S(1)} %get-tuple-element.67.mine_ref, bf16[144,1024]{1,0:T(8,128)(2,1)S(1)} %collective-permute-done.14.got_ref, bf16[256,2048]{1,0:T(8,128)(2,1)} %get-tuple-element.73.refs_0_.refs_2_), custom_call_target="tpu_custom_call" | custom-call | flops 20000000000 | tf_op jit(solution)/shard_map/unpack/pallas_call | solution.py:392
  50.6 0.1 collective-permute-done.17.refs_1_
  50.8 1.1 %finish.3 = (bf16[256,2048]{1,0:T(8,128)(2,1)}, bf16[256,2048]{1,0:T(8,128)(2,1)}) custom-call(bf16[512,1024]{1,0:T(8,128)(2,1)S(1)} %get-tuple-element.74.refs_0_, bf16[512,1024]{1,0:T(8,128)(2,1)S(1)} %collective-permute-done.17.refs_1_, bf16[256,2048]{1,0:T(8,128)(2,1)} %get-tuple-element.73.refs_0_.refs_2_, ...), custom_call_target="tpu_custom_call", output_to_operand_aliasing={{0}: (2, {}), {1}: (3, {})} | custom-call | tf_op jit(solution)/shard_map/finish/pallas_call | solution.py:353
  (30 shorter events, 0.4 us)
Async XLA Ops:
  0.6 7.4 %copy-start.2 = (bf16[2048,1024]{1,0:T(8,128)(2,1)S(1)}, bf16[2048,1024]{1,0:T(8,128)(2,1)}, u32[]{:S(2)}) copy-start(bf16[2048,1024]{1,0:T(8,128)(2,1)} %source_ref.1) | copy-start | bytes 12582916
  2.3 10.9 %collective-permute-start = (bf16[36,1024]{1,0:T(8,128)(2,1)S(1)}, bf16[36,1024]{1,0:T(8,128)(2,1)S(1)}, u32[]{:S(2)}, u32[]{:S(2)}) collective-permute-start(bf16[36,1024]{1,0:T(8,128)(2,1)S(1)} %get-tuple-element.42), channel_id=1, source_target_pairs={{0,6},{2,4},{4,2},{6,0},{1,7},{3,5},{5,3},{7,1},{8,14},{10,12},{12... | collective-permute-start | bytes 221192 | tf_op jit(solution)/shard_map/ppermute | solution.py:408
  7.4 11.2 %collective-permute-start.1 = (bf16[36,1024]{1,0:T(8,128)(2,1)S(1)}, bf16[36,1024]{1,0:T(8,128)(2,1)S(1)}, u32[]{:S(2)}, u32[]{:S(2)}) collective-permute-start(bf16[36,1024]{1,0:T(8,128)(2,1)S(1)} %get-tuple-element.43), channel_id=1, source_target_pairs={{0,4},{2,6},{4,0},{6,2},{1,5},{3,7},{5,1},{7,3},{8,12},{10,14},{12... | collective-permute-start | bytes 221192 | tf_op jit(solution)/shard_map/ppermute | solution.py:408
  7.4 11.2 %collective-permute-start.2 = (bf16[36,1024]{1,0:T(8,128)(2,1)S(1)}, bf16[36,1024]{1,0:T(8,128)(2,1)S(1)}, u32[]{:S(2)}, u32[]{:S(2)}) collective-permute-start(bf16[36,1024]{1,0:T(8,128)(2,1)S(1)} %get-tuple-element.44), channel_id=1, source_target_pairs={{0,2},{2,0},{4,6},{6,4},{1,3},{3,1},{5,7},{7,5},{8,10},{10,8},{12,... | collective-permute-start | bytes 221192 | tf_op jit(solution)/shard_map/ppermute | solution.py:408
  8.0 13.5 %copy-start.1 = (bf16[1024,2048]{1,0:T(8,128)(2,1)S(1)}, bf16[1024,2048]{1,0:T(8,128)(2,1)}, u32[]{:S(2)}) copy-start(bf16[1024,2048]{1,0:T(8,128)(2,1)} %refs_3_.7) | copy-start | bytes 12582916
  9.3 12.3 %copy-start = (bf16[1024,2048]{1,0:T(8,128)(2,1)S(1)}, bf16[1024,2048]{1,0:T(8,128)(2,1)}, u32[]{:S(2)}) copy-start(bf16[1024,2048]{1,0:T(8,128)(2,1)} %refs_2_.7) | copy-start | bytes 12582916
  9.3 14.5 %collective-permute-start.7 = (bf16[36,1024]{1,0:T(8,128)(2,1)S(1)}, bf16[36,1024]{1,0:T(8,128)(2,1)S(1)}, u32[]{:S(2)}, u32[]{:S(2)}) collective-permute-start(bf16[36,1024]{1,0:T(8,128)(2,1)S(1)} %get-tuple-element.56), channel_id=1, source_target_pairs={{0,6},{2,4},{4,2},{6,0},{1,7},{3,5},{5,3},{7,1},{8,14},{10,12},{12... | collective-permute-start | bytes 221192 | tf_op jit(solution)/shard_map/ppermute | solution.py:408
  13.1 10.7 %collective-permute-start.8 = (bf16[36,1024]{1,0:T(8,128)(2,1)S(1)}, bf16[36,1024]{1,0:T(8,128)(2,1)S(1)}, u32[]{:S(2)}, u32[]{:S(2)}) collective-permute-start(bf16[36,1024]{1,0:T(8,128)(2,1)S(1)} %get-tuple-element.57), channel_id=1, source_target_pairs={{0,4},{2,6},{4,0},{6,2},{1,5},{3,7},{5,1},{7,3},{8,12},{10,14},{12... | collective-permute-start | bytes 221192 | tf_op jit(solution)/shard_map/ppermute | solution.py:408
  13.1 10.7 %collective-permute-start.9 = (bf16[36,1024]{1,0:T(8,128)(2,1)S(1)}, bf16[36,1024]{1,0:T(8,128)(2,1)S(1)}, u32[]{:S(2)}, u32[]{:S(2)}) collective-permute-start(bf16[36,1024]{1,0:T(8,128)(2,1)S(1)} %get-tuple-element.58), channel_id=1, source_target_pairs={{0,2},{2,0},{4,6},{6,4},{1,3},{3,1},{5,7},{7,5},{8,10},{10,8},{12,... | collective-permute-start | bytes 221192 | tf_op jit(solution)/shard_map/ppermute | solution.py:408
  18.6 7.5 %collective-permute-start.3 = (bf16[144,1024]{1,0:T(8,128)(2,1)S(1)}, bf16[144,1024]{1,0:T(8,128)(2,1)S(1)}, u32[]{:S(2)}, u32[]{:S(2)}) collective-permute-start(bf16[144,1024]{1,0:T(8,128)(2,1)S(1)} %join.2.refs_0_.refs_4_), channel_id=1, source_target_pairs={{0,1},{1,0},{2,3},{3,2},{4,5},{5,4},{6,7},{7,6},{8,9},{9,8},{10,11... | collective-permute-start | bytes 884744 | tf_op jit(solution)/shard_map/ppermute | solution.py:403
  20.1 12.4 %collective-permute-start.12 = (bf16[144,1024]{1,0:T(8,128)(2,1)S(1)}, bf16[144,1024]{1,0:T(8,128)(2,1)S(1)}, u32[]{:S(2)}, u32[]{:S(2)}) collective-permute-start(bf16[144,1024]{1,0:T(8,128)(2,1)S(1)} %join.2.refs_0_.refs_4_), channel_id=1, source_target_pairs={{0,16},{16,0},{1,17},{17,1},{2,18},{18,2},{3,19},{19,3},{4,20},{20... | collective-permute-start | bytes 884744 | tf_op jit(solution)/shard_map/ppermute | solution.py:403
  23.9 9.5 %collective-permute-start.11 = (bf16[144,1024]{1,0:T(8,128)(2,1)S(1)}, bf16[144,1024]{1,0:T(8,128)(2,1)S(1)}, u32[]{:S(2)}, u32[]{:S(2)}) collective-permute-start(bf16[144,1024]{1,0:T(8,128)(2,1)S(1)} %join.3.refs_0_), channel_id=1, source_target_pairs={{0,16},{16,0},{1,17},{17,1},{2,18},{18,2},{3,19},{19,3},{4,20},{20... | collective-permute-start | bytes 884744 | tf_op jit(solution)/shard_map/ppermute | solution.py:403
  24.5 10.7 %collective-permute-start.10 = (bf16[144,1024]{1,0:T(8,128)(2,1)S(1)}, bf16[144,1024]{1,0:T(8,128)(2,1)S(1)}, u32[]{:S(2)}, u32[]{:S(2)}) collective-permute-start(bf16[144,1024]{1,0:T(8,128)(2,1)S(1)} %join.3.refs_0_), channel_id=1, source_target_pairs={{0,1},{1,0},{2,3},{3,2},{4,5},{5,4},{6,7},{7,6},{8,9},{9,8},{10,11... | collective-permute-start | bytes 884744 | tf_op jit(solution)/shard_map/ppermute | solution.py:403
  28.4 13.7 %collective-permute-start.4 = (bf16[72,1024]{1,0:T(8,128)(2,1)S(1)}, bf16[72,1024]{1,0:T(8,128)(2,1)S(1)}, u32[]{:S(2)}, u32[]{:S(2)}) collective-permute-start(bf16[72,1024]{1,0:T(8,128)(2,1)S(1)} %get-tuple-element.48), channel_id=1, source_target_pairs={{0,2},{2,0},{4,6},{6,4},{1,3},{3,1},{5,7},{7,5},{8,10},{10,8},{12,... | collective-permute-start | bytes 442376 | tf_op jit(solution)/shard_map/ppermute | solution.py:408
  28.4 13.6 %collective-permute-start.5 = (bf16[72,1024]{1,0:T(8,128)(2,1)S(1)}, bf16[72,1024]{1,0:T(8,128)(2,1)S(1)}, u32[]{:S(2)}, u32[]{:S(2)}) collective-permute-start(bf16[72,1024]{1,0:T(8,128)(2,1)S(1)} %get-tuple-element.49), channel_id=1, source_target_pairs={{0,4},{2,6},{4,0},{6,2},{1,5},{3,7},{5,1},{7,3},{8,12},{10,14},{12... | collective-permute-start | bytes 442376 | tf_op jit(solution)/shard_map/ppermute | solution.py:408
  32.4 9.7 %collective-permute-start.6 = (bf16[72,1024]{1,0:T(8,128)(2,1)S(1)}, bf16[72,1024]{1,0:T(8,128)(2,1)S(1)}, u32[]{:S(2)}, u32[]{:S(2)}) collective-permute-start(bf16[72,1024]{1,0:T(8,128)(2,1)S(1)} %get-tuple-element.50), channel_id=1, source_target_pairs={{0,6},{2,4},{4,2},{6,0},{1,7},{3,5},{5,3},{7,1},{8,14},{10,12},{12... | collective-permute-start | bytes 442376 | tf_op jit(solution)/shard_map/ppermute | solution.py:408
  33.4 7.1 %collective-permute-start.13 = (bf16[144,1024]{1,0:T(8,128)(2,1)S(1)}, bf16[144,1024]{1,0:T(8,128)(2,1)S(1)}, u32[]{:S(2)}, u32[]{:S(2)}) collective-permute-start(bf16[144,1024]{1,0:T(8,128)(2,1)S(1)} %relay.4.refs_1_), channel_id=1, source_target_pairs={{0,16},{16,0},{1,17},{17,1},{2,18},{18,2},{3,19},{19,3},{4,20},{20... | collective-permute-start | bytes 884744 | tf_op jit(solution)/shard_map/ppermute | solution.py:403
  35.2 8.1 %collective-permute-start.15 = (bf16[144,1024]{1,0:T(8,128)(2,1)S(1)}, bf16[144,1024]{1,0:T(8,128)(2,1)S(1)}, u32[]{:S(2)}, u32[]{:S(2)}) collective-permute-start(bf16[144,1024]{1,0:T(8,128)(2,1)S(1)} %relay.5.refs_0_), channel_id=1, source_target_pairs={{0,1},{1,0},{2,3},{3,2},{4,5},{5,4},{6,7},{7,6},{8,9},{9,8},{10,11... | collective-permute-start | bytes 884744 | tf_op jit(solution)/shard_map/ppermute | solution.py:403
  42.2 7.4 %collective-permute-start.14 = (bf16[144,1024]{1,0:T(8,128)(2,1)S(1)}, bf16[144,1024]{1,0:T(8,128)(2,1)S(1)}, u32[]{:S(2)}, u32[]{:S(2)}) collective-permute-start(bf16[144,1024]{1,0:T(8,128)(2,1)S(1)} %get-tuple-element.68), channel_id=1, source_target_pairs={{0,1},{1,0},{2,3},{3,2},{4,5},{5,4},{6,7},{7,6},{8,9},{9,8},{10,11... | collective-permute-start | bytes 884744 | tf_op jit(solution)/shard_map/ppermute | solution.py:403
  45.7 2.8 %collective-permute-start.16 = (bf16[512,1024]{1,0:T(8,128)(2,1)S(1)}, bf16[512,1024]{1,0:T(8,128)(2,1)S(1)}, u32[]{:S(2)}, u32[]{:S(2)}) collective-permute-start(bf16[512,1024]{1,0:T(8,128)(2,1)S(1)} %get-tuple-element.72), channel_id=1, source_target_pairs={{0,8},{8,0},{1,9},{9,1},{2,10},{10,2},{3,11},{11,3},{4,12},{12,4},... | collective-permute-start | bytes 3145736 | tf_op jit(solution)/shard_map/ppermute | solution.py:403
  47.9 2.8 %collective-permute-start.17 = (bf16[512,1024]{1,0:T(8,128)(2,1)S(1)}, bf16[512,1024]{1,0:T(8,128)(2,1)S(1)}, u32[]{:S(2)}, u32[]{:S(2)}) collective-permute-start(bf16[512,1024]{1,0:T(8,128)(2,1)S(1)} %get-tuple-element.75), channel_id=1, source_target_pairs={{0,8},{8,0},{1,9},{9,1},{2,10},{10,2},{3,11},{11,3},{4,12},{12,4},... | collective-permute-start | bytes 3145736 | tf_op jit(solution)/shard_map/ppermute | solution.py:403

commit v20 on v19

--- a/solution.py
+++ b/solution.py
@@ -93,20 +93,21 @@
     )(*scalars, kept(kind), kept(x), kept(g))
 
 
-def join_kernel(*refs):
-    refs[-1][...] = stacked(refs[-2 : -2 - EXPERTS : -1]).astype(BF16)
-
-
-def join(blocks, earlier=()):
+def join_kernel(order, *refs):
+    blocks = refs[-1 - EXPERTS : -1]
+    refs[-1][...] = stacked([blocks[order.index(k)] for k in range(EXPERTS)]).astype(BF16)
+
+
+def join(blocks, order, earlier=()):
     width = blocks[0].shape[1]
     return pl.pallas_call(
-        join_kernel,
+        functools.partial(join_kernel, order),
         out_shape=jax.ShapeDtypeStruct((EXPERTS * CAP, width), BF16),
         in_specs=[ANYWHERE] * len(earlier) + [HERE] * EXPERTS,
         compiler_params=SMALL,
         cost_estimate=CHEAP,
         name="join",
-    )(*earlier, *blocks[::-1])
+    )(*earlier, *[blocks[k] for k in order])
 
 
 def relay_kernel(n, *refs):
@@ -423,13 +424,13 @@
     placer, *blocks = pack(scalars, archetype.reshape(1, tokens), designs, cotangent)
     wd, wdt = w_down, flip(w_down, [placer])
 
-    x_own = join(across_planes(blocks[:EXPERTS]))
+    x_own = join(across_planes(blocks[:EXPERTS]), (3, 2, 1, 0))
     moved = across_planes(relay(blocks[EXPERTS:], [wdt]))
     x_far, x_near = swap(x_own, "far"), swap(x_own, "half")
 
     wg, wu = w_gate, w_up
     act0, coef0, share_own = forward([x_own], wg, wu, wd)
-    g_own = join(moved, [act0])
+    g_own = join(moved, (1, 3, 2, 0), [act0])
     g_far, g_near = swap(g_own, "far"), swap(g_own, "half")
     act1, coef1, *shares = forward([x_near], wg, wu, wd, other=share_own)
     (x_pass,) = relay([x_near], [mark(act1, x_far), g_far])

time: 53.1 us -> 49.8 us (0.938); the launches traced: 52 us -> 49.7 us
  waiting for transfers between devices: 5.88 us -> 3.14 us
    ppermute x9, waiting for transfers between devices: 4.2 us -> 1.36 us  [across_planes(): lax.ppermute(blocks[k], 'arch', [(i, i ^ k) for i in range(EXPERTS)])]
    ppermute x9, starting transfers between devices: 15.3 us -> 15.8 us  [across_planes(): lax.ppermute(blocks[k], 'arch', [(i, i ^ k) for i in range(EXPERTS)])]
  transfers between devices with their start and end apart: 18 -> 18, of which waited for: 4 -> 5; matrix products, arithmetic and copies ran while one was open for 0% -> 0% of each run, Pallas kernels for 35% -> 36%
where the time goes in v20:
time: 49.8 us; the launch traced here: 49.7 us
  starting transfers between devices  24.7 us (50%)
  Pallas kernels  20.8 us (42%)
  waiting for transfers between devices  3.14 us (6%)
  between operations  1 us (2%)
    ppermute x9, starting transfers between devices, across_planes(): lax.ppermute(blocks[k], 'arch', [(i, i ^ k) for i in range(EXPERTS)])  15.8 us
    ppermute x9, starting transfers between devices, swap(): return lax.ppermute(value, axis, [(0, 1), (1, 0)])  8.89 us
    pallas_call x4, Pallas kernels, forward(): pl.pallas_call(functools.partial(forward_kernel, n, fetch, down, pair, le...  7.63 us
    pallas_call x2, Pallas kernels, backward(): pl.pallas_call(functools.partial(backward_kernel, first), out_shape=[jax....  4.45 us
    pallas_call x2, Pallas kernels, finish(): pl.pallas_call(functools.partial(finish_kernel, spans, more, len(earlier)...  2.21 us
    pallas_call x1, Pallas kernels, slopes(): pl.pallas_call(functools.partial(slopes_kernel, n), out_shape=[jax.ShapeD...  2.19 us
    ppermute x9, waiting for transfers between devices, swap(): return lax.ppermute(value, axis, [(0, 1), (1, 0)])  1.77 us
    pallas_call x1, Pallas kernels, pack(): pl.pallas_call(pack_kernel, out_shape=[jax.ShapeDtypeStruct((EXPERTS * CA...  1.61 us
  transfers between devices with their start and end apart: 18, of which 5 were waited for; matrix products, arithmetic and copies ran while one was open for 0% of the time, Pallas kernels for 36%

profile of v20, /device:TPU:0, one launch (start us, length us, event | category | flops | bytes accessed | tf_op | source)
XLA Modules:
  0.0 49.7 jit_solution(8540891362429356451)
XLA Ops:
  0.7 1.6 %pack.1 = (bf16[144,128]{1,0:T(8,128)(2,1)S(1)}, bf16[36,1024]{1,0:T(8,128)(2,1)S(1)}, bf16[36,1024]{1,0:T(8,128)(2,1)S(1)}, bf16[36,1024]{1,0:T(8,128)(2,1)S(1)...) custom-call(s32[1]{0:T(128)} %bitcast.plane_ref, ...), custom_call_target="tpu_custom_call" | custom-call | flops 20000000000 | tf_op jit(solution)/shard_map/pack/pallas_call | solution.py:79
  2.3 5.1 %collective-permute-start = (bf16[36,1024]{1,0:T(8,128)(2,1)S(1)}, bf16[36,1024]{1,0:T(8,128)(2,1)S(1)}, u32[]{:S(2)}, u32[]{:S(2)}) collective-permute-start(bf16[36,1024]{1,0:T(8,128)(2,1)S(1)} %get-tuple-element.42), channel_id=1, source_target_pairs={{0,6},{2,4},{4,2},{6,0},{1,7},{3,5},{5,3},{7,1},{8,14},{10,12},{12... | collective-permute-start | bytes 221192 | tf_op jit(solution)/shard_map/ppermute | solution.py:409
  7.4 0.6 %collective-permute-start.2 = (bf16[36,1024]{1,0:T(8,128)(2,1)S(1)}, bf16[36,1024]{1,0:T(8,128)(2,1)S(1)}, u32[]{:S(2)}, u32[]{:S(2)}) collective-permute-start(bf16[36,1024]{1,0:T(8,128)(2,1)S(1)} %get-tuple-element.44), channel_id=1, source_target_pairs={{0,2},{2,0},{4,6},{6,4},{1,3},{3,1},{5,7},{7,5},{8,10},{10,8},{12,... | collective-permute-start | bytes 221192 | tf_op jit(solution)/shard_map/ppermute | solution.py:409
  8.0 1.2 %flip.1.refs_4_.refs_9_.wdt_ref = bf16[1024,2048]{1,0:T(8,128)(2,1)S(1)} custom-call(bf16[2048,1024]{1,0:T(8,128)(2,1)S(1)} %copy-done.2, bf16[144,128]{1,0:T(8,128)(2,1)S(1)} %get-tuple-element.41.refs_0_.placer_ref), custom_call_target="tpu_custom_call" | custom-call | tf_op jit(solution)/shard_map/flip/pallas_call | solution.py:153
  9.3 1.5 %collective-permute-start.7 = (bf16[36,1024]{1,0:T(8,128)(2,1)S(1)}, bf16[36,1024]{1,0:T(8,128)(2,1)S(1)}, u32[]{:S(2)}, u32[]{:S(2)}) collective-permute-start(bf16[36,1024]{1,0:T(8,128)(2,1)S(1)} %get-tuple-element.56), channel_id=1, source_target_pairs={{0,2},{2,0},{4,6},{6,4},{1,3},{3,1},{5,7},{7,5},{8,10},{10,8},{12,... | collective-permute-start | bytes 221192 | tf_op jit(solution)/shard_map/ppermute | solution.py:409
  10.8 2.4 %collective-permute-start.8 = (bf16[36,1024]{1,0:T(8,128)(2,1)S(1)}, bf16[36,1024]{1,0:T(8,128)(2,1)S(1)}, u32[]{:S(2)}, u32[]{:S(2)}) collective-permute-start(bf16[36,1024]{1,0:T(8,128)(2,1)S(1)} %get-tuple-element.57), channel_id=1, source_target_pairs={{0,6},{2,4},{4,2},{6,0},{1,7},{3,5},{5,3},{7,1},{8,14},{10,12},{12... | collective-permute-start | bytes 221192 | tf_op jit(solution)/shard_map/ppermute | solution.py:409
  13.2 1.7 %collective-permute-start.9 = (bf16[36,1024]{1,0:T(8,128)(2,1)S(1)}, bf16[36,1024]{1,0:T(8,128)(2,1)S(1)}, u32[]{:S(2)}, u32[]{:S(2)}) collective-permute-start(bf16[36,1024]{1,0:T(8,128)(2,1)S(1)} %get-tuple-element.58), channel_id=1, source_target_pairs={{0,4},{2,6},{4,0},{6,2},{1,5},{3,7},{5,1},{7,3},{8,12},{10,14},{12... | collective-permute-start | bytes 221192 | tf_op jit(solution)/shard_map/ppermute | solution.py:409
  14.9 0.7 %collective-permute-done.1.refs_1_ = bf16[36,1024]{1,0:T(8,128)(2,1)S(1)} collective-permute-done((bf16[36,1024]{1,0:T(8,128)(2,1)S(1)}, bf16[36,1024]{1,0:T(8,128)(2,1)S(1)}, u32[]{:S(2)}, u32[]{:S(2)}) %collective-permute-start.1) | collective-permute-done | bytes 73760 | tf_op jit(solution)/shard_map/ppermute | solution.py:409
  15.7 1.4 %collective-permute-start.3 = (bf16[144,1024]{1,0:T(8,128)(2,1)S(1)}, bf16[144,1024]{1,0:T(8,128)(2,1)S(1)}, u32[]{:S(2)}, u32[]{:S(2)}) collective-permute-start(bf16[144,1024]{1,0:T(8,128)(2,1)S(1)} %join.2.refs_0_.refs_4_), channel_id=1, source_target_pairs={{0,1},{1,0},{2,3},{3,2},{4,5},{5,4},{6,7},{7,6},{8,9},{9,8},{10,11... | collective-permute-start | bytes 884744 | tf_op jit(solution)/shard_map/ppermute | solution.py:404
  17.1 1.5 %collective-permute-start.12 = (bf16[144,1024]{1,0:T(8,128)(2,1)S(1)}, bf16[144,1024]{1,0:T(8,128)(2,1)S(1)}, u32[]{:S(2)}, u32[]{:S(2)}) collective-permute-start(bf16[144,1024]{1,0:T(8,128)(2,1)S(1)} %join.2.refs_0_.refs_4_), channel_id=1, source_target_pairs={{0,16},{16,0},{1,17},{17,1},{2,18},{18,2},{3,19},{19,3},{4,20},{20... | collective-permute-start | bytes 884744 | tf_op jit(solution)/shard_map/ppermute | solution.py:404
  18.6 2.2 %forward_down.2 = (bf16[144,2048]{1,0:T(8,128)(2,1)S(1)}, bf16[144,2048]{1,0:T(8,128)(2,1)S(1)}, bf16[144,1024]{1,0:T(8,128)(2,1)S(1)}) custom-call(bf16[144,1024]{1,0:T(8,128)(2,1)S(1)} %join.2.refs_0_.refs_4_, bf16[1024,2048]{1,0:T(8,128)(2,1)S(1)} %copy-done, bf16[1024,2048]{1,0:T(8,128)(2,1)S(1)} %copy-done.1, bf16[2048,1024]{1,0:T(8,128)(2,1)S(1)} %copy-done.2), custom_call_target="tpu_custom_call" | custom-call | tf_op jit(solution)/shard_map/forward_down/pallas_call | solution.py:232
  20.8 0.5 collective-permute-done.9.refs_3_
  21.3 1.6 %collective-permute-start.11 = (bf16[144,1024]{1,0:T(8,128)(2,1)S(1)}, bf16[144,1024]{1,0:T(8,128)(2,1)S(1)}, u32[]{:S(2)}, u32[]{:S(2)}) collective-permute-start(bf16[144,1024]{1,0:T(8,128)(2,1)S(1)} %join.3.refs_0_), channel_id=1, source_target_pairs={{0,16},{16,0},{1,17},{17,1},{2,18},{18,2},{3,19},{19,3},{4,20},{20... | collective-permute-start | bytes 884744 | tf_op jit(solution)/shard_map/ppermute | solution.py:404
  22.9 1.5 %collective-permute-start.10 = (bf16[144,1024]{1,0:T(8,128)(2,1)S(1)}, bf16[144,1024]{1,0:T(8,128)(2,1)S(1)}, u32[]{:S(2)}, u32[]{:S(2)}) collective-permute-start(bf16[144,1024]{1,0:T(8,128)(2,1)S(1)} %join.3.refs_0_), channel_id=1, source_target_pairs={{0,1},{1,0},{2,3},{3,2},{4,5},{5,4},{6,7},{7,6},{8,9},{9,8},{10,11... | collective-permute-start | bytes 884744 | tf_op jit(solution)/shard_map/ppermute | solution.py:404
  24.4 2.2 %forward_down.3 = (bf16[144,2048]{1,0:T(8,128)(2,1)S(1)}, bf16[144,2048]{1,0:T(8,128)(2,1)S(1)}, bf16[72,1024]{1,0:T(8,128)(2,1)S(1)}, bf16[72,1024]{1,0:T(8,128...) custom-call(bf16[144,1024]{1,0:T(8,128)(2,1)S(1)} %collective-permute-done.3.refs_0_.refs_1_.refs_5_, ...), custom_call_target="tpu_custom_call" | custom-call | tf_op jit(solution)/shard_map/forward_down/pallas_call | solution.py:232
  26.7 3.2 %collective-permute-start.5 = (bf16[72,1024]{1,0:T(8,128)(2,1)S(1)}, bf16[72,1024]{1,0:T(8,128)(2,1)S(1)}, u32[]{:S(2)}, u32[]{:S(2)}) collective-permute-start(bf16[72,1024]{1,0:T(8,128)(2,1)S(1)} %get-tuple-element.49), channel_id=1, source_target_pairs={{0,4},{2,6},{4,0},{6,2},{1,5},{3,7},{5,1},{7,3},{8,12},{10,14},{12... | collective-permute-start | bytes 442376 | tf_op jit(solution)/shard_map/ppermute | solution.py:409
  30.0 1.1 %collective-permute-start.6 = (bf16[72,1024]{1,0:T(8,128)(2,1)S(1)}, bf16[72,1024]{1,0:T(8,128)(2,1)S(1)}, u32[]{:S(2)}, u32[]{:S(2)}) collective-permute-start(bf16[72,1024]{1,0:T(8,128)(2,1)S(1)} %get-tuple-element.50), channel_id=1, source_target_pairs={{0,6},{2,4},{4,2},{6,0},{1,7},{3,5},{5,3},{7,1},{8,14},{10,12},{12... | collective-permute-start | bytes 442376 | tf_op jit(solution)/shard_map/ppermute | solution.py:409
  31.1 0.7 %collective-permute-start.13 = (bf16[144,1024]{1,0:T(8,128)(2,1)S(1)}, bf16[144,1024]{1,0:T(8,128)(2,1)S(1)}, u32[]{:S(2)}, u32[]{:S(2)}) collective-permute-start(bf16[144,1024]{1,0:T(8,128)(2,1)S(1)} %relay.4.refs_1_), channel_id=1, source_target_pairs={{0,16},{16,0},{1,17},{17,1},{2,18},{18,2},{3,19},{19,3},{4,20},{20... | collective-permute-start | bytes 884744 | tf_op jit(solution)/shard_map/ppermute | solution.py:404
  31.9 1.0 %collective-permute-start.15 = (bf16[144,1024]{1,0:T(8,128)(2,1)S(1)}, bf16[144,1024]{1,0:T(8,128)(2,1)S(1)}, u32[]{:S(2)}, u32[]{:S(2)}) collective-permute-start(bf16[144,1024]{1,0:T(8,128)(2,1)S(1)} %relay.5.refs_0_), channel_id=1, source_target_pairs={{0,1},{1,0},{2,3},{3,2},{4,5},{5,4},{6,7},{7,6},{8,9},{9,8},{10,11... | collective-permute-start | bytes 884744 | tf_op jit(solution)/shard_map/ppermute | solution.py:404
  32.9 1.6 %forward.2 = (bf16[144,2048]{1,0:T(8,128)(2,1)S(1)}, bf16[144,2048]{1,0:T(8,128)(2,1)S(1)}) custom-call(bf16[144,1024]{1,0:T(8,128)(2,1)S(1)} %relay.5.refs_0_, bf16[144,1024]{1,0:T(8,128)(2,1)S(1)} %collective-permute-done.12._.refs_1_.refs_2_.refs_6_, bf16[1024,2048]{1,0:T(8,128)(2,1)S(1)} %copy-done, bf16[1024,2048]{1,0:T(8,128)(2,1)S(1)} %copy-done.1), custom_call_target="tpu_custom_call" | custom-call | flops 20000000000 | tf_op jit(solution)/shard_map/forward/pallas_call | solution.py:232
  34.5 2.2 %slopes.1 = (bf16[432,2048]{1,0:T(8,128)(2,1)S(1)}, bf16[432,2048]{1,0:T(8,128)(2,1)S(1)}) custom-call(bf16[144,1024]{1,0:T(8,128)(2,1)S(1)} %join.3.refs_0_, bf16[144,1024]{1,0:T(8,128)(2,1)S(1)} %collective-permute-done.10.refs_2_.refs_1_, bf16[144,1024]{1,0:T(8,128)(2,1)S(1)} %collective-permute-done.11.refs_2_.refs_0_, ...), custom_call_target="tpu_custom_call" | custom-call | tf_op jit(solution)/shard_map/slopes/pallas_call | solution.py:291
  36.7 1.6 %collective-permute-done.13.refs_1_.refs_3_.refs_7_ = bf16[144,1024]{1,0:T(8,128)(2,1)S(1)} collective-permute-done((bf16[144,1024]{1,0:T(8,128)(2,1)S(1)}, bf16[144,1024]{1,0:T(8,128)(2,1)S(1)}, u32[]{:S(2)}, u32[]{:S(2)}) %collective-permute-start.13) | collective-permute-done | bytes 294944 | tf_op jit(solution)/shard_map/ppermute | solution.py:404
  38.3 1.6 %forward.3 = (bf16[144,2048]{1,0:T(8,128)(2,1)S(1)}, bf16[144,2048]{1,0:T(8,128)(2,1)S(1)}) custom-call(bf16[432,2048]{1,0:T(8,128)(2,1)S(1)} %get-tuple-element.65.refs_0_.dg_ref, bf16[144,1024]{1,0:T(8,128)(2,1)S(1)} %collective-permute-done.13.refs_1_.refs_3_.refs_7_, bf16[1024,2048]{1,0:T(8,128)(2,1)S(1)} %copy-done, bf16[1024,2048]{1,0:T(8,128)(2,1)S(1)} %copy-done.1), custom_call_target="tpu_custom_call" | custom-call | tf_op jit(solution)/shard_map/forward/pallas_call | solution.py:232
  39.9 0.2 collective-permute-done.5.refs_2_
  40.2 0.6 %collective-permute-start.14 = (bf16[144,1024]{1,0:T(8,128)(2,1)S(1)}, bf16[144,1024]{1,0:T(8,128)(2,1)S(1)}, u32[]{:S(2)}, u32[]{:S(2)}) collective-permute-start(bf16[144,1024]{1,0:T(8,128)(2,1)S(1)} %get-tuple-element.68), channel_id=1, source_target_pairs={{0,1},{1,0},{2,3},{3,2},{4,5},{5,4},{6,7},{7,6},{8,9},{9,8},{10,11... | collective-permute-start | bytes 884744 | tf_op jit(solution)/shard_map/ppermute | solution.py:404
  40.8 0.2 turn.1.xt_ref
  41.0 2.3 %backward.2 = (bf16[512,1024]{1,0:T(8,128)(2,1)S(1)}, bf16[512,1024]{1,0:T(8,128)(2,1)S(1)}) custom-call(bf16[512,576]{1,0:T(8,128)(2,1)S(1)} %turn.1.xt_ref, bf16[144,1024]{1,0:T(8,128)(2,1)S(1)} %collective-permute-done.15.g_ref, bf16[144,2048]{1,0:T(8,128)(2,1)S(1)} %get-tuple-element.66.refs_4_.act_ref, ...), custom_call_target="tpu_custom_call" | custom-call | flops 20000000000 | tf_op jit(solution)/shard_map/backward/pallas_call | solution.py:318
  43.4 2.1 %backward.3 = (bf16[512,1024]{1,0:T(8,128)(2,1)S(1)}, bf16[512,1024]{1,0:T(8,128)(2,1)S(1)}) custom-call(bf16[512,576]{1,0:T(8,128)(2,1)S(1)} %turn.1.xt_ref, bf16[144,1024]{1,0:T(8,128)(2,1)S(1)} %collective-permute-done.15.g_ref, bf16[144,2048]{1,0:T(8,128)(2,1)S(1)} %get-tuple-element.66.refs_4_.act_ref, ...), custom_call_target="tpu_custom_call" | custom-call | flops 20000000000 | tf_op jit(solution)/shard_map/backward/pallas_call | solution.py:318
  45.6 0.6 %collective-permute-start.17 = (bf16[512,1024]{1,0:T(8,128)(2,1)S(1)}, bf16[512,1024]{1,0:T(8,128)(2,1)S(1)}, u32[]{:S(2)}, u32[]{:S(2)}) collective-permute-start(bf16[512,1024]{1,0:T(8,128)(2,1)S(1)} %get-tuple-element.75), channel_id=1, source_target_pairs={{0,8},{8,0},{1,9},{9,1},{2,10},{10,2},{3,11},{11,3},{4,12},{12,4},... | collective-permute-start | bytes 3145736 | tf_op jit(solution)/shard_map/ppermute | solution.py:404
  46.1 1.1 %finish.2 = (bf16[256,2048]{1,0:T(8,128)(2,1)}, bf16[256,2048]{1,0:T(8,128)(2,1)}) custom-call(bf16[512,1024]{1,0:T(8,128)(2,1)S(1)} %get-tuple-element.71.refs_0_, bf16[512,1024]{1,0:T(8,128)(2,1)S(1)} %collective-permute-done.16.refs_1_), custom_call_target="tpu_custom_call" | custom-call | tf_op jit(solution)/shard_map/finish/pallas_call | solution.py:354
  47.3 1.0 %unpack.1 = bf16[128,1024]{1,0:T(8,128)(2,1)} custom-call(bf16[144,128]{1,0:T(8,128)(2,1)S(1)} %get-tuple-element.41.refs_0_.placer_ref, bf16[144,1024]{1,0:T(8,128)(2,1)S(1)} %get-tuple-element.67.mine_ref, bf16[144,1024]{1,0:T(8,128)(2,1)S(1)} %collective-permute-done.14.got_ref, bf16[256,2048]{1,0:T(8,128)(2,1)} %get-tuple-element.73.refs_0_.refs_2_), custom_call_target="tpu_custom_call" | custom-call | flops 20000000000 | tf_op jit(solution)/shard_map/unpack/pallas_call | solution.py:393
  48.4 1.1 %finish.3 = (bf16[256,2048]{1,0:T(8,128)(2,1)}, bf16[256,2048]{1,0:T(8,128)(2,1)}) custom-call(bf16[512,1024]{1,0:T(8,128)(2,1)S(1)} %get-tuple-element.74.refs_0_, bf16[512,1024]{1,0:T(8,128)(2,1)S(1)} %collective-permute-done.17.refs_1_, bf16[256,2048]{1,0:T(8,128)(2,1)} %get-tuple-element.73.refs_0_.refs_2_, ...), custom_call_target="tpu_custom_call", output_to_operand_aliasing={{0}: (2, {}), {1}: (3, {})} | custom-call | tf_op jit(solution)/shard_map/finish/pallas_call | solution.py:354
  (30 shorter events, 0.6 us)
Async XLA Ops:
  0.6 7.4 %copy-start.2 = (bf16[2048,1024]{1,0:T(8,128)(2,1)S(1)}, bf16[2048,1024]{1,0:T(8,128)(2,1)}, u32[]{:S(2)}) copy-start(bf16[2048,1024]{1,0:T(8,128)(2,1)} %source_ref.1) | copy-start | bytes 12582916
  2.3 10.9 %collective-permute-start = (bf16[36,1024]{1,0:T(8,128)(2,1)S(1)}, bf16[36,1024]{1,0:T(8,128)(2,1)S(1)}, u32[]{:S(2)}, u32[]{:S(2)}) collective-permute-start(bf16[36,1024]{1,0:T(8,128)(2,1)S(1)} %get-tuple-element.42), channel_id=1, source_target_pairs={{0,6},{2,4},{4,2},{6,0},{1,7},{3,5},{5,3},{7,1},{8,14},{10,12},{12... | collective-permute-start | bytes 221192 | tf_op jit(solution)/shard_map/ppermute | solution.py:409
  7.4 8.3 %collective-permute-start.1 = (bf16[36,1024]{1,0:T(8,128)(2,1)S(1)}, bf16[36,1024]{1,0:T(8,128)(2,1)S(1)}, u32[]{:S(2)}, u32[]{:S(2)}) collective-permute-start(bf16[36,1024]{1,0:T(8,128)(2,1)S(1)} %get-tuple-element.43), channel_id=1, source_target_pairs={{0,4},{2,6},{4,0},{6,2},{1,5},{3,7},{5,1},{7,3},{8,12},{10,14},{12... | collective-permute-start | bytes 221192 | tf_op jit(solution)/shard_map/ppermute | solution.py:409
  7.4 8.3 %collective-permute-start.2 = (bf16[36,1024]{1,0:T(8,128)(2,1)S(1)}, bf16[36,1024]{1,0:T(8,128)(2,1)S(1)}, u32[]{:S(2)}, u32[]{:S(2)}) collective-permute-start(bf16[36,1024]{1,0:T(8,128)(2,1)S(1)} %get-tuple-element.44), channel_id=1, source_target_pairs={{0,2},{2,0},{4,6},{6,4},{1,3},{3,1},{5,7},{7,5},{8,10},{10,8},{12,... | collective-permute-start | bytes 221192 | tf_op jit(solution)/shard_map/ppermute | solution.py:409
  8.0 10.5 %copy-start.1 = (bf16[1024,2048]{1,0:T(8,128)(2,1)S(1)}, bf16[1024,2048]{1,0:T(8,128)(2,1)}, u32[]{:S(2)}) copy-start(bf16[1024,2048]{1,0:T(8,128)(2,1)} %refs_3_.7) | copy-start | bytes 12582916
  9.3 9.3 %copy-start = (bf16[1024,2048]{1,0:T(8,128)(2,1)S(1)}, bf16[1024,2048]{1,0:T(8,128)(2,1)}, u32[]{:S(2)}) copy-start(bf16[1024,2048]{1,0:T(8,128)(2,1)} %refs_2_.7) | copy-start | bytes 12582916
  9.3 11.5 %collective-permute-start.7 = (bf16[36,1024]{1,0:T(8,128)(2,1)S(1)}, bf16[36,1024]{1,0:T(8,128)(2,1)S(1)}, u32[]{:S(2)}, u32[]{:S(2)}) collective-permute-start(bf16[36,1024]{1,0:T(8,128)(2,1)S(1)} %get-tuple-element.56), channel_id=1, source_target_pairs={{0,2},{2,0},{4,6},{6,4},{1,3},{3,1},{5,7},{7,5},{8,10},{10,8},{12,... | collective-permute-start | bytes 221192 | tf_op jit(solution)/shard_map/ppermute | solution.py:409
  10.8 10.0 %collective-permute-start.8 = (bf16[36,1024]{1,0:T(8,128)(2,1)S(1)}, bf16[36,1024]{1,0:T(8,128)(2,1)S(1)}, u32[]{:S(2)}, u32[]{:S(2)}) collective-permute-start(bf16[36,1024]{1,0:T(8,128)(2,1)S(1)} %get-tuple-element.57), channel_id=1, source_target_pairs={{0,6},{2,4},{4,2},{6,0},{1,7},{3,5},{5,3},{7,1},{8,14},{10,12},{12... | collective-permute-start | bytes 221192 | tf_op jit(solution)/shard_map/ppermute | solution.py:409
  13.2 8.1 %collective-permute-start.9 = (bf16[36,1024]{1,0:T(8,128)(2,1)S(1)}, bf16[36,1024]{1,0:T(8,128)(2,1)S(1)}, u32[]{:S(2)}, u32[]{:S(2)}) collective-permute-start(bf16[36,1024]{1,0:T(8,128)(2,1)S(1)} %get-tuple-element.58), channel_id=1, source_target_pairs={{0,4},{2,6},{4,0},{6,2},{1,5},{3,7},{5,1},{7,3},{8,12},{10,14},{12... | collective-permute-start | bytes 221192 | tf_op jit(solution)/shard_map/ppermute | solution.py:409
  15.7 8.7 %collective-permute-start.3 = (bf16[144,1024]{1,0:T(8,128)(2,1)S(1)}, bf16[144,1024]{1,0:T(8,128)(2,1)S(1)}, u32[]{:S(2)}, u32[]{:S(2)}) collective-permute-start(bf16[144,1024]{1,0:T(8,128)(2,1)S(1)} %join.2.refs_0_.refs_4_), channel_id=1, source_target_pairs={{0,1},{1,0},{2,3},{3,2},{4,5},{5,4},{6,7},{7,6},{8,9},{9,8},{10,11... | collective-permute-start | bytes 884744 | tf_op jit(solution)/shard_map/ppermute | solution.py:404
  17.1 12.9 %collective-permute-start.12 = (bf16[144,1024]{1,0:T(8,128)(2,1)S(1)}, bf16[144,1024]{1,0:T(8,128)(2,1)S(1)}, u32[]{:S(2)}, u32[]{:S(2)}) collective-permute-start(bf16[144,1024]{1,0:T(8,128)(2,1)S(1)} %join.2.refs_0_.refs_4_), channel_id=1, source_target_pairs={{0,16},{16,0},{1,17},{17,1},{2,18},{18,2},{3,19},{19,3},{4,20},{20... | collective-permute-start | bytes 884744 | tf_op jit(solution)/shard_map/ppermute | solution.py:404
  21.3 9.8 %collective-permute-start.11 = (bf16[144,1024]{1,0:T(8,128)(2,1)S(1)}, bf16[144,1024]{1,0:T(8,128)(2,1)S(1)}, u32[]{:S(2)}, u32[]{:S(2)}) collective-permute-start(bf16[144,1024]{1,0:T(8,128)(2,1)S(1)} %join.3.refs_0_), channel_id=1, source_target_pairs={{0,16},{16,0},{1,17},{17,1},{2,18},{18,2},{3,19},{19,3},{4,20},{20... | collective-permute-start | bytes 884744 | tf_op jit(solution)/shard_map/ppermute | solution.py:404
  22.9 9.0 %collective-permute-start.10 = (bf16[144,1024]{1,0:T(8,128)(2,1)S(1)}, bf16[144,1024]{1,0:T(8,128)(2,1)S(1)}, u32[]{:S(2)}, u32[]{:S(2)}) collective-permute-start(bf16[144,1024]{1,0:T(8,128)(2,1)S(1)} %join.3.refs_0_), channel_id=1, source_target_pairs={{0,1},{1,0},{2,3},{3,2},{4,5},{5,4},{6,7},{7,6},{8,9},{9,8},{10,11... | collective-permute-start | bytes 884744 | tf_op jit(solution)/shard_map/ppermute | solution.py:404
  26.6 13.3 %collective-permute-start.4 = (bf16[72,1024]{1,0:T(8,128)(2,1)S(1)}, bf16[72,1024]{1,0:T(8,128)(2,1)S(1)}, u32[]{:S(2)}, u32[]{:S(2)}) collective-permute-start(bf16[72,1024]{1,0:T(8,128)(2,1)S(1)} %get-tuple-element.48), channel_id=1, source_target_pairs={{0,2},{2,0},{4,6},{6,4},{1,3},{3,1},{5,7},{7,5},{8,10},{10,8},{12,... | collective-permute-start | bytes 442376 | tf_op jit(solution)/shard_map/ppermute | solution.py:409
  26.7 13.4 %collective-permute-start.5 = (bf16[72,1024]{1,0:T(8,128)(2,1)S(1)}, bf16[72,1024]{1,0:T(8,128)(2,1)S(1)}, u32[]{:S(2)}, u32[]{:S(2)}) collective-permute-start(bf16[72,1024]{1,0:T(8,128)(2,1)S(1)} %get-tuple-element.49), channel_id=1, source_target_pairs={{0,4},{2,6},{4,0},{6,2},{1,5},{3,7},{5,1},{7,3},{8,12},{10,14},{12... | collective-permute-start | bytes 442376 | tf_op jit(solution)/shard_map/ppermute | solution.py:409
  30.0 10.2 %collective-permute-start.6 = (bf16[72,1024]{1,0:T(8,128)(2,1)S(1)}, bf16[72,1024]{1,0:T(8,128)(2,1)S(1)}, u32[]{:S(2)}, u32[]{:S(2)}) collective-permute-start(bf16[72,1024]{1,0:T(8,128)(2,1)S(1)} %get-tuple-element.50), channel_id=1, source_target_pairs={{0,6},{2,4},{4,2},{6,0},{1,7},{3,5},{5,3},{7,1},{8,14},{10,12},{12... | collective-permute-start | bytes 442376 | tf_op jit(solution)/shard_map/ppermute | solution.py:409
  31.1 7.2 %collective-permute-start.13 = (bf16[144,1024]{1,0:T(8,128)(2,1)S(1)}, bf16[144,1024]{1,0:T(8,128)(2,1)S(1)}, u32[]{:S(2)}, u32[]{:S(2)}) collective-permute-start(bf16[144,1024]{1,0:T(8,128)(2,1)S(1)} %relay.4.refs_1_), channel_id=1, source_target_pairs={{0,16},{16,0},{1,17},{17,1},{2,18},{18,2},{3,19},{19,3},{4,20},{20... | collective-permute-start | bytes 884744 | tf_op jit(solution)/shard_map/ppermute | solution.py:404
  31.9 9.1 %collective-permute-start.15 = (bf16[144,1024]{1,0:T(8,128)(2,1)S(1)}, bf16[144,1024]{1,0:T(8,128)(2,1)S(1)}, u32[]{:S(2)}, u32[]{:S(2)}) collective-permute-start(bf16[144,1024]{1,0:T(8,128)(2,1)S(1)} %relay.5.refs_0_), channel_id=1, source_target_pairs={{0,1},{1,0},{2,3},{3,2},{4,5},{5,4},{6,7},{7,6},{8,9},{9,8},{10,11... | collective-permute-start | bytes 884744 | tf_op jit(solution)/shard_map/ppermute | solution.py:404
  40.2 7.0 %collective-permute-start.14 = (bf16[144,1024]{1,0:T(8,128)(2,1)S(1)}, bf16[144,1024]{1,0:T(8,128)(2,1)S(1)}, u32[]{:S(2)}, u32[]{:S(2)}) collective-permute-start(bf16[144,1024]{1,0:T(8,128)(2,1)S(1)} %get-tuple-element.68), channel_id=1, source_target_pairs={{0,1},{1,0},{2,3},{3,2},{4,5},{5,4},{6,7},{7,6},{8,9},{9,8},{10,11... | collective-permute-start | bytes 884744 | tf_op jit(solution)/shard_map/ppermute | solution.py:404
  43.4 2.8 %collective-permute-start.16 = (bf16[512,1024]{1,0:T(8,128)(2,1)S(1)}, bf16[512,1024]{1,0:T(8,128)(2,1)S(1)}, u32[]{:S(2)}, u32[]{:S(2)}) collective-permute-start(bf16[512,1024]{1,0:T(8,128)(2,1)S(1)} %get-tuple-element.72), channel_id=1, source_target_pairs={{0,8},{8,0},{1,9},{9,1},{2,10},{10,2},{3,11},{11,3},{4,12},{12,4},... | collective-permute-start | bytes 3145736 | tf_op jit(solution)/shard_map/ppermute | solution.py:404
  45.6 2.9 %collective-permute-start.17 = (bf16[512,1024]{1,0:T(8,128)(2,1)S(1)}, bf16[512,1024]{1,0:T(8,128)(2,1)S(1)}, u32[]{:S(2)}, u32[]{:S(2)}) collective-permute-start(bf16[512,1024]{1,0:T(8,128)(2,1)S(1)} %get-tuple-element.75), channel_id=1, source_target_pairs={{0,8},{8,0},{1,9},{9,1},{2,10},{10,2},{3,11},{11,3},{4,12},{12,4},... | collective-permute-start | bytes 3145736 | tf_op jit(solution)/shard_map/ppermute | solution.py:404

commit v21 on v16

--- a/solution.py
+++ b/solution.py
@@ -442,7 +442,7 @@
     (x_pass,) = relay([x_near], [mark(act1, x_far), g_far])
     (g_pass,) = relay([g_far], [x_pass, g_near])
     x_corner, g_corner = swap(x_pass, "far"), swap(g_pass, "half")
-    returned = across_planes(shares)
+    returned = across_planes([*shares[:3], *relay(shares[3:], [g_pass])])
     act2, coef2 = forward([x_far], wg, wu, earlier=[g_pass], cost=DEAR)
     dg, du = slopes([g_own, g_near, g_far], [act0, act1, act2], [coef0, coef1, coef2], wdt)
     act3, coef3 = forward([x_corner], wg, wu, earlier=[dg])

time: 49.7 us -> 51.6 us (1.038)
  starting transfers between devices: 24.8 us -> 27.6 us
  waiting for transfers between devices: 1.37 us -> 0.48 us
    ppermute x9, starting transfers between devices: 14.7 us -> 17.2 us  [across_planes(): lax.ppermute(blocks[k], 'arch', [(i, i ^ k) for i in range(EXPERTS)])]
    ppermute x9, waiting for transfers between devices: 1.03 us -> 0.14 us  [swap(): return lax.ppermute(value, axis, [(0, 1), (1, 0)])]
  transfers between devices with their start and end apart: 18 -> 18, of which waited for: 3 -> 2; matrix products, arithmetic and copies ran while one was open for 0% -> 0% of each run, Pallas kernels for 40% -> 38%
where the time goes in v21:
time: 51.6 us; the launch traced here: 51.4 us
  starting transfers between devices  27.6 us (53%)
  Pallas kernels  22.3 us (43%)
  between operations  1.01 us (2%)
    ppermute x9, starting transfers between devices, across_planes(): lax.ppermute(blocks[k], 'arch', [(i, i ^ k) for i in range(EXPERTS)])  17.2 us
    ppermute x9, starting transfers between devices, swap(): return lax.ppermute(value, axis, [(0, 1), (1, 0)])  10.4 us
    pallas_call x4, Pallas kernels, forward(): pl.pallas_call(functools.partial(forward_kernel, n, fetch, down, pair, le...  7.63 us
    pallas_call x2, Pallas kernels, backward(): pl.pallas_call(functools.partial(backward_kernel, first), out_shape=[jax....  4.42 us
    pallas_call x1, Pallas kernels, flip(): pl.pallas_call(flip_kernel, out_shape=[pltpu.VMEM(value.shape, value.dtyp...  2.88 us
    pallas_call x2, Pallas kernels, finish(): pl.pallas_call(functools.partial(finish_kernel, spans, more, len(earlier)...  2.21 us
    pallas_call x1, Pallas kernels, slopes(): pl.pallas_call(functools.partial(slopes_kernel, n), out_shape=[jax.ShapeD...  2.19 us
    pallas_call x1, Pallas kernels, pack(): pl.pallas_call(pack_kernel, out_shape=[jax.ShapeDtypeStruct((EXPERTS * CA...  1.46 us
  transfers between devices with their start and end apart: 18, of which 2 were waited for; matrix products, arithmetic and copies ran while one was open for 0% of the time, Pallas kernels for 38%

profile of v21, /device:TPU:0, one launch (start us, length us, event | category | flops | bytes accessed | tf_op | source)
XLA Modules:
  0.0 51.4 jit_solution(8283377471500693501)
XLA Ops:
  0.6 1.5 %pack.1 = (bf16[144,128]{1,0:T(8,128)(2,1)S(1)}, bf16[36,1024]{1,0:T(8,128)(2,1)S(1)}, bf16[36,1024]{1,0:T(8,128)(2,1)S(1)}, bf16[36,1024]{1,0:T(8,128)(2,1)S(1)...) custom-call(s32[1]{0:T(128)} %bitcast.plane_ref, ...), custom_call_target="tpu_custom_call" | custom-call | tf_op jit(solution)/shard_map/pack/pallas_call | solution.py:79
  2.1 5.1 %collective-permute-start = (bf16[36,1024]{1,0:T(8,128)(2,1)S(1)}, bf16[36,1024]{1,0:T(8,128)(2,1)S(1)}, u32[]{:S(2)}, u32[]{:S(2)}) collective-permute-start(bf16[36,1024]{1,0:T(8,128)(2,1)S(1)} %get-tuple-element.45), channel_id=1, source_target_pairs={{0,6},{2,4},{4,2},{6,0},{1,7},{3,5},{5,3},{7,1},{8,14},{10,12},{12... | collective-permute-start | bytes 221192 | tf_op jit(solution)/shard_map/ppermute | solution.py:415
  7.2 0.6 %collective-permute-start.2 = (bf16[36,1024]{1,0:T(8,128)(2,1)S(1)}, bf16[36,1024]{1,0:T(8,128)(2,1)S(1)}, u32[]{:S(2)}, u32[]{:S(2)}) collective-permute-start(bf16[36,1024]{1,0:T(8,128)(2,1)S(1)} %get-tuple-element.47), channel_id=1, source_target_pairs={{0,2},{2,0},{4,6},{6,4},{1,3},{3,1},{5,7},{7,5},{8,10},{10,8},{12,... | collective-permute-start | bytes 221192 | tf_op jit(solution)/shard_map/ppermute | solution.py:415
  7.9 2.9 %flip.1 = (bf16[2048,1024]{1,0:T(8,128)(2,1)S(1)}, bf16[1024,2048]{1,0:T(8,128)(2,1)S(1)}) custom-call(bf16[2048,1024]{1,0:T(8,128)(2,1)} %source_ref), custom_call_target="tpu_custom_call" | custom-call | tf_op jit(solution)/shard_map/flip/pallas_call | solution.py:158
  10.8 3.8 %collective-permute-start.6 = (bf16[36,1024]{1,0:T(8,128)(2,1)S(1)}, bf16[36,1024]{1,0:T(8,128)(2,1)S(1)}, u32[]{:S(2)}, u32[]{:S(2)}) collective-permute-start(bf16[36,1024]{1,0:T(8,128)(2,1)S(1)} %get-tuple-element.62), channel_id=1, source_target_pairs={{0,6},{2,4},{4,2},{6,0},{1,7},{3,5},{5,3},{7,1},{8,14},{10,12},{12... | collective-permute-start | bytes 221192 | tf_op jit(solution)/shard_map/ppermute | solution.py:415
  14.6 0.6 %collective-permute-start.8 = (bf16[36,1024]{1,0:T(8,128)(2,1)S(1)}, bf16[36,1024]{1,0:T(8,128)(2,1)S(1)}, u32[]{:S(2)}, u32[]{:S(2)}) collective-permute-start(bf16[36,1024]{1,0:T(8,128)(2,1)S(1)} %get-tuple-element.64), channel_id=1, source_target_pairs={{0,2},{2,0},{4,6},{6,4},{1,3},{3,1},{5,7},{7,5},{8,10},{10,8},{12,... | collective-permute-start | bytes 221192 | tf_op jit(solution)/shard_map/ppermute | solution.py:415
  15.3 1.7 %collective-permute-start.10 = (bf16[144,1024]{1,0:T(8,128)(2,1)S(1)}, bf16[144,1024]{1,0:T(8,128)(2,1)S(1)}, u32[]{:S(2)}, u32[]{:S(2)}) collective-permute-start(bf16[144,1024]{1,0:T(8,128)(2,1)S(1)} %join.2.refs_0_.refs_4_), channel_id=1, source_target_pairs={{0,16},{16,0},{1,17},{17,1},{2,18},{18,2},{3,19},{19,3},{4,20},{20... | collective-permute-start | bytes 884744 | tf_op jit(solution)/shard_map/ppermute | solution.py:410
  17.0 1.5 %collective-permute-start.3 = (bf16[144,1024]{1,0:T(8,128)(2,1)S(1)}, bf16[144,1024]{1,0:T(8,128)(2,1)S(1)}, u32[]{:S(2)}, u32[]{:S(2)}) collective-permute-start(bf16[144,1024]{1,0:T(8,128)(2,1)S(1)} %join.2.refs_0_.refs_4_), channel_id=1, source_target_pairs={{0,1},{1,0},{2,3},{3,2},{4,5},{5,4},{6,7},{7,6},{8,9},{9,8},{10,11... | collective-permute-start | bytes 884744 | tf_op jit(solution)/shard_map/ppermute | solution.py:410
  18.5 2.2 %forward_down.2 = (bf16[144,2048]{1,0:T(8,128)(2,1)S(1)}, bf16[144,2048]{1,0:T(8,128)(2,1)S(1)}, bf16[144,1024]{1,0:T(8,128)(2,1)S(1)}) custom-call(bf16[144,1024]{1,0:T(8,128)(2,1)S(1)} %join.2.refs_0_.refs_4_, bf16[1024,2048]{1,0:T(8,128)(2,1)S(1)} %copy-done, bf16[1024,2048]{1,0:T(8,128)(2,1)S(1)} %copy-done.1, ...), custom_call_target="tpu_custom_call" | custom-call | tf_op jit(solution)/shard_map/forward_down/pallas_call | solution.py:238
  20.8 0.3 collective-permute-done.7.refs_2_
  21.2 1.6 %collective-permute-start.9 = (bf16[144,1024]{1,0:T(8,128)(2,1)S(1)}, bf16[144,1024]{1,0:T(8,128)(2,1)S(1)}, u32[]{:S(2)}, u32[]{:S(2)}) collective-permute-start(bf16[144,1024]{1,0:T(8,128)(2,1)S(1)} %join.3.refs_0_), channel_id=1, source_target_pairs={{0,16},{16,0},{1,17},{17,1},{2,18},{18,2},{3,19},{19,3},{4,20},{20... | collective-permute-start | bytes 884744 | tf_op jit(solution)/shard_map/ppermute | solution.py:410
  22.7 1.5 %collective-permute-start.11 = (bf16[144,1024]{1,0:T(8,128)(2,1)S(1)}, bf16[144,1024]{1,0:T(8,128)(2,1)S(1)}, u32[]{:S(2)}, u32[]{:S(2)}) collective-permute-start(bf16[144,1024]{1,0:T(8,128)(2,1)S(1)} %join.3.refs_0_), channel_id=1, source_target_pairs={{0,1},{1,0},{2,3},{3,2},{4,5},{5,4},{6,7},{7,6},{8,9},{9,8},{10,11... | collective-permute-start | bytes 884744 | tf_op jit(solution)/shard_map/ppermute | solution.py:410
  24.2 2.2 %forward_down.3 = (bf16[144,2048]{1,0:T(8,128)(2,1)S(1)}, bf16[144,2048]{1,0:T(8,128)(2,1)S(1)}, bf16[72,1024]{1,0:T(8,128)(2,1)S(1)}, bf16[72,1024]{1,0:T(8,128...) custom-call(bf16[144,1024]{1,0:T(8,128)(2,1)S(1)} %collective-permute-done.3.refs_0_.refs_1_.refs_5_, ...), custom_call_target="tpu_custom_call" | custom-call | tf_op jit(solution)/shard_map/forward_down/pallas_call | solution.py:238
  26.5 2.4 %collective-permute-start.4 = (bf16[72,1024]{1,0:T(8,128)(2,1)S(1)}, bf16[72,1024]{1,0:T(8,128)(2,1)S(1)}, u32[]{:S(2)}, u32[]{:S(2)}) collective-permute-start(bf16[72,1024]{1,0:T(8,128)(2,1)S(1)} %get-tuple-element.53), channel_id=1, source_target_pairs={{0,2},{2,0},{4,6},{6,4},{1,3},{3,1},{5,7},{7,5},{8,10},{10,8},{12,... | collective-permute-start | bytes 442376 | tf_op jit(solution)/shard_map/ppermute | solution.py:415
  28.9 2.1 %collective-permute-start.5 = (bf16[72,1024]{1,0:T(8,128)(2,1)S(1)}, bf16[72,1024]{1,0:T(8,128)(2,1)S(1)}, u32[]{:S(2)}, u32[]{:S(2)}) collective-permute-start(bf16[72,1024]{1,0:T(8,128)(2,1)S(1)} %get-tuple-element.54), channel_id=1, source_target_pairs={{0,4},{2,6},{4,0},{6,2},{1,5},{3,7},{5,1},{7,3},{8,12},{10,14},{12... | collective-permute-start | bytes 442376 | tf_op jit(solution)/shard_map/ppermute | solution.py:415
  31.0 0.6 %collective-permute-start.13 = (bf16[144,1024]{1,0:T(8,128)(2,1)S(1)}, bf16[144,1024]{1,0:T(8,128)(2,1)S(1)}, u32[]{:S(2)}, u32[]{:S(2)}) collective-permute-start(bf16[144,1024]{1,0:T(8,128)(2,1)S(1)} %relay.5.refs_1_), channel_id=1, source_target_pairs={{0,16},{16,0},{1,17},{17,1},{2,18},{18,2},{3,19},{19,3},{4,20},{20... | collective-permute-start | bytes 884744 | tf_op jit(solution)/shard_map/ppermute | solution.py:410
  31.6 1.6 %collective-permute-start.15 = (bf16[144,1024]{1,0:T(8,128)(2,1)S(1)}, bf16[144,1024]{1,0:T(8,128)(2,1)S(1)}, u32[]{:S(2)}, u32[]{:S(2)}) collective-permute-start(bf16[144,1024]{1,0:T(8,128)(2,1)S(1)} %relay.6.refs_1_.refs_0_), channel_id=1, source_target_pairs={{0,1},{1,0},{2,3},{3,2},{4,5},{5,4},{6,7},{7,6},{8,9},{9,8},{10,11... | collective-permute-start | bytes 884744 | tf_op jit(solution)/shard_map/ppermute | solution.py:410
  33.2 2.5 %collective-permute-start.12 = (bf16[72,1024]{1,0:T(8,128)(2,1)S(1)}, bf16[72,1024]{1,0:T(8,128)(2,1)S(1)}, u32[]{:S(2)}, u32[]{:S(2)}) collective-permute-start(bf16[72,1024]{1,0:T(8,128)(2,1)S(1)} %relay.7), channel_id=1, source_target_pairs={{0,6},{2,4},{4,2},{6,0},{1,7},{3,5},{5,3},{7,1},{8,14},{10,12},{12... | collective-permute-start | bytes 442376 | tf_op jit(solution)/shard_map/ppermute | solution.py:415
  35.8 1.6 %forward.2 = (bf16[144,2048]{1,0:T(8,128)(2,1)S(1)}, bf16[144,2048]{1,0:T(8,128)(2,1)S(1)}) custom-call(bf16[144,1024]{1,0:T(8,128)(2,1)S(1)} %relay.6.refs_1_.refs_0_, bf16[144,1024]{1,0:T(8,128)(2,1)S(1)} %collective-permute-done.10._.refs_1_.refs_2_.refs_6_, bf16[1024,2048]{1,0:T(8,128)(2,1)S(1)} %copy-done, bf16[1024,2048]{1,0:T(8,128)(2,1)S(1)} %copy-done.1), custom_call_target="tpu_custom_call" | custom-call | flops 20000000000 | tf_op jit(solution)/shard_map/forward/pallas_call | solution.py:238
  37.4 2.2 %slopes.1 = (bf16[432,2048]{1,0:T(8,128)(2,1)S(1)}, bf16[432,2048]{1,0:T(8,128)(2,1)S(1)}) custom-call(bf16[144,1024]{1,0:T(8,128)(2,1)S(1)} %join.3.refs_0_, bf16[144,1024]{1,0:T(8,128)(2,1)S(1)} %collective-permute-done.11.refs_2_.refs_1_, bf16[144,1024]{1,0:T(8,128)(2,1)S(1)} %collective-permute-done.9.refs_2_.refs_0_, ...), custom_call_target="tpu_custom_call" | custom-call | tf_op jit(solution)/shard_map/slopes/pallas_call | solution.py:297
  39.6 1.6 %forward.3 = (bf16[144,2048]{1,0:T(8,128)(2,1)S(1)}, bf16[144,2048]{1,0:T(8,128)(2,1)S(1)}) custom-call(bf16[432,2048]{1,0:T(8,128)(2,1)S(1)} %get-tuple-element.71.refs_0_.dg_ref, bf16[144,1024]{1,0:T(8,128)(2,1)S(1)} %collective-permute-done.13.refs_1_.refs_3_.refs_7_, bf16[1024,2048]{1,0:T(8,128)(2,1)S(1)} %copy-done, bf16[1024,2048]{1,0:T(8,128)(2,1)S(1)} %copy-done.1), custom_call_target="tpu_custom_call" | custom-call | tf_op jit(solution)/shard_map/forward/pallas_call | solution.py:238
  41.2 0.1 split.1
  41.3 1.3 %collective-permute-start.14 = (bf16[144,1024]{1,0:T(8,128)(2,1)S(1)}, bf16[144,1024]{1,0:T(8,128)(2,1)S(1)}, u32[]{:S(2)}, u32[]{:S(2)}) collective-permute-start(bf16[144,1024]{1,0:T(8,128)(2,1)S(1)} %get-tuple-element.74), channel_id=1, source_target_pairs={{0,1},{1,0},{2,3},{3,2},{4,5},{5,4},{6,7},{7,6},{8,9},{9,8},{10,11... | collective-permute-start | bytes 884744 | tf_op jit(solution)/shard_map/ppermute | solution.py:410
  42.6 0.2 turn.1.xt_ref
  42.8 2.3 %backward.2 = (bf16[512,1024]{1,0:T(8,128)(2,1)S(1)}, bf16[512,1024]{1,0:T(8,128)(2,1)S(1)}) custom-call(bf16[512,576]{1,0:T(8,128)(2,1)S(1)} %turn.1.xt_ref, bf16[144,1024]{1,0:T(8,128)(2,1)S(1)} %collective-permute-done.15.g_ref, bf16[144,2048]{1,0:T(8,128)(2,1)S(1)} %get-tuple-element.72.refs_4_.act_ref, ...), custom_call_target="tpu_custom_call" | custom-call | flops 20000000000 | tf_op jit(solution)/shard_map/backward/pallas_call | solution.py:324
  45.1 0.1 collective-permute-start.16
  45.2 2.1 %backward.3 = (bf16[512,1024]{1,0:T(8,128)(2,1)S(1)}, bf16[512,1024]{1,0:T(8,128)(2,1)S(1)}) custom-call(bf16[512,576]{1,0:T(8,128)(2,1)S(1)} %turn.1.xt_ref, bf16[144,1024]{1,0:T(8,128)(2,1)S(1)} %collective-permute-done.15.g_ref, bf16[144,2048]{1,0:T(8,128)(2,1)S(1)} %get-tuple-element.72.refs_4_.act_ref, ...), custom_call_target="tpu_custom_call" | custom-call | flops 20000000000 | tf_op jit(solution)/shard_map/backward/pallas_call | solution.py:324
  47.3 0.6 %collective-permute-start.17 = (bf16[512,1024]{1,0:T(8,128)(2,1)S(1)}, bf16[512,1024]{1,0:T(8,128)(2,1)S(1)}, u32[]{:S(2)}, u32[]{:S(2)}) collective-permute-start(bf16[512,1024]{1,0:T(8,128)(2,1)S(1)} %get-tuple-element.81), channel_id=1, source_target_pairs={{0,8},{8,0},{1,9},{9,1},{2,10},{10,2},{3,11},{11,3},{4,12},{12,4},... | collective-permute-start | bytes 3145736 | tf_op jit(solution)/shard_map/ppermute | solution.py:410
  47.9 1.1 %finish.2 = (bf16[256,2048]{1,0:T(8,128)(2,1)}, bf16[256,2048]{1,0:T(8,128)(2,1)}) custom-call(bf16[512,1024]{1,0:T(8,128)(2,1)S(1)} %get-tuple-element.77.refs_0_, bf16[512,1024]{1,0:T(8,128)(2,1)S(1)} %collective-permute-done.16.refs_1_), custom_call_target="tpu_custom_call" | custom-call | tf_op jit(solution)/shard_map/finish/pallas_call | solution.py:360
  49.0 1.0 %unpack.1 = bf16[128,1024]{1,0:T(8,128)(2,1)} custom-call(bf16[144,128]{1,0:T(8,128)(2,1)S(1)} %get-tuple-element.44.placer_ref, bf16[144,1024]{1,0:T(8,128)(2,1)S(1)} %get-tuple-element.73.mine_ref, bf16[144,1024]{1,0:T(8,128)(2,1)S(1)} %collective-permute-done.14.got_ref, bf16[256,2048]{1,0:T(8,128)(2,1)} %get-tuple-element.79.refs_0_.refs_2_), custom_call_target="tpu_custom_call" | custom-call | flops 20000000000 | tf_op jit(solution)/shard_map/unpack/pallas_call | solution.py:399
  50.1 0.1 collective-permute-done.17.refs_1_
  50.2 1.1 %finish.3 = (bf16[256,2048]{1,0:T(8,128)(2,1)}, bf16[256,2048]{1,0:T(8,128)(2,1)}) custom-call(bf16[512,1024]{1,0:T(8,128)(2,1)S(1)} %get-tuple-element.80.refs_0_, bf16[512,1024]{1,0:T(8,128)(2,1)S(1)} %collective-permute-done.17.refs_1_, bf16[256,2048]{1,0:T(8,128)(2,1)} %get-tuple-element.79.refs_0_.refs_2_, ...), custom_call_target="tpu_custom_call", output_to_operand_aliasing={{0}: (2, {}), {1}: (3, {})} | custom-call | tf_op jit(solution)/shard_map/finish/pallas_call | solution.py:360
  (29 shorter events, 0.2 us)
Async XLA Ops:
  2.1 12.5 %collective-permute-start = (bf16[36,1024]{1,0:T(8,128)(2,1)S(1)}, bf16[36,1024]{1,0:T(8,128)(2,1)S(1)}, u32[]{:S(2)}, u32[]{:S(2)}) collective-permute-start(bf16[36,1024]{1,0:T(8,128)(2,1)S(1)} %get-tuple-element.45), channel_id=1, source_target_pairs={{0,6},{2,4},{4,2},{6,0},{1,7},{3,5},{5,3},{7,1},{8,14},{10,12},{12... | collective-permute-start | bytes 221192 | tf_op jit(solution)/shard_map/ppermute | solution.py:415
  7.2 8.0 %collective-permute-start.1 = (bf16[36,1024]{1,0:T(8,128)(2,1)S(1)}, bf16[36,1024]{1,0:T(8,128)(2,1)S(1)}, u32[]{:S(2)}, u32[]{:S(2)}) collective-permute-start(bf16[36,1024]{1,0:T(8,128)(2,1)S(1)} %get-tuple-element.46), channel_id=1, source_target_pairs={{0,4},{2,6},{4,0},{6,2},{1,5},{3,7},{5,1},{7,3},{8,12},{10,14},{12... | collective-permute-start | bytes 221192 | tf_op jit(solution)/shard_map/ppermute | solution.py:415
  7.2 8.0 %collective-permute-start.2 = (bf16[36,1024]{1,0:T(8,128)(2,1)S(1)}, bf16[36,1024]{1,0:T(8,128)(2,1)S(1)}, u32[]{:S(2)}, u32[]{:S(2)}) collective-permute-start(bf16[36,1024]{1,0:T(8,128)(2,1)S(1)} %get-tuple-element.47), channel_id=1, source_target_pairs={{0,2},{2,0},{4,6},{6,4},{1,3},{3,1},{5,7},{7,5},{8,10},{10,8},{12,... | collective-permute-start | bytes 221192 | tf_op jit(solution)/shard_map/ppermute | solution.py:415
  7.9 10.7 %copy-start = (bf16[1024,2048]{1,0:T(8,128)(2,1)S(1)}, bf16[1024,2048]{1,0:T(8,128)(2,1)}, u32[]{:S(2)}) copy-start(bf16[1024,2048]{1,0:T(8,128)(2,1)} %refs_2_.7) | copy-start | bytes 12582916
  7.9 10.7 %copy-start.1 = (bf16[1024,2048]{1,0:T(8,128)(2,1)S(1)}, bf16[1024,2048]{1,0:T(8,128)(2,1)}, u32[]{:S(2)}) copy-start(bf16[1024,2048]{1,0:T(8,128)(2,1)} %refs_3_.3) | copy-start | bytes 12582916
  10.8 10.0 %collective-permute-start.6 = (bf16[36,1024]{1,0:T(8,128)(2,1)S(1)}, bf16[36,1024]{1,0:T(8,128)(2,1)S(1)}, u32[]{:S(2)}, u32[]{:S(2)}) collective-permute-start(bf16[36,1024]{1,0:T(8,128)(2,1)S(1)} %get-tuple-element.62), channel_id=1, source_target_pairs={{0,6},{2,4},{4,2},{6,0},{1,7},{3,5},{5,3},{7,1},{8,14},{10,12},{12... | collective-permute-start | bytes 221192 | tf_op jit(solution)/shard_map/ppermute | solution.py:415
  14.6 6.5 %collective-permute-start.7 = (bf16[36,1024]{1,0:T(8,128)(2,1)S(1)}, bf16[36,1024]{1,0:T(8,128)(2,1)S(1)}, u32[]{:S(2)}, u32[]{:S(2)}) collective-permute-start(bf16[36,1024]{1,0:T(8,128)(2,1)S(1)} %get-tuple-element.63), channel_id=1, source_target_pairs={{0,4},{2,6},{4,0},{6,2},{1,5},{3,7},{5,1},{7,3},{8,12},{10,14},{12... | collective-permute-start | bytes 221192 | tf_op jit(solution)/shard_map/ppermute | solution.py:415
  14.6 6.5 %collective-permute-start.8 = (bf16[36,1024]{1,0:T(8,128)(2,1)S(1)}, bf16[36,1024]{1,0:T(8,128)(2,1)S(1)}, u32[]{:S(2)}, u32[]{:S(2)}) collective-permute-start(bf16[36,1024]{1,0:T(8,128)(2,1)S(1)} %get-tuple-element.64), channel_id=1, source_target_pairs={{0,2},{2,0},{4,6},{6,4},{1,3},{3,1},{5,7},{7,5},{8,10},{10,8},{12,... | collective-permute-start | bytes 221192 | tf_op jit(solution)/shard_map/ppermute | solution.py:415
  15.3 15.7 %collective-permute-start.10 = (bf16[144,1024]{1,0:T(8,128)(2,1)S(1)}, bf16[144,1024]{1,0:T(8,128)(2,1)S(1)}, u32[]{:S(2)}, u32[]{:S(2)}) collective-permute-start(bf16[144,1024]{1,0:T(8,128)(2,1)S(1)} %join.2.refs_0_.refs_4_), channel_id=1, source_target_pairs={{0,16},{16,0},{1,17},{17,1},{2,18},{18,2},{3,19},{19,3},{4,20},{20... | collective-permute-start | bytes 884744 | tf_op jit(solution)/shard_map/ppermute | solution.py:410
  17.0 7.2 %collective-permute-start.3 = (bf16[144,1024]{1,0:T(8,128)(2,1)S(1)}, bf16[144,1024]{1,0:T(8,128)(2,1)S(1)}, u32[]{:S(2)}, u32[]{:S(2)}) collective-permute-start(bf16[144,1024]{1,0:T(8,128)(2,1)S(1)} %join.2.refs_0_.refs_4_), channel_id=1, source_target_pairs={{0,1},{1,0},{2,3},{3,2},{4,5},{5,4},{6,7},{7,6},{8,9},{9,8},{10,11... | collective-permute-start | bytes 884744 | tf_op jit(solution)/shard_map/ppermute | solution.py:410
  21.2 9.8 %collective-permute-start.9 = (bf16[144,1024]{1,0:T(8,128)(2,1)S(1)}, bf16[144,1024]{1,0:T(8,128)(2,1)S(1)}, u32[]{:S(2)}, u32[]{:S(2)}) collective-permute-start(bf16[144,1024]{1,0:T(8,128)(2,1)S(1)} %join.3.refs_0_), channel_id=1, source_target_pairs={{0,16},{16,0},{1,17},{17,1},{2,18},{18,2},{3,19},{19,3},{4,20},{20... | collective-permute-start | bytes 884744 | tf_op jit(solution)/shard_map/ppermute | solution.py:410
  22.7 8.9 %collective-permute-start.11 = (bf16[144,1024]{1,0:T(8,128)(2,1)S(1)}, bf16[144,1024]{1,0:T(8,128)(2,1)S(1)}, u32[]{:S(2)}, u32[]{:S(2)}) collective-permute-start(bf16[144,1024]{1,0:T(8,128)(2,1)S(1)} %join.3.refs_0_), channel_id=1, source_target_pairs={{0,1},{1,0},{2,3},{3,2},{4,5},{5,4},{6,7},{7,6},{8,9},{9,8},{10,11... | collective-permute-start | bytes 884744 | tf_op jit(solution)/shard_map/ppermute | solution.py:410
  26.5 14.7 %collective-permute-start.4 = (bf16[72,1024]{1,0:T(8,128)(2,1)S(1)}, bf16[72,1024]{1,0:T(8,128)(2,1)S(1)}, u32[]{:S(2)}, u32[]{:S(2)}) collective-permute-start(bf16[72,1024]{1,0:T(8,128)(2,1)S(1)} %get-tuple-element.53), channel_id=1, source_target_pairs={{0,2},{2,0},{4,6},{6,4},{1,3},{3,1},{5,7},{7,5},{8,10},{10,8},{12,... | collective-permute-start | bytes 442376 | tf_op jit(solution)/shard_map/ppermute | solution.py:415
  28.9 12.3 %collective-permute-start.5 = (bf16[72,1024]{1,0:T(8,128)(2,1)S(1)}, bf16[72,1024]{1,0:T(8,128)(2,1)S(1)}, u32[]{:S(2)}, u32[]{:S(2)}) collective-permute-start(bf16[72,1024]{1,0:T(8,128)(2,1)S(1)} %get-tuple-element.54), channel_id=1, source_target_pairs={{0,4},{2,6},{4,0},{6,2},{1,5},{3,7},{5,1},{7,3},{8,12},{10,14},{12... | collective-permute-start | bytes 442376 | tf_op jit(solution)/shard_map/ppermute | solution.py:415
  31.0 8.5 %collective-permute-start.13 = (bf16[144,1024]{1,0:T(8,128)(2,1)S(1)}, bf16[144,1024]{1,0:T(8,128)(2,1)S(1)}, u32[]{:S(2)}, u32[]{:S(2)}) collective-permute-start(bf16[144,1024]{1,0:T(8,128)(2,1)S(1)} %relay.5.refs_1_), channel_id=1, source_target_pairs={{0,16},{16,0},{1,17},{17,1},{2,18},{18,2},{3,19},{19,3},{4,20},{20... | collective-permute-start | bytes 884744 | tf_op jit(solution)/shard_map/ppermute | solution.py:410
  31.6 11.2 %collective-permute-start.15 = (bf16[144,1024]{1,0:T(8,128)(2,1)S(1)}, bf16[144,1024]{1,0:T(8,128)(2,1)S(1)}, u32[]{:S(2)}, u32[]{:S(2)}) collective-permute-start(bf16[144,1024]{1,0:T(8,128)(2,1)S(1)} %relay.6.refs_1_.refs_0_), channel_id=1, source_target_pairs={{0,1},{1,0},{2,3},{3,2},{4,5},{5,4},{6,7},{7,6},{8,9},{9,8},{10,11... | collective-permute-start | bytes 884744 | tf_op jit(solution)/shard_map/ppermute | solution.py:410
  33.2 7.9 %collective-permute-start.12 = (bf16[72,1024]{1,0:T(8,128)(2,1)S(1)}, bf16[72,1024]{1,0:T(8,128)(2,1)S(1)}, u32[]{:S(2)}, u32[]{:S(2)}) collective-permute-start(bf16[72,1024]{1,0:T(8,128)(2,1)S(1)} %relay.7), channel_id=1, source_target_pairs={{0,6},{2,4},{4,2},{6,0},{1,7},{3,5},{5,3},{7,1},{8,14},{10,12},{12... | collective-permute-start | bytes 442376 | tf_op jit(solution)/shard_map/ppermute | solution.py:415
  41.3 7.7 %collective-permute-start.14 = (bf16[144,1024]{1,0:T(8,128)(2,1)S(1)}, bf16[144,1024]{1,0:T(8,128)(2,1)S(1)}, u32[]{:S(2)}, u32[]{:S(2)}) collective-permute-start(bf16[144,1024]{1,0:T(8,128)(2,1)S(1)} %get-tuple-element.74), channel_id=1, source_target_pairs={{0,1},{1,0},{2,3},{3,2},{4,5},{5,4},{6,7},{7,6},{8,9},{9,8},{10,11... | collective-permute-start | bytes 884744 | tf_op jit(solution)/shard_map/ppermute | solution.py:410
  45.1 2.8 %collective-permute-start.16 = (bf16[512,1024]{1,0:T(8,128)(2,1)S(1)}, bf16[512,1024]{1,0:T(8,128)(2,1)S(1)}, u32[]{:S(2)}, u32[]{:S(2)}) collective-permute-start(bf16[512,1024]{1,0:T(8,128)(2,1)S(1)} %get-tuple-element.78), channel_id=1, source_target_pairs={{0,8},{8,0},{1,9},{9,1},{2,10},{10,2},{3,11},{11,3},{4,12},{12,4},... | collective-permute-start | bytes 3145736 | tf_op jit(solution)/shard_map/ppermute | solution.py:410
  47.3 2.8 %collective-permute-start.17 = (bf16[512,1024]{1,0:T(8,128)(2,1)S(1)}, bf16[512,1024]{1,0:T(8,128)(2,1)S(1)}, u32[]{:S(2)}, u32[]{:S(2)}) collective-permute-start(bf16[512,1024]{1,0:T(8,128)(2,1)S(1)} %get-tuple-element.81), channel_id=1, source_target_pairs={{0,8},{8,0},{1,9},{9,1},{2,10},{10,2},{3,11},{11,3},{4,12},{12,4},... | collective-permute-start | bytes 3145736 | tf_op jit(solution)/shard_map/ppermute | solution.py:410

commit v22 on v16

--- a/solution.py
+++ b/solution.py
@@ -13,6 +13,7 @@
 WIDE = 1024
 STRIP = 512
 SLICE = 256
+SENT = (0, 2, 1, 3)
 MIB = 1024 * 1024
 LARGE = pltpu.CompilerParams(vmem_limit_bytes=16 * MIB)
 SMALL = pltpu.CompilerParams(vmem_limit_bytes=12 * MIB)
@@ -371,7 +372,7 @@
 
 
 def split_kernel(*refs):
-    blocks = [r[...].astype(F32) for r in refs[:EXPERTS]]
+    blocks = [refs[SENT.index(k)][...].astype(F32) for k in range(EXPERTS)]
     refs[-2][...] = jnp.concatenate([b[:CAP] for b in blocks], axis=0).astype(BF16)
     refs[-1][...] = jnp.concatenate([b[CAP:] for b in blocks], axis=0).astype(BF16)
 
@@ -385,7 +386,7 @@
         compiler_params=SMALL,
         cost_estimate=CHEAP,
         name="split",
-    )(*blocks, *earlier)
+    )(*[blocks[k] for k in SENT], *earlier)
 
 
 def unpack_kernel(placer_ref, mine_ref, got_ref, *refs):

time: 49.7 us -> 49.6 us (level)
  transfers between devices with their start and end apart: 18 -> 18, of which waited for: 3 -> 4; matrix products, arithmetic and copies ran while one was open for 0% -> 0% of each run, Pallas kernels for 40% -> 40%
where the time goes in v22:
time: 49.6 us; the launch traced here: 49.4 us
  starting transfers between devices  24.8 us (50%)
  Pallas kernels  22.3 us (45%)
  waiting for transfers between devices  1.31 us (3%)
  between operations  0.98 us (2%)
    ppermute x9, starting transfers between devices, across_planes(): lax.ppermute(blocks[k], 'arch', [(i, i ^ k) for i in range(EXPERTS)])  14.7 us
    ppermute x9, starting transfers between devices, swap(): return lax.ppermute(value, axis, [(0, 1), (1, 0)])  10.1 us
    pallas_call x4, Pallas kernels, forward(): pl.pallas_call(functools.partial(forward_kernel, n, fetch, down, pair, le...  7.62 us
    pallas_call x2, Pallas kernels, backward(): pl.pallas_call(functools.partial(backward_kernel, first), out_shape=[jax....  4.44 us
    pallas_call x1, Pallas kernels, flip(): pl.pallas_call(flip_kernel, out_shape=[pltpu.VMEM(value.shape, value.dtyp...  2.88 us
    pallas_call x2, Pallas kernels, finish(): pl.pallas_call(functools.partial(finish_kernel, spans, more, len(earlier)...  2.21 us
    pallas_call x1, Pallas kernels, slopes(): pl.pallas_call(functools.partial(slopes_kernel, n), out_shape=[jax.ShapeD...  2.19 us
    pallas_call x1, Pallas kernels, pack(): pl.pallas_call(pack_kernel, out_shape=[jax.ShapeDtypeStruct((EXPERTS * CA...  1.46 us
  transfers between devices with their start and end apart: 18, of which 4 were waited for; matrix products, arithmetic and copies ran while one was open for 0% of the time, Pallas kernels for 40%

profile of v22, /device:TPU:0, one launch (start us, length us, event | category | flops | bytes accessed | tf_op | source)
XLA Modules:
  0.0 49.4 jit_solution(18057021729802978162)
XLA Ops:
  0.6 1.5 %pack.1 = (bf16[144,128]{1,0:T(8,128)(2,1)S(1)}, bf16[36,1024]{1,0:T(8,128)(2,1)S(1)}, bf16[36,1024]{1,0:T(8,128)(2,1)S(1)}, bf16[36,1024]{1,0:T(8,128)(2,1)S(1)...) custom-call(s32[1]{0:T(128)} %bitcast.plane_ref, ...), custom_call_target="tpu_custom_call" | custom-call | tf_op jit(solution)/shard_map/pack/pallas_call | solution.py:80
  2.1 5.1 %collective-permute-start = (bf16[36,1024]{1,0:T(8,128)(2,1)S(1)}, bf16[36,1024]{1,0:T(8,128)(2,1)S(1)}, u32[]{:S(2)}, u32[]{:S(2)}) collective-permute-start(bf16[36,1024]{1,0:T(8,128)(2,1)S(1)} %get-tuple-element.45), channel_id=1, source_target_pairs={{0,6},{2,4},{4,2},{6,0},{1,7},{3,5},{5,3},{7,1},{8,14},{10,12},{12... | collective-permute-start | bytes 221192 | tf_op jit(solution)/shard_map/ppermute | solution.py:416
  7.2 0.6 %collective-permute-start.2 = (bf16[36,1024]{1,0:T(8,128)(2,1)S(1)}, bf16[36,1024]{1,0:T(8,128)(2,1)S(1)}, u32[]{:S(2)}, u32[]{:S(2)}) collective-permute-start(bf16[36,1024]{1,0:T(8,128)(2,1)S(1)} %get-tuple-element.47), channel_id=1, source_target_pairs={{0,2},{2,0},{4,6},{6,4},{1,3},{3,1},{5,7},{7,5},{8,10},{10,8},{12,... | collective-permute-start | bytes 221192 | tf_op jit(solution)/shard_map/ppermute | solution.py:416
  7.9 2.9 %flip.1 = (bf16[2048,1024]{1,0:T(8,128)(2,1)S(1)}, bf16[1024,2048]{1,0:T(8,128)(2,1)S(1)}) custom-call(bf16[2048,1024]{1,0:T(8,128)(2,1)} %source_ref), custom_call_target="tpu_custom_call" | custom-call | tf_op jit(solution)/shard_map/flip/pallas_call | solution.py:159
  10.8 3.8 %collective-permute-start.7 = (bf16[36,1024]{1,0:T(8,128)(2,1)S(1)}, bf16[36,1024]{1,0:T(8,128)(2,1)S(1)}, u32[]{:S(2)}, u32[]{:S(2)}) collective-permute-start(bf16[36,1024]{1,0:T(8,128)(2,1)S(1)} %get-tuple-element.62), channel_id=1, source_target_pairs={{0,6},{2,4},{4,2},{6,0},{1,7},{3,5},{5,3},{7,1},{8,14},{10,12},{12... | collective-permute-start | bytes 221192 | tf_op jit(solution)/shard_map/ppermute | solution.py:416
  14.6 0.6 %collective-permute-start.9 = (bf16[36,1024]{1,0:T(8,128)(2,1)S(1)}, bf16[36,1024]{1,0:T(8,128)(2,1)S(1)}, u32[]{:S(2)}, u32[]{:S(2)}) collective-permute-start(bf16[36,1024]{1,0:T(8,128)(2,1)S(1)} %get-tuple-element.64), channel_id=1, source_target_pairs={{0,2},{2,0},{4,6},{6,4},{1,3},{3,1},{5,7},{7,5},{8,10},{10,8},{12,... | collective-permute-start | bytes 221192 | tf_op jit(solution)/shard_map/ppermute | solution.py:416
  15.3 1.7 %collective-permute-start.3 = (bf16[144,1024]{1,0:T(8,128)(2,1)S(1)}, bf16[144,1024]{1,0:T(8,128)(2,1)S(1)}, u32[]{:S(2)}, u32[]{:S(2)}) collective-permute-start(bf16[144,1024]{1,0:T(8,128)(2,1)S(1)} %join.2.refs_0_.refs_4_), channel_id=1, source_target_pairs={{0,1},{1,0},{2,3},{3,2},{4,5},{5,4},{6,7},{7,6},{8,9},{9,8},{10,11... | collective-permute-start | bytes 884744 | tf_op jit(solution)/shard_map/ppermute | solution.py:411
  17.0 1.5 %collective-permute-start.12 = (bf16[144,1024]{1,0:T(8,128)(2,1)S(1)}, bf16[144,1024]{1,0:T(8,128)(2,1)S(1)}, u32[]{:S(2)}, u32[]{:S(2)}) collective-permute-start(bf16[144,1024]{1,0:T(8,128)(2,1)S(1)} %join.2.refs_0_.refs_4_), channel_id=1, source_target_pairs={{0,16},{16,0},{1,17},{17,1},{2,18},{18,2},{3,19},{19,3},{4,20},{20... | collective-permute-start | bytes 884744 | tf_op jit(solution)/shard_map/ppermute | solution.py:411
  18.5 2.2 %forward_down.2 = (bf16[144,2048]{1,0:T(8,128)(2,1)S(1)}, bf16[144,2048]{1,0:T(8,128)(2,1)S(1)}, bf16[144,1024]{1,0:T(8,128)(2,1)S(1)}) custom-call(bf16[144,1024]{1,0:T(8,128)(2,1)S(1)} %join.2.refs_0_.refs_4_, bf16[1024,2048]{1,0:T(8,128)(2,1)S(1)} %copy-done, bf16[1024,2048]{1,0:T(8,128)(2,1)S(1)} %copy-done.1, ...), custom_call_target="tpu_custom_call" | custom-call | tf_op jit(solution)/shard_map/forward_down/pallas_call | solution.py:239
  20.8 0.3 collective-permute-done.8.refs_2_
  21.2 1.6 %collective-permute-start.11 = (bf16[144,1024]{1,0:T(8,128)(2,1)S(1)}, bf16[144,1024]{1,0:T(8,128)(2,1)S(1)}, u32[]{:S(2)}, u32[]{:S(2)}) collective-permute-start(bf16[144,1024]{1,0:T(8,128)(2,1)S(1)} %join.3.refs_0_), channel_id=1, source_target_pairs={{0,16},{16,0},{1,17},{17,1},{2,18},{18,2},{3,19},{19,3},{4,20},{20... | collective-permute-start | bytes 884744 | tf_op jit(solution)/shard_map/ppermute | solution.py:411
  22.7 1.5 %collective-permute-start.10 = (bf16[144,1024]{1,0:T(8,128)(2,1)S(1)}, bf16[144,1024]{1,0:T(8,128)(2,1)S(1)}, u32[]{:S(2)}, u32[]{:S(2)}) collective-permute-start(bf16[144,1024]{1,0:T(8,128)(2,1)S(1)} %join.3.refs_0_), channel_id=1, source_target_pairs={{0,1},{1,0},{2,3},{3,2},{4,5},{5,4},{6,7},{7,6},{8,9},{9,8},{10,11... | collective-permute-start | bytes 884744 | tf_op jit(solution)/shard_map/ppermute | solution.py:411
  24.2 2.2 %forward_down.3 = (bf16[144,2048]{1,0:T(8,128)(2,1)S(1)}, bf16[144,2048]{1,0:T(8,128)(2,1)S(1)}, bf16[72,1024]{1,0:T(8,128)(2,1)S(1)}, bf16[72,1024]{1,0:T(8,128...) custom-call(bf16[144,1024]{1,0:T(8,128)(2,1)S(1)} %collective-permute-done.3.refs_0_.refs_1_.refs_5_, ...), custom_call_target="tpu_custom_call" | custom-call | tf_op jit(solution)/shard_map/forward_down/pallas_call | solution.py:239
  26.5 1.7 %collective-permute-start.4 = (bf16[72,1024]{1,0:T(8,128)(2,1)S(1)}, bf16[72,1024]{1,0:T(8,128)(2,1)S(1)}, u32[]{:S(2)}, u32[]{:S(2)}) collective-permute-start(bf16[72,1024]{1,0:T(8,128)(2,1)S(1)} %get-tuple-element.53), channel_id=1, source_target_pairs={{0,4},{2,6},{4,0},{6,2},{1,5},{3,7},{5,1},{7,3},{8,12},{10,14},{12... | collective-permute-start | bytes 442376 | tf_op jit(solution)/shard_map/ppermute | solution.py:416
  28.2 1.6 %collective-permute-start.5 = (bf16[72,1024]{1,0:T(8,128)(2,1)S(1)}, bf16[72,1024]{1,0:T(8,128)(2,1)S(1)}, u32[]{:S(2)}, u32[]{:S(2)}) collective-permute-start(bf16[72,1024]{1,0:T(8,128)(2,1)S(1)} %get-tuple-element.54), channel_id=1, source_target_pairs={{0,2},{2,0},{4,6},{6,4},{1,3},{3,1},{5,7},{7,5},{8,10},{10,8},{12,... | collective-permute-start | bytes 442376 | tf_op jit(solution)/shard_map/ppermute | solution.py:416
  29.8 1.1 %collective-permute-start.6 = (bf16[72,1024]{1,0:T(8,128)(2,1)S(1)}, bf16[72,1024]{1,0:T(8,128)(2,1)S(1)}, u32[]{:S(2)}, u32[]{:S(2)}) collective-permute-start(bf16[72,1024]{1,0:T(8,128)(2,1)S(1)} %get-tuple-element.55), channel_id=1, source_target_pairs={{0,6},{2,4},{4,2},{6,0},{1,7},{3,5},{5,3},{7,1},{8,14},{10,12},{12... | collective-permute-start | bytes 442376 | tf_op jit(solution)/shard_map/ppermute | solution.py:416
  31.0 0.9 %collective-permute-start.13 = (bf16[144,1024]{1,0:T(8,128)(2,1)S(1)}, bf16[144,1024]{1,0:T(8,128)(2,1)S(1)}, u32[]{:S(2)}, u32[]{:S(2)}) collective-permute-start(bf16[144,1024]{1,0:T(8,128)(2,1)S(1)} %relay.4.refs_1_), channel_id=1, source_target_pairs={{0,16},{16,0},{1,17},{17,1},{2,18},{18,2},{3,19},{19,3},{4,20},{20... | collective-permute-start | bytes 884744 | tf_op jit(solution)/shard_map/ppermute | solution.py:411
  31.9 2.0 %collective-permute-start.15 = (bf16[144,1024]{1,0:T(8,128)(2,1)S(1)}, bf16[144,1024]{1,0:T(8,128)(2,1)S(1)}, u32[]{:S(2)}, u32[]{:S(2)}) collective-permute-start(bf16[144,1024]{1,0:T(8,128)(2,1)S(1)} %relay.5.refs_0_), channel_id=1, source_target_pairs={{0,1},{1,0},{2,3},{3,2},{4,5},{5,4},{6,7},{7,6},{8,9},{9,8},{10,11... | collective-permute-start | bytes 884744 | tf_op jit(solution)/shard_map/ppermute | solution.py:411
  33.9 1.6 %forward.2 = (bf16[144,2048]{1,0:T(8,128)(2,1)S(1)}, bf16[144,2048]{1,0:T(8,128)(2,1)S(1)}) custom-call(bf16[144,1024]{1,0:T(8,128)(2,1)S(1)} %relay.5.refs_0_, bf16[144,1024]{1,0:T(8,128)(2,1)S(1)} %collective-permute-done.12._.refs_1_.refs_2_.refs_6_, bf16[1024,2048]{1,0:T(8,128)(2,1)S(1)} %copy-done, bf16[1024,2048]{1,0:T(8,128)(2,1)S(1)} %copy-done.1), custom_call_target="tpu_custom_call" | custom-call | flops 20000000000 | tf_op jit(solution)/shard_map/forward/pallas_call | solution.py:239
  35.5 2.2 %slopes.1 = (bf16[432,2048]{1,0:T(8,128)(2,1)S(1)}, bf16[432,2048]{1,0:T(8,128)(2,1)S(1)}) custom-call(bf16[144,1024]{1,0:T(8,128)(2,1)S(1)} %join.3.refs_0_, bf16[144,1024]{1,0:T(8,128)(2,1)S(1)} %collective-permute-done.10.refs_2_.refs_1_, bf16[144,1024]{1,0:T(8,128)(2,1)S(1)} %collective-permute-done.11.refs_2_.refs_0_, ...), custom_call_target="tpu_custom_call" | custom-call | tf_op jit(solution)/shard_map/slopes/pallas_call | solution.py:298
  37.7 0.8 %collective-permute-done.13.refs_1_.refs_3_.refs_7_ = bf16[144,1024]{1,0:T(8,128)(2,1)S(1)} collective-permute-done((bf16[144,1024]{1,0:T(8,128)(2,1)S(1)}, bf16[144,1024]{1,0:T(8,128)(2,1)S(1)}, u32[]{:S(2)}, u32[]{:S(2)}) %collective-permute-start.13) | collective-permute-done | bytes 294944 | tf_op jit(solution)/shard_map/ppermute | solution.py:411
  38.5 1.6 %forward.3 = (bf16[144,2048]{1,0:T(8,128)(2,1)S(1)}, bf16[144,2048]{1,0:T(8,128)(2,1)S(1)}) custom-call(bf16[432,2048]{1,0:T(8,128)(2,1)S(1)} %get-tuple-element.71.refs_0_.dg_ref, bf16[144,1024]{1,0:T(8,128)(2,1)S(1)} %collective-permute-done.13.refs_1_.refs_3_.refs_7_, bf16[1024,2048]{1,0:T(8,128)(2,1)S(1)} %copy-done, bf16[1024,2048]{1,0:T(8,128)(2,1)S(1)} %copy-done.1), custom_call_target="tpu_custom_call" | custom-call | tf_op jit(solution)/shard_map/forward/pallas_call | solution.py:239
  40.1 0.1 split.1
  40.2 0.3 collective-permute-start.14
  40.5 0.2 turn.1.xt_ref
  40.7 2.3 %backward.2 = (bf16[512,1024]{1,0:T(8,128)(2,1)S(1)}, bf16[512,1024]{1,0:T(8,128)(2,1)S(1)}) custom-call(bf16[512,576]{1,0:T(8,128)(2,1)S(1)} %turn.1.xt_ref, bf16[144,1024]{1,0:T(8,128)(2,1)S(1)} %collective-permute-done.15.g_ref, bf16[144,2048]{1,0:T(8,128)(2,1)S(1)} %get-tuple-element.72.refs_4_.act_ref, ...), custom_call_target="tpu_custom_call" | custom-call | flops 20000000000 | tf_op jit(solution)/shard_map/backward/pallas_call | solution.py:325
  43.2 2.1 %backward.3 = (bf16[512,1024]{1,0:T(8,128)(2,1)S(1)}, bf16[512,1024]{1,0:T(8,128)(2,1)S(1)}) custom-call(bf16[512,576]{1,0:T(8,128)(2,1)S(1)} %turn.1.xt_ref, bf16[144,1024]{1,0:T(8,128)(2,1)S(1)} %collective-permute-done.15.g_ref, bf16[144,2048]{1,0:T(8,128)(2,1)S(1)} %get-tuple-element.72.refs_4_.act_ref, ...), custom_call_target="tpu_custom_call" | custom-call | flops 20000000000 | tf_op jit(solution)/shard_map/backward/pallas_call | solution.py:325
  45.3 0.6 %collective-permute-start.17 = (bf16[512,1024]{1,0:T(8,128)(2,1)S(1)}, bf16[512,1024]{1,0:T(8,128)(2,1)S(1)}, u32[]{:S(2)}, u32[]{:S(2)}) collective-permute-start(bf16[512,1024]{1,0:T(8,128)(2,1)S(1)} %get-tuple-element.81), channel_id=1, source_target_pairs={{0,8},{8,0},{1,9},{9,1},{2,10},{10,2},{3,11},{11,3},{4,12},{12,4},... | collective-permute-start | bytes 3145736 | tf_op jit(solution)/shard_map/ppermute | solution.py:411
  45.8 1.1 %finish.2 = (bf16[256,2048]{1,0:T(8,128)(2,1)}, bf16[256,2048]{1,0:T(8,128)(2,1)}) custom-call(bf16[512,1024]{1,0:T(8,128)(2,1)S(1)} %get-tuple-element.77.refs_0_, bf16[512,1024]{1,0:T(8,128)(2,1)S(1)} %collective-permute-done.16.refs_1_), custom_call_target="tpu_custom_call" | custom-call | tf_op jit(solution)/shard_map/finish/pallas_call | solution.py:361
  47.0 1.0 %unpack.1 = bf16[128,1024]{1,0:T(8,128)(2,1)} custom-call(bf16[144,128]{1,0:T(8,128)(2,1)S(1)} %get-tuple-element.44.placer_ref, bf16[144,1024]{1,0:T(8,128)(2,1)S(1)} %get-tuple-element.73.mine_ref, bf16[144,1024]{1,0:T(8,128)(2,1)S(1)} %collective-permute-done.14.got_ref, bf16[256,2048]{1,0:T(8,128)(2,1)} %get-tuple-element.79.refs_0_.refs_2_), custom_call_target="tpu_custom_call" | custom-call | flops 20000000000 | tf_op jit(solution)/shard_map/unpack/pallas_call | solution.py:400
  48.1 0.1 collective-permute-done.17.refs_1_
  48.1 1.1 %finish.3 = (bf16[256,2048]{1,0:T(8,128)(2,1)}, bf16[256,2048]{1,0:T(8,128)(2,1)}) custom-call(bf16[512,1024]{1,0:T(8,128)(2,1)S(1)} %get-tuple-element.80.refs_0_, bf16[512,1024]{1,0:T(8,128)(2,1)S(1)} %collective-permute-done.17.refs_1_, bf16[256,2048]{1,0:T(8,128)(2,1)} %get-tuple-element.79.refs_0_.refs_2_, ...), custom_call_target="tpu_custom_call", output_to_operand_aliasing={{0}: (2, {}), {1}: (3, {})} | custom-call | tf_op jit(solution)/shard_map/finish/pallas_call | solution.py:361
  (28 shorter events, 0.3 us)
Async XLA Ops:
  2.1 12.5 %collective-permute-start = (bf16[36,1024]{1,0:T(8,128)(2,1)S(1)}, bf16[36,1024]{1,0:T(8,128)(2,1)S(1)}, u32[]{:S(2)}, u32[]{:S(2)}) collective-permute-start(bf16[36,1024]{1,0:T(8,128)(2,1)S(1)} %get-tuple-element.45), channel_id=1, source_target_pairs={{0,6},{2,4},{4,2},{6,0},{1,7},{3,5},{5,3},{7,1},{8,14},{10,12},{12... | collective-permute-start | bytes 221192 | tf_op jit(solution)/shard_map/ppermute | solution.py:416
  7.2 8.0 %collective-permute-start.1 = (bf16[36,1024]{1,0:T(8,128)(2,1)S(1)}, bf16[36,1024]{1,0:T(8,128)(2,1)S(1)}, u32[]{:S(2)}, u32[]{:S(2)}) collective-permute-start(bf16[36,1024]{1,0:T(8,128)(2,1)S(1)} %get-tuple-element.46), channel_id=1, source_target_pairs={{0,4},{2,6},{4,0},{6,2},{1,5},{3,7},{5,1},{7,3},{8,12},{10,14},{12... | collective-permute-start | bytes 221192 | tf_op jit(solution)/shard_map/ppermute | solution.py:416
  7.2 8.0 %collective-permute-start.2 = (bf16[36,1024]{1,0:T(8,128)(2,1)S(1)}, bf16[36,1024]{1,0:T(8,128)(2,1)S(1)}, u32[]{:S(2)}, u32[]{:S(2)}) collective-permute-start(bf16[36,1024]{1,0:T(8,128)(2,1)S(1)} %get-tuple-element.47), channel_id=1, source_target_pairs={{0,2},{2,0},{4,6},{6,4},{1,3},{3,1},{5,7},{7,5},{8,10},{10,8},{12,... | collective-permute-start | bytes 221192 | tf_op jit(solution)/shard_map/ppermute | solution.py:416
  7.9 10.7 %copy-start = (bf16[1024,2048]{1,0:T(8,128)(2,1)S(1)}, bf16[1024,2048]{1,0:T(8,128)(2,1)}, u32[]{:S(2)}) copy-start(bf16[1024,2048]{1,0:T(8,128)(2,1)} %refs_2_.7) | copy-start | bytes 12582916
  7.9 10.7 %copy-start.1 = (bf16[1024,2048]{1,0:T(8,128)(2,1)S(1)}, bf16[1024,2048]{1,0:T(8,128)(2,1)}, u32[]{:S(2)}) copy-start(bf16[1024,2048]{1,0:T(8,128)(2,1)} %refs_3_.3) | copy-start | bytes 12582916
  10.8 10.0 %collective-permute-start.7 = (bf16[36,1024]{1,0:T(8,128)(2,1)S(1)}, bf16[36,1024]{1,0:T(8,128)(2,1)S(1)}, u32[]{:S(2)}, u32[]{:S(2)}) collective-permute-start(bf16[36,1024]{1,0:T(8,128)(2,1)S(1)} %get-tuple-element.62), channel_id=1, source_target_pairs={{0,6},{2,4},{4,2},{6,0},{1,7},{3,5},{5,3},{7,1},{8,14},{10,12},{12... | collective-permute-start | bytes 221192 | tf_op jit(solution)/shard_map/ppermute | solution.py:416
  14.6 6.5 %collective-permute-start.8 = (bf16[36,1024]{1,0:T(8,128)(2,1)S(1)}, bf16[36,1024]{1,0:T(8,128)(2,1)S(1)}, u32[]{:S(2)}, u32[]{:S(2)}) collective-permute-start(bf16[36,1024]{1,0:T(8,128)(2,1)S(1)} %get-tuple-element.63), channel_id=1, source_target_pairs={{0,4},{2,6},{4,0},{6,2},{1,5},{3,7},{5,1},{7,3},{8,12},{10,14},{12... | collective-permute-start | bytes 221192 | tf_op jit(solution)/shard_map/ppermute | solution.py:416
  14.6 6.5 %collective-permute-start.9 = (bf16[36,1024]{1,0:T(8,128)(2,1)S(1)}, bf16[36,1024]{1,0:T(8,128)(2,1)S(1)}, u32[]{:S(2)}, u32[]{:S(2)}) collective-permute-start(bf16[36,1024]{1,0:T(8,128)(2,1)S(1)} %get-tuple-element.64), channel_id=1, source_target_pairs={{0,2},{2,0},{4,6},{6,4},{1,3},{3,1},{5,7},{7,5},{8,10},{10,8},{12,... | collective-permute-start | bytes 221192 | tf_op jit(solution)/shard_map/ppermute | solution.py:416
  15.3 8.9 %collective-permute-start.3 = (bf16[144,1024]{1,0:T(8,128)(2,1)S(1)}, bf16[144,1024]{1,0:T(8,128)(2,1)S(1)}, u32[]{:S(2)}, u32[]{:S(2)}) collective-permute-start(bf16[144,1024]{1,0:T(8,128)(2,1)S(1)} %join.2.refs_0_.refs_4_), channel_id=1, source_target_pairs={{0,1},{1,0},{2,3},{3,2},{4,5},{5,4},{6,7},{7,6},{8,9},{9,8},{10,11... | collective-permute-start | bytes 884744 | tf_op jit(solution)/shard_map/ppermute | solution.py:411
  17.0 12.8 %collective-permute-start.12 = (bf16[144,1024]{1,0:T(8,128)(2,1)S(1)}, bf16[144,1024]{1,0:T(8,128)(2,1)S(1)}, u32[]{:S(2)}, u32[]{:S(2)}) collective-permute-start(bf16[144,1024]{1,0:T(8,128)(2,1)S(1)} %join.2.refs_0_.refs_4_), channel_id=1, source_target_pairs={{0,16},{16,0},{1,17},{17,1},{2,18},{18,2},{3,19},{19,3},{4,20},{20... | collective-permute-start | bytes 884744 | tf_op jit(solution)/shard_map/ppermute | solution.py:411
  21.2 9.8 %collective-permute-start.11 = (bf16[144,1024]{1,0:T(8,128)(2,1)S(1)}, bf16[144,1024]{1,0:T(8,128)(2,1)S(1)}, u32[]{:S(2)}, u32[]{:S(2)}) collective-permute-start(bf16[144,1024]{1,0:T(8,128)(2,1)S(1)} %join.3.refs_0_), channel_id=1, source_target_pairs={{0,16},{16,0},{1,17},{17,1},{2,18},{18,2},{3,19},{19,3},{4,20},{20... | collective-permute-start | bytes 884744 | tf_op jit(solution)/shard_map/ppermute | solution.py:411
  22.7 9.2 %collective-permute-start.10 = (bf16[144,1024]{1,0:T(8,128)(2,1)S(1)}, bf16[144,1024]{1,0:T(8,128)(2,1)S(1)}, u32[]{:S(2)}, u32[]{:S(2)}) collective-permute-start(bf16[144,1024]{1,0:T(8,128)(2,1)S(1)} %join.3.refs_0_), channel_id=1, source_target_pairs={{0,1},{1,0},{2,3},{3,2},{4,5},{5,4},{6,7},{7,6},{8,9},{9,8},{10,11... | collective-permute-start | bytes 884744 | tf_op jit(solution)/shard_map/ppermute | solution.py:411
  26.5 13.6 %collective-permute-start.4 = (bf16[72,1024]{1,0:T(8,128)(2,1)S(1)}, bf16[72,1024]{1,0:T(8,128)(2,1)S(1)}, u32[]{:S(2)}, u32[]{:S(2)}) collective-permute-start(bf16[72,1024]{1,0:T(8,128)(2,1)S(1)} %get-tuple-element.53), channel_id=1, source_target_pairs={{0,4},{2,6},{4,0},{6,2},{1,5},{3,7},{5,1},{7,3},{8,12},{10,14},{12... | collective-permute-start | bytes 442376 | tf_op jit(solution)/shard_map/ppermute | solution.py:416
  28.2 11.9 %collective-permute-start.5 = (bf16[72,1024]{1,0:T(8,128)(2,1)S(1)}, bf16[72,1024]{1,0:T(8,128)(2,1)S(1)}, u32[]{:S(2)}, u32[]{:S(2)}) collective-permute-start(bf16[72,1024]{1,0:T(8,128)(2,1)S(1)} %get-tuple-element.54), channel_id=1, source_target_pairs={{0,2},{2,0},{4,6},{6,4},{1,3},{3,1},{5,7},{7,5},{8,10},{10,8},{12,... | collective-permute-start | bytes 442376 | tf_op jit(solution)/shard_map/ppermute | solution.py:416
  29.8 10.3 %collective-permute-start.6 = (bf16[72,1024]{1,0:T(8,128)(2,1)S(1)}, bf16[72,1024]{1,0:T(8,128)(2,1)S(1)}, u32[]{:S(2)}, u32[]{:S(2)}) collective-permute-start(bf16[72,1024]{1,0:T(8,128)(2,1)S(1)} %get-tuple-element.55), channel_id=1, source_target_pairs={{0,6},{2,4},{4,2},{6,0},{1,7},{3,5},{5,3},{7,1},{8,14},{10,12},{12... | collective-permute-start | bytes 442376 | tf_op jit(solution)/shard_map/ppermute | solution.py:416
  31.0 7.6 %collective-permute-start.13 = (bf16[144,1024]{1,0:T(8,128)(2,1)S(1)}, bf16[144,1024]{1,0:T(8,128)(2,1)S(1)}, u32[]{:S(2)}, u32[]{:S(2)}) collective-permute-start(bf16[144,1024]{1,0:T(8,128)(2,1)S(1)} %relay.4.refs_1_), channel_id=1, source_target_pairs={{0,16},{16,0},{1,17},{17,1},{2,18},{18,2},{3,19},{19,3},{4,20},{20... | collective-permute-start | bytes 884744 | tf_op jit(solution)/shard_map/ppermute | solution.py:411
  31.9 8.8 %collective-permute-start.15 = (bf16[144,1024]{1,0:T(8,128)(2,1)S(1)}, bf16[144,1024]{1,0:T(8,128)(2,1)S(1)}, u32[]{:S(2)}, u32[]{:S(2)}) collective-permute-start(bf16[144,1024]{1,0:T(8,128)(2,1)S(1)} %relay.5.refs_0_), channel_id=1, source_target_pairs={{0,1},{1,0},{2,3},{3,2},{4,5},{5,4},{6,7},{7,6},{8,9},{9,8},{10,11... | collective-permute-start | bytes 884744 | tf_op jit(solution)/shard_map/ppermute | solution.py:411
  40.2 6.8 %collective-permute-start.14 = (bf16[144,1024]{1,0:T(8,128)(2,1)S(1)}, bf16[144,1024]{1,0:T(8,128)(2,1)S(1)}, u32[]{:S(2)}, u32[]{:S(2)}) collective-permute-start(bf16[144,1024]{1,0:T(8,128)(2,1)S(1)} %get-tuple-element.74), channel_id=1, source_target_pairs={{0,1},{1,0},{2,3},{3,2},{4,5},{5,4},{6,7},{7,6},{8,9},{9,8},{10,11... | collective-permute-start | bytes 884744 | tf_op jit(solution)/shard_map/ppermute | solution.py:411
  43.1 2.8 %collective-permute-start.16 = (bf16[512,1024]{1,0:T(8,128)(2,1)S(1)}, bf16[512,1024]{1,0:T(8,128)(2,1)S(1)}, u32[]{:S(2)}, u32[]{:S(2)}) collective-permute-start(bf16[512,1024]{1,0:T(8,128)(2,1)S(1)} %get-tuple-element.78), channel_id=1, source_target_pairs={{0,8},{8,0},{1,9},{9,1},{2,10},{10,2},{3,11},{11,3},{4,12},{12,4},... | collective-permute-start | bytes 3145736 | tf_op jit(solution)/shard_map/ppermute | solution.py:411
  45.3 2.8 %collective-permute-start.17 = (bf16[512,1024]{1,0:T(8,128)(2,1)S(1)}, bf16[512,1024]{1,0:T(8,128)(2,1)S(1)}, u32[]{:S(2)}, u32[]{:S(2)}) collective-permute-start(bf16[512,1024]{1,0:T(8,128)(2,1)S(1)} %get-tuple-element.81), channel_id=1, source_target_pairs={{0,8},{8,0},{1,9},{9,1},{2,10},{10,2},{3,11},{11,3},{4,12},{12,4},... | collective-permute-start | bytes 3145736 | tf_op jit(solution)/shard_map/ppermute | solution.py:411

commit v23 on v22

--- a/solution.py
+++ b/solution.py
@@ -13,7 +13,7 @@
 WIDE = 1024
 STRIP = 512
 SLICE = 256
-SENT = (0, 2, 1, 3)
+SENT = (0, 2, 3, 1)
 MIB = 1024 * 1024
 LARGE = pltpu.CompilerParams(vmem_limit_bytes=16 * MIB)
 SMALL = pltpu.CompilerParams(vmem_limit_bytes=12 * MIB)

time: 49.6 us -> 50.2 us (1.012)
  waiting for transfers between devices: 1.31 us -> 2.88 us
  starting transfers between devices: 24.8 us -> 23.6 us
    ppermute x9, waiting for transfers between devices: 0.98 us -> 2.54 us  [swap(): return lax.ppermute(value, axis, [(0, 1), (1, 0)])]
    ppermute x9, starting transfers between devices: 14.7 us -> 13.8 us  [across_planes(): lax.ppermute(blocks[k], 'arch', [(i, i ^ k) for i in range(EXPERTS)])]
where the time goes in v23:
time: 50.2 us; the launch traced here: 49.8 us
  starting transfers between devices  23.6 us (47%)
  Pallas kernels  22.3 us (44%)
  waiting for transfers between devices  2.88 us (6%)
  between operations  0.98 us (2%)
    ppermute x9, starting transfers between devices, across_planes(): lax.ppermute(blocks[k], 'arch', [(i, i ^ k) for i in range(EXPERTS)])  13.8 us
    ppermute x9, starting transfers between devices, swap(): return lax.ppermute(value, axis, [(0, 1), (1, 0)])  9.87 us
    pallas_call x4, Pallas kernels, forward(): pl.pallas_call(functools.partial(forward_kernel, n, fetch, down, pair, le...  7.62 us
    pallas_call x2, Pallas kernels, backward(): pl.pallas_call(functools.partial(backward_kernel, first), out_shape=[jax....  4.44 us
    pallas_call x1, Pallas kernels, flip(): pl.pallas_call(flip_kernel, out_shape=[pltpu.VMEM(value.shape, value.dtyp...  2.88 us
    ppermute x9, waiting for transfers between devices, swap(): return lax.ppermute(value, axis, [(0, 1), (1, 0)])  2.54 us
    pallas_call x2, Pallas kernels, finish(): pl.pallas_call(functools.partial(finish_kernel, spans, more, len(earlier)...  2.21 us
    pallas_call x1, Pallas kernels, slopes(): pl.pallas_call(functools.partial(slopes_kernel, n), out_shape=[jax.ShapeD...  2.19 us
  transfers between devices with their start and end apart: 18, of which 4 were waited for; matrix products, arithmetic and copies ran while one was open for 0% of the time, Pallas kernels for 40%

profile of v23, /device:TPU:0, one launch (start us, length us, event | category | flops | bytes accessed | tf_op | source)
XLA Modules:
  0.0 49.8 jit_solution(1393269380550710604)
XLA Ops:
  0.6 1.5 %pack.1 = (bf16[144,128]{1,0:T(8,128)(2,1)S(1)}, bf16[36,1024]{1,0:T(8,128)(2,1)S(1)}, bf16[36,1024]{1,0:T(8,128)(2,1)S(1)}, bf16[36,1024]{1,0:T(8,128)(2,1)S(1)...) custom-call(s32[1]{0:T(128)} %bitcast.plane_ref, ...), custom_call_target="tpu_custom_call" | custom-call | tf_op jit(solution)/shard_map/pack/pallas_call | solution.py:80
  2.1 5.1 %collective-permute-start = (bf16[36,1024]{1,0:T(8,128)(2,1)S(1)}, bf16[36,1024]{1,0:T(8,128)(2,1)S(1)}, u32[]{:S(2)}, u32[]{:S(2)}) collective-permute-start(bf16[36,1024]{1,0:T(8,128)(2,1)S(1)} %get-tuple-element.45), channel_id=1, source_target_pairs={{0,6},{2,4},{4,2},{6,0},{1,7},{3,5},{5,3},{7,1},{8,14},{10,12},{12... | collective-permute-start | bytes 221192 | tf_op jit(solution)/shard_map/ppermute | solution.py:416
  7.2 0.6 %collective-permute-start.2 = (bf16[36,1024]{1,0:T(8,128)(2,1)S(1)}, bf16[36,1024]{1,0:T(8,128)(2,1)S(1)}, u32[]{:S(2)}, u32[]{:S(2)}) collective-permute-start(bf16[36,1024]{1,0:T(8,128)(2,1)S(1)} %get-tuple-element.47), channel_id=1, source_target_pairs={{0,2},{2,0},{4,6},{6,4},{1,3},{3,1},{5,7},{7,5},{8,10},{10,8},{12,... | collective-permute-start | bytes 221192 | tf_op jit(solution)/shard_map/ppermute | solution.py:416
  7.9 2.9 %flip.1 = (bf16[2048,1024]{1,0:T(8,128)(2,1)S(1)}, bf16[1024,2048]{1,0:T(8,128)(2,1)S(1)}) custom-call(bf16[2048,1024]{1,0:T(8,128)(2,1)} %source_ref), custom_call_target="tpu_custom_call" | custom-call | tf_op jit(solution)/shard_map/flip/pallas_call | solution.py:159
  10.8 3.8 %collective-permute-start.7 = (bf16[36,1024]{1,0:T(8,128)(2,1)S(1)}, bf16[36,1024]{1,0:T(8,128)(2,1)S(1)}, u32[]{:S(2)}, u32[]{:S(2)}) collective-permute-start(bf16[36,1024]{1,0:T(8,128)(2,1)S(1)} %get-tuple-element.62), channel_id=1, source_target_pairs={{0,6},{2,4},{4,2},{6,0},{1,7},{3,5},{5,3},{7,1},{8,14},{10,12},{12... | collective-permute-start | bytes 221192 | tf_op jit(solution)/shard_map/ppermute | solution.py:416
  14.6 0.6 %collective-permute-start.9 = (bf16[36,1024]{1,0:T(8,128)(2,1)S(1)}, bf16[36,1024]{1,0:T(8,128)(2,1)S(1)}, u32[]{:S(2)}, u32[]{:S(2)}) collective-permute-start(bf16[36,1024]{1,0:T(8,128)(2,1)S(1)} %get-tuple-element.64), channel_id=1, source_target_pairs={{0,2},{2,0},{4,6},{6,4},{1,3},{3,1},{5,7},{7,5},{8,10},{10,8},{12,... | collective-permute-start | bytes 221192 | tf_op jit(solution)/shard_map/ppermute | solution.py:416
  15.3 1.7 %collective-permute-start.3 = (bf16[144,1024]{1,0:T(8,128)(2,1)S(1)}, bf16[144,1024]{1,0:T(8,128)(2,1)S(1)}, u32[]{:S(2)}, u32[]{:S(2)}) collective-permute-start(bf16[144,1024]{1,0:T(8,128)(2,1)S(1)} %join.2.refs_0_.refs_4_), channel_id=1, source_target_pairs={{0,1},{1,0},{2,3},{3,2},{4,5},{5,4},{6,7},{7,6},{8,9},{9,8},{10,11... | collective-permute-start | bytes 884744 | tf_op jit(solution)/shard_map/ppermute | solution.py:411
  17.0 1.5 %collective-permute-start.12 = (bf16[144,1024]{1,0:T(8,128)(2,1)S(1)}, bf16[144,1024]{1,0:T(8,128)(2,1)S(1)}, u32[]{:S(2)}, u32[]{:S(2)}) collective-permute-start(bf16[144,1024]{1,0:T(8,128)(2,1)S(1)} %join.2.refs_0_.refs_4_), channel_id=1, source_target_pairs={{0,16},{16,0},{1,17},{17,1},{2,18},{18,2},{3,19},{19,3},{4,20},{20... | collective-permute-start | bytes 884744 | tf_op jit(solution)/shard_map/ppermute | solution.py:411
  18.5 2.2 %forward_down.2 = (bf16[144,2048]{1,0:T(8,128)(2,1)S(1)}, bf16[144,2048]{1,0:T(8,128)(2,1)S(1)}, bf16[144,1024]{1,0:T(8,128)(2,1)S(1)}) custom-call(bf16[144,1024]{1,0:T(8,128)(2,1)S(1)} %join.2.refs_0_.refs_4_, bf16[1024,2048]{1,0:T(8,128)(2,1)S(1)} %copy-done, bf16[1024,2048]{1,0:T(8,128)(2,1)S(1)} %copy-done.1, ...), custom_call_target="tpu_custom_call" | custom-call | tf_op jit(solution)/shard_map/forward_down/pallas_call | solution.py:239
  20.8 0.3 collective-permute-done.8.refs_2_
  21.2 1.6 %collective-permute-start.11 = (bf16[144,1024]{1,0:T(8,128)(2,1)S(1)}, bf16[144,1024]{1,0:T(8,128)(2,1)S(1)}, u32[]{:S(2)}, u32[]{:S(2)}) collective-permute-start(bf16[144,1024]{1,0:T(8,128)(2,1)S(1)} %join.3.refs_0_), channel_id=1, source_target_pairs={{0,16},{16,0},{1,17},{17,1},{2,18},{18,2},{3,19},{19,3},{4,20},{20... | collective-permute-start | bytes 884744 | tf_op jit(solution)/shard_map/ppermute | solution.py:411
  22.7 1.5 %collective-permute-start.10 = (bf16[144,1024]{1,0:T(8,128)(2,1)S(1)}, bf16[144,1024]{1,0:T(8,128)(2,1)S(1)}, u32[]{:S(2)}, u32[]{:S(2)}) collective-permute-start(bf16[144,1024]{1,0:T(8,128)(2,1)S(1)} %join.3.refs_0_), channel_id=1, source_target_pairs={{0,1},{1,0},{2,3},{3,2},{4,5},{5,4},{6,7},{7,6},{8,9},{9,8},{10,11... | collective-permute-start | bytes 884744 | tf_op jit(solution)/shard_map/ppermute | solution.py:411
  24.2 2.2 %forward_down.3 = (bf16[144,2048]{1,0:T(8,128)(2,1)S(1)}, bf16[144,2048]{1,0:T(8,128)(2,1)S(1)}, bf16[72,1024]{1,0:T(8,128)(2,1)S(1)}, bf16[72,1024]{1,0:T(8,128...) custom-call(bf16[144,1024]{1,0:T(8,128)(2,1)S(1)} %collective-permute-done.3.refs_0_.refs_1_.refs_5_, ...), custom_call_target="tpu_custom_call" | custom-call | tf_op jit(solution)/shard_map/forward_down/pallas_call | solution.py:239
  26.5 1.7 %collective-permute-start.4 = (bf16[72,1024]{1,0:T(8,128)(2,1)S(1)}, bf16[72,1024]{1,0:T(8,128)(2,1)S(1)}, u32[]{:S(2)}, u32[]{:S(2)}) collective-permute-start(bf16[72,1024]{1,0:T(8,128)(2,1)S(1)} %get-tuple-element.53), channel_id=1, source_target_pairs={{0,4},{2,6},{4,0},{6,2},{1,5},{3,7},{5,1},{7,3},{8,12},{10,14},{12... | collective-permute-start | bytes 442376 | tf_op jit(solution)/shard_map/ppermute | solution.py:416
  28.2 1.1 %collective-permute-start.5 = (bf16[72,1024]{1,0:T(8,128)(2,1)S(1)}, bf16[72,1024]{1,0:T(8,128)(2,1)S(1)}, u32[]{:S(2)}, u32[]{:S(2)}) collective-permute-start(bf16[72,1024]{1,0:T(8,128)(2,1)S(1)} %get-tuple-element.54), channel_id=1, source_target_pairs={{0,6},{2,4},{4,2},{6,0},{1,7},{3,5},{5,3},{7,1},{8,14},{10,12},{12... | collective-permute-start | bytes 442376 | tf_op jit(solution)/shard_map/ppermute | solution.py:416
  29.3 0.7 %collective-permute-start.6 = (bf16[72,1024]{1,0:T(8,128)(2,1)S(1)}, bf16[72,1024]{1,0:T(8,128)(2,1)S(1)}, u32[]{:S(2)}, u32[]{:S(2)}) collective-permute-start(bf16[72,1024]{1,0:T(8,128)(2,1)S(1)} %get-tuple-element.55), channel_id=1, source_target_pairs={{0,2},{2,0},{4,6},{6,4},{1,3},{3,1},{5,7},{7,5},{8,10},{10,8},{12,... | collective-permute-start | bytes 442376 | tf_op jit(solution)/shard_map/ppermute | solution.py:416
  30.0 0.2 collective-permute-done.11.refs_2_.refs_0_
  30.3 1.6 %collective-permute-start.13 = (bf16[144,1024]{1,0:T(8,128)(2,1)S(1)}, bf16[144,1024]{1,0:T(8,128)(2,1)S(1)}, u32[]{:S(2)}, u32[]{:S(2)}) collective-permute-start(bf16[144,1024]{1,0:T(8,128)(2,1)S(1)} %relay.4.refs_1_), channel_id=1, source_target_pairs={{0,16},{16,0},{1,17},{17,1},{2,18},{18,2},{3,19},{19,3},{4,20},{20... | collective-permute-start | bytes 884744 | tf_op jit(solution)/shard_map/ppermute | solution.py:411
  31.9 1.1 %collective-permute-start.15 = (bf16[144,1024]{1,0:T(8,128)(2,1)S(1)}, bf16[144,1024]{1,0:T(8,128)(2,1)S(1)}, u32[]{:S(2)}, u32[]{:S(2)}) collective-permute-start(bf16[144,1024]{1,0:T(8,128)(2,1)S(1)} %relay.5.refs_0_), channel_id=1, source_target_pairs={{0,1},{1,0},{2,3},{3,2},{4,5},{5,4},{6,7},{7,6},{8,9},{9,8},{10,11... | collective-permute-start | bytes 884744 | tf_op jit(solution)/shard_map/ppermute | solution.py:411
  33.0 1.6 %forward.2 = (bf16[144,2048]{1,0:T(8,128)(2,1)S(1)}, bf16[144,2048]{1,0:T(8,128)(2,1)S(1)}) custom-call(bf16[144,1024]{1,0:T(8,128)(2,1)S(1)} %relay.5.refs_0_, bf16[144,1024]{1,0:T(8,128)(2,1)S(1)} %collective-permute-done.12._.refs_1_.refs_2_.refs_6_, bf16[1024,2048]{1,0:T(8,128)(2,1)S(1)} %copy-done, bf16[1024,2048]{1,0:T(8,128)(2,1)S(1)} %copy-done.1), custom_call_target="tpu_custom_call" | custom-call | flops 20000000000 | tf_op jit(solution)/shard_map/forward/pallas_call | solution.py:239
  34.6 2.2 %slopes.1 = (bf16[432,2048]{1,0:T(8,128)(2,1)S(1)}, bf16[432,2048]{1,0:T(8,128)(2,1)S(1)}) custom-call(bf16[144,1024]{1,0:T(8,128)(2,1)S(1)} %join.3.refs_0_, bf16[144,1024]{1,0:T(8,128)(2,1)S(1)} %collective-permute-done.10.refs_2_.refs_1_, bf16[144,1024]{1,0:T(8,128)(2,1)S(1)} %collective-permute-done.11.refs_2_.refs_0_, ...), custom_call_target="tpu_custom_call" | custom-call | tf_op jit(solution)/shard_map/slopes/pallas_call | solution.py:298
  36.8 1.7 %collective-permute-done.13.refs_1_.refs_3_.refs_7_ = bf16[144,1024]{1,0:T(8,128)(2,1)S(1)} collective-permute-done((bf16[144,1024]{1,0:T(8,128)(2,1)S(1)}, bf16[144,1024]{1,0:T(8,128)(2,1)S(1)}, u32[]{:S(2)}, u32[]{:S(2)}) %collective-permute-start.13) | collective-permute-done | bytes 294944 | tf_op jit(solution)/shard_map/ppermute | solution.py:411
  38.5 1.6 %forward.3 = (bf16[144,2048]{1,0:T(8,128)(2,1)S(1)}, bf16[144,2048]{1,0:T(8,128)(2,1)S(1)}) custom-call(bf16[432,2048]{1,0:T(8,128)(2,1)S(1)} %get-tuple-element.71.refs_0_.dg_ref, bf16[144,1024]{1,0:T(8,128)(2,1)S(1)} %collective-permute-done.13.refs_1_.refs_3_.refs_7_, bf16[1024,2048]{1,0:T(8,128)(2,1)S(1)} %copy-done, bf16[1024,2048]{1,0:T(8,128)(2,1)S(1)} %copy-done.1), custom_call_target="tpu_custom_call" | custom-call | tf_op jit(solution)/shard_map/forward/pallas_call | solution.py:239
  40.2 0.3 collective-permute-start.14
  40.5 0.2 turn.1.xt_ref
  40.7 2.3 %backward.2 = (bf16[512,1024]{1,0:T(8,128)(2,1)S(1)}, bf16[512,1024]{1,0:T(8,128)(2,1)S(1)}) custom-call(bf16[512,576]{1,0:T(8,128)(2,1)S(1)} %turn.1.xt_ref, bf16[144,1024]{1,0:T(8,128)(2,1)S(1)} %collective-permute-done.15.g_ref, bf16[144,2048]{1,0:T(8,128)(2,1)S(1)} %get-tuple-element.72.refs_4_.act_ref, ...), custom_call_target="tpu_custom_call" | custom-call | flops 20000000000 | tf_op jit(solution)/shard_map/backward/pallas_call | solution.py:325
  43.2 2.1 %backward.3 = (bf16[512,1024]{1,0:T(8,128)(2,1)S(1)}, bf16[512,1024]{1,0:T(8,128)(2,1)S(1)}) custom-call(bf16[512,576]{1,0:T(8,128)(2,1)S(1)} %turn.1.xt_ref, bf16[144,1024]{1,0:T(8,128)(2,1)S(1)} %collective-permute-done.15.g_ref, bf16[144,2048]{1,0:T(8,128)(2,1)S(1)} %get-tuple-element.72.refs_4_.act_ref, ...), custom_call_target="tpu_custom_call" | custom-call | flops 20000000000 | tf_op jit(solution)/shard_map/backward/pallas_call | solution.py:325
  45.3 0.6 %collective-permute-start.17 = (bf16[512,1024]{1,0:T(8,128)(2,1)S(1)}, bf16[512,1024]{1,0:T(8,128)(2,1)S(1)}, u32[]{:S(2)}, u32[]{:S(2)}) collective-permute-start(bf16[512,1024]{1,0:T(8,128)(2,1)S(1)} %get-tuple-element.81), channel_id=1, source_target_pairs={{0,8},{8,0},{1,9},{9,1},{2,10},{10,2},{3,11},{11,3},{4,12},{12,4},... | collective-permute-start | bytes 3145736 | tf_op jit(solution)/shard_map/ppermute | solution.py:411
  45.8 1.1 %finish.2 = (bf16[256,2048]{1,0:T(8,128)(2,1)}, bf16[256,2048]{1,0:T(8,128)(2,1)}) custom-call(bf16[512,1024]{1,0:T(8,128)(2,1)S(1)} %get-tuple-element.77.refs_0_, bf16[512,1024]{1,0:T(8,128)(2,1)S(1)} %collective-permute-done.16.refs_1_), custom_call_target="tpu_custom_call" | custom-call | tf_op jit(solution)/shard_map/finish/pallas_call | solution.py:361
  47.0 0.6 %collective-permute-done.14.got_ref = bf16[144,1024]{1,0:T(8,128)(2,1)S(1)} collective-permute-done((bf16[144,1024]{1,0:T(8,128)(2,1)S(1)}, bf16[144,1024]{1,0:T(8,128)(2,1)S(1)}, u32[]{:S(2)}, u32[]{:S(2)}) %collective-permute-start.14) | collective-permute-done | bytes 294944 | tf_op jit(solution)/shard_map/ppermute | solution.py:411
  47.5 1.1 %unpack.1 = bf16[128,1024]{1,0:T(8,128)(2,1)} custom-call(bf16[144,128]{1,0:T(8,128)(2,1)S(1)} %get-tuple-element.44.placer_ref, bf16[144,1024]{1,0:T(8,128)(2,1)S(1)} %get-tuple-element.73.mine_ref, bf16[144,1024]{1,0:T(8,128)(2,1)S(1)} %collective-permute-done.14.got_ref, bf16[256,2048]{1,0:T(8,128)(2,1)} %get-tuple-element.79.refs_0_.refs_2_), custom_call_target="tpu_custom_call" | custom-call | flops 20000000000 | tf_op jit(solution)/shard_map/unpack/pallas_call | solution.py:400
  48.6 1.1 %finish.3 = (bf16[256,2048]{1,0:T(8,128)(2,1)}, bf16[256,2048]{1,0:T(8,128)(2,1)}) custom-call(bf16[512,1024]{1,0:T(8,128)(2,1)S(1)} %get-tuple-element.80.refs_0_, bf16[512,1024]{1,0:T(8,128)(2,1)S(1)} %collective-permute-done.17.refs_1_, bf16[256,2048]{1,0:T(8,128)(2,1)} %get-tuple-element.79.refs_0_.refs_2_, ...), custom_call_target="tpu_custom_call", output_to_operand_aliasing={{0}: (2, {}), {1}: (3, {})} | custom-call | tf_op jit(solution)/shard_map/finish/pallas_call | solution.py:361
  (28 shorter events, 0.4 us)
Async XLA Ops:
  2.1 12.5 %collective-permute-start = (bf16[36,1024]{1,0:T(8,128)(2,1)S(1)}, bf16[36,1024]{1,0:T(8,128)(2,1)S(1)}, u32[]{:S(2)}, u32[]{:S(2)}) collective-permute-start(bf16[36,1024]{1,0:T(8,128)(2,1)S(1)} %get-tuple-element.45), channel_id=1, source_target_pairs={{0,6},{2,4},{4,2},{6,0},{1,7},{3,5},{5,3},{7,1},{8,14},{10,12},{12... | collective-permute-start | bytes 221192 | tf_op jit(solution)/shard_map/ppermute | solution.py:416
  7.2 8.0 %collective-permute-start.1 = (bf16[36,1024]{1,0:T(8,128)(2,1)S(1)}, bf16[36,1024]{1,0:T(8,128)(2,1)S(1)}, u32[]{:S(2)}, u32[]{:S(2)}) collective-permute-start(bf16[36,1024]{1,0:T(8,128)(2,1)S(1)} %get-tuple-element.46), channel_id=1, source_target_pairs={{0,4},{2,6},{4,0},{6,2},{1,5},{3,7},{5,1},{7,3},{8,12},{10,14},{12... | collective-permute-start | bytes 221192 | tf_op jit(solution)/shard_map/ppermute | solution.py:416
  7.2 8.0 %collective-permute-start.2 = (bf16[36,1024]{1,0:T(8,128)(2,1)S(1)}, bf16[36,1024]{1,0:T(8,128)(2,1)S(1)}, u32[]{:S(2)}, u32[]{:S(2)}) collective-permute-start(bf16[36,1024]{1,0:T(8,128)(2,1)S(1)} %get-tuple-element.47), channel_id=1, source_target_pairs={{0,2},{2,0},{4,6},{6,4},{1,3},{3,1},{5,7},{7,5},{8,10},{10,8},{12,... | collective-permute-start | bytes 221192 | tf_op jit(solution)/shard_map/ppermute | solution.py:416
  7.9 10.7 %copy-start = (bf16[1024,2048]{1,0:T(8,128)(2,1)S(1)}, bf16[1024,2048]{1,0:T(8,128)(2,1)}, u32[]{:S(2)}) copy-start(bf16[1024,2048]{1,0:T(8,128)(2,1)} %refs_2_.7) | copy-start | bytes 12582916
  7.9 10.7 %copy-start.1 = (bf16[1024,2048]{1,0:T(8,128)(2,1)S(1)}, bf16[1024,2048]{1,0:T(8,128)(2,1)}, u32[]{:S(2)}) copy-start(bf16[1024,2048]{1,0:T(8,128)(2,1)} %refs_3_.3) | copy-start | bytes 12582916
  10.8 10.0 %collective-permute-start.7 = (bf16[36,1024]{1,0:T(8,128)(2,1)S(1)}, bf16[36,1024]{1,0:T(8,128)(2,1)S(1)}, u32[]{:S(2)}, u32[]{:S(2)}) collective-permute-start(bf16[36,1024]{1,0:T(8,128)(2,1)S(1)} %get-tuple-element.62), channel_id=1, source_target_pairs={{0,6},{2,4},{4,2},{6,0},{1,7},{3,5},{5,3},{7,1},{8,14},{10,12},{12... | collective-permute-start | bytes 221192 | tf_op jit(solution)/shard_map/ppermute | solution.py:416
  14.6 6.5 %collective-permute-start.8 = (bf16[36,1024]{1,0:T(8,128)(2,1)S(1)}, bf16[36,1024]{1,0:T(8,128)(2,1)S(1)}, u32[]{:S(2)}, u32[]{:S(2)}) collective-permute-start(bf16[36,1024]{1,0:T(8,128)(2,1)S(1)} %get-tuple-element.63), channel_id=1, source_target_pairs={{0,4},{2,6},{4,0},{6,2},{1,5},{3,7},{5,1},{7,3},{8,12},{10,14},{12... | collective-permute-start | bytes 221192 | tf_op jit(solution)/shard_map/ppermute | solution.py:416
  14.6 6.5 %collective-permute-start.9 = (bf16[36,1024]{1,0:T(8,128)(2,1)S(1)}, bf16[36,1024]{1,0:T(8,128)(2,1)S(1)}, u32[]{:S(2)}, u32[]{:S(2)}) collective-permute-start(bf16[36,1024]{1,0:T(8,128)(2,1)S(1)} %get-tuple-element.64), channel_id=1, source_target_pairs={{0,2},{2,0},{4,6},{6,4},{1,3},{3,1},{5,7},{7,5},{8,10},{10,8},{12,... | collective-permute-start | bytes 221192 | tf_op jit(solution)/shard_map/ppermute | solution.py:416
  15.3 8.9 %collective-permute-start.3 = (bf16[144,1024]{1,0:T(8,128)(2,1)S(1)}, bf16[144,1024]{1,0:T(8,128)(2,1)S(1)}, u32[]{:S(2)}, u32[]{:S(2)}) collective-permute-start(bf16[144,1024]{1,0:T(8,128)(2,1)S(1)} %join.2.refs_0_.refs_4_), channel_id=1, source_target_pairs={{0,1},{1,0},{2,3},{3,2},{4,5},{5,4},{6,7},{7,6},{8,9},{9,8},{10,11... | collective-permute-start | bytes 884744 | tf_op jit(solution)/shard_map/ppermute | solution.py:411
  17.0 12.3 %collective-permute-start.12 = (bf16[144,1024]{1,0:T(8,128)(2,1)S(1)}, bf16[144,1024]{1,0:T(8,128)(2,1)S(1)}, u32[]{:S(2)}, u32[]{:S(2)}) collective-permute-start(bf16[144,1024]{1,0:T(8,128)(2,1)S(1)} %join.2.refs_0_.refs_4_), channel_id=1, source_target_pairs={{0,16},{16,0},{1,17},{17,1},{2,18},{18,2},{3,19},{19,3},{4,20},{20... | collective-permute-start | bytes 884744 | tf_op jit(solution)/shard_map/ppermute | solution.py:411
  21.2 9.1 %collective-permute-start.11 = (bf16[144,1024]{1,0:T(8,128)(2,1)S(1)}, bf16[144,1024]{1,0:T(8,128)(2,1)S(1)}, u32[]{:S(2)}, u32[]{:S(2)}) collective-permute-start(bf16[144,1024]{1,0:T(8,128)(2,1)S(1)} %join.3.refs_0_), channel_id=1, source_target_pairs={{0,16},{16,0},{1,17},{17,1},{2,18},{18,2},{3,19},{19,3},{4,20},{20... | collective-permute-start | bytes 884744 | tf_op jit(solution)/shard_map/ppermute | solution.py:411
  22.7 9.2 %collective-permute-start.10 = (bf16[144,1024]{1,0:T(8,128)(2,1)S(1)}, bf16[144,1024]{1,0:T(8,128)(2,1)S(1)}, u32[]{:S(2)}, u32[]{:S(2)}) collective-permute-start(bf16[144,1024]{1,0:T(8,128)(2,1)S(1)} %join.3.refs_0_), channel_id=1, source_target_pairs={{0,1},{1,0},{2,3},{3,2},{4,5},{5,4},{6,7},{7,6},{8,9},{9,8},{10,11... | collective-permute-start | bytes 884744 | tf_op jit(solution)/shard_map/ppermute | solution.py:411
  26.5 13.6 %collective-permute-start.4 = (bf16[72,1024]{1,0:T(8,128)(2,1)S(1)}, bf16[72,1024]{1,0:T(8,128)(2,1)S(1)}, u32[]{:S(2)}, u32[]{:S(2)}) collective-permute-start(bf16[72,1024]{1,0:T(8,128)(2,1)S(1)} %get-tuple-element.53), channel_id=1, source_target_pairs={{0,4},{2,6},{4,0},{6,2},{1,5},{3,7},{5,1},{7,3},{8,12},{10,14},{12... | collective-permute-start | bytes 442376 | tf_op jit(solution)/shard_map/ppermute | solution.py:416
  28.2 11.9 %collective-permute-start.5 = (bf16[72,1024]{1,0:T(8,128)(2,1)S(1)}, bf16[72,1024]{1,0:T(8,128)(2,1)S(1)}, u32[]{:S(2)}, u32[]{:S(2)}) collective-permute-start(bf16[72,1024]{1,0:T(8,128)(2,1)S(1)} %get-tuple-element.54), channel_id=1, source_target_pairs={{0,6},{2,4},{4,2},{6,0},{1,7},{3,5},{5,3},{7,1},{8,14},{10,12},{12... | collective-permute-start | bytes 442376 | tf_op jit(solution)/shard_map/ppermute | solution.py:416
  29.3 10.8 %collective-permute-start.6 = (bf16[72,1024]{1,0:T(8,128)(2,1)S(1)}, bf16[72,1024]{1,0:T(8,128)(2,1)S(1)}, u32[]{:S(2)}, u32[]{:S(2)}) collective-permute-start(bf16[72,1024]{1,0:T(8,128)(2,1)S(1)} %get-tuple-element.55), channel_id=1, source_target_pairs={{0,2},{2,0},{4,6},{6,4},{1,3},{3,1},{5,7},{7,5},{8,10},{10,8},{12,... | collective-permute-start | bytes 442376 | tf_op jit(solution)/shard_map/ppermute | solution.py:416
  30.3 8.2 %collective-permute-start.13 = (bf16[144,1024]{1,0:T(8,128)(2,1)S(1)}, bf16[144,1024]{1,0:T(8,128)(2,1)S(1)}, u32[]{:S(2)}, u32[]{:S(2)}) collective-permute-start(bf16[144,1024]{1,0:T(8,128)(2,1)S(1)} %relay.4.refs_1_), channel_id=1, source_target_pairs={{0,16},{16,0},{1,17},{17,1},{2,18},{18,2},{3,19},{19,3},{4,20},{20... | collective-permute-start | bytes 884744 | tf_op jit(solution)/shard_map/ppermute | solution.py:411
  31.9 8.8 %collective-permute-start.15 = (bf16[144,1024]{1,0:T(8,128)(2,1)S(1)}, bf16[144,1024]{1,0:T(8,128)(2,1)S(1)}, u32[]{:S(2)}, u32[]{:S(2)}) collective-permute-start(bf16[144,1024]{1,0:T(8,128)(2,1)S(1)} %relay.5.refs_0_), channel_id=1, source_target_pairs={{0,1},{1,0},{2,3},{3,2},{4,5},{5,4},{6,7},{7,6},{8,9},{9,8},{10,11... | collective-permute-start | bytes 884744 | tf_op jit(solution)/shard_map/ppermute | solution.py:411
  40.2 7.3 %collective-permute-start.14 = (bf16[144,1024]{1,0:T(8,128)(2,1)S(1)}, bf16[144,1024]{1,0:T(8,128)(2,1)S(1)}, u32[]{:S(2)}, u32[]{:S(2)}) collective-permute-start(bf16[144,1024]{1,0:T(8,128)(2,1)S(1)} %get-tuple-element.74), channel_id=1, source_target_pairs={{0,1},{1,0},{2,3},{3,2},{4,5},{5,4},{6,7},{7,6},{8,9},{9,8},{10,11... | collective-permute-start | bytes 884744 | tf_op jit(solution)/shard_map/ppermute | solution.py:411
  43.1 2.8 %collective-permute-start.16 = (bf16[512,1024]{1,0:T(8,128)(2,1)S(1)}, bf16[512,1024]{1,0:T(8,128)(2,1)S(1)}, u32[]{:S(2)}, u32[]{:S(2)}) collective-permute-start(bf16[512,1024]{1,0:T(8,128)(2,1)S(1)} %get-tuple-element.78), channel_id=1, source_target_pairs={{0,8},{8,0},{1,9},{9,1},{2,10},{10,2},{3,11},{11,3},{4,12},{12,4},... | collective-permute-start | bytes 3145736 | tf_op jit(solution)/shard_map/ppermute | solution.py:411
  45.3 3.3 %collective-permute-start.17 = (bf16[512,1024]{1,0:T(8,128)(2,1)S(1)}, bf16[512,1024]{1,0:T(8,128)(2,1)S(1)}, u32[]{:S(2)}, u32[]{:S(2)}) collective-permute-start(bf16[512,1024]{1,0:T(8,128)(2,1)S(1)} %get-tuple-element.81), channel_id=1, source_target_pairs={{0,8},{8,0},{1,9},{9,1},{2,10},{10,2},{3,11},{11,3},{4,12},{12,4},... | collective-permute-start | bytes 3145736 | tf_op jit(solution)/shard_map/ppermute | solution.py:411

commit v24 on v20

--- a/solution.py
+++ b/solution.py
@@ -13,6 +13,7 @@
 WIDE = 1024
 STRIP = 512
 SLICE = 256
+SENT = (0, 2, 1, 3)
 MIB = 1024 * 1024
 LARGE = pltpu.CompilerParams(vmem_limit_bytes=16 * MIB)
 SMALL = pltpu.CompilerParams(vmem_limit_bytes=12 * MIB)
@@ -365,7 +366,7 @@
 
 
 def split_kernel(*refs):
-    blocks = [r[...].astype(F32) for r in refs[:EXPERTS]]
+    blocks = [refs[SENT.index(k)][...].astype(F32) for k in range(EXPERTS)]
     refs[-2][...] = jnp.concatenate([b[:CAP] for b in blocks], axis=0).astype(BF16)
     refs[-1][...] = jnp.concatenate([b[CAP:] for b in blocks], axis=0).astype(BF16)
 
@@ -379,7 +380,7 @@
         compiler_params=SMALL,
         cost_estimate=CHEAP,
         name="split",
-    )(*blocks, *earlier)
+    )(*[blocks[k] for k in SENT], *earlier)
 
 
 def unpack_kernel(placer_ref, mine_ref, got_ref, *refs):

time: 49.8 us -> 49.6 us (level)
  transfers between devices with their start and end apart: 18 -> 18, of which waited for: 5 -> 4; matrix products, arithmetic and copies ran while one was open for 0% -> 0% of each run, Pallas kernels for 36% -> 37%
where the time goes in v24:
time: 49.6 us; the launch traced here: 49.5 us
  starting transfers between devices  24.7 us (50%)
  Pallas kernels  20.8 us (42%)
  waiting for transfers between devices  2.96 us (6%)
  between operations  1.01 us (2%)
    ppermute x9, starting transfers between devices, across_planes(): lax.ppermute(blocks[k], 'arch', [(i, i ^ k) for i in range(EXPERTS)])  15.8 us
    ppermute x9, starting transfers between devices, swap(): return lax.ppermute(value, axis, [(0, 1), (1, 0)])  8.83 us
    pallas_call x4, Pallas kernels, forward(): pl.pallas_call(functools.partial(forward_kernel, n, fetch, down, pair, le...  7.63 us
    pallas_call x2, Pallas kernels, backward(): pl.pallas_call(functools.partial(backward_kernel, first), out_shape=[jax....  4.45 us
    pallas_call x2, Pallas kernels, finish(): pl.pallas_call(functools.partial(finish_kernel, spans, more, len(earlier)...  2.21 us
    pallas_call x1, Pallas kernels, slopes(): pl.pallas_call(functools.partial(slopes_kernel, n), out_shape=[jax.ShapeD...  2.19 us
    ppermute x9, waiting for transfers between devices, swap(): return lax.ppermute(value, axis, [(0, 1), (1, 0)])  1.77 us
    pallas_call x1, Pallas kernels, pack(): pl.pallas_call(pack_kernel, out_shape=[jax.ShapeDtypeStruct((EXPERTS * CA...  1.61 us
  transfers between devices with their start and end apart: 18, of which 4 were waited for; matrix products, arithmetic and copies ran while one was open for 0% of the time, Pallas kernels for 37%

profile of v24, /device:TPU:0, one launch (start us, length us, event | category | flops | bytes accessed | tf_op | source)
XLA Modules:
  0.0 49.5 jit_solution(8569263657478031708)
XLA Ops:
  0.7 1.6 %pack.1 = (bf16[144,128]{1,0:T(8,128)(2,1)S(1)}, bf16[36,1024]{1,0:T(8,128)(2,1)S(1)}, bf16[36,1024]{1,0:T(8,128)(2,1)S(1)}, bf16[36,1024]{1,0:T(8,128)(2,1)S(1)...) custom-call(s32[1]{0:T(128)} %bitcast.plane_ref, ...), custom_call_target="tpu_custom_call" | custom-call | flops 20000000000 | tf_op jit(solution)/shard_map/pack/pallas_call | solution.py:80
  2.3 5.1 %collective-permute-start = (bf16[36,1024]{1,0:T(8,128)(2,1)S(1)}, bf16[36,1024]{1,0:T(8,128)(2,1)S(1)}, u32[]{:S(2)}, u32[]{:S(2)}) collective-permute-start(bf16[36,1024]{1,0:T(8,128)(2,1)S(1)} %get-tuple-element.42), channel_id=1, source_target_pairs={{0,6},{2,4},{4,2},{6,0},{1,7},{3,5},{5,3},{7,1},{8,14},{10,12},{12... | collective-permute-start | bytes 221192 | tf_op jit(solution)/shard_map/ppermute | solution.py:410
  7.4 0.6 %collective-permute-start.2 = (bf16[36,1024]{1,0:T(8,128)(2,1)S(1)}, bf16[36,1024]{1,0:T(8,128)(2,1)S(1)}, u32[]{:S(2)}, u32[]{:S(2)}) collective-permute-start(bf16[36,1024]{1,0:T(8,128)(2,1)S(1)} %get-tuple-element.44), channel_id=1, source_target_pairs={{0,2},{2,0},{4,6},{6,4},{1,3},{3,1},{5,7},{7,5},{8,10},{10,8},{12,... | collective-permute-start | bytes 221192 | tf_op jit(solution)/shard_map/ppermute | solution.py:410
  8.0 1.2 %flip.1.refs_4_.refs_9_.wdt_ref = bf16[1024,2048]{1,0:T(8,128)(2,1)S(1)} custom-call(bf16[2048,1024]{1,0:T(8,128)(2,1)S(1)} %copy-done.2, bf16[144,128]{1,0:T(8,128)(2,1)S(1)} %get-tuple-element.41.refs_0_.placer_ref), custom_call_target="tpu_custom_call" | custom-call | tf_op jit(solution)/shard_map/flip/pallas_call | solution.py:154
  9.3 1.5 %collective-permute-start.7 = (bf16[36,1024]{1,0:T(8,128)(2,1)S(1)}, bf16[36,1024]{1,0:T(8,128)(2,1)S(1)}, u32[]{:S(2)}, u32[]{:S(2)}) collective-permute-start(bf16[36,1024]{1,0:T(8,128)(2,1)S(1)} %get-tuple-element.56), channel_id=1, source_target_pairs={{0,2},{2,0},{4,6},{6,4},{1,3},{3,1},{5,7},{7,5},{8,10},{10,8},{12,... | collective-permute-start | bytes 221192 | tf_op jit(solution)/shard_map/ppermute | solution.py:410
  10.8 2.4 %collective-permute-start.8 = (bf16[36,1024]{1,0:T(8,128)(2,1)S(1)}, bf16[36,1024]{1,0:T(8,128)(2,1)S(1)}, u32[]{:S(2)}, u32[]{:S(2)}) collective-permute-start(bf16[36,1024]{1,0:T(8,128)(2,1)S(1)} %get-tuple-element.57), channel_id=1, source_target_pairs={{0,6},{2,4},{4,2},{6,0},{1,7},{3,5},{5,3},{7,1},{8,14},{10,12},{12... | collective-permute-start | bytes 221192 | tf_op jit(solution)/shard_map/ppermute | solution.py:410
  13.2 1.7 %collective-permute-start.9 = (bf16[36,1024]{1,0:T(8,128)(2,1)S(1)}, bf16[36,1024]{1,0:T(8,128)(2,1)S(1)}, u32[]{:S(2)}, u32[]{:S(2)}) collective-permute-start(bf16[36,1024]{1,0:T(8,128)(2,1)S(1)} %get-tuple-element.58), channel_id=1, source_target_pairs={{0,4},{2,6},{4,0},{6,2},{1,5},{3,7},{5,1},{7,3},{8,12},{10,14},{12... | collective-permute-start | bytes 221192 | tf_op jit(solution)/shard_map/ppermute | solution.py:410
  14.9 0.7 %collective-permute-done.1.refs_1_ = bf16[36,1024]{1,0:T(8,128)(2,1)S(1)} collective-permute-done((bf16[36,1024]{1,0:T(8,128)(2,1)S(1)}, bf16[36,1024]{1,0:T(8,128)(2,1)S(1)}, u32[]{:S(2)}, u32[]{:S(2)}) %collective-permute-start.1) | collective-permute-done | bytes 73760 | tf_op jit(solution)/shard_map/ppermute | solution.py:410
  15.7 1.4 %collective-permute-start.3 = (bf16[144,1024]{1,0:T(8,128)(2,1)S(1)}, bf16[144,1024]{1,0:T(8,128)(2,1)S(1)}, u32[]{:S(2)}, u32[]{:S(2)}) collective-permute-start(bf16[144,1024]{1,0:T(8,128)(2,1)S(1)} %join.2.refs_0_.refs_4_), channel_id=1, source_target_pairs={{0,1},{1,0},{2,3},{3,2},{4,5},{5,4},{6,7},{7,6},{8,9},{9,8},{10,11... | collective-permute-start | bytes 884744 | tf_op jit(solution)/shard_map/ppermute | solution.py:405
  17.1 1.5 %collective-permute-start.12 = (bf16[144,1024]{1,0:T(8,128)(2,1)S(1)}, bf16[144,1024]{1,0:T(8,128)(2,1)S(1)}, u32[]{:S(2)}, u32[]{:S(2)}) collective-permute-start(bf16[144,1024]{1,0:T(8,128)(2,1)S(1)} %join.2.refs_0_.refs_4_), channel_id=1, source_target_pairs={{0,16},{16,0},{1,17},{17,1},{2,18},{18,2},{3,19},{19,3},{4,20},{20... | collective-permute-start | bytes 884744 | tf_op jit(solution)/shard_map/ppermute | solution.py:405
  18.6 2.2 %forward_down.2 = (bf16[144,2048]{1,0:T(8,128)(2,1)S(1)}, bf16[144,2048]{1,0:T(8,128)(2,1)S(1)}, bf16[144,1024]{1,0:T(8,128)(2,1)S(1)}) custom-call(bf16[144,1024]{1,0:T(8,128)(2,1)S(1)} %join.2.refs_0_.refs_4_, bf16[1024,2048]{1,0:T(8,128)(2,1)S(1)} %copy-done, bf16[1024,2048]{1,0:T(8,128)(2,1)S(1)} %copy-done.1, bf16[2048,1024]{1,0:T(8,128)(2,1)S(1)} %copy-done.2), custom_call_target="tpu_custom_call" | custom-call | tf_op jit(solution)/shard_map/forward_down/pallas_call | solution.py:233
  20.8 0.5 collective-permute-done.9.refs_3_
  21.3 1.6 %collective-permute-start.11 = (bf16[144,1024]{1,0:T(8,128)(2,1)S(1)}, bf16[144,1024]{1,0:T(8,128)(2,1)S(1)}, u32[]{:S(2)}, u32[]{:S(2)}) collective-permute-start(bf16[144,1024]{1,0:T(8,128)(2,1)S(1)} %join.3.refs_0_), channel_id=1, source_target_pairs={{0,16},{16,0},{1,17},{17,1},{2,18},{18,2},{3,19},{19,3},{4,20},{20... | collective-permute-start | bytes 884744 | tf_op jit(solution)/shard_map/ppermute | solution.py:405
  22.9 1.5 %collective-permute-start.10 = (bf16[144,1024]{1,0:T(8,128)(2,1)S(1)}, bf16[144,1024]{1,0:T(8,128)(2,1)S(1)}, u32[]{:S(2)}, u32[]{:S(2)}) collective-permute-start(bf16[144,1024]{1,0:T(8,128)(2,1)S(1)} %join.3.refs_0_), channel_id=1, source_target_pairs={{0,1},{1,0},{2,3},{3,2},{4,5},{5,4},{6,7},{7,6},{8,9},{9,8},{10,11... | collective-permute-start | bytes 884744 | tf_op jit(solution)/shard_map/ppermute | solution.py:405
  24.4 2.2 %forward_down.3 = (bf16[144,2048]{1,0:T(8,128)(2,1)S(1)}, bf16[144,2048]{1,0:T(8,128)(2,1)S(1)}, bf16[72,1024]{1,0:T(8,128)(2,1)S(1)}, bf16[72,1024]{1,0:T(8,128...) custom-call(bf16[144,1024]{1,0:T(8,128)(2,1)S(1)} %collective-permute-done.3.refs_0_.refs_1_.refs_5_, ...), custom_call_target="tpu_custom_call" | custom-call | tf_op jit(solution)/shard_map/forward_down/pallas_call | solution.py:233
  26.6 1.0 %collective-permute-start.4 = (bf16[72,1024]{1,0:T(8,128)(2,1)S(1)}, bf16[72,1024]{1,0:T(8,128)(2,1)S(1)}, u32[]{:S(2)}, u32[]{:S(2)}) collective-permute-start(bf16[72,1024]{1,0:T(8,128)(2,1)S(1)} %get-tuple-element.48), channel_id=1, source_target_pairs={{0,4},{2,6},{4,0},{6,2},{1,5},{3,7},{5,1},{7,3},{8,12},{10,14},{12... | collective-permute-start | bytes 442376 | tf_op jit(solution)/shard_map/ppermute | solution.py:410
  27.6 2.3 %collective-permute-start.5 = (bf16[72,1024]{1,0:T(8,128)(2,1)S(1)}, bf16[72,1024]{1,0:T(8,128)(2,1)S(1)}, u32[]{:S(2)}, u32[]{:S(2)}) collective-permute-start(bf16[72,1024]{1,0:T(8,128)(2,1)S(1)} %get-tuple-element.49), channel_id=1, source_target_pairs={{0,2},{2,0},{4,6},{6,4},{1,3},{3,1},{5,7},{7,5},{8,10},{10,8},{12,... | collective-permute-start | bytes 442376 | tf_op jit(solution)/shard_map/ppermute | solution.py:410
  30.0 1.1 %collective-permute-start.6 = (bf16[72,1024]{1,0:T(8,128)(2,1)S(1)}, bf16[72,1024]{1,0:T(8,128)(2,1)S(1)}, u32[]{:S(2)}, u32[]{:S(2)}) collective-permute-start(bf16[72,1024]{1,0:T(8,128)(2,1)S(1)} %get-tuple-element.50), channel_id=1, source_target_pairs={{0,6},{2,4},{4,2},{6,0},{1,7},{3,5},{5,3},{7,1},{8,14},{10,12},{12... | collective-permute-start | bytes 442376 | tf_op jit(solution)/shard_map/ppermute | solution.py:410
  31.1 0.7 %collective-permute-start.13 = (bf16[144,1024]{1,0:T(8,128)(2,1)S(1)}, bf16[144,1024]{1,0:T(8,128)(2,1)S(1)}, u32[]{:S(2)}, u32[]{:S(2)}) collective-permute-start(bf16[144,1024]{1,0:T(8,128)(2,1)S(1)} %relay.4.refs_1_), channel_id=1, source_target_pairs={{0,16},{16,0},{1,17},{17,1},{2,18},{18,2},{3,19},{19,3},{4,20},{20... | collective-permute-start | bytes 884744 | tf_op jit(solution)/shard_map/ppermute | solution.py:405
  31.9 1.0 %collective-permute-start.15 = (bf16[144,1024]{1,0:T(8,128)(2,1)S(1)}, bf16[144,1024]{1,0:T(8,128)(2,1)S(1)}, u32[]{:S(2)}, u32[]{:S(2)}) collective-permute-start(bf16[144,1024]{1,0:T(8,128)(2,1)S(1)} %relay.5.refs_0_), channel_id=1, source_target_pairs={{0,1},{1,0},{2,3},{3,2},{4,5},{5,4},{6,7},{7,6},{8,9},{9,8},{10,11... | collective-permute-start | bytes 884744 | tf_op jit(solution)/shard_map/ppermute | solution.py:405
  32.9 1.6 %forward.2 = (bf16[144,2048]{1,0:T(8,128)(2,1)S(1)}, bf16[144,2048]{1,0:T(8,128)(2,1)S(1)}) custom-call(bf16[144,1024]{1,0:T(8,128)(2,1)S(1)} %relay.5.refs_0_, bf16[144,1024]{1,0:T(8,128)(2,1)S(1)} %collective-permute-done.12._.refs_1_.refs_2_.refs_6_, bf16[1024,2048]{1,0:T(8,128)(2,1)S(1)} %copy-done, bf16[1024,2048]{1,0:T(8,128)(2,1)S(1)} %copy-done.1), custom_call_target="tpu_custom_call" | custom-call | flops 20000000000 | tf_op jit(solution)/shard_map/forward/pallas_call | solution.py:233
  34.5 2.2 %slopes.1 = (bf16[432,2048]{1,0:T(8,128)(2,1)S(1)}, bf16[432,2048]{1,0:T(8,128)(2,1)S(1)}) custom-call(bf16[144,1024]{1,0:T(8,128)(2,1)S(1)} %join.3.refs_0_, bf16[144,1024]{1,0:T(8,128)(2,1)S(1)} %collective-permute-done.10.refs_2_.refs_1_, bf16[144,1024]{1,0:T(8,128)(2,1)S(1)} %collective-permute-done.11.refs_2_.refs_0_, ...), custom_call_target="tpu_custom_call" | custom-call | tf_op jit(solution)/shard_map/slopes/pallas_call | solution.py:292
  36.7 1.6 %collective-permute-done.13.refs_1_.refs_3_.refs_7_ = bf16[144,1024]{1,0:T(8,128)(2,1)S(1)} collective-permute-done((bf16[144,1024]{1,0:T(8,128)(2,1)S(1)}, bf16[144,1024]{1,0:T(8,128)(2,1)S(1)}, u32[]{:S(2)}, u32[]{:S(2)}) %collective-permute-start.13) | collective-permute-done | bytes 294944 | tf_op jit(solution)/shard_map/ppermute | solution.py:405
  38.3 1.6 %forward.3 = (bf16[144,2048]{1,0:T(8,128)(2,1)S(1)}, bf16[144,2048]{1,0:T(8,128)(2,1)S(1)}) custom-call(bf16[432,2048]{1,0:T(8,128)(2,1)S(1)} %get-tuple-element.65.refs_0_.dg_ref, bf16[144,1024]{1,0:T(8,128)(2,1)S(1)} %collective-permute-done.13.refs_1_.refs_3_.refs_7_, bf16[1024,2048]{1,0:T(8,128)(2,1)S(1)} %copy-done, bf16[1024,2048]{1,0:T(8,128)(2,1)S(1)} %copy-done.1), custom_call_target="tpu_custom_call" | custom-call | tf_op jit(solution)/shard_map/forward/pallas_call | solution.py:233
  40.1 0.5 %collective-permute-start.14 = (bf16[144,1024]{1,0:T(8,128)(2,1)S(1)}, bf16[144,1024]{1,0:T(8,128)(2,1)S(1)}, u32[]{:S(2)}, u32[]{:S(2)}) collective-permute-start(bf16[144,1024]{1,0:T(8,128)(2,1)S(1)} %get-tuple-element.68), channel_id=1, source_target_pairs={{0,1},{1,0},{2,3},{3,2},{4,5},{5,4},{6,7},{7,6},{8,9},{9,8},{10,11... | collective-permute-start | bytes 884744 | tf_op jit(solution)/shard_map/ppermute | solution.py:405
  40.6 0.2 turn.1.xt_ref
  40.8 2.3 %backward.2 = (bf16[512,1024]{1,0:T(8,128)(2,1)S(1)}, bf16[512,1024]{1,0:T(8,128)(2,1)S(1)}) custom-call(bf16[512,576]{1,0:T(8,128)(2,1)S(1)} %turn.1.xt_ref, bf16[144,1024]{1,0:T(8,128)(2,1)S(1)} %collective-permute-done.15.g_ref, bf16[144,2048]{1,0:T(8,128)(2,1)S(1)} %get-tuple-element.66.refs_4_.act_ref, ...), custom_call_target="tpu_custom_call" | custom-call | flops 20000000000 | tf_op jit(solution)/shard_map/backward/pallas_call | solution.py:319
  43.2 2.1 %backward.3 = (bf16[512,1024]{1,0:T(8,128)(2,1)S(1)}, bf16[512,1024]{1,0:T(8,128)(2,1)S(1)}) custom-call(bf16[512,576]{1,0:T(8,128)(2,1)S(1)} %turn.1.xt_ref, bf16[144,1024]{1,0:T(8,128)(2,1)S(1)} %collective-permute-done.15.g_ref, bf16[144,2048]{1,0:T(8,128)(2,1)S(1)} %get-tuple-element.66.refs_4_.act_ref, ...), custom_call_target="tpu_custom_call" | custom-call | flops 20000000000 | tf_op jit(solution)/shard_map/backward/pallas_call | solution.py:319
  45.4 0.6 %collective-permute-start.17 = (bf16[512,1024]{1,0:T(8,128)(2,1)S(1)}, bf16[512,1024]{1,0:T(8,128)(2,1)S(1)}, u32[]{:S(2)}, u32[]{:S(2)}) collective-permute-start(bf16[512,1024]{1,0:T(8,128)(2,1)S(1)} %get-tuple-element.75), channel_id=1, source_target_pairs={{0,8},{8,0},{1,9},{9,1},{2,10},{10,2},{3,11},{11,3},{4,12},{12,4},... | collective-permute-start | bytes 3145736 | tf_op jit(solution)/shard_map/ppermute | solution.py:405
  45.9 1.1 %finish.2 = (bf16[256,2048]{1,0:T(8,128)(2,1)}, bf16[256,2048]{1,0:T(8,128)(2,1)}) custom-call(bf16[512,1024]{1,0:T(8,128)(2,1)S(1)} %get-tuple-element.71.refs_0_, bf16[512,1024]{1,0:T(8,128)(2,1)S(1)} %collective-permute-done.16.refs_1_), custom_call_target="tpu_custom_call" | custom-call | tf_op jit(solution)/shard_map/finish/pallas_call | solution.py:355
  47.0 1.0 %unpack.1 = bf16[128,1024]{1,0:T(8,128)(2,1)} custom-call(bf16[144,128]{1,0:T(8,128)(2,1)S(1)} %get-tuple-element.41.refs_0_.placer_ref, bf16[144,1024]{1,0:T(8,128)(2,1)S(1)} %get-tuple-element.67.mine_ref, bf16[144,1024]{1,0:T(8,128)(2,1)S(1)} %collective-permute-done.14.got_ref, bf16[256,2048]{1,0:T(8,128)(2,1)} %get-tuple-element.73.refs_0_.refs_2_), custom_call_target="tpu_custom_call" | custom-call | flops 20000000000 | tf_op jit(solution)/shard_map/unpack/pallas_call | solution.py:394
  48.2 1.1 %finish.3 = (bf16[256,2048]{1,0:T(8,128)(2,1)}, bf16[256,2048]{1,0:T(8,128)(2,1)}) custom-call(bf16[512,1024]{1,0:T(8,128)(2,1)S(1)} %get-tuple-element.74.refs_0_, bf16[512,1024]{1,0:T(8,128)(2,1)S(1)} %collective-permute-done.17.refs_1_, bf16[256,2048]{1,0:T(8,128)(2,1)} %get-tuple-element.73.refs_0_.refs_2_, ...), custom_call_target="tpu_custom_call", output_to_operand_aliasing={{0}: (2, {}), {1}: (3, {})} | custom-call | tf_op jit(solution)/shard_map/finish/pallas_call | solution.py:355
  (30 shorter events, 0.5 us)
Async XLA Ops:
  0.6 7.4 %copy-start.2 = (bf16[2048,1024]{1,0:T(8,128)(2,1)S(1)}, bf16[2048,1024]{1,0:T(8,128)(2,1)}, u32[]{:S(2)}) copy-start(bf16[2048,1024]{1,0:T(8,128)(2,1)} %source_ref.1) | copy-start | bytes 12582916
  2.3 10.9 %collective-permute-start = (bf16[36,1024]{1,0:T(8,128)(2,1)S(1)}, bf16[36,1024]{1,0:T(8,128)(2,1)S(1)}, u32[]{:S(2)}, u32[]{:S(2)}) collective-permute-start(bf16[36,1024]{1,0:T(8,128)(2,1)S(1)} %get-tuple-element.42), channel_id=1, source_target_pairs={{0,6},{2,4},{4,2},{6,0},{1,7},{3,5},{5,3},{7,1},{8,14},{10,12},{12... | collective-permute-start | bytes 221192 | tf_op jit(solution)/shard_map/ppermute | solution.py:410
  7.4 8.3 %collective-permute-start.1 = (bf16[36,1024]{1,0:T(8,128)(2,1)S(1)}, bf16[36,1024]{1,0:T(8,128)(2,1)S(1)}, u32[]{:S(2)}, u32[]{:S(2)}) collective-permute-start(bf16[36,1024]{1,0:T(8,128)(2,1)S(1)} %get-tuple-element.43), channel_id=1, source_target_pairs={{0,4},{2,6},{4,0},{6,2},{1,5},{3,7},{5,1},{7,3},{8,12},{10,14},{12... | collective-permute-start | bytes 221192 | tf_op jit(solution)/shard_map/ppermute | solution.py:410
  7.4 8.3 %collective-permute-start.2 = (bf16[36,1024]{1,0:T(8,128)(2,1)S(1)}, bf16[36,1024]{1,0:T(8,128)(2,1)S(1)}, u32[]{:S(2)}, u32[]{:S(2)}) collective-permute-start(bf16[36,1024]{1,0:T(8,128)(2,1)S(1)} %get-tuple-element.44), channel_id=1, source_target_pairs={{0,2},{2,0},{4,6},{6,4},{1,3},{3,1},{5,7},{7,5},{8,10},{10,8},{12,... | collective-permute-start | bytes 221192 | tf_op jit(solution)/shard_map/ppermute | solution.py:410
  8.0 10.5 %copy-start.1 = (bf16[1024,2048]{1,0:T(8,128)(2,1)S(1)}, bf16[1024,2048]{1,0:T(8,128)(2,1)}, u32[]{:S(2)}) copy-start(bf16[1024,2048]{1,0:T(8,128)(2,1)} %refs_3_.7) | copy-start | bytes 12582916
  9.3 9.3 %copy-start = (bf16[1024,2048]{1,0:T(8,128)(2,1)S(1)}, bf16[1024,2048]{1,0:T(8,128)(2,1)}, u32[]{:S(2)}) copy-start(bf16[1024,2048]{1,0:T(8,128)(2,1)} %refs_2_.7) | copy-start | bytes 12582916
  9.3 11.5 %collective-permute-start.7 = (bf16[36,1024]{1,0:T(8,128)(2,1)S(1)}, bf16[36,1024]{1,0:T(8,128)(2,1)S(1)}, u32[]{:S(2)}, u32[]{:S(2)}) collective-permute-start(bf16[36,1024]{1,0:T(8,128)(2,1)S(1)} %get-tuple-element.56), channel_id=1, source_target_pairs={{0,2},{2,0},{4,6},{6,4},{1,3},{3,1},{5,7},{7,5},{8,10},{10,8},{12,... | collective-permute-start | bytes 221192 | tf_op jit(solution)/shard_map/ppermute | solution.py:410
  10.8 10.0 %collective-permute-start.8 = (bf16[36,1024]{1,0:T(8,128)(2,1)S(1)}, bf16[36,1024]{1,0:T(8,128)(2,1)S(1)}, u32[]{:S(2)}, u32[]{:S(2)}) collective-permute-start(bf16[36,1024]{1,0:T(8,128)(2,1)S(1)} %get-tuple-element.57), channel_id=1, source_target_pairs={{0,6},{2,4},{4,2},{6,0},{1,7},{3,5},{5,3},{7,1},{8,14},{10,12},{12... | collective-permute-start | bytes 221192 | tf_op jit(solution)/shard_map/ppermute | solution.py:410
  13.2 8.1 %collective-permute-start.9 = (bf16[36,1024]{1,0:T(8,128)(2,1)S(1)}, bf16[36,1024]{1,0:T(8,128)(2,1)S(1)}, u32[]{:S(2)}, u32[]{:S(2)}) collective-permute-start(bf16[36,1024]{1,0:T(8,128)(2,1)S(1)} %get-tuple-element.58), channel_id=1, source_target_pairs={{0,4},{2,6},{4,0},{6,2},{1,5},{3,7},{5,1},{7,3},{8,12},{10,14},{12... | collective-permute-start | bytes 221192 | tf_op jit(solution)/shard_map/ppermute | solution.py:410
  15.7 8.7 %collective-permute-start.3 = (bf16[144,1024]{1,0:T(8,128)(2,1)S(1)}, bf16[144,1024]{1,0:T(8,128)(2,1)S(1)}, u32[]{:S(2)}, u32[]{:S(2)}) collective-permute-start(bf16[144,1024]{1,0:T(8,128)(2,1)S(1)} %join.2.refs_0_.refs_4_), channel_id=1, source_target_pairs={{0,1},{1,0},{2,3},{3,2},{4,5},{5,4},{6,7},{7,6},{8,9},{9,8},{10,11... | collective-permute-start | bytes 884744 | tf_op jit(solution)/shard_map/ppermute | solution.py:405
  17.1 12.9 %collective-permute-start.12 = (bf16[144,1024]{1,0:T(8,128)(2,1)S(1)}, bf16[144,1024]{1,0:T(8,128)(2,1)S(1)}, u32[]{:S(2)}, u32[]{:S(2)}) collective-permute-start(bf16[144,1024]{1,0:T(8,128)(2,1)S(1)} %join.2.refs_0_.refs_4_), channel_id=1, source_target_pairs={{0,16},{16,0},{1,17},{17,1},{2,18},{18,2},{3,19},{19,3},{4,20},{20... | collective-permute-start | bytes 884744 | tf_op jit(solution)/shard_map/ppermute | solution.py:405
  21.3 9.8 %collective-permute-start.11 = (bf16[144,1024]{1,0:T(8,128)(2,1)S(1)}, bf16[144,1024]{1,0:T(8,128)(2,1)S(1)}, u32[]{:S(2)}, u32[]{:S(2)}) collective-permute-start(bf16[144,1024]{1,0:T(8,128)(2,1)S(1)} %join.3.refs_0_), channel_id=1, source_target_pairs={{0,16},{16,0},{1,17},{17,1},{2,18},{18,2},{3,19},{19,3},{4,20},{20... | collective-permute-start | bytes 884744 | tf_op jit(solution)/shard_map/ppermute | solution.py:405
  22.9 9.0 %collective-permute-start.10 = (bf16[144,1024]{1,0:T(8,128)(2,1)S(1)}, bf16[144,1024]{1,0:T(8,128)(2,1)S(1)}, u32[]{:S(2)}, u32[]{:S(2)}) collective-permute-start(bf16[144,1024]{1,0:T(8,128)(2,1)S(1)} %join.3.refs_0_), channel_id=1, source_target_pairs={{0,1},{1,0},{2,3},{3,2},{4,5},{5,4},{6,7},{7,6},{8,9},{9,8},{10,11... | collective-permute-start | bytes 884744 | tf_op jit(solution)/shard_map/ppermute | solution.py:405
  26.6 13.3 %collective-permute-start.4 = (bf16[72,1024]{1,0:T(8,128)(2,1)S(1)}, bf16[72,1024]{1,0:T(8,128)(2,1)S(1)}, u32[]{:S(2)}, u32[]{:S(2)}) collective-permute-start(bf16[72,1024]{1,0:T(8,128)(2,1)S(1)} %get-tuple-element.48), channel_id=1, source_target_pairs={{0,4},{2,6},{4,0},{6,2},{1,5},{3,7},{5,1},{7,3},{8,12},{10,14},{12... | collective-permute-start | bytes 442376 | tf_op jit(solution)/shard_map/ppermute | solution.py:410
  27.6 12.3 %collective-permute-start.5 = (bf16[72,1024]{1,0:T(8,128)(2,1)S(1)}, bf16[72,1024]{1,0:T(8,128)(2,1)S(1)}, u32[]{:S(2)}, u32[]{:S(2)}) collective-permute-start(bf16[72,1024]{1,0:T(8,128)(2,1)S(1)} %get-tuple-element.49), channel_id=1, source_target_pairs={{0,2},{2,0},{4,6},{6,4},{1,3},{3,1},{5,7},{7,5},{8,10},{10,8},{12,... | collective-permute-start | bytes 442376 | tf_op jit(solution)/shard_map/ppermute | solution.py:410
  30.0 10.0 %collective-permute-start.6 = (bf16[72,1024]{1,0:T(8,128)(2,1)S(1)}, bf16[72,1024]{1,0:T(8,128)(2,1)S(1)}, u32[]{:S(2)}, u32[]{:S(2)}) collective-permute-start(bf16[72,1024]{1,0:T(8,128)(2,1)S(1)} %get-tuple-element.50), channel_id=1, source_target_pairs={{0,6},{2,4},{4,2},{6,0},{1,7},{3,5},{5,3},{7,1},{8,14},{10,12},{12... | collective-permute-start | bytes 442376 | tf_op jit(solution)/shard_map/ppermute | solution.py:410
  31.1 7.2 %collective-permute-start.13 = (bf16[144,1024]{1,0:T(8,128)(2,1)S(1)}, bf16[144,1024]{1,0:T(8,128)(2,1)S(1)}, u32[]{:S(2)}, u32[]{:S(2)}) collective-permute-start(bf16[144,1024]{1,0:T(8,128)(2,1)S(1)} %relay.4.refs_1_), channel_id=1, source_target_pairs={{0,16},{16,0},{1,17},{17,1},{2,18},{18,2},{3,19},{19,3},{4,20},{20... | collective-permute-start | bytes 884744 | tf_op jit(solution)/shard_map/ppermute | solution.py:405
  31.9 8.9 %collective-permute-start.15 = (bf16[144,1024]{1,0:T(8,128)(2,1)S(1)}, bf16[144,1024]{1,0:T(8,128)(2,1)S(1)}, u32[]{:S(2)}, u32[]{:S(2)}) collective-permute-start(bf16[144,1024]{1,0:T(8,128)(2,1)S(1)} %relay.5.refs_0_), channel_id=1, source_target_pairs={{0,1},{1,0},{2,3},{3,2},{4,5},{5,4},{6,7},{7,6},{8,9},{9,8},{10,11... | collective-permute-start | bytes 884744 | tf_op jit(solution)/shard_map/ppermute | solution.py:405
  40.1 7.0 %collective-permute-start.14 = (bf16[144,1024]{1,0:T(8,128)(2,1)S(1)}, bf16[144,1024]{1,0:T(8,128)(2,1)S(1)}, u32[]{:S(2)}, u32[]{:S(2)}) collective-permute-start(bf16[144,1024]{1,0:T(8,128)(2,1)S(1)} %get-tuple-element.68), channel_id=1, source_target_pairs={{0,1},{1,0},{2,3},{3,2},{4,5},{5,4},{6,7},{7,6},{8,9},{9,8},{10,11... | collective-permute-start | bytes 884744 | tf_op jit(solution)/shard_map/ppermute | solution.py:405
  43.1 2.8 %collective-permute-start.16 = (bf16[512,1024]{1,0:T(8,128)(2,1)S(1)}, bf16[512,1024]{1,0:T(8,128)(2,1)S(1)}, u32[]{:S(2)}, u32[]{:S(2)}) collective-permute-start(bf16[512,1024]{1,0:T(8,128)(2,1)S(1)} %get-tuple-element.72), channel_id=1, source_target_pairs={{0,8},{8,0},{1,9},{9,1},{2,10},{10,2},{3,11},{11,3},{4,12},{12,4},... | collective-permute-start | bytes 3145736 | tf_op jit(solution)/shard_map/ppermute | solution.py:405
  45.4 2.9 %collective-permute-start.17 = (bf16[512,1024]{1,0:T(8,128)(2,1)S(1)}, bf16[512,1024]{1,0:T(8,128)(2,1)S(1)}, u32[]{:S(2)}, u32[]{:S(2)}) collective-permute-start(bf16[512,1024]{1,0:T(8,128)(2,1)S(1)} %get-tuple-element.75), channel_id=1, source_target_pairs={{0,8},{8,0},{1,9},{9,1},{2,10},{10,2},{3,11},{11,3},{4,12},{12,4},... | collective-permute-start | bytes 3145736 | tf_op jit(solution)/shard_map/ppermute | solution.py:405

commit v25 on v22

--- a/solution.py
+++ b/solution.py
@@ -11,7 +11,7 @@
 EXPERTS = 4
 CAP = 36
 WIDE = 1024
-STRIP = 512
+STRIP = 1024
 SLICE = 256
 SENT = (0, 2, 1, 3)
 MIB = 1024 * 1024

time: 49.6 us -> 49.6 us (level)
  transfers between devices with their start and end apart: 18 -> 18, of which waited for: 4 -> 3; matrix products, arithmetic and copies ran while one was open for 0% -> 0% of each run, Pallas kernels for 40% -> 40%
where the time goes in v25:
time: 49.6 us; the launch traced here: 49.4 us
  starting transfers between devices  24.8 us (50%)
  Pallas kernels  22.4 us (45%)
  waiting for transfers between devices  1.31 us (3%)
  between operations  0.98 us (2%)
    ppermute x9, starting transfers between devices, across_planes(): lax.ppermute(blocks[k], 'arch', [(i, i ^ k) for i in range(EXPERTS)])  14.7 us
    ppermute x9, starting transfers between devices, swap(): return lax.ppermute(value, axis, [(0, 1), (1, 0)])  10.1 us
    pallas_call x4, Pallas kernels, forward(): pl.pallas_call(functools.partial(forward_kernel, n, fetch, down, pair, le...  7.62 us
    pallas_call x2, Pallas kernels, backward(): pl.pallas_call(functools.partial(backward_kernel, first), out_shape=[jax....  4.47 us
    pallas_call x1, Pallas kernels, flip(): pl.pallas_call(flip_kernel, out_shape=[pltpu.VMEM(value.shape, value.dtyp...  2.88 us
    pallas_call x2, Pallas kernels, finish(): pl.pallas_call(functools.partial(finish_kernel, spans, more, len(earlier)...  2.21 us
    pallas_call x1, Pallas kernels, slopes(): pl.pallas_call(functools.partial(slopes_kernel, n), out_shape=[jax.ShapeD...  2.19 us
    pallas_call x1, Pallas kernels, pack(): pl.pallas_call(pack_kernel, out_shape=[jax.ShapeDtypeStruct((EXPERTS * CA...  1.46 us
  transfers between devices with their start and end apart: 18, of which 3 were waited for; matrix products, arithmetic and copies ran while one was open for 0% of the time, Pallas kernels for 40%

profile of v25, /device:TPU:0, one launch (start us, length us, event | category | flops | bytes accessed | tf_op | source)
XLA Modules:
  0.0 49.4 jit_solution(5057805822785088579)
XLA Ops:
  0.6 1.5 %pack.1 = (bf16[144,128]{1,0:T(8,128)(2,1)S(1)}, bf16[36,1024]{1,0:T(8,128)(2,1)S(1)}, bf16[36,1024]{1,0:T(8,128)(2,1)S(1)}, bf16[36,1024]{1,0:T(8,128)(2,1)S(1)...) custom-call(s32[1]{0:T(128)} %bitcast.plane_ref, ...), custom_call_target="tpu_custom_call" | custom-call | tf_op jit(solution)/shard_map/pack/pallas_call | solution.py:80
  2.1 5.1 %collective-permute-start = (bf16[36,1024]{1,0:T(8,128)(2,1)S(1)}, bf16[36,1024]{1,0:T(8,128)(2,1)S(1)}, u32[]{:S(2)}, u32[]{:S(2)}) collective-permute-start(bf16[36,1024]{1,0:T(8,128)(2,1)S(1)} %get-tuple-element.45), channel_id=1, source_target_pairs={{0,6},{2,4},{4,2},{6,0},{1,7},{3,5},{5,3},{7,1},{8,14},{10,12},{12... | collective-permute-start | bytes 221192 | tf_op jit(solution)/shard_map/ppermute | solution.py:416
  7.2 0.6 %collective-permute-start.2 = (bf16[36,1024]{1,0:T(8,128)(2,1)S(1)}, bf16[36,1024]{1,0:T(8,128)(2,1)S(1)}, u32[]{:S(2)}, u32[]{:S(2)}) collective-permute-start(bf16[36,1024]{1,0:T(8,128)(2,1)S(1)} %get-tuple-element.47), channel_id=1, source_target_pairs={{0,2},{2,0},{4,6},{6,4},{1,3},{3,1},{5,7},{7,5},{8,10},{10,8},{12,... | collective-permute-start | bytes 221192 | tf_op jit(solution)/shard_map/ppermute | solution.py:416
  7.9 2.9 %flip.1 = (bf16[2048,1024]{1,0:T(8,128)(2,1)S(1)}, bf16[1024,2048]{1,0:T(8,128)(2,1)S(1)}) custom-call(bf16[2048,1024]{1,0:T(8,128)(2,1)} %source_ref), custom_call_target="tpu_custom_call" | custom-call | tf_op jit(solution)/shard_map/flip/pallas_call | solution.py:159
  10.8 3.8 %collective-permute-start.7 = (bf16[36,1024]{1,0:T(8,128)(2,1)S(1)}, bf16[36,1024]{1,0:T(8,128)(2,1)S(1)}, u32[]{:S(2)}, u32[]{:S(2)}) collective-permute-start(bf16[36,1024]{1,0:T(8,128)(2,1)S(1)} %get-tuple-element.62), channel_id=1, source_target_pairs={{0,6},{2,4},{4,2},{6,0},{1,7},{3,5},{5,3},{7,1},{8,14},{10,12},{12... | collective-permute-start | bytes 221192 | tf_op jit(solution)/shard_map/ppermute | solution.py:416
  14.6 0.6 %collective-permute-start.9 = (bf16[36,1024]{1,0:T(8,128)(2,1)S(1)}, bf16[36,1024]{1,0:T(8,128)(2,1)S(1)}, u32[]{:S(2)}, u32[]{:S(2)}) collective-permute-start(bf16[36,1024]{1,0:T(8,128)(2,1)S(1)} %get-tuple-element.64), channel_id=1, source_target_pairs={{0,2},{2,0},{4,6},{6,4},{1,3},{3,1},{5,7},{7,5},{8,10},{10,8},{12,... | collective-permute-start | bytes 221192 | tf_op jit(solution)/shard_map/ppermute | solution.py:416
  15.3 1.7 %collective-permute-start.3 = (bf16[144,1024]{1,0:T(8,128)(2,1)S(1)}, bf16[144,1024]{1,0:T(8,128)(2,1)S(1)}, u32[]{:S(2)}, u32[]{:S(2)}) collective-permute-start(bf16[144,1024]{1,0:T(8,128)(2,1)S(1)} %join.2.refs_0_.refs_4_), channel_id=1, source_target_pairs={{0,1},{1,0},{2,3},{3,2},{4,5},{5,4},{6,7},{7,6},{8,9},{9,8},{10,11... | collective-permute-start | bytes 884744 | tf_op jit(solution)/shard_map/ppermute | solution.py:411
  17.0 1.5 %collective-permute-start.12 = (bf16[144,1024]{1,0:T(8,128)(2,1)S(1)}, bf16[144,1024]{1,0:T(8,128)(2,1)S(1)}, u32[]{:S(2)}, u32[]{:S(2)}) collective-permute-start(bf16[144,1024]{1,0:T(8,128)(2,1)S(1)} %join.2.refs_0_.refs_4_), channel_id=1, source_target_pairs={{0,16},{16,0},{1,17},{17,1},{2,18},{18,2},{3,19},{19,3},{4,20},{20... | collective-permute-start | bytes 884744 | tf_op jit(solution)/shard_map/ppermute | solution.py:411
  18.5 2.2 %forward_down.2 = (bf16[144,2048]{1,0:T(8,128)(2,1)S(1)}, bf16[144,2048]{1,0:T(8,128)(2,1)S(1)}, bf16[144,1024]{1,0:T(8,128)(2,1)S(1)}) custom-call(bf16[144,1024]{1,0:T(8,128)(2,1)S(1)} %join.2.refs_0_.refs_4_, bf16[1024,2048]{1,0:T(8,128)(2,1)S(1)} %copy-done, bf16[1024,2048]{1,0:T(8,128)(2,1)S(1)} %copy-done.1, ...), custom_call_target="tpu_custom_call" | custom-call | tf_op jit(solution)/shard_map/forward_down/pallas_call | solution.py:239
  20.8 0.3 collective-permute-done.8.refs_2_
  21.2 1.6 %collective-permute-start.11 = (bf16[144,1024]{1,0:T(8,128)(2,1)S(1)}, bf16[144,1024]{1,0:T(8,128)(2,1)S(1)}, u32[]{:S(2)}, u32[]{:S(2)}) collective-permute-start(bf16[144,1024]{1,0:T(8,128)(2,1)S(1)} %join.3.refs_0_), channel_id=1, source_target_pairs={{0,16},{16,0},{1,17},{17,1},{2,18},{18,2},{3,19},{19,3},{4,20},{20... | collective-permute-start | bytes 884744 | tf_op jit(solution)/shard_map/ppermute | solution.py:411
  22.7 1.5 %collective-permute-start.10 = (bf16[144,1024]{1,0:T(8,128)(2,1)S(1)}, bf16[144,1024]{1,0:T(8,128)(2,1)S(1)}, u32[]{:S(2)}, u32[]{:S(2)}) collective-permute-start(bf16[144,1024]{1,0:T(8,128)(2,1)S(1)} %join.3.refs_0_), channel_id=1, source_target_pairs={{0,1},{1,0},{2,3},{3,2},{4,5},{5,4},{6,7},{7,6},{8,9},{9,8},{10,11... | collective-permute-start | bytes 884744 | tf_op jit(solution)/shard_map/ppermute | solution.py:411
  24.2 2.2 %forward_down.3 = (bf16[144,2048]{1,0:T(8,128)(2,1)S(1)}, bf16[144,2048]{1,0:T(8,128)(2,1)S(1)}, bf16[72,1024]{1,0:T(8,128)(2,1)S(1)}, bf16[72,1024]{1,0:T(8,128...) custom-call(bf16[144,1024]{1,0:T(8,128)(2,1)S(1)} %collective-permute-done.3.refs_0_.refs_1_.refs_5_, ...), custom_call_target="tpu_custom_call" | custom-call | tf_op jit(solution)/shard_map/forward_down/pallas_call | solution.py:239
  26.5 1.7 %collective-permute-start.4 = (bf16[72,1024]{1,0:T(8,128)(2,1)S(1)}, bf16[72,1024]{1,0:T(8,128)(2,1)S(1)}, u32[]{:S(2)}, u32[]{:S(2)}) collective-permute-start(bf16[72,1024]{1,0:T(8,128)(2,1)S(1)} %get-tuple-element.53), channel_id=1, source_target_pairs={{0,4},{2,6},{4,0},{6,2},{1,5},{3,7},{5,1},{7,3},{8,12},{10,14},{12... | collective-permute-start | bytes 442376 | tf_op jit(solution)/shard_map/ppermute | solution.py:416
  28.2 1.6 %collective-permute-start.5 = (bf16[72,1024]{1,0:T(8,128)(2,1)S(1)}, bf16[72,1024]{1,0:T(8,128)(2,1)S(1)}, u32[]{:S(2)}, u32[]{:S(2)}) collective-permute-start(bf16[72,1024]{1,0:T(8,128)(2,1)S(1)} %get-tuple-element.54), channel_id=1, source_target_pairs={{0,2},{2,0},{4,6},{6,4},{1,3},{3,1},{5,7},{7,5},{8,10},{10,8},{12,... | collective-permute-start | bytes 442376 | tf_op jit(solution)/shard_map/ppermute | solution.py:416
  29.8 1.1 %collective-permute-start.6 = (bf16[72,1024]{1,0:T(8,128)(2,1)S(1)}, bf16[72,1024]{1,0:T(8,128)(2,1)S(1)}, u32[]{:S(2)}, u32[]{:S(2)}) collective-permute-start(bf16[72,1024]{1,0:T(8,128)(2,1)S(1)} %get-tuple-element.55), channel_id=1, source_target_pairs={{0,6},{2,4},{4,2},{6,0},{1,7},{3,5},{5,3},{7,1},{8,14},{10,12},{12... | collective-permute-start | bytes 442376 | tf_op jit(solution)/shard_map/ppermute | solution.py:416
  31.0 0.9 %collective-permute-start.13 = (bf16[144,1024]{1,0:T(8,128)(2,1)S(1)}, bf16[144,1024]{1,0:T(8,128)(2,1)S(1)}, u32[]{:S(2)}, u32[]{:S(2)}) collective-permute-start(bf16[144,1024]{1,0:T(8,128)(2,1)S(1)} %relay.4.refs_1_), channel_id=1, source_target_pairs={{0,16},{16,0},{1,17},{17,1},{2,18},{18,2},{3,19},{19,3},{4,20},{20... | collective-permute-start | bytes 884744 | tf_op jit(solution)/shard_map/ppermute | solution.py:411
  31.9 2.0 %collective-permute-start.15 = (bf16[144,1024]{1,0:T(8,128)(2,1)S(1)}, bf16[144,1024]{1,0:T(8,128)(2,1)S(1)}, u32[]{:S(2)}, u32[]{:S(2)}) collective-permute-start(bf16[144,1024]{1,0:T(8,128)(2,1)S(1)} %relay.5.refs_0_), channel_id=1, source_target_pairs={{0,1},{1,0},{2,3},{3,2},{4,5},{5,4},{6,7},{7,6},{8,9},{9,8},{10,11... | collective-permute-start | bytes 884744 | tf_op jit(solution)/shard_map/ppermute | solution.py:411
  33.9 1.6 %forward.2 = (bf16[144,2048]{1,0:T(8,128)(2,1)S(1)}, bf16[144,2048]{1,0:T(8,128)(2,1)S(1)}) custom-call(bf16[144,1024]{1,0:T(8,128)(2,1)S(1)} %relay.5.refs_0_, bf16[144,1024]{1,0:T(8,128)(2,1)S(1)} %collective-permute-done.12._.refs_1_.refs_2_.refs_6_, bf16[1024,2048]{1,0:T(8,128)(2,1)S(1)} %copy-done, bf16[1024,2048]{1,0:T(8,128)(2,1)S(1)} %copy-done.1), custom_call_target="tpu_custom_call" | custom-call | flops 20000000000 | tf_op jit(solution)/shard_map/forward/pallas_call | solution.py:239
  35.5 2.2 %slopes.1 = (bf16[432,2048]{1,0:T(8,128)(2,1)S(1)}, bf16[432,2048]{1,0:T(8,128)(2,1)S(1)}) custom-call(bf16[144,1024]{1,0:T(8,128)(2,1)S(1)} %join.3.refs_0_, bf16[144,1024]{1,0:T(8,128)(2,1)S(1)} %collective-permute-done.10.refs_2_.refs_1_, bf16[144,1024]{1,0:T(8,128)(2,1)S(1)} %collective-permute-done.11.refs_2_.refs_0_, ...), custom_call_target="tpu_custom_call" | custom-call | tf_op jit(solution)/shard_map/slopes/pallas_call | solution.py:298
  37.7 0.8 %collective-permute-done.13.refs_1_.refs_3_.refs_7_ = bf16[144,1024]{1,0:T(8,128)(2,1)S(1)} collective-permute-done((bf16[144,1024]{1,0:T(8,128)(2,1)S(1)}, bf16[144,1024]{1,0:T(8,128)(2,1)S(1)}, u32[]{:S(2)}, u32[]{:S(2)}) %collective-permute-start.13) | collective-permute-done | bytes 294944 | tf_op jit(solution)/shard_map/ppermute | solution.py:411
  38.5 1.6 %forward.3 = (bf16[144,2048]{1,0:T(8,128)(2,1)S(1)}, bf16[144,2048]{1,0:T(8,128)(2,1)S(1)}) custom-call(bf16[432,2048]{1,0:T(8,128)(2,1)S(1)} %get-tuple-element.71.refs_0_.dg_ref, bf16[144,1024]{1,0:T(8,128)(2,1)S(1)} %collective-permute-done.13.refs_1_.refs_3_.refs_7_, bf16[1024,2048]{1,0:T(8,128)(2,1)S(1)} %copy-done, bf16[1024,2048]{1,0:T(8,128)(2,1)S(1)} %copy-done.1), custom_call_target="tpu_custom_call" | custom-call | tf_op jit(solution)/shard_map/forward/pallas_call | solution.py:239
  40.1 0.1 split.1
  40.2 0.3 collective-permute-start.14
  40.5 0.2 turn.1.xt_ref
  40.7 2.3 %backward.2 = (bf16[512,1024]{1,0:T(8,128)(2,1)S(1)}, bf16[512,1024]{1,0:T(8,128)(2,1)S(1)}) custom-call(bf16[512,576]{1,0:T(8,128)(2,1)S(1)} %turn.1.xt_ref, bf16[144,1024]{1,0:T(8,128)(2,1)S(1)} %collective-permute-done.15.g_ref, bf16[144,2048]{1,0:T(8,128)(2,1)S(1)} %get-tuple-element.72.refs_4_.act_ref, ...), custom_call_target="tpu_custom_call" | custom-call | flops 20000000000 | tf_op jit(solution)/shard_map/backward/pallas_call | solution.py:325
  43.2 2.1 %backward.3 = (bf16[512,1024]{1,0:T(8,128)(2,1)S(1)}, bf16[512,1024]{1,0:T(8,128)(2,1)S(1)}) custom-call(bf16[512,576]{1,0:T(8,128)(2,1)S(1)} %turn.1.xt_ref, bf16[144,1024]{1,0:T(8,128)(2,1)S(1)} %collective-permute-done.15.g_ref, bf16[144,2048]{1,0:T(8,128)(2,1)S(1)} %get-tuple-element.72.refs_4_.act_ref, ...), custom_call_target="tpu_custom_call" | custom-call | flops 20000000000 | tf_op jit(solution)/shard_map/backward/pallas_call | solution.py:325
  45.3 0.6 %collective-permute-start.17 = (bf16[512,1024]{1,0:T(8,128)(2,1)S(1)}, bf16[512,1024]{1,0:T(8,128)(2,1)S(1)}, u32[]{:S(2)}, u32[]{:S(2)}) collective-permute-start(bf16[512,1024]{1,0:T(8,128)(2,1)S(1)} %get-tuple-element.81), channel_id=1, source_target_pairs={{0,8},{8,0},{1,9},{9,1},{2,10},{10,2},{3,11},{11,3},{4,12},{12,4},... | collective-permute-start | bytes 3145736 | tf_op jit(solution)/shard_map/ppermute | solution.py:411
  45.9 1.1 %finish.2 = (bf16[256,2048]{1,0:T(8,128)(2,1)}, bf16[256,2048]{1,0:T(8,128)(2,1)}) custom-call(bf16[512,1024]{1,0:T(8,128)(2,1)S(1)} %get-tuple-element.77.refs_0_, bf16[512,1024]{1,0:T(8,128)(2,1)S(1)} %collective-permute-done.16.refs_1_), custom_call_target="tpu_custom_call" | custom-call | tf_op jit(solution)/shard_map/finish/pallas_call | solution.py:361
  47.0 1.0 %unpack.1 = bf16[128,1024]{1,0:T(8,128)(2,1)} custom-call(bf16[144,128]{1,0:T(8,128)(2,1)S(1)} %get-tuple-element.44.placer_ref, bf16[144,1024]{1,0:T(8,128)(2,1)S(1)} %get-tuple-element.73.mine_ref, bf16[144,1024]{1,0:T(8,128)(2,1)S(1)} %collective-permute-done.14.got_ref, bf16[256,2048]{1,0:T(8,128)(2,1)} %get-tuple-element.79.refs_0_.refs_2_), custom_call_target="tpu_custom_call" | custom-call | flops 20000000000 | tf_op jit(solution)/shard_map/unpack/pallas_call | solution.py:400
  48.1 0.1 collective-permute-done.17.refs_1_
  48.2 1.1 %finish.3 = (bf16[256,2048]{1,0:T(8,128)(2,1)}, bf16[256,2048]{1,0:T(8,128)(2,1)}) custom-call(bf16[512,1024]{1,0:T(8,128)(2,1)S(1)} %get-tuple-element.80.refs_0_, bf16[512,1024]{1,0:T(8,128)(2,1)S(1)} %collective-permute-done.17.refs_1_, bf16[256,2048]{1,0:T(8,128)(2,1)} %get-tuple-element.79.refs_0_.refs_2_, ...), custom_call_target="tpu_custom_call", output_to_operand_aliasing={{0}: (2, {}), {1}: (3, {})} | custom-call | tf_op jit(solution)/shard_map/finish/pallas_call | solution.py:361
  (28 shorter events, 0.3 us)
Async XLA Ops:
  2.1 12.5 %collective-permute-start = (bf16[36,1024]{1,0:T(8,128)(2,1)S(1)}, bf16[36,1024]{1,0:T(8,128)(2,1)S(1)}, u32[]{:S(2)}, u32[]{:S(2)}) collective-permute-start(bf16[36,1024]{1,0:T(8,128)(2,1)S(1)} %get-tuple-element.45), channel_id=1, source_target_pairs={{0,6},{2,4},{4,2},{6,0},{1,7},{3,5},{5,3},{7,1},{8,14},{10,12},{12... | collective-permute-start | bytes 221192 | tf_op jit(solution)/shard_map/ppermute | solution.py:416
  7.2 8.0 %collective-permute-start.1 = (bf16[36,1024]{1,0:T(8,128)(2,1)S(1)}, bf16[36,1024]{1,0:T(8,128)(2,1)S(1)}, u32[]{:S(2)}, u32[]{:S(2)}) collective-permute-start(bf16[36,1024]{1,0:T(8,128)(2,1)S(1)} %get-tuple-element.46), channel_id=1, source_target_pairs={{0,4},{2,6},{4,0},{6,2},{1,5},{3,7},{5,1},{7,3},{8,12},{10,14},{12... | collective-permute-start | bytes 221192 | tf_op jit(solution)/shard_map/ppermute | solution.py:416
  7.2 8.0 %collective-permute-start.2 = (bf16[36,1024]{1,0:T(8,128)(2,1)S(1)}, bf16[36,1024]{1,0:T(8,128)(2,1)S(1)}, u32[]{:S(2)}, u32[]{:S(2)}) collective-permute-start(bf16[36,1024]{1,0:T(8,128)(2,1)S(1)} %get-tuple-element.47), channel_id=1, source_target_pairs={{0,2},{2,0},{4,6},{6,4},{1,3},{3,1},{5,7},{7,5},{8,10},{10,8},{12,... | collective-permute-start | bytes 221192 | tf_op jit(solution)/shard_map/ppermute | solution.py:416
  7.9 10.7 %copy-start = (bf16[1024,2048]{1,0:T(8,128)(2,1)S(1)}, bf16[1024,2048]{1,0:T(8,128)(2,1)}, u32[]{:S(2)}) copy-start(bf16[1024,2048]{1,0:T(8,128)(2,1)} %refs_2_.7) | copy-start | bytes 12582916
  7.9 10.7 %copy-start.1 = (bf16[1024,2048]{1,0:T(8,128)(2,1)S(1)}, bf16[1024,2048]{1,0:T(8,128)(2,1)}, u32[]{:S(2)}) copy-start(bf16[1024,2048]{1,0:T(8,128)(2,1)} %refs_3_.3) | copy-start | bytes 12582916
  10.8 10.0 %collective-permute-start.7 = (bf16[36,1024]{1,0:T(8,128)(2,1)S(1)}, bf16[36,1024]{1,0:T(8,128)(2,1)S(1)}, u32[]{:S(2)}, u32[]{:S(2)}) collective-permute-start(bf16[36,1024]{1,0:T(8,128)(2,1)S(1)} %get-tuple-element.62), channel_id=1, source_target_pairs={{0,6},{2,4},{4,2},{6,0},{1,7},{3,5},{5,3},{7,1},{8,14},{10,12},{12... | collective-permute-start | bytes 221192 | tf_op jit(solution)/shard_map/ppermute | solution.py:416
  14.6 6.5 %collective-permute-start.8 = (bf16[36,1024]{1,0:T(8,128)(2,1)S(1)}, bf16[36,1024]{1,0:T(8,128)(2,1)S(1)}, u32[]{:S(2)}, u32[]{:S(2)}) collective-permute-start(bf16[36,1024]{1,0:T(8,128)(2,1)S(1)} %get-tuple-element.63), channel_id=1, source_target_pairs={{0,4},{2,6},{4,0},{6,2},{1,5},{3,7},{5,1},{7,3},{8,12},{10,14},{12... | collective-permute-start | bytes 221192 | tf_op jit(solution)/shard_map/ppermute | solution.py:416
  14.6 6.5 %collective-permute-start.9 = (bf16[36,1024]{1,0:T(8,128)(2,1)S(1)}, bf16[36,1024]{1,0:T(8,128)(2,1)S(1)}, u32[]{:S(2)}, u32[]{:S(2)}) collective-permute-start(bf16[36,1024]{1,0:T(8,128)(2,1)S(1)} %get-tuple-element.64), channel_id=1, source_target_pairs={{0,2},{2,0},{4,6},{6,4},{1,3},{3,1},{5,7},{7,5},{8,10},{10,8},{12,... | collective-permute-start | bytes 221192 | tf_op jit(solution)/shard_map/ppermute | solution.py:416
  15.3 8.9 %collective-permute-start.3 = (bf16[144,1024]{1,0:T(8,128)(2,1)S(1)}, bf16[144,1024]{1,0:T(8,128)(2,1)S(1)}, u32[]{:S(2)}, u32[]{:S(2)}) collective-permute-start(bf16[144,1024]{1,0:T(8,128)(2,1)S(1)} %join.2.refs_0_.refs_4_), channel_id=1, source_target_pairs={{0,1},{1,0},{2,3},{3,2},{4,5},{5,4},{6,7},{7,6},{8,9},{9,8},{10,11... | collective-permute-start | bytes 884744 | tf_op jit(solution)/shard_map/ppermute | solution.py:411
  17.0 12.8 %collective-permute-start.12 = (bf16[144,1024]{1,0:T(8,128)(2,1)S(1)}, bf16[144,1024]{1,0:T(8,128)(2,1)S(1)}, u32[]{:S(2)}, u32[]{:S(2)}) collective-permute-start(bf16[144,1024]{1,0:T(8,128)(2,1)S(1)} %join.2.refs_0_.refs_4_), channel_id=1, source_target_pairs={{0,16},{16,0},{1,17},{17,1},{2,18},{18,2},{3,19},{19,3},{4,20},{20... | collective-permute-start | bytes 884744 | tf_op jit(solution)/shard_map/ppermute | solution.py:411
  21.2 9.8 %collective-permute-start.11 = (bf16[144,1024]{1,0:T(8,128)(2,1)S(1)}, bf16[144,1024]{1,0:T(8,128)(2,1)S(1)}, u32[]{:S(2)}, u32[]{:S(2)}) collective-permute-start(bf16[144,1024]{1,0:T(8,128)(2,1)S(1)} %join.3.refs_0_), channel_id=1, source_target_pairs={{0,16},{16,0},{1,17},{17,1},{2,18},{18,2},{3,19},{19,3},{4,20},{20... | collective-permute-start | bytes 884744 | tf_op jit(solution)/shard_map/ppermute | solution.py:411
  22.7 9.2 %collective-permute-start.10 = (bf16[144,1024]{1,0:T(8,128)(2,1)S(1)}, bf16[144,1024]{1,0:T(8,128)(2,1)S(1)}, u32[]{:S(2)}, u32[]{:S(2)}) collective-permute-start(bf16[144,1024]{1,0:T(8,128)(2,1)S(1)} %join.3.refs_0_), channel_id=1, source_target_pairs={{0,1},{1,0},{2,3},{3,2},{4,5},{5,4},{6,7},{7,6},{8,9},{9,8},{10,11... | collective-permute-start | bytes 884744 | tf_op jit(solution)/shard_map/ppermute | solution.py:411
  26.5 13.6 %collective-permute-start.4 = (bf16[72,1024]{1,0:T(8,128)(2,1)S(1)}, bf16[72,1024]{1,0:T(8,128)(2,1)S(1)}, u32[]{:S(2)}, u32[]{:S(2)}) collective-permute-start(bf16[72,1024]{1,0:T(8,128)(2,1)S(1)} %get-tuple-element.53), channel_id=1, source_target_pairs={{0,4},{2,6},{4,0},{6,2},{1,5},{3,7},{5,1},{7,3},{8,12},{10,14},{12... | collective-permute-start | bytes 442376 | tf_op jit(solution)/shard_map/ppermute | solution.py:416
  28.2 11.9 %collective-permute-start.5 = (bf16[72,1024]{1,0:T(8,128)(2,1)S(1)}, bf16[72,1024]{1,0:T(8,128)(2,1)S(1)}, u32[]{:S(2)}, u32[]{:S(2)}) collective-permute-start(bf16[72,1024]{1,0:T(8,128)(2,1)S(1)} %get-tuple-element.54), channel_id=1, source_target_pairs={{0,2},{2,0},{4,6},{6,4},{1,3},{3,1},{5,7},{7,5},{8,10},{10,8},{12,... | collective-permute-start | bytes 442376 | tf_op jit(solution)/shard_map/ppermute | solution.py:416
  29.8 10.3 %collective-permute-start.6 = (bf16[72,1024]{1,0:T(8,128)(2,1)S(1)}, bf16[72,1024]{1,0:T(8,128)(2,1)S(1)}, u32[]{:S(2)}, u32[]{:S(2)}) collective-permute-start(bf16[72,1024]{1,0:T(8,128)(2,1)S(1)} %get-tuple-element.55), channel_id=1, source_target_pairs={{0,6},{2,4},{4,2},{6,0},{1,7},{3,5},{5,3},{7,1},{8,14},{10,12},{12... | collective-permute-start | bytes 442376 | tf_op jit(solution)/shard_map/ppermute | solution.py:416
  31.0 7.6 %collective-permute-start.13 = (bf16[144,1024]{1,0:T(8,128)(2,1)S(1)}, bf16[144,1024]{1,0:T(8,128)(2,1)S(1)}, u32[]{:S(2)}, u32[]{:S(2)}) collective-permute-start(bf16[144,1024]{1,0:T(8,128)(2,1)S(1)} %relay.4.refs_1_), channel_id=1, source_target_pairs={{0,16},{16,0},{1,17},{17,1},{2,18},{18,2},{3,19},{19,3},{4,20},{20... | collective-permute-start | bytes 884744 | tf_op jit(solution)/shard_map/ppermute | solution.py:411
  31.9 8.8 %collective-permute-start.15 = (bf16[144,1024]{1,0:T(8,128)(2,1)S(1)}, bf16[144,1024]{1,0:T(8,128)(2,1)S(1)}, u32[]{:S(2)}, u32[]{:S(2)}) collective-permute-start(bf16[144,1024]{1,0:T(8,128)(2,1)S(1)} %relay.5.refs_0_), channel_id=1, source_target_pairs={{0,1},{1,0},{2,3},{3,2},{4,5},{5,4},{6,7},{7,6},{8,9},{9,8},{10,11... | collective-permute-start | bytes 884744 | tf_op jit(solution)/shard_map/ppermute | solution.py:411
  40.2 6.8 %collective-permute-start.14 = (bf16[144,1024]{1,0:T(8,128)(2,1)S(1)}, bf16[144,1024]{1,0:T(8,128)(2,1)S(1)}, u32[]{:S(2)}, u32[]{:S(2)}) collective-permute-start(bf16[144,1024]{1,0:T(8,128)(2,1)S(1)} %get-tuple-element.74), channel_id=1, source_target_pairs={{0,1},{1,0},{2,3},{3,2},{4,5},{5,4},{6,7},{7,6},{8,9},{9,8},{10,11... | collective-permute-start | bytes 884744 | tf_op jit(solution)/shard_map/ppermute | solution.py:411
  43.1 2.8 %collective-permute-start.16 = (bf16[512,1024]{1,0:T(8,128)(2,1)S(1)}, bf16[512,1024]{1,0:T(8,128)(2,1)S(1)}, u32[]{:S(2)}, u32[]{:S(2)}) collective-permute-start(bf16[512,1024]{1,0:T(8,128)(2,1)S(1)} %get-tuple-element.78), channel_id=1, source_target_pairs={{0,8},{8,0},{1,9},{9,1},{2,10},{10,2},{3,11},{11,3},{4,12},{12,4},... | collective-permute-start | bytes 3145736 | tf_op jit(solution)/shard_map/ppermute | solution.py:411
  45.3 2.8 %collective-permute-start.17 = (bf16[512,1024]{1,0:T(8,128)(2,1)S(1)}, bf16[512,1024]{1,0:T(8,128)(2,1)S(1)}, u32[]{:S(2)}, u32[]{:S(2)}) collective-permute-start(bf16[512,1024]{1,0:T(8,128)(2,1)S(1)} %get-tuple-element.81), channel_id=1, source_target_pairs={{0,8},{8,0},{1,9},{9,1},{2,10},{10,2},{3,11},{11,3},{4,12},{12,4},... | collective-permute-start | bytes 3145736 | tf_op jit(solution)/shard_map/ppermute | solution.py:411
